TPU v7x, 32 devices: a whole 2x2x4 slice. The times are simulated.
32 devices in a mesh: groups: 2 (over x), labels: 16 (over z, y, core).
Axes of the slice: x: 2, y: 2, z: 4, core: 2. Of those that a mesh axis runs over, the one named last changes fastest.
Arguments:
- embeddings: bfloat16 [32768, 768], P('labels'), may hold values from -6 to 6
- edge_tiles: bfloat16 [64, 2, 512, 512], P('labels'), may hold values from -0.1875 to 0.1875
- neighbour: int32 [64, 2], replicated, may hold values from 0 to 3, as said below
- propensity: float32 [32768], P('labels'), may hold values from 0.05 to 0.5
- queries: bfloat16 [512, 768], P('groups'), parts along dimension 0, may hold values from -6 to 6
- positives: int32 [512, 8], P('groups'), parts along dimension 0, may hold values from 0 to 32767
Outputs:
- grad_embed: bfloat16 [65536, 768], P(('groups', 'labels')), parts along dimension 0
- grad_queries: float32 [512, 768], P('groups'), parts along dimension 0
There are 2 independent parts, one for each index of `groups`. A program takes and returns all parts, laid end to end along the dimension named above; an argument that names none is the same for every part. Nothing has to cross between parts.
Inputs may be any that keep to these rules, and one draw needn't show every extreme that they name: `neighbour`: on each side, the 4 blocks of one shard name exactly 2 distinct blocks of the neighbouring shard.
All inputs are finite; a program needn't handle non-finite values.
Results may differ from a plain program's by a relative error of at most 0.0059.
Values may be sent and summed in bfloat16 or wider, within the bound.
No kernel may reach another device: no remote copies, remote signals or barrier semaphores. Data moves between devices by JAX's collectives and lax.ppermute only.
A program may use at most 128 MiB of HBM per device.

v0:
```python
import math

import jax
import jax.numpy as jnp
from jax import lax
from jax.sharding import PartitionSpec as P


def with_halo(cells, sides, width):
    for axis, dim in sides:
        count = lax.axis_size(axis)
        head = lax.slice_in_dim(cells, 0, width, axis=dim)
        tail = lax.slice_in_dim(cells, cells.shape[dim] - width, cells.shape[dim], axis=dim)
        cells = jnp.concatenate(
            [
                lax.ppermute(tail, axis, [(i, (i + 1) % count) for i in range(count)]),
                cells,
                lax.ppermute(head, axis, [((i + 1) % count, i) for i in range(count)]),
            ],
            axis=dim,
        )
    return cells


def from_behind(block, axis, distance):
    devices = range(lax.axis_size(axis))
    route = [((i - distance) % len(devices), i) for i in devices]
    return lax.ppermute(block, axis, route)


def lists_of(neighbour, device, blocks_dev, side):
    first = device * blocks_dev
    return lax.dynamic_slice_in_dim(neighbour[:, side], first, blocks_dev, 0)


def per_device(embeddings, edge_tiles, neighbour, propensity, queries, positives):
    count = lax.axis_size("labels")
    device = lax.axis_index("labels")
    blocks_dev = edge_tiles.shape[0]
    block = edge_tiles.shape[2]
    width = embeddings.shape[1]
    labels_dev = embeddings.shape[0]
    queries_count = queries.shape[0]
    own_blocks = embeddings.reshape(blocks_dev, block, width)
    own_next = lists_of(neighbour, device, blocks_dev, 0)
    own_prev = lists_of(neighbour, device, blocks_dev, 1)
    cycle = with_halo(embeddings, (("labels", 0),), labels_dev)
    prev_shard = cycle[:labels_dev].reshape(blocks_dev, block, width)
    next_shard = cycle[2 * labels_dev :].reshape(blocks_dev, block, width)
    from_next = jnp.take(next_shard, own_next, axis=0)
    from_prev = jnp.take(prev_shard, own_prev, axis=0)
    mixed = own_blocks.astype(jnp.float32)
    mixed = mixed + jnp.einsum(
        "bij,bjd->bid", edge_tiles[:, 0], from_next, preferred_element_type=jnp.float32
    )
    mixed = mixed + jnp.einsum(
        "bij,bjd->bid", edge_tiles[:, 1], from_prev, preferred_element_type=jnp.float32
    )
    mixed = mixed.astype(jnp.bfloat16).reshape(labels_dev, width)
    scores = jnp.einsum(
        "qd,ld->ql", queries, mixed, preferred_element_type=jnp.float32
    ) / math.sqrt(width)
    label_ids = device * labels_dev + jnp.arange(labels_dev, dtype=jnp.int32)
    hits = jnp.zeros(scores.shape, jnp.bool_)
    for column in range(positives.shape[1]):
        hits = jnp.logical_or(hits, positives[:, column][:, None] == label_ids[None, :])
    signal = (jax.nn.sigmoid(scores) - hits.astype(jnp.float32) / propensity[None, :]).astype(
        jnp.bfloat16
    )
    partial_query = jnp.dot(signal, mixed, preferred_element_type=jnp.float32)
    grad_queries = lax.psum(partial_query, "labels") / math.sqrt(labels_dev * count)
    back = jnp.einsum("ql,qd->ld", signal, queries, preferred_element_type=jnp.float32) / math.sqrt(
        queries_count
    )
    back = back.astype(jnp.bfloat16)
    back_blocks = back.reshape(blocks_dev, block, width)
    push_next = jnp.einsum(
        "bji,bjd->bid", edge_tiles[:, 0], back_blocks, preferred_element_type=jnp.float32
    )
    push_prev = jnp.einsum(
        "bji,bjd->bid", edge_tiles[:, 1], back_blocks, preferred_element_type=jnp.float32
    )
    marks = jnp.arange(blocks_dev, dtype=jnp.int32)
    pick_next = (own_next[:, None] == marks[None, :]).astype(jnp.float32)
    pick_prev = (own_prev[:, None] == marks[None, :]).astype(jnp.float32)
    to_next = jnp.einsum(
        "bj,brd->jrd", pick_next, push_next, precision=lax.Precision.HIGHEST
    ).astype(jnp.bfloat16)
    to_prev = jnp.einsum(
        "bj,brd->jrd", pick_prev, push_prev, precision=lax.Precision.HIGHEST
    ).astype(jnp.bfloat16)
    from_before = from_behind(to_next, "labels", 1).astype(jnp.float32)
    from_after = from_behind(to_prev, "labels", -1).astype(jnp.float32)
    total = back_blocks.astype(jnp.float32) + from_before + from_after
    grad_embed = total.astype(jnp.bfloat16).reshape(labels_dev, width)
    return (grad_embed, grad_queries)


def solution(mesh):
    placed = (
        P("labels", None),
        P("labels", None, None, None),
        P(),
        P("labels"),
        P("groups", None),
        P("groups", None),
    )
    return jax.shard_map(
        per_device,
        mesh=mesh,
        in_specs=placed,
        out_specs=(P(("groups", "labels"), None), P("groups", None)),
        check_vma=False,
    )
```

profile of v0, /device:TPU:0, one launch (start us, length us, event | category | flops | bytes accessed | tf_op | source)
XLA Modules:
  0.0 266.5 jit_solution(15714789774717431239)
XLA Ops:
  7.2 0.0 copy-start
  7.2 0.0 all-reduce.2.cloned.1.call-start
  7.2 0.5 collective-permute-start.1
  7.7 5.1 %collective-permute-start = (bf16[2048,768]{1,0:T(8,128)(2,1)}, bf16[2048,768]{1,0:T(8,128)(2,1)}, u32[]{:S(2)}, u32[]{:S(2)}) collective-permute-start(bf16[2048,768]{1,0:T(8,128)(2,1)} %param.8), channel_id=1, source_target_pairs={{1,0},{2,1},{3,2},{4,3},{5,4},{6,5},{7,6},{8,7},{9,8},{10,9},{11,1... | collective-permute-start | bytes 9437192 | tf_op jit(solution)/shard_map/ppermute | solution.py:18
  12.8 0.8 fusion.40
  13.5 0.6 compare_and_fusion
  14.2 0.6 compare_and_fusion.1
  14.8 1.6 fusion.39
  16.4 31.6 %collective-permute-done.1 = bf16[2048,768]{1,0:T(8,128)(2,1)S(1)} collective-permute-done((bf16[2048,768]{1,0:T(8,128)(2,1)}, bf16[2048,768]{1,0:T(8,128)(2,1)S(1)}, u32[]{:S(2)}, u32[]{:S(2)}) %collective-permute-start.1) | collective-permute-done | bytes 3145760 | tf_op jit(solution)/shard_map/ppermute | solution.py:16
  48.0 1.7 copy-done.6
  49.7 2.6 gather_fusion.1
  52.3 4.3 %gather_fusion = bf16[4,512,768]{2,1,0:T(8,128)(2,1)} fusion(bf16[4,512,768]{2,1,0:T(8,128)(2,1)} %bitcast.2, s32[1024]{0:T(1024)S(1)} %pad_clamp_fusion.1), kind=kCustom, calls=%fused_computation.clone | custom fusion | bytes 6291472 | tf_op jit(solution)/shard_map/jit(_take)/gather | solution.py:50
  56.6 4.6 %fusion.4 = f32[4,768,512]{1,2,0:T(8,128)S(1)} fusion(bf16[4,512,768]{2,1,0:T(8,128)(2,1)} %gather_fusion, pred[4]{0:T(512)(128)(4,1)S(1)} %copy-done.20, bf16[4,2,512,512]{3,2,1,0:T(8,128)(2,1)} %param.9), kind=kOutput, calls=%fused_computation.11 | convolution fusion | flops 1612185600 | bytes 11534340 | tf_op jit(solution)/shard_map/bij,bjd->bid/dot_general | solution.py:53
  61.2 0.1 copy-done.3
  61.4 1.9 fusion.1
  63.5 3.0 %fusion.14 = bf16[256,2048]{0,1:T(8,128)(2,1)S(1)} fusion(bf16[2048,768]{1,0:T(8,128)(2,1)S(1)} %bitcast.71, bf16[256,768]{1,0:T(8,128)(2,1)S(1)} %copy-done, f32[2048]{0:T(1024)S(1)} %copy-done.21, s32[256]{0:T(256)S(1)} %bitcast.81, s32[256]{0:T(256)S(1)} %bitcast.82, s32[256]{0:T(256)S(1)} %bitcast.76, s32[256]{0:T(256)S(1)} %bitcast.77, ...), kind=kOutput, calls=%fused_computation.24 | convolution fusion | flops 817364992 | bytes 4612096 | tf_op jit(solution)/shard_map/qd,ld->ql/dot_general | solution.py:60
  66.5 1.0 multiply_convert_fusion
  67.5 4.5 %convolution_bitcast_fusion = f32[4,512,768]{1,2,0:T(8,128)} fusion(bf16[4,512,768]{2,1,0:T(8,128)(2,1)S(1)} %bitcast.67, bf16[4,2,512,512]{3,2,1,0:T(8,128)(2,1)S(1)} %copy-done.2), kind=kOutput, calls=%fused_computation.19 | convolution fusion | flops 1610612736 | bytes 11534336 | tf_op jit(solution)/shard_map/bji,bjd->bid/dot_general | solution.py:80
  72.0 4.5 %convolution_bitcast_fusion.1 = f32[4,512,768]{1,2,0:T(8,128)} fusion(bf16[4,512,768]{2,1,0:T(8,128)(2,1)S(1)} %bitcast.68, bf16[4,2,512,512]{3,2,1,0:T(8,128)(2,1)S(1)} %copy-done.2), kind=kOutput, calls=%fused_computation.20 | convolution fusion | flops 1610612736 | bytes 11534336 | tf_op jit(solution)/shard_map/bji,bjd->bid/dot_general | solution.py:77
  76.4 7.7 %copy.21 = f32[4,512,768]{2,0,1:T(4,128)} copy(f32[4,512,768]{1,2,0:T(8,128)} %convolution_bitcast_fusion) | data formatting | bytes 12582912 | tf_op jit(solution)/shard_map/bji,bjd->bid/dot_general | solution.py:80
  84.2 8.3 %fusion.33 = bf16[4,512,768]{2,0,1:T(4,128)(2,1)S(1)} fusion(f32[4,512,768]{2,0,1:T(4,128)} %copy.21, s32[4]{0:T(128)S(1)} %copy-done.11), kind=kOutput, calls=%fused_computation.46 | convolution fusion | flops 75497488 | bytes 9437200 | tf_op jit(solution)/shard_map/bj,brd->jrd/dot_general | solution.py:89
  92.4 2.1 copy.29
  94.5 0.3 collective-permute-start.3
  94.8 7.7 %copy.18 = f32[4,512,768]{2,0,1:T(4,128)} copy(f32[4,512,768]{1,2,0:T(8,128)} %convolution_bitcast_fusion.1) | data formatting | bytes 12582912 | tf_op jit(solution)/shard_map/bji,bjd->bid/dot_general | solution.py:77
  102.4 8.3 %fusion.30 = bf16[4,512,768]{2,0,1:T(4,128)(2,1)S(1)} fusion(f32[4,512,768]{2,0,1:T(4,128)} %copy.18, s32[4]{0:T(128)S(1)} %copy-done.9), kind=kOutput, calls=%fused_computation.44 | convolution fusion | flops 75497488 | bytes 9437200 | tf_op jit(solution)/shard_map/bj,brd->jrd/dot_general | solution.py:86
  110.7 2.0 copy.30
  112.8 30.3 %collective-permute-start.2 = (bf16[4,512,768]{2,1,0:T(8,128)(2,1)}, bf16[4,512,768]{2,1,0:T(8,128)(2,1)}, u32[]{:S(2)}, u32[]{:S(2)}) collective-permute-start(bf16[4,512,768]{2,1,0:T(8,128)(2,1)} %copy.30), channel_id=1, source_target_pairs={{15,0},{0,1},{1,2},{2,3},{3,4},{4,5},{5,6},{6,7},{7,8},{8,9},{9,10... | collective-permute-start | bytes 9437192 | tf_op jit(solution)/shard_map/ppermute | solution.py:28
  143.1 1.9 fusion.41
  145.0 0.0 all-reduce.2.cloned.1.call-update
  145.0 106.8 %all-reduce.2.cloned.1.call-done = f32[256,768]{1,0:T(8,128)} async-done(((f32[256,768]{1,0:T(8,128)}), f32[256,768]{1,0:T(8,128)}) %all-reduce.2.cloned.1.call-update) | async-done | bytes 786448 | tf_op jit(solution)/shard_map/psum | solution.py:71
  251.8 2.1 broadcast_multiply_fusion
  253.9 5.7 %add_convert_fusion = bf16[4,512,768]{2,1,0:T(8,128)(2,1)} fusion(bf16[4,512,768]{2,1,0:T(8,128)(2,1)} %collective-permute-done.3, bf16[4,512,768]{2,1,0:T(8,128)(2,1)} %collective-permute-done.2, bf16[4,512,768]{2,1,0:T(8,128)(2,1)S(1)} %bitcast.69), kind=kLoop, calls=%fused_computation.7 | loop fusion | flops 9437184 | bytes 12582912 | tf_op jit(solution)/shard_map/convert_element_type | solution.py:95
  (53 shorter events, 0.1 us)
Async XLA Ops:
  7.2 56.2 %copy-start = (bf16[256,768]{1,0:T(8,128)(2,1)S(1)}, bf16[256,768]{1,0:T(8,128)(2,1)}, u32[]{:S(2)}) copy-start(bf16[256,768]{1,0:T(8,128)(2,1)} %param.12) | copy-start | bytes 1179652
  7.2 244.6 %all-reduce.2.cloned.1.call-start = ((), (), s32[]{:S(2)}) async-start(), calls=%async_computation | async-start | bytes 1572864 | tf_op jit(solution)/shard_map/psum | solution.py:71
  7.2 40.8 %collective-permute-start.1 = (bf16[2048,768]{1,0:T(8,128)(2,1)}, bf16[2048,768]{1,0:T(8,128)(2,1)S(1)}, u32[]{:S(2)}, u32[]{:S(2)}) collective-permute-start(bf16[2048,768]{1,0:T(8,128)(2,1)} %param.8), channel_id=1, source_target_pairs={{0,1},{1,2},{2,3},{3,4},{4,5},{5,6},{6,7},{7,8},{8,9},{9,10},{10,1... | collective-permute-start | bytes 9437192 | tf_op jit(solution)/shard_map/ppermute | solution.py:16
  7.7 44.6 %collective-permute-start = (bf16[2048,768]{1,0:T(8,128)(2,1)}, bf16[2048,768]{1,0:T(8,128)(2,1)}, u32[]{:S(2)}, u32[]{:S(2)}) collective-permute-start(bf16[2048,768]{1,0:T(8,128)(2,1)} %param.8), channel_id=1, source_target_pairs={{1,0},{2,1},{3,2},{4,3},{5,4},{6,5},{7,6},{8,7},{9,8},{10,9},{11,1... | collective-permute-start | bytes 9437192 | tf_op jit(solution)/shard_map/ppermute | solution.py:18
  14.2 33.8 %copy-start.10 = (s32[4]{0:T(128)}, s32[4]{0:T(128)S(1)}, u32[]{:S(2)}) copy-start(s32[4]{0:T(128)S(1)} %get-tuple-element.4) | copy-start | bytes 52
  14.8 33.2 %copy-start.8 = (s32[4]{0:T(128)}, s32[4]{0:T(128)S(1)}, u32[]{:S(2)}) copy-start(s32[4]{0:T(128)S(1)} %get-tuple-element.6) | copy-start | bytes 52
  48.0 1.7 copy-start.6
  52.3 4.3 %copy-start.20 = (pred[4]{0:T(512)(128)(4,1)S(1)}, pred[4]{0:T(512)(128)(4,1)}, u32[]{:S(2)}) copy-start(pred[4]{0:T(512)(128)(4,1)} %get-tuple-element.5) | copy-start | bytes 16
  56.6 4.6 %copy-start.2 = (bf16[4,2,512,512]{3,2,1,0:T(8,128)(2,1)S(1)}, bf16[4,2,512,512]{3,2,1,0:T(8,128)(2,1)}, u32[]{:S(2)}) copy-start(bf16[4,2,512,512]{3,2,1,0:T(8,128)(2,1)} %param.9) | copy-start | bytes 12582916
  56.6 4.7 %copy-start.3 = (bf16[2048,768]{1,0:T(8,128)(2,1)S(1)}, bf16[2048,768]{1,0:T(8,128)(2,1)}, u32[]{:S(2)}) copy-start(bf16[2048,768]{1,0:T(8,128)(2,1)} %param.8) | copy-start | bytes 9437188
  56.6 4.7 %copy-start.7 = (pred[4]{0:T(512)(128)(4,1)S(1)}, pred[4]{0:T(512)(128)(4,1)}, u32[]{:S(2)}) copy-start(pred[4]{0:T(512)(128)(4,1)} %get-tuple-element.3) | copy-start | bytes 16
  61.4 2.0 copy-start.12
  61.4 2.0 copy-start.13
  61.4 2.0 copy-start.14
  61.4 2.1 copy-start.15
  61.4 2.1 copy-start.16
  61.4 2.1 copy-start.17
  61.4 2.1 copy-start.18
  61.4 2.1 copy-start.19
  61.4 2.1 copy-start.21
  63.4 3.1 %copy-start.4 = (bf16[4,512,768]{2,1,0:T(8,128)(2,1)}, bf16[4,512,768]{2,1,0:T(8,128)(2,1)S(1)}, u32[]{:S(2)}) copy-start(bf16[4,512,768]{2,1,0:T(8,128)(2,1)S(1)} %fusion.1) | copy-start | bytes 9437188
  66.5 1.0 copy-start.22
  76.4 7.7 %copy-start.11 = (s32[4]{0:T(128)S(1)}, s32[4]{0:T(128)}, u32[]{:S(2)}) copy-start(s32[4]{0:T(128)} %copy-done.10) | copy-start | bytes 52
  94.5 8.0 %copy-start.9 = (s32[4]{0:T(128)S(1)}, s32[4]{0:T(128)}, u32[]{:S(2)}) copy-start(s32[4]{0:T(128)} %copy-done.8) | copy-start | bytes 52
  94.5 159.4 %collective-permute-start.3 = (bf16[4,512,768]{2,1,0:T(8,128)(2,1)}, bf16[4,512,768]{2,1,0:T(8,128)(2,1)}, u32[]{:S(2)}, u32[]{:S(2)}) collective-permute-start(bf16[4,512,768]{2,1,0:T(8,128)(2,1)} %copy.29), channel_id=1, source_target_pairs={{1,0},{2,1},{3,2},{4,3},{5,4},{6,5},{7,6},{8,7},{9,8},{10,9},{11,1... | collective-permute-start | bytes 9437192 | tf_op jit(solution)/shard_map/ppermute | solution.py:28
  110.7 32.4 %copy-start.5 = (bf16[4,512,768]{2,1,0:T(8,128)(2,1)S(1)}, bf16[4,512,768]{2,1,0:T(8,128)(2,1)}, u32[]{:S(2)}) copy-start(bf16[4,512,768]{2,1,0:T(8,128)(2,1)} %copy-done.4) | copy-start | bytes 9437188
  110.7 32.4 %copy-start.23 = (bf16[256,2048]{0,1:T(8,128)(2,1)S(1)}, bf16[256,2048]{0,1:T(8,128)(2,1)}, u32[]{:S(2)}) copy-start(bf16[256,2048]{0,1:T(8,128)(2,1)} %copy-done.22) | copy-start | bytes 3145732
  112.8 141.1 %collective-permute-start.2 = (bf16[4,512,768]{2,1,0:T(8,128)(2,1)}, bf16[4,512,768]{2,1,0:T(8,128)(2,1)}, u32[]{:S(2)}, u32[]{:S(2)}) collective-permute-start(bf16[4,512,768]{2,1,0:T(8,128)(2,1)} %copy.30), channel_id=1, source_target_pairs={{15,0},{0,1},{1,2},{2,3},{3,4},{4,5},{5,6},{6,7},{7,8},{8,9},{9,10... | collective-permute-start | bytes 9437192 | tf_op jit(solution)/shard_map/ppermute | solution.py:28
  253.9 5.7 %copy-start.1 = (bf16[256,768]{1,0:T(8,128)(2,1)S(1)}, bf16[256,768]{1,0:T(8,128)(2,1)}, u32[]{:S(2)}) copy-start(bf16[256,768]{1,0:T(8,128)(2,1)} %param.12) | copy-start | bytes 1179652
Sparse Core Ops, SparseCore 0:
  145.1 106.6 all-reduce.1
where the time goes:
time: 267 us; the launch traced here: 266 us
  waiting for transfers between devices  138 us (52%)
  matrix products  37.8 us (14%)
  starting transfers between devices  36.2 us (14%)
  local copies, waits for them, and re-layouts  30.7 us (11%)
  between operations  14.3 us (5%)
  other arithmetic  9.08 us (3%)
    psum x1, waiting for transfers between devices, per_device(): lax.psum(partial_query, 'labels') / math.sqrt(labels_dev * count)  107 us
    ppermute x1, waiting for transfers between devices, with_halo(): lax.ppermute(tail, axis, [(i, (i + 1) % count) for i in range(count)])  31.6 us
    ppermute x2, starting transfers between devices, from_behind(): return lax.ppermute(block, axis, route)  30.6 us
    dot_general x1, matrix products, per_device(): jnp.einsum('bj,brd->jrd', pick_next, push_next, precision=lax.Precision.H...  8.26 us
    dot_general x1, matrix products, per_device(): jnp.einsum('bj,brd->jrd', pick_prev, push_prev, precision=lax.Precision.H...  8.26 us
    dot_general x1, local copies, waits for them, and re-layouts, per_device(): jnp.einsum('bji,bjd->bid', edge_tiles[:, 1], back_blocks, preferred_eleme...  7.74 us
    dot_general x1, local copies, waits for them, and re-layouts, per_device(): jnp.einsum('bji,bjd->bid', edge_tiles[:, 0], back_blocks, preferred_eleme...  7.68 us
    convert_element_type x1, other arithmetic, per_device(): grad_embed = total.astype(jnp.bfloat16).reshape(labels_dev, width)  5.73 us
  transfers between devices with their start and end apart: 5, of which 2 were waited for; matrix products, arithmetic and copies ran while one was open for 11% of the time, Pallas kernels for 0%

commit v1 on v0

v1 whole, which is shorter than its diff:
```python
import functools
import math

import jax
import jax.numpy as jnp
from jax import lax
from jax.experimental import pallas as pl
from jax.experimental.pallas import tpu as pltpu
from jax.sharding import PartitionSpec as P

BF16 = jnp.bfloat16
F32 = jnp.float32
NT = (((1,), (1,)), ((), ()))
NN = (((1,), (0,)), ((), ()))
TN = (((0,), (0,)), ((), ()))
VMEM_BYTES = 48 * 1024 * 1024

NEXT_SLOT, PREV_SLOT, FOR_PREV, FOR_NEXT, CORE = 0, 4, 8, 10, 12


def dot(a, b, dims):
    return lax.dot_general(a, b, dims, preferred_element_type=F32)


def index_table(neighbour, device, count, blocks_dev):
    def lists(shard, side):
        column = neighbour[:, side]
        return lax.dynamic_slice_in_dim(column, shard * blocks_dev, blocks_dev, 0)

    own_next = lists(device, 0)
    own_prev = lists(device, 1)
    by_prev = lists((device + count - 1) % count, 0)
    by_next = lists((device + 1) % count, 1)
    return jnp.concatenate(
        [
            (own_next != jnp.min(own_next)).astype(jnp.int32),
            (own_prev != jnp.min(own_prev)).astype(jnp.int32),
            jnp.stack(
                [
                    jnp.min(by_prev),
                    jnp.max(by_prev),
                    jnp.min(by_next),
                    jnp.max(by_next),
                    device % 2,
                ]
            ),
        ]
    )


def project_kernel(table, queries, embeddings, own, for_prev, for_next, *, scale):
    c = pl.program_id(0)
    scores = dot(queries[...], embeddings[...], NT) * scale
    own[...] = scores
    rounded = scores.astype(BF16)
    for slot in range(2):

        @pl.when(table[FOR_PREV + slot] == c)
        def _():
            for_prev[slot] = rounded

        @pl.when(table[FOR_NEXT + slot] == c)
        def _():
            for_next[slot] = rounded


def signal_kernel(
    table, own, from_next, from_prev, tiles, positives, propensity, signal, to_next, to_prev, sum_next, sum_prev
):
    g = pl.program_id(0)
    block = own.shape[1]

    @pl.when(g == 0)
    def _():
        sum_next[...] = jnp.zeros_like(sum_next)
        sum_prev[...] = jnp.zeros_like(sum_prev)

    slot0 = table[NEXT_SLOT + g]
    slot1 = table[PREV_SLOT + g]
    scores = own[...] + dot(from_next[slot0], tiles[0, 0], NT) + dot(from_prev[slot1], tiles[0, 1], NT)
    first = table[CORE + 1] + g * block
    ids = lax.broadcasted_iota(jnp.int32, own.shape, 1)
    hits = jnp.zeros(own.shape, jnp.bool_)
    for column in range(positives.shape[1]):
        hits = jnp.logical_or(hits, ids == positives[:, column : column + 1] - first)
    inverse = 1.0 / propensity[...]
    value = jax.nn.sigmoid(scores) - jnp.where(hits, inverse, 0.0)
    value = value.astype(BF16)
    signal[...] = value
    sum_next[slot0] += dot(value, tiles[0, 0], NN)
    sum_prev[slot1] += dot(value, tiles[0, 1], NN)

    @pl.when(g == pl.num_programs(0) - 1)
    def _():
        to_next[...] = sum_next[...].astype(BF16)
        to_prev[...] = sum_prev[...].astype(BF16)


def gather_kernel(table, signal, before, after, embeddings, weight, kept, sent, total):
    c = pl.program_id(0)

    def carried(received, place):
        slot = (table[place + 1] == c).astype(jnp.int32)
        named = jnp.logical_or(table[place] == c, table[place + 1] == c)
        return jnp.where(named, received[slot].astype(F32), 0.0)

    value = signal[...].astype(F32) + carried(before, FOR_PREV) + carried(after, FOR_NEXT)
    value = value.astype(BF16)
    weight[...] = value
    part = dot(value, embeddings[...], NN)

    @pl.when(c == 0)
    def _():
        total[...] = part

    @pl.when(c != 0)
    def _():
        total[...] += part

    @pl.when(c == pl.num_programs(0) - 1)
    def _():
        rows = kept.shape[0]
        core = table[CORE]
        kept[...] = total[pl.ds(pl.multiple_of(core * rows, rows), rows), :]
        sent[...] = total[pl.ds(pl.multiple_of((1 - core) * rows, rows), rows), :]


def embed_kernel(weight, queries, out, *, scale):
    out[...] = (dot(weight[...], queries[...], TN) * scale).astype(BF16)


def whole(shape):
    return pl.BlockSpec(shape, lambda *_: (0,) * len(shape))


def call(kernel, name, grid, in_specs, out_specs, out_shape, scratch, prefetch, cost):
    return pl.pallas_call(
        kernel,
        grid_spec=pltpu.PrefetchScalarGridSpec(
            num_scalar_prefetch=prefetch,
            grid=grid,
            in_specs=in_specs,
            out_specs=out_specs,
            scratch_shapes=scratch,
        ),
        out_shape=out_shape,
        name=name,
        cost_estimate=pl.CostEstimate(flops=cost[0], bytes_accessed=cost[1], transcendentals=0),
        compiler_params=pltpu.CompilerParams(vmem_limit_bytes=VMEM_BYTES),
    )


def reduce_rows(kept, sent, scale):
    count = lax.axis_size("labels")
    chips = count // 2
    core = lax.axis_index("labels") % 2
    swap = [(i, i ^ 1) for i in range(count)]
    groups = [list(range(0, count, 2)), list(range(1, count, 2))]
    rows, width = kept.shape
    half = (kept + lax.ppermute(sent, "labels", swap)).astype(BF16)
    pieces = half.reshape(chips, rows // chips, width)
    pieces = lax.all_to_all(pieces, "labels", 0, 0, axis_index_groups=groups)
    total = (jnp.sum(pieces.astype(F32), axis=0) * scale).astype(BF16)
    spread = jnp.broadcast_to(total[None], pieces.shape)
    spread = lax.all_to_all(spread, "labels", 0, 0, axis_index_groups=groups)
    mine = spread.reshape(rows, width)
    other = lax.ppermute(mine, "labels", swap)
    first = jnp.where(core == 0, mine, other)
    second = jnp.where(core == 0, other, mine)
    return jnp.concatenate([first, second], axis=0).astype(F32)


def per_device(embeddings, edge_tiles, neighbour, propensity, queries, positives):
    count = lax.axis_size("labels")
    device = lax.axis_index("labels")
    blocks_dev, _, block, _ = edge_tiles.shape
    labels_dev, width = embeddings.shape
    rows = queries.shape[0]
    ahead = [(i, (i + 1) % count) for i in range(count)]
    behind = [((i + 1) % count, i) for i in range(count)]
    table = index_table(neighbour, device, count, blocks_dev)
    table = jnp.concatenate([table, (device * labels_dev).astype(jnp.int32)[None]])
    pair = jax.ShapeDtypeStruct((2, rows, block), BF16)
    by_columns = pl.BlockSpec((rows, block), lambda g, *_: (0, g))
    by_rows = pl.BlockSpec((block, width), lambda g, *_: (g, 0))
    product = 2 * rows * labels_dev * width
    mixing = 2 * rows * labels_dev * block

    own, for_prev, for_next = call(
        functools.partial(project_kernel, scale=1.0 / math.sqrt(width)),
        "project",
        (blocks_dev,),
        [whole((rows, width)), by_rows],
        [by_columns, whole(pair.shape), whole(pair.shape)],
        [jax.ShapeDtypeStruct((rows, labels_dev), F32), pair, pair],
        [],
        1,
        (product, 2 * labels_dev * width + 4 * rows * labels_dev),
    )(table, queries, embeddings)

    from_next = lax.ppermute(for_prev, "labels", behind)
    from_prev = lax.ppermute(for_next, "labels", ahead)

    signal, to_next, to_prev = call(
        signal_kernel,
        "signal",
        (blocks_dev,),
        [
            by_columns,
            whole(pair.shape),
            whole(pair.shape),
            pl.BlockSpec((1, 2, block, block), lambda g, *_: (g, 0, 0, 0)),
            whole(positives.shape),
            pl.BlockSpec((1, block), lambda g, *_: (0, g)),
        ],
        [by_columns, whole(pair.shape), whole(pair.shape)],
        [jax.ShapeDtypeStruct((rows, labels_dev), BF16), pair, pair],
        [pltpu.VMEM((2, rows, block), F32), pltpu.VMEM((2, rows, block), F32)],
        1,
        (4 * mixing, 4 * labels_dev * block + 6 * rows * labels_dev),
    )(table, own, from_next, from_prev, edge_tiles, positives, propensity.reshape(1, labels_dev))

    before = lax.ppermute(to_next, "labels", ahead)
    after = lax.ppermute(to_prev, "labels", behind)

    weight, kept, sent = call(
        gather_kernel,
        "gather",
        (blocks_dev,),
        [by_columns, whole(pair.shape), whole(pair.shape), by_rows],
        [by_columns, whole((rows // 2, width)), whole((rows // 2, width))],
        [jax.ShapeDtypeStruct((rows, labels_dev), BF16)]
        + [jax.ShapeDtypeStruct((rows // 2, width), F32)] * 2,
        [pltpu.VMEM((rows, width), F32)],
        1,
        (product, 2 * labels_dev * width + 4 * rows * labels_dev),
    )(table, signal, before, after, embeddings)

    grad_queries = reduce_rows(kept, sent, 1.0 / math.sqrt(labels_dev * count))

    grad_embed = call(
        functools.partial(embed_kernel, scale=1.0 / math.sqrt(rows)),
        "embed",
        (blocks_dev,),
        [by_columns, whole((rows, width))],
        by_rows,
        jax.ShapeDtypeStruct((labels_dev, width), BF16),
        [],
        0,
        (product, 2 * labels_dev * width + 2 * rows * labels_dev),
    )(weight, queries)
    return (grad_embed, grad_queries)


def solution(mesh):
    placed = (
        P("labels", None),
        P("labels", None, None, None),
        P(),
        P("labels"),
        P("groups", None),
        P("groups", None),
    )
    return jax.shard_map(
        per_device,
        mesh=mesh,
        in_specs=placed,
        out_specs=(P(("groups", "labels"), None), P("groups", None)),
        check_vma=False,
    )
```

time: 267 us -> 87 us (0.33)
  waiting for transfers between devices: 138 us -> 19.7 us
  matrix products: 37.8 us -> 0 us
  local copies, waits for them, and re-layouts: 30.7 us -> 4.54 us
  blocking collectives: 0 us -> 23.4 us
  starting transfers between devices: 36.2 us -> 13.4 us
  Pallas kernels: 0 us -> 20.8 us
  between operations: 14.3 us -> 0.75 us
  other arithmetic: 9.08 us -> 3.87 us
    psum x1 -> x0, waiting for transfers between devices: 107 us -> none  [per_device(): lax.psum(partial_query, 'labels') / math.sqrt(labels_dev * count)]
    dot_general x9 -> x0, matrix products: 37.8 us -> none  [the longest x1 8.26 us: per_device(): jnp.einsum('bj,brd->jrd', pick_next, push_next, precision=lax.Precision.H...]
    all_to_all x0 -> x2, blocking collectives: none -> 23.4 us  [the longest x1 12.6 us: reduce_rows(): pieces = lax.all_to_all(pieces, 'labels', 0, 0, axis_index_groups=groups)]
    ppermute x4 -> x6, starting transfers between devices: 36.2 us -> 13.4 us  [the longest x1 5.43 us: per_device(): from_next = lax.ppermute(for_prev, 'labels', behind)]
    pallas_call x0 -> x4, Pallas kernels: none -> 20.8 us  [the longest x1 7.88 us: per_device(): call(signal_kernel, 'signal', (blocks_dev,), [by_columns, whole(pair.shap...]
    dot_general x4 -> x0, local copies, waits for them, and re-layouts: 19.5 us -> none  [the longest x1 7.74 us: per_device(): jnp.einsum('bji,bjd->bid', edge_tiles[:, 1], back_blocks, preferred_eleme...]
    ppermute x4 -> x6, waiting for transfers between devices: 31.6 us -> 19.7 us  [the longest x1 6.96 us: per_device(): before = lax.ppermute(to_next, 'labels', ahead)]
    gather x2 -> x0, local copies, waits for them, and re-layouts: 6.94 us -> none  [the longest x1 4.3 us: per_device(): from_next = jnp.take(next_shard, own_next, axis=0)]
  transfers between devices with their start and end apart: 5 -> 6, of which waited for: 2 -> 4; matrix products, arithmetic and copies ran while one was open for 11% -> 0% of each run, Pallas kernels for 0% -> 4%
where the time goes in v1:
time: 87 us; the launch traced here: 86.4 us
  blocking collectives  23.4 us (27%)
  Pallas kernels  20.8 us (24%)
  waiting for transfers between devices  19.7 us (23%)
  starting transfers between devices  13.4 us (15%)
  local copies, waits for them, and re-layouts  4.54 us (5%)
  other arithmetic  3.87 us (4%)
    all_to_all x1, blocking collectives, reduce_rows(): pieces = lax.all_to_all(pieces, 'labels', 0, 0, axis_index_groups=groups)  12.6 us
    all_to_all x1, blocking collectives, reduce_rows(): spread = lax.all_to_all(spread, 'labels', 0, 0, axis_index_groups=groups)  10.7 us
    pallas_call x1, Pallas kernels, per_device(): call(signal_kernel, 'signal', (blocks_dev,), [by_columns, whole(pair.shap...  7.88 us
    ppermute x1, waiting for transfers between devices, per_device(): before = lax.ppermute(to_next, 'labels', ahead)  6.96 us
    ppermute x1, waiting for transfers between devices, per_device(): from_next = lax.ppermute(for_prev, 'labels', behind)  6.88 us
    ppermute x1, starting transfers between devices, per_device(): from_next = lax.ppermute(for_prev, 'labels', behind)  5.43 us
    pallas_call x1, Pallas kernels, per_device(): call(functools.partial(project_kernel, scale=1.0 / math.sqrt(width)), 'pr...  5.34 us
    pallas_call x1, Pallas kernels, per_device(): call(gather_kernel, 'gather', (blocks_dev,), [by_columns, whole(pair.shap...  4.54 us
  transfers between devices with their start and end apart: 6, of which 4 were waited for; matrix products, arithmetic and copies ran while one was open for 0% of the time, Pallas kernels for 4%

profile of v1, /device:TPU:0, one launch (start us, length us, event | category | flops | bytes accessed | tf_op | source)
XLA Modules:
  0.0 86.4 jit_solution(7808159014734480246)
XLA Ops:
  0.6 0.0 copy-start.3
  0.6 0.0 copy-start.2
  0.7 0.8 fusion.8
  1.4 0.8 fusion.6
  2.2 0.7 fusion.4
  3.0 1.3 %fusion = (s32[4]{0:T(128)S(1)}, s32[4]{0:T(128)S(1)}) fusion(s32[]{:T(128)} %get-tuple-element.25, s32[64,1]{0,1:T(1,128)S(1)} %get-tuple-element.29, s32[]{:T(128)S(6)} %select_n.39, s32[]{:T(128)} %get-tuple-element.22, s32[64,1]{0,1:T(1,128)S(1)} %get-tuple-element.28), kind=kLoop, calls=%fused_computation.12 | loop fusion | flops 16 | bytes 76 | tf_op jit(solution)/shard_map/convert_element_type | solution.py:36
  4.3 2.6 %concatenate.6.table = s32[14]{0:T(128)S(1)} concatenate(s32[4]{0:T(128)S(1)} %get-tuple-element.30, s32[4]{0:T(128)S(1)} %get-tuple-element.31, s32[1]{0:T(128)} %bitcast.2, s32[1]{0:T(128)} %bitcast.3, s32[1]{0:T(128)} %bitcast.4, s32[1]{0:T(128)} %bitcast.5, s32[1]{0:T(128)} %bitcast.6, s32[1]{0:T(128)} %bitcast.7), dimensions={0} | concatenate | bytes 112 | tf_op jit(solution)/shard_map/concatenate | solution.py:182
  6.9 0.0 copy-start
  6.9 1.0 %copy-done = bf16[256,768]{1,0:T(8,128)(2,1)S(1)} copy-done((bf16[256,768]{1,0:T(8,128)(2,1)S(1)}, bf16[256,768]{1,0:T(8,128)(2,1)}, u32[]{:S(2)}) %copy-start) | copy-done | bytes 393240
  7.9 5.3 %project.1 = (f32[256,2048]{1,0:T(8,128)S(1)}, bf16[2,256,512]{2,1,0:T(8,128)(2,1)}, bf16[2,256,512]{2,1,0:T(8,128)(2,1)}) custom-call(s32[14]{0:T(128)S(1)} %concatenate.6.table, bf16[256,768]{1,0:T(8,128)(2,1)S(1)} %copy-done, bf16[2048,768]{1,0:T(8,128)(2,1)} %embeddings.3), custom_call_target="tpu_custom_call" | custom-call | flops 805306368 | bytes 5242880 | tf_op jit(solution)/shard_map/project/pallas_call | solution.py:189
  13.2 5.4 %collective-permute-start = (bf16[2,256,512]{2,1,0:T(8,128)(2,1)}, bf16[2,256,512]{2,1,0:T(8,128)(2,1)S(1)}, u32[]{:S(2)}, u32[]{:S(2)}) collective-permute-start(bf16[2,256,512]{2,1,0:T(8,128)(2,1)} %get-tuple-element.12), channel_id=1, source_target_pairs={{1,0},{2,1},{3,2},{4,3},{5,4},{6,5},{7,6},{8,7},{9,8},{10,9},{11,1... | collective-permute-start | bytes 1572872 | tf_op jit(solution)/shard_map/ppermute | solution.py:201
  18.7 0.0 collective-permute-start.1
  18.7 0.0 copy-done.3
  18.7 0.1 copy.8.positives
  18.8 6.9 %collective-permute-done.from_next = bf16[2,256,512]{2,1,0:T(8,128)(2,1)S(1)} collective-permute-done((bf16[2,256,512]{2,1,0:T(8,128)(2,1)}, bf16[2,256,512]{2,1,0:T(8,128)(2,1)S(1)}, u32[]{:S(2)}, u32[]{:S(2)}) %collective-permute-start) | collective-permute-done | bytes 524320 | tf_op jit(solution)/shard_map/ppermute | solution.py:201
  25.7 4.5 %collective-permute-done.1.from_prev = bf16[2,256,512]{2,1,0:T(8,128)(2,1)S(1)} collective-permute-done((bf16[2,256,512]{2,1,0:T(8,128)(2,1)}, bf16[2,256,512]{2,1,0:T(8,128)(2,1)S(1)}, u32[]{:S(2)}, u32[]{:S(2)}) %collective-permute-start.1) | collective-permute-done | bytes 524320 | tf_op jit(solution)/shard_map/ppermute | solution.py:202
  30.2 0.0 copy-done.2
  30.2 7.9 %signal.1 = (bf16[256,2048]{1,0:T(8,128)(2,1)S(1)}, bf16[2,256,512]{2,1,0:T(8,128)(2,1)S(1)}, bf16[2,256,512]{2,1,0:T(8,128)(2,1)S(1)}) custom-call(s32[14]{0:T(128)S(1)} %concatenate.6.table, f32[256,2048]{1,0:T(8,128)S(1)} %get-tuple-element.11.own, bf16[2,256,512]{2,1,0:T(8,128)(2,1)S(1)} %collective-permute-done.from_next, ...), custom_call_target="tpu_custom_call" | custom-call | flops 2147483648 | bytes 7340032 | tf_op jit(solution)/shard_map/signal/pallas_call | solution.py:204
  38.1 0.1 collective-permute-start.2
  38.1 4.4 %collective-permute-start.3 = (bf16[2,256,512]{2,1,0:T(8,128)(2,1)S(1)}, bf16[2,256,512]{2,1,0:T(8,128)(2,1)S(1)}, u32[]{:S(2)}, u32[]{:S(2)}) collective-permute-start(bf16[2,256,512]{2,1,0:T(8,128)(2,1)S(1)} %get-tuple-element.16), channel_id=1, source_target_pairs={{1,0},{2,1},{3,2},{4,3},{5,4},{6,5},{7,6},{8,7},{9,8},{10,9},{11,1... | collective-permute-start | bytes 1572872 | tf_op jit(solution)/shard_map/ppermute | solution.py:224
  42.6 7.0 %collective-permute-done.2.before = bf16[2,256,512]{2,1,0:T(8,128)(2,1)S(1)} collective-permute-done((bf16[2,256,512]{2,1,0:T(8,128)(2,1)S(1)}, bf16[2,256,512]{2,1,0:T(8,128)(2,1)S(1)}, u32[]{:S(2)}, u32[]{:S(2)}) %collective-permute-start.2) | collective-permute-done | bytes 524320 | tf_op jit(solution)/shard_map/ppermute | solution.py:223
  49.5 0.0 collective-permute-done.3.after
  49.5 4.5 %gather.1 = (bf16[256,2048]{1,0:T(8,128)(2,1)S(1)}, f32[128,768]{1,0:T(8,128)S(1)}, f32[128,768]{1,0:T(8,128)S(1)}) custom-call(s32[14]{0:T(128)S(1)} %concatenate.6.table, bf16[256,2048]{1,0:T(8,128)(2,1)S(1)} %get-tuple-element.14.signal, bf16[2,256,512]{2,1,0:T(8,128)(2,1)S(1)} %collective-permute-done.2.before, ...), custom_call_target="tpu_custom_call" | custom-call | flops 805306368 | bytes 5242880 | tf_op jit(solution)/shard_map/gather/pallas_call | solution.py:226
  54.1 3.4 %collective-permute-start.4 = (f32[128,768]{1,0:T(8,128)S(1)}, f32[128,768]{1,0:T(8,128)S(1)}, u32[]{:S(2)}, u32[]{:S(2)}) collective-permute-start(f32[128,768]{1,0:T(8,128)S(1)} %get-tuple-element.19), channel_id=1, source_target_pairs={{0,1},{1,0},{2,3},{3,2},{4,5},{5,4},{6,7},{7,6},{8,9},{9,8},{10,11... | collective-permute-start | bytes 1179656 | tf_op jit(solution)/shard_map/ppermute | solution.py:160
  57.5 1.3 %collective-permute-done.4 = f32[128,768]{1,0:T(8,128)S(1)} collective-permute-done((f32[128,768]{1,0:T(8,128)S(1)}, f32[128,768]{1,0:T(8,128)S(1)}, u32[]{:S(2)}, u32[]{:S(2)}) %collective-permute-start.4) | collective-permute-done | bytes 393248 | tf_op jit(solution)/shard_map/ppermute | solution.py:160
  58.9 12.6 %all_to_all.10 = bf16[8,16,768]{2,1,0:T(8,128)(2,1)S(1)} all-to-all(bf16[8,16,768]{2,1,0:T(8,128)(2,1)S(1)} %bitcast.17), channel_id=1, replica_groups={{0,2,4,6,8,10,12,14},{1,3,5,7,9,11,13,15},{16,18,20,22,24,26,28,30},{17..., dimensions={0} | all-to-all | bytes 393216 | tf_op jit(solution)/shard_map/all_to_all | solution.py:162
  71.7 10.7 %all_to_all.11 = bf16[8,16,768]{2,1,0:T(8,128)(2,1)S(1)} all-to-all(bf16[8,16,768]{2,1,0:T(8,128)(2,1)S(1)} %broadcast_in_dim.10), channel_id=1, replica_groups={{0,2,4,6,8,10,12,14},{1,3,5,7,9,11,13,15},{16,18,20,22,24,26,28,30},{17..., dimensions={0} | all-to-all | bytes 393216 | tf_op jit(solution)/shard_map/all_to_all | solution.py:165
  82.4 0.0 collective-permute-start.5
  82.4 0.0 copy-done.1
  82.4 3.1 %embed.1 = bf16[2048,768]{1,0:T(8,128)(2,1)} custom-call(bf16[256,2048]{1,0:T(8,128)(2,1)S(1)} %get-tuple-element.17.weight, bf16[256,768]{1,0:T(8,128)(2,1)S(1)} %copy-done.1), custom_call_target="tpu_custom_call" | custom-call | flops 805306368 | bytes 4194304 | tf_op jit(solution)/shard_map/embed/pallas_call | solution.py:241
  85.5 0.0 collective-permute-done.5
  85.5 0.9 %maximum_convert_fusion = f32[256,768]{1,0:T(8,128)} fusion(bf16[128,768]{1,0:T(8,128)(2,1)S(1)} %get-tuple-element.27, bf16[128,768]{1,0:T(8,128)(2,1)S(1)} %get-tuple-element.26), kind=kLoop, calls=%fused_computation | loop fusion | flops 786432 | bytes 1179648 | tf_op jit(solution)/shard_map/convert_element_type | solution.py:170
  (6 shorter events, 0.1 us)
Async XLA Ops:
  0.6 18.0 %copy-start.3 = (s32[256,8]{0,1:T(8,128)S(1)}, s32[256,8]{0,1:T(8,128)}, u32[]{:S(2)}) copy-start(s32[256,8]{0,1:T(8,128)} %param.11) | copy-start | bytes 24580
  0.6 29.5 %copy-start.2 = (f32[2048]{0:T(1024)S(1)}, f32[2048]{0:T(1024)}, u32[]{:S(2)}) copy-start(f32[2048]{0:T(1024)} %param.9) | copy-start | bytes 24580
  6.9 1.0 %copy-start = (bf16[256,768]{1,0:T(8,128)(2,1)S(1)}, bf16[256,768]{1,0:T(8,128)(2,1)}, u32[]{:S(2)}) copy-start(bf16[256,768]{1,0:T(8,128)(2,1)} %queries.3) | copy-start | bytes 1179652
  13.2 12.4 %collective-permute-start = (bf16[2,256,512]{2,1,0:T(8,128)(2,1)}, bf16[2,256,512]{2,1,0:T(8,128)(2,1)S(1)}, u32[]{:S(2)}, u32[]{:S(2)}) collective-permute-start(bf16[2,256,512]{2,1,0:T(8,128)(2,1)} %get-tuple-element.12), channel_id=1, source_target_pairs={{1,0},{2,1},{3,2},{4,3},{5,4},{6,5},{7,6},{8,7},{9,8},{10,9},{11,1... | collective-permute-start | bytes 1572872 | tf_op jit(solution)/shard_map/ppermute | solution.py:201
  18.7 11.5 %collective-permute-start.1 = (bf16[2,256,512]{2,1,0:T(8,128)(2,1)}, bf16[2,256,512]{2,1,0:T(8,128)(2,1)S(1)}, u32[]{:S(2)}, u32[]{:S(2)}) collective-permute-start(bf16[2,256,512]{2,1,0:T(8,128)(2,1)} %get-tuple-element.13), channel_id=1, source_target_pairs={{0,1},{1,2},{2,3},{3,4},{4,5},{5,6},{6,7},{7,8},{8,9},{9,10},{10,1... | collective-permute-start | bytes 1572872 | tf_op jit(solution)/shard_map/ppermute | solution.py:202
  38.1 11.5 %collective-permute-start.2 = (bf16[2,256,512]{2,1,0:T(8,128)(2,1)S(1)}, bf16[2,256,512]{2,1,0:T(8,128)(2,1)S(1)}, u32[]{:S(2)}, u32[]{:S(2)}) collective-permute-start(bf16[2,256,512]{2,1,0:T(8,128)(2,1)S(1)} %get-tuple-element.15), channel_id=1, source_target_pairs={{0,1},{1,2},{2,3},{3,4},{4,5},{5,6},{6,7},{7,8},{8,9},{9,10},{10,1... | collective-permute-start | bytes 1572872 | tf_op jit(solution)/shard_map/ppermute | solution.py:223
  38.1 11.4 %collective-permute-start.3 = (bf16[2,256,512]{2,1,0:T(8,128)(2,1)S(1)}, bf16[2,256,512]{2,1,0:T(8,128)(2,1)S(1)}, u32[]{:S(2)}, u32[]{:S(2)}) collective-permute-start(bf16[2,256,512]{2,1,0:T(8,128)(2,1)S(1)} %get-tuple-element.16), channel_id=1, source_target_pairs={{1,0},{2,1},{3,2},{4,3},{5,4},{6,5},{7,6},{8,7},{9,8},{10,9},{11,1... | collective-permute-start | bytes 1572872 | tf_op jit(solution)/shard_map/ppermute | solution.py:224
  49.5 32.9 %copy-start.1 = (bf16[256,768]{1,0:T(8,128)(2,1)S(1)}, bf16[256,768]{1,0:T(8,128)(2,1)}, u32[]{:S(2)}) copy-start(bf16[256,768]{1,0:T(8,128)(2,1)} %queries.3) | copy-start | bytes 1179652
  54.1 4.8 %collective-permute-start.4 = (f32[128,768]{1,0:T(8,128)S(1)}, f32[128,768]{1,0:T(8,128)S(1)}, u32[]{:S(2)}, u32[]{:S(2)}) collective-permute-start(f32[128,768]{1,0:T(8,128)S(1)} %get-tuple-element.19), channel_id=1, source_target_pairs={{0,1},{1,0},{2,3},{3,2},{4,5},{5,4},{6,7},{7,6},{8,9},{9,8},{10,11... | collective-permute-start | bytes 1179656 | tf_op jit(solution)/shard_map/ppermute | solution.py:160
  82.4 3.1 %collective-permute-start.5 = (bf16[128,768]{1,0:T(8,128)(2,1)S(1)}, bf16[128,768]{1,0:T(8,128)(2,1)S(1)}, u32[]{:S(2)}, u32[]{:S(2)}) collective-permute-start(bf16[128,768]{1,0:T(8,128)(2,1)S(1)} %bitcast.16), channel_id=1, source_target_pairs={{0,1},{1,0},{2,3},{3,2},{4,5},{5,4},{6,7},{7,6},{8,9},{9,8},{10,11... | collective-permute-start | bytes 589832 | tf_op jit(solution)/shard_map/ppermute | solution.py:167

commit v2 on v0

v2 whole, which is shorter than its diff:
```python
import functools
import math

import jax
import jax.numpy as jnp
from jax import lax
from jax.experimental import pallas as pl
from jax.experimental.pallas import tpu as pltpu
from jax.sharding import PartitionSpec as P

AXIS = "labels"
BF16 = jnp.bfloat16
F32 = jnp.float32
NT = (((1,), (1,)), ((), ()))
NN = (((1,), (0,)), ((), ()))
TN = (((0,), (0,)), ((), ()))
VMEM_BYTES = 16 * 1024 * 1024

OFF, ON = True, False


def dot(a, b, dims):
    return lax.dot_general(a, b, dims, preferred_element_type=F32)


def own_side(device, off):
    odd = device % 2
    return 1 - odd if off else odd


def partner_of(device, count, off):
    ahead = jnp.where(device == count - 1, 0, device + 1)
    behind = jnp.where(device == 0, count - 1, device - 1)
    return jnp.where(own_side(device, off) == 0, ahead, behind)


def own_list(lists, blocks, off):
    device = lax.axis_index(AXIS)
    side = own_side(device, off)
    return [lists[side, device * blocks + g] for g in range(blocks)]


def slots_of(lists, blocks, off):
    named = own_list(lists, blocks, off)
    least = functools.reduce(jnp.minimum, named)
    return [(value != least).astype(jnp.int32) for value in named]


def named_by_partner(lists, blocks, off):
    device = lax.axis_index(AXIS)
    partner = partner_of(device, lax.axis_size(AXIS), off)
    side = 1 - own_side(device, off)
    named = [lists[side, partner * blocks + g] for g in range(blocks)]
    return functools.reduce(jnp.minimum, named), functools.reduce(jnp.maximum, named)


def tile_side(off):
    return own_side(lax.axis_index(AXIS), off)


def block_rows(ref, index, block):
    return ref[pl.ds(pl.multiple_of(index * block, block), block), :]


def project_kernel(lists, queries, embeddings, *rest, off, scale):
    out, table, left, right, sem = rest[-5:]
    block = out.shape[2]
    blocks = embeddings.shape[0] // block
    fetches = [pltpu.make_async_copy(lists, table, sem.at[0]), pltpu.make_async_copy(queries, left, sem.at[1])]
    for g in range(blocks):
        fetches.append(pltpu.make_async_copy(embeddings.at[pl.ds(g * block, block), :], right.at[g], sem.at[2 + g]))
    for fetch in fetches:
        fetch.start()
    for fetch in fetches:
        fetch.wait()
    for slot, index in enumerate(named_by_partner(table, blocks, off)):
        out[slot] = (dot(left[...], right[index], NT) * scale).astype(BF16)


def hits_kernel(positives, propensity, out):
    blocks, rows, block = out.shape
    first = lax.axis_index(AXIS) * blocks * block
    ids = lax.broadcasted_iota(jnp.int32, (rows, block), 1)
    inverse = 1.0 / propensity[...]
    for g in range(blocks):
        hits = jnp.zeros((rows, block), jnp.bool_)
        for column in range(positives.shape[1]):
            hits = jnp.logical_or(hits, ids == positives[:, column : column + 1] - (first + g * block))
        out[g] = jnp.where(hits, inverse[:, g * block : (g + 1) * block], 0.0)


def base_kernel(lists, queries, embeddings, received, tiles, out, *, scale):
    blocks, _, block = out.shape
    side = tile_side(ON)
    for g, slot in enumerate(slots_of(lists, blocks, ON)):
        own = dot(queries[...], embeddings[g * block : (g + 1) * block, :], NT) * scale
        out[g] = own + dot(received[slot], tiles[g, side], NT)


def signal_kernel(lists, base, hits, received, tiles, signal, push, total):
    blocks = base.shape[0]
    side = tile_side(OFF)
    total[...] = jnp.zeros_like(total)
    for g, slot in enumerate(slots_of(lists, blocks, OFF)):
        scores = base[g] + dot(received[slot], tiles[g, side], NT)
        value = (jax.nn.sigmoid(scores) - hits[g]).astype(BF16)
        signal[g] = value
        total[slot] += dot(value, tiles[g, side], NN)
    push[...] = total[...].astype(BF16)


def push_kernel(lists, signal, tiles, push, total):
    blocks = signal.shape[0]
    side = tile_side(ON)
    total[...] = jnp.zeros_like(total)
    for g, slot in enumerate(slots_of(lists, blocks, ON)):
        total[slot] += dot(signal[g], tiles[g, side], NN)
    push[...] = total[...].astype(BF16)


def query_kernel(lists, signal, received, embeddings, out):
    blocks, _, block = signal.shape
    total = dot(signal[0], embeddings[0:block, :], NN)
    for g in range(1, blocks):
        total += dot(signal[g], embeddings[g * block : (g + 1) * block, :], NN)
    for slot, index in enumerate(named_by_partner(lists, blocks, ON)):
        total += dot(received[slot], block_rows(embeddings, index, block), NN)
    out[...] = total


def query_end_kernel(lists, part, received, embeddings, after, kept, sent, total, *, blocks):
    del after
    block = received.shape[2]
    first, second = named_by_partner(lists, blocks, OFF)
    total[...] = (
        part[...]
        + dot(received[0], block_rows(embeddings, first, block), NN)
        + dot(received[1], block_rows(embeddings, second, block), NN)
    )
    rows = kept.shape[0]
    core = lax.axis_index(AXIS) % 2
    kept[...] = total[pl.ds(pl.multiple_of(core * rows, rows), rows), :]
    sent[...] = total[pl.ds(pl.multiple_of((1 - core) * rows, rows), rows), :]


def embed_kernel(lists, signal, received, queries, out, held, total, ready, sem, *, scale):
    blocks, _, block = signal.shape
    for g in range(blocks):
        total[g] = dot(signal[g], queries[...], TN)
    for slot, index in enumerate(named_by_partner(lists, blocks, ON)):
        total[index] += dot(received[slot], queries[...], TN)
    copies = []
    for g in range(blocks):
        ready[g] = (total[g] * scale).astype(BF16)
        copies.append(pltpu.make_async_copy(ready.at[g], out.at[pl.ds(g * block, block), :], sem.at[g]))
        copies[-1].start()
    for slot, index in enumerate(named_by_partner(lists, blocks, OFF)):
        held[slot] = total[index]
    for copy in copies:
        copy.wait()


def embed_end_kernel(lists, held, received, queries, old, out, ready, sem, *, blocks, scale):
    del old
    block = ready.shape[1]
    copies = []
    for slot, index in enumerate(named_by_partner(lists, blocks, OFF)):
        ready[slot] = ((held[slot] + dot(received[slot], queries[...], TN)) * scale).astype(BF16)
        place = out.at[pl.ds(pl.multiple_of(index * block, block), block), :]
        copies.append(pltpu.make_async_copy(ready.at[slot], place, sem.at[slot]))
        copies[-1].start()
    for copy in copies:
        copy.wait()


VMEM = pl.BlockSpec(memory_space=pltpu.VMEM)
SMEM = pl.BlockSpec(memory_space=pltpu.SMEM)
ANY = pl.BlockSpec(memory_space=pl.ANY)
HBM = pl.BlockSpec(memory_space=pltpu.HBM)


def call(kernel, name, in_specs, out_shape, out_specs=None, scratch=(), aliases=None):
    if out_specs is None:
        out_specs = jax.tree.map(lambda _: VMEM, out_shape)
    return pl.pallas_call(
        kernel,
        in_specs=in_specs,
        out_specs=out_specs,
        out_shape=out_shape,
        scratch_shapes=scratch,
        input_output_aliases=aliases or {},
        name=name,
        cost_estimate=pl.CostEstimate(flops=0, bytes_accessed=0, transcendentals=0),
        compiler_params=pltpu.CompilerParams(vmem_limit_bytes=VMEM_BYTES),
    )


def digit_of(stride, radix):
    return (lax.axis_index(AXIS) // stride) % radix


def moved(i, stride, radix, step):
    digit = (i // stride) % radix
    return i + ((digit + step) % radix - digit) * stride


def exchange(value, stride, radix, step):
    count = lax.axis_size(AXIS)
    return lax.ppermute(value, AXIS, [(i, moved(i, stride, radix, step)) for i in range(count)])


def split_kernel(*refs, stride, radix, arrived):
    held, got = refs[0], refs[1 : 1 + arrived]
    kept, sent = refs[1 + arrived], refs[2 + arrived : 1 + arrived + radix]
    total = refs[-1]
    value = held[...]
    for ref in got:
        value = value + ref[...].astype(F32)
    total[...] = value
    rows = kept.shape[0]
    digit = digit_of(stride, radix)
    kept[...] = total[pl.ds(pl.multiple_of(digit * rows, rows), rows), :]
    for step, ref in enumerate(sent, 1):
        place = (digit + step) % radix
        ref[...] = total[pl.ds(pl.multiple_of(place * rows, rows), rows), :].astype(BF16)


def finish_kernel(*refs, scale):
    value = refs[0][...]
    for ref in refs[1:-1]:
        value = value + ref[...].astype(F32)
    refs[-1][...] = (value * scale).astype(BF16)


def join_kernel(*refs, stride, radix):
    pieces, out = refs[:-1], refs[-1]
    rows = pieces[0].shape[0]
    digit = digit_of(stride, radix)
    for step, ref in enumerate(pieces):
        place = (digit + radix - step) % radix
        out[pl.ds(pl.multiple_of(place * rows, rows), rows), :] = ref[...].astype(out.dtype)


def stages_of(count, rows):
    stages = []
    stride, radix = 2, 2
    while stride < count and count // stride % radix == 0 and rows % (16 * radix) == 0:
        stages.append((stride, radix))
        stride *= radix
        rows //= radix
        radix = 4 if radix == 2 else 2
    return stages


def sum_queries(kept, sent, scale):
    count = lax.axis_size(AXIS)
    rows, width = kept.shape
    stages = stages_of(count, rows)
    got = [exchange(sent, 1, 2, 1)]
    held = kept
    for stride, radix in stages:
        rows //= radix
        piece = jax.ShapeDtypeStruct((rows, width), F32)
        small = jax.ShapeDtypeStruct((rows, width), BF16)
        held, *parts = call(
            functools.partial(split_kernel, stride=stride, radix=radix, arrived=len(got)),
            "split",
            [VMEM] * (1 + len(got)),
            [piece] + [small] * (radix - 1),
            scratch=[pltpu.VMEM((rows * radix, width), F32)],
        )(held, *got)
        got = [exchange(part, stride, radix, step) for step, part in enumerate(parts, 1)]
    done = math.prod(radix for _, radix in stages) * 2
    if done < count:
        for ref in got:
            held = held + ref.astype(F32)
        groups = [list(range(first, count, done)) for first in range(done)]
        held, got = lax.psum(held, AXIS, axis_index_groups=groups), []
    value = call(
        functools.partial(finish_kernel, scale=scale),
        "finish",
        [VMEM] * (1 + len(got)),
        jax.ShapeDtypeStruct((rows, width), BF16),
    )(held, *got)
    for stride, radix in stages[::-1] + [(1, 2)]:
        pieces = [value] + [exchange(value, stride, radix, step) for step in range(1, radix)]
        rows *= radix
        value = call(
            functools.partial(join_kernel, stride=stride, radix=radix),
            "join",
            [VMEM] * radix,
            jax.ShapeDtypeStruct((rows, width), F32 if stride == 1 else BF16),
        )(*pieces)
    return value


def per_device(embeddings, edge_tiles, neighbour, propensity, queries, positives):
    count = lax.axis_size(AXIS)
    blocks, _, block, _ = edge_tiles.shape
    labels_dev, width = embeddings.shape
    rows = queries.shape[0]
    lists = neighbour.T
    odd = range(1, count, 2)
    off_route = [(i, (i + 1) % count) for i in odd] + [((i + 1) % count, i) for i in odd]

    def off_swap(value):
        return lax.ppermute(value, AXIS, off_route)

    def on_swap(value):
        return exchange(value, 1, 2, 1)

    pair = jax.ShapeDtypeStruct((2, rows, block), BF16)
    pair_sum = pltpu.VMEM((2, rows, block), F32)
    full = jax.ShapeDtypeStruct((blocks, rows, block), F32)
    scale = 1.0 / math.sqrt(width)

    def project(off, *after):
        return call(
            functools.partial(project_kernel, off=off, scale=scale),
            "project_off" if off else "project_on",
            [HBM] * 3 + [ANY] * len(after),
            pair,
            scratch=[
                pltpu.SMEM(lists.shape, jnp.int32),
                pltpu.VMEM((rows, width), BF16),
                pltpu.VMEM((blocks, block, width), BF16),
                pltpu.SemaphoreType.DMA((2 + blocks,)),
            ],
        )(*(pltpu.with_memory_space_constraint(x, pltpu.HBM) for x in (lists, queries, embeddings)), *after)

    for_off = project(OFF)
    from_off = off_swap(for_off)
    from_on = on_swap(project(ON, for_off))
    hits = call(
        hits_kernel, "hits", [VMEM, VMEM], full
    )(positives, propensity.reshape(1, labels_dev))
    base = call(
        functools.partial(base_kernel, scale=scale),
        "base",
        [SMEM] + [VMEM] * 4,
        full,
    )(lists, queries, embeddings, from_on, edge_tiles)
    signal, push_off = call(
        signal_kernel,
        "signal",
        [SMEM] + [VMEM] * 4,
        [jax.ShapeDtypeStruct(full.shape, BF16), pair],
        scratch=[pair_sum],
    )(lists, base, hits, from_off, edge_tiles)

    back_off = off_swap(push_off)
    push_on = call(
        push_kernel, "push", [SMEM, VMEM, VMEM], pair, scratch=[pair_sum]
    )(lists, signal, edge_tiles)
    back_on = on_swap(push_on)
    part = call(
        query_kernel,
        "query",
        [SMEM] + [VMEM] * 3,
        jax.ShapeDtypeStruct((rows, width), F32),
    )(lists, signal, back_on, embeddings)
    out, held = call(
        functools.partial(embed_kernel, scale=1.0 / math.sqrt(rows)),
        "embed",
        [SMEM] + [VMEM] * 3,
        [
            jax.ShapeDtypeStruct((labels_dev, width), BF16),
            jax.ShapeDtypeStruct((2, block, width), F32),
        ],
        out_specs=[ANY, VMEM],
        scratch=[
            pltpu.VMEM((blocks, block, width), F32),
            pltpu.VMEM((blocks, block, width), BF16),
            pltpu.SemaphoreType.DMA((blocks,)),
        ],
    )(lists, signal, back_on, queries)

    half = jax.ShapeDtypeStruct((rows // 2, width), F32)
    kept, sent = call(
        functools.partial(query_end_kernel, blocks=blocks),
        "query_end",
        [SMEM] + [VMEM] * 3 + [ANY],
        [half, half],
        scratch=[pltpu.VMEM((rows, width), F32)],
    )(lists, part, back_off, embeddings, held)
    grad_embed = call(
        functools.partial(embed_end_kernel, blocks=blocks, scale=1.0 / math.sqrt(rows)),
        "embed_end",
        [SMEM] + [VMEM] * 3 + [ANY],
        jax.ShapeDtypeStruct((labels_dev, width), BF16),
        out_specs=ANY,
        scratch=[pltpu.VMEM((2, block, width), BF16), pltpu.SemaphoreType.DMA((2,))],
        aliases={4: 0},
    )(lists, held, back_off, queries, out)
    grad_queries = sum_queries(kept, sent, 1.0 / math.sqrt(labels_dev * count))
    return (grad_embed, grad_queries)


def solution(mesh):
    placed = (
        P("labels", None),
        P("labels", None, None, None),
        P(),
        P("labels"),
        P("groups", None),
        P("groups", None),
    )
    return jax.shard_map(
        per_device,
        mesh=mesh,
        in_specs=placed,
        out_specs=(P(("groups", "labels"), None), P("groups", None)),
        check_vma=False,
    )
```

time: 267 us -> 76 us (0.28)
  waiting for transfers between devices: 138 us -> 17.5 us
  matrix products: 37.8 us -> 0 us
  Pallas kernels: 0 us -> 27.2 us
  local copies, waits for them, and re-layouts: 30.7 us -> 4.59 us
  between operations: 14.3 us -> 0.86 us
  starting transfers between devices: 36.2 us -> 25.4 us
  other arithmetic: 9.08 us -> 0 us
    psum x1 -> x0, waiting for transfers between devices: 107 us -> none  [per_device(): lax.psum(partial_query, 'labels') / math.sqrt(labels_dev * count)]
    dot_general x9 -> x0, matrix products: 37.8 us -> none  [the longest x1 8.26 us: per_device(): jnp.einsum('bj,brd->jrd', pick_next, push_next, precision=lax.Precision.H...]
    pallas_call x0 -> x16, Pallas kernels: none -> 27.2 us  [the longest x2 6.99 us: project(): call(functools.partial(project_kernel, off=off, scale=scale), 'project_of...]
    dot_general x4 -> x0, local copies, waits for them, and re-layouts: 19.5 us -> none  [the longest x1 7.74 us: per_device(): jnp.einsum('bji,bjd->bid', edge_tiles[:, 1], back_blocks, preferred_eleme...]
    ppermute x4 -> x14, waiting for transfers between devices: 31.6 us -> 17.5 us  [the longest x12 16.2 us: exchange(): lax.ppermute(value, AXIS, [(i, moved(i, stride, radix, step)) for i in ra...]
    ppermute x4 -> x14, starting transfers between devices: 36.2 us -> 25.4 us  [the longest x12 15.5 us: exchange(): lax.ppermute(value, AXIS, [(i, moved(i, stride, radix, step)) for i in ra...]
    gather x2 -> x0, local copies, waits for them, and re-layouts: 6.94 us -> none  [the longest x1 4.3 us: per_device(): from_next = jnp.take(next_shard, own_next, axis=0)]
    convert_element_type x1 -> x0, other arithmetic: 5.73 us -> none  [per_device(): grad_embed = total.astype(jnp.bfloat16).reshape(labels_dev, width)]
  transfers between devices with their start and end apart: 5 -> 14, of which waited for: 2 -> 10; matrix products, arithmetic and copies ran while one was open for 11% -> 2% of each run, Pallas kernels for 0% -> 18%
where the time goes in v2:
time: 76 us; the launch traced here: 75.6 us
  Pallas kernels  27.2 us (36%)
  starting transfers between devices  25.4 us (33%)
  waiting for transfers between devices  17.5 us (23%)
  local copies, waits for them, and re-layouts  4.59 us (6%)
  between operations  0.86 us (1%)
    ppermute x12, waiting for transfers between devices, exchange(): lax.ppermute(value, AXIS, [(i, moved(i, stride, radix, step)) for i in ra...  16.2 us
    ppermute x12, starting transfers between devices, exchange(): lax.ppermute(value, AXIS, [(i, moved(i, stride, radix, step)) for i in ra...  15.5 us
    ppermute x2, starting transfers between devices, off_swap(): return lax.ppermute(value, AXIS, off_route)  9.96 us
    pallas_call x2, Pallas kernels, project(): call(functools.partial(project_kernel, off=off, scale=scale), 'project_of...  6.99 us
    unnamed x15, local copies, waits for them, and re-layouts  4.59 us
    pallas_call x1, Pallas kernels, per_device(): call(functools.partial(embed_kernel, scale=1.0 / math.sqrt(rows)), 'embed...  3.87 us
    pallas_call x1, Pallas kernels, per_device(): call(hits_kernel, 'hits', [VMEM, VMEM], full)  2.9 us
    pallas_call x1, Pallas kernels, per_device(): call(signal_kernel, 'signal', [SMEM] + [VMEM] * 4, [jax.ShapeDtypeStruct(...  2.88 us
  transfers between devices with their start and end apart: 14, of which 10 were waited for; matrix products, arithmetic and copies ran while one was open for 2% of the time, Pallas kernels for 18%

profile of v2, /device:TPU:0, one launch (start us, length us, event | category | flops | bytes accessed | tf_op | source)
XLA Modules:
  0.0 75.6 jit_solution(18043200505643527587)
XLA Ops:
  0.6 3.4 %project_off.1.rest_0_ = bf16[2,256,512]{2,1,0:T(8,128)(2,1)} custom-call(s32[2,64]{1,0:T(2,128)} %bitcast.2, bf16[256,768]{1,0:T(8,128)(2,1)} %queries.9, bf16[2048,768]{1,0:T(8,128)(2,1)} %embeddings.9), custom_call_target="tpu_custom_call" | custom-call | tf_op jit(solution)/shard_map/project_off/pallas_call | solution.py:318
  4.1 3.6 %project_on.1 = bf16[2,256,512]{2,1,0:T(8,128)(2,1)} custom-call(s32[2,64]{1,0:T(2,128)} %bitcast.3, bf16[256,768]{1,0:T(8,128)(2,1)} %queries.9, bf16[2048,768]{1,0:T(8,128)(2,1)} %embeddings.9, bf16[2,256,512]{2,1,0:T(8,128)(2,1)} %project_off.1.rest_0_), custom_call_target="tpu_custom_call" | custom-call | tf_op jit(solution)/shard_map/project_on/pallas_call | solution.py:318
  8.2 5.7 %collective-permute-start.1 = (bf16[2,256,512]{2,1,0:T(8,128)(2,1)}, bf16[2,256,512]{2,1,0:T(8,128)(2,1)}, u32[]{:S(2)}, u32[]{:S(2)}) collective-permute-start(bf16[2,256,512]{2,1,0:T(8,128)(2,1)} %project_off.1.rest_0_), channel_id=1, source_target_pairs={{1,2},{3,4},{5,6},{7,8},{9,10},{11,12},{13,14},{15,0},{2,1},{4,3},... | collective-permute-start | bytes 1572872 | tf_op jit(solution)/shard_map/ppermute | solution.py:307
  13.9 1.5 %copy.9.positives = s32[256,8]{1,0:T(8,128)} copy(s32[256,8]{0,1:T(8,128)} %param.11) | data formatting | bytes 16384 | tf_op args[5]
  15.3 0.9 %copy-done.4 = s32[256,8]{1,0:T(8,128)S(1)} copy-done((s32[256,8]{1,0:T(8,128)S(1)}, s32[256,8]{1,0:T(8,128)}, u32[]{:S(2)}) %copy-start.4) | copy-done | bytes 8216
  16.2 2.9 %hits.1 = f32[4,256,512]{2,1,0:T(8,128)S(1)} custom-call(s32[256,8]{1,0:T(8,128)S(1)} %copy-done.4, f32[1,2048]{1,0:T(1,128)S(1)} %bitcast.11), custom_call_target="tpu_custom_call" | custom-call | tf_op jit(solution)/shard_map/hits/pallas_call | solution.py:334
  19.2 2.2 %copy-done.1 = bf16[4,2,512,512]{3,2,1,0:T(8,128)(2,1)S(1)} copy-done((bf16[4,2,512,512]{3,2,1,0:T(8,128)(2,1)S(1)}, bf16[4,2,512,512]{3,2,1,0:T(8,128)(2,1)}, u32[]{:S(2)}) %copy-start.1) | copy-done | bytes 4194328
  21.4 2.8 %base.1 = f32[4,256,512]{2,1,0:T(8,128)S(1)} custom-call(s32[2,64]{1,0:T(2,128)S(1)} %bitcast.4, bf16[256,768]{1,0:T(8,128)(2,1)S(1)} %copy-done.3, bf16[2048,768]{1,0:T(8,128)(2,1)S(1)} %copy-done, bf16[2,256,512]{2,1,0:T(8,128)(2,1)} %collective-permute-done.received, bf16[4,2,512,512]{3,2,1,0:T(8,128)(2,1)S(1)} %copy-done.1), custom_call_target="tpu_custom_call" | custom-call | tf_op jit(solution)/shard_map/base/pallas_call | solution.py:337
  24.2 2.9 %signal.1 = (bf16[4,256,512]{2,1,0:T(8,128)(2,1)S(1)}, bf16[2,256,512]{2,1,0:T(8,128)(2,1)S(1)}) custom-call(s32[2,64]{1,0:T(2,128)S(1)} %bitcast.5, f32[4,256,512]{2,1,0:T(8,128)S(1)} %base.1, f32[4,256,512]{2,1,0:T(8,128)S(1)} %hits.1, bf16[2,256,512]{2,1,0:T(8,128)(2,1)} %collective-permute-done.1.received, bf16[4,2,512,512]{3,2,1,0:T(8,128)(2,1)S(1)} %copy-done.2), custom_call_target="tpu_custom_call" | custom-call | tf_op jit(solution)/shard_map/signal/pallas_call | solution.py:343
  27.1 1.4 %push.1 = bf16[2,256,512]{2,1,0:T(8,128)(2,1)S(1)} custom-call(s32[2,64]{1,0:T(2,128)S(1)} %bitcast.6, bf16[4,256,512]{2,1,0:T(8,128)(2,1)S(1)} %get-tuple-element.14.signal, bf16[4,2,512,512]{3,2,1,0:T(8,128)(2,1)S(1)} %copy-done.2), custom_call_target="tpu_custom_call" | custom-call | tf_op jit(solution)/shard_map/push/pallas_call | solution.py:352
  28.5 4.3 %collective-permute-start.3 = (bf16[2,256,512]{2,1,0:T(8,128)(2,1)S(1)}, bf16[2,256,512]{2,1,0:T(8,128)(2,1)S(1)}, u32[]{:S(2)}, u32[]{:S(2)}) collective-permute-start(bf16[2,256,512]{2,1,0:T(8,128)(2,1)S(1)} %get-tuple-element.16), channel_id=1, source_target_pairs={{1,2},{3,4},{5,6},{7,8},{9,10},{11,12},{13,14},{15,0},{2,1},{4,3},... | collective-permute-start | bytes 1572872 | tf_op jit(solution)/shard_map/ppermute | solution.py:307
  32.8 1.9 %query.1.part = f32[256,768]{1,0:T(8,128)S(1)} custom-call(s32[2,64]{1,0:T(2,128)S(1)} %bitcast.7, bf16[4,256,512]{2,1,0:T(8,128)(2,1)S(1)} %get-tuple-element.14.signal, bf16[2,256,512]{2,1,0:T(8,128)(2,1)S(1)} %collective-permute-done.2.received, bf16[2048,768]{1,0:T(8,128)(2,1)S(1)} %copy-done), custom_call_target="tpu_custom_call" | custom-call | tf_op jit(solution)/shard_map/query/pallas_call | solution.py:356
  34.8 3.9 %embed.1 = (bf16[2048,768]{1,0:T(8,128)(2,1)}, f32[2,512,768]{2,1,0:T(8,128)S(1)}) custom-call(s32[2,64]{1,0:T(2,128)S(1)} %bitcast.8, bf16[4,256,512]{2,1,0:T(8,128)(2,1)S(1)} %get-tuple-element.14.signal, bf16[2,256,512]{2,1,0:T(8,128)(2,1)S(1)} %collective-permute-done.2.received, bf16[256,768]{1,0:T(8,128)(2,1)S(1)} %copy-done.3), custom_call_target="tpu_custom_call" | custom-call | tf_op jit(solution)/shard_map/embed/pallas_call | solution.py:362
  38.6 1.4 %collective-permute-done.3.received = bf16[2,256,512]{2,1,0:T(8,128)(2,1)S(1)} collective-permute-done((bf16[2,256,512]{2,1,0:T(8,128)(2,1)S(1)}, bf16[2,256,512]{2,1,0:T(8,128)(2,1)S(1)}, u32[]{:S(2)}, u32[]{:S(2)}) %collective-permute-start.3) | collective-permute-done | bytes 524320 | tf_op jit(solution)/shard_map/ppermute | solution.py:307
  40.0 1.2 %query_end.1 = (f32[128,768]{1,0:T(8,128)S(1)}, f32[128,768]{1,0:T(8,128)S(1)}) custom-call(s32[2,64]{1,0:T(2,128)S(1)} %bitcast.9, f32[256,768]{1,0:T(8,128)S(1)} %query.1.part, bf16[2,256,512]{2,1,0:T(8,128)(2,1)S(1)} %collective-permute-done.3.received, bf16[2048,768]{1,0:T(8,128)(2,1)S(1)} %copy-done, f32[2,512,768]{2,1,0:T(8,128)S(1)} %get-tuple-element.15.held.after), custom_call_target="tpu_custom_call" | custom-call | tf_op jit(solution)/shard_map/query_end/pallas_call | solution.py:379
  41.2 3.3 %collective-permute-start.4 = (f32[128,768]{1,0:T(8,128)S(1)}, f32[128,768]{1,0:T(8,128)S(1)}, u32[]{:S(2)}, u32[]{:S(2)}) collective-permute-start(f32[128,768]{1,0:T(8,128)S(1)} %get-tuple-element.19), channel_id=1, source_target_pairs={{0,1},{1,0},{2,3},{3,2},{4,5},{5,4},{6,7},{7,6},{8,9},{9,8},{10,11... | collective-permute-start | bytes 1179656 | tf_op jit(solution)/shard_map/ppermute | solution.py:209
  44.5 1.3 %collective-permute-done.4.refs_1_ = f32[128,768]{1,0:T(8,128)S(1)} collective-permute-done((f32[128,768]{1,0:T(8,128)S(1)}, f32[128,768]{1,0:T(8,128)S(1)}, u32[]{:S(2)}, u32[]{:S(2)}) %collective-permute-start.4) | collective-permute-done | bytes 393248 | tf_op jit(solution)/shard_map/ppermute | solution.py:209
  46.0 1.2 %collective-permute-start.5 = (bf16[64,768]{1,0:T(8,128)(2,1)S(1)}, bf16[64,768]{1,0:T(8,128)(2,1)S(1)}, u32[]{:S(2)}, u32[]{:S(2)}) collective-permute-start(bf16[64,768]{1,0:T(8,128)(2,1)S(1)} %get-tuple-element.21), channel_id=1, source_target_pairs={{0,2},{1,3},{2,0},{3,1},{4,6},{5,7},{6,4},{7,5},{8,10},{9,11},{10,... | collective-permute-start | bytes 294920 | tf_op jit(solution)/shard_map/ppermute | solution.py:209
  47.1 4.0 %collective-permute-done.5.refs_1_ = bf16[64,768]{1,0:T(8,128)(2,1)S(1)} collective-permute-done((bf16[64,768]{1,0:T(8,128)(2,1)S(1)}, bf16[64,768]{1,0:T(8,128)(2,1)S(1)}, u32[]{:S(2)}, u32[]{:S(2)}) %collective-permute-start.5) | collective-permute-done | bytes 98336 | tf_op jit(solution)/shard_map/ppermute | solution.py:209
  51.1 1.3 %collective-permute-start.6 = (bf16[16,768]{1,0:T(8,128)(2,1)S(1)}, bf16[16,768]{1,0:T(8,128)(2,1)S(1)}, u32[]{:S(2)}, u32[]{:S(2)}) collective-permute-start(bf16[16,768]{1,0:T(8,128)(2,1)S(1)} %get-tuple-element.23), channel_id=1, source_target_pairs={{0,4},{1,5},{2,6},{3,7},{4,8},{5,9},{6,10},{7,11},{8,12},{9,13},{1... | collective-permute-start | bytes 73736 | tf_op jit(solution)/shard_map/ppermute | solution.py:209
  52.4 2.6 %collective-permute-start.7 = (bf16[16,768]{1,0:T(8,128)(2,1)S(1)}, bf16[16,768]{1,0:T(8,128)(2,1)S(1)}, u32[]{:S(2)}, u32[]{:S(2)}) collective-permute-start(bf16[16,768]{1,0:T(8,128)(2,1)S(1)} %get-tuple-element.24), channel_id=1, source_target_pairs={{0,8},{1,9},{2,10},{3,11},{4,12},{5,13},{6,14},{7,15},{8,0},{9,1},... | collective-permute-start | bytes 73736 | tf_op jit(solution)/shard_map/ppermute | solution.py:209
  55.0 1.3 %collective-permute-start.8 = (bf16[16,768]{1,0:T(8,128)(2,1)S(1)}, bf16[16,768]{1,0:T(8,128)(2,1)S(1)}, u32[]{:S(2)}, u32[]{:S(2)}) collective-permute-start(bf16[16,768]{1,0:T(8,128)(2,1)S(1)} %get-tuple-element.25), channel_id=1, source_target_pairs={{0,12},{1,13},{2,14},{3,15},{4,0},{5,1},{6,2},{7,3},{8,4},{9,5},{1... | collective-permute-start | bytes 73736 | tf_op jit(solution)/shard_map/ppermute | solution.py:209
  57.4 1.5 %collective-permute-done.8.refs_3_ = bf16[16,768]{1,0:T(8,128)(2,1)S(1)} collective-permute-done((bf16[16,768]{1,0:T(8,128)(2,1)S(1)}, bf16[16,768]{1,0:T(8,128)(2,1)S(1)}, u32[]{:S(2)}, u32[]{:S(2)}) %collective-permute-start.8) | collective-permute-done | bytes 24608 | tf_op jit(solution)/shard_map/ppermute | solution.py:209
  58.8 3.2 %collective-permute-start.11 = (bf16[16,768]{1,0:T(8,128)(2,1)S(1)}, bf16[16,768]{1,0:T(8,128)(2,1)S(1)}, u32[]{:S(2)}, u32[]{:S(2)}) collective-permute-start(bf16[16,768]{1,0:T(8,128)(2,1)S(1)} %finish.1.refs_0_), channel_id=1, source_target_pairs={{0,12},{1,13},{2,14},{3,15},{4,0},{5,1},{6,2},{7,3},{8,4},{9,5},{1... | collective-permute-start | bytes 73736 | tf_op jit(solution)/shard_map/ppermute | solution.py:209
  62.0 0.6 collective-permute-start.9
  62.7 0.9 %collective-permute-done.11.refs_3_ = bf16[16,768]{1,0:T(8,128)(2,1)S(1)} collective-permute-done((bf16[16,768]{1,0:T(8,128)(2,1)S(1)}, bf16[16,768]{1,0:T(8,128)(2,1)S(1)}, u32[]{:S(2)}, u32[]{:S(2)}) %collective-permute-start.11) | collective-permute-done | bytes 24608 | tf_op jit(solution)/shard_map/ppermute | solution.py:209
  63.6 3.2 %collective-permute-done.10.refs_2_ = bf16[16,768]{1,0:T(8,128)(2,1)S(1)} collective-permute-done((bf16[16,768]{1,0:T(8,128)(2,1)S(1)}, bf16[16,768]{1,0:T(8,128)(2,1)S(1)}, u32[]{:S(2)}, u32[]{:S(2)}) %collective-permute-start.10) | collective-permute-done | bytes 24608 | tf_op jit(solution)/shard_map/ppermute | solution.py:209
  66.8 0.9 %collective-permute-done.9.refs_1_ = bf16[16,768]{1,0:T(8,128)(2,1)S(1)} collective-permute-done((bf16[16,768]{1,0:T(8,128)(2,1)S(1)}, bf16[16,768]{1,0:T(8,128)(2,1)S(1)}, u32[]{:S(2)}, u32[]{:S(2)}) %collective-permute-start.9) | collective-permute-done | bytes 24608 | tf_op jit(solution)/shard_map/ppermute | solution.py:209
  67.7 1.3 %collective-permute-start.12 = (bf16[64,768]{1,0:T(8,128)(2,1)S(1)}, bf16[64,768]{1,0:T(8,128)(2,1)S(1)}, u32[]{:S(2)}, u32[]{:S(2)}) collective-permute-start(bf16[64,768]{1,0:T(8,128)(2,1)S(1)} %join.3.refs_0_), channel_id=1, source_target_pairs={{0,2},{1,3},{2,0},{3,1},{4,6},{5,7},{6,4},{7,5},{8,10},{9,11},{10,... | collective-permute-start | bytes 294920 | tf_op jit(solution)/shard_map/ppermute | solution.py:209
  69.0 3.4 %collective-permute-done.12.refs_1_ = bf16[64,768]{1,0:T(8,128)(2,1)S(1)} collective-permute-done((bf16[64,768]{1,0:T(8,128)(2,1)S(1)}, bf16[64,768]{1,0:T(8,128)(2,1)S(1)}, u32[]{:S(2)}, u32[]{:S(2)}) %collective-permute-start.12) | collective-permute-done | bytes 98336 | tf_op jit(solution)/shard_map/ppermute | solution.py:209
  72.5 2.2 %embed_end.1 = bf16[2048,768]{1,0:T(8,128)(2,1)} custom-call(s32[2,64]{1,0:T(2,128)S(1)} %bitcast.10, f32[2,512,768]{2,1,0:T(8,128)S(1)} %get-tuple-element.15.held.after, bf16[2,256,512]{2,1,0:T(8,128)(2,1)S(1)} %collective-permute-done.3.received, bf16[256,768]{1,0:T(8,128)(2,1)S(1)} %copy-done.3, ...), custom_call_target="tpu_custom_call", output_to_operand_aliasing={{}: (4, {})} | custom-call | tf_op jit(solution)/shard_map/embed_end/pallas_call | solution.py:386
  74.7 0.9 %join.5 = f32[256,768]{1,0:T(8,128)} custom-call(bf16[128,768]{1,0:T(8,128)(2,1)S(1)} %join.4.refs_0_, bf16[128,768]{1,0:T(8,128)(2,1)S(1)} %collective-permute-done.13.refs_1_), custom_call_target="tpu_custom_call" | custom-call | tf_op jit(solution)/shard_map/join/pallas_call | solution.py:288
  (27 shorter events, 1.9 us)
Async XLA Ops:
  4.1 11.3 %copy-start.6 = (f32[2048]{0:T(1024)S(1)}, f32[2048]{0:T(1024)}, u32[]{:S(2)}) copy-start(f32[2048]{0:T(1024)} %param.9) | copy-start | bytes 24580
  4.1 15.1 %copy-start = (bf16[2048,768]{1,0:T(8,128)(2,1)S(1)}, bf16[2048,768]{1,0:T(8,128)(2,1)}, u32[]{:S(2)}) copy-start(bf16[2048,768]{1,0:T(8,128)(2,1)} %embeddings.9) | copy-start | bytes 9437188
  4.1 15.1 %copy-start.3 = (bf16[256,768]{1,0:T(8,128)(2,1)S(1)}, bf16[256,768]{1,0:T(8,128)(2,1)}, u32[]{:S(2)}) copy-start(bf16[256,768]{1,0:T(8,128)(2,1)} %queries.9) | copy-start | bytes 1179652
  4.1 15.1 %copy-start.5 = (s32[64,2]{0,1:T(2,128)S(1)}, s32[64,2]{0,1:T(2,128)}, u32[]{:S(2)}) copy-start(s32[64,2]{0,1:T(2,128)} %param.8) | copy-start | bytes 1540
  7.7 11.5 %collective-permute-start = (bf16[2,256,512]{2,1,0:T(8,128)(2,1)}, bf16[2,256,512]{2,1,0:T(8,128)(2,1)}, u32[]{:S(2)}, u32[]{:S(2)}) collective-permute-start(bf16[2,256,512]{2,1,0:T(8,128)(2,1)} %project_on.1), channel_id=1, source_target_pairs={{0,1},{1,0},{2,3},{3,2},{4,5},{5,4},{6,7},{7,6},{8,9},{9,8},{10,11... | collective-permute-start | bytes 1572872 | tf_op jit(solution)/shard_map/ppermute | solution.py:209
  8.2 16.0 %collective-permute-start.1 = (bf16[2,256,512]{2,1,0:T(8,128)(2,1)}, bf16[2,256,512]{2,1,0:T(8,128)(2,1)}, u32[]{:S(2)}, u32[]{:S(2)}) collective-permute-start(bf16[2,256,512]{2,1,0:T(8,128)(2,1)} %project_off.1.rest_0_), channel_id=1, source_target_pairs={{1,2},{3,4},{5,6},{7,8},{9,10},{11,12},{13,14},{15,0},{2,1},{4,3},... | collective-permute-start | bytes 1572872 | tf_op jit(solution)/shard_map/ppermute | solution.py:307
  15.3 0.9 %copy-start.4 = (s32[256,8]{1,0:T(8,128)S(1)}, s32[256,8]{1,0:T(8,128)}, u32[]{:S(2)}) copy-start(s32[256,8]{1,0:T(8,128)} %copy.9.positives) | copy-start | bytes 24580
  19.2 2.2 %copy-start.1 = (bf16[4,2,512,512]{3,2,1,0:T(8,128)(2,1)S(1)}, bf16[4,2,512,512]{3,2,1,0:T(8,128)(2,1)}, u32[]{:S(2)}) copy-start(bf16[4,2,512,512]{3,2,1,0:T(8,128)(2,1)} %tiles.5) | copy-start | bytes 12582916
  21.4 2.8 %copy-start.2 = (bf16[4,2,512,512]{3,2,1,0:T(8,128)(2,1)S(1)}, bf16[4,2,512,512]{3,2,1,0:T(8,128)(2,1)}, u32[]{:S(2)}) copy-start(bf16[4,2,512,512]{3,2,1,0:T(8,128)(2,1)} %tiles.5) | copy-start | bytes 12582916
  28.5 4.4 %collective-permute-start.2 = (bf16[2,256,512]{2,1,0:T(8,128)(2,1)S(1)}, bf16[2,256,512]{2,1,0:T(8,128)(2,1)S(1)}, u32[]{:S(2)}, u32[]{:S(2)}) collective-permute-start(bf16[2,256,512]{2,1,0:T(8,128)(2,1)S(1)} %push.1), channel_id=1, source_target_pairs={{0,1},{1,0},{2,3},{3,2},{4,5},{5,4},{6,7},{7,6},{8,9},{9,8},{10,11... | collective-permute-start | bytes 1572872 | tf_op jit(solution)/shard_map/ppermute | solution.py:209
  28.5 11.5 %collective-permute-start.3 = (bf16[2,256,512]{2,1,0:T(8,128)(2,1)S(1)}, bf16[2,256,512]{2,1,0:T(8,128)(2,1)S(1)}, u32[]{:S(2)}, u32[]{:S(2)}) collective-permute-start(bf16[2,256,512]{2,1,0:T(8,128)(2,1)S(1)} %get-tuple-element.16), channel_id=1, source_target_pairs={{1,2},{3,4},{5,6},{7,8},{9,10},{11,12},{13,14},{15,0},{2,1},{4,3},... | collective-permute-start | bytes 1572872 | tf_op jit(solution)/shard_map/ppermute | solution.py:307
  41.2 4.7 %collective-permute-start.4 = (f32[128,768]{1,0:T(8,128)S(1)}, f32[128,768]{1,0:T(8,128)S(1)}, u32[]{:S(2)}, u32[]{:S(2)}) collective-permute-start(f32[128,768]{1,0:T(8,128)S(1)} %get-tuple-element.19), channel_id=1, source_target_pairs={{0,1},{1,0},{2,3},{3,2},{4,5},{5,4},{6,7},{7,6},{8,9},{9,8},{10,11... | collective-permute-start | bytes 1179656 | tf_op jit(solution)/shard_map/ppermute | solution.py:209
  46.0 5.1 %collective-permute-start.5 = (bf16[64,768]{1,0:T(8,128)(2,1)S(1)}, bf16[64,768]{1,0:T(8,128)(2,1)S(1)}, u32[]{:S(2)}, u32[]{:S(2)}) collective-permute-start(bf16[64,768]{1,0:T(8,128)(2,1)S(1)} %get-tuple-element.21), channel_id=1, source_target_pairs={{0,2},{1,3},{2,0},{3,1},{4,6},{5,7},{6,4},{7,5},{8,10},{9,11},{10,... | collective-permute-start | bytes 294920 | tf_op jit(solution)/shard_map/ppermute | solution.py:209
  51.1 5.8 %collective-permute-start.6 = (bf16[16,768]{1,0:T(8,128)(2,1)S(1)}, bf16[16,768]{1,0:T(8,128)(2,1)S(1)}, u32[]{:S(2)}, u32[]{:S(2)}) collective-permute-start(bf16[16,768]{1,0:T(8,128)(2,1)S(1)} %get-tuple-element.23), channel_id=1, source_target_pairs={{0,4},{1,5},{2,6},{3,7},{4,8},{5,9},{6,10},{7,11},{8,12},{9,13},{1... | collective-permute-start | bytes 73736 | tf_op jit(solution)/shard_map/ppermute | solution.py:209
  52.4 4.9 %collective-permute-start.7 = (bf16[16,768]{1,0:T(8,128)(2,1)S(1)}, bf16[16,768]{1,0:T(8,128)(2,1)S(1)}, u32[]{:S(2)}, u32[]{:S(2)}) collective-permute-start(bf16[16,768]{1,0:T(8,128)(2,1)S(1)} %get-tuple-element.24), channel_id=1, source_target_pairs={{0,8},{1,9},{2,10},{3,11},{4,12},{5,13},{6,14},{7,15},{8,0},{9,1},... | collective-permute-start | bytes 73736 | tf_op jit(solution)/shard_map/ppermute | solution.py:209
  55.0 3.8 %collective-permute-start.8 = (bf16[16,768]{1,0:T(8,128)(2,1)S(1)}, bf16[16,768]{1,0:T(8,128)(2,1)S(1)}, u32[]{:S(2)}, u32[]{:S(2)}) collective-permute-start(bf16[16,768]{1,0:T(8,128)(2,1)S(1)} %get-tuple-element.25), channel_id=1, source_target_pairs={{0,12},{1,13},{2,14},{3,15},{4,0},{5,1},{6,2},{7,3},{8,4},{9,5},{1... | collective-permute-start | bytes 73736 | tf_op jit(solution)/shard_map/ppermute | solution.py:209
  58.8 4.7 %collective-permute-start.11 = (bf16[16,768]{1,0:T(8,128)(2,1)S(1)}, bf16[16,768]{1,0:T(8,128)(2,1)S(1)}, u32[]{:S(2)}, u32[]{:S(2)}) collective-permute-start(bf16[16,768]{1,0:T(8,128)(2,1)S(1)} %finish.1.refs_0_), channel_id=1, source_target_pairs={{0,12},{1,13},{2,14},{3,15},{4,0},{5,1},{6,2},{7,3},{8,4},{9,5},{1... | collective-permute-start | bytes 73736 | tf_op jit(solution)/shard_map/ppermute | solution.py:209
  62.0 4.7 %collective-permute-start.10 = (bf16[16,768]{1,0:T(8,128)(2,1)S(1)}, bf16[16,768]{1,0:T(8,128)(2,1)S(1)}, u32[]{:S(2)}, u32[]{:S(2)}) collective-permute-start(bf16[16,768]{1,0:T(8,128)(2,1)S(1)} %finish.1.refs_0_), channel_id=1, source_target_pairs={{0,8},{1,9},{2,10},{3,11},{4,12},{5,13},{6,14},{7,15},{8,0},{9,1},... | collective-permute-start | bytes 73736 | tf_op jit(solution)/shard_map/ppermute | solution.py:209
  62.0 5.6 %collective-permute-start.9 = (bf16[16,768]{1,0:T(8,128)(2,1)S(1)}, bf16[16,768]{1,0:T(8,128)(2,1)S(1)}, u32[]{:S(2)}, u32[]{:S(2)}) collective-permute-start(bf16[16,768]{1,0:T(8,128)(2,1)S(1)} %finish.1.refs_0_), channel_id=1, source_target_pairs={{0,4},{1,5},{2,6},{3,7},{4,8},{5,9},{6,10},{7,11},{8,12},{9,13},{1... | collective-permute-start | bytes 73736 | tf_op jit(solution)/shard_map/ppermute | solution.py:209
  67.7 4.7 %collective-permute-start.12 = (bf16[64,768]{1,0:T(8,128)(2,1)S(1)}, bf16[64,768]{1,0:T(8,128)(2,1)S(1)}, u32[]{:S(2)}, u32[]{:S(2)}) collective-permute-start(bf16[64,768]{1,0:T(8,128)(2,1)S(1)} %join.3.refs_0_), channel_id=1, source_target_pairs={{0,2},{1,3},{2,0},{3,1},{4,6},{5,7},{6,4},{7,5},{8,10},{9,11},{10,... | collective-permute-start | bytes 294920 | tf_op jit(solution)/shard_map/ppermute | solution.py:209
  72.4 2.3 %collective-permute-start.13 = (bf16[128,768]{1,0:T(8,128)(2,1)S(1)}, bf16[128,768]{1,0:T(8,128)(2,1)S(1)}, u32[]{:S(2)}, u32[]{:S(2)}) collective-permute-start(bf16[128,768]{1,0:T(8,128)(2,1)S(1)} %join.4.refs_0_), channel_id=1, source_target_pairs={{0,1},{1,0},{2,3},{3,2},{4,5},{5,4},{6,7},{7,6},{8,9},{9,8},{10,11... | collective-permute-start | bytes 589832 | tf_op jit(solution)/shard_map/ppermute | solution.py:209

commit v3 on v2

--- a/solution.py
+++ b/solution.py
@@ -62,19 +62,21 @@
     return ref[pl.ds(pl.multiple_of(index * block, block), block), :]
 
 
-def project_kernel(lists, queries, embeddings, *rest, off, scale):
-    out, table, left, right, sem = rest[-5:]
-    block = out.shape[2]
-    blocks = embeddings.shape[0] // block
+def project_kernel(lists, queries, embeddings, own, for_off, for_on, table, left, right, sem, *, scale):
+    blocks, _, block = own.shape
     fetches = [pltpu.make_async_copy(lists, table, sem.at[0]), pltpu.make_async_copy(queries, left, sem.at[1])]
     for g in range(blocks):
         fetches.append(pltpu.make_async_copy(embeddings.at[pl.ds(g * block, block), :], right.at[g], sem.at[2 + g]))
     for fetch in fetches:
         fetch.start()
-    for fetch in fetches:
+    for fetch in fetches[:2]:
         fetch.wait()
-    for slot, index in enumerate(named_by_partner(table, blocks, off)):
-        out[slot] = (dot(left[...], right[index], NT) * scale).astype(BF16)
+    for g in range(blocks):
+        fetches[2 + g].wait()
+        own[g] = dot(left[...], right[g], NT) * scale
+    for out, off in ((for_off, OFF), (for_on, ON)):
+        for slot, index in enumerate(named_by_partner(table, blocks, off)):
+            out[slot] = own[index].astype(BF16)
 
 
 def hits_kernel(positives, propensity, out):
@@ -89,12 +91,11 @@
         out[g] = jnp.where(hits, inverse[:, g * block : (g + 1) * block], 0.0)
 
 
-def base_kernel(lists, queries, embeddings, received, tiles, out, *, scale):
-    blocks, _, block = out.shape
+def base_kernel(lists, own, received, tiles, out):
+    blocks = out.shape[0]
     side = tile_side(ON)
     for g, slot in enumerate(slots_of(lists, blocks, ON)):
-        own = dot(queries[...], embeddings[g * block : (g + 1) * block, :], NT) * scale
-        out[g] = own + dot(received[slot], tiles[g, side], NT)
+        out[g] = own[g] + dot(received[slot], tiles[g, side], NT)
 
 
 def signal_kernel(lists, base, hits, received, tiles, signal, push, total):
@@ -111,10 +112,13 @@
 
 def push_kernel(lists, signal, tiles, push, total):
     blocks = signal.shape[0]
-    side = tile_side(ON)
+    other = lax.axis_index(AXIS) ^ 1
+    side = own_side(other, ON)
+    named = [lists[side, other * blocks + g] for g in range(blocks)]
+    least = functools.reduce(jnp.minimum, named)
     total[...] = jnp.zeros_like(total)
-    for g, slot in enumerate(slots_of(lists, blocks, ON)):
-        total[slot] += dot(signal[g], tiles[g, side], NN)
+    for g, value in enumerate(named):
+        total[(value != least).astype(jnp.int32)] += dot(signal[g], tiles[g, side], NN)
     push[...] = total[...].astype(BF16)
 
 
@@ -128,7 +132,7 @@
     out[...] = total
 
 
-def query_end_kernel(lists, part, received, embeddings, after, kept, sent, total, *, blocks):
+def query_end_kernel(lists, part, received, embeddings, after, kept, sent, total, *, blocks, rows):
     del after
     block = received.shape[2]
     first, second = named_by_partner(lists, blocks, OFF)
@@ -137,10 +141,11 @@
         + dot(received[0], block_rows(embeddings, first, block), NN)
         + dot(received[1], block_rows(embeddings, second, block), NN)
     )
-    rows = kept.shape[0]
     core = lax.axis_index(AXIS) % 2
-    kept[...] = total[pl.ds(pl.multiple_of(core * rows, rows), rows), :]
-    sent[...] = total[pl.ds(pl.multiple_of((1 - core) * rows, rows), rows), :]
+    for piece in range(kept.shape[0] // rows):
+        place = pl.ds(piece * rows, rows)
+        kept[place, :] = total[pl.ds(pl.multiple_of((2 * piece + core) * rows, rows), rows), :]
+        sent[place, :] = total[pl.ds(pl.multiple_of((2 * piece + 1 - core) * rows, rows), rows), :]
 
 
 def embed_kernel(lists, signal, received, queries, out, held, total, ready, sem, *, scale):
@@ -195,103 +200,43 @@
     )
 
 
-def digit_of(stride, radix):
-    return (lax.axis_index(AXIS) // stride) % radix
-
-
-def moved(i, stride, radix, step):
-    digit = (i // stride) % radix
-    return i + ((digit + step) % radix - digit) * stride
-
-
-def exchange(value, stride, radix, step):
+def exchange(value, mask):
     count = lax.axis_size(AXIS)
-    return lax.ppermute(value, AXIS, [(i, moved(i, stride, radix, step)) for i in range(count)])
-
-
-def split_kernel(*refs, stride, radix, arrived):
-    held, got = refs[0], refs[1 : 1 + arrived]
-    kept, sent = refs[1 + arrived], refs[2 + arrived : 1 + arrived + radix]
-    total = refs[-1]
-    value = held[...]
-    for ref in got:
-        value = value + ref[...].astype(F32)
-    total[...] = value
-    rows = kept.shape[0]
-    digit = digit_of(stride, radix)
-    kept[...] = total[pl.ds(pl.multiple_of(digit * rows, rows), rows), :]
-    for step, ref in enumerate(sent, 1):
-        place = (digit + step) % radix
-        ref[...] = total[pl.ds(pl.multiple_of(place * rows, rows), rows), :].astype(BF16)
-
-
-def finish_kernel(*refs, scale):
-    value = refs[0][...]
-    for ref in refs[1:-1]:
-        value = value + ref[...].astype(F32)
-    refs[-1][...] = (value * scale).astype(BF16)
-
-
-def join_kernel(*refs, stride, radix):
-    pieces, out = refs[:-1], refs[-1]
-    rows = pieces[0].shape[0]
-    digit = digit_of(stride, radix)
-    for step, ref in enumerate(pieces):
-        place = (digit + radix - step) % radix
-        out[pl.ds(pl.multiple_of(place * rows, rows), rows), :] = ref[...].astype(out.dtype)
-
-
-def stages_of(count, rows):
-    stages = []
-    stride, radix = 2, 2
-    while stride < count and count // stride % radix == 0 and rows % (16 * radix) == 0:
-        stages.append((stride, radix))
-        stride *= radix
-        rows //= radix
-        radix = 4 if radix == 2 else 2
-    return stages
+    return lax.ppermute(value, AXIS, [(i, i ^ mask) for i in range(count)])
+
+
+def finish_kernel(pieces, out, *, scale):
+    value = pieces[0].astype(F32)
+    for i in range(1, pieces.shape[0]):
+        value = value + pieces[i].astype(F32)
+    out[...] = (value * scale).astype(BF16)
+
+
+def piece_rows(count, rows):
+    return rows // count if rows % (16 * count) == 0 else 16
 
 
 def sum_queries(kept, sent, scale):
     count = lax.axis_size(AXIS)
     rows, width = kept.shape
-    stages = stages_of(count, rows)
-    got = [exchange(sent, 1, 2, 1)]
-    held = kept
-    for stride, radix in stages:
-        rows //= radix
-        piece = jax.ShapeDtypeStruct((rows, width), F32)
-        small = jax.ShapeDtypeStruct((rows, width), BF16)
-        held, *parts = call(
-            functools.partial(split_kernel, stride=stride, radix=radix, arrived=len(got)),
-            "split",
-            [VMEM] * (1 + len(got)),
-            [piece] + [small] * (radix - 1),
-            scratch=[pltpu.VMEM((rows * radix, width), F32)],
-        )(held, *got)
-        got = [exchange(part, stride, radix, step) for step, part in enumerate(parts, 1)]
-    done = math.prod(radix for _, radix in stages) * 2
-    if done < count:
-        for ref in got:
-            held = held + ref.astype(F32)
-        groups = [list(range(first, count, done)) for first in range(done)]
-        held, got = lax.psum(held, AXIS, axis_index_groups=groups), []
-    value = call(
+    chips = count // 2
+    groups = [list(range(core, count, 2)) for core in range(2)]
+    half = kept + exchange(sent, 1)
+    step = piece_rows(count, 2 * rows)
+    if step * chips != rows:
+        half = lax.psum(half, AXIS, axis_index_groups=groups) * scale
+        both = jnp.stack([half, exchange(half, 1)]).reshape(2, rows // step, step, width)
+        both = jnp.where(lax.axis_index(AXIS) % 2 == 0, both, both[::-1])
+        return both.swapaxes(0, 1).reshape(2 * rows, width)
+    half = half.astype(BF16).reshape(chips, step, width)
+    pieces = lax.all_to_all(half, AXIS, 0, 0, axis_index_groups=groups)
+    piece = call(
         functools.partial(finish_kernel, scale=scale),
         "finish",
-        [VMEM] * (1 + len(got)),
-        jax.ShapeDtypeStruct((rows, width), BF16),
-    )(held, *got)
-    for stride, radix in stages[::-1] + [(1, 2)]:
-        pieces = [value] + [exchange(value, stride, radix, step) for step in range(1, radix)]
-        rows *= radix
-        value = call(
-            functools.partial(join_kernel, stride=stride, radix=radix),
-            "join",
-            [VMEM] * radix,
-            jax.ShapeDtypeStruct((rows, width), F32 if stride == 1 else BF16),
-        )(*pieces)
-    return value
+        [VMEM],
+        jax.ShapeDtypeStruct((step, width), BF16),
+    )(pieces)
+    return lax.all_gather(piece, AXIS, axis=0, tiled=True).astype(F32)
 
 
 def per_device(embeddings, edge_tiles, neighbour, propensity, queries, positives):
@@ -307,39 +252,32 @@
         return lax.ppermute(value, AXIS, off_route)
 
     def on_swap(value):
-        return exchange(value, 1, 2, 1)
+        return exchange(value, 1)
 
     pair = jax.ShapeDtypeStruct((2, rows, block), BF16)
     pair_sum = pltpu.VMEM((2, rows, block), F32)
     full = jax.ShapeDtypeStruct((blocks, rows, block), F32)
     scale = 1.0 / math.sqrt(width)
 
-    def project(off, *after):
-        return call(
-            functools.partial(project_kernel, off=off, scale=scale),
-            "project_off" if off else "project_on",
-            [HBM] * 3 + [ANY] * len(after),
-            pair,
-            scratch=[
-                pltpu.SMEM(lists.shape, jnp.int32),
-                pltpu.VMEM((rows, width), BF16),
-                pltpu.VMEM((blocks, block, width), BF16),
-                pltpu.SemaphoreType.DMA((2 + blocks,)),
-            ],
-        )(*(pltpu.with_memory_space_constraint(x, pltpu.HBM) for x in (lists, queries, embeddings)), *after)
-
-    for_off = project(OFF)
+    own, for_off, for_on = call(
+        functools.partial(project_kernel, scale=scale),
+        "project",
+        [HBM] * 3,
+        [full, pair, pair],
+        scratch=[
+            pltpu.SMEM(lists.shape, jnp.int32),
+            pltpu.VMEM((rows, width), BF16),
+            pltpu.VMEM((blocks, block, width), BF16),
+            pltpu.SemaphoreType.DMA((2 + blocks,)),
+        ],
+    )(*(pltpu.with_memory_space_constraint(x, pltpu.HBM) for x in (lists, queries, embeddings)))
     from_off = off_swap(for_off)
-    from_on = on_swap(project(ON, for_off))
+    from_on = on_swap(for_on)
+    other_tiles = on_swap(edge_tiles)
     hits = call(
         hits_kernel, "hits", [VMEM, VMEM], full
     )(positives, propensity.reshape(1, labels_dev))
-    base = call(
-        functools.partial(base_kernel, scale=scale),
-        "base",
-        [SMEM] + [VMEM] * 4,
-        full,
-    )(lists, queries, embeddings, from_on, edge_tiles)
+    base = call(base_kernel, "base", [SMEM] + [VMEM] * 3, full)(lists, own, from_on, edge_tiles)
     signal, push_off = call(
         signal_kernel,
         "signal",
@@ -349,10 +287,10 @@
     )(lists, base, hits, from_off, edge_tiles)
 
     back_off = off_swap(push_off)
-    push_on = call(
-        push_kernel, "push", [SMEM, VMEM, VMEM], pair, scratch=[pair_sum]
-    )(lists, signal, edge_tiles)
-    back_on = on_swap(push_on)
+    other_signal = on_swap(signal)
+    back_on = call(push_kernel, "push", [SMEM, VMEM, VMEM], pair, scratch=[pair_sum])(
+        lists, other_signal, other_tiles
+    )
     part = call(
         query_kernel,
         "query",
@@ -377,7 +315,7 @@
 
     half = jax.ShapeDtypeStruct((rows // 2, width), F32)
     kept, sent = call(
-        functools.partial(query_end_kernel, blocks=blocks),
+        functools.partial(query_end_kernel, blocks=blocks, rows=piece_rows(count, rows)),
         "query_end",
         [SMEM] + [VMEM] * 3 + [ANY],
         [half, half],

time: 76 us -> 78.2 us (1.029)
  blocking collectives: 0 us -> 20 us
  waiting for transfers between devices: 17.5 us -> 7.1 us
  starting transfers between devices: 25.4 us -> 20.8 us
  Pallas kernels: 27.2 us -> 23.7 us
  other arithmetic: 0 us -> 1.65 us
  local copies, waits for them, and re-layouts: 4.59 us -> 3.64 us
    all_gather x0 -> x1, blocking collectives: none -> 20 us  [sum_queries(): return lax.all_gather(piece, AXIS, axis=0, tiled=True).astype(F32)]
    ppermute x12 -> x4, waiting for transfers between devices: 16.2 us -> 1.36 us  [exchange(): return lax.ppermute(value, AXIS, [(i, i ^ mask) for i in range(count)])]
    ppermute x12 -> x4, starting transfers between devices: 15.5 us -> 4.02 us  [exchange(): return lax.ppermute(value, AXIS, [(i, i ^ mask) for i in range(count)])]
    all_to_all x0 -> x1, starting transfers between devices: none -> 6.31 us  [sum_queries(): pieces = lax.all_to_all(half, AXIS, 0, 0, axis_index_groups=groups)]
    all_to_all x0 -> x1, waiting for transfers between devices: none -> 5.13 us  [sum_queries(): pieces = lax.all_to_all(half, AXIS, 0, 0, axis_index_groups=groups)]
    pallas_call x10 -> x4, Pallas kernels: 12.1 us -> 7.46 us  [the longest x1 3.94 us: per_device(): call(functools.partial(project_kernel, scale=scale), 'project', [HBM] * 3...]
    convert_element_type x0 -> x2, other arithmetic: none -> 1.65 us  [the longest x1 0.93 us: sum_queries(): return lax.all_gather(piece, AXIS, axis=0, tiled=True).astype(F32)]
    pallas_call x1, Pallas kernels: 1.4 us -> 3.02 us  [per_device(): call(push_kernel, 'push', [SMEM, VMEM, VMEM], pair, scratch=[pair_sum])]
  transfers between devices with their start and end apart: 14 -> 7, of which waited for: 10 -> 3; matrix products, arithmetic and copies ran while one was open for 2% -> 0% of each run, Pallas kernels for 18% -> 28%
where the time goes in v3:
time: 78.2 us; the launch traced here: 77.8 us
  Pallas kernels  23.7 us (30%)
  starting transfers between devices  20.8 us (27%)
  blocking collectives  20 us (26%)
  waiting for transfers between devices  7.1 us (9%)
  local copies, waits for them, and re-layouts  3.64 us (5%)
  other arithmetic  1.65 us (2%)
  between operations  0.83 us (1%)
    all_gather x1, blocking collectives, sum_queries(): return lax.all_gather(piece, AXIS, axis=0, tiled=True).astype(F32)  20 us
    ppermute x2, starting transfers between devices, off_swap(): return lax.ppermute(value, AXIS, off_route)  10.5 us
    all_to_all x1, starting transfers between devices, sum_queries(): pieces = lax.all_to_all(half, AXIS, 0, 0, axis_index_groups=groups)  6.31 us
    all_to_all x1, waiting for transfers between devices, sum_queries(): pieces = lax.all_to_all(half, AXIS, 0, 0, axis_index_groups=groups)  5.13 us
    ppermute x4, starting transfers between devices, exchange(): return lax.ppermute(value, AXIS, [(i, i ^ mask) for i in range(count)])  4.02 us
    pallas_call x1, Pallas kernels, per_device(): call(functools.partial(project_kernel, scale=scale), 'project', [HBM] * 3...  3.94 us
    pallas_call x1, Pallas kernels, per_device(): call(functools.partial(embed_kernel, scale=1.0 / math.sqrt(rows)), 'embed...  3.87 us
    unnamed x19, local copies, waits for them, and re-layouts  3.64 us
  transfers between devices with their start and end apart: 7, of which 3 were waited for; matrix products, arithmetic and copies ran while one was open for 0% of the time, Pallas kernels for 28%

profile of v3, /device:TPU:0, one launch (start us, length us, event | category | flops | bytes accessed | tf_op | source)
XLA Modules:
  0.0 77.8 jit_solution(12832133077453965117)
XLA Ops:
  0.7 0.5 collective-permute-start.3
  1.2 3.9 %project.1 = (f32[4,256,512]{2,1,0:T(8,128)S(1)}, bf16[2,256,512]{2,1,0:T(8,128)(2,1)}, bf16[2,256,512]{2,1,0:T(8,128)(2,1)}) custom-call(s32[2,64]{1,0:T(2,128)} %bitcast.3, bf16[256,768]{1,0:T(8,128)(2,1)} %queries.5, bf16[2048,768]{1,0:T(8,128)(2,1)} %embeddings.5), custom_call_target="tpu_custom_call" | custom-call | tf_op jit(solution)/shard_map/project/pallas_call | solution.py:262
  5.1 0.1 collective-permute-start
  5.2 5.7 %collective-permute-start.1 = (bf16[2,256,512]{2,1,0:T(8,128)(2,1)}, bf16[2,256,512]{2,1,0:T(8,128)(2,1)S(1)}, u32[]{:S(2)}, u32[]{:S(2)}) collective-permute-start(bf16[2,256,512]{2,1,0:T(8,128)(2,1)} %get-tuple-element.13), channel_id=1, source_target_pairs={{1,2},{3,4},{5,6},{7,8},{9,10},{11,12},{13,14},{15,0},{2,1},{4,3},... | collective-permute-start | bytes 1572872 | tf_op jit(solution)/shard_map/ppermute | solution.py:252
  10.9 0.1 copy.9.positives
  11.1 2.9 %hits.1 = f32[4,256,512]{2,1,0:T(8,128)S(1)} custom-call(s32[256,8]{1,0:T(8,128)S(1)} %copy.9.positives, f32[1,2048]{1,0:T(1,128)S(1)} %bitcast.11), custom_call_target="tpu_custom_call" | custom-call | tf_op jit(solution)/shard_map/hits/pallas_call | solution.py:277
  14.0 0.0 copy-start.1
  14.0 2.2 %copy-done.1 = bf16[4,2,512,512]{3,2,1,0:T(8,128)(2,1)S(1)} copy-done((bf16[4,2,512,512]{3,2,1,0:T(8,128)(2,1)S(1)}, bf16[4,2,512,512]{3,2,1,0:T(8,128)(2,1)}, u32[]{:S(2)}) %copy-start.1) | copy-done | bytes 4194328
  16.2 1.3 %base.1 = f32[4,256,512]{2,1,0:T(8,128)S(1)} custom-call(s32[2,64]{1,0:T(2,128)S(1)} %bitcast.4, f32[4,256,512]{2,1,0:T(8,128)S(1)} %get-tuple-element.11.own, bf16[2,256,512]{2,1,0:T(8,128)(2,1)S(1)} %collective-permute-done.received, bf16[4,2,512,512]{3,2,1,0:T(8,128)(2,1)S(1)} %copy-done.1), custom_call_target="tpu_custom_call" | custom-call | tf_op jit(solution)/shard_map/base/pallas_call | solution.py:280
  17.5 0.6 collective-permute-done.1.received
  18.1 0.3 copy-done.2
  18.4 2.4 %signal.1 = (bf16[4,256,512]{2,1,0:T(8,128)(2,1)S(1)}, bf16[2,256,512]{2,1,0:T(8,128)(2,1)S(1)}) custom-call(s32[2,64]{1,0:T(2,128)S(1)} %bitcast.5, f32[4,256,512]{2,1,0:T(8,128)S(1)} %base.1, f32[4,256,512]{2,1,0:T(8,128)S(1)} %hits.1, bf16[2,256,512]{2,1,0:T(8,128)(2,1)S(1)} %collective-permute-done.1.received, bf16[4,2,512,512]{3,2,1,0:T(8,128)(2,1)S(1)} %copy-done.2), custom_call_target="tpu_custom_call" | custom-call | tf_op jit(solution)/shard_map/signal/pallas_call | solution.py:281
  20.8 0.0 copy-start
  20.8 2.7 %collective-permute-start.2 = (bf16[4,256,512]{2,1,0:T(8,128)(2,1)S(1)}, bf16[4,256,512]{2,1,0:T(8,128)(2,1)S(1)}, u32[]{:S(2)}, u32[]{:S(2)}) collective-permute-start(bf16[4,256,512]{2,1,0:T(8,128)(2,1)S(1)} %get-tuple-element.14.signal), channel_id=1, source_target_pairs={{0,1},{1,0},{2,3},{3,2},{4,5},{5,4},{6,7},{7,6},{8,9},{9,8},{10,11... | collective-permute-start | bytes 3145736 | tf_op jit(solution)/shard_map/ppermute | solution.py:205
  23.5 4.8 %collective-permute-start.4 = (bf16[2,256,512]{2,1,0:T(8,128)(2,1)S(1)}, bf16[2,256,512]{2,1,0:T(8,128)(2,1)S(1)}, u32[]{:S(2)}, u32[]{:S(2)}) collective-permute-start(bf16[2,256,512]{2,1,0:T(8,128)(2,1)S(1)} %get-tuple-element.16), channel_id=1, source_target_pairs={{1,2},{3,4},{5,6},{7,8},{9,10},{11,12},{13,14},{15,0},{2,1},{4,3},... | collective-permute-start | bytes 1572872 | tf_op jit(solution)/shard_map/ppermute | solution.py:252
  28.3 3.0 %push.1.received = bf16[2,256,512]{2,1,0:T(8,128)(2,1)S(1)} custom-call(s32[2,64]{1,0:T(2,128)S(1)} %bitcast.6, bf16[4,256,512]{2,1,0:T(8,128)(2,1)S(1)} %collective-permute-done.2.signal, bf16[4,2,512,512]{3,2,1,0:T(8,128)(2,1)} %collective-permute-done.3.tiles), custom_call_target="tpu_custom_call" | custom-call | tf_op jit(solution)/shard_map/push/pallas_call | solution.py:291
  31.3 0.0 copy-start.3
  31.3 1.9 %query.1.part = f32[256,768]{1,0:T(8,128)S(1)} custom-call(s32[2,64]{1,0:T(2,128)S(1)} %bitcast.7, bf16[4,256,512]{2,1,0:T(8,128)(2,1)S(1)} %get-tuple-element.14.signal, bf16[2,256,512]{2,1,0:T(8,128)(2,1)S(1)} %push.1.received, bf16[2048,768]{1,0:T(8,128)(2,1)S(1)} %copy-done), custom_call_target="tpu_custom_call" | custom-call | tf_op jit(solution)/shard_map/query/pallas_call | solution.py:294
  33.3 3.9 %embed.1 = (bf16[2048,768]{1,0:T(8,128)(2,1)}, f32[2,512,768]{2,1,0:T(8,128)S(1)}) custom-call(s32[2,64]{1,0:T(2,128)S(1)} %bitcast.8, bf16[4,256,512]{2,1,0:T(8,128)(2,1)S(1)} %get-tuple-element.14.signal, bf16[2,256,512]{2,1,0:T(8,128)(2,1)S(1)} %push.1.received, bf16[256,768]{1,0:T(8,128)(2,1)S(1)} %copy-done.3), custom_call_target="tpu_custom_call" | custom-call | tf_op jit(solution)/shard_map/embed/pallas_call | solution.py:300
  37.1 0.0 collective-permute-done.4.received
  37.1 0.0 copy-start.4
  37.2 1.3 %query_end.1 = (f32[128,768]{1,0:T(8,128)S(1)}, f32[128,768]{1,0:T(8,128)S(1)}) custom-call(s32[2,64]{1,0:T(2,128)S(1)} %bitcast.9, f32[256,768]{1,0:T(8,128)S(1)} %query.1.part, bf16[2,256,512]{2,1,0:T(8,128)(2,1)S(1)} %collective-permute-done.4.received, bf16[2048,768]{1,0:T(8,128)(2,1)S(1)} %copy-done, f32[2,512,768]{2,1,0:T(8,128)S(1)} %get-tuple-element.15.held.after), custom_call_target="tpu_custom_call" | custom-call | tf_op jit(solution)/shard_map/query_end/pallas_call | solution.py:317
  38.4 0.7 collective-permute-start.5
  39.1 1.3 %collective-permute-done.5 = f32[128,768]{1,0:T(8,128)S(1)} collective-permute-done((f32[128,768]{1,0:T(8,128)S(1)}, f32[128,768]{1,0:T(8,128)S(1)}, u32[]{:S(2)}, u32[]{:S(2)}) %collective-permute-start.5) | collective-permute-done | bytes 393248 | tf_op jit(solution)/shard_map/ppermute | solution.py:205
  40.5 0.7 add_convert_fusion
  41.2 6.3 %all-to-all-start = ((bf16[8,16,768]{2,1,0:T(8,128)(2,1)}), bf16[8,16,768]{2,1,0:T(8,128)(2,1)}, u32[]{:S(2)}, u32[]{:S(2)}) async-start(bf16[8,16,768]{2,1,0:T(8,128)(2,1)} %bitcast.12), calls=%async_computation | async-start | bytes 393216 | tf_op jit(solution)/shard_map/all_to_all | solution.py:232
  47.5 1.0 %copy-done.5 = bf16[2,256,512]{2,1,0:T(8,128)(2,1)S(1)} copy-done((bf16[2,256,512]{2,1,0:T(8,128)(2,1)S(1)}, bf16[2,256,512]{2,1,0:T(8,128)(2,1)}, u32[]{:S(2)}) %copy-start.5) | copy-done | bytes 524312
  48.5 2.2 %embed_end.1 = bf16[2048,768]{1,0:T(8,128)(2,1)} custom-call(s32[2,64]{1,0:T(2,128)S(1)} %bitcast.10, f32[2,512,768]{2,1,0:T(8,128)S(1)} %get-tuple-element.15.held.after, bf16[2,256,512]{2,1,0:T(8,128)(2,1)S(1)} %copy-done.5, bf16[256,768]{1,0:T(8,128)(2,1)S(1)} %copy-done.3, bf16[2048,768]{1,0:T(8,128)(2,1)} %get-tuple-element.17.old), custom_call_target="tpu_custom_call", output_to_operand_aliasing={{}: (4, {})} | custom-call | tf_op jit(solution)/shard_map/embed_end/pallas_call | solution.py:324
  50.7 5.1 %all-to-all-done.pieces = bf16[8,16,768]{2,1,0:T(8,128)(2,1)} async-done(((bf16[8,16,768]{2,1,0:T(8,128)(2,1)}), bf16[8,16,768]{2,1,0:T(8,128)(2,1)}, u32[]{:S(2)}, u32[]{:S(2)}) %all-to-all-start) | async-done | bytes 196640 | tf_op jit(solution)/shard_map/all_to_all | solution.py:232
  55.9 1.0 %finish.1 = bf16[16,768]{1,0:T(8,128)(2,1)S(1)} custom-call(bf16[8,16,768]{2,1,0:T(8,128)(2,1)} %all-to-all-done.pieces), custom_call_target="tpu_custom_call" | custom-call | tf_op jit(solution)/shard_map/finish/pallas_call | solution.py:233
  56.8 20.0 %all_gather.3 = bf16[256,768]{1,0:T(8,128)(2,1)S(1)} all-gather(bf16[16,768]{1,0:T(8,128)(2,1)S(1)} %finish.1), channel_id=1, replica_groups=mesh['groups'=2,'labels'=16] {'labels'}, dimensions={0}, use_global_device_ids=true | all-gather | bytes 417792 | tf_op jit(solution)/shard_map/all_gather | solution.py:239
  76.9 0.9 %convert_element_type.7 = f32[256,768]{1,0:T(8,128)} convert(bf16[256,768]{1,0:T(8,128)(2,1)S(1)} %all_gather.3) | non-fusion elementwise | flops 196608 | bytes 1179648 | tf_op jit(solution)/shard_map/convert_element_type | solution.py:239
  (14 shorter events, 0.0 us)
Async XLA Ops:
  0.6 13.4 %copy-start.6 = (s32[64,2]{0,1:T(2,128)S(1)}, s32[64,2]{0,1:T(2,128)}, u32[]{:S(2)}) copy-start(s32[64,2]{0,1:T(2,128)} %param.8) | copy-start | bytes 1540
  0.6 10.3 %copy-start.8 = (s32[256,8]{0,1:T(8,128)S(1)}, s32[256,8]{0,1:T(8,128)}, u32[]{:S(2)}) copy-start(s32[256,8]{0,1:T(8,128)} %param.11) | copy-start | bytes 24580
  0.7 10.4 %copy-start.7 = (f32[2048]{0:T(1024)S(1)}, f32[2048]{0:T(1024)}, u32[]{:S(2)}) copy-start(f32[2048]{0:T(1024)} %param.9) | copy-start | bytes 24580
  0.7 27.6 %collective-permute-start.3 = (bf16[4,2,512,512]{3,2,1,0:T(8,128)(2,1)}, bf16[4,2,512,512]{3,2,1,0:T(8,128)(2,1)}, u32[]{:S(2)}, u32[]{:S(2)}) collective-permute-start(bf16[4,2,512,512]{3,2,1,0:T(8,128)(2,1)} %tiles.3), channel_id=1, source_target_pairs={{0,1},{1,0},{2,3},{3,2},{4,5},{5,4},{6,7},{7,6},{8,9},{9,8},{10,11... | collective-permute-start | bytes 12582920 | tf_op jit(solution)/shard_map/ppermute | solution.py:205
  5.1 8.9 %collective-permute-start = (bf16[2,256,512]{2,1,0:T(8,128)(2,1)}, bf16[2,256,512]{2,1,0:T(8,128)(2,1)S(1)}, u32[]{:S(2)}, u32[]{:S(2)}) collective-permute-start(bf16[2,256,512]{2,1,0:T(8,128)(2,1)} %get-tuple-element.12), channel_id=1, source_target_pairs={{0,1},{1,0},{2,3},{3,2},{4,5},{5,4},{6,7},{7,6},{8,9},{9,8},{10,11... | collective-permute-start | bytes 1572872 | tf_op jit(solution)/shard_map/ppermute | solution.py:205
  5.2 12.9 %collective-permute-start.1 = (bf16[2,256,512]{2,1,0:T(8,128)(2,1)}, bf16[2,256,512]{2,1,0:T(8,128)(2,1)S(1)}, u32[]{:S(2)}, u32[]{:S(2)}) collective-permute-start(bf16[2,256,512]{2,1,0:T(8,128)(2,1)} %get-tuple-element.13), channel_id=1, source_target_pairs={{1,2},{3,4},{5,6},{7,8},{9,10},{11,12},{13,14},{15,0},{2,1},{4,3},... | collective-permute-start | bytes 1572872 | tf_op jit(solution)/shard_map/ppermute | solution.py:252
  14.0 2.2 %copy-start.1 = (bf16[4,2,512,512]{3,2,1,0:T(8,128)(2,1)S(1)}, bf16[4,2,512,512]{3,2,1,0:T(8,128)(2,1)}, u32[]{:S(2)}) copy-start(bf16[4,2,512,512]{3,2,1,0:T(8,128)(2,1)} %tiles.3) | copy-start | bytes 12582916
  16.2 2.2 %copy-start.2 = (bf16[4,2,512,512]{3,2,1,0:T(8,128)(2,1)S(1)}, bf16[4,2,512,512]{3,2,1,0:T(8,128)(2,1)}, u32[]{:S(2)}) copy-start(bf16[4,2,512,512]{3,2,1,0:T(8,128)(2,1)} %tiles.3) | copy-start | bytes 12582916
  20.8 10.5 %copy-start = (bf16[2048,768]{1,0:T(8,128)(2,1)S(1)}, bf16[2048,768]{1,0:T(8,128)(2,1)}, u32[]{:S(2)}) copy-start(bf16[2048,768]{1,0:T(8,128)(2,1)} %embeddings.5) | copy-start | bytes 9437188
  20.8 7.5 %collective-permute-start.2 = (bf16[4,256,512]{2,1,0:T(8,128)(2,1)S(1)}, bf16[4,256,512]{2,1,0:T(8,128)(2,1)S(1)}, u32[]{:S(2)}, u32[]{:S(2)}) collective-permute-start(bf16[4,256,512]{2,1,0:T(8,128)(2,1)S(1)} %get-tuple-element.14.signal), channel_id=1, source_target_pairs={{0,1},{1,0},{2,3},{3,2},{4,5},{5,4},{6,7},{7,6},{8,9},{9,8},{10,11... | collective-permute-start | bytes 3145736 | tf_op jit(solution)/shard_map/ppermute | solution.py:205
  23.5 13.7 %collective-permute-start.4 = (bf16[2,256,512]{2,1,0:T(8,128)(2,1)S(1)}, bf16[2,256,512]{2,1,0:T(8,128)(2,1)S(1)}, u32[]{:S(2)}, u32[]{:S(2)}) collective-permute-start(bf16[2,256,512]{2,1,0:T(8,128)(2,1)S(1)} %get-tuple-element.16), channel_id=1, source_target_pairs={{1,2},{3,4},{5,6},{7,8},{9,10},{11,12},{13,14},{15,0},{2,1},{4,3},... | collective-permute-start | bytes 1572872 | tf_op jit(solution)/shard_map/ppermute | solution.py:252
  31.3 2.0 %copy-start.3 = (bf16[256,768]{1,0:T(8,128)(2,1)S(1)}, bf16[256,768]{1,0:T(8,128)(2,1)}, u32[]{:S(2)}) copy-start(bf16[256,768]{1,0:T(8,128)(2,1)} %queries.5) | copy-start | bytes 1179652
  37.1 1.3 %copy-start.4 = (bf16[2,256,512]{2,1,0:T(8,128)(2,1)}, bf16[2,256,512]{2,1,0:T(8,128)(2,1)S(1)}, u32[]{:S(2)}) copy-start(bf16[2,256,512]{2,1,0:T(8,128)(2,1)S(1)} %collective-permute-done.4.received) | copy-start | bytes 1572868
  38.4 2.0 %collective-permute-start.5 = (f32[128,768]{1,0:T(8,128)S(1)}, f32[128,768]{1,0:T(8,128)S(1)}, u32[]{:S(2)}, u32[]{:S(2)}) collective-permute-start(f32[128,768]{1,0:T(8,128)S(1)} %get-tuple-element.19), channel_id=1, source_target_pairs={{0,1},{1,0},{2,3},{3,2},{4,5},{5,4},{6,7},{7,6},{8,9},{9,8},{10,11... | collective-permute-start | bytes 1179656 | tf_op jit(solution)/shard_map/ppermute | solution.py:205
  41.2 14.7 %all-to-all-start = ((bf16[8,16,768]{2,1,0:T(8,128)(2,1)}), bf16[8,16,768]{2,1,0:T(8,128)(2,1)}, u32[]{:S(2)}, u32[]{:S(2)}) async-start(bf16[8,16,768]{2,1,0:T(8,128)(2,1)} %bitcast.12), calls=%async_computation | async-start | bytes 393216 | tf_op jit(solution)/shard_map/all_to_all | solution.py:232
  47.5 1.0 %copy-start.5 = (bf16[2,256,512]{2,1,0:T(8,128)(2,1)S(1)}, bf16[2,256,512]{2,1,0:T(8,128)(2,1)}, u32[]{:S(2)}) copy-start(bf16[2,256,512]{2,1,0:T(8,128)(2,1)} %copy-done.4) | copy-start | bytes 1572868

commit v4 on v3

v4 whole, which is shorter than its diff:
```python
import functools
import math

import jax
import jax.numpy as jnp
from jax import lax
from jax.experimental import pallas as pl
from jax.experimental.pallas import tpu as pltpu
from jax.sharding import PartitionSpec as P

AXIS = "labels"
BF16 = jnp.bfloat16
F32 = jnp.float32
NT = (((1,), (1,)), ((), ()))
NN = (((1,), (0,)), ((), ()))
TN = (((0,), (0,)), ((), ()))
MIB = 1024 * 1024

OFF, ON = True, False


def dot(a, b, dims):
    return lax.dot_general(a, b, dims, preferred_element_type=F32)


def own_side(device, off):
    odd = device % 2
    return 1 - odd if off else odd


def partner_of(device, count, off):
    ahead = jnp.where(device == count - 1, 0, device + 1)
    behind = jnp.where(device == 0, count - 1, device - 1)
    return jnp.where(own_side(device, off) == 0, ahead, behind)


def own_list(lists, blocks, off):
    device = lax.axis_index(AXIS)
    side = own_side(device, off)
    return [lists[side, device * blocks + g] for g in range(blocks)]


def slots_of(lists, blocks, off):
    named = own_list(lists, blocks, off)
    least = functools.reduce(jnp.minimum, named)
    return [(value != least).astype(jnp.int32) for value in named]


def named_by_partner(lists, blocks, off):
    device = lax.axis_index(AXIS)
    partner = partner_of(device, lax.axis_size(AXIS), off)
    side = 1 - own_side(device, off)
    named = [lists[side, partner * blocks + g] for g in range(blocks)]
    return functools.reduce(jnp.minimum, named), functools.reduce(jnp.maximum, named)


def tile_side(off):
    return own_side(lax.axis_index(AXIS), off)


def block_rows(ref, index, block):
    return ref[pl.ds(pl.multiple_of(index * block, block), block), :]


def project_kernel(lists, queries, embeddings, own, for_off_a, for_off_b, for_on, table, left, right, sem, *, scale):
    blocks, _, block = own.shape
    half = for_off_a.shape[1]
    fetches = [pltpu.make_async_copy(lists, table, sem.at[0]), pltpu.make_async_copy(queries, left, sem.at[1])]
    for g in range(blocks):
        fetches.append(pltpu.make_async_copy(embeddings.at[pl.ds(g * block, block), :], right.at[g], sem.at[2 + g]))
    for fetch in fetches:
        fetch.start()
    for fetch in fetches[:2]:
        fetch.wait()
    for g in range(blocks):
        fetches[2 + g].wait()
        own[g] = dot(left[...], right[g], NT) * scale
    for slot, index in enumerate(named_by_partner(table, blocks, OFF)):
        for_off_a[slot] = own[index, :half].astype(BF16)
        for_off_b[slot] = own[index, half:].astype(BF16)
    for slot, index in enumerate(named_by_partner(table, blocks, ON)):
        for_on[slot] = own[index].astype(BF16)


def hits_kernel(positives, propensity, out):
    blocks, rows, block = out.shape
    first = lax.axis_index(AXIS) * blocks * block
    ids = lax.broadcasted_iota(jnp.int32, (rows, block), 1)
    inverse = 1.0 / propensity[...]
    for g in range(blocks):
        hits = jnp.zeros((rows, block), jnp.bool_)
        for column in range(positives.shape[1]):
            hits = jnp.logical_or(hits, ids == positives[:, column : column + 1] - (first + g * block))
        out[g] = jnp.where(hits, inverse[:, g * block : (g + 1) * block], 0.0)


def base_kernel(lists, own, received, tiles, out):
    blocks = out.shape[0]
    side = tile_side(ON)
    for g, slot in enumerate(slots_of(lists, blocks, ON)):
        out[g] = own[g] + dot(received[slot], tiles[g, side], NT)


def signal_kernel(lists, base, hits, received, tiles, *rest, first):
    signal, push_off, push_on, total_off, total_on = rest[-5:]
    blocks = base.shape[0]
    rows = slice(first, first + received.shape[1])
    side_off, side_on = tile_side(OFF), tile_side(ON)
    slots_on = slots_of(lists, blocks, ON)
    total_off[...] = jnp.zeros_like(total_off)
    total_on[...] = jnp.zeros_like(total_on)
    for g, slot in enumerate(slots_of(lists, blocks, OFF)):
        scores = base[g, rows] + dot(received[slot], tiles[g, side_off], NT)
        value = (jax.nn.sigmoid(scores) - hits[g, rows]).astype(BF16)
        signal[g, rows] = value
        total_off[slot] += dot(value, tiles[g, side_off], NN)
        total_on[slots_on[g]] += dot(value, tiles[g, side_on], NN)
    push_off[...] = total_off[...].astype(BF16)
    push_on[...] = total_on[...].astype(BF16)


def query_kernel(signal, embeddings, out):
    blocks, _, block = signal.shape
    total = dot(signal[0], embeddings[0:block, :], NN)
    for g in range(1, blocks):
        total += dot(signal[g], embeddings[g * block : (g + 1) * block, :], NN)
    out[...] = total


def query_on_kernel(lists, received_a, received_b, embeddings, after, out, *, blocks):
    del after
    half, block = received_a.shape[1:]
    first, second = named_by_partner(lists, blocks, ON)
    left, right = block_rows(embeddings, first, block), block_rows(embeddings, second, block)
    for rows, received in ((slice(0, half), received_a), (slice(half, 2 * half), received_b)):
        out[rows, :] = dot(received[0], left, NN) + dot(received[1], right, NN)


def query_half_kernel(lists, part, received, embeddings, after, out, *, blocks):
    del after
    half, block = received.shape[1:]
    first, second = named_by_partner(lists, blocks, OFF)
    left, right = block_rows(embeddings, first, block), block_rows(embeddings, second, block)
    out[...] = part[:half, :] + dot(received[0], left, NN) + dot(received[1], right, NN)


def query_end_kernel(lists, part, part_on, received, embeddings, other, kept, sent, *, blocks):
    half, block = received.shape[1:]
    first, second = named_by_partner(lists, blocks, OFF)
    left, right = block_rows(embeddings, first, block), block_rows(embeddings, second, block)
    value = part[half:, :] + part_on[half:, :] + dot(received[0], left, NN) + dot(received[1], right, NN)
    above = other[...] + part_on[:half, :]
    upper = lax.axis_index(AXIS) % 2 == 0
    kept[...] = jnp.where(upper, above, value)
    sent[...] = jnp.where(upper, value, above)


def embed_kernel(signal, queries, out):
    for g in range(signal.shape[0]):
        out[g] = dot(signal[g], queries[...], TN)


def embed_end_kernel(lists, part, on_a, on_b, off_a, off_b, queries, *rest, blocks, first, last, scale):
    out, token, total, ready, sem = rest[-5:]
    block = part.shape[1]
    half = off_a.shape[1]
    token[...] = jnp.zeros_like(token)
    for g in range(first, last):
        total[g - first] = part[g]
    for slot, index in enumerate(named_by_partner(lists, blocks, ON)):

        @pl.when(jnp.logical_and(index >= first, index < last))
        def _():
            total[index - first] += dot(on_a[slot], queries[:half, :], TN) + dot(on_b[slot], queries[half:, :], TN)

    for slot, index in enumerate(named_by_partner(lists, blocks, OFF)):

        @pl.when(jnp.logical_and(index >= first, index < last))
        def _():
            total[index - first] += dot(off_a[slot], queries[:half, :], TN) + dot(off_b[slot], queries[half:, :], TN)

    copies = []
    for g in range(first, last):
        ready[g - first] = (total[g - first] * scale).astype(BF16)
        place = out.at[pl.ds(g * block, block), :]
        copies.append(pltpu.make_async_copy(ready.at[g - first], place, sem.at[g - first]))
        copies[-1].start()
    for copy in copies:
        copy.wait()


VMEM = pl.BlockSpec(memory_space=pltpu.VMEM)
SMEM = pl.BlockSpec(memory_space=pltpu.SMEM)
ANY = pl.BlockSpec(memory_space=pl.ANY)
HBM = pl.BlockSpec(memory_space=pltpu.HBM)


def call(kernel, name, in_specs, out_shape, out_specs=None, scratch=(), aliases=None, vmem=12, flops=0):
    if out_specs is None:
        out_specs = jax.tree.map(lambda _: VMEM, out_shape)
    return pl.pallas_call(
        kernel,
        in_specs=in_specs,
        out_specs=out_specs,
        out_shape=out_shape,
        scratch_shapes=scratch,
        input_output_aliases=aliases or {},
        name=name,
        cost_estimate=pl.CostEstimate(flops=flops, bytes_accessed=0, transcendentals=0),
        compiler_params=pltpu.CompilerParams(vmem_limit_bytes=vmem * MIB),
    )


def exchange(value, mask):
    count = lax.axis_size(AXIS)
    return lax.ppermute(value, AXIS, [(i, i ^ mask) for i in range(count)])


def halve_kernel(held, got, kept, sent, *, bit):
    rows = kept.shape[0]
    digit = (lax.axis_index(AXIS) // bit) % 2
    here = pl.ds(pl.multiple_of(digit * rows, rows), rows)
    there = pl.ds(pl.multiple_of((1 - digit) * rows, rows), rows)
    kept[...] = held[here, :] + got[here, :]
    sent[...] = (held[there, :] + got[there, :]).astype(BF16)


def add_kernel(held, got, *rest, scale):
    rest[-1][...] = ((held[...].astype(F32) + got[...].astype(F32)) * scale).astype(BF16)


def join_kernel(held, got, out, *, bit):
    rows = held.shape[0]
    digit = (lax.axis_index(AXIS) // bit) % 2
    out[pl.ds(pl.multiple_of(digit * rows, rows), rows), :] = held[...].astype(out.dtype)
    out[pl.ds(pl.multiple_of((1 - digit) * rows, rows), rows), :] = got[...].astype(out.dtype)


def sum_queries(kept, sent, beside, scale):
    count = lax.axis_size(AXIS)
    rows, width = kept.shape
    got = exchange(sent, 1)
    if count & (count - 1) or count < 4:
        half = lax.psum(kept + got, AXIS, axis_index_groups=[list(range(c, count, 2)) for c in range(2)])
        both = jnp.stack([half, exchange(half, 1)])
        both = jnp.where(lax.axis_index(AXIS) % 2 == 0, both, both[::-1])
        return both.reshape(2 * rows, width) * scale
    piece = jax.ShapeDtypeStruct((rows // 2, width), BF16)
    held, sent = call(
        functools.partial(halve_kernel, bit=2),
        "halve",
        [VMEM] * 2,
        [jax.ShapeDtypeStruct(piece.shape, F32), piece],
    )(kept, got)
    got = exchange(sent, 2)
    bits = [1 << k for k in range(2, count.bit_length() - 1)]
    for k in range(len(bits) + 1):
        last = k == len(bits)
        after = beside[k : k + 1]
        held = call(
            functools.partial(add_kernel, scale=scale if last else 1.0),
            "add",
            [VMEM] * 2 + [ANY] * len(after),
            piece,
        )(held, got, *after)
        if not last:
            got = exchange(held, bits[k])
    for bit in (2, 1):
        rows_out = held.shape[0] * 2
        held = call(
            functools.partial(join_kernel, bit=bit),
            "join",
            [VMEM] * 2,
            jax.ShapeDtypeStruct((rows_out, width), F32 if bit == 1 else BF16),
        )(held, exchange(held, bit))
    return held


def per_device(embeddings, edge_tiles, neighbour, propensity, queries, positives):
    count = lax.axis_size(AXIS)
    blocks, _, block, _ = edge_tiles.shape
    labels_dev, width = embeddings.shape
    rows = queries.shape[0]
    lists = neighbour.T
    odd = range(1, count, 2)
    off_route = [(i, (i + 1) % count) for i in odd] + [((i + 1) % count, i) for i in odd]

    def off_swap(value):
        return lax.ppermute(value, AXIS, off_route)

    def on_swap(value):
        return exchange(value, 1)

    pair = jax.ShapeDtypeStruct((2, rows, block), BF16)
    pair_sum = pltpu.VMEM((2, rows, block), F32)
    full = jax.ShapeDtypeStruct((blocks, rows, block), F32)
    scale = 1.0 / math.sqrt(width)

    half = jax.ShapeDtypeStruct((2, rows // 2, block), BF16)
    own, for_off_a, for_off_b, for_on = call(
        functools.partial(project_kernel, scale=scale),
        "project",
        [HBM] * 3,
        [full, half, half, pair],
        scratch=[
            pltpu.SMEM(lists.shape, jnp.int32),
            pltpu.VMEM((rows, width), BF16),
            pltpu.VMEM((blocks, block, width), BF16),
            pltpu.SemaphoreType.DMA((2 + blocks,)),
        ],
        vmem=12,
    )(*(pltpu.with_memory_space_constraint(x, pltpu.HBM) for x in (lists, queries, embeddings)))
    from_off_a = off_swap(for_off_a)
    from_off_b = off_swap(for_off_b)
    from_on = on_swap(for_on)
    hits = call(hits_kernel, "hits", [VMEM, VMEM], full)(positives, propensity.reshape(1, labels_dev))
    base = call(base_kernel, "base", [SMEM] + [VMEM] * 3, full)(lists, own, from_on, edge_tiles)

    def signal_of(received, first, *begun):
        return call(
            functools.partial(signal_kernel, first=first),
            "signal",
            [SMEM] + [VMEM] * 4 + [ANY] * len(begun),
            [jax.ShapeDtypeStruct(full.shape, BF16), half, half],
            scratch=[pltpu.VMEM(half.shape, F32)] * 2,
            aliases={5: 0} if begun else None,
        )(lists, base, hits, received, edge_tiles, *begun)

    signal, push_a, push_on_a = signal_of(from_off_a, 0)
    back_a = off_swap(push_a)
    signal, push_b, push_on_b = signal_of(from_off_b, rows // 2, signal)
    back_b = off_swap(push_b)
    on_a, on_b = on_swap(push_on_a), on_swap(push_on_b)
    part = call(query_kernel, "query", [VMEM] * 2, jax.ShapeDtypeStruct((rows, width), F32))(signal, embeddings)
    embed = call(embed_kernel, "embed", [VMEM] * 2, jax.ShapeDtypeStruct((blocks, block, width), F32))(
        signal, queries
    )
    piece = jax.ShapeDtypeStruct((rows // 2, width), F32)
    upper = call(
        functools.partial(query_half_kernel, blocks=blocks), "query_half", [SMEM] + [VMEM] * 3 + [ANY], piece, flops=10**9
    )(lists, part, back_a, embeddings, embed)
    part_on = call(
        functools.partial(query_on_kernel, blocks=blocks),
        "query_on",
        [SMEM] + [VMEM] * 3 + [ANY],
        jax.ShapeDtypeStruct((rows, width), F32),
    )(lists, on_a, on_b, embeddings, upper)
    kept, sent = call(
        functools.partial(query_end_kernel, blocks=blocks), "query_end", [SMEM] + [VMEM] * 5, [piece, piece]
    )(lists, part, part_on, back_b, embeddings, upper)

    def embed_end(first, last, *begun):
        return call(
            functools.partial(
                embed_end_kernel, blocks=blocks, first=first, last=last, scale=1.0 / math.sqrt(rows)
            ),
            "embed_end",
            [SMEM] + [VMEM] * 6 + [ANY] * len(begun),
            [jax.ShapeDtypeStruct((labels_dev, width), BF16), jax.ShapeDtypeStruct((8, 128), F32)],
            out_specs=[ANY, VMEM],
            scratch=[
                pltpu.VMEM((last - first, block, width), F32),
                pltpu.VMEM((last - first, block, width), BF16),
                pltpu.SemaphoreType.DMA((last - first,)),
            ],
            aliases={7: 0} if begun else None,
            vmem=16,
        )(lists, embed, on_a, on_b, back_a, back_b, queries, *begun)

    begun, token_a = embed_end(0, blocks // 2)
    grad_embed, token_b = embed_end(blocks // 2, blocks, begun)
    grad_queries = sum_queries(kept, sent, [token_a, token_b], 1.0 / math.sqrt(labels_dev * count))
    return (grad_embed, grad_queries)


def solution(mesh):
    placed = (
        P("labels", None),
        P("labels", None, None, None),
        P(),
        P("labels"),
        P("groups", None),
        P("groups", None),
    )
    return jax.shard_map(
        per_device,
        mesh=mesh,
        in_specs=placed,
        out_specs=(P(("groups", "labels"), None), P("groups", None)),
        check_vma=False,
    )
```

time: 78.2 us -> 64.4 us (0.82)
  blocking collectives: 20 us -> 0 us
  waiting for transfers between devices: 7.1 us -> 19 us
  starting transfers between devices: 20.8 us -> 14.7 us
  Pallas kernels: 23.7 us -> 26.1 us
  other arithmetic: 1.65 us -> 0 us
    all_gather x1 -> x0, blocking collectives: 20 us -> none  [sum_queries(): return lax.all_gather(piece, AXIS, axis=0, tiled=True).astype(F32)]
    ppermute x4 -> x9, waiting for transfers between devices: 1.36 us -> 14.6 us  [exchange(): return lax.ppermute(value, AXIS, [(i, i ^ mask) for i in range(count)])]
    all_to_all x1 -> x0, starting transfers between devices: 6.31 us -> none  [sum_queries(): pieces = lax.all_to_all(half, AXIS, 0, 0, axis_index_groups=groups)]
    all_to_all x1 -> x0, waiting for transfers between devices: 5.13 us -> none  [sum_queries(): pieces = lax.all_to_all(half, AXIS, 0, 0, axis_index_groups=groups)]
    ppermute x2 -> x4, waiting for transfers between devices: 0.62 us -> 4.39 us  [off_swap(): return lax.ppermute(value, AXIS, off_route)]
    pallas_call x7 -> x15, Pallas kernels: 15.6 us -> 18 us  [the longest x2 6.6 us: embed_end(): call(functools.partial(embed_end_kernel, blocks=blocks, first=first, last...]
    convert_element_type x2 -> x0, other arithmetic: 1.65 us -> none  [the longest x1 0.93 us: sum_queries(): return lax.all_gather(piece, AXIS, axis=0, tiled=True).astype(F32)]
    ppermute x4 -> x9, starting transfers between devices: 4.02 us -> 4.48 us  [exchange(): return lax.ppermute(value, AXIS, [(i, i ^ mask) for i in range(count)])]
  transfers between devices with their start and end apart: 7 -> 13, of which waited for: 3 -> 7; matrix products, arithmetic and copies ran while one was open for 0% -> 1% of each run, Pallas kernels for 28% -> 31%
where the time goes in v4:
time: 64.4 us; the launch traced here: 64.5 us
  Pallas kernels  26.1 us (41%)
  waiting for transfers between devices  19 us (30%)
  starting transfers between devices  14.7 us (23%)
  local copies, waits for them, and re-layouts  3.84 us (6%)
  between operations  0.88 us (1%)
    ppermute x9, waiting for transfers between devices, exchange(): return lax.ppermute(value, AXIS, [(i, i ^ mask) for i in range(count)])  14.6 us
    ppermute x4, starting transfers between devices, off_swap(): return lax.ppermute(value, AXIS, off_route)  10.2 us
    pallas_call x2, Pallas kernels, embed_end(): call(functools.partial(embed_end_kernel, blocks=blocks, first=first, last...  6.6 us
    pallas_call x2, Pallas kernels, signal_of(): call(functools.partial(signal_kernel, first=first), 'signal', [SMEM] + [V...  5.23 us
    ppermute x9, starting transfers between devices, exchange(): return lax.ppermute(value, AXIS, [(i, i ^ mask) for i in range(count)])  4.48 us
    ppermute x4, waiting for transfers between devices, off_swap(): return lax.ppermute(value, AXIS, off_route)  4.39 us
    pallas_call x1, Pallas kernels, per_device(): call(functools.partial(project_kernel, scale=scale), 'project', [HBM] * 3...  3.86 us
    unnamed x13, local copies, waits for them, and re-layouts  3.84 us
  transfers between devices with their start and end apart: 13, of which 7 were waited for; matrix products, arithmetic and copies ran while one was open for 1% of the time, Pallas kernels for 31%

profile of v4, /device:TPU:0, one launch (start us, length us, event | category | flops | bytes accessed | tf_op | source)
XLA Modules:
  0.0 64.5 jit_solution(9922280226894268082)
XLA Ops:
  0.6 3.9 %project.1 = (f32[4,256,512]{2,1,0:T(8,128)S(1)}, bf16[2,128,512]{2,1,0:T(8,128)(2,1)}, bf16[2,128,512]{2,1,0:T(8,128)(2,1)S(1)}, bf16[2,256,512]{2,1,0:T(8,128)(2,1)}) custom-call(s32[2,64]{1,0:T(2,128)} %bitcast.2, bf16[256,768]{1,0:T(8,128)(2,1)} %queries.7, bf16[2048,768]{1,0:T(8,128)(2,1)} %embeddings.9), custom_call_target="tpu_custom_call" | custom-call | tf_op jit(solution)/shard_map/project/pallas_call | solution.py:300
  4.5 0.5 collective-permute-start
  5.0 5.7 %collective-permute-start.2 = (bf16[2,128,512]{2,1,0:T(8,128)(2,1)}, bf16[2,128,512]{2,1,0:T(8,128)(2,1)S(1)}, u32[]{:S(2)}, u32[]{:S(2)}) collective-permute-start(bf16[2,128,512]{2,1,0:T(8,128)(2,1)} %get-tuple-element.23), channel_id=1, source_target_pairs={{1,2},{3,4},{5,6},{7,8},{9,10},{11,12},{13,14},{15,0},{2,1},{4,3},... | collective-permute-start | bytes 786440 | tf_op jit(solution)/shard_map/ppermute | solution.py:289
  10.7 0.8 %copy.10.positives = s32[256,8]{1,0:T(8,128)S(1)} copy(s32[256,8]{0,1:T(8,128)} %param.11) | data formatting | bytes 16384 | tf_op args[5]
  11.6 2.9 %hits.1 = f32[4,256,512]{2,1,0:T(8,128)S(1)} custom-call(s32[256,8]{1,0:T(8,128)S(1)} %copy.10.positives, f32[1,2048]{1,0:T(1,128)S(1)} %bitcast.11), custom_call_target="tpu_custom_call" | custom-call | tf_op jit(solution)/shard_map/hits/pallas_call | solution.py:316
  14.5 2.2 %copy-done.1 = bf16[4,2,512,512]{3,2,1,0:T(8,128)(2,1)S(1)} copy-done((bf16[4,2,512,512]{3,2,1,0:T(8,128)(2,1)S(1)}, bf16[4,2,512,512]{3,2,1,0:T(8,128)(2,1)}, u32[]{:S(2)}) %copy-start.1) | copy-done | bytes 4194328
  16.7 1.3 %base.1 = f32[4,256,512]{2,1,0:T(8,128)S(1)} custom-call(s32[2,64]{1,0:T(2,128)S(1)} %bitcast.3, f32[4,256,512]{2,1,0:T(8,128)S(1)} %get-tuple-element.20.own, bf16[2,256,512]{2,1,0:T(8,128)(2,1)S(1)} %collective-permute-done.received, bf16[4,2,512,512]{3,2,1,0:T(8,128)(2,1)S(1)} %copy-done.1), custom_call_target="tpu_custom_call" | custom-call | tf_op jit(solution)/shard_map/base/pallas_call | solution.py:317
  18.1 0.8 %copy-done.2 = bf16[4,2,512,512]{3,2,1,0:T(8,128)(2,1)S(1)} copy-done((bf16[4,2,512,512]{3,2,1,0:T(8,128)(2,1)S(1)}, bf16[4,2,512,512]{3,2,1,0:T(8,128)(2,1)}, u32[]{:S(2)}) %copy-start.2) | copy-done | bytes 4194328
  18.9 2.6 %signal.2 = (bf16[4,256,512]{2,1,0:T(8,128)(2,1)S(1)}, bf16[2,128,512]{2,1,0:T(8,128)(2,1)S(1)}, bf16[2,128,512]{2,1,0:T(8,128)(2,1)S(1)}) custom-call(s32[2,64]{1,0:T(2,128)S(1)} %bitcast.4, f32[4,256,512]{2,1,0:T(8,128)S(1)} %base.1, f32[4,256,512]{2,1,0:T(8,128)S(1)} %hits.1, bf16[2,128,512]{2,1,0:T(8,128)(2,1)S(1)} %collective-permute-done.2.received, ...), custom_call_target="tpu_custom_call" | custom-call | tf_op jit(solution)/shard_map/signal/pallas_call | solution.py:320
  21.5 4.5 %collective-permute-start.5 = (bf16[2,128,512]{2,1,0:T(8,128)(2,1)S(1)}, bf16[2,128,512]{2,1,0:T(8,128)(2,1)S(1)}, u32[]{:S(2)}, u32[]{:S(2)}) collective-permute-start(bf16[2,128,512]{2,1,0:T(8,128)(2,1)S(1)} %get-tuple-element.28), channel_id=1, source_target_pairs={{1,2},{3,4},{5,6},{7,8},{9,10},{11,12},{13,14},{15,0},{2,1},{4,3},... | collective-permute-start | bytes 786440 | tf_op jit(solution)/shard_map/ppermute | solution.py:289
  26.0 2.6 %signal.3 = (bf16[4,256,512]{2,1,0:T(8,128)(2,1)S(1)}, bf16[2,128,512]{2,1,0:T(8,128)(2,1)S(1)}, bf16[2,128,512]{2,1,0:T(8,128)(2,1)S(1)}) custom-call(s32[2,64]{1,0:T(2,128)S(1)} %bitcast.5, f32[4,256,512]{2,1,0:T(8,128)S(1)} %base.1, f32[4,256,512]{2,1,0:T(8,128)S(1)} %hits.1, ...), custom_call_target="tpu_custom_call", output_to_operand_aliasing={{0}: (5, {})} | custom-call | tf_op jit(solution)/shard_map/signal/pallas_call | solution.py:320
  28.6 0.1 collective-permute-start.4
  28.7 0.5 collective-permute-start.3
  29.2 1.0 %query.1.part = f32[256,768]{1,0:T(8,128)S(1)} custom-call(bf16[4,256,512]{2,1,0:T(8,128)(2,1)S(1)} %get-tuple-element.25.signal, bf16[2048,768]{1,0:T(8,128)(2,1)S(1)} %copy-done), custom_call_target="tpu_custom_call" | custom-call | tf_op jit(solution)/shard_map/query/pallas_call | solution.py:334
  30.2 1.0 %embed.1.part.after = f32[4,512,768]{2,1,0:T(8,128)S(1)} custom-call(bf16[4,256,512]{2,1,0:T(8,128)(2,1)S(1)} %get-tuple-element.25.signal, bf16[256,768]{1,0:T(8,128)(2,1)S(1)} %copy-done.3), custom_call_target="tpu_custom_call" | custom-call | tf_op jit(solution)/shard_map/embed/pallas_call | solution.py:335
  31.3 1.0 %query_half.1.after.other = f32[128,768]{1,0:T(8,128)S(1)} custom-call(s32[2,64]{1,0:T(2,128)S(1)} %bitcast.6, f32[256,768]{1,0:T(8,128)S(1)} %query.1.part, bf16[2,128,512]{2,1,0:T(8,128)(2,1)S(1)} %collective-permute-done.5.off_a.received, bf16[2048,768]{1,0:T(8,128)(2,1)S(1)} %copy-done, f32[4,512,768]{2,1,0:T(8,128)S(1)} %embed.1.part.after), custom_call_target="tpu_custom_call" | custom-call | flops 1000000000 | tf_op jit(solution)/shard_map/query_half/pallas_call | solution.py:339
  32.2 1.2 %query_on.1.part_on = f32[256,768]{1,0:T(8,128)S(1)} custom-call(s32[2,64]{1,0:T(2,128)S(1)} %bitcast.7, bf16[2,128,512]{2,1,0:T(8,128)(2,1)S(1)} %collective-permute-done.3.on_a.received_a, bf16[2,128,512]{2,1,0:T(8,128)(2,1)S(1)} %collective-permute-done.4.on_b.received_b, bf16[2048,768]{1,0:T(8,128)(2,1)S(1)} %copy-done, f32[128,768]{1,0:T(8,128)S(1)} %query_half.1.after.other), custom_call_target="tpu_custom_call" | custom-call | tf_op jit(solution)/shard_map/query_on/pallas_call | solution.py:342
  33.4 4.4 %collective-permute-done.6.off_b.received = bf16[2,128,512]{2,1,0:T(8,128)(2,1)S(1)} collective-permute-done((bf16[2,128,512]{2,1,0:T(8,128)(2,1)S(1)}, bf16[2,128,512]{2,1,0:T(8,128)(2,1)S(1)}, u32[]{:S(2)}, u32[]{:S(2)}) %collective-permute-start.6) | collective-permute-done | bytes 262176 | tf_op jit(solution)/shard_map/ppermute | solution.py:289
  37.8 1.0 %query_end.1 = (f32[128,768]{1,0:T(8,128)S(1)}, f32[128,768]{1,0:T(8,128)S(1)}) custom-call(s32[2,64]{1,0:T(2,128)S(1)} %bitcast.8, f32[256,768]{1,0:T(8,128)S(1)} %query.1.part, f32[256,768]{1,0:T(8,128)S(1)} %query_on.1.part_on, bf16[2,128,512]{2,1,0:T(8,128)(2,1)S(1)} %collective-permute-done.6.off_b.received, bf16[2048,768]{1,0:T(8,128)(2,1)S(1)} %copy-done, ...), custom_call_target="tpu_custom_call" | custom-call | tf_op jit(solution)/shard_map/query_end/pallas_call | solution.py:348
  38.8 0.2 collective-permute-start.7
  38.9 1.6 %collective-permute-done.7.got = f32[128,768]{1,0:T(8,128)S(1)} collective-permute-done((f32[128,768]{1,0:T(8,128)S(1)}, f32[128,768]{1,0:T(8,128)S(1)}, u32[]{:S(2)}, u32[]{:S(2)}) %collective-permute-start.7) | collective-permute-done | bytes 393248 | tf_op jit(solution)/shard_map/ppermute | solution.py:216
  40.6 0.1 collective-permute-start.8
  40.7 3.4 %embed_end.2 = (bf16[2048,768]{1,0:T(8,128)(2,1)}, f32[8,128]{1,0:T(8,128)S(1)}) custom-call(s32[2,64]{1,0:T(2,128)S(1)} %bitcast.9, f32[4,512,768]{2,1,0:T(8,128)S(1)} %embed.1.part.after, bf16[2,128,512]{2,1,0:T(8,128)(2,1)S(1)} %collective-permute-done.3.on_a.received_a, bf16[2,128,512]{2,1,0:T(8,128)(2,1)S(1)} %collective-permute-done.4.on_b.received_b, ...), custom_call_target="tpu_custom_call" | custom-call | tf_op jit(solution)/shard_map/embed_end/pallas_call | solution.py:353
  44.1 1.4 %collective-permute-done.8.got = bf16[64,768]{1,0:T(8,128)(2,1)S(1)} collective-permute-done((bf16[64,768]{1,0:T(8,128)(2,1)S(1)}, bf16[64,768]{1,0:T(8,128)(2,1)S(1)}, u32[]{:S(2)}, u32[]{:S(2)}) %collective-permute-start.8) | collective-permute-done | bytes 98336 | tf_op jit(solution)/shard_map/ppermute | solution.py:216
  45.6 3.2 %embed_end.3 = (bf16[2048,768]{1,0:T(8,128)(2,1)}, f32[8,128]{1,0:T(8,128)S(1)}) custom-call(s32[2,64]{1,0:T(2,128)S(1)} %bitcast.10, f32[4,512,768]{2,1,0:T(8,128)S(1)} %embed.1.part.after, bf16[2,128,512]{2,1,0:T(8,128)(2,1)S(1)} %collective-permute-done.3.on_a.received_a, ...), custom_call_target="tpu_custom_call", output_to_operand_aliasing={{0}: (7, {})} | custom-call | tf_op jit(solution)/shard_map/embed_end/pallas_call | solution.py:353
  48.8 1.4 %collective-permute-done.9.got = bf16[64,768]{1,0:T(8,128)(2,1)S(1)} collective-permute-done((bf16[64,768]{1,0:T(8,128)(2,1)S(1)}, bf16[64,768]{1,0:T(8,128)(2,1)S(1)}, u32[]{:S(2)}, u32[]{:S(2)}) %collective-permute-start.9) | collective-permute-done | bytes 98336 | tf_op jit(solution)/shard_map/ppermute | solution.py:216
  50.3 1.4 %collective-permute-start.10 = (bf16[64,768]{1,0:T(8,128)(2,1)S(1)}, bf16[64,768]{1,0:T(8,128)(2,1)S(1)}, u32[]{:S(2)}, u32[]{:S(2)}) collective-permute-start(bf16[64,768]{1,0:T(8,128)(2,1)S(1)} %add.4.held), channel_id=1, source_target_pairs={{0,8},{1,9},{2,10},{3,11},{4,12},{5,13},{6,14},{7,15},{8,0},{9,1},... | collective-permute-start | bytes 294920 | tf_op jit(solution)/shard_map/ppermute | solution.py:216
  51.6 5.6 %collective-permute-done.10.got = bf16[64,768]{1,0:T(8,128)(2,1)S(1)} collective-permute-done((bf16[64,768]{1,0:T(8,128)(2,1)S(1)}, bf16[64,768]{1,0:T(8,128)(2,1)S(1)}, u32[]{:S(2)}, u32[]{:S(2)}) %collective-permute-start.10) | collective-permute-done | bytes 98336 | tf_op jit(solution)/shard_map/ppermute | solution.py:216
  57.3 1.6 %collective-permute-start.11 = (bf16[64,768]{1,0:T(8,128)(2,1)S(1)}, bf16[64,768]{1,0:T(8,128)(2,1)S(1)}, u32[]{:S(2)}, u32[]{:S(2)}) collective-permute-start(bf16[64,768]{1,0:T(8,128)(2,1)S(1)} %add.5.held), channel_id=1, source_target_pairs={{0,2},{1,3},{2,0},{3,1},{4,6},{5,7},{6,4},{7,5},{8,10},{9,11},{10,... | collective-permute-start | bytes 294920 | tf_op jit(solution)/shard_map/ppermute | solution.py:216
  59.0 3.0 %collective-permute-done.11.got = bf16[64,768]{1,0:T(8,128)(2,1)S(1)} collective-permute-done((bf16[64,768]{1,0:T(8,128)(2,1)S(1)}, bf16[64,768]{1,0:T(8,128)(2,1)S(1)}, u32[]{:S(2)}, u32[]{:S(2)}) %collective-permute-start.11) | collective-permute-done | bytes 98336 | tf_op jit(solution)/shard_map/ppermute | solution.py:216
  62.1 1.4 %collective-permute-done.12.got = bf16[128,768]{1,0:T(8,128)(2,1)S(1)} collective-permute-done((bf16[128,768]{1,0:T(8,128)(2,1)S(1)}, bf16[128,768]{1,0:T(8,128)(2,1)S(1)}, u32[]{:S(2)}, u32[]{:S(2)}) %collective-permute-start.12) | collective-permute-done | bytes 196640 | tf_op jit(solution)/shard_map/ppermute | solution.py:216
  63.5 0.9 %join.3 = f32[256,768]{1,0:T(8,128)} custom-call(bf16[128,768]{1,0:T(8,128)(2,1)S(1)} %join.2.held, bf16[128,768]{1,0:T(8,128)(2,1)S(1)} %collective-permute-done.12.got), custom_call_target="tpu_custom_call" | custom-call | tf_op jit(solution)/shard_map/join/pallas_call | solution.py:270
  (25 shorter events, 0.4 us)
Async XLA Ops:
  0.6 13.9 %copy-start.4 = (s32[64,2]{0,1:T(2,128)S(1)}, s32[64,2]{0,1:T(2,128)}, u32[]{:S(2)}) copy-start(s32[64,2]{0,1:T(2,128)} %param.8) | copy-start | bytes 1540
  0.6 10.9 %copy-start.5 = (f32[2048]{0:T(1024)S(1)}, f32[2048]{0:T(1024)}, u32[]{:S(2)}) copy-start(f32[2048]{0:T(1024)} %param.9) | copy-start | bytes 24580
  4.5 10.0 %collective-permute-start = (bf16[2,256,512]{2,1,0:T(8,128)(2,1)}, bf16[2,256,512]{2,1,0:T(8,128)(2,1)S(1)}, u32[]{:S(2)}, u32[]{:S(2)}) collective-permute-start(bf16[2,256,512]{2,1,0:T(8,128)(2,1)} %get-tuple-element.21), channel_id=1, source_target_pairs={{0,1},{1,0},{2,3},{3,2},{4,5},{5,4},{6,7},{7,6},{8,9},{9,8},{10,11... | collective-permute-start | bytes 1572872 | tf_op jit(solution)/shard_map/ppermute | solution.py:216
  5.0 13.0 %collective-permute-start.2 = (bf16[2,128,512]{2,1,0:T(8,128)(2,1)}, bf16[2,128,512]{2,1,0:T(8,128)(2,1)S(1)}, u32[]{:S(2)}, u32[]{:S(2)}) collective-permute-start(bf16[2,128,512]{2,1,0:T(8,128)(2,1)} %get-tuple-element.23), channel_id=1, source_target_pairs={{1,2},{3,4},{5,6},{7,8},{9,10},{11,12},{13,14},{15,0},{2,1},{4,3},... | collective-permute-start | bytes 786440 | tf_op jit(solution)/shard_map/ppermute | solution.py:289
  10.7 15.3 %collective-permute-start.1 = (bf16[2,128,512]{2,1,0:T(8,128)(2,1)S(1)}, bf16[2,128,512]{2,1,0:T(8,128)(2,1)S(1)}, u32[]{:S(2)}, u32[]{:S(2)}) collective-permute-start(bf16[2,128,512]{2,1,0:T(8,128)(2,1)S(1)} %get-tuple-element.22), channel_id=1, source_target_pairs={{1,2},{3,4},{5,6},{7,8},{9,10},{11,12},{13,14},{15,0},{2,1},{4,3},... | collective-permute-start | bytes 786440 | tf_op jit(solution)/shard_map/ppermute | solution.py:289
  14.5 2.2 %copy-start.1 = (bf16[4,2,512,512]{3,2,1,0:T(8,128)(2,1)S(1)}, bf16[4,2,512,512]{3,2,1,0:T(8,128)(2,1)}, u32[]{:S(2)}) copy-start(bf16[4,2,512,512]{3,2,1,0:T(8,128)(2,1)} %tiles.5) | copy-start | bytes 12582916
  16.7 2.2 %copy-start.2 = (bf16[4,2,512,512]{3,2,1,0:T(8,128)(2,1)S(1)}, bf16[4,2,512,512]{3,2,1,0:T(8,128)(2,1)}, u32[]{:S(2)}) copy-start(bf16[4,2,512,512]{3,2,1,0:T(8,128)(2,1)} %tiles.5) | copy-start | bytes 12582916
  21.5 9.7 %collective-permute-start.5 = (bf16[2,128,512]{2,1,0:T(8,128)(2,1)S(1)}, bf16[2,128,512]{2,1,0:T(8,128)(2,1)S(1)}, u32[]{:S(2)}, u32[]{:S(2)}) collective-permute-start(bf16[2,128,512]{2,1,0:T(8,128)(2,1)S(1)} %get-tuple-element.28), channel_id=1, source_target_pairs={{1,2},{3,4},{5,6},{7,8},{9,10},{11,12},{13,14},{15,0},{2,1},{4,3},... | collective-permute-start | bytes 786440 | tf_op jit(solution)/shard_map/ppermute | solution.py:289
  26.0 3.3 %copy-start = (bf16[2048,768]{1,0:T(8,128)(2,1)S(1)}, bf16[2048,768]{1,0:T(8,128)(2,1)}, u32[]{:S(2)}) copy-start(bf16[2048,768]{1,0:T(8,128)(2,1)} %embeddings.9) | copy-start | bytes 9437188
  28.6 1.6 %copy-start.3 = (bf16[256,768]{1,0:T(8,128)(2,1)S(1)}, bf16[256,768]{1,0:T(8,128)(2,1)}, u32[]{:S(2)}) copy-start(bf16[256,768]{1,0:T(8,128)(2,1)} %queries.7) | copy-start | bytes 1179652
  28.6 3.6 %collective-permute-start.4 = (bf16[2,128,512]{2,1,0:T(8,128)(2,1)S(1)}, bf16[2,128,512]{2,1,0:T(8,128)(2,1)S(1)}, u32[]{:S(2)}, u32[]{:S(2)}) collective-permute-start(bf16[2,128,512]{2,1,0:T(8,128)(2,1)S(1)} %get-tuple-element.27), channel_id=1, source_target_pairs={{0,1},{1,0},{2,3},{3,2},{4,5},{5,4},{6,7},{7,6},{8,9},{9,8},{10,11... | collective-permute-start | bytes 786440 | tf_op jit(solution)/shard_map/ppermute | solution.py:216
  28.7 3.5 %collective-permute-start.3 = (bf16[2,128,512]{2,1,0:T(8,128)(2,1)S(1)}, bf16[2,128,512]{2,1,0:T(8,128)(2,1)S(1)}, u32[]{:S(2)}, u32[]{:S(2)}) collective-permute-start(bf16[2,128,512]{2,1,0:T(8,128)(2,1)S(1)} %get-tuple-element.26), channel_id=1, source_target_pairs={{0,1},{1,0},{2,3},{3,2},{4,5},{5,4},{6,7},{7,6},{8,9},{9,8},{10,11... | collective-permute-start | bytes 786440 | tf_op jit(solution)/shard_map/ppermute | solution.py:216
  29.2 8.6 %collective-permute-start.6 = (bf16[2,128,512]{2,1,0:T(8,128)(2,1)S(1)}, bf16[2,128,512]{2,1,0:T(8,128)(2,1)S(1)}, u32[]{:S(2)}, u32[]{:S(2)}) collective-permute-start(bf16[2,128,512]{2,1,0:T(8,128)(2,1)S(1)} %get-tuple-element.29), channel_id=1, source_target_pairs={{1,2},{3,4},{5,6},{7,8},{9,10},{11,12},{13,14},{15,0},{2,1},{4,3},... | collective-permute-start | bytes 786440 | tf_op jit(solution)/shard_map/ppermute | solution.py:289
  38.8 1.8 %collective-permute-start.7 = (f32[128,768]{1,0:T(8,128)S(1)}, f32[128,768]{1,0:T(8,128)S(1)}, u32[]{:S(2)}, u32[]{:S(2)}) collective-permute-start(f32[128,768]{1,0:T(8,128)S(1)} %get-tuple-element.33), channel_id=1, source_target_pairs={{0,1},{1,0},{2,3},{3,2},{4,5},{5,4},{6,7},{7,6},{8,9},{9,8},{10,11... | collective-permute-start | bytes 1179656 | tf_op jit(solution)/shard_map/ppermute | solution.py:216
  40.6 4.9 %collective-permute-start.8 = (bf16[64,768]{1,0:T(8,128)(2,1)S(1)}, bf16[64,768]{1,0:T(8,128)(2,1)S(1)}, u32[]{:S(2)}, u32[]{:S(2)}) collective-permute-start(bf16[64,768]{1,0:T(8,128)(2,1)S(1)} %get-tuple-element.35), channel_id=1, source_target_pairs={{0,2},{1,3},{2,0},{3,1},{4,6},{5,7},{6,4},{7,5},{8,10},{9,11},{10,... | collective-permute-start | bytes 294920 | tf_op jit(solution)/shard_map/ppermute | solution.py:216
  45.5 4.7 %collective-permute-start.9 = (bf16[64,768]{1,0:T(8,128)(2,1)S(1)}, bf16[64,768]{1,0:T(8,128)(2,1)S(1)}, u32[]{:S(2)}, u32[]{:S(2)}) collective-permute-start(bf16[64,768]{1,0:T(8,128)(2,1)S(1)} %add.3.held), channel_id=1, source_target_pairs={{0,4},{1,5},{2,6},{3,7},{4,0},{5,1},{6,2},{7,3},{8,12},{9,13},{10,... | collective-permute-start | bytes 294920 | tf_op jit(solution)/shard_map/ppermute | solution.py:216
  50.3 7.0 %collective-permute-start.10 = (bf16[64,768]{1,0:T(8,128)(2,1)S(1)}, bf16[64,768]{1,0:T(8,128)(2,1)S(1)}, u32[]{:S(2)}, u32[]{:S(2)}) collective-permute-start(bf16[64,768]{1,0:T(8,128)(2,1)S(1)} %add.4.held), channel_id=1, source_target_pairs={{0,8},{1,9},{2,10},{3,11},{4,12},{5,13},{6,14},{7,15},{8,0},{9,1},... | collective-permute-start | bytes 294920 | tf_op jit(solution)/shard_map/ppermute | solution.py:216
  57.3 4.7 %collective-permute-start.11 = (bf16[64,768]{1,0:T(8,128)(2,1)S(1)}, bf16[64,768]{1,0:T(8,128)(2,1)S(1)}, u32[]{:S(2)}, u32[]{:S(2)}) collective-permute-start(bf16[64,768]{1,0:T(8,128)(2,1)S(1)} %add.5.held), channel_id=1, source_target_pairs={{0,2},{1,3},{2,0},{3,1},{4,6},{5,7},{6,4},{7,5},{8,10},{9,11},{10,... | collective-permute-start | bytes 294920 | tf_op jit(solution)/shard_map/ppermute | solution.py:216
  62.0 1.5 %collective-permute-start.12 = (bf16[128,768]{1,0:T(8,128)(2,1)S(1)}, bf16[128,768]{1,0:T(8,128)(2,1)S(1)}, u32[]{:S(2)}, u32[]{:S(2)}) collective-permute-start(bf16[128,768]{1,0:T(8,128)(2,1)S(1)} %join.2.held), channel_id=1, source_target_pairs={{0,1},{1,0},{2,3},{3,2},{4,5},{5,4},{6,7},{7,6},{8,9},{9,8},{10,11... | collective-permute-start | bytes 589832 | tf_op jit(solution)/shard_map/ppermute | solution.py:216

commit v5 on v4

v5 whole, which is shorter than its diff:
```python
import functools
import math

import jax
import jax.numpy as jnp
from jax import lax
from jax.experimental import pallas as pl
from jax.experimental.pallas import tpu as pltpu
from jax.sharding import PartitionSpec as P

AXIS = "labels"
BF16 = jnp.bfloat16
F32 = jnp.float32
NT = (((1,), (1,)), ((), ()))
NN = (((1,), (0,)), ((), ()))
TN = (((0,), (0,)), ((), ()))
MIB = 1024 * 1024

OFF, ON = True, False


def dot(a, b, dims):
    return lax.dot_general(a, b, dims, preferred_element_type=F32)


def own_side(device, off):
    odd = device % 2
    return 1 - odd if off else odd


def partner_of(device, count, off):
    ahead = jnp.where(device == count - 1, 0, device + 1)
    behind = jnp.where(device == 0, count - 1, device - 1)
    return jnp.where(own_side(device, off) == 0, ahead, behind)


def own_list(lists, blocks, off):
    device = lax.axis_index(AXIS)
    side = own_side(device, off)
    return [lists[side, device * blocks + g] for g in range(blocks)]


def slots_of(lists, blocks, off):
    named = own_list(lists, blocks, off)
    least = functools.reduce(jnp.minimum, named)
    return [(value != least).astype(jnp.int32) for value in named]


def named_by_partner(lists, blocks, off):
    device = lax.axis_index(AXIS)
    partner = partner_of(device, lax.axis_size(AXIS), off)
    side = 1 - own_side(device, off)
    named = [lists[side, partner * blocks + g] for g in range(blocks)]
    return functools.reduce(jnp.minimum, named), functools.reduce(jnp.maximum, named)


def tile_side(off):
    return own_side(lax.axis_index(AXIS), off)


def block_rows(ref, index, block):
    return ref[pl.ds(pl.multiple_of(index * block, block), block), :]


def project_kernel(lists, queries, embeddings, own, off_a, off_b, for_on, left, right, table, sem, *, scale):
    blocks, _, block = own.shape
    fetches = [pltpu.make_async_copy(lists, table, sem.at[0]), pltpu.make_async_copy(queries, left, sem.at[1])]
    for g in range(blocks):
        rows = pl.ds(g * block, block)
        fetches.append(pltpu.make_async_copy(embeddings.at[rows, :], right.at[rows, :], sem.at[2 + g]))
    for fetch in fetches:
        fetch.start()
    for fetch in fetches[:2]:
        fetch.wait()
    for g in range(blocks):
        fetches[2 + g].wait()
        own[g] = dot(left[...], right[g * block : (g + 1) * block, :], NT) * scale
    for out, index in zip((off_a, off_b), named_by_partner(table, blocks, OFF)):
        out[...] = own[index].astype(BF16)
    for slot, index in enumerate(named_by_partner(table, blocks, ON)):
        for_on[slot] = own[index].astype(BF16)


def hits_kernel(positives, tiles, out, kept, sem):
    fetch = pltpu.make_async_copy(tiles, kept, sem)
    fetch.start()
    blocks, rows, block = out.shape
    first = lax.axis_index(AXIS) * blocks * block
    ids = lax.broadcasted_iota(jnp.int32, (rows, block), 1)
    for g in range(blocks):
        hits = jnp.zeros((rows, block), jnp.bool_)
        for column in range(positives.shape[1]):
            hits = jnp.logical_or(hits, ids == positives[:, column : column + 1] - (first + g * block))
        out[g] = jnp.where(hits, 1.0, 0.0).astype(BF16)
    fetch.wait()


def base_kernel(lists, own, received, tiles, out):
    blocks = out.shape[0]
    side = tile_side(ON)
    for g, slot in enumerate(slots_of(lists, blocks, ON)):
        out[g] = own[g] + dot(received[slot], tiles[g, side], NT)


def signal_kernel(lists, base, hits, propensity, received, tiles, *rest, slot):
    if slot == 0:
        signal, push, carry, total, total_on = rest
        total_on[...] = jnp.zeros_like(total_on)
    else:
        _, before, signal, push, push_on_a, push_on_b, total, total_on = rest
        total_on[...] = before[...]
    blocks, _, block = base.shape
    side_off, side_on = tile_side(OFF), tile_side(ON)
    slots_on = slots_of(lists, blocks, ON)
    total[...] = jnp.zeros_like(total)
    for g, taken in enumerate(slots_of(lists, blocks, OFF)):

        @pl.when(taken == slot)
        def _():
            scores = base[g] + dot(received[...], tiles[g, side_off], NT)
            inverse = 1.0 / propensity[:, g * block : (g + 1) * block]
            value = (jax.nn.sigmoid(scores) - hits[g].astype(F32) * inverse).astype(BF16)
            signal[g] = value
            total[...] += dot(value, tiles[g, side_off], NN)
            total_on[slots_on[g]] += dot(value, tiles[g, side_on], NN)

    push[...] = total[...].astype(BF16)
    if slot == 0:
        carry[...] = total_on[...]
    else:
        push_on_a[...] = total_on[0].astype(BF16)
        push_on_b[...] = total_on[1].astype(BF16)


def query_kernel(signal, embeddings, out):
    blocks, _, block = signal.shape
    total = dot(signal[0], embeddings[0:block, :], NN)
    for g in range(1, blocks):
        total += dot(signal[g], embeddings[g * block : (g + 1) * block, :], NN)
    out[...] = total


def query_half_kernel(lists, part, received, embeddings, after, out, *, blocks):
    del after
    first, _ = named_by_partner(lists, blocks, OFF)
    out[...] = part[...] + dot(received[...], block_rows(embeddings, first, received.shape[1]), NN)


def query_on_kernel(lists, part, received_a, received_b, embeddings, out, *, blocks):
    block = received_a.shape[1]
    first, second = named_by_partner(lists, blocks, ON)
    out[...] = (
        part[...]
        + dot(received_a[...], block_rows(embeddings, first, block), NN)
        + dot(received_b[...], block_rows(embeddings, second, block), NN)
    )


def query_end_kernel(lists, part, received, embeddings, kept, sent, total, *, blocks):
    _, second = named_by_partner(lists, blocks, OFF)
    total[...] = part[...] + dot(received[...], block_rows(embeddings, second, received.shape[1]), NN)
    rows = kept.shape[0]
    core = lax.axis_index(AXIS) % 2
    kept[...] = total[pl.ds(pl.multiple_of(core * rows, rows), rows), :]
    sent[...] = total[pl.ds(pl.multiple_of((1 - core) * rows, rows), rows), :]


def embed_kernel(signal, queries, out):
    for g in range(signal.shape[0]):
        out[g] = dot(signal[g], queries[...], TN)


def embed_end_kernel(lists, part, on_a, on_b, off_a, off_b, queries, *rest, blocks, g, scale):
    out, token, total, ready, sem = rest[-5:]
    block = part.shape[1]
    token[...] = jnp.zeros_like(token)
    total[...] = part[g]
    named = named_by_partner(lists, blocks, ON) + named_by_partner(lists, blocks, OFF)
    for received, index in zip((on_a, on_b, off_a, off_b), named):

        @pl.when(index == g)
        def _():
            total[...] += dot(received[...], queries[...], TN)

    ready[...] = (total[...] * scale).astype(BF16)
    copy = pltpu.make_async_copy(ready, out.at[pl.ds(g * block, block), :], sem)
    copy.start()
    copy.wait()


VMEM = pl.BlockSpec(memory_space=pltpu.VMEM)
SMEM = pl.BlockSpec(memory_space=pltpu.SMEM)
ANY = pl.BlockSpec(memory_space=pl.ANY)
HBM = pl.BlockSpec(memory_space=pltpu.HBM)


def call(kernel, name, in_specs, out_shape, out_specs=None, scratch=(), aliases=None, vmem=12, flops=0):
    if out_specs is None:
        out_specs = jax.tree.map(lambda _: VMEM, out_shape)
    return pl.pallas_call(
        kernel,
        in_specs=in_specs,
        out_specs=out_specs,
        out_shape=out_shape,
        scratch_shapes=scratch,
        input_output_aliases=aliases or {},
        name=name,
        cost_estimate=pl.CostEstimate(flops=flops, bytes_accessed=0, transcendentals=0),
        compiler_params=pltpu.CompilerParams(vmem_limit_bytes=vmem * MIB),
    )


def exchange(value, mask):
    count = lax.axis_size(AXIS)
    return lax.ppermute(value, AXIS, [(i, i ^ mask) for i in range(count)])


def halve_kernel(held, got, kept, sent, *, bit):
    rows = kept.shape[0]
    digit = (lax.axis_index(AXIS) // bit) % 2
    here = pl.ds(pl.multiple_of(digit * rows, rows), rows)
    there = pl.ds(pl.multiple_of((1 - digit) * rows, rows), rows)
    kept[...] = held[here, :] + got[here, :]
    sent[...] = (held[there, :] + got[there, :]).astype(BF16)


def add_kernel(held, got, *rest, scale):
    rest[-1][...] = ((held[...].astype(F32) + got[...].astype(F32)) * scale).astype(BF16)


def join_kernel(held, got, *rest, bit):
    out = rest[-1]
    rows = held.shape[0]
    digit = (lax.axis_index(AXIS) // bit) % 2
    out[pl.ds(pl.multiple_of(digit * rows, rows), rows), :] = held[...]
    out[pl.ds(pl.multiple_of((1 - digit) * rows, rows), rows), :] = got[...]


def place_kernel(held, *rest, own):
    out, wide, sem = rest[-3:]
    rows = held.shape[0]
    core = lax.axis_index(AXIS) % 2
    half = core if own else 1 - core
    wide[...] = held[...].astype(F32)
    copy = pltpu.make_async_copy(wide, out.at[pl.ds(pl.multiple_of(half * rows, rows), rows), :], sem)
    copy.start()
    copy.wait()


def sum_queries(kept, sent, beside, scale):
    count = lax.axis_size(AXIS)
    rows, width = kept.shape
    got = exchange(sent, 1)
    if count & (count - 1) or count < 4:
        half = lax.psum(kept + got, AXIS, axis_index_groups=[list(range(c, count, 2)) for c in range(2)])
        both = jnp.stack([half, exchange(half, 1)])
        both = jnp.where(lax.axis_index(AXIS) % 2 == 0, both, both[::-1])
        return both.reshape(2 * rows, width) * scale
    piece = jax.ShapeDtypeStruct((rows // 2, width), BF16)
    held, sent = call(
        functools.partial(halve_kernel, bit=2),
        "halve",
        [VMEM] * 2,
        [jax.ShapeDtypeStruct(piece.shape, F32), piece],
    )(kept, got)
    got = exchange(sent, 2)
    bits = [1 << k for k in range(2, count.bit_length() - 1)]
    for k in range(len(bits) + 1):
        last = k == len(bits)
        after = beside[k : k + 1]
        held = call(
            functools.partial(add_kernel, scale=scale if last else 1.0),
            "add",
            [VMEM] * 2 + [ANY] * len(after),
            piece,
        )(held, got, *after)
        if not last:
            got = exchange(held, bits[k])
    after = beside[len(bits) + 1 :]
    held = call(
        functools.partial(join_kernel, bit=2),
        "join",
        [VMEM] * 2 + [ANY] * len(after),
        jax.ShapeDtypeStruct((rows, width), BF16),
    )(held, exchange(held, 2), *after)
    got = exchange(held, 1)

    def place(half, own, *begun):
        return call(
            functools.partial(place_kernel, own=own),
            "place",
            [VMEM] + [ANY] * len(begun),
            jax.ShapeDtypeStruct((2 * rows, width), F32),
            out_specs=ANY,
            scratch=[pltpu.VMEM((rows, width), F32), pltpu.SemaphoreType.DMA],
            aliases={1: 0} if begun else None,
        )(half, *begun)

    return place(got, False, place(held, True))


def per_device(embeddings, edge_tiles, neighbour, propensity, queries, positives):
    count = lax.axis_size(AXIS)
    blocks, _, block, _ = edge_tiles.shape
    labels_dev, width = embeddings.shape
    rows = queries.shape[0]
    lists = neighbour.T
    odd = range(1, count, 2)
    off_route = [(i, (i + 1) % count) for i in odd] + [((i + 1) % count, i) for i in odd]

    def off_swap(value):
        return lax.ppermute(value, AXIS, off_route)

    def on_swap(value):
        return exchange(value, 1)

    def in_vmem(shape, dtype):
        return pltpu.VMEM(shape, dtype)

    one = in_vmem((rows, block), BF16)
    full = (blocks, rows, block)
    scale = 1.0 / math.sqrt(width)

    own, off_a, off_b, for_on, queries, embeddings = call(
        functools.partial(project_kernel, scale=scale),
        "project",
        [HBM] * 3,
        [
            in_vmem(full, F32),
            one,
            one,
            in_vmem((2, rows, block), BF16),
            in_vmem(queries.shape, BF16),
            in_vmem(embeddings.shape, BF16),
        ],
        scratch=[pltpu.SMEM(lists.shape, jnp.int32), pltpu.SemaphoreType.DMA((2 + blocks,))],
    )(*(pltpu.with_memory_space_constraint(x, pltpu.HBM) for x in (lists, queries, embeddings)))
    from_off_a = off_swap(off_a)
    from_off_b = off_swap(off_b)
    from_on = on_swap(for_on)
    hits, tiles = call(
        hits_kernel,
        "hits",
        [VMEM, HBM],
        [in_vmem(full, BF16), in_vmem(edge_tiles.shape, BF16)],
        scratch=[pltpu.SemaphoreType.DMA],
    )(positives, pltpu.with_memory_space_constraint(edge_tiles, pltpu.HBM))
    base = call(base_kernel, "base", [SMEM] + [VMEM] * 3, in_vmem(full, F32))(lists, own, from_on, tiles)
    propensity = propensity.reshape(1, labels_dev)

    def signal_of(received, slot, *begun):
        return call(
            functools.partial(signal_kernel, slot=slot),
            "signal",
            [SMEM] + [VMEM] * (5 + len(begun)),
            [in_vmem(full, BF16), one] + ([one, one] if begun else [in_vmem((2, rows, block), F32)]),
            scratch=[pltpu.VMEM((rows, block), F32), pltpu.VMEM((2, rows, block), F32)],
            aliases={6: 0} if begun else None,
        )(lists, base, hits, propensity, received, tiles, *begun)

    signal, push_a, carry = signal_of(from_off_a, 0)
    back_a = off_swap(push_a)
    signal, push_b, push_on_a, push_on_b = signal_of(from_off_b, 1, signal, carry)
    back_b = off_swap(push_b)
    on_a, on_b = on_swap(push_on_a), on_swap(push_on_b)

    whole = in_vmem((rows, width), F32)
    part = call(query_kernel, "query", [VMEM] * 2, whole)(signal, embeddings)
    embed = call(embed_kernel, "embed", [VMEM] * 2, in_vmem((blocks, block, width), F32))(signal, queries)
    part = call(
        functools.partial(query_half_kernel, blocks=blocks),
        "query_half",
        [SMEM] + [VMEM] * 3 + [ANY],
        whole,
        flops=10**9,
    )(lists, part, back_a, embeddings, embed)
    part = call(functools.partial(query_on_kernel, blocks=blocks), "query_on", [SMEM] + [VMEM] * 4, whole)(
        lists, part, on_a, on_b, embeddings
    )
    piece = in_vmem((rows // 2, width), F32)
    kept, sent = call(
        functools.partial(query_end_kernel, blocks=blocks),
        "query_end",
        [SMEM] + [VMEM] * 3,
        [piece, piece],
        scratch=[pltpu.VMEM((rows, width), F32)],
    )(lists, part, back_b, embeddings)

    def embed_end(g, *begun):
        return call(
            functools.partial(embed_end_kernel, blocks=blocks, g=g, scale=1.0 / math.sqrt(rows)),
            "embed_end",
            [SMEM] + [VMEM] * 6 + [ANY] * len(begun),
            [jax.ShapeDtypeStruct((labels_dev, width), BF16), in_vmem((8, 128), F32)],
            out_specs=[ANY, VMEM],
            scratch=[
                pltpu.VMEM((block, width), F32),
                pltpu.VMEM((block, width), BF16),
                pltpu.SemaphoreType.DMA,
            ],
            aliases={7: 0} if begun else None,
        )(lists, embed, on_a, on_b, back_a, back_b, queries, *begun)

    begun, tokens = [], []
    for g in range(blocks):
        grad_embed, token = embed_end(g, *begun)
        begun = [grad_embed]
        tokens.append(token)
    grad_queries = sum_queries(kept, sent, tokens, 1.0 / math.sqrt(labels_dev * count))
    return (grad_embed, grad_queries)


def solution(mesh):
    placed = (
        P("labels", None),
        P("labels", None, None, None),
        P(),
        P("labels"),
        P("groups", None),
        P("groups", None),
    )
    return jax.shard_map(
        per_device,
        mesh=mesh,
        in_specs=placed,
        out_specs=(P(("groups", "labels"), None), P("groups", None)),
        check_vma=False,
    )
```

time: 64.4 us -> 64.4 us (level)
  Pallas kernels: 26.1 us -> 29.1 us
  waiting for transfers between devices: 19 us -> 17.5 us
  starting transfers between devices: 14.7 us -> 13.5 us
  local copies, waits for them, and re-layouts: 3.84 us -> 3.03 us
    pallas_call x10 -> x13, Pallas kernels: 19 us -> 21.9 us  [the longest x4 8.17 us: embed_end(): call(functools.partial(embed_end_kernel, blocks=blocks, g=g, scale=1.0 /...]
    ppermute x9, starting transfers between devices: 4.48 us -> 2.43 us  [exchange(): return lax.ppermute(value, AXIS, [(i, i ^ mask) for i in range(count)])]
    ppermute x9, waiting for transfers between devices: 14.6 us -> 13.2 us  [exchange(): return lax.ppermute(value, AXIS, [(i, i ^ mask) for i in range(count)])]
    ppermute x4, starting transfers between devices: 10.2 us -> 11.1 us  [off_swap(): return lax.ppermute(value, AXIS, off_route)]
    unnamed x13, local copies, waits for them, and re-layouts: 3.84 us -> 3.03 us
  transfers between devices with their start and end apart: 13 -> 13, of which waited for: 7 -> 7; matrix products, arithmetic and copies ran while one was open for 1% -> 1% of each run, Pallas kernels for 31% -> 36%
where the time goes in v5:
time: 64.4 us; the launch traced here: 64.2 us
  Pallas kernels  29.1 us (45%)
  waiting for transfers between devices  17.5 us (27%)
  starting transfers between devices  13.5 us (21%)
  local copies, waits for them, and re-layouts  3.03 us (5%)
  between operations  1.06 us (2%)
    ppermute x9, waiting for transfers between devices, exchange(): return lax.ppermute(value, AXIS, [(i, i ^ mask) for i in range(count)])  13.2 us
    ppermute x4, starting transfers between devices, off_swap(): return lax.ppermute(value, AXIS, off_route)  11.1 us
    pallas_call x4, Pallas kernels, embed_end(): call(functools.partial(embed_end_kernel, blocks=blocks, g=g, scale=1.0 /...  8.17 us
    pallas_call x2, Pallas kernels, signal_of(): call(functools.partial(signal_kernel, slot=slot), 'signal', [SMEM] + [VME...  5.43 us
    ppermute x4, waiting for transfers between devices, off_swap(): return lax.ppermute(value, AXIS, off_route)  4.26 us
    pallas_call x1, Pallas kernels, per_device(): call(functools.partial(project_kernel, scale=scale), 'project', [HBM] * 3...  3.92 us
    unnamed x13, local copies, waits for them, and re-layouts  3.03 us
    pallas_call x1, Pallas kernels, per_device(): call(hits_kernel, 'hits', [VMEM, HBM], [in_vmem(full, BF16), in_vmem(edge...  2.92 us
  transfers between devices with their start and end apart: 13, of which 7 were waited for; matrix products, arithmetic and copies ran while one was open for 1% of the time, Pallas kernels for 36%

profile of v5, /device:TPU:0, one launch (start us, length us, event | category | flops | bytes accessed | tf_op | source)
XLA Modules:
  0.0 64.2 jit_solution(12026194264784887614)
XLA Ops:
  0.7 3.9 %project.1 = (f32[4,256,512]{2,1,0:T(8,128)S(1)}, bf16[256,512]{1,0:T(8,128)(2,1)}, bf16[256,512]{1,0:T(8,128)(2,1)}, bf16[2,256,512]{2,1,0:T(8,128)(2,1)}, bf16...) custom-call(s32[2,64]{1,0:T(2,128)} %bitcast.2, bf16[256,768]{1,0:T(8,128)(2,1)} %queries.1, ...), custom_call_target="tpu_custom_call" | custom-call | tf_op jit(solution)/shard_map/project/pallas_call | solution.py:324
  4.6 1.3 %copy-done = f32[4,256,512]{2,1,0:T(8,128)} copy-done((f32[4,256,512]{2,1,0:T(8,128)}, f32[4,256,512]{2,1,0:T(8,128)S(1)}, u32[]{:S(2)}) %copy-start) | copy-done | bytes 2097176
  5.9 0.5 collective-permute-start
  6.4 5.7 %collective-permute-start.2 = (bf16[256,512]{1,0:T(8,128)(2,1)}, bf16[256,512]{1,0:T(8,128)(2,1)}, u32[]{:S(2)}, u32[]{:S(2)}) collective-permute-start(bf16[256,512]{1,0:T(8,128)(2,1)} %get-tuple-element.34), channel_id=1, source_target_pairs={{1,2},{3,4},{5,6},{7,8},{9,10},{11,12},{13,14},{15,0},{2,1},{4,3},... | collective-permute-start | bytes 786440 | tf_op jit(solution)/shard_map/ppermute | solution.py:312
  12.1 0.8 %copy.13.positives = s32[256,8]{1,0:T(8,128)} copy(s32[256,8]{0,1:T(8,128)S(1)} %copy-done.5) | data formatting | bytes 16384 | tf_op args[5]
  12.9 0.9 %copy-done.2 = s32[256,8]{1,0:T(8,128)S(1)} copy-done((s32[256,8]{1,0:T(8,128)S(1)}, s32[256,8]{1,0:T(8,128)}, u32[]{:S(2)}) %copy-start.2) | copy-done | bytes 8216
  13.8 2.9 %hits.1 = (bf16[4,256,512]{2,1,0:T(8,128)(2,1)S(1)}, bf16[4,2,512,512]{3,2,1,0:T(8,128)(2,1)S(1)}) custom-call(s32[256,8]{1,0:T(8,128)S(1)} %copy-done.2, bf16[4,2,512,512]{3,2,1,0:T(8,128)(2,1)} %tiles.1), custom_call_target="tpu_custom_call" | custom-call | tf_op jit(solution)/shard_map/hits/pallas_call | solution.py:341
  16.7 1.8 %base.1 = f32[4,256,512]{2,1,0:T(8,128)S(1)} custom-call(s32[2,64]{1,0:T(2,128)S(1)} %bitcast.3, f32[4,256,512]{2,1,0:T(8,128)S(1)} %copy-done.1, bf16[2,256,512]{2,1,0:T(8,128)(2,1)} %collective-permute-done.received, bf16[4,2,512,512]{3,2,1,0:T(8,128)(2,1)S(1)} %get-tuple-element.31.tiles), custom_call_target="tpu_custom_call" | custom-call | tf_op jit(solution)/shard_map/base/pallas_call | solution.py:348
  18.6 2.6 %signal.2 = (bf16[4,256,512]{2,1,0:T(8,128)(2,1)S(1)}, bf16[256,512]{1,0:T(8,128)(2,1)S(1)}, f32[2,256,512]{2,1,0:T(8,128)S(1)}) custom-call(s32[2,64]{1,0:T(2,128)S(1)} %bitcast.4, f32[4,256,512]{2,1,0:T(8,128)S(1)} %base.1, bf16[4,256,512]{2,1,0:T(8,128)(2,1)S(1)} %get-tuple-element.32.hits, f32[1,2048]{1,0:T(1,128)S(1)} %bitcast.13, ...), custom_call_target="tpu_custom_call" | custom-call | tf_op jit(solution)/shard_map/signal/pallas_call | solution.py:352
  21.2 5.2 %collective-permute-start.5 = (bf16[256,512]{1,0:T(8,128)(2,1)S(1)}, bf16[256,512]{1,0:T(8,128)(2,1)S(1)}, u32[]{:S(2)}, u32[]{:S(2)}) collective-permute-start(bf16[256,512]{1,0:T(8,128)(2,1)S(1)} %get-tuple-element.41), channel_id=1, source_target_pairs={{1,2},{3,4},{5,6},{7,8},{9,10},{11,12},{13,14},{15,0},{2,1},{4,3},... | collective-permute-start | bytes 786440 | tf_op jit(solution)/shard_map/ppermute | solution.py:312
  26.5 2.8 %signal.3 = (bf16[4,256,512]{2,1,0:T(8,128)(2,1)S(1)}, bf16[256,512]{1,0:T(8,128)(2,1)S(1)}, bf16[256,512]{1,0:T(8,128)(2,1)S(1)}, bf16[256,512]{1,0:T(8,128)(2,1)S(1)}) custom-call(s32[2,64]{1,0:T(2,128)S(1)} %bitcast.5, f32[4,256,512]{2,1,0:T(8,128)S(1)} %base.1, bf16[4,256,512]{2,1,0:T(8,128)(2,1)S(1)} %get-tuple-element.32.hits, ...), custom_call_target="tpu_custom_call", output_to_operand_aliasing={{0}: (6, {})} | custom-call | tf_op jit(solution)/shard_map/signal/pallas_call | solution.py:352
  29.3 0.5 collective-permute-start.4
  29.8 0.2 collective-permute-start.6
  30.0 1.0 %query.1.part = f32[256,768]{1,0:T(8,128)S(1)} custom-call(bf16[4,256,512]{2,1,0:T(8,128)(2,1)S(1)} %get-tuple-element.37.signal, bf16[2048,768]{1,0:T(8,128)(2,1)S(1)} %get-tuple-element.47.embeddings), custom_call_target="tpu_custom_call" | custom-call | tf_op jit(solution)/shard_map/query/pallas_call | solution.py:368
  31.0 1.0 %embed.1.part.after = f32[4,512,768]{2,1,0:T(8,128)S(1)} custom-call(bf16[4,256,512]{2,1,0:T(8,128)(2,1)S(1)} %get-tuple-element.37.signal, bf16[256,768]{1,0:T(8,128)(2,1)S(1)} %get-tuple-element.38.queries), custom_call_target="tpu_custom_call" | custom-call | tf_op jit(solution)/shard_map/embed/pallas_call | solution.py:369
  32.0 1.0 %query_half.1.part = f32[256,768]{1,0:T(8,128)S(1)} custom-call(s32[2,64]{1,0:T(2,128)S(1)} %bitcast.6, f32[256,768]{1,0:T(8,128)S(1)} %query.1.part, bf16[256,512]{1,0:T(8,128)(2,1)S(1)} %collective-permute-done.5.off_a.received, bf16[2048,768]{1,0:T(8,128)(2,1)S(1)} %get-tuple-element.47.embeddings, f32[4,512,768]{2,1,0:T(8,128)S(1)} %embed.1.part.after), custom_call_target="tpu_custom_call" | custom-call | flops 1000000000 | tf_op jit(solution)/shard_map/query_half/pallas_call | solution.py:370
  33.0 1.2 %query_on.1.part = f32[256,768]{1,0:T(8,128)S(1)} custom-call(s32[2,64]{1,0:T(2,128)S(1)} %bitcast.7, f32[256,768]{1,0:T(8,128)S(1)} %query_half.1.part, bf16[256,512]{1,0:T(8,128)(2,1)S(1)} %collective-permute-done.3.on_a.received_a, bf16[256,512]{1,0:T(8,128)(2,1)S(1)} %collective-permute-done.4.on_b.received_b, ...), custom_call_target="tpu_custom_call" | custom-call | tf_op jit(solution)/shard_map/query_on/pallas_call | solution.py:377
  34.2 4.3 %collective-permute-done.6.off_b.received = bf16[256,512]{1,0:T(8,128)(2,1)S(1)} collective-permute-done((bf16[256,512]{1,0:T(8,128)(2,1)S(1)}, bf16[256,512]{1,0:T(8,128)(2,1)S(1)}, u32[]{:S(2)}, u32[]{:S(2)}) %collective-permute-start.6) | collective-permute-done | bytes 262176 | tf_op jit(solution)/shard_map/ppermute | solution.py:312
  38.4 1.0 %query_end.1 = (f32[128,768]{1,0:T(8,128)S(1)}, f32[128,768]{1,0:T(8,128)S(1)}) custom-call(s32[2,64]{1,0:T(2,128)S(1)} %bitcast.8, f32[256,768]{1,0:T(8,128)S(1)} %query_on.1.part, bf16[256,512]{1,0:T(8,128)(2,1)S(1)} %collective-permute-done.6.off_b.received, bf16[2048,768]{1,0:T(8,128)(2,1)S(1)} %get-tuple-element.47.embeddings), custom_call_target="tpu_custom_call" | custom-call | tf_op jit(solution)/shard_map/query_end/pallas_call | solution.py:381
  39.6 1.6 %collective-permute-done.7.got = f32[128,768]{1,0:T(8,128)S(1)} collective-permute-done((f32[128,768]{1,0:T(8,128)S(1)}, f32[128,768]{1,0:T(8,128)S(1)}, u32[]{:S(2)}, u32[]{:S(2)}) %collective-permute-start.7) | collective-permute-done | bytes 393248 | tf_op jit(solution)/shard_map/ppermute | solution.py:215
  41.4 2.0 %embed_end.4 = (bf16[2048,768]{1,0:T(8,128)(2,1)}, f32[8,128]{1,0:T(8,128)S(1)}) custom-call(s32[2,64]{1,0:T(2,128)S(1)} %bitcast.9, f32[4,512,768]{2,1,0:T(8,128)S(1)} %embed.1.part.after, bf16[256,512]{1,0:T(8,128)(2,1)S(1)} %collective-permute-done.3.on_a.received_a, bf16[256,512]{1,0:T(8,128)(2,1)S(1)} %collective-permute-done.4.on_b.received_b, ...), custom_call_target="tpu_custom_call" | custom-call | tf_op jit(solution)/shard_map/embed_end/pallas_call | solution.py:390
  43.4 2.8 %collective-permute-done.8.got = bf16[64,768]{1,0:T(8,128)(2,1)S(1)} collective-permute-done((bf16[64,768]{1,0:T(8,128)(2,1)S(1)}, bf16[64,768]{1,0:T(8,128)(2,1)S(1)}, u32[]{:S(2)}, u32[]{:S(2)}) %collective-permute-start.8) | collective-permute-done | bytes 98336 | tf_op jit(solution)/shard_map/ppermute | solution.py:215
  46.3 2.0 %embed_end.5 = (bf16[2048,768]{1,0:T(8,128)(2,1)}, f32[8,128]{1,0:T(8,128)S(1)}) custom-call(s32[2,64]{1,0:T(2,128)S(1)} %bitcast.10, f32[4,512,768]{2,1,0:T(8,128)S(1)} %embed.1.part.after, bf16[256,512]{1,0:T(8,128)(2,1)S(1)} %collective-permute-done.3.on_a.received_a, ...), custom_call_target="tpu_custom_call", output_to_operand_aliasing={{0}: (7, {})} | custom-call | tf_op jit(solution)/shard_map/embed_end/pallas_call | solution.py:390
  48.3 2.5 %collective-permute-done.9.got = bf16[64,768]{1,0:T(8,128)(2,1)S(1)} collective-permute-done((bf16[64,768]{1,0:T(8,128)(2,1)S(1)}, bf16[64,768]{1,0:T(8,128)(2,1)S(1)}, u32[]{:S(2)}, u32[]{:S(2)}) %collective-permute-start.9) | collective-permute-done | bytes 98336 | tf_op jit(solution)/shard_map/ppermute | solution.py:215
  51.1 2.4 %embed_end.6 = (bf16[2048,768]{1,0:T(8,128)(2,1)}, f32[8,128]{1,0:T(8,128)S(1)}) custom-call(s32[2,64]{1,0:T(2,128)S(1)} %bitcast.11, f32[4,512,768]{2,1,0:T(8,128)S(1)} %embed.1.part.after, bf16[256,512]{1,0:T(8,128)(2,1)S(1)} %collective-permute-done.3.on_a.received_a, ...), custom_call_target="tpu_custom_call", output_to_operand_aliasing={{0}: (7, {})} | custom-call | tf_op jit(solution)/shard_map/embed_end/pallas_call | solution.py:390
  53.5 3.5 %collective-permute-done.10.got = bf16[64,768]{1,0:T(8,128)(2,1)S(1)} collective-permute-done((bf16[64,768]{1,0:T(8,128)(2,1)S(1)}, bf16[64,768]{1,0:T(8,128)(2,1)S(1)}, u32[]{:S(2)}, u32[]{:S(2)}) %collective-permute-start.10) | collective-permute-done | bytes 98336 | tf_op jit(solution)/shard_map/ppermute | solution.py:215
  57.0 0.9 %collective-permute-start.11 = (bf16[64,768]{1,0:T(8,128)(2,1)S(1)}, bf16[64,768]{1,0:T(8,128)(2,1)S(1)}, u32[]{:S(2)}, u32[]{:S(2)}) collective-permute-start(bf16[64,768]{1,0:T(8,128)(2,1)S(1)} %add.5.held), channel_id=1, source_target_pairs={{0,2},{1,3},{2,0},{3,1},{4,6},{5,7},{6,4},{7,5},{8,10},{9,11},{10,... | collective-permute-start | bytes 294920 | tf_op jit(solution)/shard_map/ppermute | solution.py:215
  57.9 1.6 %embed_end.7 = (bf16[2048,768]{1,0:T(8,128)(2,1)}, f32[8,128]{1,0:T(8,128)S(1)}) custom-call(s32[2,64]{1,0:T(2,128)S(1)} %bitcast.12, f32[4,512,768]{2,1,0:T(8,128)S(1)} %embed.1.part.after, bf16[256,512]{1,0:T(8,128)(2,1)S(1)} %collective-permute-done.3.on_a.received_a, ...), custom_call_target="tpu_custom_call", output_to_operand_aliasing={{0}: (7, {})} | custom-call | tf_op jit(solution)/shard_map/embed_end/pallas_call | solution.py:390
  59.6 2.1 %collective-permute-done.11.got = bf16[64,768]{1,0:T(8,128)(2,1)S(1)} collective-permute-done((bf16[64,768]{1,0:T(8,128)(2,1)S(1)}, bf16[64,768]{1,0:T(8,128)(2,1)S(1)}, u32[]{:S(2)}, u32[]{:S(2)}) %collective-permute-start.11) | collective-permute-done | bytes 98336 | tf_op jit(solution)/shard_map/ppermute | solution.py:215
  61.8 0.8 %place.2.rest_0_ = f32[256,768]{1,0:T(8,128)} custom-call(bf16[128,768]{1,0:T(8,128)(2,1)S(1)} %join.1.held), custom_call_target="tpu_custom_call" | custom-call | tf_op jit(solution)/shard_map/place/pallas_call | solution.py:289
  62.6 0.6 collective-permute-done.12.held
  63.3 0.8 %place.3 = f32[256,768]{1,0:T(8,128)} custom-call(bf16[128,768]{1,0:T(8,128)(2,1)S(1)} %collective-permute-done.12.held, f32[256,768]{1,0:T(8,128)} %place.2.rest_0_), custom_call_target="tpu_custom_call", output_to_operand_aliasing={{}: (1, {})} | custom-call | tf_op jit(solution)/shard_map/place/pallas_call | solution.py:289
  (28 shorter events, 0.8 us)
Async XLA Ops:
  0.6 11.4 %copy-start.5 = (s32[256,8]{0,1:T(8,128)S(1)}, s32[256,8]{0,1:T(8,128)}, u32[]{:S(2)}) copy-start(s32[256,8]{0,1:T(8,128)} %param.11) | copy-start | bytes 24580
  0.6 16.1 %copy-start.3 = (s32[64,2]{0,1:T(2,128)S(1)}, s32[64,2]{0,1:T(2,128)}, u32[]{:S(2)}) copy-start(s32[64,2]{0,1:T(2,128)} %param.8) | copy-start | bytes 1540
  4.6 1.3 %copy-start = (f32[4,256,512]{2,1,0:T(8,128)}, f32[4,256,512]{2,1,0:T(8,128)S(1)}, u32[]{:S(2)}) copy-start(f32[4,256,512]{2,1,0:T(8,128)S(1)} %get-tuple-element.29.own) | copy-start | bytes 6291460
  5.9 10.8 %collective-permute-start = (bf16[2,256,512]{2,1,0:T(8,128)(2,1)}, bf16[2,256,512]{2,1,0:T(8,128)(2,1)}, u32[]{:S(2)}, u32[]{:S(2)}) collective-permute-start(bf16[2,256,512]{2,1,0:T(8,128)(2,1)} %get-tuple-element.30), channel_id=1, source_target_pairs={{0,1},{1,0},{2,3},{3,2},{4,5},{5,4},{6,7},{7,6},{8,9},{9,8},{10,11... | collective-permute-start | bytes 1572872 | tf_op jit(solution)/shard_map/ppermute | solution.py:215
  6.4 12.2 %collective-permute-start.2 = (bf16[256,512]{1,0:T(8,128)(2,1)}, bf16[256,512]{1,0:T(8,128)(2,1)}, u32[]{:S(2)}, u32[]{:S(2)}) collective-permute-start(bf16[256,512]{1,0:T(8,128)(2,1)} %get-tuple-element.34), channel_id=1, source_target_pairs={{1,2},{3,4},{5,6},{7,8},{9,10},{11,12},{13,14},{15,0},{2,1},{4,3},... | collective-permute-start | bytes 786440 | tf_op jit(solution)/shard_map/ppermute | solution.py:312
  12.0 14.4 %collective-permute-start.1 = (bf16[256,512]{1,0:T(8,128)(2,1)}, bf16[256,512]{1,0:T(8,128)(2,1)}, u32[]{:S(2)}, u32[]{:S(2)}) collective-permute-start(bf16[256,512]{1,0:T(8,128)(2,1)} %get-tuple-element.33), channel_id=1, source_target_pairs={{1,2},{3,4},{5,6},{7,8},{9,10},{11,12},{13,14},{15,0},{2,1},{4,3},... | collective-permute-start | bytes 786440 | tf_op jit(solution)/shard_map/ppermute | solution.py:312
  12.9 0.9 %copy-start.2 = (s32[256,8]{1,0:T(8,128)S(1)}, s32[256,8]{1,0:T(8,128)}, u32[]{:S(2)}) copy-start(s32[256,8]{1,0:T(8,128)} %copy.13.positives) | copy-start | bytes 24580
  13.8 3.0 %copy-start.1 = (f32[4,256,512]{2,1,0:T(8,128)S(1)}, f32[4,256,512]{2,1,0:T(8,128)}, u32[]{:S(2)}) copy-start(f32[4,256,512]{2,1,0:T(8,128)} %copy-done) | copy-start | bytes 6291460
  16.7 1.9 %copy-start.4 = (f32[2048]{0:T(1024)S(1)}, f32[2048]{0:T(1024)}, u32[]{:S(2)}) copy-start(f32[2048]{0:T(1024)} %param.9) | copy-start | bytes 24580
  21.2 10.8 %collective-permute-start.5 = (bf16[256,512]{1,0:T(8,128)(2,1)S(1)}, bf16[256,512]{1,0:T(8,128)(2,1)S(1)}, u32[]{:S(2)}, u32[]{:S(2)}) collective-permute-start(bf16[256,512]{1,0:T(8,128)(2,1)S(1)} %get-tuple-element.41), channel_id=1, source_target_pairs={{1,2},{3,4},{5,6},{7,8},{9,10},{11,12},{13,14},{15,0},{2,1},{4,3},... | collective-permute-start | bytes 786440 | tf_op jit(solution)/shard_map/ppermute | solution.py:312
  29.3 3.7 %collective-permute-start.3 = (bf16[256,512]{1,0:T(8,128)(2,1)S(1)}, bf16[256,512]{1,0:T(8,128)(2,1)S(1)}, u32[]{:S(2)}, u32[]{:S(2)}) collective-permute-start(bf16[256,512]{1,0:T(8,128)(2,1)S(1)} %get-tuple-element.39), channel_id=1, source_target_pairs={{0,1},{1,0},{2,3},{3,2},{4,5},{5,4},{6,7},{7,6},{8,9},{9,8},{10,11... | collective-permute-start | bytes 786440 | tf_op jit(solution)/shard_map/ppermute | solution.py:215
  29.3 3.7 %collective-permute-start.4 = (bf16[256,512]{1,0:T(8,128)(2,1)S(1)}, bf16[256,512]{1,0:T(8,128)(2,1)S(1)}, u32[]{:S(2)}, u32[]{:S(2)}) collective-permute-start(bf16[256,512]{1,0:T(8,128)(2,1)S(1)} %get-tuple-element.40), channel_id=1, source_target_pairs={{0,1},{1,0},{2,3},{3,2},{4,5},{5,4},{6,7},{7,6},{8,9},{9,8},{10,11... | collective-permute-start | bytes 786440 | tf_op jit(solution)/shard_map/ppermute | solution.py:215
  29.8 8.6 %collective-permute-start.6 = (bf16[256,512]{1,0:T(8,128)(2,1)S(1)}, bf16[256,512]{1,0:T(8,128)(2,1)S(1)}, u32[]{:S(2)}, u32[]{:S(2)}) collective-permute-start(bf16[256,512]{1,0:T(8,128)(2,1)S(1)} %get-tuple-element.42), channel_id=1, source_target_pairs={{1,2},{3,4},{5,6},{7,8},{9,10},{11,12},{13,14},{15,0},{2,1},{4,3},... | collective-permute-start | bytes 786440 | tf_op jit(solution)/shard_map/ppermute | solution.py:312
  39.4 1.8 %collective-permute-start.7 = (f32[128,768]{1,0:T(8,128)S(1)}, f32[128,768]{1,0:T(8,128)S(1)}, u32[]{:S(2)}, u32[]{:S(2)}) collective-permute-start(f32[128,768]{1,0:T(8,128)S(1)} %get-tuple-element.49), channel_id=1, source_target_pairs={{0,1},{1,0},{2,3},{3,2},{4,5},{5,4},{6,7},{7,6},{8,9},{9,8},{10,11... | collective-permute-start | bytes 1179656 | tf_op jit(solution)/shard_map/ppermute | solution.py:215
  41.3 4.9 %collective-permute-start.8 = (bf16[64,768]{1,0:T(8,128)(2,1)S(1)}, bf16[64,768]{1,0:T(8,128)(2,1)S(1)}, u32[]{:S(2)}, u32[]{:S(2)}) collective-permute-start(bf16[64,768]{1,0:T(8,128)(2,1)S(1)} %get-tuple-element.51), channel_id=1, source_target_pairs={{0,2},{1,3},{2,0},{3,1},{4,6},{5,7},{6,4},{7,5},{8,10},{9,11},{10,... | collective-permute-start | bytes 294920 | tf_op jit(solution)/shard_map/ppermute | solution.py:215
  46.2 4.7 %collective-permute-start.9 = (bf16[64,768]{1,0:T(8,128)(2,1)S(1)}, bf16[64,768]{1,0:T(8,128)(2,1)S(1)}, u32[]{:S(2)}, u32[]{:S(2)}) collective-permute-start(bf16[64,768]{1,0:T(8,128)(2,1)S(1)} %add.3.held), channel_id=1, source_target_pairs={{0,4},{1,5},{2,6},{3,7},{4,0},{5,1},{6,2},{7,3},{8,12},{9,13},{10,... | collective-permute-start | bytes 294920 | tf_op jit(solution)/shard_map/ppermute | solution.py:215
  50.9 6.1 %collective-permute-start.10 = (bf16[64,768]{1,0:T(8,128)(2,1)S(1)}, bf16[64,768]{1,0:T(8,128)(2,1)S(1)}, u32[]{:S(2)}, u32[]{:S(2)}) collective-permute-start(bf16[64,768]{1,0:T(8,128)(2,1)S(1)} %add.4.held), channel_id=1, source_target_pairs={{0,8},{1,9},{2,10},{3,11},{4,12},{5,13},{6,14},{7,15},{8,0},{9,1},... | collective-permute-start | bytes 294920 | tf_op jit(solution)/shard_map/ppermute | solution.py:215
  57.0 4.7 %collective-permute-start.11 = (bf16[64,768]{1,0:T(8,128)(2,1)S(1)}, bf16[64,768]{1,0:T(8,128)(2,1)S(1)}, u32[]{:S(2)}, u32[]{:S(2)}) collective-permute-start(bf16[64,768]{1,0:T(8,128)(2,1)S(1)} %add.5.held), channel_id=1, source_target_pairs={{0,2},{1,3},{2,0},{3,1},{4,6},{5,7},{6,4},{7,5},{8,10},{9,11},{10,... | collective-permute-start | bytes 294920 | tf_op jit(solution)/shard_map/ppermute | solution.py:215
  61.8 1.5 %collective-permute-start.12 = (bf16[128,768]{1,0:T(8,128)(2,1)S(1)}, bf16[128,768]{1,0:T(8,128)(2,1)S(1)}, u32[]{:S(2)}, u32[]{:S(2)}) collective-permute-start(bf16[128,768]{1,0:T(8,128)(2,1)S(1)} %join.1.held), channel_id=1, source_target_pairs={{0,1},{1,0},{2,3},{3,2},{4,5},{5,4},{6,7},{7,6},{8,9},{9,8},{10,11... | collective-permute-start | bytes 589832 | tf_op jit(solution)/shard_map/ppermute | solution.py:215

commit v6 on v5

--- a/solution.py
+++ b/solution.py
@@ -62,23 +62,54 @@
     return ref[pl.ds(pl.multiple_of(index * block, block), block), :]
 
 
-def project_kernel(lists, queries, embeddings, own, off_a, off_b, for_on, left, right, table, sem, *, scale):
-    blocks, _, block = own.shape
+def project_kernel(lists, queries, embeddings, out, left, right, table, sem, *, scale):
+    rows, block = out.shape
+    blocks = right.shape[0] // block
     fetches = [pltpu.make_async_copy(lists, table, sem.at[0]), pltpu.make_async_copy(queries, left, sem.at[1])]
     for g in range(blocks):
-        rows = pl.ds(g * block, block)
-        fetches.append(pltpu.make_async_copy(embeddings.at[rows, :], right.at[rows, :], sem.at[2 + g]))
+        place = pl.ds(g * block, block)
+        fetches.append(pltpu.make_async_copy(embeddings.at[place, :], right.at[place, :], sem.at[2 + g]))
     for fetch in fetches:
         fetch.start()
-    for fetch in fetches[:2]:
+    for fetch in fetches:
         fetch.wait()
+    first, _ = named_by_partner(table, blocks, OFF)
+    out[...] = (dot(left[...], block_rows(right, first, block), NT) * scale).astype(BF16)
+
+
+def spans_of(pieces, rows):
+    spans = []
+    begin = 0
+    for piece in pieces:
+        end = begin + piece.shape[0]
+        for slot in range(2):
+            low, high = max(begin, slot * rows), min(end, (slot + 1) * rows)
+            if low < high:
+                inside = slice(low - slot * rows, high - slot * rows)
+                spans.append((piece, slice(low - begin, high - begin), slot, inside))
+        begin = end
+    return spans
+
+
+def write_pieces(pieces, value):
+    rows = sum(piece.shape[0] for piece in pieces) // 2
+    for piece, place, slot, inside in spans_of(pieces, rows):
+        piece[place, :] = value(slot, inside).astype(BF16)
+
+
+def gather_pieces(pieces, whole):
+    for piece, place, slot, inside in spans_of(pieces, whole.shape[1]):
+        whole[slot, inside] = piece[place, :]
+
+
+def own_kernel(lists, queries, embeddings, own, off, *on, scale):
+    blocks, _, block = own.shape
     for g in range(blocks):
-        fetches[2 + g].wait()
-        own[g] = dot(left[...], right[g * block : (g + 1) * block, :], NT) * scale
-    for out, index in zip((off_a, off_b), named_by_partner(table, blocks, OFF)):
-        out[...] = own[index].astype(BF16)
-    for slot, index in enumerate(named_by_partner(table, blocks, ON)):
-        for_on[slot] = own[index].astype(BF16)
+        own[g] = dot(queries[...], embeddings[g * block : (g + 1) * block, :], NT) * scale
+    _, second = named_by_partner(lists, blocks, OFF)
+    off[...] = own[second].astype(BF16)
+    first, second = named_by_partner(lists, blocks, ON)
+    write_pieces(on, lambda slot, rows: own[(first, second)[slot], rows])
 
 
 def hits_kernel(positives, tiles, out, kept, sem):
@@ -87,15 +118,18 @@
     blocks, rows, block = out.shape
     first = lax.axis_index(AXIS) * blocks * block
     ids = lax.broadcasted_iota(jnp.int32, (rows, block), 1)
+    columns = jnp.transpose(positives[...]) - first
     for g in range(blocks):
         hits = jnp.zeros((rows, block), jnp.bool_)
-        for column in range(positives.shape[1]):
-            hits = jnp.logical_or(hits, ids == positives[:, column : column + 1] - (first + g * block))
+        for column in range(positives.shape[0]):
+            hits = jnp.logical_or(hits, ids + g * block == columns[:, column : column + 1])
         out[g] = jnp.where(hits, 1.0, 0.0).astype(BF16)
     fetch.wait()
 
 
-def base_kernel(lists, own, received, tiles, out):
+def base_kernel(lists, own, tiles, *rest):
+    *pieces, out, received = rest
+    gather_pieces(pieces, received)
     blocks = out.shape[0]
     side = tile_side(ON)
     for g, slot in enumerate(slots_of(lists, blocks, ON)):
@@ -103,33 +137,31 @@
 
 
 def signal_kernel(lists, base, hits, propensity, received, tiles, *rest, slot):
-    if slot == 0:
-        signal, push, carry, total, total_on = rest
-        total_on[...] = jnp.zeros_like(total_on)
-    else:
-        _, before, signal, push, push_on_a, push_on_b, total, total_on = rest
-        total_on[...] = before[...]
+    signal, push, total = rest[-3:]
     blocks, _, block = base.shape
-    side_off, side_on = tile_side(OFF), tile_side(ON)
-    slots_on = slots_of(lists, blocks, ON)
+    side = tile_side(OFF)
     total[...] = jnp.zeros_like(total)
     for g, taken in enumerate(slots_of(lists, blocks, OFF)):
 
         @pl.when(taken == slot)
         def _():
-            scores = base[g] + dot(received[...], tiles[g, side_off], NT)
+            scores = base[g] + dot(received[...], tiles[g, side], NT)
             inverse = 1.0 / propensity[:, g * block : (g + 1) * block]
             value = (jax.nn.sigmoid(scores) - hits[g].astype(F32) * inverse).astype(BF16)
             signal[g] = value
-            total[...] += dot(value, tiles[g, side_off], NN)
-            total_on[slots_on[g]] += dot(value, tiles[g, side_on], NN)
+            total[...] += dot(value, tiles[g, side], NN)
 
     push[...] = total[...].astype(BF16)
-    if slot == 0:
-        carry[...] = total_on[...]
-    else:
-        push_on_a[...] = total_on[0].astype(BF16)
-        push_on_b[...] = total_on[1].astype(BF16)
+
+
+def push_kernel(lists, signal, tiles, *rest):
+    *pieces, total = rest
+    blocks = signal.shape[0]
+    side = tile_side(ON)
+    total[...] = jnp.zeros_like(total)
+    for g, slot in enumerate(slots_of(lists, blocks, ON)):
+        total[slot] += dot(signal[g], tiles[g, side], NN)
+    write_pieces(pieces, lambda slot, rows: total[slot, rows])
 
 
 def query_kernel(signal, embeddings, out):
@@ -146,13 +178,15 @@
     out[...] = part[...] + dot(received[...], block_rows(embeddings, first, received.shape[1]), NN)
 
 
-def query_on_kernel(lists, part, received_a, received_b, embeddings, out, *, blocks):
-    block = received_a.shape[1]
+def query_on_kernel(lists, part, embeddings, *rest, blocks):
+    *pieces, out, received = rest
+    gather_pieces(pieces, received)
+    block = received.shape[2]
     first, second = named_by_partner(lists, blocks, ON)
     out[...] = (
         part[...]
-        + dot(received_a[...], block_rows(embeddings, first, block), NN)
-        + dot(received_b[...], block_rows(embeddings, second, block), NN)
+        + dot(received[0], block_rows(embeddings, first, block), NN)
+        + dot(received[1], block_rows(embeddings, second, block), NN)
     )
 
 
@@ -170,13 +204,13 @@
         out[g] = dot(signal[g], queries[...], TN)
 
 
-def embed_end_kernel(lists, part, on_a, on_b, off_a, off_b, queries, *rest, blocks, g, scale):
+def embed_end_kernel(lists, part, on, off_a, off_b, queries, *rest, blocks, g, scale):
     out, token, total, ready, sem = rest[-5:]
     block = part.shape[1]
     token[...] = jnp.zeros_like(token)
     total[...] = part[g]
     named = named_by_partner(lists, blocks, ON) + named_by_partner(lists, blocks, OFF)
-    for received, index in zip((on_a, on_b, off_a, off_b), named):
+    for received, index in zip((on.at[0], on.at[1], off_a, off_b), named):
 
         @pl.when(index == g)
         def _():
@@ -318,34 +352,43 @@
         return pltpu.VMEM(shape, dtype)
 
     one = in_vmem((rows, block), BF16)
+    pair = in_vmem((2, rows, block), BF16)
+    third = -(-2 * rows // 48) * 16
+    thirds = [in_vmem((size, block), BF16) for size in (third, third, 2 * rows - 2 * third)]
     full = (blocks, rows, block)
     scale = 1.0 / math.sqrt(width)
 
-    own, off_a, off_b, for_on, queries, embeddings = call(
+    off_a, queries, embeddings = call(
         functools.partial(project_kernel, scale=scale),
         "project",
         [HBM] * 3,
-        [
-            in_vmem(full, F32),
-            one,
-            one,
-            in_vmem((2, rows, block), BF16),
-            in_vmem(queries.shape, BF16),
-            in_vmem(embeddings.shape, BF16),
-        ],
+        [one, in_vmem(queries.shape, BF16), in_vmem(embeddings.shape, BF16)],
         scratch=[pltpu.SMEM(lists.shape, jnp.int32), pltpu.SemaphoreType.DMA((2 + blocks,))],
     )(*(pltpu.with_memory_space_constraint(x, pltpu.HBM) for x in (lists, queries, embeddings)))
     from_off_a = off_swap(off_a)
-    from_off_b = off_swap(off_b)
-    from_on = on_swap(for_on)
+    own, off_b, *for_on = call(
+        functools.partial(own_kernel, scale=scale),
+        "own",
+        [SMEM, VMEM, VMEM],
+        [in_vmem(full, F32), one] + thirds,
+    )(lists, queries, embeddings)
+    from_on = [on_swap(piece) for piece in for_on]
     hits, tiles = call(
         hits_kernel,
         "hits",
         [VMEM, HBM],
         [in_vmem(full, BF16), in_vmem(edge_tiles.shape, BF16)],
         scratch=[pltpu.SemaphoreType.DMA],
-    )(positives, pltpu.with_memory_space_constraint(edge_tiles, pltpu.HBM))
-    base = call(base_kernel, "base", [SMEM] + [VMEM] * 3, in_vmem(full, F32))(lists, own, from_on, tiles)
+    )(positives.T, pltpu.with_memory_space_constraint(edge_tiles, pltpu.HBM))
+    off_b, hits = lax.optimization_barrier((off_b, hits))
+    from_off_b = off_swap(off_b)
+    base = call(
+        base_kernel,
+        "base",
+        [SMEM] + [VMEM] * 5,
+        in_vmem(full, F32),
+        scratch=[pltpu.VMEM((2, rows, block), BF16)],
+    )(lists, own, tiles, *from_on)
     propensity = propensity.reshape(1, labels_dev)
 
     def signal_of(received, slot, *begun):
@@ -353,16 +396,24 @@
             functools.partial(signal_kernel, slot=slot),
             "signal",
             [SMEM] + [VMEM] * (5 + len(begun)),
-            [in_vmem(full, BF16), one] + ([one, one] if begun else [in_vmem((2, rows, block), F32)]),
-            scratch=[pltpu.VMEM((rows, block), F32), pltpu.VMEM((2, rows, block), F32)],
+            [in_vmem(full, BF16), one],
+            scratch=[pltpu.VMEM((rows, block), F32)],
             aliases={6: 0} if begun else None,
+            flops=0 if begun else 2 * 10**9,
         )(lists, base, hits, propensity, received, tiles, *begun)
 
-    signal, push_a, carry = signal_of(from_off_a, 0)
+    signal, push_a = signal_of(from_off_a, 0)
     back_a = off_swap(push_a)
-    signal, push_b, push_on_a, push_on_b = signal_of(from_off_b, 1, signal, carry)
+    signal, push_b = signal_of(from_off_b, 1, signal)
     back_b = off_swap(push_b)
-    on_a, on_b = on_swap(push_on_a), on_swap(push_on_b)
+    push_on = call(
+        push_kernel,
+        "push",
+        [SMEM, VMEM, VMEM],
+        thirds,
+        scratch=[pltpu.VMEM((2, rows, block), F32)],
+    )(lists, signal, tiles)
+    back_on = [on_swap(piece) for piece in push_on]
 
     whole = in_vmem((rows, width), F32)
     part = call(query_kernel, "query", [VMEM] * 2, whole)(signal, embeddings)
@@ -374,9 +425,9 @@
         whole,
         flops=10**9,
     )(lists, part, back_a, embeddings, embed)
-    part = call(functools.partial(query_on_kernel, blocks=blocks), "query_on", [SMEM] + [VMEM] * 4, whole)(
-        lists, part, on_a, on_b, embeddings
-    )
+    part, on = call(
+        functools.partial(query_on_kernel, blocks=blocks), "query_on", [SMEM] + [VMEM] * 5, [whole, pair]
+    )(lists, part, embeddings, *back_on)
     piece = in_vmem((rows // 2, width), F32)
     kept, sent = call(
         functools.partial(query_end_kernel, blocks=blocks),
@@ -390,7 +441,7 @@
         return call(
             functools.partial(embed_end_kernel, blocks=blocks, g=g, scale=1.0 / math.sqrt(rows)),
             "embed_end",
-            [SMEM] + [VMEM] * 6 + [ANY] * len(begun),
+            [SMEM] + [VMEM] * 5 + [ANY] * len(begun),
             [jax.ShapeDtypeStruct((labels_dev, width), BF16), in_vmem((8, 128), F32)],
             out_specs=[ANY, VMEM],
             scratch=[
@@ -398,8 +449,8 @@
                 pltpu.VMEM((block, width), BF16),
                 pltpu.SemaphoreType.DMA,
             ],
-            aliases={7: 0} if begun else None,
-        )(lists, embed, on_a, on_b, back_a, back_b, queries, *begun)
+            aliases={6: 0} if begun else None,
+        )(lists, embed, on, back_a, back_b, queries, *begun)
 
     begun, tokens = [], []
     for g in range(blocks):

time: 64.4 us -> 59.7 us (0.927)
  waiting for transfers between devices: 17.5 us -> 13.3 us
  starting transfers between devices: 13.5 us -> 17.1 us
  local copies, waits for them, and re-layouts: 3.03 us -> 0.01 us
  Pallas kernels: 29.1 us -> 28 us
    ppermute x4, waiting for transfers between devices: 4.26 us -> 0.35 us  [off_swap(): return lax.ppermute(value, AXIS, off_route)]
    ppermute x9 -> x12, starting transfers between devices: 2.43 us -> 5.84 us  [exchange(): return lax.ppermute(value, AXIS, [(i, i ^ mask) for i in range(count)])]
    unnamed x13 -> x6, local copies, waits for them, and re-layouts: 3.03 us -> 0.01 us
    pallas_call x1 -> x3, Pallas kernels: 1.85 us -> 4.39 us  [the longest x1 1.65 us: per_device(): call(functools.partial(own_kernel, scale=scale), 'own', [SMEM, VMEM, VMEM...]
    pallas_call x2, Pallas kernels: 5.43 us -> 3.53 us  [signal_of(): call(functools.partial(signal_kernel, slot=slot), 'signal', [SMEM] + [VME...]
    pallas_call x1, Pallas kernels: 3.92 us -> 2.43 us  [per_device(): call(functools.partial(project_kernel, scale=scale), 'project', [HBM] * 3...]
    ppermute x9 -> x12, waiting for transfers between devices: 13.2 us -> 13 us  [exchange(): return lax.ppermute(value, AXIS, [(i, i ^ mask) for i in range(count)])]
  transfers between devices with their start and end apart: 13 -> 16, of which waited for: 7 -> 7; matrix products, arithmetic and copies ran while one was open for 1% -> 0% of each run, Pallas kernels for 36% -> 40%
where the time goes in v6:
time: 59.7 us; the launch traced here: 59.5 us
  Pallas kernels  28 us (47%)
  starting transfers between devices  17.1 us (29%)
  waiting for transfers between devices  13.3 us (22%)
  between operations  1.07 us (2%)
    ppermute x12, waiting for transfers between devices, exchange(): return lax.ppermute(value, AXIS, [(i, i ^ mask) for i in range(count)])  13 us
    ppermute x4, starting transfers between devices, off_swap(): return lax.ppermute(value, AXIS, off_route)  11.3 us
    pallas_call x4, Pallas kernels, embed_end(): call(functools.partial(embed_end_kernel, blocks=blocks, g=g, scale=1.0 /...  8.35 us
    ppermute x12, starting transfers between devices, exchange(): return lax.ppermute(value, AXIS, [(i, i ^ mask) for i in range(count)])  5.84 us
    pallas_call x2, Pallas kernels, signal_of(): call(functools.partial(signal_kernel, slot=slot), 'signal', [SMEM] + [VME...  3.53 us
    pallas_call x1, Pallas kernels, per_device(): call(hits_kernel, 'hits', [VMEM, HBM], [in_vmem(full, BF16), in_vmem(edge...  2.45 us
    pallas_call x1, Pallas kernels, per_device(): call(functools.partial(project_kernel, scale=scale), 'project', [HBM] * 3...  2.43 us
    pallas_call x1, Pallas kernels, per_device(): call(functools.partial(own_kernel, scale=scale), 'own', [SMEM, VMEM, VMEM...  1.65 us
  transfers between devices with their start and end apart: 16, of which 7 were waited for; matrix products, arithmetic and copies ran while one was open for 0% of the time, Pallas kernels for 40%

profile of v6, /device:TPU:0, one launch (start us, length us, event | category | flops | bytes accessed | tf_op | source)
XLA Modules:
  0.0 59.5 jit_solution(5890298148114212259)
XLA Ops:
  0.7 2.4 %project.1 = (bf16[256,512]{1,0:T(8,128)(2,1)S(1)}, bf16[256,768]{1,0:T(8,128)(2,1)S(1)}, bf16[2048,768]{1,0:T(8,128)(2,1)S(1)}) custom-call(s32[2,64]{1,0:T(2,128)} %bitcast.3, bf16[256,768]{1,0:T(8,128)(2,1)} %queries.1, bf16[2048,768]{1,0:T(8,128)(2,1)} %embeddings.1), custom_call_target="tpu_custom_call" | custom-call | tf_op jit(solution)/shard_map/project/pallas_call | solution.py:361
  3.1 5.5 %collective-permute-start.4 = (bf16[256,512]{1,0:T(8,128)(2,1)S(1)}, bf16[256,512]{1,0:T(8,128)(2,1)S(1)}, u32[]{:S(2)}, u32[]{:S(2)}) collective-permute-start(bf16[256,512]{1,0:T(8,128)(2,1)S(1)} %get-tuple-element.46), channel_id=1, source_target_pairs={{1,2},{3,4},{5,6},{7,8},{9,10},{11,12},{13,14},{15,0},{2,1},{4,3},... | collective-permute-start | bytes 786440 | tf_op jit(solution)/shard_map/ppermute | solution.py:346
  8.6 1.6 %own.1 = (f32[4,256,512]{2,1,0:T(8,128)S(1)}, bf16[256,512]{1,0:T(8,128)(2,1)S(1)}, bf16[176,512]{1,0:T(8,128)(2,1)S(1)}, bf16[176,512]{1,0:T(8,128)(2,1)S(1)}, bf16[160,512]{1,0:T(8,128)(2,1)S(1)}) custom-call(s32[2,64]{1,0:T(2,128)S(1)} %bitcast.4, bf16[256,768]{1,0:T(8,128)(2,1)S(1)} %get-tuple-element.35.queries, ...), custom_call_target="tpu_custom_call" | custom-call | tf_op jit(solution)/shard_map/own/pallas_call | solution.py:369
  10.3 0.5 collective-permute-start.1
  10.9 2.4 %hits.1 = (bf16[4,256,512]{2,1,0:T(8,128)(2,1)S(1)}, bf16[4,2,512,512]{3,2,1,0:T(8,128)(2,1)S(1)}) custom-call(s32[8,256]{1,0:T(8,128)S(1)} %bitcast.18, bf16[4,2,512,512]{3,2,1,0:T(8,128)(2,1)} %tiles.1), custom_call_target="tpu_custom_call" | custom-call | tf_op jit(solution)/shard_map/hits/pallas_call | solution.py:376
  13.4 0.7 %collective-permute-start.3 = (bf16[256,512]{1,0:T(8,128)(2,1)S(1)}, bf16[256,512]{1,0:T(8,128)(2,1)S(1)}, u32[]{:S(2)}, u32[]{:S(2)}) collective-permute-start(bf16[256,512]{1,0:T(8,128)(2,1)S(1)} %get-tuple-element.45), channel_id=1, source_target_pairs={{1,2},{3,4},{5,6},{7,8},{9,10},{11,12},{13,14},{15,0},{2,1},{4,3},... | collective-permute-start | bytes 786440 | tf_op jit(solution)/shard_map/ppermute | solution.py:346
  14.1 1.3 %base.1 = f32[4,256,512]{2,1,0:T(8,128)S(1)} custom-call(s32[2,64]{1,0:T(2,128)S(1)} %bitcast.5, f32[4,256,512]{2,1,0:T(8,128)S(1)} %get-tuple-element.37.own, bf16[4,2,512,512]{3,2,1,0:T(8,128)(2,1)S(1)} %get-tuple-element.38.tiles, bf16[176,512]{1,0:T(8,128)(2,1)S(1)} %collective-permute-done.rest_0_, bf16[176,512]{1,0:T(8,128)(2,1)S(1)} %collective-permute-done.1.rest_1_, ...), custom_call_target="tpu_custom_call" | custom-call | tf_op jit(solution)/shard_map/base/pallas_call | solution.py:385
  15.5 1.2 %signal.2 = (bf16[4,256,512]{2,1,0:T(8,128)(2,1)S(1)}, bf16[256,512]{1,0:T(8,128)(2,1)S(1)}) custom-call(s32[2,64]{1,0:T(2,128)S(1)} %bitcast.6, f32[4,256,512]{2,1,0:T(8,128)S(1)} %base.1, bf16[4,256,512]{2,1,0:T(8,128)(2,1)S(1)} %get-tuple-element.44.hits, f32[1,2048]{1,0:T(1,128)S(1)} %bitcast.16, bf16[256,512]{1,0:T(8,128)(2,1)S(1)} %collective-permute-done.4.received, ...), custom_call_target="tpu_custom_call" | custom-call | flops 2000000000 | tf_op jit(solution)/shard_map/signal/pallas_call | solution.py:395
  16.7 5.0 %collective-permute-start.5 = (bf16[256,512]{1,0:T(8,128)(2,1)S(1)}, bf16[256,512]{1,0:T(8,128)(2,1)S(1)}, u32[]{:S(2)}, u32[]{:S(2)}) collective-permute-start(bf16[256,512]{1,0:T(8,128)(2,1)S(1)} %get-tuple-element.49), channel_id=1, source_target_pairs={{1,2},{3,4},{5,6},{7,8},{9,10},{11,12},{13,14},{15,0},{2,1},{4,3},... | collective-permute-start | bytes 786440 | tf_op jit(solution)/shard_map/ppermute | solution.py:346
  22.0 2.3 %signal.3 = (bf16[4,256,512]{2,1,0:T(8,128)(2,1)S(1)}, bf16[256,512]{1,0:T(8,128)(2,1)S(1)}) custom-call(s32[2,64]{1,0:T(2,128)S(1)} %bitcast.7, f32[4,256,512]{2,1,0:T(8,128)S(1)} %base.1, bf16[4,256,512]{2,1,0:T(8,128)(2,1)S(1)} %get-tuple-element.44.hits, f32[1,2048]{1,0:T(1,128)S(1)} %bitcast.17, ...), custom_call_target="tpu_custom_call", output_to_operand_aliasing={{0}: (6, {})} | custom-call | tf_op jit(solution)/shard_map/signal/pallas_call | solution.py:395
  24.5 1.4 %push.1 = (bf16[176,512]{1,0:T(8,128)(2,1)S(1)}, bf16[176,512]{1,0:T(8,128)(2,1)S(1)}, bf16[160,512]{1,0:T(8,128)(2,1)S(1)}) custom-call(s32[2,64]{1,0:T(2,128)S(1)} %bitcast.8, bf16[4,256,512]{2,1,0:T(8,128)(2,1)S(1)} %get-tuple-element.48.signal, bf16[4,2,512,512]{3,2,1,0:T(8,128)(2,1)S(1)} %get-tuple-element.38.tiles), custom_call_target="tpu_custom_call" | custom-call | tf_op jit(solution)/shard_map/push/pallas_call | solution.py:409
  25.9 2.6 %collective-permute-start.6 = (bf16[176,512]{1,0:T(8,128)(2,1)S(1)}, bf16[176,512]{1,0:T(8,128)(2,1)S(1)}, u32[]{:S(2)}, u32[]{:S(2)}) collective-permute-start(bf16[176,512]{1,0:T(8,128)(2,1)S(1)} %get-tuple-element.50), channel_id=1, source_target_pairs={{0,1},{1,0},{2,3},{3,2},{4,5},{5,4},{6,7},{7,6},{8,9},{9,8},{10,11... | collective-permute-start | bytes 540680 | tf_op jit(solution)/shard_map/ppermute | solution.py:249
  28.6 0.4 collective-permute-start.8
  29.0 1.0 %query.1.part = f32[256,768]{1,0:T(8,128)S(1)} custom-call(bf16[4,256,512]{2,1,0:T(8,128)(2,1)S(1)} %get-tuple-element.48.signal, bf16[2048,768]{1,0:T(8,128)(2,1)S(1)} %get-tuple-element.36.embeddings), custom_call_target="tpu_custom_call" | custom-call | tf_op jit(solution)/shard_map/query/pallas_call | solution.py:419
  30.0 1.0 %embed.1.after.part = f32[4,512,768]{2,1,0:T(8,128)S(1)} custom-call(bf16[4,256,512]{2,1,0:T(8,128)(2,1)S(1)} %get-tuple-element.48.signal, bf16[256,768]{1,0:T(8,128)(2,1)S(1)} %get-tuple-element.35.queries), custom_call_target="tpu_custom_call" | custom-call | tf_op jit(solution)/shard_map/embed/pallas_call | solution.py:420
  31.0 1.0 %query_half.1.part = f32[256,768]{1,0:T(8,128)S(1)} custom-call(s32[2,64]{1,0:T(2,128)S(1)} %bitcast.9, f32[256,768]{1,0:T(8,128)S(1)} %query.1.part, bf16[256,512]{1,0:T(8,128)(2,1)S(1)} %collective-permute-done.5.received.off_a, bf16[2048,768]{1,0:T(8,128)(2,1)S(1)} %get-tuple-element.36.embeddings, f32[4,512,768]{2,1,0:T(8,128)S(1)} %embed.1.after.part), custom_call_target="tpu_custom_call" | custom-call | flops 1000000000 | tf_op jit(solution)/shard_map/query_half/pallas_call | solution.py:421
  32.0 1.2 %query_on.1 = (f32[256,768]{1,0:T(8,128)S(1)}, bf16[2,256,512]{2,1,0:T(8,128)(2,1)S(1)}) custom-call(s32[2,64]{1,0:T(2,128)S(1)} %bitcast.10, f32[256,768]{1,0:T(8,128)S(1)} %query_half.1.part, bf16[2048,768]{1,0:T(8,128)(2,1)S(1)} %get-tuple-element.36.embeddings, bf16[176,512]{1,0:T(8,128)(2,1)S(1)} %collective-permute-done.6.rest_0_, ...), custom_call_target="tpu_custom_call" | custom-call | tf_op jit(solution)/shard_map/query_on/pallas_call | solution.py:428
  33.2 1.0 %query_end.1 = (f32[128,768]{1,0:T(8,128)S(1)}, f32[128,768]{1,0:T(8,128)S(1)}) custom-call(s32[2,64]{1,0:T(2,128)S(1)} %bitcast.11, f32[256,768]{1,0:T(8,128)S(1)} %get-tuple-element.59.part, bf16[256,512]{1,0:T(8,128)(2,1)S(1)} %collective-permute-done.9.off_b.received, bf16[2048,768]{1,0:T(8,128)(2,1)S(1)} %get-tuple-element.36.embeddings), custom_call_target="tpu_custom_call" | custom-call | tf_op jit(solution)/shard_map/query_end/pallas_call | solution.py:432
  34.2 0.8 %collective-permute-start.10 = (f32[128,768]{1,0:T(8,128)S(1)}, f32[128,768]{1,0:T(8,128)S(1)}, u32[]{:S(2)}, u32[]{:S(2)}) collective-permute-start(f32[128,768]{1,0:T(8,128)S(1)} %get-tuple-element.61), channel_id=1, source_target_pairs={{0,1},{1,0},{2,3},{3,2},{4,5},{5,4},{6,7},{7,6},{8,9},{9,8},{10,11... | collective-permute-start | bytes 1179656 | tf_op jit(solution)/shard_map/ppermute | solution.py:249
  35.0 1.3 %collective-permute-done.10.got = f32[128,768]{1,0:T(8,128)S(1)} collective-permute-done((f32[128,768]{1,0:T(8,128)S(1)}, f32[128,768]{1,0:T(8,128)S(1)}, u32[]{:S(2)}, u32[]{:S(2)}) %collective-permute-start.10) | collective-permute-done | bytes 393248 | tf_op jit(solution)/shard_map/ppermute | solution.py:249
  36.5 1.8 %embed_end.4 = (bf16[2048,768]{1,0:T(8,128)(2,1)}, f32[8,128]{1,0:T(8,128)S(1)}) custom-call(s32[2,64]{1,0:T(2,128)S(1)} %bitcast.12, f32[4,512,768]{2,1,0:T(8,128)S(1)} %embed.1.after.part, bf16[2,256,512]{2,1,0:T(8,128)(2,1)S(1)} %get-tuple-element.53.on, bf16[256,512]{1,0:T(8,128)(2,1)S(1)} %collective-permute-done.5.received.off_a, ...), custom_call_target="tpu_custom_call" | custom-call | tf_op jit(solution)/shard_map/embed_end/pallas_call | solution.py:441
  38.4 3.2 %collective-permute-done.11.got = bf16[64,768]{1,0:T(8,128)(2,1)S(1)} collective-permute-done((bf16[64,768]{1,0:T(8,128)(2,1)S(1)}, bf16[64,768]{1,0:T(8,128)(2,1)S(1)}, u32[]{:S(2)}, u32[]{:S(2)}) %collective-permute-start.11) | collective-permute-done | bytes 98336 | tf_op jit(solution)/shard_map/ppermute | solution.py:249
  41.6 2.0 %embed_end.5 = (bf16[2048,768]{1,0:T(8,128)(2,1)}, f32[8,128]{1,0:T(8,128)S(1)}) custom-call(s32[2,64]{1,0:T(2,128)S(1)} %bitcast.13, f32[4,512,768]{2,1,0:T(8,128)S(1)} %embed.1.after.part, bf16[2,256,512]{2,1,0:T(8,128)(2,1)S(1)} %get-tuple-element.53.on, ...), custom_call_target="tpu_custom_call", output_to_operand_aliasing={{0}: (6, {})} | custom-call | tf_op jit(solution)/shard_map/embed_end/pallas_call | solution.py:441
  43.7 2.6 %collective-permute-done.12.got = bf16[64,768]{1,0:T(8,128)(2,1)S(1)} collective-permute-done((bf16[64,768]{1,0:T(8,128)(2,1)S(1)}, bf16[64,768]{1,0:T(8,128)(2,1)S(1)}, u32[]{:S(2)}, u32[]{:S(2)}) %collective-permute-start.12) | collective-permute-done | bytes 98336 | tf_op jit(solution)/shard_map/ppermute | solution.py:249
  46.3 2.0 %embed_end.6 = (bf16[2048,768]{1,0:T(8,128)(2,1)}, f32[8,128]{1,0:T(8,128)S(1)}) custom-call(s32[2,64]{1,0:T(2,128)S(1)} %bitcast.14, f32[4,512,768]{2,1,0:T(8,128)S(1)} %embed.1.after.part, bf16[2,256,512]{2,1,0:T(8,128)(2,1)S(1)} %get-tuple-element.53.on, ...), custom_call_target="tpu_custom_call", output_to_operand_aliasing={{0}: (6, {})} | custom-call | tf_op jit(solution)/shard_map/embed_end/pallas_call | solution.py:441
  48.4 3.9 %collective-permute-done.13.got = bf16[64,768]{1,0:T(8,128)(2,1)S(1)} collective-permute-done((bf16[64,768]{1,0:T(8,128)(2,1)S(1)}, bf16[64,768]{1,0:T(8,128)(2,1)S(1)}, u32[]{:S(2)}, u32[]{:S(2)}) %collective-permute-start.13) | collective-permute-done | bytes 98336 | tf_op jit(solution)/shard_map/ppermute | solution.py:249
  52.4 0.9 %collective-permute-start.14 = (bf16[64,768]{1,0:T(8,128)(2,1)S(1)}, bf16[64,768]{1,0:T(8,128)(2,1)S(1)}, u32[]{:S(2)}, u32[]{:S(2)}) collective-permute-start(bf16[64,768]{1,0:T(8,128)(2,1)S(1)} %add.5.held), channel_id=1, source_target_pairs={{0,2},{1,3},{2,0},{3,1},{4,6},{5,7},{6,4},{7,5},{8,10},{9,11},{10,... | collective-permute-start | bytes 294920 | tf_op jit(solution)/shard_map/ppermute | solution.py:249
  53.3 2.4 %embed_end.7 = (bf16[2048,768]{1,0:T(8,128)(2,1)}, f32[8,128]{1,0:T(8,128)S(1)}) custom-call(s32[2,64]{1,0:T(2,128)S(1)} %bitcast.15, f32[4,512,768]{2,1,0:T(8,128)S(1)} %embed.1.after.part, bf16[2,256,512]{2,1,0:T(8,128)(2,1)S(1)} %get-tuple-element.53.on, ...), custom_call_target="tpu_custom_call", output_to_operand_aliasing={{0}: (6, {})} | custom-call | tf_op jit(solution)/shard_map/embed_end/pallas_call | solution.py:441
  55.7 1.3 %collective-permute-done.14.got = bf16[64,768]{1,0:T(8,128)(2,1)S(1)} collective-permute-done((bf16[64,768]{1,0:T(8,128)(2,1)S(1)}, bf16[64,768]{1,0:T(8,128)(2,1)S(1)}, u32[]{:S(2)}, u32[]{:S(2)}) %collective-permute-start.14) | collective-permute-done | bytes 98336 | tf_op jit(solution)/shard_map/ppermute | solution.py:249
  57.2 0.8 %place.2.rest_0_ = f32[256,768]{1,0:T(8,128)} custom-call(bf16[128,768]{1,0:T(8,128)(2,1)S(1)} %join.1.held), custom_call_target="tpu_custom_call" | custom-call | tf_op jit(solution)/shard_map/place/pallas_call | solution.py:323
  58.0 0.6 %collective-permute-done.15.held = bf16[128,768]{1,0:T(8,128)(2,1)S(1)} collective-permute-done((bf16[128,768]{1,0:T(8,128)(2,1)S(1)}, bf16[128,768]{1,0:T(8,128)(2,1)S(1)}, u32[]{:S(2)}, u32[]{:S(2)}) %collective-permute-start.15) | collective-permute-done | bytes 196640 | tf_op jit(solution)/shard_map/ppermute | solution.py:249
  58.6 0.8 %place.3 = f32[256,768]{1,0:T(8,128)} custom-call(bf16[128,768]{1,0:T(8,128)(2,1)S(1)} %collective-permute-done.15.held, f32[256,768]{1,0:T(8,128)} %place.2.rest_0_), custom_call_target="tpu_custom_call", output_to_operand_aliasing={{}: (1, {})} | custom-call | tf_op jit(solution)/shard_map/place/pallas_call | solution.py:323
  (29 shorter events, 1.2 us)
Async XLA Ops:
  0.6 8.0 %copy-start = (s32[64,2]{0,1:T(2,128)S(1)}, s32[64,2]{0,1:T(2,128)}, u32[]{:S(2)}) copy-start(s32[64,2]{0,1:T(2,128)} %param.8) | copy-start | bytes 1540
  0.6 10.3 %copy-start.2 = (s32[256,8]{0,1:T(8,128)S(1)}, s32[256,8]{0,1:T(8,128)}, u32[]{:S(2)}) copy-start(s32[256,8]{0,1:T(8,128)} %param.11) | copy-start | bytes 24580
  3.1 12.3 %collective-permute-start.4 = (bf16[256,512]{1,0:T(8,128)(2,1)S(1)}, bf16[256,512]{1,0:T(8,128)(2,1)S(1)}, u32[]{:S(2)}, u32[]{:S(2)}) collective-permute-start(bf16[256,512]{1,0:T(8,128)(2,1)S(1)} %get-tuple-element.46), channel_id=1, source_target_pairs={{1,2},{3,4},{5,6},{7,8},{9,10},{11,12},{13,14},{15,0},{2,1},{4,3},... | collective-permute-start | bytes 786440 | tf_op jit(solution)/shard_map/ppermute | solution.py:346
  10.3 3.8 %collective-permute-start = (bf16[176,512]{1,0:T(8,128)(2,1)S(1)}, bf16[176,512]{1,0:T(8,128)(2,1)S(1)}, u32[]{:S(2)}, u32[]{:S(2)}) collective-permute-start(bf16[176,512]{1,0:T(8,128)(2,1)S(1)} %get-tuple-element.39), channel_id=1, source_target_pairs={{0,1},{1,0},{2,3},{3,2},{4,5},{5,4},{6,7},{7,6},{8,9},{9,8},{10,11... | collective-permute-start | bytes 540680 | tf_op jit(solution)/shard_map/ppermute | solution.py:249
  10.3 3.7 %collective-permute-start.1 = (bf16[176,512]{1,0:T(8,128)(2,1)S(1)}, bf16[176,512]{1,0:T(8,128)(2,1)S(1)}, u32[]{:S(2)}, u32[]{:S(2)}) collective-permute-start(bf16[176,512]{1,0:T(8,128)(2,1)S(1)} %get-tuple-element.40), channel_id=1, source_target_pairs={{0,1},{1,0},{2,3},{3,2},{4,5},{5,4},{6,7},{7,6},{8,9},{9,8},{10,11... | collective-permute-start | bytes 540680 | tf_op jit(solution)/shard_map/ppermute | solution.py:249
  10.8 3.2 %collective-permute-start.2 = (bf16[160,512]{1,0:T(8,128)(2,1)S(1)}, bf16[160,512]{1,0:T(8,128)(2,1)S(1)}, u32[]{:S(2)}, u32[]{:S(2)}) collective-permute-start(bf16[160,512]{1,0:T(8,128)(2,1)S(1)} %get-tuple-element.41), channel_id=1, source_target_pairs={{0,1},{1,0},{2,3},{3,2},{4,5},{5,4},{6,7},{7,6},{8,9},{9,8},{10,11... | collective-permute-start | bytes 491528 | tf_op jit(solution)/shard_map/ppermute | solution.py:249
  13.4 8.7 %collective-permute-start.3 = (bf16[256,512]{1,0:T(8,128)(2,1)S(1)}, bf16[256,512]{1,0:T(8,128)(2,1)S(1)}, u32[]{:S(2)}, u32[]{:S(2)}) collective-permute-start(bf16[256,512]{1,0:T(8,128)(2,1)S(1)} %get-tuple-element.45), channel_id=1, source_target_pairs={{1,2},{3,4},{5,6},{7,8},{9,10},{11,12},{13,14},{15,0},{2,1},{4,3},... | collective-permute-start | bytes 786440 | tf_op jit(solution)/shard_map/ppermute | solution.py:346
  14.1 1.4 %copy-start.1 = (f32[2048]{0:T(1024)S(1)}, f32[2048]{0:T(1024)}, u32[]{:S(2)}) copy-start(f32[2048]{0:T(1024)} %param.9) | copy-start | bytes 24580
  16.7 14.4 %collective-permute-start.5 = (bf16[256,512]{1,0:T(8,128)(2,1)S(1)}, bf16[256,512]{1,0:T(8,128)(2,1)S(1)}, u32[]{:S(2)}, u32[]{:S(2)}) collective-permute-start(bf16[256,512]{1,0:T(8,128)(2,1)S(1)} %get-tuple-element.49), channel_id=1, source_target_pairs={{1,2},{3,4},{5,6},{7,8},{9,10},{11,12},{13,14},{15,0},{2,1},{4,3},... | collective-permute-start | bytes 786440 | tf_op jit(solution)/shard_map/ppermute | solution.py:346
  24.4 8.8 %collective-permute-start.9 = (bf16[256,512]{1,0:T(8,128)(2,1)S(1)}, bf16[256,512]{1,0:T(8,128)(2,1)S(1)}, u32[]{:S(2)}, u32[]{:S(2)}) collective-permute-start(bf16[256,512]{1,0:T(8,128)(2,1)S(1)} %get-tuple-element.54), channel_id=1, source_target_pairs={{1,2},{3,4},{5,6},{7,8},{9,10},{11,12},{13,14},{15,0},{2,1},{4,3},... | collective-permute-start | bytes 786440 | tf_op jit(solution)/shard_map/ppermute | solution.py:346
  25.9 6.1 %collective-permute-start.6 = (bf16[176,512]{1,0:T(8,128)(2,1)S(1)}, bf16[176,512]{1,0:T(8,128)(2,1)S(1)}, u32[]{:S(2)}, u32[]{:S(2)}) collective-permute-start(bf16[176,512]{1,0:T(8,128)(2,1)S(1)} %get-tuple-element.50), channel_id=1, source_target_pairs={{0,1},{1,0},{2,3},{3,2},{4,5},{5,4},{6,7},{7,6},{8,9},{9,8},{10,11... | collective-permute-start | bytes 540680 | tf_op jit(solution)/shard_map/ppermute | solution.py:249
  28.5 3.5 %collective-permute-start.7 = (bf16[176,512]{1,0:T(8,128)(2,1)S(1)}, bf16[176,512]{1,0:T(8,128)(2,1)S(1)}, u32[]{:S(2)}, u32[]{:S(2)}) collective-permute-start(bf16[176,512]{1,0:T(8,128)(2,1)S(1)} %get-tuple-element.51), channel_id=1, source_target_pairs={{0,1},{1,0},{2,3},{3,2},{4,5},{5,4},{6,7},{7,6},{8,9},{9,8},{10,11... | collective-permute-start | bytes 540680 | tf_op jit(solution)/shard_map/ppermute | solution.py:249
  28.6 3.4 %collective-permute-start.8 = (bf16[160,512]{1,0:T(8,128)(2,1)S(1)}, bf16[160,512]{1,0:T(8,128)(2,1)S(1)}, u32[]{:S(2)}, u32[]{:S(2)}) collective-permute-start(bf16[160,512]{1,0:T(8,128)(2,1)S(1)} %get-tuple-element.52), channel_id=1, source_target_pairs={{0,1},{1,0},{2,3},{3,2},{4,5},{5,4},{6,7},{7,6},{8,9},{9,8},{10,11... | collective-permute-start | bytes 491528 | tf_op jit(solution)/shard_map/ppermute | solution.py:249
  34.2 2.1 %collective-permute-start.10 = (f32[128,768]{1,0:T(8,128)S(1)}, f32[128,768]{1,0:T(8,128)S(1)}, u32[]{:S(2)}, u32[]{:S(2)}) collective-permute-start(f32[128,768]{1,0:T(8,128)S(1)} %get-tuple-element.61), channel_id=1, source_target_pairs={{0,1},{1,0},{2,3},{3,2},{4,5},{5,4},{6,7},{7,6},{8,9},{9,8},{10,11... | collective-permute-start | bytes 1179656 | tf_op jit(solution)/shard_map/ppermute | solution.py:249
  36.4 5.1 %collective-permute-start.11 = (bf16[64,768]{1,0:T(8,128)(2,1)S(1)}, bf16[64,768]{1,0:T(8,128)(2,1)S(1)}, u32[]{:S(2)}, u32[]{:S(2)}) collective-permute-start(bf16[64,768]{1,0:T(8,128)(2,1)S(1)} %get-tuple-element.63), channel_id=1, source_target_pairs={{0,2},{1,3},{2,0},{3,1},{4,6},{5,7},{6,4},{7,5},{8,10},{9,11},{10,... | collective-permute-start | bytes 294920 | tf_op jit(solution)/shard_map/ppermute | solution.py:249
  41.6 4.7 %collective-permute-start.12 = (bf16[64,768]{1,0:T(8,128)(2,1)S(1)}, bf16[64,768]{1,0:T(8,128)(2,1)S(1)}, u32[]{:S(2)}, u32[]{:S(2)}) collective-permute-start(bf16[64,768]{1,0:T(8,128)(2,1)S(1)} %add.3.held), channel_id=1, source_target_pairs={{0,4},{1,5},{2,6},{3,7},{4,0},{5,1},{6,2},{7,3},{8,12},{9,13},{10,... | collective-permute-start | bytes 294920 | tf_op jit(solution)/shard_map/ppermute | solution.py:249
  46.3 6.1 %collective-permute-start.13 = (bf16[64,768]{1,0:T(8,128)(2,1)S(1)}, bf16[64,768]{1,0:T(8,128)(2,1)S(1)}, u32[]{:S(2)}, u32[]{:S(2)}) collective-permute-start(bf16[64,768]{1,0:T(8,128)(2,1)S(1)} %add.4.held), channel_id=1, source_target_pairs={{0,8},{1,9},{2,10},{3,11},{4,12},{5,13},{6,14},{7,15},{8,0},{9,1},... | collective-permute-start | bytes 294920 | tf_op jit(solution)/shard_map/ppermute | solution.py:249
  52.4 4.7 %collective-permute-start.14 = (bf16[64,768]{1,0:T(8,128)(2,1)S(1)}, bf16[64,768]{1,0:T(8,128)(2,1)S(1)}, u32[]{:S(2)}, u32[]{:S(2)}) collective-permute-start(bf16[64,768]{1,0:T(8,128)(2,1)S(1)} %add.5.held), channel_id=1, source_target_pairs={{0,2},{1,3},{2,0},{3,1},{4,6},{5,7},{6,4},{7,5},{8,10},{9,11},{10,... | collective-permute-start | bytes 294920 | tf_op jit(solution)/shard_map/ppermute | solution.py:249
  57.1 1.5 %collective-permute-start.15 = (bf16[128,768]{1,0:T(8,128)(2,1)S(1)}, bf16[128,768]{1,0:T(8,128)(2,1)S(1)}, u32[]{:S(2)}, u32[]{:S(2)}) collective-permute-start(bf16[128,768]{1,0:T(8,128)(2,1)S(1)} %join.1.held), channel_id=1, source_target_pairs={{0,1},{1,0},{2,3},{3,2},{4,5},{5,4},{6,7},{7,6},{8,9},{9,8},{10,11... | collective-permute-start | bytes 589832 | tf_op jit(solution)/shard_map/ppermute | solution.py:249

commit v7 on v6

--- a/solution.py
+++ b/solution.py
@@ -71,10 +71,17 @@
         fetches.append(pltpu.make_async_copy(embeddings.at[place, :], right.at[place, :], sem.at[2 + g]))
     for fetch in fetches:
         fetch.start()
-    for fetch in fetches:
-        fetch.wait()
+    fetches[0].wait()
     first, _ = named_by_partner(table, blocks, OFF)
-    out[...] = (dot(left[...], block_rows(right, first, block), NT) * scale).astype(BF16)
+    fetches[1].wait()
+    place = pl.ds(pl.multiple_of(first * block, block), block)
+    pltpu.make_async_copy(embeddings.at[place, :], right.at[place, :], sem.at[2 + first]).wait()
+    out[...] = (dot(left[...], right[place, :], NT) * scale).astype(BF16)
+    for g in range(blocks):
+
+        @pl.when(g != first)
+        def _():
+            fetches[2 + g].wait()
 
 
 def spans_of(pieces, rows):
@@ -172,8 +179,7 @@
     out[...] = total
 
 
-def query_half_kernel(lists, part, received, embeddings, after, out, *, blocks):
-    del after
+def query_half_kernel(lists, part, received, embeddings, out, *, blocks):
     first, _ = named_by_partner(lists, blocks, OFF)
     out[...] = part[...] + dot(received[...], block_rows(embeddings, first, received.shape[1]), NN)
 
@@ -199,16 +205,11 @@
     sent[...] = total[pl.ds(pl.multiple_of((1 - core) * rows, rows), rows), :]
 
 
-def embed_kernel(signal, queries, out):
-    for g in range(signal.shape[0]):
-        out[g] = dot(signal[g], queries[...], TN)
-
-
-def embed_end_kernel(lists, part, on, off_a, off_b, queries, *rest, blocks, g, scale):
+def embed_kernel(lists, signal, on, off_a, off_b, queries, *rest, blocks, g, scale):
     out, token, total, ready, sem = rest[-5:]
-    block = part.shape[1]
+    block = signal.shape[2]
     token[...] = jnp.zeros_like(token)
-    total[...] = part[g]
+    total[...] = dot(signal[g], queries[...], TN)
     named = named_by_partner(lists, blocks, ON) + named_by_partner(lists, blocks, OFF)
     for received, index in zip((on.at[0], on.at[1], off_a, off_b), named):
 
@@ -249,25 +250,41 @@
     return lax.ppermute(value, AXIS, [(i, i ^ mask) for i in range(count)])
 
 
-def halve_kernel(held, got, kept, sent, *, bit):
-    rows = kept.shape[0]
-    digit = (lax.axis_index(AXIS) // bit) % 2
-    here = pl.ds(pl.multiple_of(digit * rows, rows), rows)
-    there = pl.ds(pl.multiple_of((1 - digit) * rows, rows), rows)
-    kept[...] = held[here, :] + got[here, :]
-    sent[...] = (held[there, :] + got[there, :]).astype(BF16)
-
-
-def add_kernel(held, got, *rest, scale):
-    rest[-1][...] = ((held[...].astype(F32) + got[...].astype(F32)) * scale).astype(BF16)
-
-
-def join_kernel(held, got, *rest, bit):
-    out = rest[-1]
-    rows = held.shape[0]
-    digit = (lax.axis_index(AXIS) // bit) % 2
-    out[pl.ds(pl.multiple_of(digit * rows, rows), rows), :] = held[...]
-    out[pl.ds(pl.multiple_of((1 - digit) * rows, rows), rows), :] = got[...]
+def in_vmem(shape, dtype):
+    return pltpu.VMEM(shape, dtype)
+
+
+def digit_of(bit):
+    return (lax.axis_index(AXIS) // bit) % 2
+
+
+def halve_kernel(held, got, *outs, bits):
+    total = outs[-1]
+    total[...] = held[...] + got[...]
+    rows = outs[0].shape[0]
+    for chain, bit in enumerate(bits):
+        kept, sent = outs[2 * chain], outs[2 * chain + 1]
+        begin = 2 * chain * rows
+        digit = digit_of(bit)
+        kept[...] = total[pl.ds(pl.multiple_of(begin + digit * rows, rows), rows), :]
+        sent[...] = total[pl.ds(pl.multiple_of(begin + (1 - digit) * rows, rows), rows), :].astype(BF16)
+
+
+def add_kernel(*refs, scale):
+    *ins, out_a, out_b = refs
+    for held, got, out in ((ins[0], ins[1], out_a), (ins[2], ins[3], out_b)):
+        out[...] = ((held[...].astype(F32) + got[...].astype(F32)) * scale).astype(BF16)
+
+
+def join_kernel(*refs, bits):
+    *ins, out = refs
+    rows = ins[0].shape[0]
+    for chain, bit in enumerate(bits):
+        held, got = ins[2 * chain], ins[2 * chain + 1]
+        begin = 2 * chain * rows
+        digit = digit_of(bit)
+        out[pl.ds(pl.multiple_of(begin + digit * rows, rows), rows), :] = held[...]
+        out[pl.ds(pl.multiple_of(begin + (1 - digit) * rows, rows), rows), :] = got[...]
 
 
 def place_kernel(held, *rest, own):
@@ -285,38 +302,41 @@
     count = lax.axis_size(AXIS)
     rows, width = kept.shape
     got = exchange(sent, 1)
-    if count & (count - 1) or count < 4:
+    if count & (count - 1) or count < 8:
         half = lax.psum(kept + got, AXIS, axis_index_groups=[list(range(c, count, 2)) for c in range(2)])
         both = jnp.stack([half, exchange(half, 1)])
         both = jnp.where(lax.axis_index(AXIS) % 2 == 0, both, both[::-1])
         return both.reshape(2 * rows, width) * scale
     piece = jax.ShapeDtypeStruct((rows // 2, width), BF16)
-    held, sent = call(
-        functools.partial(halve_kernel, bit=2),
+    bits = [1 << k for k in range(1, count.bit_length() - 1)]
+    orders = [[bits[0], *bits[2:], bits[1]], [bits[1], bits[0], *bits[2:]]]
+    ends = [order[0] for order in orders]
+    wide, narrow = in_vmem((rows // 4, width), F32), in_vmem((rows // 4, width), BF16)
+    kept_a, sent_a, kept_b, sent_b = call(
+        functools.partial(halve_kernel, bits=ends),
         "halve",
         [VMEM] * 2,
-        [jax.ShapeDtypeStruct(piece.shape, F32), piece],
+        [wide, narrow, wide, narrow],
+        scratch=[pltpu.VMEM((rows, width), F32)],
     )(kept, got)
-    got = exchange(sent, 2)
-    bits = [1 << k for k in range(2, count.bit_length() - 1)]
-    for k in range(len(bits) + 1):
-        last = k == len(bits)
+    held, sent = [kept_a, kept_b], [sent_a, sent_b]
+    for k in range(len(bits)):
+        got = [exchange(piece, order[k]) for piece, order in zip(sent, orders)]
         after = beside[k : k + 1]
-        held = call(
-            functools.partial(add_kernel, scale=scale if last else 1.0),
+        held = sent = call(
+            functools.partial(add_kernel, scale=scale if k == len(bits) - 1 else 1.0),
             "add",
-            [VMEM] * 2 + [ANY] * len(after),
-            piece,
-        )(held, got, *after)
-        if not last:
-            got = exchange(held, bits[k])
-    after = beside[len(bits) + 1 :]
+            [VMEM] * 4 + [ANY] * len(after),
+            [narrow, narrow],
+        )(held[0], got[0], held[1], got[1], *after)
+    got = [exchange(piece, bit) for piece, bit in zip(held, ends)]
+    after = beside[len(bits) :]
     held = call(
-        functools.partial(join_kernel, bit=2),
+        functools.partial(join_kernel, bits=ends),
         "join",
-        [VMEM] * 2 + [ANY] * len(after),
-        jax.ShapeDtypeStruct((rows, width), BF16),
-    )(held, exchange(held, 2), *after)
+        [VMEM] * 4 + [ANY] * len(after),
+        in_vmem((rows, width), BF16),
+    )(held[0], got[0], held[1], got[1], *after)
     got = exchange(held, 1)
 
     def place(half, own, *begun):
@@ -347,9 +367,6 @@
 
     def on_swap(value):
         return exchange(value, 1)
-
-    def in_vmem(shape, dtype):
-        return pltpu.VMEM(shape, dtype)
 
     one = in_vmem((rows, block), BF16)
     pair = in_vmem((2, rows, block), BF16)
@@ -417,14 +434,13 @@
 
     whole = in_vmem((rows, width), F32)
     part = call(query_kernel, "query", [VMEM] * 2, whole)(signal, embeddings)
-    embed = call(embed_kernel, "embed", [VMEM] * 2, in_vmem((blocks, block, width), F32))(signal, queries)
     part = call(
         functools.partial(query_half_kernel, blocks=blocks),
         "query_half",
-        [SMEM] + [VMEM] * 3 + [ANY],
+        [SMEM] + [VMEM] * 3,
         whole,
         flops=10**9,
-    )(lists, part, back_a, embeddings, embed)
+    )(lists, part, back_a, embeddings)
     part, on = call(
         functools.partial(query_on_kernel, blocks=blocks), "query_on", [SMEM] + [VMEM] * 5, [whole, pair]
     )(lists, part, embeddings, *back_on)
@@ -437,10 +453,10 @@
         scratch=[pltpu.VMEM((rows, width), F32)],
     )(lists, part, back_b, embeddings)
 
-    def embed_end(g, *begun):
+    def embed(g, *begun):
         return call(
-            functools.partial(embed_end_kernel, blocks=blocks, g=g, scale=1.0 / math.sqrt(rows)),
-            "embed_end",
+            functools.partial(embed_kernel, blocks=blocks, g=g, scale=1.0 / math.sqrt(rows)),
+            "embed",
             [SMEM] + [VMEM] * 5 + [ANY] * len(begun),
             [jax.ShapeDtypeStruct((labels_dev, width), BF16), in_vmem((8, 128), F32)],
             out_specs=[ANY, VMEM],
@@ -450,11 +466,11 @@
                 pltpu.SemaphoreType.DMA,
             ],
             aliases={6: 0} if begun else None,
-        )(lists, embed, on, back_a, back_b, queries, *begun)
+        )(lists, signal, on, back_a, back_b, queries, *begun)
 
     begun, tokens = [], []
     for g in range(blocks):
-        grad_embed, token = embed_end(g, *begun)
+        grad_embed, token = embed(g, *begun)
         begun = [grad_embed]
         tokens.append(token)
     grad_queries = sum_queries(kept, sent, tokens, 1.0 / math.sqrt(labels_dev * count))

time: 59.7 us -> 61 us (1.022)
  starting transfers between devices: 17.1 us -> 24 us
  waiting for transfers between devices: 13.3 us -> 7.81 us
    ppermute x12 -> x16, starting transfers between devices: 5.84 us -> 13.3 us  [exchange(): return lax.ppermute(value, AXIS, [(i, i ^ mask) for i in range(count)])]
    ppermute x12 -> x16, waiting for transfers between devices: 13 us -> 7.46 us  [exchange(): return lax.ppermute(value, AXIS, [(i, i ^ mask) for i in range(count)])]
    pallas_call x10 -> x9, Pallas kernels: 9.54 us -> 9.69 us  [the longest x4 9.51 us: embed(): call(functools.partial(embed_kernel, blocks=blocks, g=g, scale=1.0 / math...]
  transfers between devices with their start and end apart: 16 -> 20, of which waited for: 7 -> 10; matrix products, arithmetic and copies ran while one was open for 0% -> 0% of each run, Pallas kernels for 40% -> 39%
where the time goes in v7:
time: 61 us; the launch traced here: 60.7 us
  Pallas kernels  27.7 us (45%)
  starting transfers between devices  24 us (39%)
  waiting for transfers between devices  7.81 us (13%)
  between operations  1.07 us (2%)
    ppermute x16, starting transfers between devices, exchange(): return lax.ppermute(value, AXIS, [(i, i ^ mask) for i in range(count)])  13.3 us
    ppermute x4, starting transfers between devices, off_swap(): return lax.ppermute(value, AXIS, off_route)  10.8 us
    pallas_call x4, Pallas kernels, embed(): call(functools.partial(embed_kernel, blocks=blocks, g=g, scale=1.0 / math...  9.51 us
    ppermute x16, waiting for transfers between devices, exchange(): return lax.ppermute(value, AXIS, [(i, i ^ mask) for i in range(count)])  7.46 us
    pallas_call x2, Pallas kernels, signal_of(): call(functools.partial(signal_kernel, slot=slot), 'signal', [SMEM] + [VME...  3.53 us
    pallas_call x1, Pallas kernels, per_device(): call(hits_kernel, 'hits', [VMEM, HBM], [in_vmem(full, BF16), in_vmem(edge...  2.45 us
    pallas_call x1, Pallas kernels, per_device(): call(functools.partial(project_kernel, scale=scale), 'project', [HBM] * 3...  2.03 us
    pallas_call x1, Pallas kernels, per_device(): call(functools.partial(own_kernel, scale=scale), 'own', [SMEM, VMEM, VMEM...  1.65 us
  transfers between devices with their start and end apart: 20, of which 10 were waited for; matrix products, arithmetic and copies ran while one was open for 0% of the time, Pallas kernels for 39%

profile of v7, /device:TPU:0, one launch (start us, length us, event | category | flops | bytes accessed | tf_op | source)
XLA Modules:
  0.0 60.7 jit_solution(13485650348847682196)
XLA Ops:
  0.7 2.0 %project.1 = (bf16[256,512]{1,0:T(8,128)(2,1)S(1)}, bf16[256,768]{1,0:T(8,128)(2,1)S(1)}, bf16[2048,768]{1,0:T(8,128)(2,1)S(1)}) custom-call(s32[2,64]{1,0:T(2,128)} %bitcast.3, bf16[256,768]{1,0:T(8,128)(2,1)} %queries.1, bf16[2048,768]{1,0:T(8,128)(2,1)} %embeddings.1), custom_call_target="tpu_custom_call" | custom-call | tf_op jit(solution)/shard_map/project/pallas_call | solution.py:378
  2.7 5.5 %collective-permute-start.4 = (bf16[256,512]{1,0:T(8,128)(2,1)S(1)}, bf16[256,512]{1,0:T(8,128)(2,1)S(1)}, u32[]{:S(2)}, u32[]{:S(2)}) collective-permute-start(bf16[256,512]{1,0:T(8,128)(2,1)S(1)} %get-tuple-element.54), channel_id=1, source_target_pairs={{1,2},{3,4},{5,6},{7,8},{9,10},{11,12},{13,14},{15,0},{2,1},{4,3},... | collective-permute-start | bytes 786440 | tf_op jit(solution)/shard_map/ppermute | solution.py:366
  8.2 1.6 %own.1 = (f32[4,256,512]{2,1,0:T(8,128)S(1)}, bf16[256,512]{1,0:T(8,128)(2,1)S(1)}, bf16[176,512]{1,0:T(8,128)(2,1)S(1)}, bf16[176,512]{1,0:T(8,128)(2,1)S(1)}, bf16[160,512]{1,0:T(8,128)(2,1)S(1)}) custom-call(s32[2,64]{1,0:T(2,128)S(1)} %bitcast.4, bf16[256,768]{1,0:T(8,128)(2,1)S(1)} %get-tuple-element.43.queries, ...), custom_call_target="tpu_custom_call" | custom-call | tf_op jit(solution)/shard_map/own/pallas_call | solution.py:386
  10.5 2.4 %hits.1 = (bf16[4,256,512]{2,1,0:T(8,128)(2,1)S(1)}, bf16[4,2,512,512]{3,2,1,0:T(8,128)(2,1)S(1)}) custom-call(s32[8,256]{1,0:T(8,128)S(1)} %bitcast.18, bf16[4,2,512,512]{3,2,1,0:T(8,128)(2,1)} %tiles.1), custom_call_target="tpu_custom_call" | custom-call | tf_op jit(solution)/shard_map/hits/pallas_call | solution.py:393
  13.0 0.7 %collective-permute-start.3 = (bf16[256,512]{1,0:T(8,128)(2,1)S(1)}, bf16[256,512]{1,0:T(8,128)(2,1)S(1)}, u32[]{:S(2)}, u32[]{:S(2)}) collective-permute-start(bf16[256,512]{1,0:T(8,128)(2,1)S(1)} %get-tuple-element.53), channel_id=1, source_target_pairs={{1,2},{3,4},{5,6},{7,8},{9,10},{11,12},{13,14},{15,0},{2,1},{4,3},... | collective-permute-start | bytes 786440 | tf_op jit(solution)/shard_map/ppermute | solution.py:366
  13.7 1.4 %base.1 = f32[4,256,512]{2,1,0:T(8,128)S(1)} custom-call(s32[2,64]{1,0:T(2,128)S(1)} %bitcast.5, f32[4,256,512]{2,1,0:T(8,128)S(1)} %get-tuple-element.45.own, bf16[4,2,512,512]{3,2,1,0:T(8,128)(2,1)S(1)} %get-tuple-element.46.tiles, bf16[176,512]{1,0:T(8,128)(2,1)S(1)} %collective-permute-done.rest_0_, bf16[176,512]{1,0:T(8,128)(2,1)S(1)} %collective-permute-done.1.rest_1_, ...), custom_call_target="tpu_custom_call" | custom-call | tf_op jit(solution)/shard_map/base/pallas_call | solution.py:402
  15.1 2.3 %signal.2 = (bf16[4,256,512]{2,1,0:T(8,128)(2,1)S(1)}, bf16[256,512]{1,0:T(8,128)(2,1)S(1)}) custom-call(s32[2,64]{1,0:T(2,128)S(1)} %bitcast.6, f32[4,256,512]{2,1,0:T(8,128)S(1)} %base.1, bf16[4,256,512]{2,1,0:T(8,128)(2,1)S(1)} %get-tuple-element.52.hits, f32[1,2048]{1,0:T(1,128)S(1)} %bitcast.16, bf16[256,512]{1,0:T(8,128)(2,1)S(1)} %collective-permute-done.4.received, ...), custom_call_target="tpu_custom_call" | custom-call | flops 2000000000 | tf_op jit(solution)/shard_map/signal/pallas_call | solution.py:412
  17.4 3.9 %collective-permute-start.5 = (bf16[256,512]{1,0:T(8,128)(2,1)S(1)}, bf16[256,512]{1,0:T(8,128)(2,1)S(1)}, u32[]{:S(2)}, u32[]{:S(2)}) collective-permute-start(bf16[256,512]{1,0:T(8,128)(2,1)S(1)} %get-tuple-element.57), channel_id=1, source_target_pairs={{1,2},{3,4},{5,6},{7,8},{9,10},{11,12},{13,14},{15,0},{2,1},{4,3},... | collective-permute-start | bytes 786440 | tf_op jit(solution)/shard_map/ppermute | solution.py:366
  21.6 1.2 %signal.3 = (bf16[4,256,512]{2,1,0:T(8,128)(2,1)S(1)}, bf16[256,512]{1,0:T(8,128)(2,1)S(1)}) custom-call(s32[2,64]{1,0:T(2,128)S(1)} %bitcast.7, f32[4,256,512]{2,1,0:T(8,128)S(1)} %base.1, bf16[4,256,512]{2,1,0:T(8,128)(2,1)S(1)} %get-tuple-element.52.hits, f32[1,2048]{1,0:T(1,128)S(1)} %bitcast.17, ...), custom_call_target="tpu_custom_call", output_to_operand_aliasing={{0}: (6, {})} | custom-call | tf_op jit(solution)/shard_map/signal/pallas_call | solution.py:412
  22.8 0.7 %collective-permute-start.9 = (bf16[256,512]{1,0:T(8,128)(2,1)S(1)}, bf16[256,512]{1,0:T(8,128)(2,1)S(1)}, u32[]{:S(2)}, u32[]{:S(2)}) collective-permute-start(bf16[256,512]{1,0:T(8,128)(2,1)S(1)} %get-tuple-element.62), channel_id=1, source_target_pairs={{1,2},{3,4},{5,6},{7,8},{9,10},{11,12},{13,14},{15,0},{2,1},{4,3},... | collective-permute-start | bytes 786440 | tf_op jit(solution)/shard_map/ppermute | solution.py:366
  23.5 1.4 %push.1 = (bf16[176,512]{1,0:T(8,128)(2,1)S(1)}, bf16[176,512]{1,0:T(8,128)(2,1)S(1)}, bf16[160,512]{1,0:T(8,128)(2,1)S(1)}) custom-call(s32[2,64]{1,0:T(2,128)S(1)} %bitcast.8, bf16[4,256,512]{2,1,0:T(8,128)(2,1)S(1)} %get-tuple-element.56.signal, bf16[4,2,512,512]{3,2,1,0:T(8,128)(2,1)S(1)} %get-tuple-element.46.tiles), custom_call_target="tpu_custom_call" | custom-call | tf_op jit(solution)/shard_map/push/pallas_call | solution.py:426
  24.9 3.8 %collective-permute-start.6 = (bf16[176,512]{1,0:T(8,128)(2,1)S(1)}, bf16[176,512]{1,0:T(8,128)(2,1)S(1)}, u32[]{:S(2)}, u32[]{:S(2)}) collective-permute-start(bf16[176,512]{1,0:T(8,128)(2,1)S(1)} %get-tuple-element.58), channel_id=1, source_target_pairs={{0,1},{1,0},{2,3},{3,2},{4,5},{5,4},{6,7},{7,6},{8,9},{9,8},{10,11... | collective-permute-start | bytes 540680 | tf_op jit(solution)/shard_map/ppermute | solution.py:250
  29.3 1.0 %query.1.part = f32[256,768]{1,0:T(8,128)S(1)} custom-call(bf16[4,256,512]{2,1,0:T(8,128)(2,1)S(1)} %get-tuple-element.56.signal, bf16[2048,768]{1,0:T(8,128)(2,1)S(1)} %get-tuple-element.44.embeddings), custom_call_target="tpu_custom_call" | custom-call | tf_op jit(solution)/shard_map/query/pallas_call | solution.py:436
  30.3 0.9 %query_half.1.part = f32[256,768]{1,0:T(8,128)S(1)} custom-call(s32[2,64]{1,0:T(2,128)S(1)} %bitcast.9, f32[256,768]{1,0:T(8,128)S(1)} %query.1.part, bf16[256,512]{1,0:T(8,128)(2,1)S(1)} %collective-permute-done.5.received.off_a, bf16[2048,768]{1,0:T(8,128)(2,1)S(1)} %get-tuple-element.44.embeddings), custom_call_target="tpu_custom_call" | custom-call | flops 1000000000 | tf_op jit(solution)/shard_map/query_half/pallas_call | solution.py:437
  31.3 1.2 %query_on.1 = (f32[256,768]{1,0:T(8,128)S(1)}, bf16[2,256,512]{2,1,0:T(8,128)(2,1)S(1)}) custom-call(s32[2,64]{1,0:T(2,128)S(1)} %bitcast.10, f32[256,768]{1,0:T(8,128)S(1)} %query_half.1.part, bf16[2048,768]{1,0:T(8,128)(2,1)S(1)} %get-tuple-element.44.embeddings, bf16[176,512]{1,0:T(8,128)(2,1)S(1)} %collective-permute-done.6.rest_0_, ...), custom_call_target="tpu_custom_call" | custom-call | tf_op jit(solution)/shard_map/query_on/pallas_call | solution.py:444
  32.4 1.0 %query_end.1 = (f32[128,768]{1,0:T(8,128)S(1)}, f32[128,768]{1,0:T(8,128)S(1)}) custom-call(s32[2,64]{1,0:T(2,128)S(1)} %bitcast.11, f32[256,768]{1,0:T(8,128)S(1)} %get-tuple-element.67.part, bf16[256,512]{1,0:T(8,128)(2,1)S(1)} %collective-permute-done.9.off_b.received, bf16[2048,768]{1,0:T(8,128)(2,1)S(1)} %get-tuple-element.44.embeddings), custom_call_target="tpu_custom_call" | custom-call | tf_op jit(solution)/shard_map/query_end/pallas_call | solution.py:448
  33.5 1.6 %collective-permute-start.10 = (f32[128,768]{1,0:T(8,128)S(1)}, f32[128,768]{1,0:T(8,128)S(1)}, u32[]{:S(2)}, u32[]{:S(2)}) collective-permute-start(f32[128,768]{1,0:T(8,128)S(1)} %get-tuple-element.69), channel_id=1, source_target_pairs={{0,1},{1,0},{2,3},{3,2},{4,5},{5,4},{6,7},{7,6},{8,9},{9,8},{10,11... | collective-permute-start | bytes 1179656 | tf_op jit(solution)/shard_map/ppermute | solution.py:250
  35.1 1.3 %collective-permute-done.10.got = f32[128,768]{1,0:T(8,128)S(1)} collective-permute-done((f32[128,768]{1,0:T(8,128)S(1)}, f32[128,768]{1,0:T(8,128)S(1)}, u32[]{:S(2)}, u32[]{:S(2)}) %collective-permute-start.10) | collective-permute-done | bytes 393248 | tf_op jit(solution)/shard_map/ppermute | solution.py:250
  36.7 2.9 %embed.4 = (bf16[2048,768]{1,0:T(8,128)(2,1)}, f32[8,128]{1,0:T(8,128)S(1)}) custom-call(s32[2,64]{1,0:T(2,128)S(1)} %bitcast.12, bf16[4,256,512]{2,1,0:T(8,128)(2,1)S(1)} %get-tuple-element.56.signal, bf16[2,256,512]{2,1,0:T(8,128)(2,1)S(1)} %get-tuple-element.61.on, bf16[256,512]{1,0:T(8,128)(2,1)S(1)} %collective-permute-done.5.received.off_a, ...), custom_call_target="tpu_custom_call" | custom-call | tf_op jit(solution)/shard_map/embed/pallas_call | solution.py:457
  39.6 1.1 %collective-permute-done.11.refs_1_ = bf16[32,768]{1,0:T(8,128)(2,1)S(1)} collective-permute-done((bf16[32,768]{1,0:T(8,128)(2,1)S(1)}, bf16[32,768]{1,0:T(8,128)(2,1)S(1)}, u32[]{:S(2)}, u32[]{:S(2)}) %collective-permute-start.11) | collective-permute-done | bytes 49184 | tf_op jit(solution)/shard_map/ppermute | solution.py:250
  40.8 2.2 %collective-permute-start.13 = (bf16[32,768]{1,0:T(8,128)(2,1)S(1)}, bf16[32,768]{1,0:T(8,128)(2,1)S(1)}, u32[]{:S(2)}, u32[]{:S(2)}) collective-permute-start(bf16[32,768]{1,0:T(8,128)(2,1)S(1)} %get-tuple-element.75.refs_0_), channel_id=1, source_target_pairs={{0,8},{1,9},{2,10},{3,11},{4,12},{5,13},{6,14},{7,15},{8,0},{9,1},... | collective-permute-start | bytes 147464 | tf_op jit(solution)/shard_map/ppermute | solution.py:250
  43.1 1.9 %embed.5 = (bf16[2048,768]{1,0:T(8,128)(2,1)}, f32[8,128]{1,0:T(8,128)S(1)}) custom-call(s32[2,64]{1,0:T(2,128)S(1)} %bitcast.13, bf16[4,256,512]{2,1,0:T(8,128)(2,1)S(1)} %get-tuple-element.56.signal, bf16[2,256,512]{2,1,0:T(8,128)(2,1)S(1)} %get-tuple-element.61.on, ...), custom_call_target="tpu_custom_call", output_to_operand_aliasing={{0}: (6, {})} | custom-call | tf_op jit(solution)/shard_map/embed/pallas_call | solution.py:457
  45.0 1.2 %collective-permute-done.13.refs_1_ = bf16[32,768]{1,0:T(8,128)(2,1)S(1)} collective-permute-done((bf16[32,768]{1,0:T(8,128)(2,1)S(1)}, bf16[32,768]{1,0:T(8,128)(2,1)S(1)}, u32[]{:S(2)}, u32[]{:S(2)}) %collective-permute-start.13) | collective-permute-done | bytes 49184 | tf_op jit(solution)/shard_map/ppermute | solution.py:250
  46.2 0.9 %collective-permute-done.14.refs_3_ = bf16[32,768]{1,0:T(8,128)(2,1)S(1)} collective-permute-done((bf16[32,768]{1,0:T(8,128)(2,1)S(1)}, bf16[32,768]{1,0:T(8,128)(2,1)S(1)}, u32[]{:S(2)}, u32[]{:S(2)}) %collective-permute-start.14) | collective-permute-done | bytes 49184 | tf_op jit(solution)/shard_map/ppermute | solution.py:250
  47.2 1.2 %collective-permute-start.15 = (bf16[32,768]{1,0:T(8,128)(2,1)S(1)}, bf16[32,768]{1,0:T(8,128)(2,1)S(1)}, u32[]{:S(2)}, u32[]{:S(2)}) collective-permute-start(bf16[32,768]{1,0:T(8,128)(2,1)S(1)} %get-tuple-element.78.refs_0_), channel_id=1, source_target_pairs={{0,4},{1,5},{2,6},{3,7},{4,0},{5,1},{6,2},{7,3},{8,12},{9,13},{10,... | collective-permute-start | bytes 147464 | tf_op jit(solution)/shard_map/ppermute | solution.py:250
  48.4 1.4 %collective-permute-start.16 = (bf16[32,768]{1,0:T(8,128)(2,1)S(1)}, bf16[32,768]{1,0:T(8,128)(2,1)S(1)}, u32[]{:S(2)}, u32[]{:S(2)}) collective-permute-start(bf16[32,768]{1,0:T(8,128)(2,1)S(1)} %get-tuple-element.79.refs_2_), channel_id=1, source_target_pairs={{0,8},{1,9},{2,10},{3,11},{4,12},{5,13},{6,14},{7,15},{8,0},{9,1},... | collective-permute-start | bytes 147464 | tf_op jit(solution)/shard_map/ppermute | solution.py:250
  49.8 2.3 %embed.6 = (bf16[2048,768]{1,0:T(8,128)(2,1)}, f32[8,128]{1,0:T(8,128)S(1)}) custom-call(s32[2,64]{1,0:T(2,128)S(1)} %bitcast.14, bf16[4,256,512]{2,1,0:T(8,128)(2,1)S(1)} %get-tuple-element.56.signal, bf16[2,256,512]{2,1,0:T(8,128)(2,1)S(1)} %get-tuple-element.61.on, ...), custom_call_target="tpu_custom_call", output_to_operand_aliasing={{0}: (6, {})} | custom-call | tf_op jit(solution)/shard_map/embed/pallas_call | solution.py:457
  52.2 1.7 %collective-permute-done.16.refs_3_ = bf16[32,768]{1,0:T(8,128)(2,1)S(1)} collective-permute-done((bf16[32,768]{1,0:T(8,128)(2,1)S(1)}, bf16[32,768]{1,0:T(8,128)(2,1)S(1)}, u32[]{:S(2)}, u32[]{:S(2)}) %collective-permute-start.16) | collective-permute-done | bytes 49184 | tf_op jit(solution)/shard_map/ppermute | solution.py:250
  54.0 1.4 %collective-permute-start.18 = (bf16[32,768]{1,0:T(8,128)(2,1)S(1)}, bf16[32,768]{1,0:T(8,128)(2,1)S(1)}, u32[]{:S(2)}, u32[]{:S(2)}) collective-permute-start(bf16[32,768]{1,0:T(8,128)(2,1)S(1)} %get-tuple-element.82.refs_2_), channel_id=1, source_target_pairs={{0,4},{1,5},{2,6},{3,7},{4,0},{5,1},{6,2},{7,3},{8,12},{9,13},{10,... | collective-permute-start | bytes 147464 | tf_op jit(solution)/shard_map/ppermute | solution.py:250
  55.5 2.3 %embed.7 = (bf16[2048,768]{1,0:T(8,128)(2,1)}, f32[8,128]{1,0:T(8,128)S(1)}) custom-call(s32[2,64]{1,0:T(2,128)S(1)} %bitcast.15, bf16[4,256,512]{2,1,0:T(8,128)(2,1)S(1)} %get-tuple-element.56.signal, bf16[2,256,512]{2,1,0:T(8,128)(2,1)S(1)} %get-tuple-element.61.on, ...), custom_call_target="tpu_custom_call", output_to_operand_aliasing={{0}: (6, {})} | custom-call | tf_op jit(solution)/shard_map/embed/pallas_call | solution.py:457
  58.3 0.8 %place.2.rest_0_ = f32[256,768]{1,0:T(8,128)} custom-call(bf16[128,768]{1,0:T(8,128)(2,1)S(1)} %join.1.held), custom_call_target="tpu_custom_call" | custom-call | tf_op jit(solution)/shard_map/place/pallas_call | solution.py:343
  59.7 0.8 %place.3 = f32[256,768]{1,0:T(8,128)} custom-call(bf16[128,768]{1,0:T(8,128)(2,1)S(1)} %collective-permute-done.19.held, f32[256,768]{1,0:T(8,128)} %place.2.rest_0_), custom_call_target="tpu_custom_call", output_to_operand_aliasing={{}: (1, {})} | custom-call | tf_op jit(solution)/shard_map/place/pallas_call | solution.py:343
  (36 shorter events, 3.1 us)
Async XLA Ops:
  0.6 7.6 %copy-start = (s32[64,2]{0,1:T(2,128)S(1)}, s32[64,2]{0,1:T(2,128)}, u32[]{:S(2)}) copy-start(s32[64,2]{0,1:T(2,128)} %param.8) | copy-start | bytes 1540
  0.6 9.9 %copy-start.2 = (s32[256,8]{0,1:T(8,128)S(1)}, s32[256,8]{0,1:T(8,128)}, u32[]{:S(2)}) copy-start(s32[256,8]{0,1:T(8,128)} %param.11) | copy-start | bytes 24580
  2.7 12.3 %collective-permute-start.4 = (bf16[256,512]{1,0:T(8,128)(2,1)S(1)}, bf16[256,512]{1,0:T(8,128)(2,1)S(1)}, u32[]{:S(2)}, u32[]{:S(2)}) collective-permute-start(bf16[256,512]{1,0:T(8,128)(2,1)S(1)} %get-tuple-element.54), channel_id=1, source_target_pairs={{1,2},{3,4},{5,6},{7,8},{9,10},{11,12},{13,14},{15,0},{2,1},{4,3},... | collective-permute-start | bytes 786440 | tf_op jit(solution)/shard_map/ppermute | solution.py:366
  9.9 3.8 %collective-permute-start = (bf16[176,512]{1,0:T(8,128)(2,1)S(1)}, bf16[176,512]{1,0:T(8,128)(2,1)S(1)}, u32[]{:S(2)}, u32[]{:S(2)}) collective-permute-start(bf16[176,512]{1,0:T(8,128)(2,1)S(1)} %get-tuple-element.47), channel_id=1, source_target_pairs={{0,1},{1,0},{2,3},{3,2},{4,5},{5,4},{6,7},{7,6},{8,9},{9,8},{10,11... | collective-permute-start | bytes 540680 | tf_op jit(solution)/shard_map/ppermute | solution.py:250
  9.9 3.7 %collective-permute-start.1 = (bf16[176,512]{1,0:T(8,128)(2,1)S(1)}, bf16[176,512]{1,0:T(8,128)(2,1)S(1)}, u32[]{:S(2)}, u32[]{:S(2)}) collective-permute-start(bf16[176,512]{1,0:T(8,128)(2,1)S(1)} %get-tuple-element.48), channel_id=1, source_target_pairs={{0,1},{1,0},{2,3},{3,2},{4,5},{5,4},{6,7},{7,6},{8,9},{9,8},{10,11... | collective-permute-start | bytes 540680 | tf_op jit(solution)/shard_map/ppermute | solution.py:250
  10.4 3.2 %collective-permute-start.2 = (bf16[160,512]{1,0:T(8,128)(2,1)S(1)}, bf16[160,512]{1,0:T(8,128)(2,1)S(1)}, u32[]{:S(2)}, u32[]{:S(2)}) collective-permute-start(bf16[160,512]{1,0:T(8,128)(2,1)S(1)} %get-tuple-element.49), channel_id=1, source_target_pairs={{0,1},{1,0},{2,3},{3,2},{4,5},{5,4},{6,7},{7,6},{8,9},{9,8},{10,11... | collective-permute-start | bytes 491528 | tf_op jit(solution)/shard_map/ppermute | solution.py:250
  13.0 8.7 %collective-permute-start.3 = (bf16[256,512]{1,0:T(8,128)(2,1)S(1)}, bf16[256,512]{1,0:T(8,128)(2,1)S(1)}, u32[]{:S(2)}, u32[]{:S(2)}) collective-permute-start(bf16[256,512]{1,0:T(8,128)(2,1)S(1)} %get-tuple-element.53), channel_id=1, source_target_pairs={{1,2},{3,4},{5,6},{7,8},{9,10},{11,12},{13,14},{15,0},{2,1},{4,3},... | collective-permute-start | bytes 786440 | tf_op jit(solution)/shard_map/ppermute | solution.py:366
  13.7 1.4 %copy-start.1 = (f32[2048]{0:T(1024)S(1)}, f32[2048]{0:T(1024)}, u32[]{:S(2)}) copy-start(f32[2048]{0:T(1024)} %param.9) | copy-start | bytes 24580
  17.4 12.9 %collective-permute-start.5 = (bf16[256,512]{1,0:T(8,128)(2,1)S(1)}, bf16[256,512]{1,0:T(8,128)(2,1)S(1)}, u32[]{:S(2)}, u32[]{:S(2)}) collective-permute-start(bf16[256,512]{1,0:T(8,128)(2,1)S(1)} %get-tuple-element.57), channel_id=1, source_target_pairs={{1,2},{3,4},{5,6},{7,8},{9,10},{11,12},{13,14},{15,0},{2,1},{4,3},... | collective-permute-start | bytes 786440 | tf_op jit(solution)/shard_map/ppermute | solution.py:366
  22.8 9.6 %collective-permute-start.9 = (bf16[256,512]{1,0:T(8,128)(2,1)S(1)}, bf16[256,512]{1,0:T(8,128)(2,1)S(1)}, u32[]{:S(2)}, u32[]{:S(2)}) collective-permute-start(bf16[256,512]{1,0:T(8,128)(2,1)S(1)} %get-tuple-element.62), channel_id=1, source_target_pairs={{1,2},{3,4},{5,6},{7,8},{9,10},{11,12},{13,14},{15,0},{2,1},{4,3},... | collective-permute-start | bytes 786440 | tf_op jit(solution)/shard_map/ppermute | solution.py:366
  24.9 6.3 %collective-permute-start.6 = (bf16[176,512]{1,0:T(8,128)(2,1)S(1)}, bf16[176,512]{1,0:T(8,128)(2,1)S(1)}, u32[]{:S(2)}, u32[]{:S(2)}) collective-permute-start(bf16[176,512]{1,0:T(8,128)(2,1)S(1)} %get-tuple-element.58), channel_id=1, source_target_pairs={{0,1},{1,0},{2,3},{3,2},{4,5},{5,4},{6,7},{7,6},{8,9},{9,8},{10,11... | collective-permute-start | bytes 540680 | tf_op jit(solution)/shard_map/ppermute | solution.py:250
  28.8 2.5 %collective-permute-start.7 = (bf16[176,512]{1,0:T(8,128)(2,1)S(1)}, bf16[176,512]{1,0:T(8,128)(2,1)S(1)}, u32[]{:S(2)}, u32[]{:S(2)}) collective-permute-start(bf16[176,512]{1,0:T(8,128)(2,1)S(1)} %get-tuple-element.59), channel_id=1, source_target_pairs={{0,1},{1,0},{2,3},{3,2},{4,5},{5,4},{6,7},{7,6},{8,9},{9,8},{10,11... | collective-permute-start | bytes 540680 | tf_op jit(solution)/shard_map/ppermute | solution.py:250
  28.8 2.4 %collective-permute-start.8 = (bf16[160,512]{1,0:T(8,128)(2,1)S(1)}, bf16[160,512]{1,0:T(8,128)(2,1)S(1)}, u32[]{:S(2)}, u32[]{:S(2)}) collective-permute-start(bf16[160,512]{1,0:T(8,128)(2,1)S(1)} %get-tuple-element.60), channel_id=1, source_target_pairs={{0,1},{1,0},{2,3},{3,2},{4,5},{5,4},{6,7},{7,6},{8,9},{9,8},{10,11... | collective-permute-start | bytes 491528 | tf_op jit(solution)/shard_map/ppermute | solution.py:250
  33.5 3.0 %collective-permute-start.10 = (f32[128,768]{1,0:T(8,128)S(1)}, f32[128,768]{1,0:T(8,128)S(1)}, u32[]{:S(2)}, u32[]{:S(2)}) collective-permute-start(f32[128,768]{1,0:T(8,128)S(1)} %get-tuple-element.69), channel_id=1, source_target_pairs={{0,1},{1,0},{2,3},{3,2},{4,5},{5,4},{6,7},{7,6},{8,9},{9,8},{10,11... | collective-permute-start | bytes 1179656 | tf_op jit(solution)/shard_map/ppermute | solution.py:250
  36.5 4.2 %collective-permute-start.11 = (bf16[32,768]{1,0:T(8,128)(2,1)S(1)}, bf16[32,768]{1,0:T(8,128)(2,1)S(1)}, u32[]{:S(2)}, u32[]{:S(2)}) collective-permute-start(bf16[32,768]{1,0:T(8,128)(2,1)S(1)} %get-tuple-element.71), channel_id=1, source_target_pairs={{0,2},{1,3},{2,0},{3,1},{4,6},{5,7},{6,4},{7,5},{8,10},{9,11},{10,... | collective-permute-start | bytes 147464 | tf_op jit(solution)/shard_map/ppermute | solution.py:250
  36.7 4.1 %collective-permute-start.12 = (bf16[32,768]{1,0:T(8,128)(2,1)S(1)}, bf16[32,768]{1,0:T(8,128)(2,1)S(1)}, u32[]{:S(2)}, u32[]{:S(2)}) collective-permute-start(bf16[32,768]{1,0:T(8,128)(2,1)S(1)} %get-tuple-element.73), channel_id=1, source_target_pairs={{0,4},{1,5},{2,6},{3,7},{4,0},{5,1},{6,2},{7,3},{8,12},{9,13},{10,... | collective-permute-start | bytes 147464 | tf_op jit(solution)/shard_map/ppermute | solution.py:250
  40.8 5.4 %collective-permute-start.13 = (bf16[32,768]{1,0:T(8,128)(2,1)S(1)}, bf16[32,768]{1,0:T(8,128)(2,1)S(1)}, u32[]{:S(2)}, u32[]{:S(2)}) collective-permute-start(bf16[32,768]{1,0:T(8,128)(2,1)S(1)} %get-tuple-element.75.refs_0_), channel_id=1, source_target_pairs={{0,8},{1,9},{2,10},{3,11},{4,12},{5,13},{6,14},{7,15},{8,0},{9,1},... | collective-permute-start | bytes 147464 | tf_op jit(solution)/shard_map/ppermute | solution.py:250
  43.1 4.1 %collective-permute-start.14 = (bf16[32,768]{1,0:T(8,128)(2,1)S(1)}, bf16[32,768]{1,0:T(8,128)(2,1)S(1)}, u32[]{:S(2)}, u32[]{:S(2)}) collective-permute-start(bf16[32,768]{1,0:T(8,128)(2,1)S(1)} %get-tuple-element.76.refs_2_), channel_id=1, source_target_pairs={{0,2},{1,3},{2,0},{3,1},{4,6},{5,7},{6,4},{7,5},{8,10},{9,11},{10,... | collective-permute-start | bytes 147464 | tf_op jit(solution)/shard_map/ppermute | solution.py:250
  47.2 5.0 %collective-permute-start.15 = (bf16[32,768]{1,0:T(8,128)(2,1)S(1)}, bf16[32,768]{1,0:T(8,128)(2,1)S(1)}, u32[]{:S(2)}, u32[]{:S(2)}) collective-permute-start(bf16[32,768]{1,0:T(8,128)(2,1)S(1)} %get-tuple-element.78.refs_0_), channel_id=1, source_target_pairs={{0,4},{1,5},{2,6},{3,7},{4,0},{5,1},{6,2},{7,3},{8,12},{9,13},{10,... | collective-permute-start | bytes 147464 | tf_op jit(solution)/shard_map/ppermute | solution.py:250
  48.4 5.5 %collective-permute-start.16 = (bf16[32,768]{1,0:T(8,128)(2,1)S(1)}, bf16[32,768]{1,0:T(8,128)(2,1)S(1)}, u32[]{:S(2)}, u32[]{:S(2)}) collective-permute-start(bf16[32,768]{1,0:T(8,128)(2,1)S(1)} %get-tuple-element.79.refs_2_), channel_id=1, source_target_pairs={{0,8},{1,9},{2,10},{3,11},{4,12},{5,13},{6,14},{7,15},{8,0},{9,1},... | collective-permute-start | bytes 147464 | tf_op jit(solution)/shard_map/ppermute | solution.py:250
  54.0 4.2 %collective-permute-start.17 = (bf16[32,768]{1,0:T(8,128)(2,1)S(1)}, bf16[32,768]{1,0:T(8,128)(2,1)S(1)}, u32[]{:S(2)}, u32[]{:S(2)}) collective-permute-start(bf16[32,768]{1,0:T(8,128)(2,1)S(1)} %get-tuple-element.81.refs_0_), channel_id=1, source_target_pairs={{0,2},{1,3},{2,0},{3,1},{4,6},{5,7},{6,4},{7,5},{8,10},{9,11},{10,... | collective-permute-start | bytes 147464 | tf_op jit(solution)/shard_map/ppermute | solution.py:250
  54.0 4.2 %collective-permute-start.18 = (bf16[32,768]{1,0:T(8,128)(2,1)S(1)}, bf16[32,768]{1,0:T(8,128)(2,1)S(1)}, u32[]{:S(2)}, u32[]{:S(2)}) collective-permute-start(bf16[32,768]{1,0:T(8,128)(2,1)S(1)} %get-tuple-element.82.refs_2_), channel_id=1, source_target_pairs={{0,4},{1,5},{2,6},{3,7},{4,0},{5,1},{6,2},{7,3},{8,12},{9,13},{10,... | collective-permute-start | bytes 147464 | tf_op jit(solution)/shard_map/ppermute | solution.py:250
  58.2 1.5 %collective-permute-start.19 = (bf16[128,768]{1,0:T(8,128)(2,1)S(1)}, bf16[128,768]{1,0:T(8,128)(2,1)S(1)}, u32[]{:S(2)}, u32[]{:S(2)}) collective-permute-start(bf16[128,768]{1,0:T(8,128)(2,1)S(1)} %join.1.held), channel_id=1, source_target_pairs={{0,1},{1,0},{2,3},{3,2},{4,5},{5,4},{6,7},{7,6},{8,9},{9,8},{10,11... | collective-permute-start | bytes 589832 | tf_op jit(solution)/shard_map/ppermute | solution.py:250

commit v8 on v7

--- a/solution.py
+++ b/solution.py
@@ -209,15 +209,15 @@
     out, token, total, ready, sem = rest[-5:]
     block = signal.shape[2]
     token[...] = jnp.zeros_like(token)
-    total[...] = dot(signal[g], queries[...], TN)
+    total[...] = signal[g].astype(F32)
     named = named_by_partner(lists, blocks, ON) + named_by_partner(lists, blocks, OFF)
     for received, index in zip((on.at[0], on.at[1], off_a, off_b), named):
 
         @pl.when(index == g)
         def _():
-            total[...] += dot(received[...], queries[...], TN)
-
-    ready[...] = (total[...] * scale).astype(BF16)
+            total[...] += received[...].astype(F32)
+
+    ready[...] = (dot(total[...].astype(BF16), queries[...], TN) * scale).astype(BF16)
     copy = pltpu.make_async_copy(ready, out.at[pl.ds(g * block, block), :], sem)
     copy.start()
     copy.wait()
@@ -397,7 +397,6 @@
         [in_vmem(full, BF16), in_vmem(edge_tiles.shape, BF16)],
         scratch=[pltpu.SemaphoreType.DMA],
     )(positives.T, pltpu.with_memory_space_constraint(edge_tiles, pltpu.HBM))
-    off_b, hits = lax.optimization_barrier((off_b, hits))
     from_off_b = off_swap(off_b)
     base = call(
         base_kernel,
@@ -461,7 +460,7 @@
             [jax.ShapeDtypeStruct((labels_dev, width), BF16), in_vmem((8, 128), F32)],
             out_specs=[ANY, VMEM],
             scratch=[
-                pltpu.VMEM((block, width), F32),
+                pltpu.VMEM((rows, block), F32),
                 pltpu.VMEM((block, width), BF16),
                 pltpu.SemaphoreType.DMA,
             ],

time: 61 us -> 59.9 us (0.982)
  waiting for transfers between devices: 7.81 us -> 12.9 us
  starting transfers between devices: 24 us -> 19.7 us
  Pallas kernels: 27.7 us -> 26.1 us
    ppermute x16, starting transfers between devices: 13.3 us -> 8.84 us  [exchange(): return lax.ppermute(value, AXIS, [(i, i ^ mask) for i in range(count)])]
    ppermute x4, waiting for transfers between devices: 0.35 us -> 3.38 us  [off_swap(): return lax.ppermute(value, AXIS, off_route)]
    ppermute x16, waiting for transfers between devices: 7.46 us -> 9.55 us  [exchange(): return lax.ppermute(value, AXIS, [(i, i ^ mask) for i in range(count)])]
    pallas_call x4, Pallas kernels: 9.51 us -> 7.83 us  [embed(): call(functools.partial(embed_kernel, blocks=blocks, g=g, scale=1.0 / math...]
  transfers between devices with their start and end apart: 20 -> 20, of which waited for: 10 -> 10; matrix products, arithmetic and copies ran while one was open for 0% -> 0% of each run, Pallas kernels for 39% -> 37%
where the time goes in v8:
time: 59.9 us; the launch traced here: 59.6 us
  Pallas kernels  26.1 us (44%)
  starting transfers between devices  19.7 us (33%)
  waiting for transfers between devices  12.9 us (22%)
  between operations  0.93 us (2%)
    ppermute x4, starting transfers between devices, off_swap(): return lax.ppermute(value, AXIS, off_route)  10.8 us
    ppermute x16, waiting for transfers between devices, exchange(): return lax.ppermute(value, AXIS, [(i, i ^ mask) for i in range(count)])  9.55 us
    ppermute x16, starting transfers between devices, exchange(): return lax.ppermute(value, AXIS, [(i, i ^ mask) for i in range(count)])  8.84 us
    pallas_call x4, Pallas kernels, embed(): call(functools.partial(embed_kernel, blocks=blocks, g=g, scale=1.0 / math...  7.83 us
    pallas_call x2, Pallas kernels, signal_of(): call(functools.partial(signal_kernel, slot=slot), 'signal', [SMEM] + [VME...  3.53 us
    ppermute x4, waiting for transfers between devices, off_swap(): return lax.ppermute(value, AXIS, off_route)  3.38 us
    pallas_call x1, Pallas kernels, per_device(): call(hits_kernel, 'hits', [VMEM, HBM], [in_vmem(full, BF16), in_vmem(edge...  2.45 us
    pallas_call x1, Pallas kernels, per_device(): call(functools.partial(project_kernel, scale=scale), 'project', [HBM] * 3...  2.03 us
  transfers between devices with their start and end apart: 20, of which 10 were waited for; matrix products, arithmetic and copies ran while one was open for 0% of the time, Pallas kernels for 37%

profile of v8, /device:TPU:0, one launch (start us, length us, event | category | flops | bytes accessed | tf_op | source)
XLA Modules:
  0.0 59.6 jit_solution(16242141793563018074)
XLA Ops:
  0.7 2.0 %project.1 = (bf16[256,512]{1,0:T(8,128)(2,1)S(1)}, bf16[256,768]{1,0:T(8,128)(2,1)S(1)}, bf16[2048,768]{1,0:T(8,128)(2,1)S(1)}) custom-call(s32[2,64]{1,0:T(2,128)} %bitcast.3, bf16[256,768]{1,0:T(8,128)(2,1)} %queries.1, bf16[2048,768]{1,0:T(8,128)(2,1)} %embeddings.1), custom_call_target="tpu_custom_call" | custom-call | tf_op jit(solution)/shard_map/project/pallas_call | solution.py:378
  2.7 5.7 %collective-permute-start.4 = (bf16[256,512]{1,0:T(8,128)(2,1)S(1)}, bf16[256,512]{1,0:T(8,128)(2,1)S(1)}, u32[]{:S(2)}, u32[]{:S(2)}) collective-permute-start(bf16[256,512]{1,0:T(8,128)(2,1)S(1)} %get-tuple-element.50), channel_id=1, source_target_pairs={{1,2},{3,4},{5,6},{7,8},{9,10},{11,12},{13,14},{15,0},{2,1},{4,3},... | collective-permute-start | bytes 786440 | tf_op jit(solution)/shard_map/ppermute | solution.py:366
  8.4 1.6 %own.1 = (f32[4,256,512]{2,1,0:T(8,128)S(1)}, bf16[256,512]{1,0:T(8,128)(2,1)S(1)}, bf16[176,512]{1,0:T(8,128)(2,1)S(1)}, bf16[176,512]{1,0:T(8,128)(2,1)S(1)}, bf16[160,512]{1,0:T(8,128)(2,1)S(1)}) custom-call(s32[2,64]{1,0:T(2,128)S(1)} %bitcast.4, bf16[256,768]{1,0:T(8,128)(2,1)S(1)} %get-tuple-element.41.queries, ...), custom_call_target="tpu_custom_call" | custom-call | tf_op jit(solution)/shard_map/own/pallas_call | solution.py:386
  11.1 2.4 %hits.1 = (bf16[4,256,512]{2,1,0:T(8,128)(2,1)S(1)}, bf16[4,2,512,512]{3,2,1,0:T(8,128)(2,1)S(1)}) custom-call(s32[8,256]{1,0:T(8,128)S(1)} %bitcast.18, bf16[4,2,512,512]{3,2,1,0:T(8,128)(2,1)} %tiles.1), custom_call_target="tpu_custom_call" | custom-call | tf_op jit(solution)/shard_map/hits/pallas_call | solution.py:393
  13.6 1.4 %base.1 = f32[4,256,512]{2,1,0:T(8,128)S(1)} custom-call(s32[2,64]{1,0:T(2,128)S(1)} %bitcast.5, f32[4,256,512]{2,1,0:T(8,128)S(1)} %get-tuple-element.43.own, bf16[4,2,512,512]{3,2,1,0:T(8,128)(2,1)S(1)} %get-tuple-element.44.tiles, bf16[176,512]{1,0:T(8,128)(2,1)S(1)} %collective-permute-done.rest_0_, bf16[176,512]{1,0:T(8,128)(2,1)S(1)} %collective-permute-done.1.rest_1_, ...), custom_call_target="tpu_custom_call" | custom-call | tf_op jit(solution)/shard_map/base/pallas_call | solution.py:401
  15.0 1.2 %signal.2 = (bf16[4,256,512]{2,1,0:T(8,128)(2,1)S(1)}, bf16[256,512]{1,0:T(8,128)(2,1)S(1)}) custom-call(s32[2,64]{1,0:T(2,128)S(1)} %bitcast.6, f32[4,256,512]{2,1,0:T(8,128)S(1)} %base.1, bf16[4,256,512]{2,1,0:T(8,128)(2,1)S(1)} %get-tuple-element.48.hits, f32[1,2048]{1,0:T(1,128)S(1)} %bitcast.16, bf16[256,512]{1,0:T(8,128)(2,1)S(1)} %collective-permute-done.4.received, ...), custom_call_target="tpu_custom_call" | custom-call | flops 2000000000 | tf_op jit(solution)/shard_map/signal/pallas_call | solution.py:411
  16.2 4.6 %collective-permute-start.5 = (bf16[256,512]{1,0:T(8,128)(2,1)S(1)}, bf16[256,512]{1,0:T(8,128)(2,1)S(1)}, u32[]{:S(2)}, u32[]{:S(2)}) collective-permute-start(bf16[256,512]{1,0:T(8,128)(2,1)S(1)} %get-tuple-element.53), channel_id=1, source_target_pairs={{1,2},{3,4},{5,6},{7,8},{9,10},{11,12},{13,14},{15,0},{2,1},{4,3},... | collective-permute-start | bytes 786440 | tf_op jit(solution)/shard_map/ppermute | solution.py:366
  20.8 2.3 %signal.3 = (bf16[4,256,512]{2,1,0:T(8,128)(2,1)S(1)}, bf16[256,512]{1,0:T(8,128)(2,1)S(1)}) custom-call(s32[2,64]{1,0:T(2,128)S(1)} %bitcast.7, f32[4,256,512]{2,1,0:T(8,128)S(1)} %base.1, bf16[4,256,512]{2,1,0:T(8,128)(2,1)S(1)} %get-tuple-element.48.hits, f32[1,2048]{1,0:T(1,128)S(1)} %bitcast.17, ...), custom_call_target="tpu_custom_call", output_to_operand_aliasing={{0}: (6, {})} | custom-call | tf_op jit(solution)/shard_map/signal/pallas_call | solution.py:411
  23.3 1.4 %push.1 = (bf16[176,512]{1,0:T(8,128)(2,1)S(1)}, bf16[176,512]{1,0:T(8,128)(2,1)S(1)}, bf16[160,512]{1,0:T(8,128)(2,1)S(1)}) custom-call(s32[2,64]{1,0:T(2,128)S(1)} %bitcast.8, bf16[4,256,512]{2,1,0:T(8,128)(2,1)S(1)} %get-tuple-element.52.signal, bf16[4,2,512,512]{3,2,1,0:T(8,128)(2,1)S(1)} %get-tuple-element.44.tiles), custom_call_target="tpu_custom_call" | custom-call | tf_op jit(solution)/shard_map/push/pallas_call | solution.py:425
  25.3 1.0 %query.1.part = f32[256,768]{1,0:T(8,128)S(1)} custom-call(bf16[4,256,512]{2,1,0:T(8,128)(2,1)S(1)} %get-tuple-element.52.signal, bf16[2048,768]{1,0:T(8,128)(2,1)S(1)} %get-tuple-element.42.embeddings), custom_call_target="tpu_custom_call" | custom-call | tf_op jit(solution)/shard_map/query/pallas_call | solution.py:435
  26.3 0.9 %query_half.1.part = f32[256,768]{1,0:T(8,128)S(1)} custom-call(s32[2,64]{1,0:T(2,128)S(1)} %bitcast.9, f32[256,768]{1,0:T(8,128)S(1)} %query.1.part, bf16[256,512]{1,0:T(8,128)(2,1)S(1)} %collective-permute-done.5.received.off_a, bf16[2048,768]{1,0:T(8,128)(2,1)S(1)} %get-tuple-element.42.embeddings), custom_call_target="tpu_custom_call" | custom-call | flops 1000000000 | tf_op jit(solution)/shard_map/query_half/pallas_call | solution.py:436
  27.3 1.2 %query_on.1 = (f32[256,768]{1,0:T(8,128)S(1)}, bf16[2,256,512]{2,1,0:T(8,128)(2,1)S(1)}) custom-call(s32[2,64]{1,0:T(2,128)S(1)} %bitcast.10, f32[256,768]{1,0:T(8,128)S(1)} %query_half.1.part, bf16[2048,768]{1,0:T(8,128)(2,1)S(1)} %get-tuple-element.42.embeddings, bf16[176,512]{1,0:T(8,128)(2,1)S(1)} %collective-permute-done.6.rest_0_, ...), custom_call_target="tpu_custom_call" | custom-call | tf_op jit(solution)/shard_map/query_on/pallas_call | solution.py:443
  28.5 3.4 %collective-permute-done.9.off_b.received = bf16[256,512]{1,0:T(8,128)(2,1)S(1)} collective-permute-done((bf16[256,512]{1,0:T(8,128)(2,1)S(1)}, bf16[256,512]{1,0:T(8,128)(2,1)S(1)}, u32[]{:S(2)}, u32[]{:S(2)}) %collective-permute-start.9) | collective-permute-done | bytes 262176 | tf_op jit(solution)/shard_map/ppermute | solution.py:366
  31.9 1.0 %query_end.1 = (f32[128,768]{1,0:T(8,128)S(1)}, f32[128,768]{1,0:T(8,128)S(1)}) custom-call(s32[2,64]{1,0:T(2,128)S(1)} %bitcast.11, f32[256,768]{1,0:T(8,128)S(1)} %get-tuple-element.63.part, bf16[256,512]{1,0:T(8,128)(2,1)S(1)} %collective-permute-done.9.off_b.received, bf16[2048,768]{1,0:T(8,128)(2,1)S(1)} %get-tuple-element.42.embeddings), custom_call_target="tpu_custom_call" | custom-call | tf_op jit(solution)/shard_map/query_end/pallas_call | solution.py:447
  33.2 1.4 %collective-permute-done.10.got = f32[128,768]{1,0:T(8,128)S(1)} collective-permute-done((f32[128,768]{1,0:T(8,128)S(1)}, f32[128,768]{1,0:T(8,128)S(1)}, u32[]{:S(2)}, u32[]{:S(2)}) %collective-permute-start.10) | collective-permute-done | bytes 393248 | tf_op jit(solution)/shard_map/ppermute | solution.py:250
  34.7 1.0 %collective-permute-start.11 = (bf16[32,768]{1,0:T(8,128)(2,1)S(1)}, bf16[32,768]{1,0:T(8,128)(2,1)S(1)}, u32[]{:S(2)}, u32[]{:S(2)}) collective-permute-start(bf16[32,768]{1,0:T(8,128)(2,1)S(1)} %get-tuple-element.67), channel_id=1, source_target_pairs={{0,2},{1,3},{2,0},{3,1},{4,6},{5,7},{6,4},{7,5},{8,10},{9,11},{10,... | collective-permute-start | bytes 147464 | tf_op jit(solution)/shard_map/ppermute | solution.py:250
  35.8 1.0 %collective-permute-start.12 = (bf16[32,768]{1,0:T(8,128)(2,1)S(1)}, bf16[32,768]{1,0:T(8,128)(2,1)S(1)}, u32[]{:S(2)}, u32[]{:S(2)}) collective-permute-start(bf16[32,768]{1,0:T(8,128)(2,1)S(1)} %get-tuple-element.69), channel_id=1, source_target_pairs={{0,4},{1,5},{2,6},{3,7},{4,0},{5,1},{6,2},{7,3},{8,12},{9,13},{10,... | collective-permute-start | bytes 147464 | tf_op jit(solution)/shard_map/ppermute | solution.py:250
  36.7 2.0 %embed.4 = (bf16[2048,768]{1,0:T(8,128)(2,1)}, f32[8,128]{1,0:T(8,128)S(1)}) custom-call(s32[2,64]{1,0:T(2,128)S(1)} %bitcast.12, bf16[4,256,512]{2,1,0:T(8,128)(2,1)S(1)} %get-tuple-element.52.signal, bf16[2,256,512]{2,1,0:T(8,128)(2,1)S(1)} %get-tuple-element.57.on, bf16[256,512]{1,0:T(8,128)(2,1)S(1)} %collective-permute-done.5.received.off_a, ...), custom_call_target="tpu_custom_call" | custom-call | tf_op jit(solution)/shard_map/embed/pallas_call | solution.py:456
  38.9 1.0 %collective-permute-done.12.refs_3_ = bf16[32,768]{1,0:T(8,128)(2,1)S(1)} collective-permute-done((bf16[32,768]{1,0:T(8,128)(2,1)S(1)}, bf16[32,768]{1,0:T(8,128)(2,1)S(1)}, u32[]{:S(2)}, u32[]{:S(2)}) %collective-permute-start.12) | collective-permute-done | bytes 49184 | tf_op jit(solution)/shard_map/ppermute | solution.py:250
  39.9 1.9 %collective-permute-start.13 = (bf16[32,768]{1,0:T(8,128)(2,1)S(1)}, bf16[32,768]{1,0:T(8,128)(2,1)S(1)}, u32[]{:S(2)}, u32[]{:S(2)}) collective-permute-start(bf16[32,768]{1,0:T(8,128)(2,1)S(1)} %get-tuple-element.71.refs_0_), channel_id=1, source_target_pairs={{0,8},{1,9},{2,10},{3,11},{4,12},{5,13},{6,14},{7,15},{8,0},{9,1},... | collective-permute-start | bytes 147464 | tf_op jit(solution)/shard_map/ppermute | solution.py:250
  41.8 2.0 %embed.5 = (bf16[2048,768]{1,0:T(8,128)(2,1)}, f32[8,128]{1,0:T(8,128)S(1)}) custom-call(s32[2,64]{1,0:T(2,128)S(1)} %bitcast.13, bf16[4,256,512]{2,1,0:T(8,128)(2,1)S(1)} %get-tuple-element.52.signal, bf16[2,256,512]{2,1,0:T(8,128)(2,1)S(1)} %get-tuple-element.57.on, ...), custom_call_target="tpu_custom_call", output_to_operand_aliasing={{0}: (6, {})} | custom-call | tf_op jit(solution)/shard_map/embed/pallas_call | solution.py:456
  43.8 1.1 %collective-permute-done.13.refs_1_ = bf16[32,768]{1,0:T(8,128)(2,1)S(1)} collective-permute-done((bf16[32,768]{1,0:T(8,128)(2,1)S(1)}, bf16[32,768]{1,0:T(8,128)(2,1)S(1)}, u32[]{:S(2)}, u32[]{:S(2)}) %collective-permute-start.13) | collective-permute-done | bytes 49184 | tf_op jit(solution)/shard_map/ppermute | solution.py:250
  44.9 0.9 %collective-permute-done.14.refs_3_ = bf16[32,768]{1,0:T(8,128)(2,1)S(1)} collective-permute-done((bf16[32,768]{1,0:T(8,128)(2,1)S(1)}, bf16[32,768]{1,0:T(8,128)(2,1)S(1)}, u32[]{:S(2)}, u32[]{:S(2)}) %collective-permute-start.14) | collective-permute-done | bytes 49184 | tf_op jit(solution)/shard_map/ppermute | solution.py:250
  45.9 2.1 %collective-permute-start.15 = (bf16[32,768]{1,0:T(8,128)(2,1)S(1)}, bf16[32,768]{1,0:T(8,128)(2,1)S(1)}, u32[]{:S(2)}, u32[]{:S(2)}) collective-permute-start(bf16[32,768]{1,0:T(8,128)(2,1)S(1)} %get-tuple-element.74.refs_0_), channel_id=1, source_target_pairs={{0,4},{1,5},{2,6},{3,7},{4,0},{5,1},{6,2},{7,3},{8,12},{9,13},{10,... | collective-permute-start | bytes 147464 | tf_op jit(solution)/shard_map/ppermute | solution.py:250
  48.0 0.9 %collective-permute-start.16 = (bf16[32,768]{1,0:T(8,128)(2,1)S(1)}, bf16[32,768]{1,0:T(8,128)(2,1)S(1)}, u32[]{:S(2)}, u32[]{:S(2)}) collective-permute-start(bf16[32,768]{1,0:T(8,128)(2,1)S(1)} %get-tuple-element.75.refs_2_), channel_id=1, source_target_pairs={{0,8},{1,9},{2,10},{3,11},{4,12},{5,13},{6,14},{7,15},{8,0},{9,1},... | collective-permute-start | bytes 147464 | tf_op jit(solution)/shard_map/ppermute | solution.py:250
  48.9 1.9 %embed.6 = (bf16[2048,768]{1,0:T(8,128)(2,1)}, f32[8,128]{1,0:T(8,128)S(1)}) custom-call(s32[2,64]{1,0:T(2,128)S(1)} %bitcast.14, bf16[4,256,512]{2,1,0:T(8,128)(2,1)S(1)} %get-tuple-element.52.signal, bf16[2,256,512]{2,1,0:T(8,128)(2,1)S(1)} %get-tuple-element.57.on, ...), custom_call_target="tpu_custom_call", output_to_operand_aliasing={{0}: (6, {})} | custom-call | tf_op jit(solution)/shard_map/embed/pallas_call | solution.py:456
  50.8 2.2 %collective-permute-done.16.refs_3_ = bf16[32,768]{1,0:T(8,128)(2,1)S(1)} collective-permute-done((bf16[32,768]{1,0:T(8,128)(2,1)S(1)}, bf16[32,768]{1,0:T(8,128)(2,1)S(1)}, u32[]{:S(2)}, u32[]{:S(2)}) %collective-permute-start.16) | collective-permute-done | bytes 49184 | tf_op jit(solution)/shard_map/ppermute | solution.py:250
  53.2 2.0 %embed.7 = (bf16[2048,768]{1,0:T(8,128)(2,1)}, f32[8,128]{1,0:T(8,128)S(1)}) custom-call(s32[2,64]{1,0:T(2,128)S(1)} %bitcast.15, bf16[4,256,512]{2,1,0:T(8,128)(2,1)S(1)} %get-tuple-element.52.signal, bf16[2,256,512]{2,1,0:T(8,128)(2,1)S(1)} %get-tuple-element.57.on, ...), custom_call_target="tpu_custom_call", output_to_operand_aliasing={{0}: (6, {})} | custom-call | tf_op jit(solution)/shard_map/embed/pallas_call | solution.py:456
  55.2 2.0 %collective-permute-done.17.refs_1_ = bf16[32,768]{1,0:T(8,128)(2,1)S(1)} collective-permute-done((bf16[32,768]{1,0:T(8,128)(2,1)S(1)}, bf16[32,768]{1,0:T(8,128)(2,1)S(1)}, u32[]{:S(2)}, u32[]{:S(2)}) %collective-permute-start.17) | collective-permute-done | bytes 49184 | tf_op jit(solution)/shard_map/ppermute | solution.py:250
  57.4 0.8 %place.2.rest_0_ = f32[256,768]{1,0:T(8,128)} custom-call(bf16[128,768]{1,0:T(8,128)(2,1)S(1)} %join.1.held), custom_call_target="tpu_custom_call" | custom-call | tf_op jit(solution)/shard_map/place/pallas_call | solution.py:343
  58.2 0.6 %collective-permute-done.19.held = bf16[128,768]{1,0:T(8,128)(2,1)S(1)} collective-permute-done((bf16[128,768]{1,0:T(8,128)(2,1)S(1)}, bf16[128,768]{1,0:T(8,128)(2,1)S(1)}, u32[]{:S(2)}, u32[]{:S(2)}) %collective-permute-start.19) | collective-permute-done | bytes 196640 | tf_op jit(solution)/shard_map/ppermute | solution.py:250
  58.8 0.8 %place.3 = f32[256,768]{1,0:T(8,128)} custom-call(bf16[128,768]{1,0:T(8,128)(2,1)S(1)} %collective-permute-done.19.held, f32[256,768]{1,0:T(8,128)} %place.2.rest_0_), custom_call_target="tpu_custom_call", output_to_operand_aliasing={{}: (1, {})} | custom-call | tf_op jit(solution)/shard_map/place/pallas_call | solution.py:343
  (36 shorter events, 2.9 us)
Async XLA Ops:
  0.6 7.7 %copy-start = (s32[64,2]{0,1:T(2,128)S(1)}, s32[64,2]{0,1:T(2,128)}, u32[]{:S(2)}) copy-start(s32[64,2]{0,1:T(2,128)} %param.8) | copy-start | bytes 1540
  0.6 10.5 %copy-start.2 = (s32[256,8]{0,1:T(8,128)S(1)}, s32[256,8]{0,1:T(8,128)}, u32[]{:S(2)}) copy-start(s32[256,8]{0,1:T(8,128)} %param.11) | copy-start | bytes 24580
  2.7 12.3 %collective-permute-start.4 = (bf16[256,512]{1,0:T(8,128)(2,1)S(1)}, bf16[256,512]{1,0:T(8,128)(2,1)S(1)}, u32[]{:S(2)}, u32[]{:S(2)}) collective-permute-start(bf16[256,512]{1,0:T(8,128)(2,1)S(1)} %get-tuple-element.50), channel_id=1, source_target_pairs={{1,2},{3,4},{5,6},{7,8},{9,10},{11,12},{13,14},{15,0},{2,1},{4,3},... | collective-permute-start | bytes 786440 | tf_op jit(solution)/shard_map/ppermute | solution.py:366
  10.0 3.6 %collective-permute-start = (bf16[176,512]{1,0:T(8,128)(2,1)S(1)}, bf16[176,512]{1,0:T(8,128)(2,1)S(1)}, u32[]{:S(2)}, u32[]{:S(2)}) collective-permute-start(bf16[176,512]{1,0:T(8,128)(2,1)S(1)} %get-tuple-element.45), channel_id=1, source_target_pairs={{0,1},{1,0},{2,3},{3,2},{4,5},{5,4},{6,7},{7,6},{8,9},{9,8},{10,11... | collective-permute-start | bytes 540680 | tf_op jit(solution)/shard_map/ppermute | solution.py:250
  10.1 3.5 %collective-permute-start.1 = (bf16[176,512]{1,0:T(8,128)(2,1)S(1)}, bf16[176,512]{1,0:T(8,128)(2,1)S(1)}, u32[]{:S(2)}, u32[]{:S(2)}) collective-permute-start(bf16[176,512]{1,0:T(8,128)(2,1)S(1)} %get-tuple-element.46), channel_id=1, source_target_pairs={{0,1},{1,0},{2,3},{3,2},{4,5},{5,4},{6,7},{7,6},{8,9},{9,8},{10,11... | collective-permute-start | bytes 540680 | tf_op jit(solution)/shard_map/ppermute | solution.py:250
  10.6 3.0 %collective-permute-start.2 = (bf16[160,512]{1,0:T(8,128)(2,1)S(1)}, bf16[160,512]{1,0:T(8,128)(2,1)S(1)}, u32[]{:S(2)}, u32[]{:S(2)}) collective-permute-start(bf16[160,512]{1,0:T(8,128)(2,1)S(1)} %get-tuple-element.47), channel_id=1, source_target_pairs={{0,1},{1,0},{2,3},{3,2},{4,5},{5,4},{6,7},{7,6},{8,9},{9,8},{10,11... | collective-permute-start | bytes 491528 | tf_op jit(solution)/shard_map/ppermute | solution.py:250
  10.7 10.2 %collective-permute-start.3 = (bf16[256,512]{1,0:T(8,128)(2,1)S(1)}, bf16[256,512]{1,0:T(8,128)(2,1)S(1)}, u32[]{:S(2)}, u32[]{:S(2)}) collective-permute-start(bf16[256,512]{1,0:T(8,128)(2,1)S(1)} %get-tuple-element.49), channel_id=1, source_target_pairs={{1,2},{3,4},{5,6},{7,8},{9,10},{11,12},{13,14},{15,0},{2,1},{4,3},... | collective-permute-start | bytes 786440 | tf_op jit(solution)/shard_map/ppermute | solution.py:366
  13.6 1.4 %copy-start.1 = (f32[2048]{0:T(1024)S(1)}, f32[2048]{0:T(1024)}, u32[]{:S(2)}) copy-start(f32[2048]{0:T(1024)} %param.9) | copy-start | bytes 24580
  16.2 10.1 %collective-permute-start.5 = (bf16[256,512]{1,0:T(8,128)(2,1)S(1)}, bf16[256,512]{1,0:T(8,128)(2,1)S(1)}, u32[]{:S(2)}, u32[]{:S(2)}) collective-permute-start(bf16[256,512]{1,0:T(8,128)(2,1)S(1)} %get-tuple-element.53), channel_id=1, source_target_pairs={{1,2},{3,4},{5,6},{7,8},{9,10},{11,12},{13,14},{15,0},{2,1},{4,3},... | collective-permute-start | bytes 786440 | tf_op jit(solution)/shard_map/ppermute | solution.py:366
  23.2 8.7 %collective-permute-start.9 = (bf16[256,512]{1,0:T(8,128)(2,1)S(1)}, bf16[256,512]{1,0:T(8,128)(2,1)S(1)}, u32[]{:S(2)}, u32[]{:S(2)}) collective-permute-start(bf16[256,512]{1,0:T(8,128)(2,1)S(1)} %get-tuple-element.58), channel_id=1, source_target_pairs={{1,2},{3,4},{5,6},{7,8},{9,10},{11,12},{13,14},{15,0},{2,1},{4,3},... | collective-permute-start | bytes 786440 | tf_op jit(solution)/shard_map/ppermute | solution.py:366
  24.7 2.6 %collective-permute-start.6 = (bf16[176,512]{1,0:T(8,128)(2,1)S(1)}, bf16[176,512]{1,0:T(8,128)(2,1)S(1)}, u32[]{:S(2)}, u32[]{:S(2)}) collective-permute-start(bf16[176,512]{1,0:T(8,128)(2,1)S(1)} %get-tuple-element.54), channel_id=1, source_target_pairs={{0,1},{1,0},{2,3},{3,2},{4,5},{5,4},{6,7},{7,6},{8,9},{9,8},{10,11... | collective-permute-start | bytes 540680 | tf_op jit(solution)/shard_map/ppermute | solution.py:250
  24.8 2.6 %collective-permute-start.7 = (bf16[176,512]{1,0:T(8,128)(2,1)S(1)}, bf16[176,512]{1,0:T(8,128)(2,1)S(1)}, u32[]{:S(2)}, u32[]{:S(2)}) collective-permute-start(bf16[176,512]{1,0:T(8,128)(2,1)S(1)} %get-tuple-element.55), channel_id=1, source_target_pairs={{0,1},{1,0},{2,3},{3,2},{4,5},{5,4},{6,7},{7,6},{8,9},{9,8},{10,11... | collective-permute-start | bytes 540680 | tf_op jit(solution)/shard_map/ppermute | solution.py:250
  25.3 2.0 %collective-permute-start.8 = (bf16[160,512]{1,0:T(8,128)(2,1)S(1)}, bf16[160,512]{1,0:T(8,128)(2,1)S(1)}, u32[]{:S(2)}, u32[]{:S(2)}) collective-permute-start(bf16[160,512]{1,0:T(8,128)(2,1)S(1)} %get-tuple-element.56), channel_id=1, source_target_pairs={{0,1},{1,0},{2,3},{3,2},{4,5},{5,4},{6,7},{7,6},{8,9},{9,8},{10,11... | collective-permute-start | bytes 491528 | tf_op jit(solution)/shard_map/ppermute | solution.py:250
  32.9 1.8 %collective-permute-start.10 = (f32[128,768]{1,0:T(8,128)S(1)}, f32[128,768]{1,0:T(8,128)S(1)}, u32[]{:S(2)}, u32[]{:S(2)}) collective-permute-start(f32[128,768]{1,0:T(8,128)S(1)} %get-tuple-element.65), channel_id=1, source_target_pairs={{0,1},{1,0},{2,3},{3,2},{4,5},{5,4},{6,7},{7,6},{8,9},{9,8},{10,11... | collective-permute-start | bytes 1179656 | tf_op jit(solution)/shard_map/ppermute | solution.py:250
  34.7 4.2 %collective-permute-start.11 = (bf16[32,768]{1,0:T(8,128)(2,1)S(1)}, bf16[32,768]{1,0:T(8,128)(2,1)S(1)}, u32[]{:S(2)}, u32[]{:S(2)}) collective-permute-start(bf16[32,768]{1,0:T(8,128)(2,1)S(1)} %get-tuple-element.67), channel_id=1, source_target_pairs={{0,2},{1,3},{2,0},{3,1},{4,6},{5,7},{6,4},{7,5},{8,10},{9,11},{10,... | collective-permute-start | bytes 147464 | tf_op jit(solution)/shard_map/ppermute | solution.py:250
  35.8 4.1 %collective-permute-start.12 = (bf16[32,768]{1,0:T(8,128)(2,1)S(1)}, bf16[32,768]{1,0:T(8,128)(2,1)S(1)}, u32[]{:S(2)}, u32[]{:S(2)}) collective-permute-start(bf16[32,768]{1,0:T(8,128)(2,1)S(1)} %get-tuple-element.69), channel_id=1, source_target_pairs={{0,4},{1,5},{2,6},{3,7},{4,0},{5,1},{6,2},{7,3},{8,12},{9,13},{10,... | collective-permute-start | bytes 147464 | tf_op jit(solution)/shard_map/ppermute | solution.py:250
  39.9 5.1 %collective-permute-start.13 = (bf16[32,768]{1,0:T(8,128)(2,1)S(1)}, bf16[32,768]{1,0:T(8,128)(2,1)S(1)}, u32[]{:S(2)}, u32[]{:S(2)}) collective-permute-start(bf16[32,768]{1,0:T(8,128)(2,1)S(1)} %get-tuple-element.71.refs_0_), channel_id=1, source_target_pairs={{0,8},{1,9},{2,10},{3,11},{4,12},{5,13},{6,14},{7,15},{8,0},{9,1},... | collective-permute-start | bytes 147464 | tf_op jit(solution)/shard_map/ppermute | solution.py:250
  41.7 4.1 %collective-permute-start.14 = (bf16[32,768]{1,0:T(8,128)(2,1)S(1)}, bf16[32,768]{1,0:T(8,128)(2,1)S(1)}, u32[]{:S(2)}, u32[]{:S(2)}) collective-permute-start(bf16[32,768]{1,0:T(8,128)(2,1)S(1)} %get-tuple-element.72.refs_2_), channel_id=1, source_target_pairs={{0,2},{1,3},{2,0},{3,1},{4,6},{5,7},{6,4},{7,5},{8,10},{9,11},{10,... | collective-permute-start | bytes 147464 | tf_op jit(solution)/shard_map/ppermute | solution.py:250
  45.9 4.9 %collective-permute-start.15 = (bf16[32,768]{1,0:T(8,128)(2,1)S(1)}, bf16[32,768]{1,0:T(8,128)(2,1)S(1)}, u32[]{:S(2)}, u32[]{:S(2)}) collective-permute-start(bf16[32,768]{1,0:T(8,128)(2,1)S(1)} %get-tuple-element.74.refs_0_), channel_id=1, source_target_pairs={{0,4},{1,5},{2,6},{3,7},{4,0},{5,1},{6,2},{7,3},{8,12},{9,13},{10,... | collective-permute-start | bytes 147464 | tf_op jit(solution)/shard_map/ppermute | solution.py:250
  48.0 5.1 %collective-permute-start.16 = (bf16[32,768]{1,0:T(8,128)(2,1)S(1)}, bf16[32,768]{1,0:T(8,128)(2,1)S(1)}, u32[]{:S(2)}, u32[]{:S(2)}) collective-permute-start(bf16[32,768]{1,0:T(8,128)(2,1)S(1)} %get-tuple-element.75.refs_2_), channel_id=1, source_target_pairs={{0,8},{1,9},{2,10},{3,11},{4,12},{5,13},{6,14},{7,15},{8,0},{9,1},... | collective-permute-start | bytes 147464 | tf_op jit(solution)/shard_map/ppermute | solution.py:250
  53.1 4.2 %collective-permute-start.17 = (bf16[32,768]{1,0:T(8,128)(2,1)S(1)}, bf16[32,768]{1,0:T(8,128)(2,1)S(1)}, u32[]{:S(2)}, u32[]{:S(2)}) collective-permute-start(bf16[32,768]{1,0:T(8,128)(2,1)S(1)} %get-tuple-element.77.refs_0_), channel_id=1, source_target_pairs={{0,2},{1,3},{2,0},{3,1},{4,6},{5,7},{6,4},{7,5},{8,10},{9,11},{10,... | collective-permute-start | bytes 147464 | tf_op jit(solution)/shard_map/ppermute | solution.py:250
  53.2 4.1 %collective-permute-start.18 = (bf16[32,768]{1,0:T(8,128)(2,1)S(1)}, bf16[32,768]{1,0:T(8,128)(2,1)S(1)}, u32[]{:S(2)}, u32[]{:S(2)}) collective-permute-start(bf16[32,768]{1,0:T(8,128)(2,1)S(1)} %get-tuple-element.78.refs_2_), channel_id=1, source_target_pairs={{0,4},{1,5},{2,6},{3,7},{4,0},{5,1},{6,2},{7,3},{8,12},{9,13},{10,... | collective-permute-start | bytes 147464 | tf_op jit(solution)/shard_map/ppermute | solution.py:250
  57.3 1.5 %collective-permute-start.19 = (bf16[128,768]{1,0:T(8,128)(2,1)S(1)}, bf16[128,768]{1,0:T(8,128)(2,1)S(1)}, u32[]{:S(2)}, u32[]{:S(2)}) collective-permute-start(bf16[128,768]{1,0:T(8,128)(2,1)S(1)} %join.1.held), channel_id=1, source_target_pairs={{0,1},{1,0},{2,3},{3,2},{4,5},{5,4},{6,7},{7,6},{8,9},{9,8},{10,11... | collective-permute-start | bytes 589832 | tf_op jit(solution)/shard_map/ppermute | solution.py:250

commit v9 on v8

--- a/solution.py
+++ b/solution.py
@@ -202,7 +202,7 @@
     rows = kept.shape[0]
     core = lax.axis_index(AXIS) % 2
     kept[...] = total[pl.ds(pl.multiple_of(core * rows, rows), rows), :]
-    sent[...] = total[pl.ds(pl.multiple_of((1 - core) * rows, rows), rows), :]
+    sent[...] = total[pl.ds(pl.multiple_of((1 - core) * rows, rows), rows), :].astype(BF16)
 
 
 def embed_kernel(lists, signal, on, off_a, off_b, queries, *rest, blocks, g, scale):
@@ -258,33 +258,24 @@
     return (lax.axis_index(AXIS) // bit) % 2
 
 
-def halve_kernel(held, got, *outs, bits):
-    total = outs[-1]
-    total[...] = held[...] + got[...]
-    rows = outs[0].shape[0]
-    for chain, bit in enumerate(bits):
-        kept, sent = outs[2 * chain], outs[2 * chain + 1]
-        begin = 2 * chain * rows
-        digit = digit_of(bit)
-        kept[...] = total[pl.ds(pl.multiple_of(begin + digit * rows, rows), rows), :]
-        sent[...] = total[pl.ds(pl.multiple_of(begin + (1 - digit) * rows, rows), rows), :].astype(BF16)
-
-
-def add_kernel(*refs, scale):
-    *ins, out_a, out_b = refs
-    for held, got, out in ((ins[0], ins[1], out_a), (ins[2], ins[3], out_b)):
-        out[...] = ((held[...].astype(F32) + got[...].astype(F32)) * scale).astype(BF16)
-
-
-def join_kernel(*refs, bits):
-    *ins, out = refs
-    rows = ins[0].shape[0]
-    for chain, bit in enumerate(bits):
-        held, got = ins[2 * chain], ins[2 * chain + 1]
-        begin = 2 * chain * rows
-        digit = digit_of(bit)
-        out[pl.ds(pl.multiple_of(begin + digit * rows, rows), rows), :] = held[...]
-        out[pl.ds(pl.multiple_of(begin + (1 - digit) * rows, rows), rows), :] = got[...]
+def halve_kernel(held, got, kept, sent, total, *, bit):
+    total[...] = held[...] + got[...].astype(F32)
+    rows = kept.shape[0]
+    digit = digit_of(bit)
+    kept[...] = total[pl.ds(pl.multiple_of(digit * rows, rows), rows), :]
+    sent[...] = total[pl.ds(pl.multiple_of((1 - digit) * rows, rows), rows), :].astype(BF16)
+
+
+def add_kernel(held, got, *rest, scale):
+    rest[-1][...] = ((held[...].astype(F32) + got[...].astype(F32)) * scale).astype(BF16)
+
+
+def join_kernel(held, got, *rest, bit):
+    out = rest[-1]
+    rows = held.shape[0]
+    digit = digit_of(bit)
+    out[pl.ds(pl.multiple_of(digit * rows, rows), rows), :] = held[...]
+    out[pl.ds(pl.multiple_of((1 - digit) * rows, rows), rows), :] = got[...]
 
 
 def place_kernel(held, *rest, own):
@@ -302,41 +293,36 @@
     count = lax.axis_size(AXIS)
     rows, width = kept.shape
     got = exchange(sent, 1)
-    if count & (count - 1) or count < 8:
-        half = lax.psum(kept + got, AXIS, axis_index_groups=[list(range(c, count, 2)) for c in range(2)])
+    if count & (count - 1) or count < 4:
+        half = kept + got.astype(F32)
+        half = lax.psum(half, AXIS, axis_index_groups=[list(range(c, count, 2)) for c in range(2)])
         both = jnp.stack([half, exchange(half, 1)])
         both = jnp.where(lax.axis_index(AXIS) % 2 == 0, both, both[::-1])
         return both.reshape(2 * rows, width) * scale
-    piece = jax.ShapeDtypeStruct((rows // 2, width), BF16)
     bits = [1 << k for k in range(1, count.bit_length() - 1)]
-    orders = [[bits[0], *bits[2:], bits[1]], [bits[1], bits[0], *bits[2:]]]
-    ends = [order[0] for order in orders]
-    wide, narrow = in_vmem((rows // 4, width), F32), in_vmem((rows // 4, width), BF16)
-    kept_a, sent_a, kept_b, sent_b = call(
-        functools.partial(halve_kernel, bits=ends),
+    narrow = in_vmem((rows // 2, width), BF16)
+    held, sent = call(
+        functools.partial(halve_kernel, bit=bits[0]),
         "halve",
         [VMEM] * 2,
-        [wide, narrow, wide, narrow],
+        [in_vmem(narrow.shape, F32), narrow],
         scratch=[pltpu.VMEM((rows, width), F32)],
     )(kept, got)
-    held, sent = [kept_a, kept_b], [sent_a, sent_b]
-    for k in range(len(bits)):
-        got = [exchange(piece, order[k]) for piece, order in zip(sent, orders)]
+    for k, bit in enumerate(bits):
         after = beside[k : k + 1]
         held = sent = call(
             functools.partial(add_kernel, scale=scale if k == len(bits) - 1 else 1.0),
             "add",
-            [VMEM] * 4 + [ANY] * len(after),
-            [narrow, narrow],
-        )(held[0], got[0], held[1], got[1], *after)
-    got = [exchange(piece, bit) for piece, bit in zip(held, ends)]
+            [VMEM] * 2 + [ANY] * len(after),
+            narrow,
+        )(held, exchange(sent, bit), *after)
     after = beside[len(bits) :]
     held = call(
-        functools.partial(join_kernel, bits=ends),
+        functools.partial(join_kernel, bit=bits[0]),
         "join",
-        [VMEM] * 4 + [ANY] * len(after),
+        [VMEM] * 2 + [ANY] * len(after),
         in_vmem((rows, width), BF16),
-    )(held[0], got[0], held[1], got[1], *after)
+    )(held, exchange(held, bits[0]), *after)
     got = exchange(held, 1)
 
     def place(half, own, *begun):
@@ -443,12 +429,12 @@
     part, on = call(
         functools.partial(query_on_kernel, blocks=blocks), "query_on", [SMEM] + [VMEM] * 5, [whole, pair]
     )(lists, part, embeddings, *back_on)
-    piece = in_vmem((rows // 2, width), F32)
+    kept, sent = (in_vmem((rows // 2, width), kind) for kind in (F32, BF16))
     kept, sent = call(
         functools.partial(query_end_kernel, blocks=blocks),
         "query_end",
         [SMEM] + [VMEM] * 3,
-        [piece, piece],
+        [kept, sent],
         scratch=[pltpu.VMEM((rows, width), F32)],
     )(lists, part, back_b, embeddings)
 

time: 59.9 us -> 57.3 us (0.957)
  waiting for transfers between devices: 12.9 us -> 11 us
    ppermute x4, waiting for transfers between devices: 3.38 us -> 1.63 us  [off_swap(): return lax.ppermute(value, AXIS, off_route)]
    ppermute x16 -> x12, starting transfers between devices: 8.84 us -> 8.11 us  [exchange(): return lax.ppermute(value, AXIS, [(i, i ^ mask) for i in range(count)])]
    ppermute x16 -> x12, waiting for transfers between devices: 9.55 us -> 9.39 us  [exchange(): return lax.ppermute(value, AXIS, [(i, i ^ mask) for i in range(count)])]
  transfers between devices with their start and end apart: 20 -> 16, of which waited for: 10 -> 7; matrix products, arithmetic and copies ran while one was open for 0% -> 0% of each run, Pallas kernels for 37% -> 38%
where the time goes in v9:
time: 57.3 us; the launch traced here: 57.4 us
  Pallas kernels  26 us (45%)
  starting transfers between devices  19.4 us (34%)
  waiting for transfers between devices  11 us (19%)
  between operations  0.9 us (2%)
    ppermute x4, starting transfers between devices, off_swap(): return lax.ppermute(value, AXIS, off_route)  11.3 us
    ppermute x12, waiting for transfers between devices, exchange(): return lax.ppermute(value, AXIS, [(i, i ^ mask) for i in range(count)])  9.39 us
    ppermute x12, starting transfers between devices, exchange(): return lax.ppermute(value, AXIS, [(i, i ^ mask) for i in range(count)])  8.11 us
    pallas_call x4, Pallas kernels, embed(): call(functools.partial(embed_kernel, blocks=blocks, g=g, scale=1.0 / math...  7.8 us
    pallas_call x2, Pallas kernels, signal_of(): call(functools.partial(signal_kernel, slot=slot), 'signal', [SMEM] + [VME...  3.53 us
    pallas_call x1, Pallas kernels, per_device(): call(hits_kernel, 'hits', [VMEM, HBM], [in_vmem(full, BF16), in_vmem(edge...  2.45 us
    pallas_call x1, Pallas kernels, per_device(): call(functools.partial(project_kernel, scale=scale), 'project', [HBM] * 3...  2.03 us
    pallas_call x1, Pallas kernels, per_device(): call(functools.partial(own_kernel, scale=scale), 'own', [SMEM, VMEM, VMEM...  1.65 us
  transfers between devices with their start and end apart: 16, of which 7 were waited for; matrix products, arithmetic and copies ran while one was open for 0% of the time, Pallas kernels for 38%

profile of v9, /device:TPU:0, one launch (start us, length us, event | category | flops | bytes accessed | tf_op | source)
XLA Modules:
  0.0 57.4 jit_solution(15530729040364122839)
XLA Ops:
  0.7 2.0 %project.1 = (bf16[256,512]{1,0:T(8,128)(2,1)S(1)}, bf16[256,768]{1,0:T(8,128)(2,1)S(1)}, bf16[2048,768]{1,0:T(8,128)(2,1)S(1)}) custom-call(s32[2,64]{1,0:T(2,128)} %bitcast.3, bf16[256,768]{1,0:T(8,128)(2,1)} %queries.1, bf16[2048,768]{1,0:T(8,128)(2,1)} %embeddings.1), custom_call_target="tpu_custom_call" | custom-call | tf_op jit(solution)/shard_map/project/pallas_call | solution.py:364
  2.7 5.5 %collective-permute-start.4 = (bf16[256,512]{1,0:T(8,128)(2,1)S(1)}, bf16[256,512]{1,0:T(8,128)(2,1)S(1)}, u32[]{:S(2)}, u32[]{:S(2)}) collective-permute-start(bf16[256,512]{1,0:T(8,128)(2,1)S(1)} %get-tuple-element.42), channel_id=1, source_target_pairs={{1,2},{3,4},{5,6},{7,8},{9,10},{11,12},{13,14},{15,0},{2,1},{4,3},... | collective-permute-start | bytes 786440 | tf_op jit(solution)/shard_map/ppermute | solution.py:352
  8.2 1.6 %own.1 = (f32[4,256,512]{2,1,0:T(8,128)S(1)}, bf16[256,512]{1,0:T(8,128)(2,1)S(1)}, bf16[176,512]{1,0:T(8,128)(2,1)S(1)}, bf16[176,512]{1,0:T(8,128)(2,1)S(1)}, bf16[160,512]{1,0:T(8,128)(2,1)S(1)}) custom-call(s32[2,64]{1,0:T(2,128)S(1)} %bitcast.4, bf16[256,768]{1,0:T(8,128)(2,1)S(1)} %get-tuple-element.33.queries, ...), custom_call_target="tpu_custom_call" | custom-call | tf_op jit(solution)/shard_map/own/pallas_call | solution.py:372
  10.5 0.6 %collective-permute-start.3 = (bf16[256,512]{1,0:T(8,128)(2,1)S(1)}, bf16[256,512]{1,0:T(8,128)(2,1)S(1)}, u32[]{:S(2)}, u32[]{:S(2)}) collective-permute-start(bf16[256,512]{1,0:T(8,128)(2,1)S(1)} %get-tuple-element.41), channel_id=1, source_target_pairs={{1,2},{3,4},{5,6},{7,8},{9,10},{11,12},{13,14},{15,0},{2,1},{4,3},... | collective-permute-start | bytes 786440 | tf_op jit(solution)/shard_map/ppermute | solution.py:352
  11.1 2.4 %hits.1 = (bf16[4,256,512]{2,1,0:T(8,128)(2,1)S(1)}, bf16[4,2,512,512]{3,2,1,0:T(8,128)(2,1)S(1)}) custom-call(s32[8,256]{1,0:T(8,128)S(1)} %bitcast.18, bf16[4,2,512,512]{3,2,1,0:T(8,128)(2,1)} %tiles.1), custom_call_target="tpu_custom_call" | custom-call | tf_op jit(solution)/shard_map/hits/pallas_call | solution.py:379
  13.6 1.3 %base.1 = f32[4,256,512]{2,1,0:T(8,128)S(1)} custom-call(s32[2,64]{1,0:T(2,128)S(1)} %bitcast.5, f32[4,256,512]{2,1,0:T(8,128)S(1)} %get-tuple-element.35.own, bf16[4,2,512,512]{3,2,1,0:T(8,128)(2,1)S(1)} %get-tuple-element.36.tiles, bf16[176,512]{1,0:T(8,128)(2,1)S(1)} %collective-permute-done.rest_0_, bf16[176,512]{1,0:T(8,128)(2,1)S(1)} %collective-permute-done.1.rest_1_, ...), custom_call_target="tpu_custom_call" | custom-call | tf_op jit(solution)/shard_map/base/pallas_call | solution.py:387
  15.0 1.8 %signal.2 = (bf16[4,256,512]{2,1,0:T(8,128)(2,1)S(1)}, bf16[256,512]{1,0:T(8,128)(2,1)S(1)}) custom-call(s32[2,64]{1,0:T(2,128)S(1)} %bitcast.6, f32[4,256,512]{2,1,0:T(8,128)S(1)} %base.1, bf16[4,256,512]{2,1,0:T(8,128)(2,1)S(1)} %get-tuple-element.40.hits, f32[1,2048]{1,0:T(1,128)S(1)} %bitcast.16, bf16[256,512]{1,0:T(8,128)(2,1)S(1)} %collective-permute-done.4.received, ...), custom_call_target="tpu_custom_call" | custom-call | flops 2000000000 | tf_op jit(solution)/shard_map/signal/pallas_call | solution.py:397
  16.8 3.3 %collective-permute-start.5 = (bf16[256,512]{1,0:T(8,128)(2,1)S(1)}, bf16[256,512]{1,0:T(8,128)(2,1)S(1)}, u32[]{:S(2)}, u32[]{:S(2)}) collective-permute-start(bf16[256,512]{1,0:T(8,128)(2,1)S(1)} %get-tuple-element.45), channel_id=1, source_target_pairs={{1,2},{3,4},{5,6},{7,8},{9,10},{11,12},{13,14},{15,0},{2,1},{4,3},... | collective-permute-start | bytes 786440 | tf_op jit(solution)/shard_map/ppermute | solution.py:352
  20.1 1.8 %signal.3 = (bf16[4,256,512]{2,1,0:T(8,128)(2,1)S(1)}, bf16[256,512]{1,0:T(8,128)(2,1)S(1)}) custom-call(s32[2,64]{1,0:T(2,128)S(1)} %bitcast.7, f32[4,256,512]{2,1,0:T(8,128)S(1)} %base.1, bf16[4,256,512]{2,1,0:T(8,128)(2,1)S(1)} %get-tuple-element.40.hits, f32[1,2048]{1,0:T(1,128)S(1)} %bitcast.17, ...), custom_call_target="tpu_custom_call", output_to_operand_aliasing={{0}: (6, {})} | custom-call | tf_op jit(solution)/shard_map/signal/pallas_call | solution.py:397
  21.9 1.8 %collective-permute-start.9 = (bf16[256,512]{1,0:T(8,128)(2,1)S(1)}, bf16[256,512]{1,0:T(8,128)(2,1)S(1)}, u32[]{:S(2)}, u32[]{:S(2)}) collective-permute-start(bf16[256,512]{1,0:T(8,128)(2,1)S(1)} %get-tuple-element.50), channel_id=1, source_target_pairs={{1,2},{3,4},{5,6},{7,8},{9,10},{11,12},{13,14},{15,0},{2,1},{4,3},... | collective-permute-start | bytes 786440 | tf_op jit(solution)/shard_map/ppermute | solution.py:352
  23.7 1.4 %push.1 = (bf16[176,512]{1,0:T(8,128)(2,1)S(1)}, bf16[176,512]{1,0:T(8,128)(2,1)S(1)}, bf16[160,512]{1,0:T(8,128)(2,1)S(1)}) custom-call(s32[2,64]{1,0:T(2,128)S(1)} %bitcast.8, bf16[4,256,512]{2,1,0:T(8,128)(2,1)S(1)} %get-tuple-element.44.signal, bf16[4,2,512,512]{3,2,1,0:T(8,128)(2,1)S(1)} %get-tuple-element.36.tiles), custom_call_target="tpu_custom_call" | custom-call | tf_op jit(solution)/shard_map/push/pallas_call | solution.py:411
  25.8 1.0 %query.1.part = f32[256,768]{1,0:T(8,128)S(1)} custom-call(bf16[4,256,512]{2,1,0:T(8,128)(2,1)S(1)} %get-tuple-element.44.signal, bf16[2048,768]{1,0:T(8,128)(2,1)S(1)} %get-tuple-element.34.embeddings), custom_call_target="tpu_custom_call" | custom-call | tf_op jit(solution)/shard_map/query/pallas_call | solution.py:421
  26.8 0.9 %query_half.1.part = f32[256,768]{1,0:T(8,128)S(1)} custom-call(s32[2,64]{1,0:T(2,128)S(1)} %bitcast.9, f32[256,768]{1,0:T(8,128)S(1)} %query.1.part, bf16[256,512]{1,0:T(8,128)(2,1)S(1)} %collective-permute-done.5.received.off_a, bf16[2048,768]{1,0:T(8,128)(2,1)S(1)} %get-tuple-element.34.embeddings), custom_call_target="tpu_custom_call" | custom-call | flops 1000000000 | tf_op jit(solution)/shard_map/query_half/pallas_call | solution.py:422
  27.7 1.2 %query_on.1 = (f32[256,768]{1,0:T(8,128)S(1)}, bf16[2,256,512]{2,1,0:T(8,128)(2,1)S(1)}) custom-call(s32[2,64]{1,0:T(2,128)S(1)} %bitcast.10, f32[256,768]{1,0:T(8,128)S(1)} %query_half.1.part, bf16[2048,768]{1,0:T(8,128)(2,1)S(1)} %get-tuple-element.34.embeddings, bf16[176,512]{1,0:T(8,128)(2,1)S(1)} %collective-permute-done.6.rest_0_, ...), custom_call_target="tpu_custom_call" | custom-call | tf_op jit(solution)/shard_map/query_on/pallas_call | solution.py:429
  28.9 1.6 %collective-permute-done.9.off_b.received = bf16[256,512]{1,0:T(8,128)(2,1)S(1)} collective-permute-done((bf16[256,512]{1,0:T(8,128)(2,1)S(1)}, bf16[256,512]{1,0:T(8,128)(2,1)S(1)}, u32[]{:S(2)}, u32[]{:S(2)}) %collective-permute-start.9) | collective-permute-done | bytes 262176 | tf_op jit(solution)/shard_map/ppermute | solution.py:352
  30.5 1.0 %query_end.1 = (f32[128,768]{1,0:T(8,128)S(1)}, bf16[128,768]{1,0:T(8,128)(2,1)S(1)}) custom-call(s32[2,64]{1,0:T(2,128)S(1)} %bitcast.11, f32[256,768]{1,0:T(8,128)S(1)} %get-tuple-element.55.part, bf16[256,512]{1,0:T(8,128)(2,1)S(1)} %collective-permute-done.9.off_b.received, bf16[2048,768]{1,0:T(8,128)(2,1)S(1)} %get-tuple-element.34.embeddings), custom_call_target="tpu_custom_call" | custom-call | tf_op jit(solution)/shard_map/query_end/pallas_call | solution.py:433
  31.6 1.1 %collective-permute-start.10 = (bf16[128,768]{1,0:T(8,128)(2,1)S(1)}, bf16[128,768]{1,0:T(8,128)(2,1)S(1)}, u32[]{:S(2)}, u32[]{:S(2)}) collective-permute-start(bf16[128,768]{1,0:T(8,128)(2,1)S(1)} %get-tuple-element.57), channel_id=1, source_target_pairs={{0,1},{1,0},{2,3},{3,2},{4,5},{5,4},{6,7},{7,6},{8,9},{9,8},{10,11... | collective-permute-start | bytes 589832 | tf_op jit(solution)/shard_map/ppermute | solution.py:250
  32.7 1.1 %collective-permute-done.10.got = bf16[128,768]{1,0:T(8,128)(2,1)S(1)} collective-permute-done((bf16[128,768]{1,0:T(8,128)(2,1)S(1)}, bf16[128,768]{1,0:T(8,128)(2,1)S(1)}, u32[]{:S(2)}, u32[]{:S(2)}) %collective-permute-start.10) | collective-permute-done | bytes 196640 | tf_op jit(solution)/shard_map/ppermute | solution.py:250
  33.8 1.7 %collective-permute-start.11 = (bf16[64,768]{1,0:T(8,128)(2,1)S(1)}, bf16[64,768]{1,0:T(8,128)(2,1)S(1)}, u32[]{:S(2)}, u32[]{:S(2)}) collective-permute-start(bf16[64,768]{1,0:T(8,128)(2,1)S(1)} %get-tuple-element.59), channel_id=1, source_target_pairs={{0,2},{1,3},{2,0},{3,1},{4,6},{5,7},{6,4},{7,5},{8,10},{9,11},{10,... | collective-permute-start | bytes 294920 | tf_op jit(solution)/shard_map/ppermute | solution.py:250
  35.5 1.9 %embed.4 = (bf16[2048,768]{1,0:T(8,128)(2,1)}, f32[8,128]{1,0:T(8,128)S(1)}) custom-call(s32[2,64]{1,0:T(2,128)S(1)} %bitcast.12, bf16[4,256,512]{2,1,0:T(8,128)(2,1)S(1)} %get-tuple-element.44.signal, bf16[2,256,512]{2,1,0:T(8,128)(2,1)S(1)} %get-tuple-element.49.on, bf16[256,512]{1,0:T(8,128)(2,1)S(1)} %collective-permute-done.5.received.off_a, ...), custom_call_target="tpu_custom_call" | custom-call | tf_op jit(solution)/shard_map/embed/pallas_call | solution.py:442
  37.4 1.5 %collective-permute-done.11.got = bf16[64,768]{1,0:T(8,128)(2,1)S(1)} collective-permute-done((bf16[64,768]{1,0:T(8,128)(2,1)S(1)}, bf16[64,768]{1,0:T(8,128)(2,1)S(1)}, u32[]{:S(2)}, u32[]{:S(2)}) %collective-permute-start.11) | collective-permute-done | bytes 98336 | tf_op jit(solution)/shard_map/ppermute | solution.py:250
  39.0 1.3 %collective-permute-start.12 = (bf16[64,768]{1,0:T(8,128)(2,1)S(1)}, bf16[64,768]{1,0:T(8,128)(2,1)S(1)}, u32[]{:S(2)}, u32[]{:S(2)}) collective-permute-start(bf16[64,768]{1,0:T(8,128)(2,1)S(1)} %add.3.held), channel_id=1, source_target_pairs={{0,4},{1,5},{2,6},{3,7},{4,0},{5,1},{6,2},{7,3},{8,12},{9,13},{10,... | collective-permute-start | bytes 294920 | tf_op jit(solution)/shard_map/ppermute | solution.py:250
  40.3 1.9 %embed.5 = (bf16[2048,768]{1,0:T(8,128)(2,1)}, f32[8,128]{1,0:T(8,128)S(1)}) custom-call(s32[2,64]{1,0:T(2,128)S(1)} %bitcast.13, bf16[4,256,512]{2,1,0:T(8,128)(2,1)S(1)} %get-tuple-element.44.signal, bf16[2,256,512]{2,1,0:T(8,128)(2,1)S(1)} %get-tuple-element.49.on, ...), custom_call_target="tpu_custom_call", output_to_operand_aliasing={{0}: (6, {})} | custom-call | tf_op jit(solution)/shard_map/embed/pallas_call | solution.py:442
  42.2 1.4 %collective-permute-done.12.got = bf16[64,768]{1,0:T(8,128)(2,1)S(1)} collective-permute-done((bf16[64,768]{1,0:T(8,128)(2,1)S(1)}, bf16[64,768]{1,0:T(8,128)(2,1)S(1)}, u32[]{:S(2)}, u32[]{:S(2)}) %collective-permute-start.12) | collective-permute-done | bytes 98336 | tf_op jit(solution)/shard_map/ppermute | solution.py:250
  43.7 2.3 %collective-permute-start.13 = (bf16[64,768]{1,0:T(8,128)(2,1)S(1)}, bf16[64,768]{1,0:T(8,128)(2,1)S(1)}, u32[]{:S(2)}, u32[]{:S(2)}) collective-permute-start(bf16[64,768]{1,0:T(8,128)(2,1)S(1)} %add.4.held), channel_id=1, source_target_pairs={{0,8},{1,9},{2,10},{3,11},{4,12},{5,13},{6,14},{7,15},{8,0},{9,1},... | collective-permute-start | bytes 294920 | tf_op jit(solution)/shard_map/ppermute | solution.py:250
  46.0 2.0 %embed.6 = (bf16[2048,768]{1,0:T(8,128)(2,1)}, f32[8,128]{1,0:T(8,128)S(1)}) custom-call(s32[2,64]{1,0:T(2,128)S(1)} %bitcast.14, bf16[4,256,512]{2,1,0:T(8,128)(2,1)S(1)} %get-tuple-element.44.signal, bf16[2,256,512]{2,1,0:T(8,128)(2,1)S(1)} %get-tuple-element.49.on, ...), custom_call_target="tpu_custom_call", output_to_operand_aliasing={{0}: (6, {})} | custom-call | tf_op jit(solution)/shard_map/embed/pallas_call | solution.py:442
  47.9 2.4 %collective-permute-done.13.got = bf16[64,768]{1,0:T(8,128)(2,1)S(1)} collective-permute-done((bf16[64,768]{1,0:T(8,128)(2,1)S(1)}, bf16[64,768]{1,0:T(8,128)(2,1)S(1)}, u32[]{:S(2)}, u32[]{:S(2)}) %collective-permute-start.13) | collective-permute-done | bytes 98336 | tf_op jit(solution)/shard_map/ppermute | solution.py:250
  50.8 1.9 %embed.7 = (bf16[2048,768]{1,0:T(8,128)(2,1)}, f32[8,128]{1,0:T(8,128)S(1)}) custom-call(s32[2,64]{1,0:T(2,128)S(1)} %bitcast.15, bf16[4,256,512]{2,1,0:T(8,128)(2,1)S(1)} %get-tuple-element.44.signal, bf16[2,256,512]{2,1,0:T(8,128)(2,1)S(1)} %get-tuple-element.49.on, ...), custom_call_target="tpu_custom_call", output_to_operand_aliasing={{0}: (6, {})} | custom-call | tf_op jit(solution)/shard_map/embed/pallas_call | solution.py:442
  52.7 2.3 %collective-permute-done.14.got = bf16[64,768]{1,0:T(8,128)(2,1)S(1)} collective-permute-done((bf16[64,768]{1,0:T(8,128)(2,1)S(1)}, bf16[64,768]{1,0:T(8,128)(2,1)S(1)}, u32[]{:S(2)}, u32[]{:S(2)}) %collective-permute-start.14) | collective-permute-done | bytes 98336 | tf_op jit(solution)/shard_map/ppermute | solution.py:250
  55.2 0.8 %place.2.rest_0_ = f32[256,768]{1,0:T(8,128)} custom-call(bf16[128,768]{1,0:T(8,128)(2,1)S(1)} %join.1.held), custom_call_target="tpu_custom_call" | custom-call | tf_op jit(solution)/shard_map/place/pallas_call | solution.py:329
  55.9 0.6 %collective-permute-done.15.held = bf16[128,768]{1,0:T(8,128)(2,1)S(1)} collective-permute-done((bf16[128,768]{1,0:T(8,128)(2,1)S(1)}, bf16[128,768]{1,0:T(8,128)(2,1)S(1)}, u32[]{:S(2)}, u32[]{:S(2)}) %collective-permute-start.15) | collective-permute-done | bytes 196640 | tf_op jit(solution)/shard_map/ppermute | solution.py:250
  56.6 0.8 %place.3 = f32[256,768]{1,0:T(8,128)} custom-call(bf16[128,768]{1,0:T(8,128)(2,1)S(1)} %collective-permute-done.15.held, f32[256,768]{1,0:T(8,128)} %place.2.rest_0_), custom_call_target="tpu_custom_call", output_to_operand_aliasing={{}: (1, {})} | custom-call | tf_op jit(solution)/shard_map/place/pallas_call | solution.py:329
  (28 shorter events, 2.0 us)
Async XLA Ops:
  0.6 7.6 %copy-start = (s32[64,2]{0,1:T(2,128)S(1)}, s32[64,2]{0,1:T(2,128)}, u32[]{:S(2)}) copy-start(s32[64,2]{0,1:T(2,128)} %param.8) | copy-start | bytes 1540
  0.6 10.5 %copy-start.2 = (s32[256,8]{0,1:T(8,128)S(1)}, s32[256,8]{0,1:T(8,128)}, u32[]{:S(2)}) copy-start(s32[256,8]{0,1:T(8,128)} %param.11) | copy-start | bytes 24580
  2.7 12.3 %collective-permute-start.4 = (bf16[256,512]{1,0:T(8,128)(2,1)S(1)}, bf16[256,512]{1,0:T(8,128)(2,1)S(1)}, u32[]{:S(2)}, u32[]{:S(2)}) collective-permute-start(bf16[256,512]{1,0:T(8,128)(2,1)S(1)} %get-tuple-element.42), channel_id=1, source_target_pairs={{1,2},{3,4},{5,6},{7,8},{9,10},{11,12},{13,14},{15,0},{2,1},{4,3},... | collective-permute-start | bytes 786440 | tf_op jit(solution)/shard_map/ppermute | solution.py:352
  9.9 3.7 %collective-permute-start = (bf16[176,512]{1,0:T(8,128)(2,1)S(1)}, bf16[176,512]{1,0:T(8,128)(2,1)S(1)}, u32[]{:S(2)}, u32[]{:S(2)}) collective-permute-start(bf16[176,512]{1,0:T(8,128)(2,1)S(1)} %get-tuple-element.37), channel_id=1, source_target_pairs={{0,1},{1,0},{2,3},{3,2},{4,5},{5,4},{6,7},{7,6},{8,9},{9,8},{10,11... | collective-permute-start | bytes 540680 | tf_op jit(solution)/shard_map/ppermute | solution.py:250
  9.9 3.7 %collective-permute-start.1 = (bf16[176,512]{1,0:T(8,128)(2,1)S(1)}, bf16[176,512]{1,0:T(8,128)(2,1)S(1)}, u32[]{:S(2)}, u32[]{:S(2)}) collective-permute-start(bf16[176,512]{1,0:T(8,128)(2,1)S(1)} %get-tuple-element.38), channel_id=1, source_target_pairs={{0,1},{1,0},{2,3},{3,2},{4,5},{5,4},{6,7},{7,6},{8,9},{9,8},{10,11... | collective-permute-start | bytes 540680 | tf_op jit(solution)/shard_map/ppermute | solution.py:250
  10.4 3.2 %collective-permute-start.2 = (bf16[160,512]{1,0:T(8,128)(2,1)S(1)}, bf16[160,512]{1,0:T(8,128)(2,1)S(1)}, u32[]{:S(2)}, u32[]{:S(2)}) collective-permute-start(bf16[160,512]{1,0:T(8,128)(2,1)S(1)} %get-tuple-element.39), channel_id=1, source_target_pairs={{0,1},{1,0},{2,3},{3,2},{4,5},{5,4},{6,7},{7,6},{8,9},{9,8},{10,11... | collective-permute-start | bytes 491528 | tf_op jit(solution)/shard_map/ppermute | solution.py:250
  10.5 9.6 %collective-permute-start.3 = (bf16[256,512]{1,0:T(8,128)(2,1)S(1)}, bf16[256,512]{1,0:T(8,128)(2,1)S(1)}, u32[]{:S(2)}, u32[]{:S(2)}) collective-permute-start(bf16[256,512]{1,0:T(8,128)(2,1)S(1)} %get-tuple-element.41), channel_id=1, source_target_pairs={{1,2},{3,4},{5,6},{7,8},{9,10},{11,12},{13,14},{15,0},{2,1},{4,3},... | collective-permute-start | bytes 786440 | tf_op jit(solution)/shard_map/ppermute | solution.py:352
  13.6 1.4 %copy-start.1 = (f32[2048]{0:T(1024)S(1)}, f32[2048]{0:T(1024)}, u32[]{:S(2)}) copy-start(f32[2048]{0:T(1024)} %param.9) | copy-start | bytes 24580
  16.8 10.0 %collective-permute-start.5 = (bf16[256,512]{1,0:T(8,128)(2,1)S(1)}, bf16[256,512]{1,0:T(8,128)(2,1)S(1)}, u32[]{:S(2)}, u32[]{:S(2)}) collective-permute-start(bf16[256,512]{1,0:T(8,128)(2,1)S(1)} %get-tuple-element.45), channel_id=1, source_target_pairs={{1,2},{3,4},{5,6},{7,8},{9,10},{11,12},{13,14},{15,0},{2,1},{4,3},... | collective-permute-start | bytes 786440 | tf_op jit(solution)/shard_map/ppermute | solution.py:352
  21.9 8.7 %collective-permute-start.9 = (bf16[256,512]{1,0:T(8,128)(2,1)S(1)}, bf16[256,512]{1,0:T(8,128)(2,1)S(1)}, u32[]{:S(2)}, u32[]{:S(2)}) collective-permute-start(bf16[256,512]{1,0:T(8,128)(2,1)S(1)} %get-tuple-element.50), channel_id=1, source_target_pairs={{1,2},{3,4},{5,6},{7,8},{9,10},{11,12},{13,14},{15,0},{2,1},{4,3},... | collective-permute-start | bytes 786440 | tf_op jit(solution)/shard_map/ppermute | solution.py:352
  25.1 2.6 %collective-permute-start.6 = (bf16[176,512]{1,0:T(8,128)(2,1)S(1)}, bf16[176,512]{1,0:T(8,128)(2,1)S(1)}, u32[]{:S(2)}, u32[]{:S(2)}) collective-permute-start(bf16[176,512]{1,0:T(8,128)(2,1)S(1)} %get-tuple-element.46), channel_id=1, source_target_pairs={{0,1},{1,0},{2,3},{3,2},{4,5},{5,4},{6,7},{7,6},{8,9},{9,8},{10,11... | collective-permute-start | bytes 540680 | tf_op jit(solution)/shard_map/ppermute | solution.py:250
  25.2 2.6 %collective-permute-start.7 = (bf16[176,512]{1,0:T(8,128)(2,1)S(1)}, bf16[176,512]{1,0:T(8,128)(2,1)S(1)}, u32[]{:S(2)}, u32[]{:S(2)}) collective-permute-start(bf16[176,512]{1,0:T(8,128)(2,1)S(1)} %get-tuple-element.47), channel_id=1, source_target_pairs={{0,1},{1,0},{2,3},{3,2},{4,5},{5,4},{6,7},{7,6},{8,9},{9,8},{10,11... | collective-permute-start | bytes 540680 | tf_op jit(solution)/shard_map/ppermute | solution.py:250
  25.7 2.0 %collective-permute-start.8 = (bf16[160,512]{1,0:T(8,128)(2,1)S(1)}, bf16[160,512]{1,0:T(8,128)(2,1)S(1)}, u32[]{:S(2)}, u32[]{:S(2)}) collective-permute-start(bf16[160,512]{1,0:T(8,128)(2,1)S(1)} %get-tuple-element.48), channel_id=1, source_target_pairs={{0,1},{1,0},{2,3},{3,2},{4,5},{5,4},{6,7},{7,6},{8,9},{9,8},{10,11... | collective-permute-start | bytes 491528 | tf_op jit(solution)/shard_map/ppermute | solution.py:250
  31.6 2.2 %collective-permute-start.10 = (bf16[128,768]{1,0:T(8,128)(2,1)S(1)}, bf16[128,768]{1,0:T(8,128)(2,1)S(1)}, u32[]{:S(2)}, u32[]{:S(2)}) collective-permute-start(bf16[128,768]{1,0:T(8,128)(2,1)S(1)} %get-tuple-element.57), channel_id=1, source_target_pairs={{0,1},{1,0},{2,3},{3,2},{4,5},{5,4},{6,7},{7,6},{8,9},{9,8},{10,11... | collective-permute-start | bytes 589832 | tf_op jit(solution)/shard_map/ppermute | solution.py:250
  33.8 5.1 %collective-permute-start.11 = (bf16[64,768]{1,0:T(8,128)(2,1)S(1)}, bf16[64,768]{1,0:T(8,128)(2,1)S(1)}, u32[]{:S(2)}, u32[]{:S(2)}) collective-permute-start(bf16[64,768]{1,0:T(8,128)(2,1)S(1)} %get-tuple-element.59), channel_id=1, source_target_pairs={{0,2},{1,3},{2,0},{3,1},{4,6},{5,7},{6,4},{7,5},{8,10},{9,11},{10,... | collective-permute-start | bytes 294920 | tf_op jit(solution)/shard_map/ppermute | solution.py:250
  39.0 4.7 %collective-permute-start.12 = (bf16[64,768]{1,0:T(8,128)(2,1)S(1)}, bf16[64,768]{1,0:T(8,128)(2,1)S(1)}, u32[]{:S(2)}, u32[]{:S(2)}) collective-permute-start(bf16[64,768]{1,0:T(8,128)(2,1)S(1)} %add.3.held), channel_id=1, source_target_pairs={{0,4},{1,5},{2,6},{3,7},{4,0},{5,1},{6,2},{7,3},{8,12},{9,13},{10,... | collective-permute-start | bytes 294920 | tf_op jit(solution)/shard_map/ppermute | solution.py:250
  43.7 6.6 %collective-permute-start.13 = (bf16[64,768]{1,0:T(8,128)(2,1)S(1)}, bf16[64,768]{1,0:T(8,128)(2,1)S(1)}, u32[]{:S(2)}, u32[]{:S(2)}) collective-permute-start(bf16[64,768]{1,0:T(8,128)(2,1)S(1)} %add.4.held), channel_id=1, source_target_pairs={{0,8},{1,9},{2,10},{3,11},{4,12},{5,13},{6,14},{7,15},{8,0},{9,1},... | collective-permute-start | bytes 294920 | tf_op jit(solution)/shard_map/ppermute | solution.py:250
  50.4 4.7 %collective-permute-start.14 = (bf16[64,768]{1,0:T(8,128)(2,1)S(1)}, bf16[64,768]{1,0:T(8,128)(2,1)S(1)}, u32[]{:S(2)}, u32[]{:S(2)}) collective-permute-start(bf16[64,768]{1,0:T(8,128)(2,1)S(1)} %add.5.held), channel_id=1, source_target_pairs={{0,2},{1,3},{2,0},{3,1},{4,6},{5,7},{6,4},{7,5},{8,10},{9,11},{10,... | collective-permute-start | bytes 294920 | tf_op jit(solution)/shard_map/ppermute | solution.py:250
  55.1 1.5 %collective-permute-start.15 = (bf16[128,768]{1,0:T(8,128)(2,1)S(1)}, bf16[128,768]{1,0:T(8,128)(2,1)S(1)}, u32[]{:S(2)}, u32[]{:S(2)}) collective-permute-start(bf16[128,768]{1,0:T(8,128)(2,1)S(1)} %join.1.held), channel_id=1, source_target_pairs={{0,1},{1,0},{2,3},{3,2},{4,5},{5,4},{6,7},{7,6},{8,9},{9,8},{10,11... | collective-permute-start | bytes 589832 | tf_op jit(solution)/shard_map/ppermute | solution.py:250

commit v10 on v9

--- a/solution.py
+++ b/solution.py
@@ -258,24 +258,24 @@
     return (lax.axis_index(AXIS) // bit) % 2
 
 
-def halve_kernel(held, got, kept, sent, total, *, bit):
-    total[...] = held[...] + got[...].astype(F32)
-    rows = kept.shape[0]
-    digit = digit_of(bit)
-    kept[...] = total[pl.ds(pl.multiple_of(digit * rows, rows), rows), :]
-    sent[...] = total[pl.ds(pl.multiple_of((1 - digit) * rows, rows), rows), :].astype(BF16)
-
-
-def add_kernel(held, got, *rest, scale):
-    rest[-1][...] = ((held[...].astype(F32) + got[...].astype(F32)) * scale).astype(BF16)
-
-
-def join_kernel(held, got, *rest, bit):
+def cores_kernel(held, got, out):
+    out[...] = (held[...] + got[...].astype(F32)).astype(BF16)
+
+
+def pieces_kernel(pieces, *rest, scale):
+    rows = pieces.shape[0] // 4
+    value = pieces[:rows, :].astype(F32)
+    for k in range(1, 4):
+        value = value + pieces[k * rows : (k + 1) * rows, :].astype(F32)
+    rest[-1][...] = (value * scale).astype(BF16)
+
+
+def add_kernel(held, got, *rest, scale, copies):
     out = rest[-1]
     rows = held.shape[0]
-    digit = digit_of(bit)
-    out[pl.ds(pl.multiple_of(digit * rows, rows), rows), :] = held[...]
-    out[pl.ds(pl.multiple_of((1 - digit) * rows, rows), rows), :] = got[...]
+    value = ((held[...].astype(F32) + got[...].astype(F32)) * scale).astype(BF16)
+    for k in range(copies):
+        out[k * rows : (k + 1) * rows, :] = value
 
 
 def place_kernel(held, *rest, own):
@@ -293,36 +293,35 @@
     count = lax.axis_size(AXIS)
     rows, width = kept.shape
     got = exchange(sent, 1)
-    if count & (count - 1) or count < 4:
+    if count & (count - 1) or count < 16:
         half = kept + got.astype(F32)
         half = lax.psum(half, AXIS, axis_index_groups=[list(range(c, count, 2)) for c in range(2)])
         both = jnp.stack([half, exchange(half, 1)])
         both = jnp.where(lax.axis_index(AXIS) % 2 == 0, both, both[::-1])
         return both.reshape(2 * rows, width) * scale
-    bits = [1 << k for k in range(1, count.bit_length() - 1)]
-    narrow = in_vmem((rows // 2, width), BF16)
-    held, sent = call(
-        functools.partial(halve_kernel, bit=bits[0]),
-        "halve",
-        [VMEM] * 2,
-        [in_vmem(narrow.shape, F32), narrow],
-        scratch=[pltpu.VMEM((rows, width), F32)],
-    )(kept, got)
+    half = call(cores_kernel, "cores", [VMEM] * 2, in_vmem((rows, width), BF16))(kept, got)
+    near = [0, 2, 4, 6]
+    groups = [[first + step for step in near] for first in range(count) if first & 6 == 0]
+
+    def swap_pieces(value):
+        value = lax.all_to_all(value.reshape(4, rows // 4, width), AXIS, 0, 0, axis_index_groups=groups)
+        return value.reshape(rows, width)
+
+    bits = [1 << k for k in range(3, count.bit_length() - 1)]
+    narrow = in_vmem((rows // 4, width), BF16)
+    held = call(
+        functools.partial(pieces_kernel, scale=1.0), "pieces", [VMEM, ANY], narrow
+    )(swap_pieces(half), beside[0])
     for k, bit in enumerate(bits):
-        after = beside[k : k + 1]
-        held = sent = call(
-            functools.partial(add_kernel, scale=scale if k == len(bits) - 1 else 1.0),
+        last = k == len(bits) - 1
+        after = [beside[1]] if k == 0 else []
+        held = call(
+            functools.partial(add_kernel, scale=scale if last else 1.0, copies=4 if last else 1),
             "add",
             [VMEM] * 2 + [ANY] * len(after),
-            narrow,
-        )(held, exchange(sent, bit), *after)
-    after = beside[len(bits) :]
-    held = call(
-        functools.partial(join_kernel, bit=bits[0]),
-        "join",
-        [VMEM] * 2 + [ANY] * len(after),
-        in_vmem((rows, width), BF16),
-    )(held, exchange(held, bits[0]), *after)
+            in_vmem((rows, width), BF16) if last else narrow,
+        )(held, exchange(held, bit), *after)
+    held, *_ = lax.optimization_barrier((swap_pieces(held), *beside[2:]))
     got = exchange(held, 1)
 
     def place(half, own, *begun):

time: 57.3 us -> 64.1 us (1.12); the launches traced: 57.4 us -> 63.2 us
  blocking collectives: 0 us -> 8.23 us
  waiting for transfers between devices: 11 us -> 7.77 us
  Pallas kernels: 26 us -> 27.8 us
  starting transfers between devices: 19.4 us -> 18.5 us
    all_to_all x0 -> x1, blocking collectives: none -> 8.23 us  [swap_pieces(): lax.all_to_all(value.reshape(4, rows // 4, width), AXIS, 0, 0, axis_index...]
    ppermute x12 -> x9, waiting for transfers between devices: 9.39 us -> 1.54 us  [exchange(): return lax.ppermute(value, AXIS, [(i, i ^ mask) for i in range(count)])]
    ppermute x12 -> x9, starting transfers between devices: 8.11 us -> 4.38 us  [exchange(): return lax.ppermute(value, AXIS, [(i, i ^ mask) for i in range(count)])]
    all_to_all x0 -> x1, waiting for transfers between devices: none -> 3.46 us  [swap_pieces(): lax.all_to_all(value.reshape(4, rows // 4, width), AXIS, 0, 0, axis_index...]
    all_to_all x0 -> x1, starting transfers between devices: none -> 3.41 us  [swap_pieces(): lax.all_to_all(value.reshape(4, rows // 4, width), AXIS, 0, 0, axis_index...]
    pallas_call x4, Pallas kernels: 7.8 us -> 8.97 us  [embed(): call(functools.partial(embed_kernel, blocks=blocks, g=g, scale=1.0 / math...]
    ppermute x4, waiting for transfers between devices: 1.63 us -> 2.78 us  [off_swap(): return lax.ppermute(value, AXIS, off_route)]
  transfers between devices with their start and end apart: 16 -> 14, of which waited for: 7 -> 4; matrix products, arithmetic and copies ran while one was open for 0% -> 0% of each run, Pallas kernels for 38% -> 37%
where the time goes in v10:
time: 64.1 us; the launch traced here: 63.2 us
  Pallas kernels  27.8 us (43%)
  starting transfers between devices  18.5 us (29%)
  blocking collectives  8.23 us (13%)
  waiting for transfers between devices  7.77 us (12%)
  between operations  0.89 us (1%)
    ppermute x4, starting transfers between devices, off_swap(): return lax.ppermute(value, AXIS, off_route)  10.7 us
    pallas_call x4, Pallas kernels, embed(): call(functools.partial(embed_kernel, blocks=blocks, g=g, scale=1.0 / math...  8.97 us
    all_to_all x1, blocking collectives, swap_pieces(): lax.all_to_all(value.reshape(4, rows // 4, width), AXIS, 0, 0, axis_index...  8.23 us
    ppermute x9, starting transfers between devices, exchange(): return lax.ppermute(value, AXIS, [(i, i ^ mask) for i in range(count)])  4.38 us
    pallas_call x2, Pallas kernels, signal_of(): call(functools.partial(signal_kernel, slot=slot), 'signal', [SMEM] + [VME...  3.53 us
    all_to_all x1, waiting for transfers between devices, swap_pieces(): lax.all_to_all(value.reshape(4, rows // 4, width), AXIS, 0, 0, axis_index...  3.46 us
    all_to_all x1, starting transfers between devices, swap_pieces(): lax.all_to_all(value.reshape(4, rows // 4, width), AXIS, 0, 0, axis_index...  3.41 us
    ppermute x4, waiting for transfers between devices, off_swap(): return lax.ppermute(value, AXIS, off_route)  2.78 us
  transfers between devices with their start and end apart: 14, of which 4 were waited for; matrix products, arithmetic and copies ran while one was open for 0% of the time, Pallas kernels for 37%

profile of v10, /device:TPU:0, one launch (start us, length us, event | category | flops | bytes accessed | tf_op | source)
XLA Modules:
  0.0 63.2 jit_solution(10208487531076217102)
XLA Ops:
  0.7 2.0 %project.1 = (bf16[256,512]{1,0:T(8,128)(2,1)S(1)}, bf16[256,768]{1,0:T(8,128)(2,1)S(1)}, bf16[2048,768]{1,0:T(8,128)(2,1)S(1)}) custom-call(s32[2,64]{1,0:T(2,128)} %bitcast.11, bf16[256,768]{1,0:T(8,128)(2,1)} %queries.1, bf16[2048,768]{1,0:T(8,128)(2,1)} %embeddings.1), custom_call_target="tpu_custom_call" | custom-call | tf_op jit(solution)/shard_map/project/pallas_call | solution.py:363
  2.7 5.5 %collective-permute-start.4 = (bf16[256,512]{1,0:T(8,128)(2,1)S(1)}, bf16[256,512]{1,0:T(8,128)(2,1)S(1)}, u32[]{:S(2)}, u32[]{:S(2)}) collective-permute-start(bf16[256,512]{1,0:T(8,128)(2,1)S(1)} %get-tuple-element.38), channel_id=1, source_target_pairs={{1,2},{3,4},{5,6},{7,8},{9,10},{11,12},{13,14},{15,0},{2,1},{4,3},... | collective-permute-start | bytes 786440 | tf_op jit(solution)/shard_map/ppermute | solution.py:351
  8.2 1.6 %own.1 = (f32[4,256,512]{2,1,0:T(8,128)S(1)}, bf16[256,512]{1,0:T(8,128)(2,1)S(1)}, bf16[176,512]{1,0:T(8,128)(2,1)S(1)}, bf16[176,512]{1,0:T(8,128)(2,1)S(1)}, bf16[160,512]{1,0:T(8,128)(2,1)S(1)}) custom-call(s32[2,64]{1,0:T(2,128)S(1)} %bitcast.12, bf16[256,768]{1,0:T(8,128)(2,1)S(1)} %get-tuple-element.29.queries, ...), custom_call_target="tpu_custom_call" | custom-call | tf_op jit(solution)/shard_map/own/pallas_call | solution.py:371
  9.9 0.5 collective-permute-start.1
  10.5 0.6 collective-permute-start.3
  11.1 2.4 %hits.1 = (bf16[4,256,512]{2,1,0:T(8,128)(2,1)S(1)}, bf16[4,2,512,512]{3,2,1,0:T(8,128)(2,1)S(1)}) custom-call(s32[8,256]{1,0:T(8,128)S(1)} %bitcast.26, bf16[4,2,512,512]{3,2,1,0:T(8,128)(2,1)} %tiles.1), custom_call_target="tpu_custom_call" | custom-call | tf_op jit(solution)/shard_map/hits/pallas_call | solution.py:378
  13.6 1.3 %base.1 = f32[4,256,512]{2,1,0:T(8,128)S(1)} custom-call(s32[2,64]{1,0:T(2,128)S(1)} %bitcast.13, f32[4,256,512]{2,1,0:T(8,128)S(1)} %get-tuple-element.31.own, bf16[4,2,512,512]{3,2,1,0:T(8,128)(2,1)S(1)} %get-tuple-element.32.tiles, bf16[176,512]{1,0:T(8,128)(2,1)S(1)} %collective-permute-done.rest_0_, ...), custom_call_target="tpu_custom_call" | custom-call | tf_op jit(solution)/shard_map/base/pallas_call | solution.py:386
  15.0 2.3 %signal.2 = (bf16[4,256,512]{2,1,0:T(8,128)(2,1)S(1)}, bf16[256,512]{1,0:T(8,128)(2,1)S(1)}) custom-call(s32[2,64]{1,0:T(2,128)S(1)} %bitcast.14, f32[4,256,512]{2,1,0:T(8,128)S(1)} %base.1, bf16[4,256,512]{2,1,0:T(8,128)(2,1)S(1)} %get-tuple-element.36.hits, f32[1,2048]{1,0:T(1,128)S(1)} %bitcast.24, bf16[256,512]{1,0:T(8,128)(2,1)S(1)} %collective-permute-done.4.received, ...), custom_call_target="tpu_custom_call" | custom-call | flops 2000000000 | tf_op jit(solution)/shard_map/signal/pallas_call | solution.py:396
  17.4 3.9 %collective-permute-start.5 = (bf16[256,512]{1,0:T(8,128)(2,1)S(1)}, bf16[256,512]{1,0:T(8,128)(2,1)S(1)}, u32[]{:S(2)}, u32[]{:S(2)}) collective-permute-start(bf16[256,512]{1,0:T(8,128)(2,1)S(1)} %get-tuple-element.41), channel_id=1, source_target_pairs={{1,2},{3,4},{5,6},{7,8},{9,10},{11,12},{13,14},{15,0},{2,1},{4,3},... | collective-permute-start | bytes 786440 | tf_op jit(solution)/shard_map/ppermute | solution.py:351
  21.2 1.2 %signal.3 = (bf16[4,256,512]{2,1,0:T(8,128)(2,1)S(1)}, bf16[256,512]{1,0:T(8,128)(2,1)S(1)}) custom-call(s32[2,64]{1,0:T(2,128)S(1)} %bitcast.15, f32[4,256,512]{2,1,0:T(8,128)S(1)} %base.1, bf16[4,256,512]{2,1,0:T(8,128)(2,1)S(1)} %get-tuple-element.36.hits, f32[1,2048]{1,0:T(1,128)S(1)} %bitcast.25, ...), custom_call_target="tpu_custom_call", output_to_operand_aliasing={{0}: (6, {})} | custom-call | tf_op jit(solution)/shard_map/signal/pallas_call | solution.py:396
  22.5 0.7 %collective-permute-start.9 = (bf16[256,512]{1,0:T(8,128)(2,1)S(1)}, bf16[256,512]{1,0:T(8,128)(2,1)S(1)}, u32[]{:S(2)}, u32[]{:S(2)}) collective-permute-start(bf16[256,512]{1,0:T(8,128)(2,1)S(1)} %get-tuple-element.46), channel_id=1, source_target_pairs={{1,2},{3,4},{5,6},{7,8},{9,10},{11,12},{13,14},{15,0},{2,1},{4,3},... | collective-permute-start | bytes 786440 | tf_op jit(solution)/shard_map/ppermute | solution.py:351
  23.1 1.4 %push.1 = (bf16[176,512]{1,0:T(8,128)(2,1)S(1)}, bf16[176,512]{1,0:T(8,128)(2,1)S(1)}, bf16[160,512]{1,0:T(8,128)(2,1)S(1)}) custom-call(s32[2,64]{1,0:T(2,128)S(1)} %bitcast.16, bf16[4,256,512]{2,1,0:T(8,128)(2,1)S(1)} %get-tuple-element.40.signal, bf16[4,2,512,512]{3,2,1,0:T(8,128)(2,1)S(1)} %get-tuple-element.32.tiles), custom_call_target="tpu_custom_call" | custom-call | tf_op jit(solution)/shard_map/push/pallas_call | solution.py:410
  24.6 0.5 collective-permute-start.7
  25.2 1.0 %query.1.part = f32[256,768]{1,0:T(8,128)S(1)} custom-call(bf16[4,256,512]{2,1,0:T(8,128)(2,1)S(1)} %get-tuple-element.40.signal, bf16[2048,768]{1,0:T(8,128)(2,1)S(1)} %get-tuple-element.30.embeddings), custom_call_target="tpu_custom_call" | custom-call | tf_op jit(solution)/shard_map/query/pallas_call | solution.py:420
  26.2 1.0 %query_half.1.part = f32[256,768]{1,0:T(8,128)S(1)} custom-call(s32[2,64]{1,0:T(2,128)S(1)} %bitcast.17, f32[256,768]{1,0:T(8,128)S(1)} %query.1.part, bf16[256,512]{1,0:T(8,128)(2,1)S(1)} %collective-permute-done.5.received.off_a, bf16[2048,768]{1,0:T(8,128)(2,1)S(1)} %get-tuple-element.30.embeddings), custom_call_target="tpu_custom_call" | custom-call | flops 1000000000 | tf_op jit(solution)/shard_map/query_half/pallas_call | solution.py:421
  27.2 1.2 %query_on.1 = (f32[256,768]{1,0:T(8,128)S(1)}, bf16[2,256,512]{2,1,0:T(8,128)(2,1)S(1)}) custom-call(s32[2,64]{1,0:T(2,128)S(1)} %bitcast.18, f32[256,768]{1,0:T(8,128)S(1)} %query_half.1.part, bf16[2048,768]{1,0:T(8,128)(2,1)S(1)} %get-tuple-element.30.embeddings, bf16[176,512]{1,0:T(8,128)(2,1)S(1)} %collective-permute-done.6.rest_0_, ...), custom_call_target="tpu_custom_call" | custom-call | tf_op jit(solution)/shard_map/query_on/pallas_call | solution.py:428
  28.3 2.8 %collective-permute-done.9.off_b.received = bf16[256,512]{1,0:T(8,128)(2,1)S(1)} collective-permute-done((bf16[256,512]{1,0:T(8,128)(2,1)S(1)}, bf16[256,512]{1,0:T(8,128)(2,1)S(1)}, u32[]{:S(2)}, u32[]{:S(2)}) %collective-permute-start.9) | collective-permute-done | bytes 262176 | tf_op jit(solution)/shard_map/ppermute | solution.py:351
  31.1 1.0 %query_end.1 = (f32[128,768]{1,0:T(8,128)S(1)}, bf16[128,768]{1,0:T(8,128)(2,1)S(1)}) custom-call(s32[2,64]{1,0:T(2,128)S(1)} %bitcast.19, f32[256,768]{1,0:T(8,128)S(1)} %get-tuple-element.51.part, bf16[256,512]{1,0:T(8,128)(2,1)S(1)} %collective-permute-done.9.off_b.received, bf16[2048,768]{1,0:T(8,128)(2,1)S(1)} %get-tuple-element.30.embeddings), custom_call_target="tpu_custom_call" | custom-call | tf_op jit(solution)/shard_map/query_end/pallas_call | solution.py:432
  32.1 0.3 collective-permute-start.10
  32.4 1.2 %collective-permute-done.10.got = bf16[128,768]{1,0:T(8,128)(2,1)S(1)} collective-permute-done((bf16[128,768]{1,0:T(8,128)(2,1)S(1)}, bf16[128,768]{1,0:T(8,128)(2,1)S(1)}, u32[]{:S(2)}, u32[]{:S(2)}) %collective-permute-start.10) | collective-permute-done | bytes 196640 | tf_op jit(solution)/shard_map/ppermute | solution.py:250
  33.6 0.7 %cores.1 = bf16[128,768]{1,0:T(8,128)(2,1)} custom-call(f32[128,768]{1,0:T(8,128)S(1)} %get-tuple-element.52.held, bf16[128,768]{1,0:T(8,128)(2,1)S(1)} %collective-permute-done.10.got), custom_call_target="tpu_custom_call" | custom-call | tf_op jit(solution)/shard_map/cores/pallas_call | solution.py:302
  34.4 3.4 %all-to-all-start = ((bf16[4,32,768]{2,1,0:T(8,128)(2,1)}), bf16[4,32,768]{2,1,0:T(8,128)(2,1)S(1)}, u32[]{:S(2)}, u32[]{:S(2)}) async-start(bf16[4,32,768]{2,1,0:T(8,128)(2,1)} %bitcast.3), calls=%async_computation | async-start | bytes 393216 | tf_op jit(solution)/shard_map/all_to_all | solution.py:307
  37.8 2.0 %embed.4 = (bf16[2048,768]{1,0:T(8,128)(2,1)}, f32[8,128]{1,0:T(8,128)S(1)}) custom-call(s32[2,64]{1,0:T(2,128)S(1)} %bitcast.20, bf16[4,256,512]{2,1,0:T(8,128)(2,1)S(1)} %get-tuple-element.40.signal, bf16[2,256,512]{2,1,0:T(8,128)(2,1)S(1)} %get-tuple-element.45.on, bf16[256,512]{1,0:T(8,128)(2,1)S(1)} %collective-permute-done.5.received.off_a, ...), custom_call_target="tpu_custom_call" | custom-call | tf_op jit(solution)/shard_map/embed/pallas_call | solution.py:441
  39.8 3.5 %all-to-all-done = bf16[4,32,768]{2,1,0:T(8,128)(2,1)S(1)} async-done(((bf16[4,32,768]{2,1,0:T(8,128)(2,1)}), bf16[4,32,768]{2,1,0:T(8,128)(2,1)S(1)}, u32[]{:S(2)}, u32[]{:S(2)}) %all-to-all-start) | async-done | bytes 196640 | tf_op jit(solution)/shard_map/all_to_all | solution.py:307
  43.3 2.8 %collective-permute-start.11 = (bf16[32,768]{1,0:T(8,128)(2,1)S(1)}, bf16[32,768]{1,0:T(8,128)(2,1)S(1)}, u32[]{:S(2)}, u32[]{:S(2)}) collective-permute-start(bf16[32,768]{1,0:T(8,128)(2,1)S(1)} %pieces.1.held), channel_id=1, source_target_pairs={{0,8},{1,9},{2,10},{3,11},{4,12},{5,13},{6,14},{7,15},{8,0},{9,1},... | collective-permute-start | bytes 147464 | tf_op jit(solution)/shard_map/ppermute | solution.py:250
  46.0 1.9 %embed.5 = (bf16[2048,768]{1,0:T(8,128)(2,1)}, f32[8,128]{1,0:T(8,128)S(1)}) custom-call(s32[2,64]{1,0:T(2,128)S(1)} %bitcast.21, bf16[4,256,512]{2,1,0:T(8,128)(2,1)S(1)} %get-tuple-element.40.signal, bf16[2,256,512]{2,1,0:T(8,128)(2,1)S(1)} %get-tuple-element.45.on, ...), custom_call_target="tpu_custom_call", output_to_operand_aliasing={{0}: (6, {})} | custom-call | tf_op jit(solution)/shard_map/embed/pallas_call | solution.py:441
  48.0 0.3 collective-permute-done.11.got
  48.3 8.2 %all_to_all.10 = bf16[4,32,768]{2,1,0:T(8,128)(2,1)S(1)} all-to-all(bf16[4,32,768]{2,1,0:T(8,128)(2,1)S(1)} %bitcast.8), channel_id=1, replica_groups={{0,2,4,6},{1,3,5,7},{8,10,12,14},{9,11,13,15},{16,18,20,22},{17,19,21,2..., dimensions={0} | all-to-all | bytes 393216 | tf_op jit(solution)/shard_map/all_to_all | solution.py:307
  56.6 2.5 %embed.6 = (bf16[2048,768]{1,0:T(8,128)(2,1)}, f32[8,128]{1,0:T(8,128)}) custom-call(s32[2,64]{1,0:T(2,128)S(1)} %bitcast.22, bf16[4,256,512]{2,1,0:T(8,128)(2,1)S(1)} %get-tuple-element.40.signal, bf16[2,256,512]{2,1,0:T(8,128)(2,1)S(1)} %get-tuple-element.45.on, ...), custom_call_target="tpu_custom_call", output_to_operand_aliasing={{0}: (6, {})} | custom-call | tf_op jit(solution)/shard_map/embed/pallas_call | solution.py:441
  59.1 2.5 %embed.7 = (bf16[2048,768]{1,0:T(8,128)(2,1)}, f32[8,128]{1,0:T(8,128)}) custom-call(s32[2,64]{1,0:T(2,128)S(1)} %bitcast.23, bf16[4,256,512]{2,1,0:T(8,128)(2,1)S(1)} %get-tuple-element.40.signal, bf16[2,256,512]{2,1,0:T(8,128)(2,1)S(1)} %get-tuple-element.45.on, ...), custom_call_target="tpu_custom_call", output_to_operand_aliasing={{0}: (6, {})} | custom-call | tf_op jit(solution)/shard_map/embed/pallas_call | solution.py:441
  61.6 0.8 %place.2.rest_0_ = f32[256,768]{1,0:T(8,128)} custom-call(bf16[128,768]{1,0:T(8,128)(2,1)S(1)} %bitcast.10), custom_call_target="tpu_custom_call" | custom-call | tf_op jit(solution)/shard_map/place/pallas_call | solution.py:328
  62.4 0.8 %place.3 = f32[256,768]{1,0:T(8,128)} custom-call(bf16[128,768]{1,0:T(8,128)(2,1)S(1)} %collective-permute-done.12.held, f32[256,768]{1,0:T(8,128)} %place.2.rest_0_), custom_call_target="tpu_custom_call", output_to_operand_aliasing={{}: (1, {})} | custom-call | tf_op jit(solution)/shard_map/place/pallas_call | solution.py:328
  (23 shorter events, 0.4 us)
Async XLA Ops:
  0.6 7.6 %copy-start = (s32[64,2]{0,1:T(2,128)S(1)}, s32[64,2]{0,1:T(2,128)}, u32[]{:S(2)}) copy-start(s32[64,2]{0,1:T(2,128)} %param.8) | copy-start | bytes 1540
  0.6 10.5 %copy-start.2 = (s32[256,8]{0,1:T(8,128)S(1)}, s32[256,8]{0,1:T(8,128)}, u32[]{:S(2)}) copy-start(s32[256,8]{0,1:T(8,128)} %param.11) | copy-start | bytes 24580
  2.7 12.3 %collective-permute-start.4 = (bf16[256,512]{1,0:T(8,128)(2,1)S(1)}, bf16[256,512]{1,0:T(8,128)(2,1)S(1)}, u32[]{:S(2)}, u32[]{:S(2)}) collective-permute-start(bf16[256,512]{1,0:T(8,128)(2,1)S(1)} %get-tuple-element.38), channel_id=1, source_target_pairs={{1,2},{3,4},{5,6},{7,8},{9,10},{11,12},{13,14},{15,0},{2,1},{4,3},... | collective-permute-start | bytes 786440 | tf_op jit(solution)/shard_map/ppermute | solution.py:351
  9.9 3.7 %collective-permute-start = (bf16[176,512]{1,0:T(8,128)(2,1)S(1)}, bf16[176,512]{1,0:T(8,128)(2,1)S(1)}, u32[]{:S(2)}, u32[]{:S(2)}) collective-permute-start(bf16[176,512]{1,0:T(8,128)(2,1)S(1)} %get-tuple-element.33), channel_id=1, source_target_pairs={{0,1},{1,0},{2,3},{3,2},{4,5},{5,4},{6,7},{7,6},{8,9},{9,8},{10,11... | collective-permute-start | bytes 540680 | tf_op jit(solution)/shard_map/ppermute | solution.py:250
  9.9 3.7 %collective-permute-start.1 = (bf16[176,512]{1,0:T(8,128)(2,1)S(1)}, bf16[176,512]{1,0:T(8,128)(2,1)S(1)}, u32[]{:S(2)}, u32[]{:S(2)}) collective-permute-start(bf16[176,512]{1,0:T(8,128)(2,1)S(1)} %get-tuple-element.34), channel_id=1, source_target_pairs={{0,1},{1,0},{2,3},{3,2},{4,5},{5,4},{6,7},{7,6},{8,9},{9,8},{10,11... | collective-permute-start | bytes 540680 | tf_op jit(solution)/shard_map/ppermute | solution.py:250
  10.4 3.2 %collective-permute-start.2 = (bf16[160,512]{1,0:T(8,128)(2,1)S(1)}, bf16[160,512]{1,0:T(8,128)(2,1)S(1)}, u32[]{:S(2)}, u32[]{:S(2)}) collective-permute-start(bf16[160,512]{1,0:T(8,128)(2,1)S(1)} %get-tuple-element.35), channel_id=1, source_target_pairs={{0,1},{1,0},{2,3},{3,2},{4,5},{5,4},{6,7},{7,6},{8,9},{9,8},{10,11... | collective-permute-start | bytes 491528 | tf_op jit(solution)/shard_map/ppermute | solution.py:250
  10.5 10.7 %collective-permute-start.3 = (bf16[256,512]{1,0:T(8,128)(2,1)S(1)}, bf16[256,512]{1,0:T(8,128)(2,1)S(1)}, u32[]{:S(2)}, u32[]{:S(2)}) collective-permute-start(bf16[256,512]{1,0:T(8,128)(2,1)S(1)} %get-tuple-element.37), channel_id=1, source_target_pairs={{1,2},{3,4},{5,6},{7,8},{9,10},{11,12},{13,14},{15,0},{2,1},{4,3},... | collective-permute-start | bytes 786440 | tf_op jit(solution)/shard_map/ppermute | solution.py:351
  13.6 1.4 %copy-start.1 = (f32[2048]{0:T(1024)S(1)}, f32[2048]{0:T(1024)}, u32[]{:S(2)}) copy-start(f32[2048]{0:T(1024)} %param.9) | copy-start | bytes 24580
  17.4 8.8 %collective-permute-start.5 = (bf16[256,512]{1,0:T(8,128)(2,1)S(1)}, bf16[256,512]{1,0:T(8,128)(2,1)S(1)}, u32[]{:S(2)}, u32[]{:S(2)}) collective-permute-start(bf16[256,512]{1,0:T(8,128)(2,1)S(1)} %get-tuple-element.41), channel_id=1, source_target_pairs={{1,2},{3,4},{5,6},{7,8},{9,10},{11,12},{13,14},{15,0},{2,1},{4,3},... | collective-permute-start | bytes 786440 | tf_op jit(solution)/shard_map/ppermute | solution.py:351
  22.5 8.7 %collective-permute-start.9 = (bf16[256,512]{1,0:T(8,128)(2,1)S(1)}, bf16[256,512]{1,0:T(8,128)(2,1)S(1)}, u32[]{:S(2)}, u32[]{:S(2)}) collective-permute-start(bf16[256,512]{1,0:T(8,128)(2,1)S(1)} %get-tuple-element.46), channel_id=1, source_target_pairs={{1,2},{3,4},{5,6},{7,8},{9,10},{11,12},{13,14},{15,0},{2,1},{4,3},... | collective-permute-start | bytes 786440 | tf_op jit(solution)/shard_map/ppermute | solution.py:351
  24.5 2.6 %collective-permute-start.6 = (bf16[176,512]{1,0:T(8,128)(2,1)S(1)}, bf16[176,512]{1,0:T(8,128)(2,1)S(1)}, u32[]{:S(2)}, u32[]{:S(2)}) collective-permute-start(bf16[176,512]{1,0:T(8,128)(2,1)S(1)} %get-tuple-element.42), channel_id=1, source_target_pairs={{0,1},{1,0},{2,3},{3,2},{4,5},{5,4},{6,7},{7,6},{8,9},{9,8},{10,11... | collective-permute-start | bytes 540680 | tf_op jit(solution)/shard_map/ppermute | solution.py:250
  24.6 2.6 %collective-permute-start.7 = (bf16[176,512]{1,0:T(8,128)(2,1)S(1)}, bf16[176,512]{1,0:T(8,128)(2,1)S(1)}, u32[]{:S(2)}, u32[]{:S(2)}) collective-permute-start(bf16[176,512]{1,0:T(8,128)(2,1)S(1)} %get-tuple-element.43), channel_id=1, source_target_pairs={{0,1},{1,0},{2,3},{3,2},{4,5},{5,4},{6,7},{7,6},{8,9},{9,8},{10,11... | collective-permute-start | bytes 540680 | tf_op jit(solution)/shard_map/ppermute | solution.py:250
  25.1 2.0 %collective-permute-start.8 = (bf16[160,512]{1,0:T(8,128)(2,1)S(1)}, bf16[160,512]{1,0:T(8,128)(2,1)S(1)}, u32[]{:S(2)}, u32[]{:S(2)}) collective-permute-start(bf16[160,512]{1,0:T(8,128)(2,1)S(1)} %get-tuple-element.44), channel_id=1, source_target_pairs={{0,1},{1,0},{2,3},{3,2},{4,5},{5,4},{6,7},{7,6},{8,9},{9,8},{10,11... | collective-permute-start | bytes 491528 | tf_op jit(solution)/shard_map/ppermute | solution.py:250
  32.1 1.5 %collective-permute-start.10 = (bf16[128,768]{1,0:T(8,128)(2,1)S(1)}, bf16[128,768]{1,0:T(8,128)(2,1)S(1)}, u32[]{:S(2)}, u32[]{:S(2)}) collective-permute-start(bf16[128,768]{1,0:T(8,128)(2,1)S(1)} %get-tuple-element.53), channel_id=1, source_target_pairs={{0,1},{1,0},{2,3},{3,2},{4,5},{5,4},{6,7},{7,6},{8,9},{9,8},{10,11... | collective-permute-start | bytes 589832 | tf_op jit(solution)/shard_map/ppermute | solution.py:250
  34.4 8.9 %all-to-all-start = ((bf16[4,32,768]{2,1,0:T(8,128)(2,1)}), bf16[4,32,768]{2,1,0:T(8,128)(2,1)S(1)}, u32[]{:S(2)}, u32[]{:S(2)}) async-start(bf16[4,32,768]{2,1,0:T(8,128)(2,1)} %bitcast.3), calls=%async_computation | async-start | bytes 393216 | tf_op jit(solution)/shard_map/all_to_all | solution.py:307
  43.3 5.1 %collective-permute-start.11 = (bf16[32,768]{1,0:T(8,128)(2,1)S(1)}, bf16[32,768]{1,0:T(8,128)(2,1)S(1)}, u32[]{:S(2)}, u32[]{:S(2)}) collective-permute-start(bf16[32,768]{1,0:T(8,128)(2,1)S(1)} %pieces.1.held), channel_id=1, source_target_pairs={{0,8},{1,9},{2,10},{3,11},{4,12},{5,13},{6,14},{7,15},{8,0},{9,1},... | collective-permute-start | bytes 147464 | tf_op jit(solution)/shard_map/ppermute | solution.py:250
  56.6 5.9 %collective-permute-start.12 = (bf16[128,768]{1,0:T(8,128)(2,1)S(1)}, bf16[128,768]{1,0:T(8,128)(2,1)S(1)}, u32[]{:S(2)}, u32[]{:S(2)}) collective-permute-start(bf16[128,768]{1,0:T(8,128)(2,1)S(1)} %bitcast.9), channel_id=1, source_target_pairs={{0,1},{1,0},{2,3},{3,2},{4,5},{5,4},{6,7},{7,6},{8,9},{9,8},{10,11... | collective-permute-start | bytes 589832 | tf_op jit(solution)/shard_map/ppermute | solution.py:250

commit v11 on v8

--- a/solution.py
+++ b/solution.py
@@ -202,12 +202,24 @@
     rows = kept.shape[0]
     core = lax.axis_index(AXIS) % 2
     kept[...] = total[pl.ds(pl.multiple_of(core * rows, rows), rows), :]
-    sent[...] = total[pl.ds(pl.multiple_of((1 - core) * rows, rows), rows), :]
+    sent[...] = total[pl.ds(pl.multiple_of((1 - core) * rows, rows), rows), :].astype(BF16)
 
 
 def embed_kernel(lists, signal, on, off_a, off_b, queries, *rest, blocks, g, scale):
-    out, token, total, ready, sem = rest[-5:]
-    block = signal.shape[2]
+    if g == 0:
+        ready, token, total = rest
+    else:
+        before = rest[0]
+        out, ready, token, total, sem = rest[-5:]
+    rows, block = total.shape
+    writes = []
+
+    def write(source, index, slot):
+        writes.append(pltpu.make_async_copy(source, out.at[pl.ds(index * block, block), :], sem.at[slot]))
+        writes[-1].start()
+
+    if g > 0:
+        write(before, g - 1, 0)
     token[...] = jnp.zeros_like(token)
     total[...] = signal[g].astype(F32)
     named = named_by_partner(lists, blocks, ON) + named_by_partner(lists, blocks, OFF)
@@ -218,9 +230,10 @@
             total[...] += received[...].astype(F32)
 
     ready[...] = (dot(total[...].astype(BF16), queries[...], TN) * scale).astype(BF16)
-    copy = pltpu.make_async_copy(ready, out.at[pl.ds(g * block, block), :], sem)
-    copy.start()
-    copy.wait()
+    if g == blocks - 1:
+        write(ready, g, 1)
+    for copy in writes:
+        copy.wait()
 
 
 VMEM = pl.BlockSpec(memory_space=pltpu.VMEM)
@@ -260,7 +273,7 @@
 
 def halve_kernel(held, got, *outs, bits):
     total = outs[-1]
-    total[...] = held[...] + got[...]
+    total[...] = held[...] + got[...].astype(F32)
     rows = outs[0].shape[0]
     for chain, bit in enumerate(bits):
         kept, sent = outs[2 * chain], outs[2 * chain + 1]
@@ -270,21 +283,19 @@
         sent[...] = total[pl.ds(pl.multiple_of(begin + (1 - digit) * rows, rows), rows), :].astype(BF16)
 
 
-def add_kernel(*refs, scale):
-    *ins, out_a, out_b = refs
-    for held, got, out in ((ins[0], ins[1], out_a), (ins[2], ins[3], out_b)):
-        out[...] = ((held[...].astype(F32) + got[...].astype(F32)) * scale).astype(BF16)
-
-
-def join_kernel(*refs, bits):
-    *ins, out = refs
-    rows = ins[0].shape[0]
-    for chain, bit in enumerate(bits):
-        held, got = ins[2 * chain], ins[2 * chain + 1]
-        begin = 2 * chain * rows
-        digit = digit_of(bit)
-        out[pl.ds(pl.multiple_of(begin + digit * rows, rows), rows), :] = held[...]
-        out[pl.ds(pl.multiple_of(begin + (1 - digit) * rows, rows), rows), :] = got[...]
+def add_kernel(held, got, *rest, scale):
+    rest[-1][...] = ((held[...].astype(F32) + got[...].astype(F32)) * scale).astype(BF16)
+
+
+def join_kernel(held, got, *rest, bit):
+    out = rest[-1]
+    rows = held.shape[0]
+    begin = out.shape[0] - 2 * rows
+    if begin:
+        out[:begin, :] = rest[0][...]
+    digit = digit_of(bit)
+    out[pl.ds(pl.multiple_of(begin + digit * rows, rows), rows), :] = held[...]
+    out[pl.ds(pl.multiple_of(begin + (1 - digit) * rows, rows), rows), :] = got[...]
 
 
 def place_kernel(held, *rest, own):
@@ -303,11 +314,11 @@
     rows, width = kept.shape
     got = exchange(sent, 1)
     if count & (count - 1) or count < 8:
-        half = lax.psum(kept + got, AXIS, axis_index_groups=[list(range(c, count, 2)) for c in range(2)])
+        half = kept + got.astype(F32)
+        half = lax.psum(half, AXIS, axis_index_groups=[list(range(c, count, 2)) for c in range(2)])
         both = jnp.stack([half, exchange(half, 1)])
         both = jnp.where(lax.axis_index(AXIS) % 2 == 0, both, both[::-1])
         return both.reshape(2 * rows, width) * scale
-    piece = jax.ShapeDtypeStruct((rows // 2, width), BF16)
     bits = [1 << k for k in range(1, count.bit_length() - 1)]
     orders = [[bits[0], *bits[2:], bits[1]], [bits[1], bits[0], *bits[2:]]]
     ends = [order[0] for order in orders]
@@ -322,21 +333,30 @@
     held, sent = [kept_a, kept_b], [sent_a, sent_b]
     for k in range(len(bits)):
         got = [exchange(piece, order[k]) for piece, order in zip(sent, orders)]
-        after = beside[k : k + 1]
-        held = sent = call(
-            functools.partial(add_kernel, scale=scale if k == len(bits) - 1 else 1.0),
-            "add",
-            [VMEM] * 4 + [ANY] * len(after),
-            [narrow, narrow],
-        )(held[0], got[0], held[1], got[1], *after)
+        for chain in range(2):
+            after = beside[k : k + 1] if chain == 0 else []
+            held[chain] = call(
+                functools.partial(add_kernel, scale=scale if k == len(bits) - 1 else 1.0),
+                "add",
+                [VMEM] * 2 + [ANY] * len(after),
+                narrow,
+            )(held[chain], got[chain], *after)
+        sent = list(held)
     got = [exchange(piece, bit) for piece, bit in zip(held, ends)]
-    after = beside[len(bits) :]
-    held = call(
-        functools.partial(join_kernel, bits=ends),
-        "join",
-        [VMEM] * 4 + [ANY] * len(after),
-        in_vmem((rows, width), BF16),
-    )(held[0], got[0], held[1], got[1], *after)
+    joined = []
+    for chain, bit in enumerate(ends):
+        rows_out = (chain + 1) * rows // 2
+        after = beside[len(bits) :] if chain == 0 else []
+        joined = [
+            call(
+                functools.partial(join_kernel, bit=bit),
+                "join",
+                [VMEM] * (2 + len(joined)) + [ANY] * len(after),
+                in_vmem((rows_out, width), BF16),
+                flops=2 * 10**8,
+            )(held[chain], got[chain], *joined, *after)
+        ]
+    held = joined[0]
     got = exchange(held, 1)
 
     def place(half, own, *begun):
@@ -443,35 +463,30 @@
     part, on = call(
         functools.partial(query_on_kernel, blocks=blocks), "query_on", [SMEM] + [VMEM] * 5, [whole, pair]
     )(lists, part, embeddings, *back_on)
-    piece = in_vmem((rows // 2, width), F32)
+    kept, sent = (in_vmem((rows // 2, width), kind) for kind in (F32, BF16))
     kept, sent = call(
         functools.partial(query_end_kernel, blocks=blocks),
         "query_end",
         [SMEM] + [VMEM] * 3,
-        [piece, piece],
+        [kept, sent],
         scratch=[pltpu.VMEM((rows, width), F32)],
     )(lists, part, back_b, embeddings)
 
-    def embed(g, *begun):
-        return call(
+    ready = in_vmem((block, width), BF16)
+    written = jax.ShapeDtypeStruct((labels_dev, width), BF16)
+    outs, tokens = [], []
+    for g in range(blocks):
+        *outs, token = call(
             functools.partial(embed_kernel, blocks=blocks, g=g, scale=1.0 / math.sqrt(rows)),
             "embed",
-            [SMEM] + [VMEM] * 5 + [ANY] * len(begun),
-            [jax.ShapeDtypeStruct((labels_dev, width), BF16), in_vmem((8, 128), F32)],
-            out_specs=[ANY, VMEM],
-            scratch=[
-                pltpu.VMEM((rows, block), F32),
-                pltpu.VMEM((block, width), BF16),
-                pltpu.SemaphoreType.DMA,
-            ],
-            aliases={6: 0} if begun else None,
-        )(lists, signal, on, back_a, back_b, queries, *begun)
-
-    begun, tokens = [], []
-    for g in range(blocks):
-        grad_embed, token = embed(g, *begun)
-        begun = [grad_embed]
+            [SMEM] + [VMEM] * (5 + min(g, 1)) + [ANY] * (len(outs) - 1),
+            ([written] if g else []) + [ready, in_vmem((8, 128), F32)],
+            out_specs=([ANY] if g else []) + [VMEM] * 2,
+            scratch=[pltpu.VMEM((rows, block), F32)] + ([pltpu.SemaphoreType.DMA((2,))] if g else []),
+            aliases={7: 0} if g > 1 else None,
+        )(lists, signal, on, back_a, back_b, queries, *outs[::-1])
         tokens.append(token)
+    grad_embed = outs[0]
     grad_queries = sum_queries(kept, sent, tokens, 1.0 / math.sqrt(labels_dev * count))
     return (grad_embed, grad_queries)
 

time: 59.9 us -> 57.3 us (0.957)
  waiting for transfers between devices: 12.9 us -> 6.32 us
  starting transfers between devices: 19.7 us -> 24.6 us
  Pallas kernels: 26.1 us -> 25.2 us
    ppermute x16, waiting for transfers between devices: 9.55 us -> 3.54 us  [exchange(): return lax.ppermute(value, AXIS, [(i, i ^ mask) for i in range(count)])]
    ppermute x16, starting transfers between devices: 8.84 us -> 14.1 us  [exchange(): return lax.ppermute(value, AXIS, [(i, i ^ mask) for i in range(count)])]
    pallas_call x5 -> x6, Pallas kernels: 7.86 us -> 6.8 us  [the longest x4 6.74 us: per_device(): call(functools.partial(embed_kernel, blocks=blocks, g=g, scale=1.0 / math...]
    ppermute x4, waiting for transfers between devices: 3.38 us -> 2.78 us  [off_swap(): return lax.ppermute(value, AXIS, off_route)]
  transfers between devices with their start and end apart: 20 -> 20, of which waited for: 10 -> 6; matrix products, arithmetic and copies ran while one was open for 0% -> 0% of each run, Pallas kernels for 37% -> 37%
where the time goes in v11:
time: 57.3 us; the launch traced here: 57 us
  Pallas kernels  25.2 us (44%)
  starting transfers between devices  24.6 us (43%)
  waiting for transfers between devices  6.32 us (11%)
  between operations  0.94 us (2%)
    ppermute x16, starting transfers between devices, exchange(): return lax.ppermute(value, AXIS, [(i, i ^ mask) for i in range(count)])  14.1 us
    ppermute x4, starting transfers between devices, off_swap(): return lax.ppermute(value, AXIS, off_route)  10.5 us
    pallas_call x4, Pallas kernels, per_device(): call(functools.partial(embed_kernel, blocks=blocks, g=g, scale=1.0 / math...  6.74 us
    ppermute x16, waiting for transfers between devices, exchange(): return lax.ppermute(value, AXIS, [(i, i ^ mask) for i in range(count)])  3.54 us
    pallas_call x2, Pallas kernels, signal_of(): call(functools.partial(signal_kernel, slot=slot), 'signal', [SMEM] + [VME...  3.54 us
    ppermute x4, waiting for transfers between devices, off_swap(): return lax.ppermute(value, AXIS, off_route)  2.78 us
    pallas_call x1, Pallas kernels, per_device(): call(hits_kernel, 'hits', [VMEM, HBM], [in_vmem(full, BF16), in_vmem(edge...  2.45 us
    pallas_call x1, Pallas kernels, per_device(): call(functools.partial(project_kernel, scale=scale), 'project', [HBM] * 3...  2.2 us
  transfers between devices with their start and end apart: 20, of which 6 were waited for; matrix products, arithmetic and copies ran while one was open for 0% of the time, Pallas kernels for 37%

profile of v11, /device:TPU:0, one launch (start us, length us, event | category | flops | bytes accessed | tf_op | source)
XLA Modules:
  0.0 57.0 jit_solution(7498815420034989494)
XLA Ops:
  0.7 2.2 %project.1 = (bf16[256,512]{1,0:T(8,128)(2,1)S(1)}, bf16[256,768]{1,0:T(8,128)(2,1)S(1)}, bf16[2048,768]{1,0:T(8,128)(2,1)S(1)}) custom-call(s32[2,64]{1,0:T(2,128)} %bitcast.3, bf16[256,768]{1,0:T(8,128)(2,1)} %queries.1, bf16[2048,768]{1,0:T(8,128)(2,1)} %embeddings.1), custom_call_target="tpu_custom_call" | custom-call | tf_op jit(solution)/shard_map/project/pallas_call | solution.py:398
  2.9 5.3 %collective-permute-start.4 = (bf16[256,512]{1,0:T(8,128)(2,1)S(1)}, bf16[256,512]{1,0:T(8,128)(2,1)S(1)}, u32[]{:S(2)}, u32[]{:S(2)}) collective-permute-start(bf16[256,512]{1,0:T(8,128)(2,1)S(1)} %get-tuple-element.46), channel_id=1, source_target_pairs={{1,2},{3,4},{5,6},{7,8},{9,10},{11,12},{13,14},{15,0},{2,1},{4,3},... | collective-permute-start | bytes 786440 | tf_op jit(solution)/shard_map/ppermute | solution.py:386
  8.2 1.6 %own.1 = (f32[4,256,512]{2,1,0:T(8,128)S(1)}, bf16[256,512]{1,0:T(8,128)(2,1)S(1)}, bf16[176,512]{1,0:T(8,128)(2,1)S(1)}, bf16[176,512]{1,0:T(8,128)(2,1)S(1)}, bf16[160,512]{1,0:T(8,128)(2,1)S(1)}) custom-call(s32[2,64]{1,0:T(2,128)S(1)} %bitcast.4, bf16[256,768]{1,0:T(8,128)(2,1)S(1)} %get-tuple-element.37.queries, ...), custom_call_target="tpu_custom_call" | custom-call | tf_op jit(solution)/shard_map/own/pallas_call | solution.py:406
  11.1 2.4 %hits.1 = (bf16[4,256,512]{2,1,0:T(8,128)(2,1)S(1)}, bf16[4,2,512,512]{3,2,1,0:T(8,128)(2,1)S(1)}) custom-call(s32[8,256]{1,0:T(8,128)S(1)} %bitcast.18, bf16[4,2,512,512]{3,2,1,0:T(8,128)(2,1)} %tiles.1), custom_call_target="tpu_custom_call" | custom-call | tf_op jit(solution)/shard_map/hits/pallas_call | solution.py:413
  13.6 1.3 %base.1 = f32[4,256,512]{2,1,0:T(8,128)S(1)} custom-call(s32[2,64]{1,0:T(2,128)S(1)} %bitcast.5, f32[4,256,512]{2,1,0:T(8,128)S(1)} %get-tuple-element.39.own, bf16[4,2,512,512]{3,2,1,0:T(8,128)(2,1)S(1)} %get-tuple-element.40.tiles, bf16[176,512]{1,0:T(8,128)(2,1)S(1)} %collective-permute-done.rest_0_, bf16[176,512]{1,0:T(8,128)(2,1)S(1)} %collective-permute-done.1.rest_1_, ...), custom_call_target="tpu_custom_call" | custom-call | tf_op jit(solution)/shard_map/base/pallas_call | solution.py:421
  15.0 1.8 %signal.2 = (bf16[4,256,512]{2,1,0:T(8,128)(2,1)S(1)}, bf16[256,512]{1,0:T(8,128)(2,1)S(1)}) custom-call(s32[2,64]{1,0:T(2,128)S(1)} %bitcast.6, f32[4,256,512]{2,1,0:T(8,128)S(1)} %base.1, bf16[4,256,512]{2,1,0:T(8,128)(2,1)S(1)} %get-tuple-element.44.hits, f32[1,2048]{1,0:T(1,128)S(1)} %bitcast.16, bf16[256,512]{1,0:T(8,128)(2,1)S(1)} %collective-permute-done.4.received, ...), custom_call_target="tpu_custom_call" | custom-call | flops 2000000000 | tf_op jit(solution)/shard_map/signal/pallas_call | solution.py:431
  16.8 3.9 %collective-permute-start.5 = (bf16[256,512]{1,0:T(8,128)(2,1)S(1)}, bf16[256,512]{1,0:T(8,128)(2,1)S(1)}, u32[]{:S(2)}, u32[]{:S(2)}) collective-permute-start(bf16[256,512]{1,0:T(8,128)(2,1)S(1)} %get-tuple-element.49), channel_id=1, source_target_pairs={{1,2},{3,4},{5,6},{7,8},{9,10},{11,12},{13,14},{15,0},{2,1},{4,3},... | collective-permute-start | bytes 786440 | tf_op jit(solution)/shard_map/ppermute | solution.py:386
  20.7 1.8 %signal.3 = (bf16[4,256,512]{2,1,0:T(8,128)(2,1)S(1)}, bf16[256,512]{1,0:T(8,128)(2,1)S(1)}) custom-call(s32[2,64]{1,0:T(2,128)S(1)} %bitcast.7, f32[4,256,512]{2,1,0:T(8,128)S(1)} %base.1, bf16[4,256,512]{2,1,0:T(8,128)(2,1)S(1)} %get-tuple-element.44.hits, f32[1,2048]{1,0:T(1,128)S(1)} %bitcast.17, ...), custom_call_target="tpu_custom_call", output_to_operand_aliasing={{0}: (6, {})} | custom-call | tf_op jit(solution)/shard_map/signal/pallas_call | solution.py:431
  22.4 0.7 %collective-permute-start.9 = (bf16[256,512]{1,0:T(8,128)(2,1)S(1)}, bf16[256,512]{1,0:T(8,128)(2,1)S(1)}, u32[]{:S(2)}, u32[]{:S(2)}) collective-permute-start(bf16[256,512]{1,0:T(8,128)(2,1)S(1)} %get-tuple-element.54), channel_id=1, source_target_pairs={{1,2},{3,4},{5,6},{7,8},{9,10},{11,12},{13,14},{15,0},{2,1},{4,3},... | collective-permute-start | bytes 786440 | tf_op jit(solution)/shard_map/ppermute | solution.py:386
  23.1 1.4 %push.1 = (bf16[176,512]{1,0:T(8,128)(2,1)S(1)}, bf16[176,512]{1,0:T(8,128)(2,1)S(1)}, bf16[160,512]{1,0:T(8,128)(2,1)S(1)}) custom-call(s32[2,64]{1,0:T(2,128)S(1)} %bitcast.8, bf16[4,256,512]{2,1,0:T(8,128)(2,1)S(1)} %get-tuple-element.48.signal, bf16[4,2,512,512]{3,2,1,0:T(8,128)(2,1)S(1)} %get-tuple-element.40.tiles), custom_call_target="tpu_custom_call" | custom-call | tf_op jit(solution)/shard_map/push/pallas_call | solution.py:445
  25.2 1.0 %query.1.part = f32[256,768]{1,0:T(8,128)S(1)} custom-call(bf16[4,256,512]{2,1,0:T(8,128)(2,1)S(1)} %get-tuple-element.48.signal, bf16[2048,768]{1,0:T(8,128)(2,1)S(1)} %get-tuple-element.38.embeddings), custom_call_target="tpu_custom_call" | custom-call | tf_op jit(solution)/shard_map/query/pallas_call | solution.py:455
  26.2 0.9 %query_half.1.part = f32[256,768]{1,0:T(8,128)S(1)} custom-call(s32[2,64]{1,0:T(2,128)S(1)} %bitcast.9, f32[256,768]{1,0:T(8,128)S(1)} %query.1.part, bf16[256,512]{1,0:T(8,128)(2,1)S(1)} %collective-permute-done.5.received.off_a, bf16[2048,768]{1,0:T(8,128)(2,1)S(1)} %get-tuple-element.38.embeddings), custom_call_target="tpu_custom_call" | custom-call | flops 1000000000 | tf_op jit(solution)/shard_map/query_half/pallas_call | solution.py:456
  27.2 1.2 %query_on.1 = (f32[256,768]{1,0:T(8,128)S(1)}, bf16[2,256,512]{2,1,0:T(8,128)(2,1)S(1)}) custom-call(s32[2,64]{1,0:T(2,128)S(1)} %bitcast.10, f32[256,768]{1,0:T(8,128)S(1)} %query_half.1.part, bf16[2048,768]{1,0:T(8,128)(2,1)S(1)} %get-tuple-element.38.embeddings, bf16[176,512]{1,0:T(8,128)(2,1)S(1)} %collective-permute-done.6.rest_0_, ...), custom_call_target="tpu_custom_call" | custom-call | tf_op jit(solution)/shard_map/query_on/pallas_call | solution.py:463
  28.3 2.8 %collective-permute-done.9.off_b.received = bf16[256,512]{1,0:T(8,128)(2,1)S(1)} collective-permute-done((bf16[256,512]{1,0:T(8,128)(2,1)S(1)}, bf16[256,512]{1,0:T(8,128)(2,1)S(1)}, u32[]{:S(2)}, u32[]{:S(2)}) %collective-permute-start.9) | collective-permute-done | bytes 262176 | tf_op jit(solution)/shard_map/ppermute | solution.py:386
  31.1 1.0 %query_end.1 = (f32[128,768]{1,0:T(8,128)S(1)}, bf16[128,768]{1,0:T(8,128)(2,1)S(1)}) custom-call(s32[2,64]{1,0:T(2,128)S(1)} %bitcast.11, f32[256,768]{1,0:T(8,128)S(1)} %get-tuple-element.61.part, bf16[256,512]{1,0:T(8,128)(2,1)S(1)} %collective-permute-done.9.off_b.received, bf16[2048,768]{1,0:T(8,128)(2,1)S(1)} %get-tuple-element.38.embeddings), custom_call_target="tpu_custom_call" | custom-call | tf_op jit(solution)/shard_map/query_end/pallas_call | solution.py:467
  32.1 1.1 %collective-permute-start.10 = (bf16[128,768]{1,0:T(8,128)(2,1)S(1)}, bf16[128,768]{1,0:T(8,128)(2,1)S(1)}, u32[]{:S(2)}, u32[]{:S(2)}) collective-permute-start(bf16[128,768]{1,0:T(8,128)(2,1)S(1)} %get-tuple-element.63), channel_id=1, source_target_pairs={{0,1},{1,0},{2,3},{3,2},{4,5},{5,4},{6,7},{7,6},{8,9},{9,8},{10,11... | collective-permute-start | bytes 589832 | tf_op jit(solution)/shard_map/ppermute | solution.py:263
  33.2 1.1 %collective-permute-done.10.got = bf16[128,768]{1,0:T(8,128)(2,1)S(1)} collective-permute-done((bf16[128,768]{1,0:T(8,128)(2,1)S(1)}, bf16[128,768]{1,0:T(8,128)(2,1)S(1)}, u32[]{:S(2)}, u32[]{:S(2)}) %collective-permute-start.10) | collective-permute-done | bytes 196640 | tf_op jit(solution)/shard_map/ppermute | solution.py:263
  34.9 2.1 %collective-permute-start.11 = (bf16[32,768]{1,0:T(8,128)(2,1)S(1)}, bf16[32,768]{1,0:T(8,128)(2,1)S(1)}, u32[]{:S(2)}, u32[]{:S(2)}) collective-permute-start(bf16[32,768]{1,0:T(8,128)(2,1)S(1)} %get-tuple-element.65), channel_id=1, source_target_pairs={{0,4},{1,5},{2,6},{3,7},{4,0},{5,1},{6,2},{7,3},{8,12},{9,13},{10,... | collective-permute-start | bytes 147464 | tf_op jit(solution)/shard_map/ppermute | solution.py:263
  37.1 1.0 %embed.4 = (bf16[512,768]{1,0:T(8,128)(2,1)S(1)}, f32[8,128]{1,0:T(8,128)S(1)}) custom-call(s32[2,64]{1,0:T(2,128)S(1)} %bitcast.12, bf16[4,256,512]{2,1,0:T(8,128)(2,1)S(1)} %get-tuple-element.48.signal, bf16[2,256,512]{2,1,0:T(8,128)(2,1)S(1)} %get-tuple-element.53.on, bf16[256,512]{1,0:T(8,128)(2,1)S(1)} %collective-permute-done.5.received.off_a, ...), custom_call_target="tpu_custom_call" | custom-call | tf_op jit(solution)/shard_map/embed/pallas_call | solution.py:479
  38.6 1.8 %collective-permute-start.16 = (bf16[32,768]{1,0:T(8,128)(2,1)S(1)}, bf16[32,768]{1,0:T(8,128)(2,1)S(1)}, u32[]{:S(2)}, u32[]{:S(2)}) collective-permute-start(bf16[32,768]{1,0:T(8,128)(2,1)S(1)} %add.9.held), channel_id=1, source_target_pairs={{0,8},{1,9},{2,10},{3,11},{4,12},{5,13},{6,14},{7,15},{8,0},{9,1},... | collective-permute-start | bytes 147464 | tf_op jit(solution)/shard_map/ppermute | solution.py:263
  40.4 1.4 %collective-permute-start.12 = (bf16[32,768]{1,0:T(8,128)(2,1)S(1)}, bf16[32,768]{1,0:T(8,128)(2,1)S(1)}, u32[]{:S(2)}, u32[]{:S(2)}) collective-permute-start(bf16[32,768]{1,0:T(8,128)(2,1)S(1)} %add.6.held), channel_id=1, source_target_pairs={{0,2},{1,3},{2,0},{3,1},{4,6},{5,7},{6,4},{7,5},{8,10},{9,11},{10,... | collective-permute-start | bytes 147464 | tf_op jit(solution)/shard_map/ppermute | solution.py:263
  41.8 1.4 %embed.5 = (bf16[2048,768]{1,0:T(8,128)(2,1)}, bf16[512,768]{1,0:T(8,128)(2,1)S(1)}, f32[8,128]{1,0:T(8,128)S(1)}) custom-call(s32[2,64]{1,0:T(2,128)S(1)} %bitcast.13, bf16[4,256,512]{2,1,0:T(8,128)(2,1)S(1)} %get-tuple-element.48.signal, bf16[2,256,512]{2,1,0:T(8,128)(2,1)S(1)} %get-tuple-element.53.on, ...), custom_call_target="tpu_custom_call" | custom-call | tf_op jit(solution)/shard_map/embed/pallas_call | solution.py:479
  43.2 0.9 %collective-permute-done.16.got = bf16[32,768]{1,0:T(8,128)(2,1)S(1)} collective-permute-done((bf16[32,768]{1,0:T(8,128)(2,1)S(1)}, bf16[32,768]{1,0:T(8,128)(2,1)S(1)}, u32[]{:S(2)}, u32[]{:S(2)}) %collective-permute-start.16) | collective-permute-done | bytes 49184 | tf_op jit(solution)/shard_map/ppermute | solution.py:263
  44.2 0.8 %collective-permute-start.17 = (bf16[32,768]{1,0:T(8,128)(2,1)S(1)}, bf16[32,768]{1,0:T(8,128)(2,1)S(1)}, u32[]{:S(2)}, u32[]{:S(2)}) collective-permute-start(bf16[32,768]{1,0:T(8,128)(2,1)S(1)} %add.10.held), channel_id=1, source_target_pairs={{0,4},{1,5},{2,6},{3,7},{4,0},{5,1},{6,2},{7,3},{8,12},{9,13},{10,... | collective-permute-start | bytes 147464 | tf_op jit(solution)/shard_map/ppermute | solution.py:263
  45.0 1.5 %collective-permute-start.13 = (bf16[32,768]{1,0:T(8,128)(2,1)S(1)}, bf16[32,768]{1,0:T(8,128)(2,1)S(1)}, u32[]{:S(2)}, u32[]{:S(2)}) collective-permute-start(bf16[32,768]{1,0:T(8,128)(2,1)S(1)} %add.7.held), channel_id=1, source_target_pairs={{0,8},{1,9},{2,10},{3,11},{4,12},{5,13},{6,14},{7,15},{8,0},{9,1},... | collective-permute-start | bytes 147464 | tf_op jit(solution)/shard_map/ppermute | solution.py:263
  46.5 1.4 %embed.6 = (bf16[2048,768]{1,0:T(8,128)(2,1)}, bf16[512,768]{1,0:T(8,128)(2,1)S(1)}, f32[8,128]{1,0:T(8,128)S(1)}) custom-call(s32[2,64]{1,0:T(2,128)S(1)} %bitcast.14, bf16[4,256,512]{2,1,0:T(8,128)(2,1)S(1)} %get-tuple-element.48.signal, bf16[2,256,512]{2,1,0:T(8,128)(2,1)S(1)} %get-tuple-element.53.on, ...), custom_call_target="tpu_custom_call", output_to_operand_aliasing={{0}: (7, {})} | custom-call | tf_op jit(solution)/shard_map/embed/pallas_call | solution.py:479
  48.3 2.0 %collective-permute-start.18 = (bf16[32,768]{1,0:T(8,128)(2,1)S(1)}, bf16[32,768]{1,0:T(8,128)(2,1)S(1)}, u32[]{:S(2)}, u32[]{:S(2)}) collective-permute-start(bf16[32,768]{1,0:T(8,128)(2,1)S(1)} %add.11.held), channel_id=1, source_target_pairs={{0,2},{1,3},{2,0},{3,1},{4,6},{5,7},{6,4},{7,5},{8,10},{9,11},{10,... | collective-permute-start | bytes 147464 | tf_op jit(solution)/shard_map/ppermute | solution.py:263
  50.4 1.4 %collective-permute-start.14 = (bf16[32,768]{1,0:T(8,128)(2,1)S(1)}, bf16[32,768]{1,0:T(8,128)(2,1)S(1)}, u32[]{:S(2)}, u32[]{:S(2)}) collective-permute-start(bf16[32,768]{1,0:T(8,128)(2,1)S(1)} %add.8.held), channel_id=1, source_target_pairs={{0,4},{1,5},{2,6},{3,7},{4,0},{5,1},{6,2},{7,3},{8,12},{9,13},{10,... | collective-permute-start | bytes 147464 | tf_op jit(solution)/shard_map/ppermute | solution.py:263
  51.8 2.8 %embed.7 = (bf16[2048,768]{1,0:T(8,128)(2,1)}, bf16[512,768]{1,0:T(8,128)(2,1)}, f32[8,128]{1,0:T(8,128)S(1)}) custom-call(s32[2,64]{1,0:T(2,128)S(1)} %bitcast.15, bf16[4,256,512]{2,1,0:T(8,128)(2,1)S(1)} %get-tuple-element.48.signal, bf16[2,256,512]{2,1,0:T(8,128)(2,1)S(1)} %get-tuple-element.53.on, ...), custom_call_target="tpu_custom_call", output_to_operand_aliasing={{0}: (7, {})} | custom-call | tf_op jit(solution)/shard_map/embed/pallas_call | solution.py:479
  54.8 0.8 %place.2.rest_0_ = f32[256,768]{1,0:T(8,128)} custom-call(bf16[128,768]{1,0:T(8,128)(2,1)S(1)} %join.3.held), custom_call_target="tpu_custom_call" | custom-call | tf_op jit(solution)/shard_map/place/pallas_call | solution.py:363
  55.6 0.6 %collective-permute-done.19.held = bf16[128,768]{1,0:T(8,128)(2,1)S(1)} collective-permute-done((bf16[128,768]{1,0:T(8,128)(2,1)S(1)}, bf16[128,768]{1,0:T(8,128)(2,1)S(1)}, u32[]{:S(2)}, u32[]{:S(2)}) %collective-permute-start.19) | collective-permute-done | bytes 196640 | tf_op jit(solution)/shard_map/ppermute | solution.py:263
  56.3 0.8 %place.3 = f32[256,768]{1,0:T(8,128)} custom-call(bf16[128,768]{1,0:T(8,128)(2,1)S(1)} %collective-permute-done.19.held, f32[256,768]{1,0:T(8,128)} %place.2.rest_0_), custom_call_target="tpu_custom_call", output_to_operand_aliasing={{}: (1, {})} | custom-call | tf_op jit(solution)/shard_map/place/pallas_call | solution.py:363
  (40 shorter events, 3.6 us)
Async XLA Ops:
  0.6 7.6 %copy-start = (s32[64,2]{0,1:T(2,128)S(1)}, s32[64,2]{0,1:T(2,128)}, u32[]{:S(2)}) copy-start(s32[64,2]{0,1:T(2,128)} %param.8) | copy-start | bytes 1540
  0.6 10.5 %copy-start.2 = (s32[256,8]{0,1:T(8,128)S(1)}, s32[256,8]{0,1:T(8,128)}, u32[]{:S(2)}) copy-start(s32[256,8]{0,1:T(8,128)} %param.11) | copy-start | bytes 24580
  2.9 12.1 %collective-permute-start.4 = (bf16[256,512]{1,0:T(8,128)(2,1)S(1)}, bf16[256,512]{1,0:T(8,128)(2,1)S(1)}, u32[]{:S(2)}, u32[]{:S(2)}) collective-permute-start(bf16[256,512]{1,0:T(8,128)(2,1)S(1)} %get-tuple-element.46), channel_id=1, source_target_pairs={{1,2},{3,4},{5,6},{7,8},{9,10},{11,12},{13,14},{15,0},{2,1},{4,3},... | collective-permute-start | bytes 786440 | tf_op jit(solution)/shard_map/ppermute | solution.py:386
  9.9 3.7 %collective-permute-start = (bf16[176,512]{1,0:T(8,128)(2,1)S(1)}, bf16[176,512]{1,0:T(8,128)(2,1)S(1)}, u32[]{:S(2)}, u32[]{:S(2)}) collective-permute-start(bf16[176,512]{1,0:T(8,128)(2,1)S(1)} %get-tuple-element.41), channel_id=1, source_target_pairs={{0,1},{1,0},{2,3},{3,2},{4,5},{5,4},{6,7},{7,6},{8,9},{9,8},{10,11... | collective-permute-start | bytes 540680 | tf_op jit(solution)/shard_map/ppermute | solution.py:263
  9.9 3.7 %collective-permute-start.1 = (bf16[176,512]{1,0:T(8,128)(2,1)S(1)}, bf16[176,512]{1,0:T(8,128)(2,1)S(1)}, u32[]{:S(2)}, u32[]{:S(2)}) collective-permute-start(bf16[176,512]{1,0:T(8,128)(2,1)S(1)} %get-tuple-element.42), channel_id=1, source_target_pairs={{0,1},{1,0},{2,3},{3,2},{4,5},{5,4},{6,7},{7,6},{8,9},{9,8},{10,11... | collective-permute-start | bytes 540680 | tf_op jit(solution)/shard_map/ppermute | solution.py:263
  10.4 3.2 %collective-permute-start.2 = (bf16[160,512]{1,0:T(8,128)(2,1)S(1)}, bf16[160,512]{1,0:T(8,128)(2,1)S(1)}, u32[]{:S(2)}, u32[]{:S(2)}) collective-permute-start(bf16[160,512]{1,0:T(8,128)(2,1)S(1)} %get-tuple-element.43), channel_id=1, source_target_pairs={{0,1},{1,0},{2,3},{3,2},{4,5},{5,4},{6,7},{7,6},{8,9},{9,8},{10,11... | collective-permute-start | bytes 491528 | tf_op jit(solution)/shard_map/ppermute | solution.py:263
  10.5 10.2 %collective-permute-start.3 = (bf16[256,512]{1,0:T(8,128)(2,1)S(1)}, bf16[256,512]{1,0:T(8,128)(2,1)S(1)}, u32[]{:S(2)}, u32[]{:S(2)}) collective-permute-start(bf16[256,512]{1,0:T(8,128)(2,1)S(1)} %get-tuple-element.45), channel_id=1, source_target_pairs={{1,2},{3,4},{5,6},{7,8},{9,10},{11,12},{13,14},{15,0},{2,1},{4,3},... | collective-permute-start | bytes 786440 | tf_op jit(solution)/shard_map/ppermute | solution.py:386
  13.6 1.4 %copy-start.1 = (f32[2048]{0:T(1024)S(1)}, f32[2048]{0:T(1024)}, u32[]{:S(2)}) copy-start(f32[2048]{0:T(1024)} %param.9) | copy-start | bytes 24580
  16.8 9.4 %collective-permute-start.5 = (bf16[256,512]{1,0:T(8,128)(2,1)S(1)}, bf16[256,512]{1,0:T(8,128)(2,1)S(1)}, u32[]{:S(2)}, u32[]{:S(2)}) collective-permute-start(bf16[256,512]{1,0:T(8,128)(2,1)S(1)} %get-tuple-element.49), channel_id=1, source_target_pairs={{1,2},{3,4},{5,6},{7,8},{9,10},{11,12},{13,14},{15,0},{2,1},{4,3},... | collective-permute-start | bytes 786440 | tf_op jit(solution)/shard_map/ppermute | solution.py:386
  22.4 8.7 %collective-permute-start.9 = (bf16[256,512]{1,0:T(8,128)(2,1)S(1)}, bf16[256,512]{1,0:T(8,128)(2,1)S(1)}, u32[]{:S(2)}, u32[]{:S(2)}) collective-permute-start(bf16[256,512]{1,0:T(8,128)(2,1)S(1)} %get-tuple-element.54), channel_id=1, source_target_pairs={{1,2},{3,4},{5,6},{7,8},{9,10},{11,12},{13,14},{15,0},{2,1},{4,3},... | collective-permute-start | bytes 786440 | tf_op jit(solution)/shard_map/ppermute | solution.py:386
  24.5 2.6 %collective-permute-start.6 = (bf16[176,512]{1,0:T(8,128)(2,1)S(1)}, bf16[176,512]{1,0:T(8,128)(2,1)S(1)}, u32[]{:S(2)}, u32[]{:S(2)}) collective-permute-start(bf16[176,512]{1,0:T(8,128)(2,1)S(1)} %get-tuple-element.50), channel_id=1, source_target_pairs={{0,1},{1,0},{2,3},{3,2},{4,5},{5,4},{6,7},{7,6},{8,9},{9,8},{10,11... | collective-permute-start | bytes 540680 | tf_op jit(solution)/shard_map/ppermute | solution.py:263
  24.6 2.6 %collective-permute-start.7 = (bf16[176,512]{1,0:T(8,128)(2,1)S(1)}, bf16[176,512]{1,0:T(8,128)(2,1)S(1)}, u32[]{:S(2)}, u32[]{:S(2)}) collective-permute-start(bf16[176,512]{1,0:T(8,128)(2,1)S(1)} %get-tuple-element.51), channel_id=1, source_target_pairs={{0,1},{1,0},{2,3},{3,2},{4,5},{5,4},{6,7},{7,6},{8,9},{9,8},{10,11... | collective-permute-start | bytes 540680 | tf_op jit(solution)/shard_map/ppermute | solution.py:263
  25.1 2.0 %collective-permute-start.8 = (bf16[160,512]{1,0:T(8,128)(2,1)S(1)}, bf16[160,512]{1,0:T(8,128)(2,1)S(1)}, u32[]{:S(2)}, u32[]{:S(2)}) collective-permute-start(bf16[160,512]{1,0:T(8,128)(2,1)S(1)} %get-tuple-element.52), channel_id=1, source_target_pairs={{0,1},{1,0},{2,3},{3,2},{4,5},{5,4},{6,7},{7,6},{8,9},{9,8},{10,11... | collective-permute-start | bytes 491528 | tf_op jit(solution)/shard_map/ppermute | solution.py:263
  32.1 2.2 %collective-permute-start.10 = (bf16[128,768]{1,0:T(8,128)(2,1)S(1)}, bf16[128,768]{1,0:T(8,128)(2,1)S(1)}, u32[]{:S(2)}, u32[]{:S(2)}) collective-permute-start(bf16[128,768]{1,0:T(8,128)(2,1)S(1)} %get-tuple-element.63), channel_id=1, source_target_pairs={{0,1},{1,0},{2,3},{3,2},{4,5},{5,4},{6,7},{7,6},{8,9},{9,8},{10,11... | collective-permute-start | bytes 589832 | tf_op jit(solution)/shard_map/ppermute | solution.py:263
  34.4 4.2 %collective-permute-start.15 = (bf16[32,768]{1,0:T(8,128)(2,1)S(1)}, bf16[32,768]{1,0:T(8,128)(2,1)S(1)}, u32[]{:S(2)}, u32[]{:S(2)}) collective-permute-start(bf16[32,768]{1,0:T(8,128)(2,1)S(1)} %get-tuple-element.67), channel_id=1, source_target_pairs={{0,2},{1,3},{2,0},{3,1},{4,6},{5,7},{6,4},{7,5},{8,10},{9,11},{10,... | collective-permute-start | bytes 147464 | tf_op jit(solution)/shard_map/ppermute | solution.py:263
  34.9 5.4 %collective-permute-start.11 = (bf16[32,768]{1,0:T(8,128)(2,1)S(1)}, bf16[32,768]{1,0:T(8,128)(2,1)S(1)}, u32[]{:S(2)}, u32[]{:S(2)}) collective-permute-start(bf16[32,768]{1,0:T(8,128)(2,1)S(1)} %get-tuple-element.65), channel_id=1, source_target_pairs={{0,4},{1,5},{2,6},{3,7},{4,0},{5,1},{6,2},{7,3},{8,12},{9,13},{10,... | collective-permute-start | bytes 147464 | tf_op jit(solution)/shard_map/ppermute | solution.py:263
  38.6 5.6 %collective-permute-start.16 = (bf16[32,768]{1,0:T(8,128)(2,1)S(1)}, bf16[32,768]{1,0:T(8,128)(2,1)S(1)}, u32[]{:S(2)}, u32[]{:S(2)}) collective-permute-start(bf16[32,768]{1,0:T(8,128)(2,1)S(1)} %add.9.held), channel_id=1, source_target_pairs={{0,8},{1,9},{2,10},{3,11},{4,12},{5,13},{6,14},{7,15},{8,0},{9,1},... | collective-permute-start | bytes 147464 | tf_op jit(solution)/shard_map/ppermute | solution.py:263
  40.4 4.6 %collective-permute-start.12 = (bf16[32,768]{1,0:T(8,128)(2,1)S(1)}, bf16[32,768]{1,0:T(8,128)(2,1)S(1)}, u32[]{:S(2)}, u32[]{:S(2)}) collective-permute-start(bf16[32,768]{1,0:T(8,128)(2,1)S(1)} %add.6.held), channel_id=1, source_target_pairs={{0,2},{1,3},{2,0},{3,1},{4,6},{5,7},{6,4},{7,5},{8,10},{9,11},{10,... | collective-permute-start | bytes 147464 | tf_op jit(solution)/shard_map/ppermute | solution.py:263
  44.2 4.2 %collective-permute-start.17 = (bf16[32,768]{1,0:T(8,128)(2,1)S(1)}, bf16[32,768]{1,0:T(8,128)(2,1)S(1)}, u32[]{:S(2)}, u32[]{:S(2)}) collective-permute-start(bf16[32,768]{1,0:T(8,128)(2,1)S(1)} %add.10.held), channel_id=1, source_target_pairs={{0,4},{1,5},{2,6},{3,7},{4,0},{5,1},{6,2},{7,3},{8,12},{9,13},{10,... | collective-permute-start | bytes 147464 | tf_op jit(solution)/shard_map/ppermute | solution.py:263
  45.0 5.4 %collective-permute-start.13 = (bf16[32,768]{1,0:T(8,128)(2,1)S(1)}, bf16[32,768]{1,0:T(8,128)(2,1)S(1)}, u32[]{:S(2)}, u32[]{:S(2)}) collective-permute-start(bf16[32,768]{1,0:T(8,128)(2,1)S(1)} %add.7.held), channel_id=1, source_target_pairs={{0,8},{1,9},{2,10},{3,11},{4,12},{5,13},{6,14},{7,15},{8,0},{9,1},... | collective-permute-start | bytes 147464 | tf_op jit(solution)/shard_map/ppermute | solution.py:263
  48.3 6.3 %collective-permute-start.18 = (bf16[32,768]{1,0:T(8,128)(2,1)S(1)}, bf16[32,768]{1,0:T(8,128)(2,1)S(1)}, u32[]{:S(2)}, u32[]{:S(2)}) collective-permute-start(bf16[32,768]{1,0:T(8,128)(2,1)S(1)} %add.11.held), channel_id=1, source_target_pairs={{0,2},{1,3},{2,0},{3,1},{4,6},{5,7},{6,4},{7,5},{8,10},{9,11},{10,... | collective-permute-start | bytes 147464 | tf_op jit(solution)/shard_map/ppermute | solution.py:263
  50.4 4.3 %collective-permute-start.14 = (bf16[32,768]{1,0:T(8,128)(2,1)S(1)}, bf16[32,768]{1,0:T(8,128)(2,1)S(1)}, u32[]{:S(2)}, u32[]{:S(2)}) collective-permute-start(bf16[32,768]{1,0:T(8,128)(2,1)S(1)} %add.8.held), channel_id=1, source_target_pairs={{0,4},{1,5},{2,6},{3,7},{4,0},{5,1},{6,2},{7,3},{8,12},{9,13},{10,... | collective-permute-start | bytes 147464 | tf_op jit(solution)/shard_map/ppermute | solution.py:263
  54.8 1.5 %collective-permute-start.19 = (bf16[128,768]{1,0:T(8,128)(2,1)S(1)}, bf16[128,768]{1,0:T(8,128)(2,1)S(1)}, u32[]{:S(2)}, u32[]{:S(2)}) collective-permute-start(bf16[128,768]{1,0:T(8,128)(2,1)S(1)} %join.3.held), channel_id=1, source_target_pairs={{0,1},{1,0},{2,3},{3,2},{4,5},{5,4},{6,7},{7,6},{8,9},{9,8},{10,11... | collective-permute-start | bytes 589832 | tf_op jit(solution)/shard_map/ppermute | solution.py:263

commit v12 on v11

--- a/solution.py
+++ b/solution.py
@@ -196,13 +196,14 @@
     )
 
 
-def query_end_kernel(lists, part, received, embeddings, kept, sent, total, *, blocks):
+def query_end_kernel(lists, part, received, embeddings, out, *, blocks, own):
     _, second = named_by_partner(lists, blocks, OFF)
-    total[...] = part[...] + dot(received[...], block_rows(embeddings, second, received.shape[1]), NN)
-    rows = kept.shape[0]
+    rows = out.shape[0]
     core = lax.axis_index(AXIS) % 2
-    kept[...] = total[pl.ds(pl.multiple_of(core * rows, rows), rows), :]
-    sent[...] = total[pl.ds(pl.multiple_of((1 - core) * rows, rows), rows), :].astype(BF16)
+    half = core if own else 1 - core
+    place = pl.ds(pl.multiple_of(half * rows, rows), rows)
+    right = block_rows(embeddings, second, received.shape[1])
+    out[...] = (part[place, :] + dot(received[place, :], right, NN)).astype(out.dtype)
 
 
 def embed_kernel(lists, signal, on, off_a, off_b, queries, *rest, blocks, g, scale):
@@ -290,23 +291,24 @@
 def join_kernel(held, got, *rest, bit):
     out = rest[-1]
     rows = held.shape[0]
-    begin = out.shape[0] - 2 * rows
-    if begin:
-        out[:begin, :] = rest[0][...]
     digit = digit_of(bit)
-    out[pl.ds(pl.multiple_of(begin + digit * rows, rows), rows), :] = held[...]
-    out[pl.ds(pl.multiple_of(begin + (1 - digit) * rows, rows), rows), :] = got[...]
-
-
-def place_kernel(held, *rest, own):
-    out, wide, sem = rest[-3:]
-    rows = held.shape[0]
+    out[pl.ds(pl.multiple_of(digit * rows, rows), rows), :] = held[...]
+    out[pl.ds(pl.multiple_of((1 - digit) * rows, rows), rows), :] = got[...]
+
+
+def place_kernel(*refs, places):
+    out, wide, sem = refs[-3:]
+    rows = refs[0].shape[0]
     core = lax.axis_index(AXIS) % 2
-    half = core if own else 1 - core
-    wide[...] = held[...].astype(F32)
-    copy = pltpu.make_async_copy(wide, out.at[pl.ds(pl.multiple_of(half * rows, rows), rows), :], sem)
-    copy.start()
-    copy.wait()
+    copies = []
+    for k, (chain, own) in enumerate(places):
+        wide[k] = refs[k][...].astype(F32)
+        half = core if own else 1 - core
+        begin = pl.multiple_of((2 * half + chain) * rows, rows)
+        copies.append(pltpu.make_async_copy(wide.at[k], out.at[pl.ds(begin, rows), :], sem.at[k]))
+        copies[-1].start()
+    for copy in copies:
+        copy.wait()
 
 
 def sum_queries(kept, sent, beside, scale):
@@ -343,34 +345,36 @@
             )(held[chain], got[chain], *after)
         sent = list(held)
     got = [exchange(piece, bit) for piece, bit in zip(held, ends)]
-    joined = []
+    joined, swapped = [], []
     for chain, bit in enumerate(ends):
-        rows_out = (chain + 1) * rows // 2
-        after = beside[len(bits) :] if chain == 0 else []
-        joined = [
+        after = beside[len(bits) :] if chain == 0 else joined
+        joined.append(
             call(
                 functools.partial(join_kernel, bit=bit),
                 "join",
-                [VMEM] * (2 + len(joined)) + [ANY] * len(after),
-                in_vmem((rows_out, width), BF16),
+                [VMEM] * 2 + [ANY] * len(after),
+                in_vmem((rows // 2, width), BF16),
                 flops=2 * 10**8,
-            )(held[chain], got[chain], *joined, *after)
-        ]
-    held = joined[0]
-    got = exchange(held, 1)
-
-    def place(half, own, *begun):
+            )(held[chain], got[chain], *after)
+        )
+        swapped.append(exchange(joined[chain], 1))
+
+    def place(values, places, *begun):
         return call(
-            functools.partial(place_kernel, own=own),
+            functools.partial(place_kernel, places=places),
             "place",
-            [VMEM] + [ANY] * len(begun),
+            [VMEM] * len(values) + [ANY] * len(begun),
             jax.ShapeDtypeStruct((2 * rows, width), F32),
             out_specs=ANY,
-            scratch=[pltpu.VMEM((rows, width), F32), pltpu.SemaphoreType.DMA],
-            aliases={1: 0} if begun else None,
-        )(half, *begun)
-
-    return place(got, False, place(held, True))
+            scratch=[
+                pltpu.VMEM((len(values), rows // 2, width), F32),
+                pltpu.SemaphoreType.DMA((len(values),)),
+            ],
+            aliases={len(values): 0} if begun else None,
+        )(*values, *begun)
+
+    early = place([joined[0], joined[1], swapped[0]], [(0, True), (1, True), (0, False)])
+    return place([swapped[1]], [(1, False)], early)
 
 
 def per_device(embeddings, edge_tiles, neighbour, propensity, queries, positives):
@@ -463,15 +467,15 @@
     part, on = call(
         functools.partial(query_on_kernel, blocks=blocks), "query_on", [SMEM] + [VMEM] * 5, [whole, pair]
     )(lists, part, embeddings, *back_on)
-    kept, sent = (in_vmem((rows // 2, width), kind) for kind in (F32, BF16))
-    kept, sent = call(
-        functools.partial(query_end_kernel, blocks=blocks),
-        "query_end",
-        [SMEM] + [VMEM] * 3,
-        [kept, sent],
-        scratch=[pltpu.VMEM((rows, width), F32)],
-    )(lists, part, back_b, embeddings)
-
+    def query_end(own, kind):
+        return call(
+            functools.partial(query_end_kernel, blocks=blocks, own=own),
+            "query_end",
+            [SMEM] + [VMEM] * 3,
+            in_vmem((rows // 2, width), kind),
+        )(lists, part, back_b, embeddings)
+
+    sent, kept = query_end(False, BF16), query_end(True, F32)
     ready = in_vmem((block, width), BF16)
     written = jax.ShapeDtypeStruct((labels_dev, width), BF16)
     outs, tokens = [], []

time: 57.3 us -> 56.9 us (level)
  starting transfers between devices: 24.6 us -> 23.2 us
  waiting for transfers between devices: 6.32 us -> 7.03 us
    ppermute x16 -> x17, starting transfers between devices: 14.1 us -> 12.5 us  [exchange(): return lax.ppermute(value, AXIS, [(i, i ^ mask) for i in range(count)])]
    pallas_call x5 -> x6, Pallas kernels: 2.63 us -> 3.28 us  [the longest x2 1.7 us: query_end(): call(functools.partial(query_end_kernel, blocks=blocks, own=own), 'query_...]
    ppermute x4, waiting for transfers between devices: 2.78 us -> 3.38 us  [off_swap(): return lax.ppermute(value, AXIS, off_route)]
    ppermute x16 -> x17, waiting for transfers between devices: 3.54 us -> 3.66 us  [exchange(): return lax.ppermute(value, AXIS, [(i, i ^ mask) for i in range(count)])]
  transfers between devices with their start and end apart: 20 -> 21, of which waited for: 6 -> 8; matrix products, arithmetic and copies ran while one was open for 0% -> 0% of each run, Pallas kernels for 37% -> 39%
where the time goes in v12:
time: 56.9 us
  Pallas kernels  25.7 us (45%)
  starting transfers between devices  23.2 us (41%)
  waiting for transfers between devices  7.03 us (12%)
  between operations  0.96 us (2%)
    ppermute x17, starting transfers between devices, exchange(): return lax.ppermute(value, AXIS, [(i, i ^ mask) for i in range(count)])  12.5 us
    ppermute x4, starting transfers between devices, off_swap(): return lax.ppermute(value, AXIS, off_route)  10.7 us
    pallas_call x4, Pallas kernels, per_device(): call(functools.partial(embed_kernel, blocks=blocks, g=g, scale=1.0 / math...  6.74 us
    ppermute x17, waiting for transfers between devices, exchange(): return lax.ppermute(value, AXIS, [(i, i ^ mask) for i in range(count)])  3.66 us
    pallas_call x2, Pallas kernels, signal_of(): call(functools.partial(signal_kernel, slot=slot), 'signal', [SMEM] + [VME...  3.54 us
    ppermute x4, waiting for transfers between devices, off_swap(): return lax.ppermute(value, AXIS, off_route)  3.38 us
    pallas_call x1, Pallas kernels, per_device(): call(hits_kernel, 'hits', [VMEM, HBM], [in_vmem(full, BF16), in_vmem(edge...  2.45 us
    pallas_call x1, Pallas kernels, per_device(): call(functools.partial(project_kernel, scale=scale), 'project', [HBM] * 3...  2.03 us
  transfers between devices with their start and end apart: 21, of which 8 were waited for; matrix products, arithmetic and copies ran while one was open for 0% of the time, Pallas kernels for 39%

profile of v12, /device:TPU:0, one launch (start us, length us, event | category | flops | bytes accessed | tf_op | source)
XLA Modules:
  0.0 56.9 jit_solution(12768658272369670925)
XLA Ops:
  0.7 2.0 %project.1 = (bf16[256,512]{1,0:T(8,128)(2,1)S(1)}, bf16[256,768]{1,0:T(8,128)(2,1)S(1)}, bf16[2048,768]{1,0:T(8,128)(2,1)S(1)}) custom-call(s32[2,64]{1,0:T(2,128)} %bitcast.3, bf16[256,768]{1,0:T(8,128)(2,1)} %queries.1, bf16[2048,768]{1,0:T(8,128)(2,1)} %embeddings.1), custom_call_target="tpu_custom_call" | custom-call | tf_op jit(solution)/shard_map/project/pallas_call | solution.py:402
  2.7 5.5 %collective-permute-start.4 = (bf16[256,512]{1,0:T(8,128)(2,1)S(1)}, bf16[256,512]{1,0:T(8,128)(2,1)S(1)}, u32[]{:S(2)}, u32[]{:S(2)}) collective-permute-start(bf16[256,512]{1,0:T(8,128)(2,1)S(1)} %get-tuple-element.44), channel_id=1, source_target_pairs={{1,2},{3,4},{5,6},{7,8},{9,10},{11,12},{13,14},{15,0},{2,1},{4,3},... | collective-permute-start | bytes 786440 | tf_op jit(solution)/shard_map/ppermute | solution.py:390
  8.2 1.6 %own.1 = (f32[4,256,512]{2,1,0:T(8,128)S(1)}, bf16[256,512]{1,0:T(8,128)(2,1)S(1)}, bf16[176,512]{1,0:T(8,128)(2,1)S(1)}, bf16[176,512]{1,0:T(8,128)(2,1)S(1)}, bf16[160,512]{1,0:T(8,128)(2,1)S(1)}) custom-call(s32[2,64]{1,0:T(2,128)S(1)} %bitcast.4, bf16[256,768]{1,0:T(8,128)(2,1)S(1)} %get-tuple-element.35.queries, ...), custom_call_target="tpu_custom_call" | custom-call | tf_op jit(solution)/shard_map/own/pallas_call | solution.py:410
  11.1 2.4 %hits.1 = (bf16[4,256,512]{2,1,0:T(8,128)(2,1)S(1)}, bf16[4,2,512,512]{3,2,1,0:T(8,128)(2,1)S(1)}) custom-call(s32[8,256]{1,0:T(8,128)S(1)} %bitcast.19, bf16[4,2,512,512]{3,2,1,0:T(8,128)(2,1)} %tiles.1), custom_call_target="tpu_custom_call" | custom-call | tf_op jit(solution)/shard_map/hits/pallas_call | solution.py:417
  13.6 1.3 %base.1 = f32[4,256,512]{2,1,0:T(8,128)S(1)} custom-call(s32[2,64]{1,0:T(2,128)S(1)} %bitcast.5, f32[4,256,512]{2,1,0:T(8,128)S(1)} %get-tuple-element.37.own, bf16[4,2,512,512]{3,2,1,0:T(8,128)(2,1)S(1)} %get-tuple-element.38.tiles, bf16[176,512]{1,0:T(8,128)(2,1)S(1)} %collective-permute-done.rest_0_, bf16[176,512]{1,0:T(8,128)(2,1)S(1)} %collective-permute-done.1.rest_1_, ...), custom_call_target="tpu_custom_call" | custom-call | tf_op jit(solution)/shard_map/base/pallas_call | solution.py:425
  15.0 1.2 %signal.2 = (bf16[4,256,512]{2,1,0:T(8,128)(2,1)S(1)}, bf16[256,512]{1,0:T(8,128)(2,1)S(1)}) custom-call(s32[2,64]{1,0:T(2,128)S(1)} %bitcast.6, f32[4,256,512]{2,1,0:T(8,128)S(1)} %base.1, bf16[4,256,512]{2,1,0:T(8,128)(2,1)S(1)} %get-tuple-element.42.hits, f32[1,2048]{1,0:T(1,128)S(1)} %bitcast.17, bf16[256,512]{1,0:T(8,128)(2,1)S(1)} %collective-permute-done.4.received, ...), custom_call_target="tpu_custom_call" | custom-call | flops 2000000000 | tf_op jit(solution)/shard_map/signal/pallas_call | solution.py:435
  16.2 4.5 %collective-permute-start.5 = (bf16[256,512]{1,0:T(8,128)(2,1)S(1)}, bf16[256,512]{1,0:T(8,128)(2,1)S(1)}, u32[]{:S(2)}, u32[]{:S(2)}) collective-permute-start(bf16[256,512]{1,0:T(8,128)(2,1)S(1)} %get-tuple-element.47), channel_id=1, source_target_pairs={{1,2},{3,4},{5,6},{7,8},{9,10},{11,12},{13,14},{15,0},{2,1},{4,3},... | collective-permute-start | bytes 786440 | tf_op jit(solution)/shard_map/ppermute | solution.py:390
  20.7 2.3 %signal.3 = (bf16[4,256,512]{2,1,0:T(8,128)(2,1)S(1)}, bf16[256,512]{1,0:T(8,128)(2,1)S(1)}) custom-call(s32[2,64]{1,0:T(2,128)S(1)} %bitcast.7, f32[4,256,512]{2,1,0:T(8,128)S(1)} %base.1, bf16[4,256,512]{2,1,0:T(8,128)(2,1)S(1)} %get-tuple-element.42.hits, f32[1,2048]{1,0:T(1,128)S(1)} %bitcast.18, ...), custom_call_target="tpu_custom_call", output_to_operand_aliasing={{0}: (6, {})} | custom-call | tf_op jit(solution)/shard_map/signal/pallas_call | solution.py:435
  23.1 1.4 %push.1 = (bf16[176,512]{1,0:T(8,128)(2,1)S(1)}, bf16[176,512]{1,0:T(8,128)(2,1)S(1)}, bf16[160,512]{1,0:T(8,128)(2,1)S(1)}) custom-call(s32[2,64]{1,0:T(2,128)S(1)} %bitcast.8, bf16[4,256,512]{2,1,0:T(8,128)(2,1)S(1)} %get-tuple-element.46.signal, bf16[4,2,512,512]{3,2,1,0:T(8,128)(2,1)S(1)} %get-tuple-element.38.tiles), custom_call_target="tpu_custom_call" | custom-call | tf_op jit(solution)/shard_map/push/pallas_call | solution.py:449
  25.2 1.0 %query.1.part = f32[256,768]{1,0:T(8,128)S(1)} custom-call(bf16[4,256,512]{2,1,0:T(8,128)(2,1)S(1)} %get-tuple-element.46.signal, bf16[2048,768]{1,0:T(8,128)(2,1)S(1)} %get-tuple-element.36.embeddings), custom_call_target="tpu_custom_call" | custom-call | tf_op jit(solution)/shard_map/query/pallas_call | solution.py:459
  26.2 1.0 %query_half.1.part = f32[256,768]{1,0:T(8,128)S(1)} custom-call(s32[2,64]{1,0:T(2,128)S(1)} %bitcast.9, f32[256,768]{1,0:T(8,128)S(1)} %query.1.part, bf16[256,512]{1,0:T(8,128)(2,1)S(1)} %collective-permute-done.5.received.off_a, bf16[2048,768]{1,0:T(8,128)(2,1)S(1)} %get-tuple-element.36.embeddings), custom_call_target="tpu_custom_call" | custom-call | flops 1000000000 | tf_op jit(solution)/shard_map/query_half/pallas_call | solution.py:460
  27.2 1.2 %query_on.1 = (f32[256,768]{1,0:T(8,128)S(1)}, bf16[2,256,512]{2,1,0:T(8,128)(2,1)S(1)}) custom-call(s32[2,64]{1,0:T(2,128)S(1)} %bitcast.10, f32[256,768]{1,0:T(8,128)S(1)} %query_half.1.part, bf16[2048,768]{1,0:T(8,128)(2,1)S(1)} %get-tuple-element.36.embeddings, bf16[176,512]{1,0:T(8,128)(2,1)S(1)} %collective-permute-done.6.rest_0_, ...), custom_call_target="tpu_custom_call" | custom-call | tf_op jit(solution)/shard_map/query_on/pallas_call | solution.py:467
  28.3 3.4 %collective-permute-done.9.off_b.received = bf16[256,512]{1,0:T(8,128)(2,1)S(1)} collective-permute-done((bf16[256,512]{1,0:T(8,128)(2,1)S(1)}, bf16[256,512]{1,0:T(8,128)(2,1)S(1)}, u32[]{:S(2)}, u32[]{:S(2)}) %collective-permute-start.9) | collective-permute-done | bytes 262176 | tf_op jit(solution)/shard_map/ppermute | solution.py:390
  31.7 0.8 %query_end.3 = bf16[128,768]{1,0:T(8,128)(2,1)S(1)} custom-call(s32[2,64]{1,0:T(2,128)S(1)} %bitcast.11, f32[256,768]{1,0:T(8,128)S(1)} %get-tuple-element.59.part, bf16[256,512]{1,0:T(8,128)(2,1)S(1)} %collective-permute-done.9.off_b.received, bf16[2048,768]{1,0:T(8,128)(2,1)S(1)} %get-tuple-element.36.embeddings), custom_call_target="tpu_custom_call" | custom-call | tf_op jit(solution)/shard_map/query_end/pallas_call | solution.py:471
  32.5 0.7 %collective-permute-start.10 = (bf16[128,768]{1,0:T(8,128)(2,1)S(1)}, bf16[128,768]{1,0:T(8,128)(2,1)S(1)}, u32[]{:S(2)}, u32[]{:S(2)}) collective-permute-start(bf16[128,768]{1,0:T(8,128)(2,1)S(1)} %query_end.3), channel_id=1, source_target_pairs={{0,1},{1,0},{2,3},{3,2},{4,5},{5,4},{6,7},{7,6},{8,9},{9,8},{10,11... | collective-permute-start | bytes 589832 | tf_op jit(solution)/shard_map/ppermute | solution.py:264
  33.2 0.8 %query_end.2.held = f32[128,768]{1,0:T(8,128)S(1)} custom-call(s32[2,64]{1,0:T(2,128)S(1)} %bitcast.12, f32[256,768]{1,0:T(8,128)S(1)} %get-tuple-element.59.part, bf16[256,512]{1,0:T(8,128)(2,1)S(1)} %collective-permute-done.9.off_b.received, bf16[2048,768]{1,0:T(8,128)(2,1)S(1)} %get-tuple-element.36.embeddings), custom_call_target="tpu_custom_call" | custom-call | tf_op jit(solution)/shard_map/query_end/pallas_call | solution.py:471
  34.4 0.9 %collective-permute-start.15 = (bf16[32,768]{1,0:T(8,128)(2,1)S(1)}, bf16[32,768]{1,0:T(8,128)(2,1)S(1)}, u32[]{:S(2)}, u32[]{:S(2)}) collective-permute-start(bf16[32,768]{1,0:T(8,128)(2,1)S(1)} %get-tuple-element.63), channel_id=1, source_target_pairs={{0,2},{1,3},{2,0},{3,1},{4,6},{5,7},{6,4},{7,5},{8,10},{9,11},{10,... | collective-permute-start | bytes 147464 | tf_op jit(solution)/shard_map/ppermute | solution.py:264
  35.3 1.0 %collective-permute-start.11 = (bf16[32,768]{1,0:T(8,128)(2,1)S(1)}, bf16[32,768]{1,0:T(8,128)(2,1)S(1)}, u32[]{:S(2)}, u32[]{:S(2)}) collective-permute-start(bf16[32,768]{1,0:T(8,128)(2,1)S(1)} %get-tuple-element.61), channel_id=1, source_target_pairs={{0,4},{1,5},{2,6},{3,7},{4,0},{5,1},{6,2},{7,3},{8,12},{9,13},{10,... | collective-permute-start | bytes 147464 | tf_op jit(solution)/shard_map/ppermute | solution.py:264
  36.3 1.0 %embed.4 = (bf16[512,768]{1,0:T(8,128)(2,1)S(1)}, f32[8,128]{1,0:T(8,128)S(1)}) custom-call(s32[2,64]{1,0:T(2,128)S(1)} %bitcast.13, bf16[4,256,512]{2,1,0:T(8,128)(2,1)S(1)} %get-tuple-element.46.signal, bf16[2,256,512]{2,1,0:T(8,128)(2,1)S(1)} %get-tuple-element.51.on, bf16[256,512]{1,0:T(8,128)(2,1)S(1)} %collective-permute-done.5.received.off_a, ...), custom_call_target="tpu_custom_call" | custom-call | tf_op jit(solution)/shard_map/embed/pallas_call | solution.py:483
  37.3 1.2 %collective-permute-done.15.got = bf16[32,768]{1,0:T(8,128)(2,1)S(1)} collective-permute-done((bf16[32,768]{1,0:T(8,128)(2,1)S(1)}, bf16[32,768]{1,0:T(8,128)(2,1)S(1)}, u32[]{:S(2)}, u32[]{:S(2)}) %collective-permute-start.15) | collective-permute-done | bytes 49184 | tf_op jit(solution)/shard_map/ppermute | solution.py:264
  38.6 1.6 %collective-permute-start.16 = (bf16[32,768]{1,0:T(8,128)(2,1)S(1)}, bf16[32,768]{1,0:T(8,128)(2,1)S(1)}, u32[]{:S(2)}, u32[]{:S(2)}) collective-permute-start(bf16[32,768]{1,0:T(8,128)(2,1)S(1)} %add.9.held), channel_id=1, source_target_pairs={{0,8},{1,9},{2,10},{3,11},{4,12},{5,13},{6,14},{7,15},{8,0},{9,1},... | collective-permute-start | bytes 147464 | tf_op jit(solution)/shard_map/ppermute | solution.py:264
  40.2 1.4 %collective-permute-start.12 = (bf16[32,768]{1,0:T(8,128)(2,1)S(1)}, bf16[32,768]{1,0:T(8,128)(2,1)S(1)}, u32[]{:S(2)}, u32[]{:S(2)}) collective-permute-start(bf16[32,768]{1,0:T(8,128)(2,1)S(1)} %add.6.held), channel_id=1, source_target_pairs={{0,2},{1,3},{2,0},{3,1},{4,6},{5,7},{6,4},{7,5},{8,10},{9,11},{10,... | collective-permute-start | bytes 147464 | tf_op jit(solution)/shard_map/ppermute | solution.py:264
  41.6 1.4 %embed.5 = (bf16[2048,768]{1,0:T(8,128)(2,1)}, bf16[512,768]{1,0:T(8,128)(2,1)S(1)}, f32[8,128]{1,0:T(8,128)S(1)}) custom-call(s32[2,64]{1,0:T(2,128)S(1)} %bitcast.14, bf16[4,256,512]{2,1,0:T(8,128)(2,1)S(1)} %get-tuple-element.46.signal, bf16[2,256,512]{2,1,0:T(8,128)(2,1)S(1)} %get-tuple-element.51.on, ...), custom_call_target="tpu_custom_call" | custom-call | tf_op jit(solution)/shard_map/embed/pallas_call | solution.py:483
  43.7 1.1 %collective-permute-start.17 = (bf16[32,768]{1,0:T(8,128)(2,1)S(1)}, bf16[32,768]{1,0:T(8,128)(2,1)S(1)}, u32[]{:S(2)}, u32[]{:S(2)}) collective-permute-start(bf16[32,768]{1,0:T(8,128)(2,1)S(1)} %add.10.held), channel_id=1, source_target_pairs={{0,4},{1,5},{2,6},{3,7},{4,0},{5,1},{6,2},{7,3},{8,12},{9,13},{10,... | collective-permute-start | bytes 147464 | tf_op jit(solution)/shard_map/ppermute | solution.py:264
  44.8 1.5 %collective-permute-start.13 = (bf16[32,768]{1,0:T(8,128)(2,1)S(1)}, bf16[32,768]{1,0:T(8,128)(2,1)S(1)}, u32[]{:S(2)}, u32[]{:S(2)}) collective-permute-start(bf16[32,768]{1,0:T(8,128)(2,1)S(1)} %add.7.held), channel_id=1, source_target_pairs={{0,8},{1,9},{2,10},{3,11},{4,12},{5,13},{6,14},{7,15},{8,0},{9,1},... | collective-permute-start | bytes 147464 | tf_op jit(solution)/shard_map/ppermute | solution.py:264
  46.3 1.4 %embed.6 = (bf16[2048,768]{1,0:T(8,128)(2,1)}, bf16[512,768]{1,0:T(8,128)(2,1)S(1)}, f32[8,128]{1,0:T(8,128)S(1)}) custom-call(s32[2,64]{1,0:T(2,128)S(1)} %bitcast.15, bf16[4,256,512]{2,1,0:T(8,128)(2,1)S(1)} %get-tuple-element.46.signal, bf16[2,256,512]{2,1,0:T(8,128)(2,1)S(1)} %get-tuple-element.51.on, ...), custom_call_target="tpu_custom_call", output_to_operand_aliasing={{0}: (7, {})} | custom-call | tf_op jit(solution)/shard_map/embed/pallas_call | solution.py:483
  48.0 2.2 %collective-permute-start.18 = (bf16[32,768]{1,0:T(8,128)(2,1)S(1)}, bf16[32,768]{1,0:T(8,128)(2,1)S(1)}, u32[]{:S(2)}, u32[]{:S(2)}) collective-permute-start(bf16[32,768]{1,0:T(8,128)(2,1)S(1)} %add.11.held), channel_id=1, source_target_pairs={{0,2},{1,3},{2,0},{3,1},{4,6},{5,7},{6,4},{7,5},{8,10},{9,11},{10,... | collective-permute-start | bytes 147464 | tf_op jit(solution)/shard_map/ppermute | solution.py:264
  50.4 0.6 %collective-permute-start.14 = (bf16[32,768]{1,0:T(8,128)(2,1)S(1)}, bf16[32,768]{1,0:T(8,128)(2,1)S(1)}, u32[]{:S(2)}, u32[]{:S(2)}) collective-permute-start(bf16[32,768]{1,0:T(8,128)(2,1)S(1)} %add.8.held), channel_id=1, source_target_pairs={{0,4},{1,5},{2,6},{3,7},{4,0},{5,1},{6,2},{7,3},{8,12},{9,13},{10,... | collective-permute-start | bytes 147464 | tf_op jit(solution)/shard_map/ppermute | solution.py:264
  51.0 2.8 %embed.7 = (bf16[2048,768]{1,0:T(8,128)(2,1)}, bf16[512,768]{1,0:T(8,128)(2,1)}, f32[8,128]{1,0:T(8,128)S(1)}) custom-call(s32[2,64]{1,0:T(2,128)S(1)} %bitcast.16, bf16[4,256,512]{2,1,0:T(8,128)(2,1)S(1)} %get-tuple-element.46.signal, bf16[2,256,512]{2,1,0:T(8,128)(2,1)S(1)} %get-tuple-element.51.on, ...), custom_call_target="tpu_custom_call", output_to_operand_aliasing={{0}: (7, {})} | custom-call | tf_op jit(solution)/shard_map/embed/pallas_call | solution.py:483
  54.7 0.6 %collective-permute-done.20.refs_2_ = bf16[64,768]{1,0:T(8,128)(2,1)S(1)} collective-permute-done((bf16[64,768]{1,0:T(8,128)(2,1)S(1)}, bf16[64,768]{1,0:T(8,128)(2,1)S(1)}, u32[]{:S(2)}, u32[]{:S(2)}) %collective-permute-start.20) | collective-permute-done | bytes 98336 | tf_op jit(solution)/shard_map/ppermute | solution.py:264
  55.3 0.8 %place.2.refs_1_ = f32[256,768]{1,0:T(8,128)} custom-call(bf16[64,768]{1,0:T(8,128)(2,1)S(1)} %join.2.rest_0_.refs_0_, bf16[64,768]{1,0:T(8,128)(2,1)S(1)} %join.3.refs_1_, bf16[64,768]{1,0:T(8,128)(2,1)S(1)} %collective-permute-done.20.refs_2_), custom_call_target="tpu_custom_call" | custom-call | tf_op jit(solution)/shard_map/place/pallas_call | solution.py:363
  56.2 0.7 %place.3 = f32[256,768]{1,0:T(8,128)} custom-call(bf16[64,768]{1,0:T(8,128)(2,1)S(1)} %collective-permute-done.19.refs_0_, f32[256,768]{1,0:T(8,128)} %place.2.refs_1_), custom_call_target="tpu_custom_call", output_to_operand_aliasing={{}: (1, {})} | custom-call | tf_op jit(solution)/shard_map/place/pallas_call | solution.py:363
  (43 shorter events, 4.2 us)
Async XLA Ops:
  0.6 7.6 %copy-start = (s32[64,2]{0,1:T(2,128)S(1)}, s32[64,2]{0,1:T(2,128)}, u32[]{:S(2)}) copy-start(s32[64,2]{0,1:T(2,128)} %param.8) | copy-start | bytes 1540
  0.6 10.5 %copy-start.2 = (s32[256,8]{0,1:T(8,128)S(1)}, s32[256,8]{0,1:T(8,128)}, u32[]{:S(2)}) copy-start(s32[256,8]{0,1:T(8,128)} %param.11) | copy-start | bytes 24580
  2.7 12.3 %collective-permute-start.4 = (bf16[256,512]{1,0:T(8,128)(2,1)S(1)}, bf16[256,512]{1,0:T(8,128)(2,1)S(1)}, u32[]{:S(2)}, u32[]{:S(2)}) collective-permute-start(bf16[256,512]{1,0:T(8,128)(2,1)S(1)} %get-tuple-element.44), channel_id=1, source_target_pairs={{1,2},{3,4},{5,6},{7,8},{9,10},{11,12},{13,14},{15,0},{2,1},{4,3},... | collective-permute-start | bytes 786440 | tf_op jit(solution)/shard_map/ppermute | solution.py:390
  9.9 3.7 %collective-permute-start = (bf16[176,512]{1,0:T(8,128)(2,1)S(1)}, bf16[176,512]{1,0:T(8,128)(2,1)S(1)}, u32[]{:S(2)}, u32[]{:S(2)}) collective-permute-start(bf16[176,512]{1,0:T(8,128)(2,1)S(1)} %get-tuple-element.39), channel_id=1, source_target_pairs={{0,1},{1,0},{2,3},{3,2},{4,5},{5,4},{6,7},{7,6},{8,9},{9,8},{10,11... | collective-permute-start | bytes 540680 | tf_op jit(solution)/shard_map/ppermute | solution.py:264
  9.9 3.7 %collective-permute-start.1 = (bf16[176,512]{1,0:T(8,128)(2,1)S(1)}, bf16[176,512]{1,0:T(8,128)(2,1)S(1)}, u32[]{:S(2)}, u32[]{:S(2)}) collective-permute-start(bf16[176,512]{1,0:T(8,128)(2,1)S(1)} %get-tuple-element.40), channel_id=1, source_target_pairs={{0,1},{1,0},{2,3},{3,2},{4,5},{5,4},{6,7},{7,6},{8,9},{9,8},{10,11... | collective-permute-start | bytes 540680 | tf_op jit(solution)/shard_map/ppermute | solution.py:264
  10.4 3.2 %collective-permute-start.2 = (bf16[160,512]{1,0:T(8,128)(2,1)S(1)}, bf16[160,512]{1,0:T(8,128)(2,1)S(1)}, u32[]{:S(2)}, u32[]{:S(2)}) collective-permute-start(bf16[160,512]{1,0:T(8,128)(2,1)S(1)} %get-tuple-element.41), channel_id=1, source_target_pairs={{0,1},{1,0},{2,3},{3,2},{4,5},{5,4},{6,7},{7,6},{8,9},{9,8},{10,11... | collective-permute-start | bytes 491528 | tf_op jit(solution)/shard_map/ppermute | solution.py:264
  10.5 10.2 %collective-permute-start.3 = (bf16[256,512]{1,0:T(8,128)(2,1)S(1)}, bf16[256,512]{1,0:T(8,128)(2,1)S(1)}, u32[]{:S(2)}, u32[]{:S(2)}) collective-permute-start(bf16[256,512]{1,0:T(8,128)(2,1)S(1)} %get-tuple-element.43), channel_id=1, source_target_pairs={{1,2},{3,4},{5,6},{7,8},{9,10},{11,12},{13,14},{15,0},{2,1},{4,3},... | collective-permute-start | bytes 786440 | tf_op jit(solution)/shard_map/ppermute | solution.py:390
  13.6 1.4 %copy-start.1 = (f32[2048]{0:T(1024)S(1)}, f32[2048]{0:T(1024)}, u32[]{:S(2)}) copy-start(f32[2048]{0:T(1024)} %param.9) | copy-start | bytes 24580
  16.2 9.9 %collective-permute-start.5 = (bf16[256,512]{1,0:T(8,128)(2,1)S(1)}, bf16[256,512]{1,0:T(8,128)(2,1)S(1)}, u32[]{:S(2)}, u32[]{:S(2)}) collective-permute-start(bf16[256,512]{1,0:T(8,128)(2,1)S(1)} %get-tuple-element.47), channel_id=1, source_target_pairs={{1,2},{3,4},{5,6},{7,8},{9,10},{11,12},{13,14},{15,0},{2,1},{4,3},... | collective-permute-start | bytes 786440 | tf_op jit(solution)/shard_map/ppermute | solution.py:390
  23.0 8.7 %collective-permute-start.9 = (bf16[256,512]{1,0:T(8,128)(2,1)S(1)}, bf16[256,512]{1,0:T(8,128)(2,1)S(1)}, u32[]{:S(2)}, u32[]{:S(2)}) collective-permute-start(bf16[256,512]{1,0:T(8,128)(2,1)S(1)} %get-tuple-element.52), channel_id=1, source_target_pairs={{1,2},{3,4},{5,6},{7,8},{9,10},{11,12},{13,14},{15,0},{2,1},{4,3},... | collective-permute-start | bytes 786440 | tf_op jit(solution)/shard_map/ppermute | solution.py:390
  24.5 2.6 %collective-permute-start.6 = (bf16[176,512]{1,0:T(8,128)(2,1)S(1)}, bf16[176,512]{1,0:T(8,128)(2,1)S(1)}, u32[]{:S(2)}, u32[]{:S(2)}) collective-permute-start(bf16[176,512]{1,0:T(8,128)(2,1)S(1)} %get-tuple-element.48), channel_id=1, source_target_pairs={{0,1},{1,0},{2,3},{3,2},{4,5},{5,4},{6,7},{7,6},{8,9},{9,8},{10,11... | collective-permute-start | bytes 540680 | tf_op jit(solution)/shard_map/ppermute | solution.py:264
  24.6 2.6 %collective-permute-start.7 = (bf16[176,512]{1,0:T(8,128)(2,1)S(1)}, bf16[176,512]{1,0:T(8,128)(2,1)S(1)}, u32[]{:S(2)}, u32[]{:S(2)}) collective-permute-start(bf16[176,512]{1,0:T(8,128)(2,1)S(1)} %get-tuple-element.49), channel_id=1, source_target_pairs={{0,1},{1,0},{2,3},{3,2},{4,5},{5,4},{6,7},{7,6},{8,9},{9,8},{10,11... | collective-permute-start | bytes 540680 | tf_op jit(solution)/shard_map/ppermute | solution.py:264
  25.1 2.0 %collective-permute-start.8 = (bf16[160,512]{1,0:T(8,128)(2,1)S(1)}, bf16[160,512]{1,0:T(8,128)(2,1)S(1)}, u32[]{:S(2)}, u32[]{:S(2)}) collective-permute-start(bf16[160,512]{1,0:T(8,128)(2,1)S(1)} %get-tuple-element.50), channel_id=1, source_target_pairs={{0,1},{1,0},{2,3},{3,2},{4,5},{5,4},{6,7},{7,6},{8,9},{9,8},{10,11... | collective-permute-start | bytes 491528 | tf_op jit(solution)/shard_map/ppermute | solution.py:264
  32.5 1.8 %collective-permute-start.10 = (bf16[128,768]{1,0:T(8,128)(2,1)S(1)}, bf16[128,768]{1,0:T(8,128)(2,1)S(1)}, u32[]{:S(2)}, u32[]{:S(2)}) collective-permute-start(bf16[128,768]{1,0:T(8,128)(2,1)S(1)} %query_end.3), channel_id=1, source_target_pairs={{0,1},{1,0},{2,3},{3,2},{4,5},{5,4},{6,7},{7,6},{8,9},{9,8},{10,11... | collective-permute-start | bytes 589832 | tf_op jit(solution)/shard_map/ppermute | solution.py:264
  34.4 4.2 %collective-permute-start.15 = (bf16[32,768]{1,0:T(8,128)(2,1)S(1)}, bf16[32,768]{1,0:T(8,128)(2,1)S(1)}, u32[]{:S(2)}, u32[]{:S(2)}) collective-permute-start(bf16[32,768]{1,0:T(8,128)(2,1)S(1)} %get-tuple-element.63), channel_id=1, source_target_pairs={{0,2},{1,3},{2,0},{3,1},{4,6},{5,7},{6,4},{7,5},{8,10},{9,11},{10,... | collective-permute-start | bytes 147464 | tf_op jit(solution)/shard_map/ppermute | solution.py:264
  35.3 4.9 %collective-permute-start.11 = (bf16[32,768]{1,0:T(8,128)(2,1)S(1)}, bf16[32,768]{1,0:T(8,128)(2,1)S(1)}, u32[]{:S(2)}, u32[]{:S(2)}) collective-permute-start(bf16[32,768]{1,0:T(8,128)(2,1)S(1)} %get-tuple-element.61), channel_id=1, source_target_pairs={{0,4},{1,5},{2,6},{3,7},{4,0},{5,1},{6,2},{7,3},{8,12},{9,13},{10,... | collective-permute-start | bytes 147464 | tf_op jit(solution)/shard_map/ppermute | solution.py:264
  38.6 5.1 %collective-permute-start.16 = (bf16[32,768]{1,0:T(8,128)(2,1)S(1)}, bf16[32,768]{1,0:T(8,128)(2,1)S(1)}, u32[]{:S(2)}, u32[]{:S(2)}) collective-permute-start(bf16[32,768]{1,0:T(8,128)(2,1)S(1)} %add.9.held), channel_id=1, source_target_pairs={{0,8},{1,9},{2,10},{3,11},{4,12},{5,13},{6,14},{7,15},{8,0},{9,1},... | collective-permute-start | bytes 147464 | tf_op jit(solution)/shard_map/ppermute | solution.py:264
  40.2 4.6 %collective-permute-start.12 = (bf16[32,768]{1,0:T(8,128)(2,1)S(1)}, bf16[32,768]{1,0:T(8,128)(2,1)S(1)}, u32[]{:S(2)}, u32[]{:S(2)}) collective-permute-start(bf16[32,768]{1,0:T(8,128)(2,1)S(1)} %add.6.held), channel_id=1, source_target_pairs={{0,2},{1,3},{2,0},{3,1},{4,6},{5,7},{6,4},{7,5},{8,10},{9,11},{10,... | collective-permute-start | bytes 147464 | tf_op jit(solution)/shard_map/ppermute | solution.py:264
  43.7 4.3 %collective-permute-start.17 = (bf16[32,768]{1,0:T(8,128)(2,1)S(1)}, bf16[32,768]{1,0:T(8,128)(2,1)S(1)}, u32[]{:S(2)}, u32[]{:S(2)}) collective-permute-start(bf16[32,768]{1,0:T(8,128)(2,1)S(1)} %add.10.held), channel_id=1, source_target_pairs={{0,4},{1,5},{2,6},{3,7},{4,0},{5,1},{6,2},{7,3},{8,12},{9,13},{10,... | collective-permute-start | bytes 147464 | tf_op jit(solution)/shard_map/ppermute | solution.py:264
  44.8 5.6 %collective-permute-start.13 = (bf16[32,768]{1,0:T(8,128)(2,1)S(1)}, bf16[32,768]{1,0:T(8,128)(2,1)S(1)}, u32[]{:S(2)}, u32[]{:S(2)}) collective-permute-start(bf16[32,768]{1,0:T(8,128)(2,1)S(1)} %add.7.held), channel_id=1, source_target_pairs={{0,8},{1,9},{2,10},{3,11},{4,12},{5,13},{6,14},{7,15},{8,0},{9,1},... | collective-permute-start | bytes 147464 | tf_op jit(solution)/shard_map/ppermute | solution.py:264
  48.0 5.9 %collective-permute-start.18 = (bf16[32,768]{1,0:T(8,128)(2,1)S(1)}, bf16[32,768]{1,0:T(8,128)(2,1)S(1)}, u32[]{:S(2)}, u32[]{:S(2)}) collective-permute-start(bf16[32,768]{1,0:T(8,128)(2,1)S(1)} %add.11.held), channel_id=1, source_target_pairs={{0,2},{1,3},{2,0},{3,1},{4,6},{5,7},{6,4},{7,5},{8,10},{9,11},{10,... | collective-permute-start | bytes 147464 | tf_op jit(solution)/shard_map/ppermute | solution.py:264
  50.4 4.2 %collective-permute-start.14 = (bf16[32,768]{1,0:T(8,128)(2,1)S(1)}, bf16[32,768]{1,0:T(8,128)(2,1)S(1)}, u32[]{:S(2)}, u32[]{:S(2)}) collective-permute-start(bf16[32,768]{1,0:T(8,128)(2,1)S(1)} %add.8.held), channel_id=1, source_target_pairs={{0,4},{1,5},{2,6},{3,7},{4,0},{5,1},{6,2},{7,3},{8,12},{9,13},{10,... | collective-permute-start | bytes 147464 | tf_op jit(solution)/shard_map/ppermute | solution.py:264
  53.9 1.4 %collective-permute-start.20 = (bf16[64,768]{1,0:T(8,128)(2,1)S(1)}, bf16[64,768]{1,0:T(8,128)(2,1)S(1)}, u32[]{:S(2)}, u32[]{:S(2)}) collective-permute-start(bf16[64,768]{1,0:T(8,128)(2,1)S(1)} %join.2.rest_0_.refs_0_), channel_id=1, source_target_pairs={{0,1},{1,0},{2,3},{3,2},{4,5},{5,4},{6,7},{7,6},{8,9},{9,8},{10,11... | collective-permute-start | bytes 294920 | tf_op jit(solution)/shard_map/ppermute | solution.py:264
  54.6 1.6 %collective-permute-start.19 = (bf16[64,768]{1,0:T(8,128)(2,1)S(1)}, bf16[64,768]{1,0:T(8,128)(2,1)S(1)}, u32[]{:S(2)}, u32[]{:S(2)}) collective-permute-start(bf16[64,768]{1,0:T(8,128)(2,1)S(1)} %join.3.refs_1_), channel_id=1, source_target_pairs={{0,1},{1,0},{2,3},{3,2},{4,5},{5,4},{6,7},{7,6},{8,9},{9,8},{10,11... | collective-permute-start | bytes 294920 | tf_op jit(solution)/shard_map/ppermute | solution.py:264

commit v13 on v12

--- a/solution.py
+++ b/solution.py
@@ -196,14 +196,10 @@
     )
 
 
-def query_end_kernel(lists, part, received, embeddings, out, *, blocks, own):
+def query_end_kernel(lists, part, received, embeddings, out, *, blocks):
     _, second = named_by_partner(lists, blocks, OFF)
-    rows = out.shape[0]
-    core = lax.axis_index(AXIS) % 2
-    half = core if own else 1 - core
-    place = pl.ds(pl.multiple_of(half * rows, rows), rows)
     right = block_rows(embeddings, second, received.shape[1])
-    out[...] = (part[place, :] + dot(received[place, :], right, NN)).astype(out.dtype)
+    out[...] = (part[...] + dot(received[...], right, NN)).astype(out.dtype)
 
 
 def embed_kernel(lists, signal, on, off_a, off_b, queries, *rest, blocks, g, scale):
@@ -296,31 +292,25 @@
     out[pl.ds(pl.multiple_of((1 - digit) * rows, rows), rows), :] = got[...]
 
 
-def place_kernel(*refs, places):
-    out, wide, sem = refs[-3:]
-    rows = refs[0].shape[0]
-    core = lax.axis_index(AXIS) % 2
-    copies = []
-    for k, (chain, own) in enumerate(places):
-        wide[k] = refs[k][...].astype(F32)
-        half = core if own else 1 - core
-        begin = pl.multiple_of((2 * half + chain) * rows, rows)
-        copies.append(pltpu.make_async_copy(wide.at[k], out.at[pl.ds(begin, rows), :], sem.at[k]))
-        copies[-1].start()
-    for copy in copies:
-        copy.wait()
+def place_kernel(held, got, *rest, chain):
+    out, wide, sem = rest[-3:]
+    rows = held.shape[0]
+    wide[...] = jnp.where(lax.axis_index(AXIS) % 2 == 1, held[...], got[...]).astype(F32)
+    copy = pltpu.make_async_copy(wide, out.at[pl.ds(chain * rows, rows), :], sem)
+    copy.start()
+    copy.wait()
 
 
 def sum_queries(kept, sent, beside, scale):
     count = lax.axis_size(AXIS)
     rows, width = kept.shape
-    got = exchange(sent, 1)
     if count & (count - 1) or count < 8:
-        half = kept + got.astype(F32)
-        half = lax.psum(half, AXIS, axis_index_groups=[list(range(c, count, 2)) for c in range(2)])
-        both = jnp.stack([half, exchange(half, 1)])
-        both = jnp.where(lax.axis_index(AXIS) % 2 == 0, both, both[::-1])
-        return both.reshape(2 * rows, width) * scale
+        return lax.psum(kept, AXIS) * scale
+    got = lax.ppermute(sent, AXIS, [(i, i + 1) for i in range(0, count, 2)])
+
+    def chip_exchange(value, bit):
+        return lax.ppermute(value, AXIS, [(i, i ^ bit) for i in range(1, count, 2)])
+
     bits = [1 << k for k in range(1, count.bit_length() - 1)]
     orders = [[bits[0], *bits[2:], bits[1]], [bits[1], bits[0], *bits[2:]]]
     ends = [order[0] for order in orders]
@@ -334,7 +324,7 @@
     )(kept, got)
     held, sent = [kept_a, kept_b], [sent_a, sent_b]
     for k in range(len(bits)):
-        got = [exchange(piece, order[k]) for piece, order in zip(sent, orders)]
+        got = [chip_exchange(piece, order[k]) for piece, order in zip(sent, orders)]
         for chain in range(2):
             after = beside[k : k + 1] if chain == 0 else []
             held[chain] = call(
@@ -344,8 +334,8 @@
                 narrow,
             )(held[chain], got[chain], *after)
         sent = list(held)
-    got = [exchange(piece, bit) for piece, bit in zip(held, ends)]
-    joined, swapped = [], []
+    got = [chip_exchange(piece, bit) for piece, bit in zip(held, ends)]
+    joined, handed = [], []
     for chain, bit in enumerate(ends):
         after = beside[len(bits) :] if chain == 0 else joined
         joined.append(
@@ -357,24 +347,21 @@
                 flops=2 * 10**8,
             )(held[chain], got[chain], *after)
         )
-        swapped.append(exchange(joined[chain], 1))
-
-    def place(values, places, *begun):
-        return call(
-            functools.partial(place_kernel, places=places),
-            "place",
-            [VMEM] * len(values) + [ANY] * len(begun),
-            jax.ShapeDtypeStruct((2 * rows, width), F32),
-            out_specs=ANY,
-            scratch=[
-                pltpu.VMEM((len(values), rows // 2, width), F32),
-                pltpu.SemaphoreType.DMA((len(values),)),
-            ],
-            aliases={len(values): 0} if begun else None,
-        )(*values, *begun)
-
-    early = place([joined[0], joined[1], swapped[0]], [(0, True), (1, True), (0, False)])
-    return place([swapped[1]], [(1, False)], early)
+        handed.append(lax.ppermute(joined[chain], AXIS, [(i + 1, i) for i in range(0, count, 2)]))
+    begun = []
+    for chain in range(2):
+        begun = [
+            call(
+                functools.partial(place_kernel, chain=chain),
+                "place",
+                [VMEM] * 2 + [ANY] * chain,
+                jax.ShapeDtypeStruct((rows, width), F32),
+                out_specs=ANY,
+                scratch=[pltpu.VMEM((rows // 2, width), F32), pltpu.SemaphoreType.DMA],
+                aliases={2: 0} if chain else None,
+            )(joined[chain], handed[chain], *begun)
+        ]
+    return begun[0]
 
 
 def per_device(embeddings, edge_tiles, neighbour, propensity, queries, positives):
@@ -467,15 +454,15 @@
     part, on = call(
         functools.partial(query_on_kernel, blocks=blocks), "query_on", [SMEM] + [VMEM] * 5, [whole, pair]
     )(lists, part, embeddings, *back_on)
-    def query_end(own, kind):
+    def query_end(kind):
         return call(
-            functools.partial(query_end_kernel, blocks=blocks, own=own),
+            functools.partial(query_end_kernel, blocks=blocks),
             "query_end",
             [SMEM] + [VMEM] * 3,
-            in_vmem((rows // 2, width), kind),
+            in_vmem((rows, width), kind),
         )(lists, part, back_b, embeddings)
 
-    sent, kept = query_end(False, BF16), query_end(True, F32)
+    sent, kept = query_end(BF16), query_end(F32)
     ready = in_vmem((block, width), BF16)
     written = jax.ShapeDtypeStruct((labels_dev, width), BF16)
     outs, tokens = [], []

time: 56.9 us -> 70.1 us (1.23)
  waiting for transfers between devices: 7.03 us -> 20.9 us
  starting transfers between devices: 23.2 us -> 21.8 us
    ppermute x0 -> x11, waiting for transfers between devices: none -> 17.6 us  [the longest x2 17.2 us: sum_queries(): lax.ppermute(joined[chain], AXIS, [(i + 1, i) for i in range(0, count, 2)])]
    ppermute x17 -> x6, starting transfers between devices: 12.5 us -> 1.29 us  [exchange(): return lax.ppermute(value, AXIS, [(i, i ^ mask) for i in range(count)])]
    ppermute x0 -> x11, starting transfers between devices: none -> 9.23 us  [the longest x8 5.33 us: chip_exchange(): return lax.ppermute(value, AXIS, [(i, i ^ bit) for i in range(1, count, 2)])]
    ppermute x17 -> x6, waiting for transfers between devices: 3.66 us -> 0.02 us  [exchange(): return lax.ppermute(value, AXIS, [(i, i ^ mask) for i in range(count)])]
  transfers between devices with their start and end apart: 21 -> 21, of which waited for: 8 -> 4; matrix products, arithmetic and copies ran while one was open for 0% -> 0% of each run, Pallas kernels for 39% -> 32%
where the time goes in v13:
time: 70.1 us; the launch traced here: 69.9 us
  Pallas kernels  26.2 us (37%)
  starting transfers between devices  21.8 us (31%)
  waiting for transfers between devices  20.9 us (30%)
  between operations  1.09 us (2%)
    ppermute x2, waiting for transfers between devices, sum_queries(): lax.ppermute(joined[chain], AXIS, [(i + 1, i) for i in range(0, count, 2)])  17.2 us
    ppermute x4, starting transfers between devices, off_swap(): return lax.ppermute(value, AXIS, off_route)  11.2 us
    pallas_call x4, Pallas kernels, per_device(): call(functools.partial(embed_kernel, blocks=blocks, g=g, scale=1.0 / math...  6.8 us
    ppermute x8, starting transfers between devices, chip_exchange(): return lax.ppermute(value, AXIS, [(i, i ^ bit) for i in range(1, count, 2)])  5.33 us
    pallas_call x2, Pallas kernels, signal_of(): call(functools.partial(signal_kernel, slot=slot), 'signal', [SMEM] + [VME...  3.54 us
    ppermute x4, waiting for transfers between devices, off_swap(): return lax.ppermute(value, AXIS, off_route)  3.27 us
    ppermute x2, starting transfers between devices, sum_queries(): lax.ppermute(joined[chain], AXIS, [(i + 1, i) for i in range(0, count, 2)])  2.58 us
    pallas_call x1, Pallas kernels, per_device(): call(hits_kernel, 'hits', [VMEM, HBM], [in_vmem(full, BF16), in_vmem(edge...  2.45 us
  transfers between devices with their start and end apart: 21, of which 4 were waited for; matrix products, arithmetic and copies ran while one was open for 0% of the time, Pallas kernels for 32%

profile of v13, /device:TPU:0, one launch (start us, length us, event | category | flops | bytes accessed | tf_op | source)
XLA Modules:
  0.0 69.9 jit_solution(13355643126917972285)
XLA Ops:
  0.7 2.0 %project.1 = (bf16[256,512]{1,0:T(8,128)(2,1)S(1)}, bf16[256,768]{1,0:T(8,128)(2,1)S(1)}, bf16[2048,768]{1,0:T(8,128)(2,1)S(1)}) custom-call(s32[2,64]{1,0:T(2,128)} %bitcast.3, bf16[256,768]{1,0:T(8,128)(2,1)} %queries.1, bf16[2048,768]{1,0:T(8,128)(2,1)} %embeddings.1), custom_call_target="tpu_custom_call" | custom-call | tf_op jit(solution)/shard_map/project/pallas_call | solution.py:389
  2.7 5.5 %collective-permute-start.4 = (bf16[256,512]{1,0:T(8,128)(2,1)S(1)}, bf16[256,512]{1,0:T(8,128)(2,1)S(1)}, u32[]{:S(2)}, u32[]{:S(2)}) collective-permute-start(bf16[256,512]{1,0:T(8,128)(2,1)S(1)} %get-tuple-element.44), channel_id=1, source_target_pairs={{1,2},{3,4},{5,6},{7,8},{9,10},{11,12},{13,14},{15,0},{2,1},{4,3},... | collective-permute-start | bytes 786440 | tf_op jit(solution)/shard_map/ppermute | solution.py:377
  8.2 1.6 %own.1 = (f32[4,256,512]{2,1,0:T(8,128)S(1)}, bf16[256,512]{1,0:T(8,128)(2,1)S(1)}, bf16[176,512]{1,0:T(8,128)(2,1)S(1)}, bf16[176,512]{1,0:T(8,128)(2,1)S(1)}, bf16[160,512]{1,0:T(8,128)(2,1)S(1)}) custom-call(s32[2,64]{1,0:T(2,128)S(1)} %bitcast.4, bf16[256,768]{1,0:T(8,128)(2,1)S(1)} %get-tuple-element.35.queries, ...), custom_call_target="tpu_custom_call" | custom-call | tf_op jit(solution)/shard_map/own/pallas_call | solution.py:397
  10.5 0.7 %collective-permute-start.3 = (bf16[256,512]{1,0:T(8,128)(2,1)S(1)}, bf16[256,512]{1,0:T(8,128)(2,1)S(1)}, u32[]{:S(2)}, u32[]{:S(2)}) collective-permute-start(bf16[256,512]{1,0:T(8,128)(2,1)S(1)} %get-tuple-element.43), channel_id=1, source_target_pairs={{1,2},{3,4},{5,6},{7,8},{9,10},{11,12},{13,14},{15,0},{2,1},{4,3},... | collective-permute-start | bytes 786440 | tf_op jit(solution)/shard_map/ppermute | solution.py:377
  11.2 2.4 %hits.1 = (bf16[4,256,512]{2,1,0:T(8,128)(2,1)S(1)}, bf16[4,2,512,512]{3,2,1,0:T(8,128)(2,1)S(1)}) custom-call(s32[8,256]{1,0:T(8,128)S(1)} %bitcast.19, bf16[4,2,512,512]{3,2,1,0:T(8,128)(2,1)} %tiles.1), custom_call_target="tpu_custom_call" | custom-call | tf_op jit(solution)/shard_map/hits/pallas_call | solution.py:404
  13.7 1.3 %base.1 = f32[4,256,512]{2,1,0:T(8,128)S(1)} custom-call(s32[2,64]{1,0:T(2,128)S(1)} %bitcast.5, f32[4,256,512]{2,1,0:T(8,128)S(1)} %get-tuple-element.37.own, bf16[4,2,512,512]{3,2,1,0:T(8,128)(2,1)S(1)} %get-tuple-element.38.tiles, bf16[176,512]{1,0:T(8,128)(2,1)S(1)} %collective-permute-done.rest_0_, bf16[176,512]{1,0:T(8,128)(2,1)S(1)} %collective-permute-done.1.rest_1_, ...), custom_call_target="tpu_custom_call" | custom-call | tf_op jit(solution)/shard_map/base/pallas_call | solution.py:412
  15.1 1.2 %signal.2 = (bf16[4,256,512]{2,1,0:T(8,128)(2,1)S(1)}, bf16[256,512]{1,0:T(8,128)(2,1)S(1)}) custom-call(s32[2,64]{1,0:T(2,128)S(1)} %bitcast.6, f32[4,256,512]{2,1,0:T(8,128)S(1)} %base.1, bf16[4,256,512]{2,1,0:T(8,128)(2,1)S(1)} %get-tuple-element.42.hits, f32[1,2048]{1,0:T(1,128)S(1)} %bitcast.17, bf16[256,512]{1,0:T(8,128)(2,1)S(1)} %collective-permute-done.4.received, ...), custom_call_target="tpu_custom_call" | custom-call | flops 2000000000 | tf_op jit(solution)/shard_map/signal/pallas_call | solution.py:422
  16.3 4.9 %collective-permute-start.5 = (bf16[256,512]{1,0:T(8,128)(2,1)S(1)}, bf16[256,512]{1,0:T(8,128)(2,1)S(1)}, u32[]{:S(2)}, u32[]{:S(2)}) collective-permute-start(bf16[256,512]{1,0:T(8,128)(2,1)S(1)} %get-tuple-element.47), channel_id=1, source_target_pairs={{1,2},{3,4},{5,6},{7,8},{9,10},{11,12},{13,14},{15,0},{2,1},{4,3},... | collective-permute-start | bytes 786440 | tf_op jit(solution)/shard_map/ppermute | solution.py:377
  21.2 2.3 %signal.3 = (bf16[4,256,512]{2,1,0:T(8,128)(2,1)S(1)}, bf16[256,512]{1,0:T(8,128)(2,1)S(1)}) custom-call(s32[2,64]{1,0:T(2,128)S(1)} %bitcast.7, f32[4,256,512]{2,1,0:T(8,128)S(1)} %base.1, bf16[4,256,512]{2,1,0:T(8,128)(2,1)S(1)} %get-tuple-element.42.hits, f32[1,2048]{1,0:T(1,128)S(1)} %bitcast.18, ...), custom_call_target="tpu_custom_call", output_to_operand_aliasing={{0}: (6, {})} | custom-call | tf_op jit(solution)/shard_map/signal/pallas_call | solution.py:422
  23.7 1.4 %push.1 = (bf16[176,512]{1,0:T(8,128)(2,1)S(1)}, bf16[176,512]{1,0:T(8,128)(2,1)S(1)}, bf16[160,512]{1,0:T(8,128)(2,1)S(1)}) custom-call(s32[2,64]{1,0:T(2,128)S(1)} %bitcast.8, bf16[4,256,512]{2,1,0:T(8,128)(2,1)S(1)} %get-tuple-element.46.signal, bf16[4,2,512,512]{3,2,1,0:T(8,128)(2,1)S(1)} %get-tuple-element.38.tiles), custom_call_target="tpu_custom_call" | custom-call | tf_op jit(solution)/shard_map/push/pallas_call | solution.py:436
  25.7 1.0 %query.1.part = f32[256,768]{1,0:T(8,128)S(1)} custom-call(bf16[4,256,512]{2,1,0:T(8,128)(2,1)S(1)} %get-tuple-element.46.signal, bf16[2048,768]{1,0:T(8,128)(2,1)S(1)} %get-tuple-element.36.embeddings), custom_call_target="tpu_custom_call" | custom-call | tf_op jit(solution)/shard_map/query/pallas_call | solution.py:446
  26.7 1.0 %query_half.1.part = f32[256,768]{1,0:T(8,128)S(1)} custom-call(s32[2,64]{1,0:T(2,128)S(1)} %bitcast.9, f32[256,768]{1,0:T(8,128)S(1)} %query.1.part, bf16[256,512]{1,0:T(8,128)(2,1)S(1)} %collective-permute-done.5.received.off_a, bf16[2048,768]{1,0:T(8,128)(2,1)S(1)} %get-tuple-element.36.embeddings), custom_call_target="tpu_custom_call" | custom-call | flops 1000000000 | tf_op jit(solution)/shard_map/query_half/pallas_call | solution.py:447
  27.7 1.2 %query_on.1 = (f32[256,768]{1,0:T(8,128)S(1)}, bf16[2,256,512]{2,1,0:T(8,128)(2,1)S(1)}) custom-call(s32[2,64]{1,0:T(2,128)S(1)} %bitcast.10, f32[256,768]{1,0:T(8,128)S(1)} %query_half.1.part, bf16[2048,768]{1,0:T(8,128)(2,1)S(1)} %get-tuple-element.36.embeddings, bf16[176,512]{1,0:T(8,128)(2,1)S(1)} %collective-permute-done.6.rest_0_, ...), custom_call_target="tpu_custom_call" | custom-call | tf_op jit(solution)/shard_map/query_on/pallas_call | solution.py:454
  28.9 3.3 %collective-permute-done.9.off_b.received = bf16[256,512]{1,0:T(8,128)(2,1)S(1)} collective-permute-done((bf16[256,512]{1,0:T(8,128)(2,1)S(1)}, bf16[256,512]{1,0:T(8,128)(2,1)S(1)}, u32[]{:S(2)}, u32[]{:S(2)}) %collective-permute-start.9) | collective-permute-done | bytes 262176 | tf_op jit(solution)/shard_map/ppermute | solution.py:377
  32.2 0.9 %query_end.3 = bf16[256,768]{1,0:T(8,128)(2,1)S(1)} custom-call(s32[2,64]{1,0:T(2,128)S(1)} %bitcast.11, f32[256,768]{1,0:T(8,128)S(1)} %get-tuple-element.59.part, bf16[256,512]{1,0:T(8,128)(2,1)S(1)} %collective-permute-done.9.off_b.received, bf16[2048,768]{1,0:T(8,128)(2,1)S(1)} %get-tuple-element.36.embeddings), custom_call_target="tpu_custom_call" | custom-call | tf_op jit(solution)/shard_map/query_end/pallas_call | solution.py:458
  33.1 1.3 %collective-permute-start.10 = (bf16[256,768]{1,0:T(8,128)(2,1)S(1)}, bf16[256,768]{1,0:T(8,128)(2,1)S(1)}, u32[]{:S(2)}, u32[]{:S(2)}) collective-permute-start(bf16[256,768]{1,0:T(8,128)(2,1)S(1)} %query_end.3), channel_id=1, source_target_pairs={{0,1},{2,3},{4,5},{6,7},{8,9},{10,11},{12,13},{14,15},{16,17},{18,... | collective-permute-start | bytes 1179656 | tf_op jit(solution)/shard_map/ppermute | solution.py:309
  34.4 1.0 %query_end.2.held = f32[256,768]{1,0:T(8,128)S(1)} custom-call(s32[2,64]{1,0:T(2,128)S(1)} %bitcast.12, f32[256,768]{1,0:T(8,128)S(1)} %get-tuple-element.59.part, bf16[256,512]{1,0:T(8,128)(2,1)S(1)} %collective-permute-done.9.off_b.received, bf16[2048,768]{1,0:T(8,128)(2,1)S(1)} %get-tuple-element.36.embeddings), custom_call_target="tpu_custom_call" | custom-call | tf_op jit(solution)/shard_map/query_end/pallas_call | solution.py:458
  35.9 0.7 collective-permute-start.15
  36.6 0.7 collective-permute-start.11
  37.2 1.1 %embed.4 = (bf16[512,768]{1,0:T(8,128)(2,1)S(1)}, f32[8,128]{1,0:T(8,128)S(1)}) custom-call(s32[2,64]{1,0:T(2,128)S(1)} %bitcast.13, bf16[4,256,512]{2,1,0:T(8,128)(2,1)S(1)} %get-tuple-element.46.signal, bf16[2,256,512]{2,1,0:T(8,128)(2,1)S(1)} %get-tuple-element.51.on, bf16[256,512]{1,0:T(8,128)(2,1)S(1)} %collective-permute-done.5.received.off_a, ...), custom_call_target="tpu_custom_call" | custom-call | tf_op jit(solution)/shard_map/embed/pallas_call | solution.py:470
  38.4 0.7 collective-permute-start.16
  39.1 0.7 collective-permute-start.12
  39.7 1.4 %embed.5 = (bf16[2048,768]{1,0:T(8,128)(2,1)}, bf16[512,768]{1,0:T(8,128)(2,1)S(1)}, f32[8,128]{1,0:T(8,128)S(1)}) custom-call(s32[2,64]{1,0:T(2,128)S(1)} %bitcast.14, bf16[4,256,512]{2,1,0:T(8,128)(2,1)S(1)} %get-tuple-element.46.signal, bf16[2,256,512]{2,1,0:T(8,128)(2,1)S(1)} %get-tuple-element.51.on, ...), custom_call_target="tpu_custom_call" | custom-call | tf_op jit(solution)/shard_map/embed/pallas_call | solution.py:470
  41.2 0.7 collective-permute-start.17
  42.0 0.7 collective-permute-start.13
  42.6 1.5 %embed.6 = (bf16[2048,768]{1,0:T(8,128)(2,1)}, bf16[512,768]{1,0:T(8,128)(2,1)S(1)}, f32[8,128]{1,0:T(8,128)S(1)}) custom-call(s32[2,64]{1,0:T(2,128)S(1)} %bitcast.15, bf16[4,256,512]{2,1,0:T(8,128)(2,1)S(1)} %get-tuple-element.46.signal, bf16[2,256,512]{2,1,0:T(8,128)(2,1)S(1)} %get-tuple-element.51.on, ...), custom_call_target="tpu_custom_call", output_to_operand_aliasing={{0}: (7, {})} | custom-call | tf_op jit(solution)/shard_map/embed/pallas_call | solution.py:470
  45.5 2.8 %embed.7 = (bf16[2048,768]{1,0:T(8,128)(2,1)}, bf16[512,768]{1,0:T(8,128)(2,1)}, f32[8,128]{1,0:T(8,128)S(1)}) custom-call(s32[2,64]{1,0:T(2,128)S(1)} %bitcast.16, bf16[4,256,512]{2,1,0:T(8,128)(2,1)S(1)} %get-tuple-element.46.signal, bf16[2,256,512]{2,1,0:T(8,128)(2,1)S(1)} %get-tuple-element.51.on, ...), custom_call_target="tpu_custom_call", output_to_operand_aliasing={{0}: (7, {})} | custom-call | tf_op jit(solution)/shard_map/embed/pallas_call | solution.py:470
  48.5 1.3 %collective-permute-start.20 = (bf16[128,768]{1,0:T(8,128)(2,1)S(1)}, bf16[128,768]{1,0:T(8,128)(2,1)S(1)}, u32[]{:S(2)}, u32[]{:S(2)}) collective-permute-start(bf16[128,768]{1,0:T(8,128)(2,1)S(1)} %join.2.rest_0_.held), channel_id=1, source_target_pairs={{1,0},{3,2},{5,4},{7,6},{9,8},{11,10},{13,12},{15,14},{17,16},{19,... | collective-permute-start | bytes 589832 | tf_op jit(solution)/shard_map/ppermute | solution.py:350
  49.8 1.3 %collective-permute-start.19 = (bf16[128,768]{1,0:T(8,128)(2,1)S(1)}, bf16[128,768]{1,0:T(8,128)(2,1)S(1)}, u32[]{:S(2)}, u32[]{:S(2)}) collective-permute-start(bf16[128,768]{1,0:T(8,128)(2,1)S(1)} %join.3.held), channel_id=1, source_target_pairs={{1,0},{3,2},{5,4},{7,6},{9,8},{11,10},{13,12},{15,14},{17,16},{19,... | collective-permute-start | bytes 589832 | tf_op jit(solution)/shard_map/ppermute | solution.py:350
  51.1 16.6 %collective-permute-done.20.got = bf16[128,768]{1,0:T(8,128)(2,1)S(1)} collective-permute-done((bf16[128,768]{1,0:T(8,128)(2,1)S(1)}, bf16[128,768]{1,0:T(8,128)(2,1)S(1)}, u32[]{:S(2)}, u32[]{:S(2)}) %collective-permute-start.20) | collective-permute-done | bytes 196640 | tf_op jit(solution)/shard_map/ppermute | solution.py:350
  67.7 0.8 %place.2.rest_0_ = f32[256,768]{1,0:T(8,128)} custom-call(bf16[128,768]{1,0:T(8,128)(2,1)S(1)} %join.2.rest_0_.held, bf16[128,768]{1,0:T(8,128)(2,1)S(1)} %collective-permute-done.20.got), custom_call_target="tpu_custom_call" | custom-call | tf_op jit(solution)/shard_map/place/pallas_call | solution.py:354
  69.1 0.8 %place.3 = f32[256,768]{1,0:T(8,128)} custom-call(bf16[128,768]{1,0:T(8,128)(2,1)S(1)} %join.3.held, bf16[128,768]{1,0:T(8,128)(2,1)S(1)} %collective-permute-done.19.got, f32[256,768]{1,0:T(8,128)} %place.2.rest_0_), custom_call_target="tpu_custom_call", output_to_operand_aliasing={{}: (2, {})} | custom-call | tf_op jit(solution)/shard_map/place/pallas_call | solution.py:354
  (43 shorter events, 4.1 us)
Async XLA Ops:
  0.6 7.6 %copy-start = (s32[64,2]{0,1:T(2,128)S(1)}, s32[64,2]{0,1:T(2,128)}, u32[]{:S(2)}) copy-start(s32[64,2]{0,1:T(2,128)} %param.8) | copy-start | bytes 1540
  0.6 10.6 %copy-start.2 = (s32[256,8]{0,1:T(8,128)S(1)}, s32[256,8]{0,1:T(8,128)}, u32[]{:S(2)}) copy-start(s32[256,8]{0,1:T(8,128)} %param.11) | copy-start | bytes 24580
  2.7 12.4 %collective-permute-start.4 = (bf16[256,512]{1,0:T(8,128)(2,1)S(1)}, bf16[256,512]{1,0:T(8,128)(2,1)S(1)}, u32[]{:S(2)}, u32[]{:S(2)}) collective-permute-start(bf16[256,512]{1,0:T(8,128)(2,1)S(1)} %get-tuple-element.44), channel_id=1, source_target_pairs={{1,2},{3,4},{5,6},{7,8},{9,10},{11,12},{13,14},{15,0},{2,1},{4,3},... | collective-permute-start | bytes 786440 | tf_op jit(solution)/shard_map/ppermute | solution.py:377
  9.9 3.8 %collective-permute-start = (bf16[176,512]{1,0:T(8,128)(2,1)S(1)}, bf16[176,512]{1,0:T(8,128)(2,1)S(1)}, u32[]{:S(2)}, u32[]{:S(2)}) collective-permute-start(bf16[176,512]{1,0:T(8,128)(2,1)S(1)} %get-tuple-element.39), channel_id=1, source_target_pairs={{0,1},{1,0},{2,3},{3,2},{4,5},{5,4},{6,7},{7,6},{8,9},{9,8},{10,11... | collective-permute-start | bytes 540680 | tf_op jit(solution)/shard_map/ppermute | solution.py:260
  9.9 3.8 %collective-permute-start.1 = (bf16[176,512]{1,0:T(8,128)(2,1)S(1)}, bf16[176,512]{1,0:T(8,128)(2,1)S(1)}, u32[]{:S(2)}, u32[]{:S(2)}) collective-permute-start(bf16[176,512]{1,0:T(8,128)(2,1)S(1)} %get-tuple-element.40), channel_id=1, source_target_pairs={{0,1},{1,0},{2,3},{3,2},{4,5},{5,4},{6,7},{7,6},{8,9},{9,8},{10,11... | collective-permute-start | bytes 540680 | tf_op jit(solution)/shard_map/ppermute | solution.py:260
  10.4 3.3 %collective-permute-start.2 = (bf16[160,512]{1,0:T(8,128)(2,1)S(1)}, bf16[160,512]{1,0:T(8,128)(2,1)S(1)}, u32[]{:S(2)}, u32[]{:S(2)}) collective-permute-start(bf16[160,512]{1,0:T(8,128)(2,1)S(1)} %get-tuple-element.41), channel_id=1, source_target_pairs={{0,1},{1,0},{2,3},{3,2},{4,5},{5,4},{6,7},{7,6},{8,9},{9,8},{10,11... | collective-permute-start | bytes 491528 | tf_op jit(solution)/shard_map/ppermute | solution.py:260
  10.5 10.7 %collective-permute-start.3 = (bf16[256,512]{1,0:T(8,128)(2,1)S(1)}, bf16[256,512]{1,0:T(8,128)(2,1)S(1)}, u32[]{:S(2)}, u32[]{:S(2)}) collective-permute-start(bf16[256,512]{1,0:T(8,128)(2,1)S(1)} %get-tuple-element.43), channel_id=1, source_target_pairs={{1,2},{3,4},{5,6},{7,8},{9,10},{11,12},{13,14},{15,0},{2,1},{4,3},... | collective-permute-start | bytes 786440 | tf_op jit(solution)/shard_map/ppermute | solution.py:377
  13.7 1.4 %copy-start.1 = (f32[2048]{0:T(1024)S(1)}, f32[2048]{0:T(1024)}, u32[]{:S(2)}) copy-start(f32[2048]{0:T(1024)} %param.9) | copy-start | bytes 24580
  16.3 10.4 %collective-permute-start.5 = (bf16[256,512]{1,0:T(8,128)(2,1)S(1)}, bf16[256,512]{1,0:T(8,128)(2,1)S(1)}, u32[]{:S(2)}, u32[]{:S(2)}) collective-permute-start(bf16[256,512]{1,0:T(8,128)(2,1)S(1)} %get-tuple-element.47), channel_id=1, source_target_pairs={{1,2},{3,4},{5,6},{7,8},{9,10},{11,12},{13,14},{15,0},{2,1},{4,3},... | collective-permute-start | bytes 786440 | tf_op jit(solution)/shard_map/ppermute | solution.py:377
  23.6 8.6 %collective-permute-start.9 = (bf16[256,512]{1,0:T(8,128)(2,1)S(1)}, bf16[256,512]{1,0:T(8,128)(2,1)S(1)}, u32[]{:S(2)}, u32[]{:S(2)}) collective-permute-start(bf16[256,512]{1,0:T(8,128)(2,1)S(1)} %get-tuple-element.52), channel_id=1, source_target_pairs={{1,2},{3,4},{5,6},{7,8},{9,10},{11,12},{13,14},{15,0},{2,1},{4,3},... | collective-permute-start | bytes 786440 | tf_op jit(solution)/shard_map/ppermute | solution.py:377
  25.1 2.6 %collective-permute-start.6 = (bf16[176,512]{1,0:T(8,128)(2,1)S(1)}, bf16[176,512]{1,0:T(8,128)(2,1)S(1)}, u32[]{:S(2)}, u32[]{:S(2)}) collective-permute-start(bf16[176,512]{1,0:T(8,128)(2,1)S(1)} %get-tuple-element.48), channel_id=1, source_target_pairs={{0,1},{1,0},{2,3},{3,2},{4,5},{5,4},{6,7},{7,6},{8,9},{9,8},{10,11... | collective-permute-start | bytes 540680 | tf_op jit(solution)/shard_map/ppermute | solution.py:260
  25.2 2.6 %collective-permute-start.7 = (bf16[176,512]{1,0:T(8,128)(2,1)S(1)}, bf16[176,512]{1,0:T(8,128)(2,1)S(1)}, u32[]{:S(2)}, u32[]{:S(2)}) collective-permute-start(bf16[176,512]{1,0:T(8,128)(2,1)S(1)} %get-tuple-element.49), channel_id=1, source_target_pairs={{0,1},{1,0},{2,3},{3,2},{4,5},{5,4},{6,7},{7,6},{8,9},{9,8},{10,11... | collective-permute-start | bytes 540680 | tf_op jit(solution)/shard_map/ppermute | solution.py:260
  25.7 2.0 %collective-permute-start.8 = (bf16[160,512]{1,0:T(8,128)(2,1)S(1)}, bf16[160,512]{1,0:T(8,128)(2,1)S(1)}, u32[]{:S(2)}, u32[]{:S(2)}) collective-permute-start(bf16[160,512]{1,0:T(8,128)(2,1)S(1)} %get-tuple-element.50), channel_id=1, source_target_pairs={{0,1},{1,0},{2,3},{3,2},{4,5},{5,4},{6,7},{7,6},{8,9},{9,8},{10,11... | collective-permute-start | bytes 491528 | tf_op jit(solution)/shard_map/ppermute | solution.py:260
  33.1 2.6 %collective-permute-start.10 = (bf16[256,768]{1,0:T(8,128)(2,1)S(1)}, bf16[256,768]{1,0:T(8,128)(2,1)S(1)}, u32[]{:S(2)}, u32[]{:S(2)}) collective-permute-start(bf16[256,768]{1,0:T(8,128)(2,1)S(1)} %query_end.3), channel_id=1, source_target_pairs={{0,1},{2,3},{4,5},{6,7},{8,9},{10,11},{12,13},{14,15},{16,17},{18,... | collective-permute-start | bytes 1179656 | tf_op jit(solution)/shard_map/ppermute | solution.py:309
  35.9 2.4 %collective-permute-start.15 = (bf16[64,768]{1,0:T(8,128)(2,1)S(1)}, bf16[64,768]{1,0:T(8,128)(2,1)S(1)}, u32[]{:S(2)}, u32[]{:S(2)}) collective-permute-start(bf16[64,768]{1,0:T(8,128)(2,1)S(1)} %get-tuple-element.63), channel_id=1, source_target_pairs={{1,3},{3,1},{5,7},{7,5},{9,11},{11,9},{13,15},{15,13},{17,19},{19,... | collective-permute-start | bytes 294920 | tf_op jit(solution)/shard_map/ppermute | solution.py:312
  36.6 2.5 %collective-permute-start.11 = (bf16[64,768]{1,0:T(8,128)(2,1)S(1)}, bf16[64,768]{1,0:T(8,128)(2,1)S(1)}, u32[]{:S(2)}, u32[]{:S(2)}) collective-permute-start(bf16[64,768]{1,0:T(8,128)(2,1)S(1)} %get-tuple-element.61), channel_id=1, source_target_pairs={{1,5},{3,7},{5,1},{7,3},{9,13},{11,15},{13,9},{15,11},{17,21},{19,... | collective-permute-start | bytes 294920 | tf_op jit(solution)/shard_map/ppermute | solution.py:312
  38.4 2.8 %collective-permute-start.16 = (bf16[64,768]{1,0:T(8,128)(2,1)S(1)}, bf16[64,768]{1,0:T(8,128)(2,1)S(1)}, u32[]{:S(2)}, u32[]{:S(2)}) collective-permute-start(bf16[64,768]{1,0:T(8,128)(2,1)S(1)} %add.9.held), channel_id=1, source_target_pairs={{1,9},{3,11},{5,13},{7,15},{9,1},{11,3},{13,5},{15,7},{17,25},{19,... | collective-permute-start | bytes 294920 | tf_op jit(solution)/shard_map/ppermute | solution.py:312
  39.1 2.9 %collective-permute-start.12 = (bf16[64,768]{1,0:T(8,128)(2,1)S(1)}, bf16[64,768]{1,0:T(8,128)(2,1)S(1)}, u32[]{:S(2)}, u32[]{:S(2)}) collective-permute-start(bf16[64,768]{1,0:T(8,128)(2,1)S(1)} %add.6.held), channel_id=1, source_target_pairs={{1,3},{3,1},{5,7},{7,5},{9,11},{11,9},{13,15},{15,13},{17,19},{19,... | collective-permute-start | bytes 294920 | tf_op jit(solution)/shard_map/ppermute | solution.py:312
  41.2 2.9 %collective-permute-start.17 = (bf16[64,768]{1,0:T(8,128)(2,1)S(1)}, bf16[64,768]{1,0:T(8,128)(2,1)S(1)}, u32[]{:S(2)}, u32[]{:S(2)}) collective-permute-start(bf16[64,768]{1,0:T(8,128)(2,1)S(1)} %add.10.held), channel_id=1, source_target_pairs={{1,5},{3,7},{5,1},{7,3},{9,13},{11,15},{13,9},{15,11},{17,21},{19,... | collective-permute-start | bytes 294920 | tf_op jit(solution)/shard_map/ppermute | solution.py:312
  42.0 2.9 %collective-permute-start.13 = (bf16[64,768]{1,0:T(8,128)(2,1)S(1)}, bf16[64,768]{1,0:T(8,128)(2,1)S(1)}, u32[]{:S(2)}, u32[]{:S(2)}) collective-permute-start(bf16[64,768]{1,0:T(8,128)(2,1)S(1)} %add.7.held), channel_id=1, source_target_pairs={{1,9},{3,11},{5,13},{7,15},{9,1},{11,3},{13,5},{15,7},{17,25},{19,... | collective-permute-start | bytes 294920 | tf_op jit(solution)/shard_map/ppermute | solution.py:312
  44.1 4.3 %collective-permute-start.18 = (bf16[64,768]{1,0:T(8,128)(2,1)S(1)}, bf16[64,768]{1,0:T(8,128)(2,1)S(1)}, u32[]{:S(2)}, u32[]{:S(2)}) collective-permute-start(bf16[64,768]{1,0:T(8,128)(2,1)S(1)} %add.11.held), channel_id=1, source_target_pairs={{1,3},{3,1},{5,7},{7,5},{9,11},{11,9},{13,15},{15,13},{17,19},{19,... | collective-permute-start | bytes 294920 | tf_op jit(solution)/shard_map/ppermute | solution.py:312
  44.9 4.9 %collective-permute-start.14 = (bf16[64,768]{1,0:T(8,128)(2,1)S(1)}, bf16[64,768]{1,0:T(8,128)(2,1)S(1)}, u32[]{:S(2)}, u32[]{:S(2)}) collective-permute-start(bf16[64,768]{1,0:T(8,128)(2,1)S(1)} %add.8.held), channel_id=1, source_target_pairs={{1,5},{3,7},{5,1},{7,3},{9,13},{11,15},{13,9},{15,11},{17,21},{19,... | collective-permute-start | bytes 294920 | tf_op jit(solution)/shard_map/ppermute | solution.py:312
  48.5 19.3 %collective-permute-start.20 = (bf16[128,768]{1,0:T(8,128)(2,1)S(1)}, bf16[128,768]{1,0:T(8,128)(2,1)S(1)}, u32[]{:S(2)}, u32[]{:S(2)}) collective-permute-start(bf16[128,768]{1,0:T(8,128)(2,1)S(1)} %join.2.rest_0_.held), channel_id=1, source_target_pairs={{1,0},{3,2},{5,4},{7,6},{9,8},{11,10},{13,12},{15,14},{17,16},{19,... | collective-permute-start | bytes 589832 | tf_op jit(solution)/shard_map/ppermute | solution.py:350
  49.8 19.3 %collective-permute-start.19 = (bf16[128,768]{1,0:T(8,128)(2,1)S(1)}, bf16[128,768]{1,0:T(8,128)(2,1)S(1)}, u32[]{:S(2)}, u32[]{:S(2)}) collective-permute-start(bf16[128,768]{1,0:T(8,128)(2,1)S(1)} %join.3.held), channel_id=1, source_target_pairs={{1,0},{3,2},{5,4},{7,6},{9,8},{11,10},{13,12},{15,14},{17,16},{19,... | collective-permute-start | bytes 589832 | tf_op jit(solution)/shard_map/ppermute | solution.py:350

commit v14 on v13

--- a/solution.py
+++ b/solution.py
@@ -306,10 +306,10 @@
     rows, width = kept.shape
     if count & (count - 1) or count < 8:
         return lax.psum(kept, AXIS) * scale
-    got = lax.ppermute(sent, AXIS, [(i, i + 1) for i in range(0, count, 2)])
+    got = exchange(sent, 1)
 
     def chip_exchange(value, bit):
-        return lax.ppermute(value, AXIS, [(i, i ^ bit) for i in range(1, count, 2)])
+        return lax.ppermute(value, AXIS, [(i, i ^ bit if i % 2 else i) for i in range(count)])
 
     bits = [1 << k for k in range(1, count.bit_length() - 1)]
     orders = [[bits[0], *bits[2:], bits[1]], [bits[1], bits[0], *bits[2:]]]
@@ -347,7 +347,7 @@
                 flops=2 * 10**8,
             )(held[chain], got[chain], *after)
         )
-        handed.append(lax.ppermute(joined[chain], AXIS, [(i + 1, i) for i in range(0, count, 2)]))
+        handed.append(exchange(joined[chain], 1))
     begun = []
     for chain in range(2):
         begun = [

time: 70.1 us -> 66.9 us (0.954)
  waiting for transfers between devices: 20.9 us -> 1.74 us
  starting transfers between devices: 21.8 us -> 37.6 us
    ppermute x6 -> x9, starting transfers between devices: 1.29 us -> 20.2 us  [exchange(): return lax.ppermute(value, AXIS, [(i, i ^ mask) for i in range(count)])]
    ppermute x11 -> x8, waiting for transfers between devices: 17.6 us -> 0.02 us  [chip_exchange(): lax.ppermute(value, AXIS, [(i, i ^ bit if i % 2 else i) for i in range(co...]
    ppermute x11 -> x8, starting transfers between devices: 9.23 us -> 5.33 us  [chip_exchange(): lax.ppermute(value, AXIS, [(i, i ^ bit if i % 2 else i) for i in range(co...]
    ppermute x4, waiting for transfers between devices: 3.27 us -> 0.48 us  [off_swap(): return lax.ppermute(value, AXIS, off_route)]
    ppermute x6 -> x9, waiting for transfers between devices: 0.02 us -> 1.24 us  [exchange(): return lax.ppermute(value, AXIS, [(i, i ^ mask) for i in range(count)])]
    ppermute x4, starting transfers between devices: 11.2 us -> 12 us  [off_swap(): return lax.ppermute(value, AXIS, off_route)]
  transfers between devices with their start and end apart: 21 -> 21, of which waited for: 4 -> 3; matrix products, arithmetic and copies ran while one was open for 0% -> 0% of each run, Pallas kernels for 32% -> 33%
where the time goes in v14:
time: 66.9 us; the launch traced here: 66.5 us
  starting transfers between devices  37.6 us (56%)
  Pallas kernels  26.2 us (39%)
  waiting for transfers between devices  1.74 us (3%)
  between operations  1.06 us (2%)
    ppermute x9, starting transfers between devices, exchange(): return lax.ppermute(value, AXIS, [(i, i ^ mask) for i in range(count)])  20.2 us
    ppermute x4, starting transfers between devices, off_swap(): return lax.ppermute(value, AXIS, off_route)  12 us
    pallas_call x4, Pallas kernels, per_device(): call(functools.partial(embed_kernel, blocks=blocks, g=g, scale=1.0 / math...  6.8 us
    ppermute x8, starting transfers between devices, chip_exchange(): lax.ppermute(value, AXIS, [(i, i ^ bit if i % 2 else i) for i in range(co...  5.33 us
    pallas_call x2, Pallas kernels, signal_of(): call(functools.partial(signal_kernel, slot=slot), 'signal', [SMEM] + [VME...  3.53 us
    pallas_call x1, Pallas kernels, per_device(): call(hits_kernel, 'hits', [VMEM, HBM], [in_vmem(full, BF16), in_vmem(edge...  2.45 us
    pallas_call x1, Pallas kernels, per_device(): call(functools.partial(project_kernel, scale=scale), 'project', [HBM] * 3...  2.03 us
    pallas_call x2, Pallas kernels, query_end(): call(functools.partial(query_end_kernel, blocks=blocks), 'query_end', [SM...  1.9 us
  transfers between devices with their start and end apart: 21, of which 3 were waited for; matrix products, arithmetic and copies ran while one was open for 0% of the time, Pallas kernels for 33%

profile of v14, /device:TPU:0, one launch (start us, length us, event | category | flops | bytes accessed | tf_op | source)
XLA Modules:
  0.0 66.5 jit_solution(4735761424422000890)
XLA Ops:
  0.7 2.0 %project.1 = (bf16[256,512]{1,0:T(8,128)(2,1)S(1)}, bf16[256,768]{1,0:T(8,128)(2,1)S(1)}, bf16[2048,768]{1,0:T(8,128)(2,1)S(1)}) custom-call(s32[2,64]{1,0:T(2,128)} %bitcast.3, bf16[256,768]{1,0:T(8,128)(2,1)} %queries.1, bf16[2048,768]{1,0:T(8,128)(2,1)} %embeddings.1), custom_call_target="tpu_custom_call" | custom-call | tf_op jit(solution)/shard_map/project/pallas_call | solution.py:389
  2.7 5.7 %collective-permute-start.4 = (bf16[256,512]{1,0:T(8,128)(2,1)S(1)}, bf16[256,512]{1,0:T(8,128)(2,1)S(1)}, u32[]{:S(2)}, u32[]{:S(2)}) collective-permute-start(bf16[256,512]{1,0:T(8,128)(2,1)S(1)} %get-tuple-element.44), channel_id=1, source_target_pairs={{1,2},{3,4},{5,6},{7,8},{9,10},{11,12},{13,14},{15,0},{2,1},{4,3},... | collective-permute-start | bytes 786440 | tf_op jit(solution)/shard_map/ppermute | solution.py:377
  8.4 1.6 %own.1 = (f32[4,256,512]{2,1,0:T(8,128)S(1)}, bf16[256,512]{1,0:T(8,128)(2,1)S(1)}, bf16[176,512]{1,0:T(8,128)(2,1)S(1)}, bf16[176,512]{1,0:T(8,128)(2,1)S(1)}, bf16[160,512]{1,0:T(8,128)(2,1)S(1)}) custom-call(s32[2,64]{1,0:T(2,128)S(1)} %bitcast.4, bf16[256,768]{1,0:T(8,128)(2,1)S(1)} %get-tuple-element.35.queries, ...), custom_call_target="tpu_custom_call" | custom-call | tf_op jit(solution)/shard_map/own/pallas_call | solution.py:397
  11.3 2.4 %hits.1 = (bf16[4,256,512]{2,1,0:T(8,128)(2,1)S(1)}, bf16[4,2,512,512]{3,2,1,0:T(8,128)(2,1)S(1)}) custom-call(s32[8,256]{1,0:T(8,128)S(1)} %bitcast.19, bf16[4,2,512,512]{3,2,1,0:T(8,128)(2,1)} %tiles.1), custom_call_target="tpu_custom_call" | custom-call | tf_op jit(solution)/shard_map/hits/pallas_call | solution.py:404
  13.8 1.3 %base.1 = f32[4,256,512]{2,1,0:T(8,128)S(1)} custom-call(s32[2,64]{1,0:T(2,128)S(1)} %bitcast.5, f32[4,256,512]{2,1,0:T(8,128)S(1)} %get-tuple-element.37.own, bf16[4,2,512,512]{3,2,1,0:T(8,128)(2,1)S(1)} %get-tuple-element.38.tiles, bf16[176,512]{1,0:T(8,128)(2,1)S(1)} %collective-permute-done.rest_0_, bf16[176,512]{1,0:T(8,128)(2,1)S(1)} %collective-permute-done.1.rest_1_, ...), custom_call_target="tpu_custom_call" | custom-call | tf_op jit(solution)/shard_map/base/pallas_call | solution.py:412
  15.2 2.3 %signal.2 = (bf16[4,256,512]{2,1,0:T(8,128)(2,1)S(1)}, bf16[256,512]{1,0:T(8,128)(2,1)S(1)}) custom-call(s32[2,64]{1,0:T(2,128)S(1)} %bitcast.6, f32[4,256,512]{2,1,0:T(8,128)S(1)} %base.1, bf16[4,256,512]{2,1,0:T(8,128)(2,1)S(1)} %get-tuple-element.42.hits, f32[1,2048]{1,0:T(1,128)S(1)} %bitcast.17, bf16[256,512]{1,0:T(8,128)(2,1)S(1)} %collective-permute-done.4.received, ...), custom_call_target="tpu_custom_call" | custom-call | flops 2000000000 | tf_op jit(solution)/shard_map/signal/pallas_call | solution.py:422
  17.5 2.7 %collective-permute-start.5 = (bf16[256,512]{1,0:T(8,128)(2,1)S(1)}, bf16[256,512]{1,0:T(8,128)(2,1)S(1)}, u32[]{:S(2)}, u32[]{:S(2)}) collective-permute-start(bf16[256,512]{1,0:T(8,128)(2,1)S(1)} %get-tuple-element.47), channel_id=1, source_target_pairs={{1,2},{3,4},{5,6},{7,8},{9,10},{11,12},{13,14},{15,0},{2,1},{4,3},... | collective-permute-start | bytes 786440 | tf_op jit(solution)/shard_map/ppermute | solution.py:377
  20.3 1.2 %signal.3 = (bf16[4,256,512]{2,1,0:T(8,128)(2,1)S(1)}, bf16[256,512]{1,0:T(8,128)(2,1)S(1)}) custom-call(s32[2,64]{1,0:T(2,128)S(1)} %bitcast.7, f32[4,256,512]{2,1,0:T(8,128)S(1)} %base.1, bf16[4,256,512]{2,1,0:T(8,128)(2,1)S(1)} %get-tuple-element.42.hits, f32[1,2048]{1,0:T(1,128)S(1)} %bitcast.18, ...), custom_call_target="tpu_custom_call", output_to_operand_aliasing={{0}: (6, {})} | custom-call | tf_op jit(solution)/shard_map/signal/pallas_call | solution.py:422
  21.5 3.0 %collective-permute-start.9 = (bf16[256,512]{1,0:T(8,128)(2,1)S(1)}, bf16[256,512]{1,0:T(8,128)(2,1)S(1)}, u32[]{:S(2)}, u32[]{:S(2)}) collective-permute-start(bf16[256,512]{1,0:T(8,128)(2,1)S(1)} %get-tuple-element.52), channel_id=1, source_target_pairs={{1,2},{3,4},{5,6},{7,8},{9,10},{11,12},{13,14},{15,0},{2,1},{4,3},... | collective-permute-start | bytes 786440 | tf_op jit(solution)/shard_map/ppermute | solution.py:377
  24.5 1.4 %push.1 = (bf16[176,512]{1,0:T(8,128)(2,1)S(1)}, bf16[176,512]{1,0:T(8,128)(2,1)S(1)}, bf16[160,512]{1,0:T(8,128)(2,1)S(1)}) custom-call(s32[2,64]{1,0:T(2,128)S(1)} %bitcast.8, bf16[4,256,512]{2,1,0:T(8,128)(2,1)S(1)} %get-tuple-element.46.signal, bf16[4,2,512,512]{3,2,1,0:T(8,128)(2,1)S(1)} %get-tuple-element.38.tiles), custom_call_target="tpu_custom_call" | custom-call | tf_op jit(solution)/shard_map/push/pallas_call | solution.py:436
  26.5 1.0 %query.1.part = f32[256,768]{1,0:T(8,128)S(1)} custom-call(bf16[4,256,512]{2,1,0:T(8,128)(2,1)S(1)} %get-tuple-element.46.signal, bf16[2048,768]{1,0:T(8,128)(2,1)S(1)} %get-tuple-element.36.embeddings), custom_call_target="tpu_custom_call" | custom-call | tf_op jit(solution)/shard_map/query/pallas_call | solution.py:446
  27.5 1.0 %query_half.1.part = f32[256,768]{1,0:T(8,128)S(1)} custom-call(s32[2,64]{1,0:T(2,128)S(1)} %bitcast.9, f32[256,768]{1,0:T(8,128)S(1)} %query.1.part, bf16[256,512]{1,0:T(8,128)(2,1)S(1)} %collective-permute-done.5.received.off_a, bf16[2048,768]{1,0:T(8,128)(2,1)S(1)} %get-tuple-element.36.embeddings), custom_call_target="tpu_custom_call" | custom-call | flops 1000000000 | tf_op jit(solution)/shard_map/query_half/pallas_call | solution.py:447
  28.5 1.2 %query_on.1 = (f32[256,768]{1,0:T(8,128)S(1)}, bf16[2,256,512]{2,1,0:T(8,128)(2,1)S(1)}) custom-call(s32[2,64]{1,0:T(2,128)S(1)} %bitcast.10, f32[256,768]{1,0:T(8,128)S(1)} %query_half.1.part, bf16[2048,768]{1,0:T(8,128)(2,1)S(1)} %get-tuple-element.36.embeddings, bf16[176,512]{1,0:T(8,128)(2,1)S(1)} %collective-permute-done.6.rest_0_, ...), custom_call_target="tpu_custom_call" | custom-call | tf_op jit(solution)/shard_map/query_on/pallas_call | solution.py:454
  30.1 0.9 %query_end.3 = bf16[256,768]{1,0:T(8,128)(2,1)S(1)} custom-call(s32[2,64]{1,0:T(2,128)S(1)} %bitcast.11, f32[256,768]{1,0:T(8,128)S(1)} %get-tuple-element.59.part, bf16[256,512]{1,0:T(8,128)(2,1)S(1)} %collective-permute-done.9.off_b.received, bf16[2048,768]{1,0:T(8,128)(2,1)S(1)} %get-tuple-element.36.embeddings), custom_call_target="tpu_custom_call" | custom-call | tf_op jit(solution)/shard_map/query_end/pallas_call | solution.py:458
  31.1 1.5 %collective-permute-start.10 = (bf16[256,768]{1,0:T(8,128)(2,1)S(1)}, bf16[256,768]{1,0:T(8,128)(2,1)S(1)}, u32[]{:S(2)}, u32[]{:S(2)}) collective-permute-start(bf16[256,768]{1,0:T(8,128)(2,1)S(1)} %query_end.3), channel_id=1, source_target_pairs={{0,1},{1,0},{2,3},{3,2},{4,5},{5,4},{6,7},{7,6},{8,9},{9,8},{10,11... | collective-permute-start | bytes 1179656 | tf_op jit(solution)/shard_map/ppermute | solution.py:260
  32.6 1.0 %query_end.2.held = f32[256,768]{1,0:T(8,128)S(1)} custom-call(s32[2,64]{1,0:T(2,128)S(1)} %bitcast.12, f32[256,768]{1,0:T(8,128)S(1)} %get-tuple-element.59.part, bf16[256,512]{1,0:T(8,128)(2,1)S(1)} %collective-permute-done.9.off_b.received, bf16[2048,768]{1,0:T(8,128)(2,1)S(1)} %get-tuple-element.36.embeddings), custom_call_target="tpu_custom_call" | custom-call | tf_op jit(solution)/shard_map/query_end/pallas_call | solution.py:458
  34.1 0.7 %collective-permute-start.15 = (bf16[64,768]{1,0:T(8,128)(2,1)S(1)}, bf16[64,768]{1,0:T(8,128)(2,1)S(1)}, u32[]{:S(2)}, u32[]{:S(2)}) collective-permute-start(bf16[64,768]{1,0:T(8,128)(2,1)S(1)} %get-tuple-element.63), channel_id=1, source_target_pairs={{0,0},{1,3},{2,2},{3,1},{4,4},{5,7},{6,6},{7,5},{8,8},{9,11},{10,1... | collective-permute-start | bytes 294920 | tf_op jit(solution)/shard_map/ppermute | solution.py:312
  34.8 0.7 %collective-permute-start.11 = (bf16[64,768]{1,0:T(8,128)(2,1)S(1)}, bf16[64,768]{1,0:T(8,128)(2,1)S(1)}, u32[]{:S(2)}, u32[]{:S(2)}) collective-permute-start(bf16[64,768]{1,0:T(8,128)(2,1)S(1)} %get-tuple-element.61), channel_id=1, source_target_pairs={{0,0},{1,5},{2,2},{3,7},{4,4},{5,1},{6,6},{7,3},{8,8},{9,13},{10,1... | collective-permute-start | bytes 294920 | tf_op jit(solution)/shard_map/ppermute | solution.py:312
  35.4 1.1 %embed.4 = (bf16[512,768]{1,0:T(8,128)(2,1)S(1)}, f32[8,128]{1,0:T(8,128)S(1)}) custom-call(s32[2,64]{1,0:T(2,128)S(1)} %bitcast.13, bf16[4,256,512]{2,1,0:T(8,128)(2,1)S(1)} %get-tuple-element.46.signal, bf16[2,256,512]{2,1,0:T(8,128)(2,1)S(1)} %get-tuple-element.51.on, bf16[256,512]{1,0:T(8,128)(2,1)S(1)} %collective-permute-done.5.received.off_a, ...), custom_call_target="tpu_custom_call" | custom-call | tf_op jit(solution)/shard_map/embed/pallas_call | solution.py:470
  36.6 0.7 %collective-permute-start.16 = (bf16[64,768]{1,0:T(8,128)(2,1)S(1)}, bf16[64,768]{1,0:T(8,128)(2,1)S(1)}, u32[]{:S(2)}, u32[]{:S(2)}) collective-permute-start(bf16[64,768]{1,0:T(8,128)(2,1)S(1)} %add.9.held), channel_id=1, source_target_pairs={{0,0},{1,9},{2,2},{3,11},{4,4},{5,13},{6,6},{7,15},{8,8},{9,1},{10... | collective-permute-start | bytes 294920 | tf_op jit(solution)/shard_map/ppermute | solution.py:312
  37.3 0.7 %collective-permute-start.12 = (bf16[64,768]{1,0:T(8,128)(2,1)S(1)}, bf16[64,768]{1,0:T(8,128)(2,1)S(1)}, u32[]{:S(2)}, u32[]{:S(2)}) collective-permute-start(bf16[64,768]{1,0:T(8,128)(2,1)S(1)} %add.6.held), channel_id=1, source_target_pairs={{0,0},{1,3},{2,2},{3,1},{4,4},{5,7},{6,6},{7,5},{8,8},{9,11},{10,1... | collective-permute-start | bytes 294920 | tf_op jit(solution)/shard_map/ppermute | solution.py:312
  37.9 1.4 %embed.5 = (bf16[2048,768]{1,0:T(8,128)(2,1)}, bf16[512,768]{1,0:T(8,128)(2,1)S(1)}, f32[8,128]{1,0:T(8,128)S(1)}) custom-call(s32[2,64]{1,0:T(2,128)S(1)} %bitcast.14, bf16[4,256,512]{2,1,0:T(8,128)(2,1)S(1)} %get-tuple-element.46.signal, bf16[2,256,512]{2,1,0:T(8,128)(2,1)S(1)} %get-tuple-element.51.on, ...), custom_call_target="tpu_custom_call" | custom-call | tf_op jit(solution)/shard_map/embed/pallas_call | solution.py:470
  39.4 0.7 %collective-permute-start.17 = (bf16[64,768]{1,0:T(8,128)(2,1)S(1)}, bf16[64,768]{1,0:T(8,128)(2,1)S(1)}, u32[]{:S(2)}, u32[]{:S(2)}) collective-permute-start(bf16[64,768]{1,0:T(8,128)(2,1)S(1)} %add.10.held), channel_id=1, source_target_pairs={{0,0},{1,5},{2,2},{3,7},{4,4},{5,1},{6,6},{7,3},{8,8},{9,13},{10,1... | collective-permute-start | bytes 294920 | tf_op jit(solution)/shard_map/ppermute | solution.py:312
  40.2 0.7 %collective-permute-start.13 = (bf16[64,768]{1,0:T(8,128)(2,1)S(1)}, bf16[64,768]{1,0:T(8,128)(2,1)S(1)}, u32[]{:S(2)}, u32[]{:S(2)}) collective-permute-start(bf16[64,768]{1,0:T(8,128)(2,1)S(1)} %add.7.held), channel_id=1, source_target_pairs={{0,0},{1,9},{2,2},{3,11},{4,4},{5,13},{6,6},{7,15},{8,8},{9,1},{10... | collective-permute-start | bytes 294920 | tf_op jit(solution)/shard_map/ppermute | solution.py:312
  40.8 1.5 %embed.6 = (bf16[2048,768]{1,0:T(8,128)(2,1)}, bf16[512,768]{1,0:T(8,128)(2,1)S(1)}, f32[8,128]{1,0:T(8,128)S(1)}) custom-call(s32[2,64]{1,0:T(2,128)S(1)} %bitcast.15, bf16[4,256,512]{2,1,0:T(8,128)(2,1)S(1)} %get-tuple-element.46.signal, bf16[2,256,512]{2,1,0:T(8,128)(2,1)S(1)} %get-tuple-element.51.on, ...), custom_call_target="tpu_custom_call", output_to_operand_aliasing={{0}: (7, {})} | custom-call | tf_op jit(solution)/shard_map/embed/pallas_call | solution.py:470
  42.3 0.7 %collective-permute-start.18 = (bf16[64,768]{1,0:T(8,128)(2,1)S(1)}, bf16[64,768]{1,0:T(8,128)(2,1)S(1)}, u32[]{:S(2)}, u32[]{:S(2)}) collective-permute-start(bf16[64,768]{1,0:T(8,128)(2,1)S(1)} %add.11.held), channel_id=1, source_target_pairs={{0,0},{1,3},{2,2},{3,1},{4,4},{5,7},{6,6},{7,5},{8,8},{9,11},{10,1... | collective-permute-start | bytes 294920 | tf_op jit(solution)/shard_map/ppermute | solution.py:312
  43.1 0.7 %collective-permute-start.14 = (bf16[64,768]{1,0:T(8,128)(2,1)S(1)}, bf16[64,768]{1,0:T(8,128)(2,1)S(1)}, u32[]{:S(2)}, u32[]{:S(2)}) collective-permute-start(bf16[64,768]{1,0:T(8,128)(2,1)S(1)} %add.8.held), channel_id=1, source_target_pairs={{0,0},{1,5},{2,2},{3,7},{4,4},{5,1},{6,6},{7,3},{8,8},{9,13},{10,1... | collective-permute-start | bytes 294920 | tf_op jit(solution)/shard_map/ppermute | solution.py:312
  43.8 2.8 %embed.7 = (bf16[2048,768]{1,0:T(8,128)(2,1)}, bf16[512,768]{1,0:T(8,128)(2,1)}, f32[8,128]{1,0:T(8,128)S(1)}) custom-call(s32[2,64]{1,0:T(2,128)S(1)} %bitcast.16, bf16[4,256,512]{2,1,0:T(8,128)(2,1)S(1)} %get-tuple-element.46.signal, bf16[2,256,512]{2,1,0:T(8,128)(2,1)S(1)} %get-tuple-element.51.on, ...), custom_call_target="tpu_custom_call", output_to_operand_aliasing={{0}: (7, {})} | custom-call | tf_op jit(solution)/shard_map/embed/pallas_call | solution.py:470
  46.7 17.2 %collective-permute-start.20 = (bf16[128,768]{1,0:T(8,128)(2,1)S(1)}, bf16[128,768]{1,0:T(8,128)(2,1)S(1)}, u32[]{:S(2)}, u32[]{:S(2)}) collective-permute-start(bf16[128,768]{1,0:T(8,128)(2,1)S(1)} %join.2.rest_0_.held), channel_id=1, source_target_pairs={{0,1},{1,0},{2,3},{3,2},{4,5},{5,4},{6,7},{7,6},{8,9},{9,8},{10,11... | collective-permute-start | bytes 589832 | tf_op jit(solution)/shard_map/ppermute | solution.py:260
  64.1 0.8 %collective-permute-done.20.got = bf16[128,768]{1,0:T(8,128)(2,1)S(1)} collective-permute-done((bf16[128,768]{1,0:T(8,128)(2,1)S(1)}, bf16[128,768]{1,0:T(8,128)(2,1)S(1)}, u32[]{:S(2)}, u32[]{:S(2)}) %collective-permute-start.20) | collective-permute-done | bytes 196640 | tf_op jit(solution)/shard_map/ppermute | solution.py:260
  64.9 0.8 %place.2.rest_0_ = f32[256,768]{1,0:T(8,128)} custom-call(bf16[128,768]{1,0:T(8,128)(2,1)S(1)} %join.2.rest_0_.held, bf16[128,768]{1,0:T(8,128)(2,1)S(1)} %collective-permute-done.20.got), custom_call_target="tpu_custom_call" | custom-call | tf_op jit(solution)/shard_map/place/pallas_call | solution.py:354
  65.7 0.8 %place.3 = f32[256,768]{1,0:T(8,128)} custom-call(bf16[128,768]{1,0:T(8,128)(2,1)S(1)} %join.3.held, bf16[128,768]{1,0:T(8,128)(2,1)S(1)} %collective-permute-done.19.got, f32[256,768]{1,0:T(8,128)} %place.2.rest_0_), custom_call_target="tpu_custom_call", output_to_operand_aliasing={{}: (2, {})} | custom-call | tf_op jit(solution)/shard_map/place/pallas_call | solution.py:354
  (43 shorter events, 3.4 us)
Async XLA Ops:
  0.6 7.7 %copy-start = (s32[64,2]{0,1:T(2,128)S(1)}, s32[64,2]{0,1:T(2,128)}, u32[]{:S(2)}) copy-start(s32[64,2]{0,1:T(2,128)} %param.8) | copy-start | bytes 1540
  0.6 10.7 %copy-start.2 = (s32[256,8]{0,1:T(8,128)S(1)}, s32[256,8]{0,1:T(8,128)}, u32[]{:S(2)}) copy-start(s32[256,8]{0,1:T(8,128)} %param.11) | copy-start | bytes 24580
  2.7 12.5 %collective-permute-start.4 = (bf16[256,512]{1,0:T(8,128)(2,1)S(1)}, bf16[256,512]{1,0:T(8,128)(2,1)S(1)}, u32[]{:S(2)}, u32[]{:S(2)}) collective-permute-start(bf16[256,512]{1,0:T(8,128)(2,1)S(1)} %get-tuple-element.44), channel_id=1, source_target_pairs={{1,2},{3,4},{5,6},{7,8},{9,10},{11,12},{13,14},{15,0},{2,1},{4,3},... | collective-permute-start | bytes 786440 | tf_op jit(solution)/shard_map/ppermute | solution.py:377
  10.0 3.7 %collective-permute-start = (bf16[176,512]{1,0:T(8,128)(2,1)S(1)}, bf16[176,512]{1,0:T(8,128)(2,1)S(1)}, u32[]{:S(2)}, u32[]{:S(2)}) collective-permute-start(bf16[176,512]{1,0:T(8,128)(2,1)S(1)} %get-tuple-element.39), channel_id=1, source_target_pairs={{0,1},{1,0},{2,3},{3,2},{4,5},{5,4},{6,7},{7,6},{8,9},{9,8},{10,11... | collective-permute-start | bytes 540680 | tf_op jit(solution)/shard_map/ppermute | solution.py:260
  10.1 3.7 %collective-permute-start.1 = (bf16[176,512]{1,0:T(8,128)(2,1)S(1)}, bf16[176,512]{1,0:T(8,128)(2,1)S(1)}, u32[]{:S(2)}, u32[]{:S(2)}) collective-permute-start(bf16[176,512]{1,0:T(8,128)(2,1)S(1)} %get-tuple-element.40), channel_id=1, source_target_pairs={{0,1},{1,0},{2,3},{3,2},{4,5},{5,4},{6,7},{7,6},{8,9},{9,8},{10,11... | collective-permute-start | bytes 540680 | tf_op jit(solution)/shard_map/ppermute | solution.py:260
  10.6 3.2 %collective-permute-start.2 = (bf16[160,512]{1,0:T(8,128)(2,1)S(1)}, bf16[160,512]{1,0:T(8,128)(2,1)S(1)}, u32[]{:S(2)}, u32[]{:S(2)}) collective-permute-start(bf16[160,512]{1,0:T(8,128)(2,1)S(1)} %get-tuple-element.41), channel_id=1, source_target_pairs={{0,1},{1,0},{2,3},{3,2},{4,5},{5,4},{6,7},{7,6},{8,9},{9,8},{10,11... | collective-permute-start | bytes 491528 | tf_op jit(solution)/shard_map/ppermute | solution.py:260
  10.7 9.6 %collective-permute-start.3 = (bf16[256,512]{1,0:T(8,128)(2,1)S(1)}, bf16[256,512]{1,0:T(8,128)(2,1)S(1)}, u32[]{:S(2)}, u32[]{:S(2)}) collective-permute-start(bf16[256,512]{1,0:T(8,128)(2,1)S(1)} %get-tuple-element.43), channel_id=1, source_target_pairs={{1,2},{3,4},{5,6},{7,8},{9,10},{11,12},{13,14},{15,0},{2,1},{4,3},... | collective-permute-start | bytes 786440 | tf_op jit(solution)/shard_map/ppermute | solution.py:377
  13.8 1.4 %copy-start.1 = (f32[2048]{0:T(1024)S(1)}, f32[2048]{0:T(1024)}, u32[]{:S(2)}) copy-start(f32[2048]{0:T(1024)} %param.9) | copy-start | bytes 24580
  17.5 10.0 %collective-permute-start.5 = (bf16[256,512]{1,0:T(8,128)(2,1)S(1)}, bf16[256,512]{1,0:T(8,128)(2,1)S(1)}, u32[]{:S(2)}, u32[]{:S(2)}) collective-permute-start(bf16[256,512]{1,0:T(8,128)(2,1)S(1)} %get-tuple-element.47), channel_id=1, source_target_pairs={{1,2},{3,4},{5,6},{7,8},{9,10},{11,12},{13,14},{15,0},{2,1},{4,3},... | collective-permute-start | bytes 786440 | tf_op jit(solution)/shard_map/ppermute | solution.py:377
  21.5 8.7 %collective-permute-start.9 = (bf16[256,512]{1,0:T(8,128)(2,1)S(1)}, bf16[256,512]{1,0:T(8,128)(2,1)S(1)}, u32[]{:S(2)}, u32[]{:S(2)}) collective-permute-start(bf16[256,512]{1,0:T(8,128)(2,1)S(1)} %get-tuple-element.52), channel_id=1, source_target_pairs={{1,2},{3,4},{5,6},{7,8},{9,10},{11,12},{13,14},{15,0},{2,1},{4,3},... | collective-permute-start | bytes 786440 | tf_op jit(solution)/shard_map/ppermute | solution.py:377
  25.9 2.6 %collective-permute-start.6 = (bf16[176,512]{1,0:T(8,128)(2,1)S(1)}, bf16[176,512]{1,0:T(8,128)(2,1)S(1)}, u32[]{:S(2)}, u32[]{:S(2)}) collective-permute-start(bf16[176,512]{1,0:T(8,128)(2,1)S(1)} %get-tuple-element.48), channel_id=1, source_target_pairs={{0,1},{1,0},{2,3},{3,2},{4,5},{5,4},{6,7},{7,6},{8,9},{9,8},{10,11... | collective-permute-start | bytes 540680 | tf_op jit(solution)/shard_map/ppermute | solution.py:260
  25.9 2.6 %collective-permute-start.7 = (bf16[176,512]{1,0:T(8,128)(2,1)S(1)}, bf16[176,512]{1,0:T(8,128)(2,1)S(1)}, u32[]{:S(2)}, u32[]{:S(2)}) collective-permute-start(bf16[176,512]{1,0:T(8,128)(2,1)S(1)} %get-tuple-element.49), channel_id=1, source_target_pairs={{0,1},{1,0},{2,3},{3,2},{4,5},{5,4},{6,7},{7,6},{8,9},{9,8},{10,11... | collective-permute-start | bytes 540680 | tf_op jit(solution)/shard_map/ppermute | solution.py:260
  26.4 2.0 %collective-permute-start.8 = (bf16[160,512]{1,0:T(8,128)(2,1)S(1)}, bf16[160,512]{1,0:T(8,128)(2,1)S(1)}, u32[]{:S(2)}, u32[]{:S(2)}) collective-permute-start(bf16[160,512]{1,0:T(8,128)(2,1)S(1)} %get-tuple-element.50), channel_id=1, source_target_pairs={{0,1},{1,0},{2,3},{3,2},{4,5},{5,4},{6,7},{7,6},{8,9},{9,8},{10,11... | collective-permute-start | bytes 491528 | tf_op jit(solution)/shard_map/ppermute | solution.py:260
  31.1 2.8 %collective-permute-start.10 = (bf16[256,768]{1,0:T(8,128)(2,1)S(1)}, bf16[256,768]{1,0:T(8,128)(2,1)S(1)}, u32[]{:S(2)}, u32[]{:S(2)}) collective-permute-start(bf16[256,768]{1,0:T(8,128)(2,1)S(1)} %query_end.3), channel_id=1, source_target_pairs={{0,1},{1,0},{2,3},{3,2},{4,5},{5,4},{6,7},{7,6},{8,9},{9,8},{10,11... | collective-permute-start | bytes 1179656 | tf_op jit(solution)/shard_map/ppermute | solution.py:260
  34.1 2.4 %collective-permute-start.15 = (bf16[64,768]{1,0:T(8,128)(2,1)S(1)}, bf16[64,768]{1,0:T(8,128)(2,1)S(1)}, u32[]{:S(2)}, u32[]{:S(2)}) collective-permute-start(bf16[64,768]{1,0:T(8,128)(2,1)S(1)} %get-tuple-element.63), channel_id=1, source_target_pairs={{0,0},{1,3},{2,2},{3,1},{4,4},{5,7},{6,6},{7,5},{8,8},{9,11},{10,1... | collective-permute-start | bytes 294920 | tf_op jit(solution)/shard_map/ppermute | solution.py:312
  34.8 2.5 %collective-permute-start.11 = (bf16[64,768]{1,0:T(8,128)(2,1)S(1)}, bf16[64,768]{1,0:T(8,128)(2,1)S(1)}, u32[]{:S(2)}, u32[]{:S(2)}) collective-permute-start(bf16[64,768]{1,0:T(8,128)(2,1)S(1)} %get-tuple-element.61), channel_id=1, source_target_pairs={{0,0},{1,5},{2,2},{3,7},{4,4},{5,1},{6,6},{7,3},{8,8},{9,13},{10,1... | collective-permute-start | bytes 294920 | tf_op jit(solution)/shard_map/ppermute | solution.py:312
  36.6 2.8 %collective-permute-start.16 = (bf16[64,768]{1,0:T(8,128)(2,1)S(1)}, bf16[64,768]{1,0:T(8,128)(2,1)S(1)}, u32[]{:S(2)}, u32[]{:S(2)}) collective-permute-start(bf16[64,768]{1,0:T(8,128)(2,1)S(1)} %add.9.held), channel_id=1, source_target_pairs={{0,0},{1,9},{2,2},{3,11},{4,4},{5,13},{6,6},{7,15},{8,8},{9,1},{10... | collective-permute-start | bytes 294920 | tf_op jit(solution)/shard_map/ppermute | solution.py:312
  37.3 2.9 %collective-permute-start.12 = (bf16[64,768]{1,0:T(8,128)(2,1)S(1)}, bf16[64,768]{1,0:T(8,128)(2,1)S(1)}, u32[]{:S(2)}, u32[]{:S(2)}) collective-permute-start(bf16[64,768]{1,0:T(8,128)(2,1)S(1)} %add.6.held), channel_id=1, source_target_pairs={{0,0},{1,3},{2,2},{3,1},{4,4},{5,7},{6,6},{7,5},{8,8},{9,11},{10,1... | collective-permute-start | bytes 294920 | tf_op jit(solution)/shard_map/ppermute | solution.py:312
  39.4 2.9 %collective-permute-start.17 = (bf16[64,768]{1,0:T(8,128)(2,1)S(1)}, bf16[64,768]{1,0:T(8,128)(2,1)S(1)}, u32[]{:S(2)}, u32[]{:S(2)}) collective-permute-start(bf16[64,768]{1,0:T(8,128)(2,1)S(1)} %add.10.held), channel_id=1, source_target_pairs={{0,0},{1,5},{2,2},{3,7},{4,4},{5,1},{6,6},{7,3},{8,8},{9,13},{10,1... | collective-permute-start | bytes 294920 | tf_op jit(solution)/shard_map/ppermute | solution.py:312
  40.2 2.9 %collective-permute-start.13 = (bf16[64,768]{1,0:T(8,128)(2,1)S(1)}, bf16[64,768]{1,0:T(8,128)(2,1)S(1)}, u32[]{:S(2)}, u32[]{:S(2)}) collective-permute-start(bf16[64,768]{1,0:T(8,128)(2,1)S(1)} %add.7.held), channel_id=1, source_target_pairs={{0,0},{1,9},{2,2},{3,11},{4,4},{5,13},{6,6},{7,15},{8,8},{9,1},{10... | collective-permute-start | bytes 294920 | tf_op jit(solution)/shard_map/ppermute | solution.py:312
  42.3 4.3 %collective-permute-start.18 = (bf16[64,768]{1,0:T(8,128)(2,1)S(1)}, bf16[64,768]{1,0:T(8,128)(2,1)S(1)}, u32[]{:S(2)}, u32[]{:S(2)}) collective-permute-start(bf16[64,768]{1,0:T(8,128)(2,1)S(1)} %add.11.held), channel_id=1, source_target_pairs={{0,0},{1,3},{2,2},{3,1},{4,4},{5,7},{6,6},{7,5},{8,8},{9,11},{10,1... | collective-permute-start | bytes 294920 | tf_op jit(solution)/shard_map/ppermute | solution.py:312
  43.1 20.8 %collective-permute-start.14 = (bf16[64,768]{1,0:T(8,128)(2,1)S(1)}, bf16[64,768]{1,0:T(8,128)(2,1)S(1)}, u32[]{:S(2)}, u32[]{:S(2)}) collective-permute-start(bf16[64,768]{1,0:T(8,128)(2,1)S(1)} %add.8.held), channel_id=1, source_target_pairs={{0,0},{1,5},{2,2},{3,7},{4,4},{5,1},{6,6},{7,3},{8,8},{9,13},{10,1... | collective-permute-start | bytes 294920 | tf_op jit(solution)/shard_map/ppermute | solution.py:312
  46.7 18.3 %collective-permute-start.20 = (bf16[128,768]{1,0:T(8,128)(2,1)S(1)}, bf16[128,768]{1,0:T(8,128)(2,1)S(1)}, u32[]{:S(2)}, u32[]{:S(2)}) collective-permute-start(bf16[128,768]{1,0:T(8,128)(2,1)S(1)} %join.2.rest_0_.held), channel_id=1, source_target_pairs={{0,1},{1,0},{2,3},{3,2},{4,5},{5,4},{6,7},{7,6},{8,9},{9,8},{10,11... | collective-permute-start | bytes 589832 | tf_op jit(solution)/shard_map/ppermute | solution.py:260
  63.9 1.8 %collective-permute-start.19 = (bf16[128,768]{1,0:T(8,128)(2,1)S(1)}, bf16[128,768]{1,0:T(8,128)(2,1)S(1)}, u32[]{:S(2)}, u32[]{:S(2)}) collective-permute-start(bf16[128,768]{1,0:T(8,128)(2,1)S(1)} %join.3.held), channel_id=1, source_target_pairs={{0,1},{1,0},{2,3},{3,2},{4,5},{5,4},{6,7},{7,6},{8,9},{9,8},{10,11... | collective-permute-start | bytes 589832 | tf_op jit(solution)/shard_map/ppermute | solution.py:260

commit v15 on v12

--- a/solution.py
+++ b/solution.py
@@ -196,7 +196,8 @@
     )
 
 
-def query_end_kernel(lists, part, received, embeddings, out, *, blocks, own):
+def query_end_kernel(lists, part, received, embeddings, after, out, *, blocks, own):
+    del after
     _, second = named_by_partner(lists, blocks, OFF)
     rows = out.shape[0]
     core = lax.axis_index(AXIS) % 2
@@ -206,8 +207,13 @@
     out[...] = (part[place, :] + dot(received[place, :], right, NN)).astype(out.dtype)
 
 
-def embed_kernel(lists, signal, on, off_a, off_b, queries, *rest, blocks, g, scale):
-    if g == 0:
+def embed_kernel(lists, signal, on, off_a, queries, *rest, blocks, turn, scale):
+    last = turn == blocks - 1
+    off = [off_a]
+    if last:
+        off.append(rest[0])
+        rest = rest[1:]
+    if turn == 0:
         ready, token, total = rest
     else:
         before = rest[0]
@@ -216,22 +222,24 @@
     writes = []
 
     def write(source, index, slot):
-        writes.append(pltpu.make_async_copy(source, out.at[pl.ds(index * block, block), :], sem.at[slot]))
+        place = out.at[pl.ds(pl.multiple_of(index * block, block), block), :]
+        writes.append(pltpu.make_async_copy(source, place, sem.at[slot]))
         writes[-1].start()
 
-    if g > 0:
-        write(before, g - 1, 0)
+    named = named_by_partner(lists, blocks, ON) + named_by_partner(lists, blocks, OFF)
+    g = (named[3] + 1 + turn) % blocks
+    if turn > 0:
+        write(before, (named[3] + turn) % blocks, 0)
     token[...] = jnp.zeros_like(token)
     total[...] = signal[g].astype(F32)
-    named = named_by_partner(lists, blocks, ON) + named_by_partner(lists, blocks, OFF)
-    for received, index in zip((on.at[0], on.at[1], off_a, off_b), named):
+    for received, index in zip([on.at[0], on.at[1], *off], named):
 
         @pl.when(index == g)
         def _():
             total[...] += received[...].astype(F32)
 
     ready[...] = (dot(total[...].astype(BF16), queries[...], TN) * scale).astype(BF16)
-    if g == blocks - 1:
+    if last:
         write(ready, g, 1)
     for copy in writes:
         copy.wait()
@@ -272,28 +280,15 @@
     return (lax.axis_index(AXIS) // bit) % 2
 
 
-def halve_kernel(held, got, *outs, bits):
-    total = outs[-1]
-    total[...] = held[...] + got[...].astype(F32)
+def halve_kernel(held, got, *outs):
+    total = held[...] + got[...].astype(F32)
     rows = outs[0].shape[0]
-    for chain, bit in enumerate(bits):
-        kept, sent = outs[2 * chain], outs[2 * chain + 1]
-        begin = 2 * chain * rows
-        digit = digit_of(bit)
-        kept[...] = total[pl.ds(pl.multiple_of(begin + digit * rows, rows), rows), :]
-        sent[...] = total[pl.ds(pl.multiple_of(begin + (1 - digit) * rows, rows), rows), :].astype(BF16)
+    for chain, out in enumerate(outs):
+        out[...] = total[chain * rows : (chain + 1) * rows, :].astype(BF16)
 
 
 def add_kernel(held, got, *rest, scale):
     rest[-1][...] = ((held[...].astype(F32) + got[...].astype(F32)) * scale).astype(BF16)
-
-
-def join_kernel(held, got, *rest, bit):
-    out = rest[-1]
-    rows = held.shape[0]
-    digit = digit_of(bit)
-    out[pl.ds(pl.multiple_of(digit * rows, rows), rows), :] = held[...]
-    out[pl.ds(pl.multiple_of((1 - digit) * rows, rows), rows), :] = got[...]
 
 
 def place_kernel(*refs, places):
@@ -323,41 +318,22 @@
         return both.reshape(2 * rows, width) * scale
     bits = [1 << k for k in range(1, count.bit_length() - 1)]
     orders = [[bits[0], *bits[2:], bits[1]], [bits[1], bits[0], *bits[2:]]]
-    ends = [order[0] for order in orders]
-    wide, narrow = in_vmem((rows // 4, width), F32), in_vmem((rows // 4, width), BF16)
-    kept_a, sent_a, kept_b, sent_b = call(
-        functools.partial(halve_kernel, bits=ends),
-        "halve",
-        [VMEM] * 2,
-        [wide, narrow, wide, narrow],
-        scratch=[pltpu.VMEM((rows, width), F32)],
-    )(kept, got)
-    held, sent = [kept_a, kept_b], [sent_a, sent_b]
+    piece = in_vmem((rows // 2, width), BF16)
+    held = list(call(halve_kernel, "halve", [VMEM] * 2, [piece, piece])(kept, got))
+    swapped = []
     for k in range(len(bits)):
-        got = [exchange(piece, order[k]) for piece, order in zip(sent, orders)]
+        last = k == len(bits) - 1
+        got = [exchange(value, order[k]) for value, order in zip(held, orders)]
         for chain in range(2):
             after = beside[k : k + 1] if chain == 0 else []
             held[chain] = call(
-                functools.partial(add_kernel, scale=scale if k == len(bits) - 1 else 1.0),
+                functools.partial(add_kernel, scale=scale if last else 1.0),
                 "add",
                 [VMEM] * 2 + [ANY] * len(after),
-                narrow,
+                piece,
+                flops=2 * 10**8 if last else 0,
             )(held[chain], got[chain], *after)
-        sent = list(held)
-    got = [exchange(piece, bit) for piece, bit in zip(held, ends)]
-    joined, swapped = [], []
-    for chain, bit in enumerate(ends):
-        after = beside[len(bits) :] if chain == 0 else joined
-        joined.append(
-            call(
-                functools.partial(join_kernel, bit=bit),
-                "join",
-                [VMEM] * 2 + [ANY] * len(after),
-                in_vmem((rows // 2, width), BF16),
-                flops=2 * 10**8,
-            )(held[chain], got[chain], *after)
-        )
-        swapped.append(exchange(joined[chain], 1))
+    swapped = [exchange(value, 1) for value in held]
 
     def place(values, places, *begun):
         return call(
@@ -373,7 +349,7 @@
             aliases={len(values): 0} if begun else None,
         )(*values, *begun)
 
-    early = place([joined[0], joined[1], swapped[0]], [(0, True), (1, True), (0, False)])
+    early = place([held[0], held[1], swapped[0]], [(0, True), (1, True), (0, False)])
     return place([swapped[1]], [(1, False)], early)
 
 
@@ -467,31 +443,38 @@
     part, on = call(
         functools.partial(query_on_kernel, blocks=blocks), "query_on", [SMEM] + [VMEM] * 5, [whole, pair]
     )(lists, part, embeddings, *back_on)
+    ready = in_vmem((block, width), BF16)
+    written = jax.ShapeDtypeStruct((labels_dev, width), BF16)
+
+    def embed(turn, outs):
+        values = [lists, signal, on, back_a, queries] + ([back_b] if turn == blocks - 1 else []) + outs[::-1]
+        return call(
+            functools.partial(embed_kernel, blocks=blocks, turn=turn, scale=1.0 / math.sqrt(rows)),
+            "embed",
+            [SMEM] + [VMEM] * (len(values) - 1 - (turn > 1)) + [ANY] * (turn > 1),
+            ([written] if turn else []) + [ready, in_vmem((8, 128), F32)],
+            out_specs=([ANY] if turn else []) + [VMEM] * 2,
+            scratch=[pltpu.VMEM((rows, block), F32)] + ([pltpu.SemaphoreType.DMA((2,))] if turn else []),
+            aliases={len(values) - 1: 0} if turn > 1 else None,
+        )(*values)
+
+    *outs, token = embed(0, [])
+    tokens = [token]
+
     def query_end(own, kind):
         return call(
             functools.partial(query_end_kernel, blocks=blocks, own=own),
             "query_end",
-            [SMEM] + [VMEM] * 3,
+            [SMEM] + [VMEM] * 3 + [ANY],
             in_vmem((rows // 2, width), kind),
-        )(lists, part, back_b, embeddings)
+        )(lists, part, back_b, embeddings, tokens[0])
 
     sent, kept = query_end(False, BF16), query_end(True, F32)
-    ready = in_vmem((block, width), BF16)
-    written = jax.ShapeDtypeStruct((labels_dev, width), BF16)
-    outs, tokens = [], []
-    for g in range(blocks):
-        *outs, token = call(
-            functools.partial(embed_kernel, blocks=blocks, g=g, scale=1.0 / math.sqrt(rows)),
-            "embed",
-            [SMEM] + [VMEM] * (5 + min(g, 1)) + [ANY] * (len(outs) - 1),
-            ([written] if g else []) + [ready, in_vmem((8, 128), F32)],
-            out_specs=([ANY] if g else []) + [VMEM] * 2,
-            scratch=[pltpu.VMEM((rows, block), F32)] + ([pltpu.SemaphoreType.DMA((2,))] if g else []),
-            aliases={7: 0} if g > 1 else None,
-        )(lists, signal, on, back_a, back_b, queries, *outs[::-1])
+    for turn in range(1, blocks):
+        *outs, token = embed(turn, outs)
         tokens.append(token)
     grad_embed = outs[0]
-    grad_queries = sum_queries(kept, sent, tokens, 1.0 / math.sqrt(labels_dev * count))
+    grad_queries = sum_queries(kept, sent, tokens[1:], 1.0 / math.sqrt(labels_dev * count))
     return (grad_embed, grad_queries)
 
 

time: 56.9 us -> 56.8 us (level)
  starting transfers between devices: 23.2 us -> 22.6 us
    ppermute x17 -> x15, waiting for transfers between devices: 3.66 us -> 5.05 us  [exchange(): return lax.ppermute(value, AXIS, [(i, i ^ mask) for i in range(count)])]
    ppermute x4, waiting for transfers between devices: 3.38 us -> 2.28 us  [off_swap(): return lax.ppermute(value, AXIS, off_route)]
    ppermute x17 -> x15, starting transfers between devices: 12.5 us -> 11.9 us  [exchange(): return lax.ppermute(value, AXIS, [(i, i ^ mask) for i in range(count)])]
    pallas_call x13 -> x11, Pallas kernels: 6.94 us -> 7.15 us  [the longest x4 6.94 us: embed(): call(functools.partial(embed_kernel, blocks=blocks, turn=turn, scale=1.0...]
  transfers between devices with their start and end apart: 21 -> 19, of which waited for: 8 -> 6; matrix products, arithmetic and copies ran while one was open for 0% -> 0% of each run, Pallas kernels for 39% -> 39%
where the time goes in v15:
time: 56.8 us; the launch traced here: 56.7 us
  Pallas kernels  25.9 us (46%)
  starting transfers between devices  22.6 us (40%)
  waiting for transfers between devices  7.33 us (13%)
  between operations  0.96 us (2%)
    ppermute x15, starting transfers between devices, exchange(): return lax.ppermute(value, AXIS, [(i, i ^ mask) for i in range(count)])  11.9 us
    ppermute x4, starting transfers between devices, off_swap(): return lax.ppermute(value, AXIS, off_route)  10.7 us
    pallas_call x4, Pallas kernels, embed(): call(functools.partial(embed_kernel, blocks=blocks, turn=turn, scale=1.0...  6.94 us
    ppermute x15, waiting for transfers between devices, exchange(): return lax.ppermute(value, AXIS, [(i, i ^ mask) for i in range(count)])  5.05 us
    pallas_call x2, Pallas kernels, signal_of(): call(functools.partial(signal_kernel, slot=slot), 'signal', [SMEM] + [VME...  3.53 us
    pallas_call x1, Pallas kernels, per_device(): call(hits_kernel, 'hits', [VMEM, HBM], [in_vmem(full, BF16), in_vmem(edge...  2.45 us
    ppermute x4, waiting for transfers between devices, off_swap(): return lax.ppermute(value, AXIS, off_route)  2.28 us
    pallas_call x1, Pallas kernels, per_device(): call(functools.partial(project_kernel, scale=scale), 'project', [HBM] * 3...  2.03 us
  transfers between devices with their start and end apart: 19, of which 6 were waited for; matrix products, arithmetic and copies ran while one was open for 0% of the time, Pallas kernels for 39%

profile of v15, /device:TPU:0, one launch (start us, length us, event | category | flops | bytes accessed | tf_op | source)
XLA Modules:
  0.0 56.7 jit_solution(8634894366011918080)
XLA Ops:
  0.7 2.0 %project.1 = (bf16[256,512]{1,0:T(8,128)(2,1)S(1)}, bf16[256,768]{1,0:T(8,128)(2,1)S(1)}, bf16[2048,768]{1,0:T(8,128)(2,1)S(1)}) custom-call(s32[2,64]{1,0:T(2,128)} %bitcast.3, bf16[256,768]{1,0:T(8,128)(2,1)} %queries.1, bf16[2048,768]{1,0:T(8,128)(2,1)} %embeddings.1), custom_call_target="tpu_custom_call" | custom-call | tf_op jit(solution)/shard_map/project/pallas_call | solution.py:378
  2.7 5.5 %collective-permute-start.4 = (bf16[256,512]{1,0:T(8,128)(2,1)S(1)}, bf16[256,512]{1,0:T(8,128)(2,1)S(1)}, u32[]{:S(2)}, u32[]{:S(2)}) collective-permute-start(bf16[256,512]{1,0:T(8,128)(2,1)S(1)} %get-tuple-element.42), channel_id=1, source_target_pairs={{1,2},{3,4},{5,6},{7,8},{9,10},{11,12},{13,14},{15,0},{2,1},{4,3},... | collective-permute-start | bytes 786440 | tf_op jit(solution)/shard_map/ppermute | solution.py:366
  8.2 1.6 %own.1 = (f32[4,256,512]{2,1,0:T(8,128)S(1)}, bf16[256,512]{1,0:T(8,128)(2,1)S(1)}, bf16[176,512]{1,0:T(8,128)(2,1)S(1)}, bf16[176,512]{1,0:T(8,128)(2,1)S(1)}, bf16[160,512]{1,0:T(8,128)(2,1)S(1)}) custom-call(s32[2,64]{1,0:T(2,128)S(1)} %bitcast.4, bf16[256,768]{1,0:T(8,128)(2,1)S(1)} %get-tuple-element.33.queries, ...), custom_call_target="tpu_custom_call" | custom-call | tf_op jit(solution)/shard_map/own/pallas_call | solution.py:386
  10.5 0.6 %collective-permute-start.3 = (bf16[256,512]{1,0:T(8,128)(2,1)S(1)}, bf16[256,512]{1,0:T(8,128)(2,1)S(1)}, u32[]{:S(2)}, u32[]{:S(2)}) collective-permute-start(bf16[256,512]{1,0:T(8,128)(2,1)S(1)} %get-tuple-element.41), channel_id=1, source_target_pairs={{1,2},{3,4},{5,6},{7,8},{9,10},{11,12},{13,14},{15,0},{2,1},{4,3},... | collective-permute-start | bytes 786440 | tf_op jit(solution)/shard_map/ppermute | solution.py:366
  11.1 2.4 %hits.1 = (bf16[4,256,512]{2,1,0:T(8,128)(2,1)S(1)}, bf16[4,2,512,512]{3,2,1,0:T(8,128)(2,1)S(1)}) custom-call(s32[8,256]{1,0:T(8,128)S(1)} %bitcast.19, bf16[4,2,512,512]{3,2,1,0:T(8,128)(2,1)} %tiles.1), custom_call_target="tpu_custom_call" | custom-call | tf_op jit(solution)/shard_map/hits/pallas_call | solution.py:393
  13.6 1.3 %base.1 = f32[4,256,512]{2,1,0:T(8,128)S(1)} custom-call(s32[2,64]{1,0:T(2,128)S(1)} %bitcast.5, f32[4,256,512]{2,1,0:T(8,128)S(1)} %get-tuple-element.35.own, bf16[4,2,512,512]{3,2,1,0:T(8,128)(2,1)S(1)} %get-tuple-element.36.tiles, bf16[176,512]{1,0:T(8,128)(2,1)S(1)} %collective-permute-done.rest_0_, bf16[176,512]{1,0:T(8,128)(2,1)S(1)} %collective-permute-done.1.rest_1_, ...), custom_call_target="tpu_custom_call" | custom-call | tf_op jit(solution)/shard_map/base/pallas_call | solution.py:401
  15.0 1.8 %signal.2 = (bf16[4,256,512]{2,1,0:T(8,128)(2,1)S(1)}, bf16[256,512]{1,0:T(8,128)(2,1)S(1)}) custom-call(s32[2,64]{1,0:T(2,128)S(1)} %bitcast.6, f32[4,256,512]{2,1,0:T(8,128)S(1)} %base.1, bf16[4,256,512]{2,1,0:T(8,128)(2,1)S(1)} %get-tuple-element.40.hits, f32[1,2048]{1,0:T(1,128)S(1)} %bitcast.17, bf16[256,512]{1,0:T(8,128)(2,1)S(1)} %collective-permute-done.4.received, ...), custom_call_target="tpu_custom_call" | custom-call | flops 2000000000 | tf_op jit(solution)/shard_map/signal/pallas_call | solution.py:411
  16.8 4.5 %collective-permute-start.5 = (bf16[256,512]{1,0:T(8,128)(2,1)S(1)}, bf16[256,512]{1,0:T(8,128)(2,1)S(1)}, u32[]{:S(2)}, u32[]{:S(2)}) collective-permute-start(bf16[256,512]{1,0:T(8,128)(2,1)S(1)} %get-tuple-element.45), channel_id=1, source_target_pairs={{1,2},{3,4},{5,6},{7,8},{9,10},{11,12},{13,14},{15,0},{2,1},{4,3},... | collective-permute-start | bytes 786440 | tf_op jit(solution)/shard_map/ppermute | solution.py:366
  21.2 1.8 %signal.3 = (bf16[4,256,512]{2,1,0:T(8,128)(2,1)S(1)}, bf16[256,512]{1,0:T(8,128)(2,1)S(1)}) custom-call(s32[2,64]{1,0:T(2,128)S(1)} %bitcast.7, f32[4,256,512]{2,1,0:T(8,128)S(1)} %base.1, bf16[4,256,512]{2,1,0:T(8,128)(2,1)S(1)} %get-tuple-element.40.hits, f32[1,2048]{1,0:T(1,128)S(1)} %bitcast.18, ...), custom_call_target="tpu_custom_call", output_to_operand_aliasing={{0}: (6, {})} | custom-call | tf_op jit(solution)/shard_map/signal/pallas_call | solution.py:411
  23.1 1.4 %push.1 = (bf16[176,512]{1,0:T(8,128)(2,1)S(1)}, bf16[176,512]{1,0:T(8,128)(2,1)S(1)}, bf16[160,512]{1,0:T(8,128)(2,1)S(1)}) custom-call(s32[2,64]{1,0:T(2,128)S(1)} %bitcast.8, bf16[4,256,512]{2,1,0:T(8,128)(2,1)S(1)} %get-tuple-element.44.signal, bf16[4,2,512,512]{3,2,1,0:T(8,128)(2,1)S(1)} %get-tuple-element.36.tiles), custom_call_target="tpu_custom_call" | custom-call | tf_op jit(solution)/shard_map/push/pallas_call | solution.py:425
  25.2 1.0 %query.1.part = f32[256,768]{1,0:T(8,128)S(1)} custom-call(bf16[4,256,512]{2,1,0:T(8,128)(2,1)S(1)} %get-tuple-element.44.signal, bf16[2048,768]{1,0:T(8,128)(2,1)S(1)} %get-tuple-element.34.embeddings), custom_call_target="tpu_custom_call" | custom-call | tf_op jit(solution)/shard_map/query/pallas_call | solution.py:435
  26.2 0.9 %query_half.1.part = f32[256,768]{1,0:T(8,128)S(1)} custom-call(s32[2,64]{1,0:T(2,128)S(1)} %bitcast.9, f32[256,768]{1,0:T(8,128)S(1)} %query.1.part, bf16[256,512]{1,0:T(8,128)(2,1)S(1)} %collective-permute-done.5.received.off_a, bf16[2048,768]{1,0:T(8,128)(2,1)S(1)} %get-tuple-element.34.embeddings), custom_call_target="tpu_custom_call" | custom-call | flops 1000000000 | tf_op jit(solution)/shard_map/query_half/pallas_call | solution.py:436
  27.1 1.2 %query_on.1 = (f32[256,768]{1,0:T(8,128)S(1)}, bf16[2,256,512]{2,1,0:T(8,128)(2,1)S(1)}) custom-call(s32[2,64]{1,0:T(2,128)S(1)} %bitcast.10, f32[256,768]{1,0:T(8,128)S(1)} %query_half.1.part, bf16[2048,768]{1,0:T(8,128)(2,1)S(1)} %get-tuple-element.34.embeddings, bf16[176,512]{1,0:T(8,128)(2,1)S(1)} %collective-permute-done.6.rest_0_, ...), custom_call_target="tpu_custom_call" | custom-call | tf_op jit(solution)/shard_map/query_on/pallas_call | solution.py:443
  28.3 1.0 %embed.4 = (bf16[512,768]{1,0:T(8,128)(2,1)S(1)}, f32[8,128]{1,0:T(8,128)S(1)}) custom-call(s32[2,64]{1,0:T(2,128)S(1)} %bitcast.11, bf16[4,256,512]{2,1,0:T(8,128)(2,1)S(1)} %get-tuple-element.44.signal, bf16[2,256,512]{2,1,0:T(8,128)(2,1)S(1)} %get-tuple-element.49.on, bf16[256,512]{1,0:T(8,128)(2,1)S(1)} %collective-permute-done.5.received.off_a, ...), custom_call_target="tpu_custom_call" | custom-call | tf_op jit(solution)/shard_map/embed/pallas_call | solution.py:451
  29.4 2.3 %collective-permute-done.9.rest_0_.received = bf16[256,512]{1,0:T(8,128)(2,1)S(1)} collective-permute-done((bf16[256,512]{1,0:T(8,128)(2,1)S(1)}, bf16[256,512]{1,0:T(8,128)(2,1)S(1)}, u32[]{:S(2)}, u32[]{:S(2)}) %collective-permute-start.9) | collective-permute-done | bytes 262176 | tf_op jit(solution)/shard_map/ppermute | solution.py:366
  31.6 0.8 %query_end.3 = bf16[128,768]{1,0:T(8,128)(2,1)S(1)} custom-call(s32[2,64]{1,0:T(2,128)S(1)} %bitcast.12, f32[256,768]{1,0:T(8,128)S(1)} %get-tuple-element.57.part, bf16[256,512]{1,0:T(8,128)(2,1)S(1)} %collective-permute-done.9.rest_0_.received, bf16[2048,768]{1,0:T(8,128)(2,1)S(1)} %get-tuple-element.34.embeddings, f32[8,128]{1,0:T(8,128)S(1)} %get-tuple-element.58.after), custom_call_target="tpu_custom_call" | custom-call | tf_op jit(solution)/shard_map/query_end/pallas_call | solution.py:465
  32.6 0.9 %query_end.2.held = f32[128,768]{1,0:T(8,128)S(1)} custom-call(s32[2,64]{1,0:T(2,128)S(1)} %bitcast.13, f32[256,768]{1,0:T(8,128)S(1)} %get-tuple-element.57.part, bf16[256,512]{1,0:T(8,128)(2,1)S(1)} %collective-permute-done.9.rest_0_.received, bf16[2048,768]{1,0:T(8,128)(2,1)S(1)} %get-tuple-element.34.embeddings, f32[8,128]{1,0:T(8,128)S(1)} %get-tuple-element.58.after), custom_call_target="tpu_custom_call" | custom-call | tf_op jit(solution)/shard_map/query_end/pallas_call | solution.py:465
  33.4 0.6 %collective-permute-done.10.got = bf16[128,768]{1,0:T(8,128)(2,1)S(1)} collective-permute-done((bf16[128,768]{1,0:T(8,128)(2,1)S(1)}, bf16[128,768]{1,0:T(8,128)(2,1)S(1)}, u32[]{:S(2)}, u32[]{:S(2)}) %collective-permute-start.10) | collective-permute-done | bytes 196640 | tf_op jit(solution)/shard_map/ppermute | solution.py:272
  34.0 1.1 %collective-permute-start.15 = (bf16[64,768]{1,0:T(8,128)(2,1)S(1)}, bf16[64,768]{1,0:T(8,128)(2,1)S(1)}, u32[]{:S(2)}, u32[]{:S(2)}) collective-permute-start(bf16[64,768]{1,0:T(8,128)(2,1)S(1)} %get-tuple-element.60.held), channel_id=1, source_target_pairs={{0,2},{1,3},{2,0},{3,1},{4,6},{5,7},{6,4},{7,5},{8,10},{9,11},{10,... | collective-permute-start | bytes 294920 | tf_op jit(solution)/shard_map/ppermute | solution.py:272
  35.2 1.6 %collective-permute-start.11 = (bf16[64,768]{1,0:T(8,128)(2,1)S(1)}, bf16[64,768]{1,0:T(8,128)(2,1)S(1)}, u32[]{:S(2)}, u32[]{:S(2)}) collective-permute-start(bf16[64,768]{1,0:T(8,128)(2,1)S(1)} %get-tuple-element.59.held), channel_id=1, source_target_pairs={{0,4},{1,5},{2,6},{3,7},{4,0},{5,1},{6,2},{7,3},{8,12},{9,13},{10,... | collective-permute-start | bytes 294920 | tf_op jit(solution)/shard_map/ppermute | solution.py:272
  36.7 1.5 %embed.5 = (bf16[2048,768]{1,0:T(8,128)(2,1)}, bf16[512,768]{1,0:T(8,128)(2,1)S(1)}, f32[8,128]{1,0:T(8,128)S(1)}) custom-call(s32[2,64]{1,0:T(2,128)S(1)} %bitcast.14, bf16[4,256,512]{2,1,0:T(8,128)(2,1)S(1)} %get-tuple-element.44.signal, bf16[2,256,512]{2,1,0:T(8,128)(2,1)S(1)} %get-tuple-element.49.on, ...), custom_call_target="tpu_custom_call" | custom-call | tf_op jit(solution)/shard_map/embed/pallas_call | solution.py:451
  38.2 0.7 %collective-permute-done.15.got = bf16[64,768]{1,0:T(8,128)(2,1)S(1)} collective-permute-done((bf16[64,768]{1,0:T(8,128)(2,1)S(1)}, bf16[64,768]{1,0:T(8,128)(2,1)S(1)}, u32[]{:S(2)}, u32[]{:S(2)}) %collective-permute-start.15) | collective-permute-done | bytes 98336 | tf_op jit(solution)/shard_map/ppermute | solution.py:272
  39.0 2.2 %collective-permute-start.16 = (bf16[64,768]{1,0:T(8,128)(2,1)S(1)}, bf16[64,768]{1,0:T(8,128)(2,1)S(1)}, u32[]{:S(2)}, u32[]{:S(2)}) collective-permute-start(bf16[64,768]{1,0:T(8,128)(2,1)S(1)} %add.9.held), channel_id=1, source_target_pairs={{0,8},{1,9},{2,10},{3,11},{4,12},{5,13},{6,14},{7,15},{8,0},{9,1},... | collective-permute-start | bytes 294920 | tf_op jit(solution)/shard_map/ppermute | solution.py:272
  41.2 1.6 %collective-permute-start.12 = (bf16[64,768]{1,0:T(8,128)(2,1)S(1)}, bf16[64,768]{1,0:T(8,128)(2,1)S(1)}, u32[]{:S(2)}, u32[]{:S(2)}) collective-permute-start(bf16[64,768]{1,0:T(8,128)(2,1)S(1)} %add.6.held), channel_id=1, source_target_pairs={{0,2},{1,3},{2,0},{3,1},{4,6},{5,7},{6,4},{7,5},{8,10},{9,11},{10,... | collective-permute-start | bytes 294920 | tf_op jit(solution)/shard_map/ppermute | solution.py:272
  42.7 1.5 %embed.6 = (bf16[2048,768]{1,0:T(8,128)(2,1)}, bf16[512,768]{1,0:T(8,128)(2,1)S(1)}, f32[8,128]{1,0:T(8,128)S(1)}) custom-call(s32[2,64]{1,0:T(2,128)S(1)} %bitcast.15, bf16[4,256,512]{2,1,0:T(8,128)(2,1)S(1)} %get-tuple-element.44.signal, bf16[2,256,512]{2,1,0:T(8,128)(2,1)S(1)} %get-tuple-element.49.on, ...), custom_call_target="tpu_custom_call", output_to_operand_aliasing={{0}: (6, {})} | custom-call | tf_op jit(solution)/shard_map/embed/pallas_call | solution.py:451
  44.2 1.8 %collective-permute-done.16.got = bf16[64,768]{1,0:T(8,128)(2,1)S(1)} collective-permute-done((bf16[64,768]{1,0:T(8,128)(2,1)S(1)}, bf16[64,768]{1,0:T(8,128)(2,1)S(1)}, u32[]{:S(2)}, u32[]{:S(2)}) %collective-permute-start.16) | collective-permute-done | bytes 98336 | tf_op jit(solution)/shard_map/ppermute | solution.py:272
  46.1 0.5 collective-permute-start.17
  46.6 3.4 %collective-permute-start.13 = (bf16[64,768]{1,0:T(8,128)(2,1)S(1)}, bf16[64,768]{1,0:T(8,128)(2,1)S(1)}, u32[]{:S(2)}, u32[]{:S(2)}) collective-permute-start(bf16[64,768]{1,0:T(8,128)(2,1)S(1)} %add.7.held), channel_id=1, source_target_pairs={{0,8},{1,9},{2,10},{3,11},{4,12},{5,13},{6,14},{7,15},{8,0},{9,1},... | collective-permute-start | bytes 294920 | tf_op jit(solution)/shard_map/ppermute | solution.py:272
  50.1 2.9 %embed.7 = (bf16[2048,768]{1,0:T(8,128)(2,1)}, bf16[512,768]{1,0:T(8,128)(2,1)}, f32[8,128]{1,0:T(8,128)S(1)}) custom-call(s32[2,64]{1,0:T(2,128)S(1)} %bitcast.16, bf16[4,256,512]{2,1,0:T(8,128)(2,1)S(1)} %get-tuple-element.44.signal, bf16[2,256,512]{2,1,0:T(8,128)(2,1)S(1)} %get-tuple-element.49.on, ...), custom_call_target="tpu_custom_call", output_to_operand_aliasing={{0}: (7, {})} | custom-call | tf_op jit(solution)/shard_map/embed/pallas_call | solution.py:451
  53.1 1.5 %collective-permute-done.13.got = bf16[64,768]{1,0:T(8,128)(2,1)S(1)} collective-permute-done((bf16[64,768]{1,0:T(8,128)(2,1)S(1)}, bf16[64,768]{1,0:T(8,128)(2,1)S(1)}, u32[]{:S(2)}, u32[]{:S(2)}) %collective-permute-start.13) | collective-permute-done | bytes 98336 | tf_op jit(solution)/shard_map/ppermute | solution.py:272
  54.8 0.8 %place.2.refs_1_ = f32[256,768]{1,0:T(8,128)} custom-call(bf16[64,768]{1,0:T(8,128)(2,1)S(1)} %add.11.refs_0_, bf16[64,768]{1,0:T(8,128)(2,1)S(1)} %add.8.refs_1_, bf16[64,768]{1,0:T(8,128)(2,1)S(1)} %collective-permute-done.18.refs_2_), custom_call_target="tpu_custom_call" | custom-call | tf_op jit(solution)/shard_map/place/pallas_call | solution.py:339
  56.0 0.7 %place.3 = f32[256,768]{1,0:T(8,128)} custom-call(bf16[64,768]{1,0:T(8,128)(2,1)S(1)} %collective-permute-done.14.refs_0_, f32[256,768]{1,0:T(8,128)} %place.2.refs_1_), custom_call_target="tpu_custom_call", output_to_operand_aliasing={{}: (1, {})} | custom-call | tf_op jit(solution)/shard_map/place/pallas_call | solution.py:339
  (37 shorter events, 2.3 us)
Async XLA Ops:
  0.6 7.6 %copy-start = (s32[64,2]{0,1:T(2,128)S(1)}, s32[64,2]{0,1:T(2,128)}, u32[]{:S(2)}) copy-start(s32[64,2]{0,1:T(2,128)} %param.8) | copy-start | bytes 1540
  0.6 10.5 %copy-start.2 = (s32[256,8]{0,1:T(8,128)S(1)}, s32[256,8]{0,1:T(8,128)}, u32[]{:S(2)}) copy-start(s32[256,8]{0,1:T(8,128)} %param.11) | copy-start | bytes 24580
  2.7 12.3 %collective-permute-start.4 = (bf16[256,512]{1,0:T(8,128)(2,1)S(1)}, bf16[256,512]{1,0:T(8,128)(2,1)S(1)}, u32[]{:S(2)}, u32[]{:S(2)}) collective-permute-start(bf16[256,512]{1,0:T(8,128)(2,1)S(1)} %get-tuple-element.42), channel_id=1, source_target_pairs={{1,2},{3,4},{5,6},{7,8},{9,10},{11,12},{13,14},{15,0},{2,1},{4,3},... | collective-permute-start | bytes 786440 | tf_op jit(solution)/shard_map/ppermute | solution.py:366
  9.9 3.7 %collective-permute-start = (bf16[176,512]{1,0:T(8,128)(2,1)S(1)}, bf16[176,512]{1,0:T(8,128)(2,1)S(1)}, u32[]{:S(2)}, u32[]{:S(2)}) collective-permute-start(bf16[176,512]{1,0:T(8,128)(2,1)S(1)} %get-tuple-element.37), channel_id=1, source_target_pairs={{0,1},{1,0},{2,3},{3,2},{4,5},{5,4},{6,7},{7,6},{8,9},{9,8},{10,11... | collective-permute-start | bytes 540680 | tf_op jit(solution)/shard_map/ppermute | solution.py:272
  9.9 3.7 %collective-permute-start.1 = (bf16[176,512]{1,0:T(8,128)(2,1)S(1)}, bf16[176,512]{1,0:T(8,128)(2,1)S(1)}, u32[]{:S(2)}, u32[]{:S(2)}) collective-permute-start(bf16[176,512]{1,0:T(8,128)(2,1)S(1)} %get-tuple-element.38), channel_id=1, source_target_pairs={{0,1},{1,0},{2,3},{3,2},{4,5},{5,4},{6,7},{7,6},{8,9},{9,8},{10,11... | collective-permute-start | bytes 540680 | tf_op jit(solution)/shard_map/ppermute | solution.py:272
  10.4 3.2 %collective-permute-start.2 = (bf16[160,512]{1,0:T(8,128)(2,1)S(1)}, bf16[160,512]{1,0:T(8,128)(2,1)S(1)}, u32[]{:S(2)}, u32[]{:S(2)}) collective-permute-start(bf16[160,512]{1,0:T(8,128)(2,1)S(1)} %get-tuple-element.39), channel_id=1, source_target_pairs={{0,1},{1,0},{2,3},{3,2},{4,5},{5,4},{6,7},{7,6},{8,9},{9,8},{10,11... | collective-permute-start | bytes 491528 | tf_op jit(solution)/shard_map/ppermute | solution.py:272
  10.5 10.7 %collective-permute-start.3 = (bf16[256,512]{1,0:T(8,128)(2,1)S(1)}, bf16[256,512]{1,0:T(8,128)(2,1)S(1)}, u32[]{:S(2)}, u32[]{:S(2)}) collective-permute-start(bf16[256,512]{1,0:T(8,128)(2,1)S(1)} %get-tuple-element.41), channel_id=1, source_target_pairs={{1,2},{3,4},{5,6},{7,8},{9,10},{11,12},{13,14},{15,0},{2,1},{4,3},... | collective-permute-start | bytes 786440 | tf_op jit(solution)/shard_map/ppermute | solution.py:366
  13.6 1.4 %copy-start.1 = (f32[2048]{0:T(1024)S(1)}, f32[2048]{0:T(1024)}, u32[]{:S(2)}) copy-start(f32[2048]{0:T(1024)} %param.9) | copy-start | bytes 24580
  16.8 9.4 %collective-permute-start.5 = (bf16[256,512]{1,0:T(8,128)(2,1)S(1)}, bf16[256,512]{1,0:T(8,128)(2,1)S(1)}, u32[]{:S(2)}, u32[]{:S(2)}) collective-permute-start(bf16[256,512]{1,0:T(8,128)(2,1)S(1)} %get-tuple-element.45), channel_id=1, source_target_pairs={{1,2},{3,4},{5,6},{7,8},{9,10},{11,12},{13,14},{15,0},{2,1},{4,3},... | collective-permute-start | bytes 786440 | tf_op jit(solution)/shard_map/ppermute | solution.py:366
  23.0 8.6 %collective-permute-start.9 = (bf16[256,512]{1,0:T(8,128)(2,1)S(1)}, bf16[256,512]{1,0:T(8,128)(2,1)S(1)}, u32[]{:S(2)}, u32[]{:S(2)}) collective-permute-start(bf16[256,512]{1,0:T(8,128)(2,1)S(1)} %get-tuple-element.50), channel_id=1, source_target_pairs={{1,2},{3,4},{5,6},{7,8},{9,10},{11,12},{13,14},{15,0},{2,1},{4,3},... | collective-permute-start | bytes 786440 | tf_op jit(solution)/shard_map/ppermute | solution.py:366
  24.5 2.6 %collective-permute-start.6 = (bf16[176,512]{1,0:T(8,128)(2,1)S(1)}, bf16[176,512]{1,0:T(8,128)(2,1)S(1)}, u32[]{:S(2)}, u32[]{:S(2)}) collective-permute-start(bf16[176,512]{1,0:T(8,128)(2,1)S(1)} %get-tuple-element.46), channel_id=1, source_target_pairs={{0,1},{1,0},{2,3},{3,2},{4,5},{5,4},{6,7},{7,6},{8,9},{9,8},{10,11... | collective-permute-start | bytes 540680 | tf_op jit(solution)/shard_map/ppermute | solution.py:272
  24.6 2.6 %collective-permute-start.7 = (bf16[176,512]{1,0:T(8,128)(2,1)S(1)}, bf16[176,512]{1,0:T(8,128)(2,1)S(1)}, u32[]{:S(2)}, u32[]{:S(2)}) collective-permute-start(bf16[176,512]{1,0:T(8,128)(2,1)S(1)} %get-tuple-element.47), channel_id=1, source_target_pairs={{0,1},{1,0},{2,3},{3,2},{4,5},{5,4},{6,7},{7,6},{8,9},{9,8},{10,11... | collective-permute-start | bytes 540680 | tf_op jit(solution)/shard_map/ppermute | solution.py:272
  25.1 2.0 %collective-permute-start.8 = (bf16[160,512]{1,0:T(8,128)(2,1)S(1)}, bf16[160,512]{1,0:T(8,128)(2,1)S(1)}, u32[]{:S(2)}, u32[]{:S(2)}) collective-permute-start(bf16[160,512]{1,0:T(8,128)(2,1)S(1)} %get-tuple-element.48), channel_id=1, source_target_pairs={{0,1},{1,0},{2,3},{3,2},{4,5},{5,4},{6,7},{7,6},{8,9},{9,8},{10,11... | collective-permute-start | bytes 491528 | tf_op jit(solution)/shard_map/ppermute | solution.py:272
  32.5 1.5 %collective-permute-start.10 = (bf16[128,768]{1,0:T(8,128)(2,1)S(1)}, bf16[128,768]{1,0:T(8,128)(2,1)S(1)}, u32[]{:S(2)}, u32[]{:S(2)}) collective-permute-start(bf16[128,768]{1,0:T(8,128)(2,1)S(1)} %query_end.3), channel_id=1, source_target_pairs={{0,1},{1,0},{2,3},{3,2},{4,5},{5,4},{6,7},{7,6},{8,9},{9,8},{10,11... | collective-permute-start | bytes 589832 | tf_op jit(solution)/shard_map/ppermute | solution.py:272
  34.0 4.9 %collective-permute-start.15 = (bf16[64,768]{1,0:T(8,128)(2,1)S(1)}, bf16[64,768]{1,0:T(8,128)(2,1)S(1)}, u32[]{:S(2)}, u32[]{:S(2)}) collective-permute-start(bf16[64,768]{1,0:T(8,128)(2,1)S(1)} %get-tuple-element.60.held), channel_id=1, source_target_pairs={{0,2},{1,3},{2,0},{3,1},{4,6},{5,7},{6,4},{7,5},{8,10},{9,11},{10,... | collective-permute-start | bytes 294920 | tf_op jit(solution)/shard_map/ppermute | solution.py:272
  35.2 6.0 %collective-permute-start.11 = (bf16[64,768]{1,0:T(8,128)(2,1)S(1)}, bf16[64,768]{1,0:T(8,128)(2,1)S(1)}, u32[]{:S(2)}, u32[]{:S(2)}) collective-permute-start(bf16[64,768]{1,0:T(8,128)(2,1)S(1)} %get-tuple-element.59.held), channel_id=1, source_target_pairs={{0,4},{1,5},{2,6},{3,7},{4,0},{5,1},{6,2},{7,3},{8,12},{9,13},{10,... | collective-permute-start | bytes 294920 | tf_op jit(solution)/shard_map/ppermute | solution.py:272
  39.0 7.1 %collective-permute-start.16 = (bf16[64,768]{1,0:T(8,128)(2,1)S(1)}, bf16[64,768]{1,0:T(8,128)(2,1)S(1)}, u32[]{:S(2)}, u32[]{:S(2)}) collective-permute-start(bf16[64,768]{1,0:T(8,128)(2,1)S(1)} %add.9.held), channel_id=1, source_target_pairs={{0,8},{1,9},{2,10},{3,11},{4,12},{5,13},{6,14},{7,15},{8,0},{9,1},... | collective-permute-start | bytes 294920 | tf_op jit(solution)/shard_map/ppermute | solution.py:272
  41.2 5.4 %collective-permute-start.12 = (bf16[64,768]{1,0:T(8,128)(2,1)S(1)}, bf16[64,768]{1,0:T(8,128)(2,1)S(1)}, u32[]{:S(2)}, u32[]{:S(2)}) collective-permute-start(bf16[64,768]{1,0:T(8,128)(2,1)S(1)} %add.6.held), channel_id=1, source_target_pairs={{0,2},{1,3},{2,0},{3,1},{4,6},{5,7},{6,4},{7,5},{8,10},{9,11},{10,... | collective-permute-start | bytes 294920 | tf_op jit(solution)/shard_map/ppermute | solution.py:272
  46.1 6.9 %collective-permute-start.17 = (bf16[64,768]{1,0:T(8,128)(2,1)S(1)}, bf16[64,768]{1,0:T(8,128)(2,1)S(1)}, u32[]{:S(2)}, u32[]{:S(2)}) collective-permute-start(bf16[64,768]{1,0:T(8,128)(2,1)S(1)} %add.10.held), channel_id=1, source_target_pairs={{0,4},{1,5},{2,6},{3,7},{4,0},{5,1},{6,2},{7,3},{8,12},{9,13},{10,... | collective-permute-start | bytes 294920 | tf_op jit(solution)/shard_map/ppermute | solution.py:272
  46.6 8.0 %collective-permute-start.13 = (bf16[64,768]{1,0:T(8,128)(2,1)S(1)}, bf16[64,768]{1,0:T(8,128)(2,1)S(1)}, u32[]{:S(2)}, u32[]{:S(2)}) collective-permute-start(bf16[64,768]{1,0:T(8,128)(2,1)S(1)} %add.7.held), channel_id=1, source_target_pairs={{0,8},{1,9},{2,10},{3,11},{4,12},{5,13},{6,14},{7,15},{8,0},{9,1},... | collective-permute-start | bytes 294920 | tf_op jit(solution)/shard_map/ppermute | solution.py:272
  53.0 1.7 %collective-permute-start.18 = (bf16[64,768]{1,0:T(8,128)(2,1)S(1)}, bf16[64,768]{1,0:T(8,128)(2,1)S(1)}, u32[]{:S(2)}, u32[]{:S(2)}) collective-permute-start(bf16[64,768]{1,0:T(8,128)(2,1)S(1)} %add.11.refs_0_), channel_id=1, source_target_pairs={{0,1},{1,0},{2,3},{3,2},{4,5},{5,4},{6,7},{7,6},{8,9},{9,8},{10,11... | collective-permute-start | bytes 294920 | tf_op jit(solution)/shard_map/ppermute | solution.py:272
  54.7 1.4 %collective-permute-start.14 = (bf16[64,768]{1,0:T(8,128)(2,1)S(1)}, bf16[64,768]{1,0:T(8,128)(2,1)S(1)}, u32[]{:S(2)}, u32[]{:S(2)}) collective-permute-start(bf16[64,768]{1,0:T(8,128)(2,1)S(1)} %add.8.refs_1_), channel_id=1, source_target_pairs={{0,1},{1,0},{2,3},{3,2},{4,5},{5,4},{6,7},{7,6},{8,9},{9,8},{10,11... | collective-permute-start | bytes 294920 | tf_op jit(solution)/shard_map/ppermute | solution.py:272

commit v16 on v15

--- a/solution.py
+++ b/solution.py
@@ -375,12 +375,18 @@
     full = (blocks, rows, block)
     scale = 1.0 / math.sqrt(width)
 
-    off_a, queries, embeddings = call(
+    off_a, queries, embeddings, lists = call(
         functools.partial(project_kernel, scale=scale),
         "project",
         [HBM] * 3,
-        [one, in_vmem(queries.shape, BF16), in_vmem(embeddings.shape, BF16)],
-        scratch=[pltpu.SMEM(lists.shape, jnp.int32), pltpu.SemaphoreType.DMA((2 + blocks,))],
+        [
+            one,
+            in_vmem(queries.shape, BF16),
+            in_vmem(embeddings.shape, BF16),
+            pltpu.SMEM(lists.shape, jnp.int32),
+        ],
+        out_specs=[VMEM] * 3 + [SMEM],
+        scratch=[pltpu.SemaphoreType.DMA((2 + blocks,))],
     )(*(pltpu.with_memory_space_constraint(x, pltpu.HBM) for x in (lists, queries, embeddings)))
     from_off_a = off_swap(off_a)
     own, off_b, *for_on = call(

time: 56.8 us -> 55.8 us (0.982)
  Pallas kernels: 25.9 us -> 18.5 us
  starting transfers between devices: 22.6 us -> 26.8 us
  waiting for transfers between devices: 7.33 us -> 9.25 us
    ppermute x15, starting transfers between devices: 11.9 us -> 16.1 us  [exchange(): return lax.ppermute(value, AXIS, [(i, i ^ mask) for i in range(count)])]
    ppermute x15, waiting for transfers between devices: 5.05 us -> 9.24 us  [exchange(): return lax.ppermute(value, AXIS, [(i, i ^ mask) for i in range(count)])]
    pallas_call x4, Pallas kernels: 6.94 us -> 4.57 us  [embed(): call(functools.partial(embed_kernel, blocks=blocks, turn=turn, scale=1.0...]
    ppermute x4, waiting for transfers between devices: 2.28 us -> 0.01 us  [off_swap(): return lax.ppermute(value, AXIS, off_route)]
    pallas_call x2, Pallas kernels: 1.7 us -> 0.58 us  [query_end(): call(functools.partial(query_end_kernel, blocks=blocks, own=own), 'query_...]
    pallas_call x2, Pallas kernels: 3.53 us -> 2.42 us  [signal_of(): call(functools.partial(signal_kernel, slot=slot), 'signal', [SMEM] + [VME...]
    pallas_call x1, Pallas kernels: 1.35 us -> 0.76 us  [per_device(): call(base_kernel, 'base', [SMEM] + [VMEM] * 5, in_vmem(full, F32), scratc...]
    pallas_call x1, Pallas kernels: 1.4 us -> 0.82 us  [per_device(): call(push_kernel, 'push', [SMEM, VMEM, VMEM], thirds, scratch=[pltpu.VMEM...]
  transfers between devices with their start and end apart: 19 -> 19, of which waited for: 6 -> 6; matrix products, arithmetic and copies ran while one was open for 0% -> 0% of each run, Pallas kernels for 39% -> 28%
where the time goes in v16:
time: 55.8 us; the launch traced here: 55.4 us
  starting transfers between devices  26.8 us (48%)
  Pallas kernels  18.5 us (33%)
  waiting for transfers between devices  9.25 us (17%)
  between operations  0.95 us (2%)
    ppermute x15, starting transfers between devices, exchange(): return lax.ppermute(value, AXIS, [(i, i ^ mask) for i in range(count)])  16.1 us
    ppermute x4, starting transfers between devices, off_swap(): return lax.ppermute(value, AXIS, off_route)  10.7 us
    ppermute x15, waiting for transfers between devices, exchange(): return lax.ppermute(value, AXIS, [(i, i ^ mask) for i in range(count)])  9.24 us
    pallas_call x4, Pallas kernels, embed(): call(functools.partial(embed_kernel, blocks=blocks, turn=turn, scale=1.0...  4.57 us
    pallas_call x1, Pallas kernels, per_device(): call(hits_kernel, 'hits', [VMEM, HBM], [in_vmem(full, BF16), in_vmem(edge...  2.45 us
    pallas_call x2, Pallas kernels, signal_of(): call(functools.partial(signal_kernel, slot=slot), 'signal', [SMEM] + [VME...  2.42 us
    pallas_call x1, Pallas kernels, per_device(): call(functools.partial(project_kernel, scale=scale), 'project', [HBM] * 3...  2.02 us
    pallas_call x2, Pallas kernels, place(): call(functools.partial(place_kernel, places=places), 'place', [VMEM] * le...  1.55 us
  transfers between devices with their start and end apart: 19, of which 6 were waited for; matrix products, arithmetic and copies ran while one was open for 0% of the time, Pallas kernels for 28%

profile of v16, /device:TPU:0, one launch (start us, length us, event | category | flops | bytes accessed | tf_op | source)
XLA Modules:
  0.0 55.4 jit_solution(5983536660792853757)
XLA Ops:
  0.6 2.0 %project.1 = (bf16[256,512]{1,0:T(8,128)(2,1)S(1)}, bf16[256,768]{1,0:T(8,128)(2,1)S(1)}, bf16[2048,768]{1,0:T(8,128)(2,1)S(1)}, s32[2,64]{1,0:T(2,128)S(4)}) custom-call(s32[2,64]{1,0:T(2,128)} %bitcast.6, bf16[256,768]{1,0:T(8,128)(2,1)} %queries.1, bf16[2048,768]{1,0:T(8,128)(2,1)} %embeddings.1), custom_call_target="tpu_custom_call" | custom-call | tf_op jit(solution)/shard_map/project/pallas_call | solution.py:378
  2.7 5.5 %collective-permute-start.4 = (bf16[256,512]{1,0:T(8,128)(2,1)S(1)}, bf16[256,512]{1,0:T(8,128)(2,1)S(1)}, u32[]{:S(2)}, u32[]{:S(2)}) collective-permute-start(bf16[256,512]{1,0:T(8,128)(2,1)S(1)} %get-tuple-element.44), channel_id=1, source_target_pairs={{1,2},{3,4},{5,6},{7,8},{9,10},{11,12},{13,14},{15,0},{2,1},{4,3},... | collective-permute-start | bytes 786440 | tf_op jit(solution)/shard_map/ppermute | solution.py:366
  8.2 1.1 %own.1 = (f32[4,256,512]{2,1,0:T(8,128)S(1)}, bf16[256,512]{1,0:T(8,128)(2,1)S(1)}, bf16[176,512]{1,0:T(8,128)(2,1)S(1)}, bf16[176,512]{1,0:T(8,128)(2,1)S(1)}, bf16[160,512]{1,0:T(8,128)(2,1)S(1)}) custom-call(s32[2,64]{1,0:T(2,128)S(4)} %get-tuple-element.34.lists, bf16[256,768]{1,0:T(8,128)(2,1)S(1)} %get-tuple-element.35.queries, ...), custom_call_target="tpu_custom_call" | custom-call | tf_op jit(solution)/shard_map/own/pallas_call | solution.py:392
  9.4 0.5 collective-permute-start.1
  9.9 0.7 %collective-permute-start.3 = (bf16[256,512]{1,0:T(8,128)(2,1)S(1)}, bf16[256,512]{1,0:T(8,128)(2,1)S(1)}, u32[]{:S(2)}, u32[]{:S(2)}) collective-permute-start(bf16[256,512]{1,0:T(8,128)(2,1)S(1)} %get-tuple-element.43), channel_id=1, source_target_pairs={{1,2},{3,4},{5,6},{7,8},{9,10},{11,12},{13,14},{15,0},{2,1},{4,3},... | collective-permute-start | bytes 786440 | tf_op jit(solution)/shard_map/ppermute | solution.py:366
  10.7 2.4 %hits.1 = (bf16[4,256,512]{2,1,0:T(8,128)(2,1)S(1)}, bf16[4,2,512,512]{3,2,1,0:T(8,128)(2,1)S(1)}) custom-call(s32[8,256]{1,0:T(8,128)S(1)} %bitcast.5, bf16[4,2,512,512]{3,2,1,0:T(8,128)(2,1)} %tiles.1), custom_call_target="tpu_custom_call" | custom-call | tf_op jit(solution)/shard_map/hits/pallas_call | solution.py:399
  13.2 0.8 %base.1 = f32[4,256,512]{2,1,0:T(8,128)S(1)} custom-call(s32[2,64]{1,0:T(2,128)S(4)} %get-tuple-element.34.lists, f32[4,256,512]{2,1,0:T(8,128)S(1)} %get-tuple-element.37.own, bf16[4,2,512,512]{3,2,1,0:T(8,128)(2,1)S(1)} %get-tuple-element.38.tiles, bf16[176,512]{1,0:T(8,128)(2,1)S(1)} %collective-permute-done.rest_0_, ...), custom_call_target="tpu_custom_call" | custom-call | tf_op jit(solution)/shard_map/base/pallas_call | solution.py:407
  13.9 1.2 %signal.2 = (bf16[4,256,512]{2,1,0:T(8,128)(2,1)S(1)}, bf16[256,512]{1,0:T(8,128)(2,1)S(1)}) custom-call(s32[2,64]{1,0:T(2,128)S(4)} %get-tuple-element.34.lists, f32[4,256,512]{2,1,0:T(8,128)S(1)} %base.1, bf16[4,256,512]{2,1,0:T(8,128)(2,1)S(1)} %get-tuple-element.42.hits, f32[1,2048]{1,0:T(1,128)S(1)} %bitcast.3, ...), custom_call_target="tpu_custom_call" | custom-call | flops 2000000000 | tf_op jit(solution)/shard_map/signal/pallas_call | solution.py:417
  15.2 4.4 %collective-permute-start.5 = (bf16[256,512]{1,0:T(8,128)(2,1)S(1)}, bf16[256,512]{1,0:T(8,128)(2,1)S(1)}, u32[]{:S(2)}, u32[]{:S(2)}) collective-permute-start(bf16[256,512]{1,0:T(8,128)(2,1)S(1)} %get-tuple-element.47), channel_id=1, source_target_pairs={{1,2},{3,4},{5,6},{7,8},{9,10},{11,12},{13,14},{15,0},{2,1},{4,3},... | collective-permute-start | bytes 786440 | tf_op jit(solution)/shard_map/ppermute | solution.py:366
  19.5 1.2 %signal.3 = (bf16[4,256,512]{2,1,0:T(8,128)(2,1)S(1)}, bf16[256,512]{1,0:T(8,128)(2,1)S(1)}) custom-call(s32[2,64]{1,0:T(2,128)S(4)} %get-tuple-element.34.lists, f32[4,256,512]{2,1,0:T(8,128)S(1)} %base.1, bf16[4,256,512]{2,1,0:T(8,128)(2,1)S(1)} %get-tuple-element.42.hits, f32[1,2048]{1,0:T(1,128)S(1)} %bitcast.4, ...), custom_call_target="tpu_custom_call", output_to_operand_aliasing={{0}: (6, {})} | custom-call | tf_op jit(solution)/shard_map/signal/pallas_call | solution.py:417
  20.8 0.8 %push.1 = (bf16[176,512]{1,0:T(8,128)(2,1)S(1)}, bf16[176,512]{1,0:T(8,128)(2,1)S(1)}, bf16[160,512]{1,0:T(8,128)(2,1)S(1)}) custom-call(s32[2,64]{1,0:T(2,128)S(4)} %get-tuple-element.34.lists, bf16[4,256,512]{2,1,0:T(8,128)(2,1)S(1)} %get-tuple-element.46.signal, bf16[4,2,512,512]{3,2,1,0:T(8,128)(2,1)S(1)} %get-tuple-element.38.tiles), custom_call_target="tpu_custom_call" | custom-call | tf_op jit(solution)/shard_map/push/pallas_call | solution.py:431
  21.7 6.7 %collective-permute-start.6 = (bf16[176,512]{1,0:T(8,128)(2,1)S(1)}, bf16[176,512]{1,0:T(8,128)(2,1)S(1)}, u32[]{:S(2)}, u32[]{:S(2)}) collective-permute-start(bf16[176,512]{1,0:T(8,128)(2,1)S(1)} %get-tuple-element.48), channel_id=1, source_target_pairs={{0,1},{1,0},{2,3},{3,2},{4,5},{5,4},{6,7},{7,6},{8,9},{9,8},{10,11... | collective-permute-start | bytes 540680 | tf_op jit(solution)/shard_map/ppermute | solution.py:272
  28.5 0.4 collective-permute-start.8
  28.9 1.0 %query.1.part = f32[256,768]{1,0:T(8,128)S(1)} custom-call(bf16[4,256,512]{2,1,0:T(8,128)(2,1)S(1)} %get-tuple-element.46.signal, bf16[2048,768]{1,0:T(8,128)(2,1)S(1)} %get-tuple-element.36.embeddings), custom_call_target="tpu_custom_call" | custom-call | tf_op jit(solution)/shard_map/query/pallas_call | solution.py:441
  30.3 0.6 %query_on.1 = (f32[256,768]{1,0:T(8,128)S(1)}, bf16[2,256,512]{2,1,0:T(8,128)(2,1)S(1)}) custom-call(s32[2,64]{1,0:T(2,128)S(4)} %get-tuple-element.34.lists, f32[256,768]{1,0:T(8,128)S(1)} %query_half.1.part, bf16[2048,768]{1,0:T(8,128)(2,1)S(1)} %get-tuple-element.36.embeddings, bf16[176,512]{1,0:T(8,128)(2,1)S(1)} %collective-permute-done.6.rest_0_, ...), custom_call_target="tpu_custom_call" | custom-call | tf_op jit(solution)/shard_map/query_on/pallas_call | solution.py:449
  31.0 0.5 embed.4
  31.8 0.5 collective-permute-start.10
  32.6 0.8 %collective-permute-done.10.got = bf16[128,768]{1,0:T(8,128)(2,1)S(1)} collective-permute-done((bf16[128,768]{1,0:T(8,128)(2,1)S(1)}, bf16[128,768]{1,0:T(8,128)(2,1)S(1)}, u32[]{:S(2)}, u32[]{:S(2)}) %collective-permute-start.10) | collective-permute-done | bytes 196640 | tf_op jit(solution)/shard_map/ppermute | solution.py:272
  33.4 1.7 %collective-permute-start.15 = (bf16[64,768]{1,0:T(8,128)(2,1)S(1)}, bf16[64,768]{1,0:T(8,128)(2,1)S(1)}, u32[]{:S(2)}, u32[]{:S(2)}) collective-permute-start(bf16[64,768]{1,0:T(8,128)(2,1)S(1)} %get-tuple-element.62.held), channel_id=1, source_target_pairs={{0,2},{1,3},{2,0},{3,1},{4,6},{5,7},{6,4},{7,5},{8,10},{9,11},{10,... | collective-permute-start | bytes 294920 | tf_op jit(solution)/shard_map/ppermute | solution.py:272
  35.1 0.4 collective-permute-start.11
  35.5 0.9 %embed.5 = (bf16[2048,768]{1,0:T(8,128)(2,1)}, bf16[512,768]{1,0:T(8,128)(2,1)S(1)}, f32[8,128]{1,0:T(8,128)S(1)}) custom-call(s32[2,64]{1,0:T(2,128)S(4)} %get-tuple-element.34.lists, bf16[4,256,512]{2,1,0:T(8,128)(2,1)S(1)} %get-tuple-element.46.signal, bf16[2,256,512]{2,1,0:T(8,128)(2,1)S(1)} %get-tuple-element.51.on, ...), custom_call_target="tpu_custom_call" | custom-call | tf_op jit(solution)/shard_map/embed/pallas_call | solution.py:457
  36.4 2.1 %collective-permute-done.15.got = bf16[64,768]{1,0:T(8,128)(2,1)S(1)} collective-permute-done((bf16[64,768]{1,0:T(8,128)(2,1)S(1)}, bf16[64,768]{1,0:T(8,128)(2,1)S(1)}, u32[]{:S(2)}, u32[]{:S(2)}) %collective-permute-start.15) | collective-permute-done | bytes 98336 | tf_op jit(solution)/shard_map/ppermute | solution.py:272
  38.6 1.7 %collective-permute-start.16 = (bf16[64,768]{1,0:T(8,128)(2,1)S(1)}, bf16[64,768]{1,0:T(8,128)(2,1)S(1)}, u32[]{:S(2)}, u32[]{:S(2)}) collective-permute-start(bf16[64,768]{1,0:T(8,128)(2,1)S(1)} %add.9.held), channel_id=1, source_target_pairs={{0,8},{1,9},{2,10},{3,11},{4,12},{5,13},{6,14},{7,15},{8,0},{9,1},... | collective-permute-start | bytes 294920 | tf_op jit(solution)/shard_map/ppermute | solution.py:272
  40.7 0.9 %embed.6 = (bf16[2048,768]{1,0:T(8,128)(2,1)}, bf16[512,768]{1,0:T(8,128)(2,1)S(1)}, f32[8,128]{1,0:T(8,128)S(1)}) custom-call(s32[2,64]{1,0:T(2,128)S(4)} %get-tuple-element.34.lists, bf16[4,256,512]{2,1,0:T(8,128)(2,1)S(1)} %get-tuple-element.46.signal, bf16[2,256,512]{2,1,0:T(8,128)(2,1)S(1)} %get-tuple-element.51.on, ...), custom_call_target="tpu_custom_call", output_to_operand_aliasing={{0}: (6, {})} | custom-call | tf_op jit(solution)/shard_map/embed/pallas_call | solution.py:457
  41.6 3.8 %collective-permute-done.16.got = bf16[64,768]{1,0:T(8,128)(2,1)S(1)} collective-permute-done((bf16[64,768]{1,0:T(8,128)(2,1)S(1)}, bf16[64,768]{1,0:T(8,128)(2,1)S(1)}, u32[]{:S(2)}, u32[]{:S(2)}) %collective-permute-start.16) | collective-permute-done | bytes 98336 | tf_op jit(solution)/shard_map/ppermute | solution.py:272
  45.6 3.2 %collective-permute-start.13 = (bf16[64,768]{1,0:T(8,128)(2,1)S(1)}, bf16[64,768]{1,0:T(8,128)(2,1)S(1)}, u32[]{:S(2)}, u32[]{:S(2)}) collective-permute-start(bf16[64,768]{1,0:T(8,128)(2,1)S(1)} %add.7.held), channel_id=1, source_target_pairs={{0,8},{1,9},{2,10},{3,11},{4,12},{5,13},{6,14},{7,15},{8,0},{9,1},... | collective-permute-start | bytes 294920 | tf_op jit(solution)/shard_map/ppermute | solution.py:272
  48.9 2.3 %embed.7 = (bf16[2048,768]{1,0:T(8,128)(2,1)}, bf16[512,768]{1,0:T(8,128)(2,1)}, f32[8,128]{1,0:T(8,128)S(1)}) custom-call(s32[2,64]{1,0:T(2,128)S(4)} %get-tuple-element.34.lists, bf16[4,256,512]{2,1,0:T(8,128)(2,1)S(1)} %get-tuple-element.46.signal, bf16[2,256,512]{2,1,0:T(8,128)(2,1)S(1)} %get-tuple-element.51.on, ...), custom_call_target="tpu_custom_call", output_to_operand_aliasing={{0}: (7, {})} | custom-call | tf_op jit(solution)/shard_map/embed/pallas_call | solution.py:457
  51.1 0.7 %collective-permute-done.17.got = bf16[64,768]{1,0:T(8,128)(2,1)S(1)} collective-permute-done((bf16[64,768]{1,0:T(8,128)(2,1)S(1)}, bf16[64,768]{1,0:T(8,128)(2,1)S(1)}, u32[]{:S(2)}, u32[]{:S(2)}) %collective-permute-start.17) | collective-permute-done | bytes 98336 | tf_op jit(solution)/shard_map/ppermute | solution.py:272
  52.0 1.4 %collective-permute-done.13.got = bf16[64,768]{1,0:T(8,128)(2,1)S(1)} collective-permute-done((bf16[64,768]{1,0:T(8,128)(2,1)S(1)}, bf16[64,768]{1,0:T(8,128)(2,1)S(1)}, u32[]{:S(2)}, u32[]{:S(2)}) %collective-permute-start.13) | collective-permute-done | bytes 98336 | tf_op jit(solution)/shard_map/ppermute | solution.py:272
  53.5 0.8 %place.2.refs_1_ = f32[256,768]{1,0:T(8,128)} custom-call(bf16[64,768]{1,0:T(8,128)(2,1)S(1)} %add.11.refs_0_, bf16[64,768]{1,0:T(8,128)(2,1)S(1)} %add.8.refs_1_, bf16[64,768]{1,0:T(8,128)(2,1)S(1)} %collective-permute-done.18.refs_2_), custom_call_target="tpu_custom_call" | custom-call | tf_op jit(solution)/shard_map/place/pallas_call | solution.py:339
  54.3 0.4 collective-permute-done.14.refs_0_
  54.7 0.7 %place.3 = f32[256,768]{1,0:T(8,128)} custom-call(bf16[64,768]{1,0:T(8,128)(2,1)S(1)} %collective-permute-done.14.refs_0_, f32[256,768]{1,0:T(8,128)} %place.2.refs_1_), custom_call_target="tpu_custom_call", output_to_operand_aliasing={{}: (1, {})} | custom-call | tf_op jit(solution)/shard_map/place/pallas_call | solution.py:339
  (35 shorter events, 2.1 us)
Async XLA Ops:
  0.6 10.0 %copy-start.1 = (s32[256,8]{0,1:T(8,128)S(1)}, s32[256,8]{0,1:T(8,128)}, u32[]{:S(2)}) copy-start(s32[256,8]{0,1:T(8,128)} %param.11) | copy-start | bytes 24580
  2.7 11.3 %collective-permute-start.4 = (bf16[256,512]{1,0:T(8,128)(2,1)S(1)}, bf16[256,512]{1,0:T(8,128)(2,1)S(1)}, u32[]{:S(2)}, u32[]{:S(2)}) collective-permute-start(bf16[256,512]{1,0:T(8,128)(2,1)S(1)} %get-tuple-element.44), channel_id=1, source_target_pairs={{1,2},{3,4},{5,6},{7,8},{9,10},{11,12},{13,14},{15,0},{2,1},{4,3},... | collective-permute-start | bytes 786440 | tf_op jit(solution)/shard_map/ppermute | solution.py:366
  9.3 3.8 %collective-permute-start = (bf16[176,512]{1,0:T(8,128)(2,1)S(1)}, bf16[176,512]{1,0:T(8,128)(2,1)S(1)}, u32[]{:S(2)}, u32[]{:S(2)}) collective-permute-start(bf16[176,512]{1,0:T(8,128)(2,1)S(1)} %get-tuple-element.39), channel_id=1, source_target_pairs={{0,1},{1,0},{2,3},{3,2},{4,5},{5,4},{6,7},{7,6},{8,9},{9,8},{10,11... | collective-permute-start | bytes 540680 | tf_op jit(solution)/shard_map/ppermute | solution.py:272
  9.4 3.8 %collective-permute-start.1 = (bf16[176,512]{1,0:T(8,128)(2,1)S(1)}, bf16[176,512]{1,0:T(8,128)(2,1)S(1)}, u32[]{:S(2)}, u32[]{:S(2)}) collective-permute-start(bf16[176,512]{1,0:T(8,128)(2,1)S(1)} %get-tuple-element.40), channel_id=1, source_target_pairs={{0,1},{1,0},{2,3},{3,2},{4,5},{5,4},{6,7},{7,6},{8,9},{9,8},{10,11... | collective-permute-start | bytes 540680 | tf_op jit(solution)/shard_map/ppermute | solution.py:272
  9.9 3.3 %collective-permute-start.2 = (bf16[160,512]{1,0:T(8,128)(2,1)S(1)}, bf16[160,512]{1,0:T(8,128)(2,1)S(1)}, u32[]{:S(2)}, u32[]{:S(2)}) collective-permute-start(bf16[160,512]{1,0:T(8,128)(2,1)S(1)} %get-tuple-element.41), channel_id=1, source_target_pairs={{0,1},{1,0},{2,3},{3,2},{4,5},{5,4},{6,7},{7,6},{8,9},{9,8},{10,11... | collective-permute-start | bytes 491528 | tf_op jit(solution)/shard_map/ppermute | solution.py:272
  9.9 9.6 %collective-permute-start.3 = (bf16[256,512]{1,0:T(8,128)(2,1)S(1)}, bf16[256,512]{1,0:T(8,128)(2,1)S(1)}, u32[]{:S(2)}, u32[]{:S(2)}) collective-permute-start(bf16[256,512]{1,0:T(8,128)(2,1)S(1)} %get-tuple-element.43), channel_id=1, source_target_pairs={{1,2},{3,4},{5,6},{7,8},{9,10},{11,12},{13,14},{15,0},{2,1},{4,3},... | collective-permute-start | bytes 786440 | tf_op jit(solution)/shard_map/ppermute | solution.py:366
  13.1 0.8 %copy-start = (f32[2048]{0:T(1024)S(1)}, f32[2048]{0:T(1024)}, u32[]{:S(2)}) copy-start(f32[2048]{0:T(1024)} %param.9) | copy-start | bytes 24580
  15.2 14.7 %collective-permute-start.5 = (bf16[256,512]{1,0:T(8,128)(2,1)S(1)}, bf16[256,512]{1,0:T(8,128)(2,1)S(1)}, u32[]{:S(2)}, u32[]{:S(2)}) collective-permute-start(bf16[256,512]{1,0:T(8,128)(2,1)S(1)} %get-tuple-element.47), channel_id=1, source_target_pairs={{1,2},{3,4},{5,6},{7,8},{9,10},{11,12},{13,14},{15,0},{2,1},{4,3},... | collective-permute-start | bytes 786440 | tf_op jit(solution)/shard_map/ppermute | solution.py:366
  20.7 10.7 %collective-permute-start.9 = (bf16[256,512]{1,0:T(8,128)(2,1)S(1)}, bf16[256,512]{1,0:T(8,128)(2,1)S(1)}, u32[]{:S(2)}, u32[]{:S(2)}) collective-permute-start(bf16[256,512]{1,0:T(8,128)(2,1)S(1)} %get-tuple-element.52), channel_id=1, source_target_pairs={{1,2},{3,4},{5,6},{7,8},{9,10},{11,12},{13,14},{15,0},{2,1},{4,3},... | collective-permute-start | bytes 786440 | tf_op jit(solution)/shard_map/ppermute | solution.py:366
  21.7 8.7 %collective-permute-start.6 = (bf16[176,512]{1,0:T(8,128)(2,1)S(1)}, bf16[176,512]{1,0:T(8,128)(2,1)S(1)}, u32[]{:S(2)}, u32[]{:S(2)}) collective-permute-start(bf16[176,512]{1,0:T(8,128)(2,1)S(1)} %get-tuple-element.48), channel_id=1, source_target_pairs={{0,1},{1,0},{2,3},{3,2},{4,5},{5,4},{6,7},{7,6},{8,9},{9,8},{10,11... | collective-permute-start | bytes 540680 | tf_op jit(solution)/shard_map/ppermute | solution.py:272
  28.4 1.9 %collective-permute-start.7 = (bf16[176,512]{1,0:T(8,128)(2,1)S(1)}, bf16[176,512]{1,0:T(8,128)(2,1)S(1)}, u32[]{:S(2)}, u32[]{:S(2)}) collective-permute-start(bf16[176,512]{1,0:T(8,128)(2,1)S(1)} %get-tuple-element.49), channel_id=1, source_target_pairs={{0,1},{1,0},{2,3},{3,2},{4,5},{5,4},{6,7},{7,6},{8,9},{9,8},{10,11... | collective-permute-start | bytes 540680 | tf_op jit(solution)/shard_map/ppermute | solution.py:272
  28.5 1.8 %collective-permute-start.8 = (bf16[160,512]{1,0:T(8,128)(2,1)S(1)}, bf16[160,512]{1,0:T(8,128)(2,1)S(1)}, u32[]{:S(2)}, u32[]{:S(2)}) collective-permute-start(bf16[160,512]{1,0:T(8,128)(2,1)S(1)} %get-tuple-element.50), channel_id=1, source_target_pairs={{0,1},{1,0},{2,3},{3,2},{4,5},{5,4},{6,7},{7,6},{8,9},{9,8},{10,11... | collective-permute-start | bytes 491528 | tf_op jit(solution)/shard_map/ppermute | solution.py:272
  31.8 1.6 %collective-permute-start.10 = (bf16[128,768]{1,0:T(8,128)(2,1)S(1)}, bf16[128,768]{1,0:T(8,128)(2,1)S(1)}, u32[]{:S(2)}, u32[]{:S(2)}) collective-permute-start(bf16[128,768]{1,0:T(8,128)(2,1)S(1)} %query_end.3), channel_id=1, source_target_pairs={{0,1},{1,0},{2,3},{3,2},{4,5},{5,4},{6,7},{7,6},{8,9},{9,8},{10,11... | collective-permute-start | bytes 589832 | tf_op jit(solution)/shard_map/ppermute | solution.py:272
  33.4 5.1 %collective-permute-start.15 = (bf16[64,768]{1,0:T(8,128)(2,1)S(1)}, bf16[64,768]{1,0:T(8,128)(2,1)S(1)}, u32[]{:S(2)}, u32[]{:S(2)}) collective-permute-start(bf16[64,768]{1,0:T(8,128)(2,1)S(1)} %get-tuple-element.62.held), channel_id=1, source_target_pairs={{0,2},{1,3},{2,0},{3,1},{4,6},{5,7},{6,4},{7,5},{8,10},{9,11},{10,... | collective-permute-start | bytes 294920 | tf_op jit(solution)/shard_map/ppermute | solution.py:272
  35.1 5.2 %collective-permute-start.11 = (bf16[64,768]{1,0:T(8,128)(2,1)S(1)}, bf16[64,768]{1,0:T(8,128)(2,1)S(1)}, u32[]{:S(2)}, u32[]{:S(2)}) collective-permute-start(bf16[64,768]{1,0:T(8,128)(2,1)S(1)} %get-tuple-element.61.held), channel_id=1, source_target_pairs={{0,4},{1,5},{2,6},{3,7},{4,0},{5,1},{6,2},{7,3},{8,12},{9,13},{10,... | collective-permute-start | bytes 294920 | tf_op jit(solution)/shard_map/ppermute | solution.py:272
  38.6 6.9 %collective-permute-start.16 = (bf16[64,768]{1,0:T(8,128)(2,1)S(1)}, bf16[64,768]{1,0:T(8,128)(2,1)S(1)}, u32[]{:S(2)}, u32[]{:S(2)}) collective-permute-start(bf16[64,768]{1,0:T(8,128)(2,1)S(1)} %add.9.held), channel_id=1, source_target_pairs={{0,8},{1,9},{2,10},{3,11},{4,12},{5,13},{6,14},{7,15},{8,0},{9,1},... | collective-permute-start | bytes 294920 | tf_op jit(solution)/shard_map/ppermute | solution.py:272
  40.3 5.3 %collective-permute-start.12 = (bf16[64,768]{1,0:T(8,128)(2,1)S(1)}, bf16[64,768]{1,0:T(8,128)(2,1)S(1)}, u32[]{:S(2)}, u32[]{:S(2)}) collective-permute-start(bf16[64,768]{1,0:T(8,128)(2,1)S(1)} %add.6.held), channel_id=1, source_target_pairs={{0,2},{1,3},{2,0},{3,1},{4,6},{5,7},{6,4},{7,5},{8,10},{9,11},{10,... | collective-permute-start | bytes 294920 | tf_op jit(solution)/shard_map/ppermute | solution.py:272
  45.5 6.4 %collective-permute-start.17 = (bf16[64,768]{1,0:T(8,128)(2,1)S(1)}, bf16[64,768]{1,0:T(8,128)(2,1)S(1)}, u32[]{:S(2)}, u32[]{:S(2)}) collective-permute-start(bf16[64,768]{1,0:T(8,128)(2,1)S(1)} %add.10.held), channel_id=1, source_target_pairs={{0,4},{1,5},{2,6},{3,7},{4,0},{5,1},{6,2},{7,3},{8,12},{9,13},{10,... | collective-permute-start | bytes 294920 | tf_op jit(solution)/shard_map/ppermute | solution.py:272
  45.6 7.7 %collective-permute-start.13 = (bf16[64,768]{1,0:T(8,128)(2,1)S(1)}, bf16[64,768]{1,0:T(8,128)(2,1)S(1)}, u32[]{:S(2)}, u32[]{:S(2)}) collective-permute-start(bf16[64,768]{1,0:T(8,128)(2,1)S(1)} %add.7.held), channel_id=1, source_target_pairs={{0,8},{1,9},{2,10},{3,11},{4,12},{5,13},{6,14},{7,15},{8,0},{9,1},... | collective-permute-start | bytes 294920 | tf_op jit(solution)/shard_map/ppermute | solution.py:272
  51.9 1.6 %collective-permute-start.18 = (bf16[64,768]{1,0:T(8,128)(2,1)S(1)}, bf16[64,768]{1,0:T(8,128)(2,1)S(1)}, u32[]{:S(2)}, u32[]{:S(2)}) collective-permute-start(bf16[64,768]{1,0:T(8,128)(2,1)S(1)} %add.11.refs_0_), channel_id=1, source_target_pairs={{0,1},{1,0},{2,3},{3,2},{4,5},{5,4},{6,7},{7,6},{8,9},{9,8},{10,11... | collective-permute-start | bytes 294920 | tf_op jit(solution)/shard_map/ppermute | solution.py:272
  53.4 1.4 %collective-permute-start.14 = (bf16[64,768]{1,0:T(8,128)(2,1)S(1)}, bf16[64,768]{1,0:T(8,128)(2,1)S(1)}, u32[]{:S(2)}, u32[]{:S(2)}) collective-permute-start(bf16[64,768]{1,0:T(8,128)(2,1)S(1)} %add.8.refs_1_), channel_id=1, source_target_pairs={{0,1},{1,0},{2,3},{3,2},{4,5},{5,4},{6,7},{7,6},{8,9},{9,8},{10,11... | collective-permute-start | bytes 294920 | tf_op jit(solution)/shard_map/ppermute | solution.py:272

commit v17 on v16

--- a/solution.py
+++ b/solution.py
@@ -317,7 +317,7 @@
         both = jnp.where(lax.axis_index(AXIS) % 2 == 0, both, both[::-1])
         return both.reshape(2 * rows, width) * scale
     bits = [1 << k for k in range(1, count.bit_length() - 1)]
-    orders = [[bits[0], *bits[2:], bits[1]], [bits[1], bits[0], *bits[2:]]]
+    orders = [bits, bits[-1:] + bits[:-1]]
     piece = in_vmem((rows // 2, width), BF16)
     held = list(call(halve_kernel, "halve", [VMEM] * 2, [piece, piece])(kept, got))
     swapped = []

time: 55.8 us -> 55.2 us (0.989)
  waiting for transfers between devices: 9.25 us -> 7.66 us
  starting transfers between devices: 26.8 us -> 27.4 us
    ppermute x15, waiting for transfers between devices: 9.24 us -> 4.51 us  [exchange(): return lax.ppermute(value, AXIS, [(i, i ^ mask) for i in range(count)])]
    ppermute x4, waiting for transfers between devices: 0.01 us -> 3.15 us  [off_swap(): return lax.ppermute(value, AXIS, off_route)]
  transfers between devices with their start and end apart: 19 -> 19, of which waited for: 6 -> 8; matrix products, arithmetic and copies ran while one was open for 0% -> 0% of each run, Pallas kernels for 28% -> 28%
where the time goes in v17:
time: 55.2 us; the launch traced here: 54.4 us
  starting transfers between devices  27.4 us (50%)
  Pallas kernels  18.5 us (34%)
  waiting for transfers between devices  7.66 us (14%)
  between operations  0.91 us (2%)
    ppermute x15, starting transfers between devices, exchange(): return lax.ppermute(value, AXIS, [(i, i ^ mask) for i in range(count)])  16.5 us
    ppermute x4, starting transfers between devices, off_swap(): return lax.ppermute(value, AXIS, off_route)  10.9 us
    pallas_call x4, Pallas kernels, embed(): call(functools.partial(embed_kernel, blocks=blocks, turn=turn, scale=1.0...  4.61 us
    ppermute x15, waiting for transfers between devices, exchange(): return lax.ppermute(value, AXIS, [(i, i ^ mask) for i in range(count)])  4.51 us
    ppermute x4, waiting for transfers between devices, off_swap(): return lax.ppermute(value, AXIS, off_route)  3.15 us
    pallas_call x1, Pallas kernels, per_device(): call(hits_kernel, 'hits', [VMEM, HBM], [in_vmem(full, BF16), in_vmem(edge...  2.45 us
    pallas_call x2, Pallas kernels, signal_of(): call(functools.partial(signal_kernel, slot=slot), 'signal', [SMEM] + [VME...  2.41 us
    pallas_call x1, Pallas kernels, per_device(): call(functools.partial(project_kernel, scale=scale), 'project', [HBM] * 3...  2.02 us
  transfers between devices with their start and end apart: 19, of which 8 were waited for; matrix products, arithmetic and copies ran while one was open for 0% of the time, Pallas kernels for 28%

profile of v17, /device:TPU:0, one launch (start us, length us, event | category | flops | bytes accessed | tf_op | source)
XLA Modules:
  0.0 54.4 jit_solution(14497683449928964083)
XLA Ops:
  0.6 2.0 %project.1 = (bf16[256,512]{1,0:T(8,128)(2,1)S(1)}, bf16[256,768]{1,0:T(8,128)(2,1)S(1)}, bf16[2048,768]{1,0:T(8,128)(2,1)S(1)}, s32[2,64]{1,0:T(2,128)S(4)}) custom-call(s32[2,64]{1,0:T(2,128)} %bitcast.6, bf16[256,768]{1,0:T(8,128)(2,1)} %queries.1, bf16[2048,768]{1,0:T(8,128)(2,1)} %embeddings.1), custom_call_target="tpu_custom_call" | custom-call | tf_op jit(solution)/shard_map/project/pallas_call | solution.py:378
  2.7 5.7 %collective-permute-start.4 = (bf16[256,512]{1,0:T(8,128)(2,1)S(1)}, bf16[256,512]{1,0:T(8,128)(2,1)S(1)}, u32[]{:S(2)}, u32[]{:S(2)}) collective-permute-start(bf16[256,512]{1,0:T(8,128)(2,1)S(1)} %get-tuple-element.44), channel_id=1, source_target_pairs={{1,2},{3,4},{5,6},{7,8},{9,10},{11,12},{13,14},{15,0},{2,1},{4,3},... | collective-permute-start | bytes 786440 | tf_op jit(solution)/shard_map/ppermute | solution.py:366
  8.4 1.1 %own.1 = (f32[4,256,512]{2,1,0:T(8,128)S(1)}, bf16[256,512]{1,0:T(8,128)(2,1)S(1)}, bf16[176,512]{1,0:T(8,128)(2,1)S(1)}, bf16[176,512]{1,0:T(8,128)(2,1)S(1)}, bf16[160,512]{1,0:T(8,128)(2,1)S(1)}) custom-call(s32[2,64]{1,0:T(2,128)S(4)} %get-tuple-element.34.lists, bf16[256,768]{1,0:T(8,128)(2,1)S(1)} %get-tuple-element.35.queries, ...), custom_call_target="tpu_custom_call" | custom-call | tf_op jit(solution)/shard_map/own/pallas_call | solution.py:392
  9.5 0.5 collective-permute-start.1
  10.6 2.4 %hits.1 = (bf16[4,256,512]{2,1,0:T(8,128)(2,1)S(1)}, bf16[4,2,512,512]{3,2,1,0:T(8,128)(2,1)S(1)}) custom-call(s32[8,256]{1,0:T(8,128)S(1)} %bitcast.5, bf16[4,2,512,512]{3,2,1,0:T(8,128)(2,1)} %tiles.1), custom_call_target="tpu_custom_call" | custom-call | tf_op jit(solution)/shard_map/hits/pallas_call | solution.py:399
  13.1 0.8 %base.1 = f32[4,256,512]{2,1,0:T(8,128)S(1)} custom-call(s32[2,64]{1,0:T(2,128)S(4)} %get-tuple-element.34.lists, f32[4,256,512]{2,1,0:T(8,128)S(1)} %get-tuple-element.37.own, bf16[4,2,512,512]{3,2,1,0:T(8,128)(2,1)S(1)} %get-tuple-element.38.tiles, bf16[176,512]{1,0:T(8,128)(2,1)S(1)} %collective-permute-done.rest_0_, ...), custom_call_target="tpu_custom_call" | custom-call | tf_op jit(solution)/shard_map/base/pallas_call | solution.py:407
  13.8 1.2 %signal.2 = (bf16[4,256,512]{2,1,0:T(8,128)(2,1)S(1)}, bf16[256,512]{1,0:T(8,128)(2,1)S(1)}) custom-call(s32[2,64]{1,0:T(2,128)S(4)} %get-tuple-element.34.lists, f32[4,256,512]{2,1,0:T(8,128)S(1)} %base.1, bf16[4,256,512]{2,1,0:T(8,128)(2,1)S(1)} %get-tuple-element.42.hits, f32[1,2048]{1,0:T(1,128)S(1)} %bitcast.3, ...), custom_call_target="tpu_custom_call" | custom-call | flops 2000000000 | tf_op jit(solution)/shard_map/signal/pallas_call | solution.py:417
  15.1 4.1 %collective-permute-start.5 = (bf16[256,512]{1,0:T(8,128)(2,1)S(1)}, bf16[256,512]{1,0:T(8,128)(2,1)S(1)}, u32[]{:S(2)}, u32[]{:S(2)}) collective-permute-start(bf16[256,512]{1,0:T(8,128)(2,1)S(1)} %get-tuple-element.47), channel_id=1, source_target_pairs={{1,2},{3,4},{5,6},{7,8},{9,10},{11,12},{13,14},{15,0},{2,1},{4,3},... | collective-permute-start | bytes 786440 | tf_op jit(solution)/shard_map/ppermute | solution.py:366
  19.1 1.2 %signal.3 = (bf16[4,256,512]{2,1,0:T(8,128)(2,1)S(1)}, bf16[256,512]{1,0:T(8,128)(2,1)S(1)}) custom-call(s32[2,64]{1,0:T(2,128)S(4)} %get-tuple-element.34.lists, f32[4,256,512]{2,1,0:T(8,128)S(1)} %base.1, bf16[4,256,512]{2,1,0:T(8,128)(2,1)S(1)} %get-tuple-element.42.hits, f32[1,2048]{1,0:T(1,128)S(1)} %bitcast.4, ...), custom_call_target="tpu_custom_call", output_to_operand_aliasing={{0}: (6, {})} | custom-call | tf_op jit(solution)/shard_map/signal/pallas_call | solution.py:417
  20.3 0.7 %collective-permute-start.9 = (bf16[256,512]{1,0:T(8,128)(2,1)S(1)}, bf16[256,512]{1,0:T(8,128)(2,1)S(1)}, u32[]{:S(2)}, u32[]{:S(2)}) collective-permute-start(bf16[256,512]{1,0:T(8,128)(2,1)S(1)} %get-tuple-element.52), channel_id=1, source_target_pairs={{1,2},{3,4},{5,6},{7,8},{9,10},{11,12},{13,14},{15,0},{2,1},{4,3},... | collective-permute-start | bytes 786440 | tf_op jit(solution)/shard_map/ppermute | solution.py:366
  21.0 0.8 %push.1 = (bf16[176,512]{1,0:T(8,128)(2,1)S(1)}, bf16[176,512]{1,0:T(8,128)(2,1)S(1)}, bf16[160,512]{1,0:T(8,128)(2,1)S(1)}) custom-call(s32[2,64]{1,0:T(2,128)S(4)} %get-tuple-element.34.lists, bf16[4,256,512]{2,1,0:T(8,128)(2,1)S(1)} %get-tuple-element.46.signal, bf16[4,2,512,512]{3,2,1,0:T(8,128)(2,1)S(1)} %get-tuple-element.38.tiles), custom_call_target="tpu_custom_call" | custom-call | tf_op jit(solution)/shard_map/push/pallas_call | solution.py:431
  21.9 0.9 %collective-permute-start.6 = (bf16[176,512]{1,0:T(8,128)(2,1)S(1)}, bf16[176,512]{1,0:T(8,128)(2,1)S(1)}, u32[]{:S(2)}, u32[]{:S(2)}) collective-permute-start(bf16[176,512]{1,0:T(8,128)(2,1)S(1)} %get-tuple-element.48), channel_id=1, source_target_pairs={{0,1},{1,0},{2,3},{3,2},{4,5},{5,4},{6,7},{7,6},{8,9},{9,8},{10,11... | collective-permute-start | bytes 540680 | tf_op jit(solution)/shard_map/ppermute | solution.py:272
  23.3 1.0 %query.1.part = f32[256,768]{1,0:T(8,128)S(1)} custom-call(bf16[4,256,512]{2,1,0:T(8,128)(2,1)S(1)} %get-tuple-element.46.signal, bf16[2048,768]{1,0:T(8,128)(2,1)S(1)} %get-tuple-element.36.embeddings), custom_call_target="tpu_custom_call" | custom-call | tf_op jit(solution)/shard_map/query/pallas_call | solution.py:441
  24.7 0.6 %query_on.1 = (f32[256,768]{1,0:T(8,128)S(1)}, bf16[2,256,512]{2,1,0:T(8,128)(2,1)S(1)}) custom-call(s32[2,64]{1,0:T(2,128)S(4)} %get-tuple-element.34.lists, f32[256,768]{1,0:T(8,128)S(1)} %query_half.1.part, bf16[2048,768]{1,0:T(8,128)(2,1)S(1)} %get-tuple-element.36.embeddings, bf16[176,512]{1,0:T(8,128)(2,1)S(1)} %collective-permute-done.6.rest_0_, ...), custom_call_target="tpu_custom_call" | custom-call | tf_op jit(solution)/shard_map/query_on/pallas_call | solution.py:449
  25.4 0.5 embed.4
  25.9 3.1 %collective-permute-done.9.rest_0_.received = bf16[256,512]{1,0:T(8,128)(2,1)S(1)} collective-permute-done((bf16[256,512]{1,0:T(8,128)(2,1)S(1)}, bf16[256,512]{1,0:T(8,128)(2,1)S(1)}, u32[]{:S(2)}, u32[]{:S(2)}) %collective-permute-start.9) | collective-permute-done | bytes 262176 | tf_op jit(solution)/shard_map/ppermute | solution.py:366
  29.3 1.5 %collective-permute-start.10 = (bf16[128,768]{1,0:T(8,128)(2,1)S(1)}, bf16[128,768]{1,0:T(8,128)(2,1)S(1)}, u32[]{:S(2)}, u32[]{:S(2)}) collective-permute-start(bf16[128,768]{1,0:T(8,128)(2,1)S(1)} %query_end.3), channel_id=1, source_target_pairs={{0,1},{1,0},{2,3},{3,2},{4,5},{5,4},{6,7},{7,6},{8,9},{9,8},{10,11... | collective-permute-start | bytes 589832 | tf_op jit(solution)/shard_map/ppermute | solution.py:272
  31.1 0.8 %collective-permute-done.10.got = bf16[128,768]{1,0:T(8,128)(2,1)S(1)} collective-permute-done((bf16[128,768]{1,0:T(8,128)(2,1)S(1)}, bf16[128,768]{1,0:T(8,128)(2,1)S(1)}, u32[]{:S(2)}, u32[]{:S(2)}) %collective-permute-start.10) | collective-permute-done | bytes 196640 | tf_op jit(solution)/shard_map/ppermute | solution.py:272
  31.9 1.2 %collective-permute-start.15 = (bf16[64,768]{1,0:T(8,128)(2,1)S(1)}, bf16[64,768]{1,0:T(8,128)(2,1)S(1)}, u32[]{:S(2)}, u32[]{:S(2)}) collective-permute-start(bf16[64,768]{1,0:T(8,128)(2,1)S(1)} %get-tuple-element.62.held), channel_id=1, source_target_pairs={{0,2},{1,3},{2,0},{3,1},{4,6},{5,7},{6,4},{7,5},{8,10},{9,11},{10,... | collective-permute-start | bytes 294920 | tf_op jit(solution)/shard_map/ppermute | solution.py:272
  33.1 3.0 %collective-permute-start.11 = (bf16[64,768]{1,0:T(8,128)(2,1)S(1)}, bf16[64,768]{1,0:T(8,128)(2,1)S(1)}, u32[]{:S(2)}, u32[]{:S(2)}) collective-permute-start(bf16[64,768]{1,0:T(8,128)(2,1)S(1)} %get-tuple-element.61.held), channel_id=1, source_target_pairs={{0,8},{1,9},{2,10},{3,11},{4,12},{5,13},{6,14},{7,15},{8,0},{9,1},... | collective-permute-start | bytes 294920 | tf_op jit(solution)/shard_map/ppermute | solution.py:272
  36.0 0.9 %embed.5 = (bf16[2048,768]{1,0:T(8,128)(2,1)}, bf16[512,768]{1,0:T(8,128)(2,1)S(1)}, f32[8,128]{1,0:T(8,128)S(1)}) custom-call(s32[2,64]{1,0:T(2,128)S(4)} %get-tuple-element.34.lists, bf16[4,256,512]{2,1,0:T(8,128)(2,1)S(1)} %get-tuple-element.46.signal, bf16[2,256,512]{2,1,0:T(8,128)(2,1)S(1)} %get-tuple-element.51.on, ...), custom_call_target="tpu_custom_call" | custom-call | tf_op jit(solution)/shard_map/embed/pallas_call | solution.py:457
  37.1 2.8 %collective-permute-start.16 = (bf16[64,768]{1,0:T(8,128)(2,1)S(1)}, bf16[64,768]{1,0:T(8,128)(2,1)S(1)}, u32[]{:S(2)}, u32[]{:S(2)}) collective-permute-start(bf16[64,768]{1,0:T(8,128)(2,1)S(1)} %add.9.held), channel_id=1, source_target_pairs={{0,4},{1,5},{2,6},{3,7},{4,0},{5,1},{6,2},{7,3},{8,12},{9,13},{10,... | collective-permute-start | bytes 294920 | tf_op jit(solution)/shard_map/ppermute | solution.py:272
  39.9 1.4 %collective-permute-done.11.got = bf16[64,768]{1,0:T(8,128)(2,1)S(1)} collective-permute-done((bf16[64,768]{1,0:T(8,128)(2,1)S(1)}, bf16[64,768]{1,0:T(8,128)(2,1)S(1)}, u32[]{:S(2)}, u32[]{:S(2)}) %collective-permute-start.11) | collective-permute-done | bytes 98336 | tf_op jit(solution)/shard_map/ppermute | solution.py:272
  41.3 1.7 %collective-permute-start.12 = (bf16[64,768]{1,0:T(8,128)(2,1)S(1)}, bf16[64,768]{1,0:T(8,128)(2,1)S(1)}, u32[]{:S(2)}, u32[]{:S(2)}) collective-permute-start(bf16[64,768]{1,0:T(8,128)(2,1)S(1)} %add.6.held), channel_id=1, source_target_pairs={{0,2},{1,3},{2,0},{3,1},{4,6},{5,7},{6,4},{7,5},{8,10},{9,11},{10,... | collective-permute-start | bytes 294920 | tf_op jit(solution)/shard_map/ppermute | solution.py:272
  43.1 0.9 %embed.6 = (bf16[2048,768]{1,0:T(8,128)(2,1)}, bf16[512,768]{1,0:T(8,128)(2,1)S(1)}, f32[8,128]{1,0:T(8,128)S(1)}) custom-call(s32[2,64]{1,0:T(2,128)S(4)} %get-tuple-element.34.lists, bf16[4,256,512]{2,1,0:T(8,128)(2,1)S(1)} %get-tuple-element.46.signal, bf16[2,256,512]{2,1,0:T(8,128)(2,1)S(1)} %get-tuple-element.51.on, ...), custom_call_target="tpu_custom_call", output_to_operand_aliasing={{0}: (6, {})} | custom-call | tf_op jit(solution)/shard_map/embed/pallas_call | solution.py:457
  44.0 1.5 %collective-permute-start.17 = (bf16[64,768]{1,0:T(8,128)(2,1)S(1)}, bf16[64,768]{1,0:T(8,128)(2,1)S(1)}, u32[]{:S(2)}, u32[]{:S(2)}) collective-permute-start(bf16[64,768]{1,0:T(8,128)(2,1)S(1)} %add.10.held), channel_id=1, source_target_pairs={{0,8},{1,9},{2,10},{3,11},{4,12},{5,13},{6,14},{7,15},{8,0},{9,1},... | collective-permute-start | bytes 294920 | tf_op jit(solution)/shard_map/ppermute | solution.py:272
  46.0 2.2 %collective-permute-start.13 = (bf16[64,768]{1,0:T(8,128)(2,1)S(1)}, bf16[64,768]{1,0:T(8,128)(2,1)S(1)}, u32[]{:S(2)}, u32[]{:S(2)}) collective-permute-start(bf16[64,768]{1,0:T(8,128)(2,1)S(1)} %add.7.held), channel_id=1, source_target_pairs={{0,4},{1,5},{2,6},{3,7},{4,0},{5,1},{6,2},{7,3},{8,12},{9,13},{10,... | collective-permute-start | bytes 294920 | tf_op jit(solution)/shard_map/ppermute | solution.py:272
  48.3 2.3 %embed.7 = (bf16[2048,768]{1,0:T(8,128)(2,1)}, bf16[512,768]{1,0:T(8,128)(2,1)}, f32[8,128]{1,0:T(8,128)S(1)}) custom-call(s32[2,64]{1,0:T(2,128)S(4)} %get-tuple-element.34.lists, bf16[4,256,512]{2,1,0:T(8,128)(2,1)S(1)} %get-tuple-element.46.signal, bf16[2,256,512]{2,1,0:T(8,128)(2,1)S(1)} %get-tuple-element.51.on, ...), custom_call_target="tpu_custom_call", output_to_operand_aliasing={{0}: (7, {})} | custom-call | tf_op jit(solution)/shard_map/embed/pallas_call | solution.py:457
  50.6 0.8 %collective-permute-done.17.got = bf16[64,768]{1,0:T(8,128)(2,1)S(1)} collective-permute-done((bf16[64,768]{1,0:T(8,128)(2,1)S(1)}, bf16[64,768]{1,0:T(8,128)(2,1)S(1)}, u32[]{:S(2)}, u32[]{:S(2)}) %collective-permute-start.17) | collective-permute-done | bytes 98336 | tf_op jit(solution)/shard_map/ppermute | solution.py:272
  52.1 0.7 %collective-permute-done.18.refs_2_ = bf16[64,768]{1,0:T(8,128)(2,1)S(1)} collective-permute-done((bf16[64,768]{1,0:T(8,128)(2,1)S(1)}, bf16[64,768]{1,0:T(8,128)(2,1)S(1)}, u32[]{:S(2)}, u32[]{:S(2)}) %collective-permute-start.18) | collective-permute-done | bytes 98336 | tf_op jit(solution)/shard_map/ppermute | solution.py:272
  52.8 0.8 %place.2.refs_1_ = f32[256,768]{1,0:T(8,128)} custom-call(bf16[64,768]{1,0:T(8,128)(2,1)S(1)} %add.11.refs_0_, bf16[64,768]{1,0:T(8,128)(2,1)S(1)} %add.8.refs_1_, bf16[64,768]{1,0:T(8,128)(2,1)S(1)} %collective-permute-done.18.refs_2_), custom_call_target="tpu_custom_call" | custom-call | tf_op jit(solution)/shard_map/place/pallas_call | solution.py:339
  53.7 0.7 %place.3 = f32[256,768]{1,0:T(8,128)} custom-call(bf16[64,768]{1,0:T(8,128)(2,1)S(1)} %collective-permute-done.14.refs_0_, f32[256,768]{1,0:T(8,128)} %place.2.refs_1_), custom_call_target="tpu_custom_call", output_to_operand_aliasing={{}: (1, {})} | custom-call | tf_op jit(solution)/shard_map/place/pallas_call | solution.py:339
  (35 shorter events, 3.5 us)
Async XLA Ops:
  0.6 9.9 %copy-start.1 = (s32[256,8]{0,1:T(8,128)S(1)}, s32[256,8]{0,1:T(8,128)}, u32[]{:S(2)}) copy-start(s32[256,8]{0,1:T(8,128)} %param.11) | copy-start | bytes 24580
  2.7 11.2 %collective-permute-start.4 = (bf16[256,512]{1,0:T(8,128)(2,1)S(1)}, bf16[256,512]{1,0:T(8,128)(2,1)S(1)}, u32[]{:S(2)}, u32[]{:S(2)}) collective-permute-start(bf16[256,512]{1,0:T(8,128)(2,1)S(1)} %get-tuple-element.44), channel_id=1, source_target_pairs={{1,2},{3,4},{5,6},{7,8},{9,10},{11,12},{13,14},{15,0},{2,1},{4,3},... | collective-permute-start | bytes 786440 | tf_op jit(solution)/shard_map/ppermute | solution.py:366
  9.5 3.6 %collective-permute-start = (bf16[176,512]{1,0:T(8,128)(2,1)S(1)}, bf16[176,512]{1,0:T(8,128)(2,1)S(1)}, u32[]{:S(2)}, u32[]{:S(2)}) collective-permute-start(bf16[176,512]{1,0:T(8,128)(2,1)S(1)} %get-tuple-element.39), channel_id=1, source_target_pairs={{0,1},{1,0},{2,3},{3,2},{4,5},{5,4},{6,7},{7,6},{8,9},{9,8},{10,11... | collective-permute-start | bytes 540680 | tf_op jit(solution)/shard_map/ppermute | solution.py:272
  9.5 3.5 %collective-permute-start.1 = (bf16[176,512]{1,0:T(8,128)(2,1)S(1)}, bf16[176,512]{1,0:T(8,128)(2,1)S(1)}, u32[]{:S(2)}, u32[]{:S(2)}) collective-permute-start(bf16[176,512]{1,0:T(8,128)(2,1)S(1)} %get-tuple-element.40), channel_id=1, source_target_pairs={{0,1},{1,0},{2,3},{3,2},{4,5},{5,4},{6,7},{7,6},{8,9},{9,8},{10,11... | collective-permute-start | bytes 540680 | tf_op jit(solution)/shard_map/ppermute | solution.py:272
  10.0 3.0 %collective-permute-start.2 = (bf16[160,512]{1,0:T(8,128)(2,1)S(1)}, bf16[160,512]{1,0:T(8,128)(2,1)S(1)}, u32[]{:S(2)}, u32[]{:S(2)}) collective-permute-start(bf16[160,512]{1,0:T(8,128)(2,1)S(1)} %get-tuple-element.41), channel_id=1, source_target_pairs={{0,1},{1,0},{2,3},{3,2},{4,5},{5,4},{6,7},{7,6},{8,9},{9,8},{10,11... | collective-permute-start | bytes 491528 | tf_op jit(solution)/shard_map/ppermute | solution.py:272
  10.1 9.0 %collective-permute-start.3 = (bf16[256,512]{1,0:T(8,128)(2,1)S(1)}, bf16[256,512]{1,0:T(8,128)(2,1)S(1)}, u32[]{:S(2)}, u32[]{:S(2)}) collective-permute-start(bf16[256,512]{1,0:T(8,128)(2,1)S(1)} %get-tuple-element.43), channel_id=1, source_target_pairs={{1,2},{3,4},{5,6},{7,8},{9,10},{11,12},{13,14},{15,0},{2,1},{4,3},... | collective-permute-start | bytes 786440 | tf_op jit(solution)/shard_map/ppermute | solution.py:366
  13.0 0.8 %copy-start = (f32[2048]{0:T(1024)S(1)}, f32[2048]{0:T(1024)}, u32[]{:S(2)}) copy-start(f32[2048]{0:T(1024)} %param.9) | copy-start | bytes 24580
  15.1 9.2 %collective-permute-start.5 = (bf16[256,512]{1,0:T(8,128)(2,1)S(1)}, bf16[256,512]{1,0:T(8,128)(2,1)S(1)}, u32[]{:S(2)}, u32[]{:S(2)}) collective-permute-start(bf16[256,512]{1,0:T(8,128)(2,1)S(1)} %get-tuple-element.47), channel_id=1, source_target_pairs={{1,2},{3,4},{5,6},{7,8},{9,10},{11,12},{13,14},{15,0},{2,1},{4,3},... | collective-permute-start | bytes 786440 | tf_op jit(solution)/shard_map/ppermute | solution.py:366
  20.3 8.7 %collective-permute-start.9 = (bf16[256,512]{1,0:T(8,128)(2,1)S(1)}, bf16[256,512]{1,0:T(8,128)(2,1)S(1)}, u32[]{:S(2)}, u32[]{:S(2)}) collective-permute-start(bf16[256,512]{1,0:T(8,128)(2,1)S(1)} %get-tuple-element.52), channel_id=1, source_target_pairs={{1,2},{3,4},{5,6},{7,8},{9,10},{11,12},{13,14},{15,0},{2,1},{4,3},... | collective-permute-start | bytes 786440 | tf_op jit(solution)/shard_map/ppermute | solution.py:366
  21.9 2.9 %collective-permute-start.6 = (bf16[176,512]{1,0:T(8,128)(2,1)S(1)}, bf16[176,512]{1,0:T(8,128)(2,1)S(1)}, u32[]{:S(2)}, u32[]{:S(2)}) collective-permute-start(bf16[176,512]{1,0:T(8,128)(2,1)S(1)} %get-tuple-element.48), channel_id=1, source_target_pairs={{0,1},{1,0},{2,3},{3,2},{4,5},{5,4},{6,7},{7,6},{8,9},{9,8},{10,11... | collective-permute-start | bytes 540680 | tf_op jit(solution)/shard_map/ppermute | solution.py:272
  22.8 1.9 %collective-permute-start.7 = (bf16[176,512]{1,0:T(8,128)(2,1)S(1)}, bf16[176,512]{1,0:T(8,128)(2,1)S(1)}, u32[]{:S(2)}, u32[]{:S(2)}) collective-permute-start(bf16[176,512]{1,0:T(8,128)(2,1)S(1)} %get-tuple-element.49), channel_id=1, source_target_pairs={{0,1},{1,0},{2,3},{3,2},{4,5},{5,4},{6,7},{7,6},{8,9},{9,8},{10,11... | collective-permute-start | bytes 540680 | tf_op jit(solution)/shard_map/ppermute | solution.py:272
  22.9 1.8 %collective-permute-start.8 = (bf16[160,512]{1,0:T(8,128)(2,1)S(1)}, bf16[160,512]{1,0:T(8,128)(2,1)S(1)}, u32[]{:S(2)}, u32[]{:S(2)}) collective-permute-start(bf16[160,512]{1,0:T(8,128)(2,1)S(1)} %get-tuple-element.50), channel_id=1, source_target_pairs={{0,1},{1,0},{2,3},{3,2},{4,5},{5,4},{6,7},{7,6},{8,9},{9,8},{10,11... | collective-permute-start | bytes 491528 | tf_op jit(solution)/shard_map/ppermute | solution.py:272
  29.3 2.6 %collective-permute-start.10 = (bf16[128,768]{1,0:T(8,128)(2,1)S(1)}, bf16[128,768]{1,0:T(8,128)(2,1)S(1)}, u32[]{:S(2)}, u32[]{:S(2)}) collective-permute-start(bf16[128,768]{1,0:T(8,128)(2,1)S(1)} %query_end.3), channel_id=1, source_target_pairs={{0,1},{1,0},{2,3},{3,2},{4,5},{5,4},{6,7},{7,6},{8,9},{9,8},{10,11... | collective-permute-start | bytes 589832 | tf_op jit(solution)/shard_map/ppermute | solution.py:272
  31.9 5.1 %collective-permute-start.15 = (bf16[64,768]{1,0:T(8,128)(2,1)S(1)}, bf16[64,768]{1,0:T(8,128)(2,1)S(1)}, u32[]{:S(2)}, u32[]{:S(2)}) collective-permute-start(bf16[64,768]{1,0:T(8,128)(2,1)S(1)} %get-tuple-element.62.held), channel_id=1, source_target_pairs={{0,2},{1,3},{2,0},{3,1},{4,6},{5,7},{6,4},{7,5},{8,10},{9,11},{10,... | collective-permute-start | bytes 294920 | tf_op jit(solution)/shard_map/ppermute | solution.py:272
  33.1 8.2 %collective-permute-start.11 = (bf16[64,768]{1,0:T(8,128)(2,1)S(1)}, bf16[64,768]{1,0:T(8,128)(2,1)S(1)}, u32[]{:S(2)}, u32[]{:S(2)}) collective-permute-start(bf16[64,768]{1,0:T(8,128)(2,1)S(1)} %get-tuple-element.61.held), channel_id=1, source_target_pairs={{0,8},{1,9},{2,10},{3,11},{4,12},{5,13},{6,14},{7,15},{8,0},{9,1},... | collective-permute-start | bytes 294920 | tf_op jit(solution)/shard_map/ppermute | solution.py:272
  37.1 6.9 %collective-permute-start.16 = (bf16[64,768]{1,0:T(8,128)(2,1)S(1)}, bf16[64,768]{1,0:T(8,128)(2,1)S(1)}, u32[]{:S(2)}, u32[]{:S(2)}) collective-permute-start(bf16[64,768]{1,0:T(8,128)(2,1)S(1)} %add.9.held), channel_id=1, source_target_pairs={{0,4},{1,5},{2,6},{3,7},{4,0},{5,1},{6,2},{7,3},{8,12},{9,13},{10,... | collective-permute-start | bytes 294920 | tf_op jit(solution)/shard_map/ppermute | solution.py:272
  41.3 4.7 %collective-permute-start.12 = (bf16[64,768]{1,0:T(8,128)(2,1)S(1)}, bf16[64,768]{1,0:T(8,128)(2,1)S(1)}, u32[]{:S(2)}, u32[]{:S(2)}) collective-permute-start(bf16[64,768]{1,0:T(8,128)(2,1)S(1)} %add.6.held), channel_id=1, source_target_pairs={{0,2},{1,3},{2,0},{3,1},{4,6},{5,7},{6,4},{7,5},{8,10},{9,11},{10,... | collective-permute-start | bytes 294920 | tf_op jit(solution)/shard_map/ppermute | solution.py:272
  44.0 7.4 %collective-permute-start.17 = (bf16[64,768]{1,0:T(8,128)(2,1)S(1)}, bf16[64,768]{1,0:T(8,128)(2,1)S(1)}, u32[]{:S(2)}, u32[]{:S(2)}) collective-permute-start(bf16[64,768]{1,0:T(8,128)(2,1)S(1)} %add.10.held), channel_id=1, source_target_pairs={{0,8},{1,9},{2,10},{3,11},{4,12},{5,13},{6,14},{7,15},{8,0},{9,1},... | collective-permute-start | bytes 294920 | tf_op jit(solution)/shard_map/ppermute | solution.py:272
  46.0 5.7 %collective-permute-start.13 = (bf16[64,768]{1,0:T(8,128)(2,1)S(1)}, bf16[64,768]{1,0:T(8,128)(2,1)S(1)}, u32[]{:S(2)}, u32[]{:S(2)}) collective-permute-start(bf16[64,768]{1,0:T(8,128)(2,1)S(1)} %add.7.held), channel_id=1, source_target_pairs={{0,4},{1,5},{2,6},{3,7},{4,0},{5,1},{6,2},{7,3},{8,12},{9,13},{10,... | collective-permute-start | bytes 294920 | tf_op jit(solution)/shard_map/ppermute | solution.py:272
  51.5 1.4 %collective-permute-start.18 = (bf16[64,768]{1,0:T(8,128)(2,1)S(1)}, bf16[64,768]{1,0:T(8,128)(2,1)S(1)}, u32[]{:S(2)}, u32[]{:S(2)}) collective-permute-start(bf16[64,768]{1,0:T(8,128)(2,1)S(1)} %add.11.refs_0_), channel_id=1, source_target_pairs={{0,1},{1,0},{2,3},{3,2},{4,5},{5,4},{6,7},{7,6},{8,9},{9,8},{10,11... | collective-permute-start | bytes 294920 | tf_op jit(solution)/shard_map/ppermute | solution.py:272
  51.8 1.9 %collective-permute-start.14 = (bf16[64,768]{1,0:T(8,128)(2,1)S(1)}, bf16[64,768]{1,0:T(8,128)(2,1)S(1)}, u32[]{:S(2)}, u32[]{:S(2)}) collective-permute-start(bf16[64,768]{1,0:T(8,128)(2,1)S(1)} %add.8.refs_1_), channel_id=1, source_target_pairs={{0,1},{1,0},{2,3},{3,2},{4,5},{5,4},{6,7},{7,6},{8,9},{9,8},{10,11... | collective-permute-start | bytes 294920 | tf_op jit(solution)/shard_map/ppermute | solution.py:272

commit v18 on v15

--- a/solution.py
+++ b/solution.py
@@ -62,26 +62,20 @@
     return ref[pl.ds(pl.multiple_of(index * block, block), block), :]
 
 
-def project_kernel(lists, queries, embeddings, out, left, right, table, sem, *, scale):
-    rows, block = out.shape
-    blocks = right.shape[0] // block
-    fetches = [pltpu.make_async_copy(lists, table, sem.at[0]), pltpu.make_async_copy(queries, left, sem.at[1])]
-    for g in range(blocks):
-        place = pl.ds(g * block, block)
-        fetches.append(pltpu.make_async_copy(embeddings.at[place, :], right.at[place, :], sem.at[2 + g]))
-    for fetch in fetches:
-        fetch.start()
-    fetches[0].wait()
-    first, _ = named_by_partner(table, blocks, OFF)
-    fetches[1].wait()
+def project_kernel(lists, queries, embeddings, out, left, table, right, sem, *, scale):
+    block = out.shape[1]
+    fetch_lists = pltpu.make_async_copy(lists, table, sem.at[0])
+    fetch_queries = pltpu.make_async_copy(queries, left, sem.at[1])
+    fetch_lists.start()
+    fetch_queries.start()
+    fetch_lists.wait()
+    first, _ = named_by_partner(table, embeddings.shape[0] // block, OFF)
     place = pl.ds(pl.multiple_of(first * block, block), block)
-    pltpu.make_async_copy(embeddings.at[place, :], right.at[place, :], sem.at[2 + first]).wait()
-    out[...] = (dot(left[...], right[place, :], NT) * scale).astype(BF16)
-    for g in range(blocks):
-
-        @pl.when(g != first)
-        def _():
-            fetches[2 + g].wait()
+    fetch = pltpu.make_async_copy(embeddings.at[place, :], right, sem.at[2])
+    fetch.start()
+    fetch_queries.wait()
+    fetch.wait()
+    out[...] = (dot(left[...], right[...], NT) * scale).astype(BF16)
 
 
 def spans_of(pieces, rows):
@@ -109,10 +103,17 @@
         whole[slot, inside] = piece[place, :]
 
 
-def own_kernel(lists, queries, embeddings, own, off, *on, scale):
+def own_kernel(lists, queries, embeddings, own, off, right, *rest, scale):
+    *on, sem = rest
     blocks, _, block = own.shape
+    fetches = []
     for g in range(blocks):
-        own[g] = dot(queries[...], embeddings[g * block : (g + 1) * block, :], NT) * scale
+        rows = pl.ds(g * block, block)
+        fetches.append(pltpu.make_async_copy(embeddings.at[rows, :], right.at[rows, :], sem.at[g]))
+        fetches[-1].start()
+    for g in range(blocks):
+        fetches[g].wait()
+        own[g] = dot(queries[...], right[g * block : (g + 1) * block, :], NT) * scale
     _, second = named_by_partner(lists, blocks, OFF)
     off[...] = own[second].astype(BF16)
     first, second = named_by_partner(lists, blocks, ON)
@@ -317,7 +318,7 @@
         both = jnp.where(lax.axis_index(AXIS) % 2 == 0, both, both[::-1])
         return both.reshape(2 * rows, width) * scale
     bits = [1 << k for k in range(1, count.bit_length() - 1)]
-    orders = [[bits[0], *bits[2:], bits[1]], [bits[1], bits[0], *bits[2:]]]
+    orders = [bits, bits[-1:] + bits[:-1]]
     piece = in_vmem((rows // 2, width), BF16)
     held = list(call(halve_kernel, "halve", [VMEM] * 2, [piece, piece])(kept, got))
     swapped = []
@@ -349,8 +350,8 @@
             aliases={len(values): 0} if begun else None,
         )(*values, *begun)
 
-    early = place([held[0], held[1], swapped[0]], [(0, True), (1, True), (0, False)])
-    return place([swapped[1]], [(1, False)], early)
+    early = place(held, [(0, True), (1, True)])
+    return place(swapped, [(0, False), (1, False)], early)
 
 
 def per_device(embeddings, edge_tiles, neighbour, propensity, queries, positives):
@@ -375,20 +376,24 @@
     full = (blocks, rows, block)
     scale = 1.0 / math.sqrt(width)
 
-    off_a, queries, embeddings = call(
+    lists, narrow, stored = (pltpu.with_memory_space_constraint(x, pltpu.HBM) for x in (lists, queries, embeddings))
+    off_a, queries, lists = call(
         functools.partial(project_kernel, scale=scale),
         "project",
         [HBM] * 3,
-        [one, in_vmem(queries.shape, BF16), in_vmem(embeddings.shape, BF16)],
-        scratch=[pltpu.SMEM(lists.shape, jnp.int32), pltpu.SemaphoreType.DMA((2 + blocks,))],
-    )(*(pltpu.with_memory_space_constraint(x, pltpu.HBM) for x in (lists, queries, embeddings)))
+        [one, in_vmem(queries.shape, BF16), pltpu.SMEM(lists.shape, jnp.int32)],
+        out_specs=[VMEM] * 2 + [SMEM],
+        scratch=[pltpu.VMEM((block, width), BF16), pltpu.SemaphoreType.DMA((3,))],
+    )(lists, narrow, stored)
     from_off_a = off_swap(off_a)
-    own, off_b, *for_on = call(
+    own, off_b, embeddings, *for_on = call(
         functools.partial(own_kernel, scale=scale),
         "own",
-        [SMEM, VMEM, VMEM],
-        [in_vmem(full, F32), one] + thirds,
-    )(lists, queries, embeddings)
+        [SMEM, VMEM, HBM],
+        [in_vmem(full, F32), one, in_vmem(embeddings.shape, BF16)] + thirds,
+        scratch=[pltpu.SemaphoreType.DMA((blocks,))],
+    )(lists, queries, stored)
+    from_off_b = off_swap(off_b)
     from_on = [on_swap(piece) for piece in for_on]
     hits, tiles = call(
         hits_kernel,
@@ -397,7 +402,6 @@
         [in_vmem(full, BF16), in_vmem(edge_tiles.shape, BF16)],
         scratch=[pltpu.SemaphoreType.DMA],
     )(positives.T, pltpu.with_memory_space_constraint(edge_tiles, pltpu.HBM))
-    from_off_b = off_swap(off_b)
     base = call(
         base_kernel,
         "base",

time: 56.8 us -> 57.5 us (1.012)
  waiting for transfers between devices: 7.33 us -> 15.2 us
  Pallas kernels: 25.9 us -> 20.6 us
  starting transfers between devices: 22.6 us -> 20.5 us
    ppermute x15, waiting for transfers between devices: 5.05 us -> 13.2 us  [exchange(): return lax.ppermute(value, AXIS, [(i, i ^ mask) for i in range(count)])]
    ppermute x15, starting transfers between devices: 11.9 us -> 8.83 us  [exchange(): return lax.ppermute(value, AXIS, [(i, i ^ mask) for i in range(count)])]
    pallas_call x4, Pallas kernels: 6.94 us -> 4.61 us  [embed(): call(functools.partial(embed_kernel, blocks=blocks, turn=turn, scale=1.0...]
    pallas_call x1, Pallas kernels: 1.65 us -> 2.86 us  [per_device(): call(functools.partial(own_kernel, scale=scale), 'own', [SMEM, VMEM, HBM]...]
    pallas_call x2, Pallas kernels: 1.7 us -> 0.55 us  [query_end(): call(functools.partial(query_end_kernel, blocks=blocks, own=own), 'query_...]
    pallas_call x2, Pallas kernels: 3.53 us -> 2.42 us  [signal_of(): call(functools.partial(signal_kernel, slot=slot), 'signal', [SMEM] + [VME...]
    ppermute x4, starting transfers between devices: 10.7 us -> 11.7 us  [off_swap(): return lax.ppermute(value, AXIS, off_route)]
    pallas_call x1, Pallas kernels: 1.35 us -> 0.76 us  [per_device(): call(base_kernel, 'base', [SMEM] + [VMEM] * 5, in_vmem(full, F32), scratc...]
  transfers between devices with their start and end apart: 19 -> 19, of which waited for: 6 -> 8; matrix products, arithmetic and copies ran while one was open for 0% -> 0% of each run, Pallas kernels for 39% -> 30%
where the time goes in v18:
time: 57.5 us; the launch traced here: 57.3 us
  Pallas kernels  20.6 us (36%)
  starting transfers between devices  20.5 us (36%)
  waiting for transfers between devices  15.2 us (26%)
  between operations  0.95 us (2%)
    ppermute x15, waiting for transfers between devices, exchange(): return lax.ppermute(value, AXIS, [(i, i ^ mask) for i in range(count)])  13.2 us
    ppermute x4, starting transfers between devices, off_swap(): return lax.ppermute(value, AXIS, off_route)  11.7 us
    ppermute x15, starting transfers between devices, exchange(): return lax.ppermute(value, AXIS, [(i, i ^ mask) for i in range(count)])  8.83 us
    pallas_call x4, Pallas kernels, embed(): call(functools.partial(embed_kernel, blocks=blocks, turn=turn, scale=1.0...  4.61 us
    pallas_call x1, Pallas kernels, per_device(): call(functools.partial(own_kernel, scale=scale), 'own', [SMEM, VMEM, HBM]...  2.86 us
    pallas_call x1, Pallas kernels, per_device(): call(hits_kernel, 'hits', [VMEM, HBM], [in_vmem(full, BF16), in_vmem(edge...  2.45 us
    pallas_call x1, Pallas kernels, per_device(): call(functools.partial(project_kernel, scale=scale), 'project', [HBM] * 3...  2.43 us
    pallas_call x2, Pallas kernels, signal_of(): call(functools.partial(signal_kernel, slot=slot), 'signal', [SMEM] + [VME...  2.42 us
  transfers between devices with their start and end apart: 19, of which 8 were waited for; matrix products, arithmetic and copies ran while one was open for 0% of the time, Pallas kernels for 30%

profile of v18, /device:TPU:0, one launch (start us, length us, event | category | flops | bytes accessed | tf_op | source)
XLA Modules:
  0.0 57.3 jit_solution(5606376066269815625)
XLA Ops:
  0.6 2.4 %project.1 = (bf16[256,512]{1,0:T(8,128)(2,1)S(1)}, bf16[256,768]{1,0:T(8,128)(2,1)S(1)}, s32[2,64]{1,0:T(2,128)S(4)}) custom-call(s32[2,64]{1,0:T(2,128)} %bitcast.6, bf16[256,768]{1,0:T(8,128)(2,1)} %queries.1, bf16[2048,768]{1,0:T(8,128)(2,1)} %embeddings.3), custom_call_target="tpu_custom_call" | custom-call | tf_op jit(solution)/shard_map/project/pallas_call | solution.py:380
  3.1 5.5 %collective-permute-start.4 = (bf16[256,512]{1,0:T(8,128)(2,1)S(1)}, bf16[256,512]{1,0:T(8,128)(2,1)S(1)}, u32[]{:S(2)}, u32[]{:S(2)}) collective-permute-start(bf16[256,512]{1,0:T(8,128)(2,1)S(1)} %get-tuple-element.43), channel_id=1, source_target_pairs={{1,2},{3,4},{5,6},{7,8},{9,10},{11,12},{13,14},{15,0},{2,1},{4,3},... | collective-permute-start | bytes 786440 | tf_op jit(solution)/shard_map/ppermute | solution.py:367
  8.6 2.9 %own.1 = (f32[4,256,512]{2,1,0:T(8,128)S(1)}, bf16[256,512]{1,0:T(8,128)(2,1)S(1)}, bf16[2048,768]{1,0:T(8,128)(2,1)S(1)}, bf16[176,512]{1,0:T(8,128)(2,1)S(1)},...) custom-call(s32[2,64]{1,0:T(2,128)S(4)} %get-tuple-element.34.lists, ...), custom_call_target="tpu_custom_call" | custom-call | tf_op jit(solution)/shard_map/own/pallas_call | solution.py:389
  11.5 0.5 collective-permute-start.1
  12.1 0.6 %collective-permute-start.3 = (bf16[256,512]{1,0:T(8,128)(2,1)S(1)}, bf16[256,512]{1,0:T(8,128)(2,1)S(1)}, u32[]{:S(2)}, u32[]{:S(2)}) collective-permute-start(bf16[256,512]{1,0:T(8,128)(2,1)S(1)} %get-tuple-element.42), channel_id=1, source_target_pairs={{1,2},{3,4},{5,6},{7,8},{9,10},{11,12},{13,14},{15,0},{2,1},{4,3},... | collective-permute-start | bytes 786440 | tf_op jit(solution)/shard_map/ppermute | solution.py:367
  12.7 2.4 %hits.1 = (bf16[4,256,512]{2,1,0:T(8,128)(2,1)S(1)}, bf16[4,2,512,512]{3,2,1,0:T(8,128)(2,1)S(1)}) custom-call(s32[8,256]{1,0:T(8,128)S(1)} %bitcast.5, bf16[4,2,512,512]{3,2,1,0:T(8,128)(2,1)} %tiles.1), custom_call_target="tpu_custom_call" | custom-call | tf_op jit(solution)/shard_map/hits/pallas_call | solution.py:398
  15.2 0.8 %base.1 = f32[4,256,512]{2,1,0:T(8,128)S(1)} custom-call(s32[2,64]{1,0:T(2,128)S(4)} %get-tuple-element.34.lists, f32[4,256,512]{2,1,0:T(8,128)S(1)} %get-tuple-element.36.own, bf16[4,2,512,512]{3,2,1,0:T(8,128)(2,1)S(1)} %get-tuple-element.37.tiles, bf16[176,512]{1,0:T(8,128)(2,1)S(1)} %collective-permute-done.rest_0_, ...), custom_call_target="tpu_custom_call" | custom-call | tf_op jit(solution)/shard_map/base/pallas_call | solution.py:405
  16.0 1.8 %signal.2 = (bf16[4,256,512]{2,1,0:T(8,128)(2,1)S(1)}, bf16[256,512]{1,0:T(8,128)(2,1)S(1)}) custom-call(s32[2,64]{1,0:T(2,128)S(4)} %get-tuple-element.34.lists, f32[4,256,512]{2,1,0:T(8,128)S(1)} %base.1, bf16[4,256,512]{2,1,0:T(8,128)(2,1)S(1)} %get-tuple-element.41.hits, f32[1,2048]{1,0:T(1,128)S(1)} %bitcast.3, ...), custom_call_target="tpu_custom_call" | custom-call | flops 2000000000 | tf_op jit(solution)/shard_map/signal/pallas_call | solution.py:415
  17.8 2.8 %collective-permute-start.5 = (bf16[256,512]{1,0:T(8,128)(2,1)S(1)}, bf16[256,512]{1,0:T(8,128)(2,1)S(1)}, u32[]{:S(2)}, u32[]{:S(2)}) collective-permute-start(bf16[256,512]{1,0:T(8,128)(2,1)S(1)} %get-tuple-element.47), channel_id=1, source_target_pairs={{1,2},{3,4},{5,6},{7,8},{9,10},{11,12},{13,14},{15,0},{2,1},{4,3},... | collective-permute-start | bytes 786440 | tf_op jit(solution)/shard_map/ppermute | solution.py:367
  20.7 0.6 %signal.3 = (bf16[4,256,512]{2,1,0:T(8,128)(2,1)S(1)}, bf16[256,512]{1,0:T(8,128)(2,1)S(1)}) custom-call(s32[2,64]{1,0:T(2,128)S(4)} %get-tuple-element.34.lists, f32[4,256,512]{2,1,0:T(8,128)S(1)} %base.1, bf16[4,256,512]{2,1,0:T(8,128)(2,1)S(1)} %get-tuple-element.41.hits, f32[1,2048]{1,0:T(1,128)S(1)} %bitcast.4, ...), custom_call_target="tpu_custom_call", output_to_operand_aliasing={{0}: (6, {})} | custom-call | tf_op jit(solution)/shard_map/signal/pallas_call | solution.py:415
  21.4 2.8 %collective-permute-start.9 = (bf16[256,512]{1,0:T(8,128)(2,1)S(1)}, bf16[256,512]{1,0:T(8,128)(2,1)S(1)}, u32[]{:S(2)}, u32[]{:S(2)}) collective-permute-start(bf16[256,512]{1,0:T(8,128)(2,1)S(1)} %get-tuple-element.52), channel_id=1, source_target_pairs={{1,2},{3,4},{5,6},{7,8},{9,10},{11,12},{13,14},{15,0},{2,1},{4,3},... | collective-permute-start | bytes 786440 | tf_op jit(solution)/shard_map/ppermute | solution.py:367
  24.2 0.8 %push.1 = (bf16[176,512]{1,0:T(8,128)(2,1)S(1)}, bf16[176,512]{1,0:T(8,128)(2,1)S(1)}, bf16[160,512]{1,0:T(8,128)(2,1)S(1)}) custom-call(s32[2,64]{1,0:T(2,128)S(4)} %get-tuple-element.34.lists, bf16[4,256,512]{2,1,0:T(8,128)(2,1)S(1)} %get-tuple-element.45.signal, bf16[4,2,512,512]{3,2,1,0:T(8,128)(2,1)S(1)} %get-tuple-element.37.tiles), custom_call_target="tpu_custom_call" | custom-call | tf_op jit(solution)/shard_map/push/pallas_call | solution.py:429
  25.1 0.5 collective-permute-start.7
  25.6 1.0 %query.1.part = f32[256,768]{1,0:T(8,128)S(1)} custom-call(bf16[4,256,512]{2,1,0:T(8,128)(2,1)S(1)} %get-tuple-element.45.signal, bf16[2048,768]{1,0:T(8,128)(2,1)S(1)} %get-tuple-element.46.embeddings), custom_call_target="tpu_custom_call" | custom-call | tf_op jit(solution)/shard_map/query/pallas_call | solution.py:439
  27.1 0.6 %query_on.1 = (f32[256,768]{1,0:T(8,128)S(1)}, bf16[2,256,512]{2,1,0:T(8,128)(2,1)S(1)}) custom-call(s32[2,64]{1,0:T(2,128)S(4)} %get-tuple-element.34.lists, f32[256,768]{1,0:T(8,128)S(1)} %query_half.1.part, bf16[2048,768]{1,0:T(8,128)(2,1)S(1)} %get-tuple-element.46.embeddings, bf16[176,512]{1,0:T(8,128)(2,1)S(1)} %collective-permute-done.6.rest_0_, ...), custom_call_target="tpu_custom_call" | custom-call | tf_op jit(solution)/shard_map/query_on/pallas_call | solution.py:447
  27.7 0.5 embed.4
  28.2 1.8 %collective-permute-done.9.rest_0_.received = bf16[256,512]{1,0:T(8,128)(2,1)S(1)} collective-permute-done((bf16[256,512]{1,0:T(8,128)(2,1)S(1)}, bf16[256,512]{1,0:T(8,128)(2,1)S(1)}, u32[]{:S(2)}, u32[]{:S(2)}) %collective-permute-start.9) | collective-permute-done | bytes 262176 | tf_op jit(solution)/shard_map/ppermute | solution.py:367
  30.3 2.4 %collective-permute-start.10 = (bf16[128,768]{1,0:T(8,128)(2,1)S(1)}, bf16[128,768]{1,0:T(8,128)(2,1)S(1)}, u32[]{:S(2)}, u32[]{:S(2)}) collective-permute-start(bf16[128,768]{1,0:T(8,128)(2,1)S(1)} %query_end.3), channel_id=1, source_target_pairs={{0,1},{1,0},{2,3},{3,2},{4,5},{5,4},{6,7},{7,6},{8,9},{9,8},{10,11... | collective-permute-start | bytes 589832 | tf_op jit(solution)/shard_map/ppermute | solution.py:273
  33.0 0.8 %collective-permute-done.10.got = bf16[128,768]{1,0:T(8,128)(2,1)S(1)} collective-permute-done((bf16[128,768]{1,0:T(8,128)(2,1)S(1)}, bf16[128,768]{1,0:T(8,128)(2,1)S(1)}, u32[]{:S(2)}, u32[]{:S(2)}) %collective-permute-start.10) | collective-permute-done | bytes 196640 | tf_op jit(solution)/shard_map/ppermute | solution.py:273
  33.8 1.0 %collective-permute-start.15 = (bf16[64,768]{1,0:T(8,128)(2,1)S(1)}, bf16[64,768]{1,0:T(8,128)(2,1)S(1)}, u32[]{:S(2)}, u32[]{:S(2)}) collective-permute-start(bf16[64,768]{1,0:T(8,128)(2,1)S(1)} %get-tuple-element.65.held), channel_id=1, source_target_pairs={{0,8},{1,9},{2,10},{3,11},{4,12},{5,13},{6,14},{7,15},{8,0},{9,1},... | collective-permute-start | bytes 294920 | tf_op jit(solution)/shard_map/ppermute | solution.py:273
  34.8 1.3 %collective-permute-start.11 = (bf16[64,768]{1,0:T(8,128)(2,1)S(1)}, bf16[64,768]{1,0:T(8,128)(2,1)S(1)}, u32[]{:S(2)}, u32[]{:S(2)}) collective-permute-start(bf16[64,768]{1,0:T(8,128)(2,1)S(1)} %get-tuple-element.61.held), channel_id=1, source_target_pairs={{0,2},{1,3},{2,0},{3,1},{4,6},{5,7},{6,4},{7,5},{8,10},{9,11},{10,... | collective-permute-start | bytes 294920 | tf_op jit(solution)/shard_map/ppermute | solution.py:273
  36.1 4.8 %collective-permute-done.15.got = bf16[64,768]{1,0:T(8,128)(2,1)S(1)} collective-permute-done((bf16[64,768]{1,0:T(8,128)(2,1)S(1)}, bf16[64,768]{1,0:T(8,128)(2,1)S(1)}, u32[]{:S(2)}, u32[]{:S(2)}) %collective-permute-start.15) | collective-permute-done | bytes 98336 | tf_op jit(solution)/shard_map/ppermute | solution.py:273
  40.9 1.9 %collective-permute-start.16 = (bf16[64,768]{1,0:T(8,128)(2,1)S(1)}, bf16[64,768]{1,0:T(8,128)(2,1)S(1)}, u32[]{:S(2)}, u32[]{:S(2)}) collective-permute-start(bf16[64,768]{1,0:T(8,128)(2,1)S(1)} %add.9.held), channel_id=1, source_target_pairs={{0,2},{1,3},{2,0},{3,1},{4,6},{5,7},{6,4},{7,5},{8,10},{9,11},{10,... | collective-permute-start | bytes 294920 | tf_op jit(solution)/shard_map/ppermute | solution.py:273
  42.8 0.9 %embed.5 = (bf16[2048,768]{1,0:T(8,128)(2,1)}, bf16[512,768]{1,0:T(8,128)(2,1)S(1)}, f32[8,128]{1,0:T(8,128)S(1)}) custom-call(s32[2,64]{1,0:T(2,128)S(4)} %get-tuple-element.34.lists, bf16[4,256,512]{2,1,0:T(8,128)(2,1)S(1)} %get-tuple-element.45.signal, bf16[2,256,512]{2,1,0:T(8,128)(2,1)S(1)} %get-tuple-element.51.on, ...), custom_call_target="tpu_custom_call" | custom-call | tf_op jit(solution)/shard_map/embed/pallas_call | solution.py:455
  43.8 1.9 %collective-permute-done.16.got = bf16[64,768]{1,0:T(8,128)(2,1)S(1)} collective-permute-done((bf16[64,768]{1,0:T(8,128)(2,1)S(1)}, bf16[64,768]{1,0:T(8,128)(2,1)S(1)}, u32[]{:S(2)}, u32[]{:S(2)}) %collective-permute-start.16) | collective-permute-done | bytes 98336 | tf_op jit(solution)/shard_map/ppermute | solution.py:273
  45.9 0.9 %embed.6 = (bf16[2048,768]{1,0:T(8,128)(2,1)}, bf16[512,768]{1,0:T(8,128)(2,1)S(1)}, f32[8,128]{1,0:T(8,128)S(1)}) custom-call(s32[2,64]{1,0:T(2,128)S(4)} %get-tuple-element.34.lists, bf16[4,256,512]{2,1,0:T(8,128)(2,1)S(1)} %get-tuple-element.45.signal, bf16[2,256,512]{2,1,0:T(8,128)(2,1)S(1)} %get-tuple-element.51.on, ...), custom_call_target="tpu_custom_call", output_to_operand_aliasing={{0}: (6, {})} | custom-call | tf_op jit(solution)/shard_map/embed/pallas_call | solution.py:455
  46.8 2.4 %collective-permute-done.12.got = bf16[64,768]{1,0:T(8,128)(2,1)S(1)} collective-permute-done((bf16[64,768]{1,0:T(8,128)(2,1)S(1)}, bf16[64,768]{1,0:T(8,128)(2,1)S(1)}, u32[]{:S(2)}, u32[]{:S(2)}) %collective-permute-start.12) | collective-permute-done | bytes 98336 | tf_op jit(solution)/shard_map/ppermute | solution.py:273
  49.3 0.6 %collective-permute-start.13 = (bf16[64,768]{1,0:T(8,128)(2,1)S(1)}, bf16[64,768]{1,0:T(8,128)(2,1)S(1)}, u32[]{:S(2)}, u32[]{:S(2)}) collective-permute-start(bf16[64,768]{1,0:T(8,128)(2,1)S(1)} %add.7.held), channel_id=1, source_target_pairs={{0,8},{1,9},{2,10},{3,11},{4,12},{5,13},{6,14},{7,15},{8,0},{9,1},... | collective-permute-start | bytes 294920 | tf_op jit(solution)/shard_map/ppermute | solution.py:273
  49.9 2.3 %embed.7 = (bf16[2048,768]{1,0:T(8,128)(2,1)}, bf16[512,768]{1,0:T(8,128)(2,1)}, f32[8,128]{1,0:T(8,128)S(1)}) custom-call(s32[2,64]{1,0:T(2,128)S(4)} %get-tuple-element.34.lists, bf16[4,256,512]{2,1,0:T(8,128)(2,1)S(1)} %get-tuple-element.45.signal, bf16[2,256,512]{2,1,0:T(8,128)(2,1)S(1)} %get-tuple-element.51.on, ...), custom_call_target="tpu_custom_call", output_to_operand_aliasing={{0}: (7, {})} | custom-call | tf_op jit(solution)/shard_map/embed/pallas_call | solution.py:455
  52.3 2.8 %collective-permute-done.13.got = bf16[64,768]{1,0:T(8,128)(2,1)S(1)} collective-permute-done((bf16[64,768]{1,0:T(8,128)(2,1)S(1)}, bf16[64,768]{1,0:T(8,128)(2,1)S(1)}, u32[]{:S(2)}, u32[]{:S(2)}) %collective-permute-start.13) | collective-permute-done | bytes 98336 | tf_op jit(solution)/shard_map/ppermute | solution.py:273
  55.3 0.8 %place.2.refs_2_ = f32[256,768]{1,0:T(8,128)} custom-call(bf16[64,768]{1,0:T(8,128)(2,1)S(1)} %add.8.refs_0_, bf16[64,768]{1,0:T(8,128)(2,1)S(1)} %add.11.refs_1_), custom_call_target="tpu_custom_call" | custom-call | tf_op jit(solution)/shard_map/place/pallas_call | solution.py:340
  56.5 0.8 %place.3 = f32[256,768]{1,0:T(8,128)} custom-call(bf16[64,768]{1,0:T(8,128)(2,1)S(1)} %collective-permute-done.14.refs_0_, bf16[64,768]{1,0:T(8,128)(2,1)S(1)} %collective-permute-done.18.refs_1_, f32[256,768]{1,0:T(8,128)} %place.2.refs_2_), custom_call_target="tpu_custom_call", output_to_operand_aliasing={{}: (2, {})} | custom-call | tf_op jit(solution)/shard_map/place/pallas_call | solution.py:340
  (35 shorter events, 2.5 us)
Async XLA Ops:
  0.6 12.1 %copy-start.1 = (s32[256,8]{0,1:T(8,128)S(1)}, s32[256,8]{0,1:T(8,128)}, u32[]{:S(2)}) copy-start(s32[256,8]{0,1:T(8,128)} %param.11) | copy-start | bytes 24580
  3.1 12.9 %collective-permute-start.4 = (bf16[256,512]{1,0:T(8,128)(2,1)S(1)}, bf16[256,512]{1,0:T(8,128)(2,1)S(1)}, u32[]{:S(2)}, u32[]{:S(2)}) collective-permute-start(bf16[256,512]{1,0:T(8,128)(2,1)S(1)} %get-tuple-element.43), channel_id=1, source_target_pairs={{1,2},{3,4},{5,6},{7,8},{9,10},{11,12},{13,14},{15,0},{2,1},{4,3},... | collective-permute-start | bytes 786440 | tf_op jit(solution)/shard_map/ppermute | solution.py:367
  11.5 3.7 %collective-permute-start = (bf16[176,512]{1,0:T(8,128)(2,1)S(1)}, bf16[176,512]{1,0:T(8,128)(2,1)S(1)}, u32[]{:S(2)}, u32[]{:S(2)}) collective-permute-start(bf16[176,512]{1,0:T(8,128)(2,1)S(1)} %get-tuple-element.38), channel_id=1, source_target_pairs={{0,1},{1,0},{2,3},{3,2},{4,5},{5,4},{6,7},{7,6},{8,9},{9,8},{10,11... | collective-permute-start | bytes 540680 | tf_op jit(solution)/shard_map/ppermute | solution.py:273
  11.5 3.7 %collective-permute-start.1 = (bf16[176,512]{1,0:T(8,128)(2,1)S(1)}, bf16[176,512]{1,0:T(8,128)(2,1)S(1)}, u32[]{:S(2)}, u32[]{:S(2)}) collective-permute-start(bf16[176,512]{1,0:T(8,128)(2,1)S(1)} %get-tuple-element.39), channel_id=1, source_target_pairs={{0,1},{1,0},{2,3},{3,2},{4,5},{5,4},{6,7},{7,6},{8,9},{9,8},{10,11... | collective-permute-start | bytes 540680 | tf_op jit(solution)/shard_map/ppermute | solution.py:273
  12.0 3.2 %collective-permute-start.2 = (bf16[160,512]{1,0:T(8,128)(2,1)S(1)}, bf16[160,512]{1,0:T(8,128)(2,1)S(1)}, u32[]{:S(2)}, u32[]{:S(2)}) collective-permute-start(bf16[160,512]{1,0:T(8,128)(2,1)S(1)} %get-tuple-element.40), channel_id=1, source_target_pairs={{0,1},{1,0},{2,3},{3,2},{4,5},{5,4},{6,7},{7,6},{8,9},{9,8},{10,11... | collective-permute-start | bytes 491528 | tf_op jit(solution)/shard_map/ppermute | solution.py:273
  12.1 8.6 %collective-permute-start.3 = (bf16[256,512]{1,0:T(8,128)(2,1)S(1)}, bf16[256,512]{1,0:T(8,128)(2,1)S(1)}, u32[]{:S(2)}, u32[]{:S(2)}) collective-permute-start(bf16[256,512]{1,0:T(8,128)(2,1)S(1)} %get-tuple-element.42), channel_id=1, source_target_pairs={{1,2},{3,4},{5,6},{7,8},{9,10},{11,12},{13,14},{15,0},{2,1},{4,3},... | collective-permute-start | bytes 786440 | tf_op jit(solution)/shard_map/ppermute | solution.py:367
  15.2 0.8 %copy-start = (f32[2048]{0:T(1024)S(1)}, f32[2048]{0:T(1024)}, u32[]{:S(2)}) copy-start(f32[2048]{0:T(1024)} %param.9) | copy-start | bytes 24580
  17.8 8.8 %collective-permute-start.5 = (bf16[256,512]{1,0:T(8,128)(2,1)S(1)}, bf16[256,512]{1,0:T(8,128)(2,1)S(1)}, u32[]{:S(2)}, u32[]{:S(2)}) collective-permute-start(bf16[256,512]{1,0:T(8,128)(2,1)S(1)} %get-tuple-element.47), channel_id=1, source_target_pairs={{1,2},{3,4},{5,6},{7,8},{9,10},{11,12},{13,14},{15,0},{2,1},{4,3},... | collective-permute-start | bytes 786440 | tf_op jit(solution)/shard_map/ppermute | solution.py:367
  21.4 8.7 %collective-permute-start.9 = (bf16[256,512]{1,0:T(8,128)(2,1)S(1)}, bf16[256,512]{1,0:T(8,128)(2,1)S(1)}, u32[]{:S(2)}, u32[]{:S(2)}) collective-permute-start(bf16[256,512]{1,0:T(8,128)(2,1)S(1)} %get-tuple-element.52), channel_id=1, source_target_pairs={{1,2},{3,4},{5,6},{7,8},{9,10},{11,12},{13,14},{15,0},{2,1},{4,3},... | collective-permute-start | bytes 786440 | tf_op jit(solution)/shard_map/ppermute | solution.py:367
  25.0 2.1 %collective-permute-start.6 = (bf16[176,512]{1,0:T(8,128)(2,1)S(1)}, bf16[176,512]{1,0:T(8,128)(2,1)S(1)}, u32[]{:S(2)}, u32[]{:S(2)}) collective-permute-start(bf16[176,512]{1,0:T(8,128)(2,1)S(1)} %get-tuple-element.48), channel_id=1, source_target_pairs={{0,1},{1,0},{2,3},{3,2},{4,5},{5,4},{6,7},{7,6},{8,9},{9,8},{10,11... | collective-permute-start | bytes 540680 | tf_op jit(solution)/shard_map/ppermute | solution.py:273
  25.1 2.0 %collective-permute-start.7 = (bf16[176,512]{1,0:T(8,128)(2,1)S(1)}, bf16[176,512]{1,0:T(8,128)(2,1)S(1)}, u32[]{:S(2)}, u32[]{:S(2)}) collective-permute-start(bf16[176,512]{1,0:T(8,128)(2,1)S(1)} %get-tuple-element.49), channel_id=1, source_target_pairs={{0,1},{1,0},{2,3},{3,2},{4,5},{5,4},{6,7},{7,6},{8,9},{9,8},{10,11... | collective-permute-start | bytes 540680 | tf_op jit(solution)/shard_map/ppermute | solution.py:273
  25.6 1.5 %collective-permute-start.8 = (bf16[160,512]{1,0:T(8,128)(2,1)S(1)}, bf16[160,512]{1,0:T(8,128)(2,1)S(1)}, u32[]{:S(2)}, u32[]{:S(2)}) collective-permute-start(bf16[160,512]{1,0:T(8,128)(2,1)S(1)} %get-tuple-element.50), channel_id=1, source_target_pairs={{0,1},{1,0},{2,3},{3,2},{4,5},{5,4},{6,7},{7,6},{8,9},{9,8},{10,11... | collective-permute-start | bytes 491528 | tf_op jit(solution)/shard_map/ppermute | solution.py:273
  30.3 3.5 %collective-permute-start.10 = (bf16[128,768]{1,0:T(8,128)(2,1)S(1)}, bf16[128,768]{1,0:T(8,128)(2,1)S(1)}, u32[]{:S(2)}, u32[]{:S(2)}) collective-permute-start(bf16[128,768]{1,0:T(8,128)(2,1)S(1)} %query_end.3), channel_id=1, source_target_pairs={{0,1},{1,0},{2,3},{3,2},{4,5},{5,4},{6,7},{7,6},{8,9},{9,8},{10,11... | collective-permute-start | bytes 589832 | tf_op jit(solution)/shard_map/ppermute | solution.py:273
  33.8 7.0 %collective-permute-start.15 = (bf16[64,768]{1,0:T(8,128)(2,1)S(1)}, bf16[64,768]{1,0:T(8,128)(2,1)S(1)}, u32[]{:S(2)}, u32[]{:S(2)}) collective-permute-start(bf16[64,768]{1,0:T(8,128)(2,1)S(1)} %get-tuple-element.65.held), channel_id=1, source_target_pairs={{0,8},{1,9},{2,10},{3,11},{4,12},{5,13},{6,14},{7,15},{8,0},{9,1},... | collective-permute-start | bytes 294920 | tf_op jit(solution)/shard_map/ppermute | solution.py:273
  34.8 8.9 %collective-permute-start.11 = (bf16[64,768]{1,0:T(8,128)(2,1)S(1)}, bf16[64,768]{1,0:T(8,128)(2,1)S(1)}, u32[]{:S(2)}, u32[]{:S(2)}) collective-permute-start(bf16[64,768]{1,0:T(8,128)(2,1)S(1)} %get-tuple-element.61.held), channel_id=1, source_target_pairs={{0,2},{1,3},{2,0},{3,1},{4,6},{5,7},{6,4},{7,5},{8,10},{9,11},{10,... | collective-permute-start | bytes 294920 | tf_op jit(solution)/shard_map/ppermute | solution.py:273
  40.9 4.8 %collective-permute-start.16 = (bf16[64,768]{1,0:T(8,128)(2,1)S(1)}, bf16[64,768]{1,0:T(8,128)(2,1)S(1)}, u32[]{:S(2)}, u32[]{:S(2)}) collective-permute-start(bf16[64,768]{1,0:T(8,128)(2,1)S(1)} %add.9.held), channel_id=1, source_target_pairs={{0,2},{1,3},{2,0},{3,1},{4,6},{5,7},{6,4},{7,5},{8,10},{9,11},{10,... | collective-permute-start | bytes 294920 | tf_op jit(solution)/shard_map/ppermute | solution.py:273
  43.7 5.5 %collective-permute-start.12 = (bf16[64,768]{1,0:T(8,128)(2,1)S(1)}, bf16[64,768]{1,0:T(8,128)(2,1)S(1)}, u32[]{:S(2)}, u32[]{:S(2)}) collective-permute-start(bf16[64,768]{1,0:T(8,128)(2,1)S(1)} %add.6.held), channel_id=1, source_target_pairs={{0,4},{1,5},{2,6},{3,7},{4,0},{5,1},{6,2},{7,3},{8,12},{9,13},{10,... | collective-permute-start | bytes 294920 | tf_op jit(solution)/shard_map/ppermute | solution.py:273
  45.8 6.4 %collective-permute-start.17 = (bf16[64,768]{1,0:T(8,128)(2,1)S(1)}, bf16[64,768]{1,0:T(8,128)(2,1)S(1)}, u32[]{:S(2)}, u32[]{:S(2)}) collective-permute-start(bf16[64,768]{1,0:T(8,128)(2,1)S(1)} %add.10.held), channel_id=1, source_target_pairs={{0,4},{1,5},{2,6},{3,7},{4,0},{5,1},{6,2},{7,3},{8,12},{9,13},{10,... | collective-permute-start | bytes 294920 | tf_op jit(solution)/shard_map/ppermute | solution.py:273
  49.3 5.9 %collective-permute-start.13 = (bf16[64,768]{1,0:T(8,128)(2,1)S(1)}, bf16[64,768]{1,0:T(8,128)(2,1)S(1)}, u32[]{:S(2)}, u32[]{:S(2)}) collective-permute-start(bf16[64,768]{1,0:T(8,128)(2,1)S(1)} %add.7.held), channel_id=1, source_target_pairs={{0,8},{1,9},{2,10},{3,11},{4,12},{5,13},{6,14},{7,15},{8,0},{9,1},... | collective-permute-start | bytes 294920 | tf_op jit(solution)/shard_map/ppermute | solution.py:273
  52.3 3.8 %collective-permute-start.18 = (bf16[64,768]{1,0:T(8,128)(2,1)S(1)}, bf16[64,768]{1,0:T(8,128)(2,1)S(1)}, u32[]{:S(2)}, u32[]{:S(2)}) collective-permute-start(bf16[64,768]{1,0:T(8,128)(2,1)S(1)} %add.11.refs_1_), channel_id=1, source_target_pairs={{0,1},{1,0},{2,3},{3,2},{4,5},{5,4},{6,7},{7,6},{8,9},{9,8},{10,11... | collective-permute-start | bytes 294920 | tf_op jit(solution)/shard_map/ppermute | solution.py:273
  55.2 1.4 %collective-permute-start.14 = (bf16[64,768]{1,0:T(8,128)(2,1)S(1)}, bf16[64,768]{1,0:T(8,128)(2,1)S(1)}, u32[]{:S(2)}, u32[]{:S(2)}) collective-permute-start(bf16[64,768]{1,0:T(8,128)(2,1)S(1)} %add.8.refs_0_), channel_id=1, source_target_pairs={{0,1},{1,0},{2,3},{3,2},{4,5},{5,4},{6,7},{7,6},{8,9},{9,8},{10,11... | collective-permute-start | bytes 294920 | tf_op jit(solution)/shard_map/ppermute | solution.py:273

commit v19 on v17

--- a/solution.py
+++ b/solution.py
@@ -62,26 +62,39 @@
     return ref[pl.ds(pl.multiple_of(index * block, block), block), :]
 
 
-def project_kernel(lists, queries, embeddings, out, left, right, table, sem, *, scale):
+def project_kernel(lists, queries, embeddings, out, left, right, table, sem, list_sem, *, scale):
     rows, block = out.shape
     blocks = right.shape[0] // block
-    fetches = [pltpu.make_async_copy(lists, table, sem.at[0]), pltpu.make_async_copy(queries, left, sem.at[1])]
-    for g in range(blocks):
-        place = pl.ds(g * block, block)
-        fetches.append(pltpu.make_async_copy(embeddings.at[place, :], right.at[place, :], sem.at[2 + g]))
-    for fetch in fetches:
-        fetch.start()
-    fetches[0].wait()
+    parts = sem.shape[0] // (blocks + 1)
+
+    def fetches_of(source, target, begin, size, slot):
+        copies = []
+        for part in range(parts):
+            place = pl.ds(pl.multiple_of(begin + part * size // parts, size // parts), size // parts)
+            copies.append(pltpu.make_async_copy(source.at[place, :], target.at[place, :], sem.at[slot * parts + part]))
+        return copies
+
+    def wait_all(copies):
+        for copy in copies:
+            copy.wait()
+
+    fetch_lists = pltpu.make_async_copy(lists, table, list_sem)
+    fetch_lists.start()
+    fetch_queries = fetches_of(queries, left, 0, rows, blocks)
+    fetch_blocks = [fetches_of(embeddings, right, g * block, block, g) for g in range(blocks)]
+    for copies in [fetch_queries, *fetch_blocks]:
+        for copy in copies:
+            copy.start()
+    fetch_lists.wait()
     first, _ = named_by_partner(table, blocks, OFF)
-    fetches[1].wait()
-    place = pl.ds(pl.multiple_of(first * block, block), block)
-    pltpu.make_async_copy(embeddings.at[place, :], right.at[place, :], sem.at[2 + first]).wait()
-    out[...] = (dot(left[...], right[place, :], NT) * scale).astype(BF16)
+    wait_all(fetch_queries)
+    wait_all(fetches_of(embeddings, right, first * block, block, first))
+    out[...] = (dot(left[...], block_rows(right, first, block), NT) * scale).astype(BF16)
     for g in range(blocks):
 
         @pl.when(g != first)
         def _():
-            fetches[2 + g].wait()
+            wait_all(fetch_blocks[g])
 
 
 def spans_of(pieces, rows):
@@ -386,7 +399,7 @@
             pltpu.SMEM(lists.shape, jnp.int32),
         ],
         out_specs=[VMEM] * 3 + [SMEM],
-        scratch=[pltpu.SemaphoreType.DMA((2 + blocks,))],
+        scratch=[pltpu.SemaphoreType.DMA((4 * (blocks + 1),)), pltpu.SemaphoreType.DMA],
     )(*(pltpu.with_memory_space_constraint(x, pltpu.HBM) for x in (lists, queries, embeddings)))
     from_off_a = off_swap(off_a)
     own, off_b, *for_on = call(

time: 55.2 us -> 54.7 us (level); the launches traced: 54.4 us -> 54.5 us
  starting transfers between devices: 27.4 us -> 23.8 us
  waiting for transfers between devices: 7.66 us -> 11 us
    ppermute x15, waiting for transfers between devices: 4.51 us -> 10.8 us  [exchange(): return lax.ppermute(value, AXIS, [(i, i ^ mask) for i in range(count)])]
    ppermute x15, starting transfers between devices: 16.5 us -> 12.5 us  [exchange(): return lax.ppermute(value, AXIS, [(i, i ^ mask) for i in range(count)])]
    ppermute x4, waiting for transfers between devices: 3.15 us -> 0.18 us  [off_swap(): return lax.ppermute(value, AXIS, off_route)]
  transfers between devices with their start and end apart: 19 -> 19, of which waited for: 8 -> 9; matrix products, arithmetic and copies ran while one was open for 0% -> 0% of each run, Pallas kernels for 28% -> 29%
where the time goes in v19:
time: 54.7 us; the launch traced here: 54.5 us
  starting transfers between devices  23.8 us (44%)
  Pallas kernels  18.8 us (34%)
  waiting for transfers between devices  11 us (20%)
  between operations  0.94 us (2%)
    ppermute x15, starting transfers between devices, exchange(): return lax.ppermute(value, AXIS, [(i, i ^ mask) for i in range(count)])  12.5 us
    ppermute x4, starting transfers between devices, off_swap(): return lax.ppermute(value, AXIS, off_route)  11.3 us
    ppermute x15, waiting for transfers between devices, exchange(): return lax.ppermute(value, AXIS, [(i, i ^ mask) for i in range(count)])  10.8 us
    pallas_call x4, Pallas kernels, embed(): call(functools.partial(embed_kernel, blocks=blocks, turn=turn, scale=1.0...  4.7 us
    pallas_call x1, Pallas kernels, per_device(): call(hits_kernel, 'hits', [VMEM, HBM], [in_vmem(full, BF16), in_vmem(edge...  2.45 us
    pallas_call x2, Pallas kernels, signal_of(): call(functools.partial(signal_kernel, slot=slot), 'signal', [SMEM] + [VME...  2.41 us
    pallas_call x1, Pallas kernels, per_device(): call(functools.partial(project_kernel, scale=scale), 'project', [HBM] * 3...  2.24 us
    pallas_call x2, Pallas kernels, place(): call(functools.partial(place_kernel, places=places), 'place', [VMEM] * le...  1.54 us
  transfers between devices with their start and end apart: 19, of which 9 were waited for; matrix products, arithmetic and copies ran while one was open for 0% of the time, Pallas kernels for 29%

profile of v19, /device:TPU:0, one launch (start us, length us, event | category | flops | bytes accessed | tf_op | source)
XLA Modules:
  0.0 54.5 jit_solution(3279469048366762221)
XLA Ops:
  0.6 2.2 %project.1 = (bf16[256,512]{1,0:T(8,128)(2,1)S(1)}, bf16[256,768]{1,0:T(8,128)(2,1)S(1)}, bf16[2048,768]{1,0:T(8,128)(2,1)S(1)}, s32[2,64]{1,0:T(2,128)S(4)}) custom-call(s32[2,64]{1,0:T(2,128)} %bitcast.6, bf16[256,768]{1,0:T(8,128)(2,1)} %queries.1, bf16[2048,768]{1,0:T(8,128)(2,1)} %embeddings.1), custom_call_target="tpu_custom_call" | custom-call | tf_op jit(solution)/shard_map/project/pallas_call | solution.py:391
  2.9 5.5 %collective-permute-start.4 = (bf16[256,512]{1,0:T(8,128)(2,1)S(1)}, bf16[256,512]{1,0:T(8,128)(2,1)S(1)}, u32[]{:S(2)}, u32[]{:S(2)}) collective-permute-start(bf16[256,512]{1,0:T(8,128)(2,1)S(1)} %get-tuple-element.44), channel_id=1, source_target_pairs={{1,2},{3,4},{5,6},{7,8},{9,10},{11,12},{13,14},{15,0},{2,1},{4,3},... | collective-permute-start | bytes 786440 | tf_op jit(solution)/shard_map/ppermute | solution.py:379
  8.4 1.1 %own.1 = (f32[4,256,512]{2,1,0:T(8,128)S(1)}, bf16[256,512]{1,0:T(8,128)(2,1)S(1)}, bf16[176,512]{1,0:T(8,128)(2,1)S(1)}, bf16[176,512]{1,0:T(8,128)(2,1)S(1)}, bf16[160,512]{1,0:T(8,128)(2,1)S(1)}) custom-call(s32[2,64]{1,0:T(2,128)S(4)} %get-tuple-element.34.lists, bf16[256,768]{1,0:T(8,128)(2,1)S(1)} %get-tuple-element.35.queries, ...), custom_call_target="tpu_custom_call" | custom-call | tf_op jit(solution)/shard_map/own/pallas_call | solution.py:405
  9.6 0.5 collective-permute-start.1
  10.2 0.8 %collective-permute-start.3 = (bf16[256,512]{1,0:T(8,128)(2,1)S(1)}, bf16[256,512]{1,0:T(8,128)(2,1)S(1)}, u32[]{:S(2)}, u32[]{:S(2)}) collective-permute-start(bf16[256,512]{1,0:T(8,128)(2,1)S(1)} %get-tuple-element.43), channel_id=1, source_target_pairs={{1,2},{3,4},{5,6},{7,8},{9,10},{11,12},{13,14},{15,0},{2,1},{4,3},... | collective-permute-start | bytes 786440 | tf_op jit(solution)/shard_map/ppermute | solution.py:379
  11.0 2.4 %hits.1 = (bf16[4,256,512]{2,1,0:T(8,128)(2,1)S(1)}, bf16[4,2,512,512]{3,2,1,0:T(8,128)(2,1)S(1)}) custom-call(s32[8,256]{1,0:T(8,128)S(1)} %bitcast.5, bf16[4,2,512,512]{3,2,1,0:T(8,128)(2,1)} %tiles.1), custom_call_target="tpu_custom_call" | custom-call | tf_op jit(solution)/shard_map/hits/pallas_call | solution.py:412
  13.5 0.8 %base.1 = f32[4,256,512]{2,1,0:T(8,128)S(1)} custom-call(s32[2,64]{1,0:T(2,128)S(4)} %get-tuple-element.34.lists, f32[4,256,512]{2,1,0:T(8,128)S(1)} %get-tuple-element.37.own, bf16[4,2,512,512]{3,2,1,0:T(8,128)(2,1)S(1)} %get-tuple-element.38.tiles, bf16[176,512]{1,0:T(8,128)(2,1)S(1)} %collective-permute-done.rest_0_, ...), custom_call_target="tpu_custom_call" | custom-call | tf_op jit(solution)/shard_map/base/pallas_call | solution.py:420
  14.2 1.2 %signal.2 = (bf16[4,256,512]{2,1,0:T(8,128)(2,1)S(1)}, bf16[256,512]{1,0:T(8,128)(2,1)S(1)}) custom-call(s32[2,64]{1,0:T(2,128)S(4)} %get-tuple-element.34.lists, f32[4,256,512]{2,1,0:T(8,128)S(1)} %base.1, bf16[4,256,512]{2,1,0:T(8,128)(2,1)S(1)} %get-tuple-element.42.hits, f32[1,2048]{1,0:T(1,128)S(1)} %bitcast.3, ...), custom_call_target="tpu_custom_call" | custom-call | flops 2000000000 | tf_op jit(solution)/shard_map/signal/pallas_call | solution.py:430
  15.5 3.1 %collective-permute-start.5 = (bf16[256,512]{1,0:T(8,128)(2,1)S(1)}, bf16[256,512]{1,0:T(8,128)(2,1)S(1)}, u32[]{:S(2)}, u32[]{:S(2)}) collective-permute-start(bf16[256,512]{1,0:T(8,128)(2,1)S(1)} %get-tuple-element.47), channel_id=1, source_target_pairs={{1,2},{3,4},{5,6},{7,8},{9,10},{11,12},{13,14},{15,0},{2,1},{4,3},... | collective-permute-start | bytes 786440 | tf_op jit(solution)/shard_map/ppermute | solution.py:379
  18.8 1.2 %signal.3 = (bf16[4,256,512]{2,1,0:T(8,128)(2,1)S(1)}, bf16[256,512]{1,0:T(8,128)(2,1)S(1)}) custom-call(s32[2,64]{1,0:T(2,128)S(4)} %get-tuple-element.34.lists, f32[4,256,512]{2,1,0:T(8,128)S(1)} %base.1, bf16[4,256,512]{2,1,0:T(8,128)(2,1)S(1)} %get-tuple-element.42.hits, f32[1,2048]{1,0:T(1,128)S(1)} %bitcast.4, ...), custom_call_target="tpu_custom_call", output_to_operand_aliasing={{0}: (6, {})} | custom-call | tf_op jit(solution)/shard_map/signal/pallas_call | solution.py:430
  20.0 1.9 %collective-permute-start.9 = (bf16[256,512]{1,0:T(8,128)(2,1)S(1)}, bf16[256,512]{1,0:T(8,128)(2,1)S(1)}, u32[]{:S(2)}, u32[]{:S(2)}) collective-permute-start(bf16[256,512]{1,0:T(8,128)(2,1)S(1)} %get-tuple-element.52), channel_id=1, source_target_pairs={{1,2},{3,4},{5,6},{7,8},{9,10},{11,12},{13,14},{15,0},{2,1},{4,3},... | collective-permute-start | bytes 786440 | tf_op jit(solution)/shard_map/ppermute | solution.py:379
  21.8 0.8 %push.1 = (bf16[176,512]{1,0:T(8,128)(2,1)S(1)}, bf16[176,512]{1,0:T(8,128)(2,1)S(1)}, bf16[160,512]{1,0:T(8,128)(2,1)S(1)}) custom-call(s32[2,64]{1,0:T(2,128)S(4)} %get-tuple-element.34.lists, bf16[4,256,512]{2,1,0:T(8,128)(2,1)S(1)} %get-tuple-element.46.signal, bf16[4,2,512,512]{3,2,1,0:T(8,128)(2,1)S(1)} %get-tuple-element.38.tiles), custom_call_target="tpu_custom_call" | custom-call | tf_op jit(solution)/shard_map/push/pallas_call | solution.py:444
  22.6 6.0 %collective-permute-start.6 = (bf16[176,512]{1,0:T(8,128)(2,1)S(1)}, bf16[176,512]{1,0:T(8,128)(2,1)S(1)}, u32[]{:S(2)}, u32[]{:S(2)}) collective-permute-start(bf16[176,512]{1,0:T(8,128)(2,1)S(1)} %get-tuple-element.48), channel_id=1, source_target_pairs={{0,1},{1,0},{2,3},{3,2},{4,5},{5,4},{6,7},{7,6},{8,9},{9,8},{10,11... | collective-permute-start | bytes 540680 | tf_op jit(solution)/shard_map/ppermute | solution.py:285
  29.1 1.0 %query.1.part = f32[256,768]{1,0:T(8,128)S(1)} custom-call(bf16[4,256,512]{2,1,0:T(8,128)(2,1)S(1)} %get-tuple-element.46.signal, bf16[2048,768]{1,0:T(8,128)(2,1)S(1)} %get-tuple-element.36.embeddings), custom_call_target="tpu_custom_call" | custom-call | tf_op jit(solution)/shard_map/query/pallas_call | solution.py:454
  30.6 0.6 %query_on.1 = (f32[256,768]{1,0:T(8,128)S(1)}, bf16[2,256,512]{2,1,0:T(8,128)(2,1)S(1)}) custom-call(s32[2,64]{1,0:T(2,128)S(4)} %get-tuple-element.34.lists, f32[256,768]{1,0:T(8,128)S(1)} %query_half.1.part, bf16[2048,768]{1,0:T(8,128)(2,1)S(1)} %get-tuple-element.36.embeddings, bf16[176,512]{1,0:T(8,128)(2,1)S(1)} %collective-permute-done.6.rest_0_, ...), custom_call_target="tpu_custom_call" | custom-call | tf_op jit(solution)/shard_map/query_on/pallas_call | solution.py:462
  31.2 0.6 %embed.4 = (bf16[512,768]{1,0:T(8,128)(2,1)S(1)}, f32[8,128]{1,0:T(8,128)S(1)}) custom-call(s32[2,64]{1,0:T(2,128)S(4)} %get-tuple-element.34.lists, bf16[4,256,512]{2,1,0:T(8,128)(2,1)S(1)} %get-tuple-element.46.signal, bf16[2,256,512]{2,1,0:T(8,128)(2,1)S(1)} %get-tuple-element.51.on, bf16[256,512]{1,0:T(8,128)(2,1)S(1)} %collective-permute-done.5.received.off_a, ...), custom_call_target="tpu_custom_call" | custom-call | tf_op jit(solution)/shard_map/embed/pallas_call | solution.py:470
  32.5 1.1 %collective-permute-done.10.got = bf16[128,768]{1,0:T(8,128)(2,1)S(1)} collective-permute-done((bf16[128,768]{1,0:T(8,128)(2,1)S(1)}, bf16[128,768]{1,0:T(8,128)(2,1)S(1)}, u32[]{:S(2)}, u32[]{:S(2)}) %collective-permute-start.10) | collective-permute-done | bytes 196640 | tf_op jit(solution)/shard_map/ppermute | solution.py:285
  33.6 1.7 %collective-permute-start.15 = (bf16[64,768]{1,0:T(8,128)(2,1)S(1)}, bf16[64,768]{1,0:T(8,128)(2,1)S(1)}, u32[]{:S(2)}, u32[]{:S(2)}) collective-permute-start(bf16[64,768]{1,0:T(8,128)(2,1)S(1)} %get-tuple-element.62.held), channel_id=1, source_target_pairs={{0,2},{1,3},{2,0},{3,1},{4,6},{5,7},{6,4},{7,5},{8,10},{9,11},{10,... | collective-permute-start | bytes 294920 | tf_op jit(solution)/shard_map/ppermute | solution.py:285
  35.3 0.7 %collective-permute-start.11 = (bf16[64,768]{1,0:T(8,128)(2,1)S(1)}, bf16[64,768]{1,0:T(8,128)(2,1)S(1)}, u32[]{:S(2)}, u32[]{:S(2)}) collective-permute-start(bf16[64,768]{1,0:T(8,128)(2,1)S(1)} %get-tuple-element.61.held), channel_id=1, source_target_pairs={{0,8},{1,9},{2,10},{3,11},{4,12},{5,13},{6,14},{7,15},{8,0},{9,1},... | collective-permute-start | bytes 294920 | tf_op jit(solution)/shard_map/ppermute | solution.py:285
  36.0 0.9 %embed.5 = (bf16[2048,768]{1,0:T(8,128)(2,1)}, bf16[512,768]{1,0:T(8,128)(2,1)S(1)}, f32[8,128]{1,0:T(8,128)S(1)}) custom-call(s32[2,64]{1,0:T(2,128)S(4)} %get-tuple-element.34.lists, bf16[4,256,512]{2,1,0:T(8,128)(2,1)S(1)} %get-tuple-element.46.signal, bf16[2,256,512]{2,1,0:T(8,128)(2,1)S(1)} %get-tuple-element.51.on, ...), custom_call_target="tpu_custom_call" | custom-call | tf_op jit(solution)/shard_map/embed/pallas_call | solution.py:470
  36.9 1.6 %collective-permute-done.15.got = bf16[64,768]{1,0:T(8,128)(2,1)S(1)} collective-permute-done((bf16[64,768]{1,0:T(8,128)(2,1)S(1)}, bf16[64,768]{1,0:T(8,128)(2,1)S(1)}, u32[]{:S(2)}, u32[]{:S(2)}) %collective-permute-start.15) | collective-permute-done | bytes 98336 | tf_op jit(solution)/shard_map/ppermute | solution.py:285
  38.6 1.5 %collective-permute-start.16 = (bf16[64,768]{1,0:T(8,128)(2,1)S(1)}, bf16[64,768]{1,0:T(8,128)(2,1)S(1)}, u32[]{:S(2)}, u32[]{:S(2)}) collective-permute-start(bf16[64,768]{1,0:T(8,128)(2,1)S(1)} %add.9.held), channel_id=1, source_target_pairs={{0,4},{1,5},{2,6},{3,7},{4,0},{5,1},{6,2},{7,3},{8,12},{9,13},{10,... | collective-permute-start | bytes 294920 | tf_op jit(solution)/shard_map/ppermute | solution.py:285
  40.1 2.9 %collective-permute-done.11.got = bf16[64,768]{1,0:T(8,128)(2,1)S(1)} collective-permute-done((bf16[64,768]{1,0:T(8,128)(2,1)S(1)}, bf16[64,768]{1,0:T(8,128)(2,1)S(1)}, u32[]{:S(2)}, u32[]{:S(2)}) %collective-permute-start.11) | collective-permute-done | bytes 98336 | tf_op jit(solution)/shard_map/ppermute | solution.py:285
  43.0 0.5 collective-permute-start.12
  43.5 0.9 %embed.6 = (bf16[2048,768]{1,0:T(8,128)(2,1)}, bf16[512,768]{1,0:T(8,128)(2,1)S(1)}, f32[8,128]{1,0:T(8,128)S(1)}) custom-call(s32[2,64]{1,0:T(2,128)S(4)} %get-tuple-element.34.lists, bf16[4,256,512]{2,1,0:T(8,128)(2,1)S(1)} %get-tuple-element.46.signal, bf16[2,256,512]{2,1,0:T(8,128)(2,1)S(1)} %get-tuple-element.51.on, ...), custom_call_target="tpu_custom_call", output_to_operand_aliasing={{0}: (6, {})} | custom-call | tf_op jit(solution)/shard_map/embed/pallas_call | solution.py:470
  44.4 0.7 %collective-permute-start.17 = (bf16[64,768]{1,0:T(8,128)(2,1)S(1)}, bf16[64,768]{1,0:T(8,128)(2,1)S(1)}, u32[]{:S(2)}, u32[]{:S(2)}) collective-permute-start(bf16[64,768]{1,0:T(8,128)(2,1)S(1)} %add.10.held), channel_id=1, source_target_pairs={{0,8},{1,9},{2,10},{3,11},{4,12},{5,13},{6,14},{7,15},{8,0},{9,1},... | collective-permute-start | bytes 294920 | tf_op jit(solution)/shard_map/ppermute | solution.py:285
  45.1 2.6 %collective-permute-done.12.got = bf16[64,768]{1,0:T(8,128)(2,1)S(1)} collective-permute-done((bf16[64,768]{1,0:T(8,128)(2,1)S(1)}, bf16[64,768]{1,0:T(8,128)(2,1)S(1)}, u32[]{:S(2)}, u32[]{:S(2)}) %collective-permute-start.12) | collective-permute-done | bytes 98336 | tf_op jit(solution)/shard_map/ppermute | solution.py:285
  47.8 2.3 %embed.7 = (bf16[2048,768]{1,0:T(8,128)(2,1)}, bf16[512,768]{1,0:T(8,128)(2,1)}, f32[8,128]{1,0:T(8,128)S(1)}) custom-call(s32[2,64]{1,0:T(2,128)S(4)} %get-tuple-element.34.lists, bf16[4,256,512]{2,1,0:T(8,128)(2,1)S(1)} %get-tuple-element.46.signal, bf16[2,256,512]{2,1,0:T(8,128)(2,1)S(1)} %get-tuple-element.51.on, ...), custom_call_target="tpu_custom_call", output_to_operand_aliasing={{0}: (7, {})} | custom-call | tf_op jit(solution)/shard_map/embed/pallas_call | solution.py:470
  50.1 1.2 %collective-permute-done.17.got = bf16[64,768]{1,0:T(8,128)(2,1)S(1)} collective-permute-done((bf16[64,768]{1,0:T(8,128)(2,1)S(1)}, bf16[64,768]{1,0:T(8,128)(2,1)S(1)}, u32[]{:S(2)}, u32[]{:S(2)}) %collective-permute-start.17) | collective-permute-done | bytes 98336 | tf_op jit(solution)/shard_map/ppermute | solution.py:285
  51.4 1.0 %collective-permute-done.13.got = bf16[64,768]{1,0:T(8,128)(2,1)S(1)} collective-permute-done((bf16[64,768]{1,0:T(8,128)(2,1)S(1)}, bf16[64,768]{1,0:T(8,128)(2,1)S(1)}, u32[]{:S(2)}, u32[]{:S(2)}) %collective-permute-start.13) | collective-permute-done | bytes 98336 | tf_op jit(solution)/shard_map/ppermute | solution.py:285
  52.7 0.8 %place.2.refs_1_ = f32[256,768]{1,0:T(8,128)} custom-call(bf16[64,768]{1,0:T(8,128)(2,1)S(1)} %add.11.refs_0_, bf16[64,768]{1,0:T(8,128)(2,1)S(1)} %add.8.refs_1_, bf16[64,768]{1,0:T(8,128)(2,1)S(1)} %collective-permute-done.18.refs_2_), custom_call_target="tpu_custom_call" | custom-call | tf_op jit(solution)/shard_map/place/pallas_call | solution.py:352
  53.8 0.7 %place.3 = f32[256,768]{1,0:T(8,128)} custom-call(bf16[64,768]{1,0:T(8,128)(2,1)S(1)} %collective-permute-done.14.refs_0_, f32[256,768]{1,0:T(8,128)} %place.2.refs_1_), custom_call_target="tpu_custom_call", output_to_operand_aliasing={{}: (1, {})} | custom-call | tf_op jit(solution)/shard_map/place/pallas_call | solution.py:352
  (35 shorter events, 2.8 us)
Async XLA Ops:
  0.6 10.3 %copy-start.1 = (s32[256,8]{0,1:T(8,128)S(1)}, s32[256,8]{0,1:T(8,128)}, u32[]{:S(2)}) copy-start(s32[256,8]{0,1:T(8,128)} %param.11) | copy-start | bytes 24580
  2.9 11.3 %collective-permute-start.4 = (bf16[256,512]{1,0:T(8,128)(2,1)S(1)}, bf16[256,512]{1,0:T(8,128)(2,1)S(1)}, u32[]{:S(2)}, u32[]{:S(2)}) collective-permute-start(bf16[256,512]{1,0:T(8,128)(2,1)S(1)} %get-tuple-element.44), channel_id=1, source_target_pairs={{1,2},{3,4},{5,6},{7,8},{9,10},{11,12},{13,14},{15,0},{2,1},{4,3},... | collective-permute-start | bytes 786440 | tf_op jit(solution)/shard_map/ppermute | solution.py:379
  9.5 3.9 %collective-permute-start = (bf16[176,512]{1,0:T(8,128)(2,1)S(1)}, bf16[176,512]{1,0:T(8,128)(2,1)S(1)}, u32[]{:S(2)}, u32[]{:S(2)}) collective-permute-start(bf16[176,512]{1,0:T(8,128)(2,1)S(1)} %get-tuple-element.39), channel_id=1, source_target_pairs={{0,1},{1,0},{2,3},{3,2},{4,5},{5,4},{6,7},{7,6},{8,9},{9,8},{10,11... | collective-permute-start | bytes 540680 | tf_op jit(solution)/shard_map/ppermute | solution.py:285
  9.6 3.9 %collective-permute-start.1 = (bf16[176,512]{1,0:T(8,128)(2,1)S(1)}, bf16[176,512]{1,0:T(8,128)(2,1)S(1)}, u32[]{:S(2)}, u32[]{:S(2)}) collective-permute-start(bf16[176,512]{1,0:T(8,128)(2,1)S(1)} %get-tuple-element.40), channel_id=1, source_target_pairs={{0,1},{1,0},{2,3},{3,2},{4,5},{5,4},{6,7},{7,6},{8,9},{9,8},{10,11... | collective-permute-start | bytes 540680 | tf_op jit(solution)/shard_map/ppermute | solution.py:285
  10.1 3.3 %collective-permute-start.2 = (bf16[160,512]{1,0:T(8,128)(2,1)S(1)}, bf16[160,512]{1,0:T(8,128)(2,1)S(1)}, u32[]{:S(2)}, u32[]{:S(2)}) collective-permute-start(bf16[160,512]{1,0:T(8,128)(2,1)S(1)} %get-tuple-element.41), channel_id=1, source_target_pairs={{0,1},{1,0},{2,3},{3,2},{4,5},{5,4},{6,7},{7,6},{8,9},{9,8},{10,11... | collective-permute-start | bytes 491528 | tf_op jit(solution)/shard_map/ppermute | solution.py:285
  10.2 8.6 %collective-permute-start.3 = (bf16[256,512]{1,0:T(8,128)(2,1)S(1)}, bf16[256,512]{1,0:T(8,128)(2,1)S(1)}, u32[]{:S(2)}, u32[]{:S(2)}) collective-permute-start(bf16[256,512]{1,0:T(8,128)(2,1)S(1)} %get-tuple-element.43), channel_id=1, source_target_pairs={{1,2},{3,4},{5,6},{7,8},{9,10},{11,12},{13,14},{15,0},{2,1},{4,3},... | collective-permute-start | bytes 786440 | tf_op jit(solution)/shard_map/ppermute | solution.py:379
  13.4 0.8 %copy-start = (f32[2048]{0:T(1024)S(1)}, f32[2048]{0:T(1024)}, u32[]{:S(2)}) copy-start(f32[2048]{0:T(1024)} %param.9) | copy-start | bytes 24580
  15.5 14.7 %collective-permute-start.5 = (bf16[256,512]{1,0:T(8,128)(2,1)S(1)}, bf16[256,512]{1,0:T(8,128)(2,1)S(1)}, u32[]{:S(2)}, u32[]{:S(2)}) collective-permute-start(bf16[256,512]{1,0:T(8,128)(2,1)S(1)} %get-tuple-element.47), channel_id=1, source_target_pairs={{1,2},{3,4},{5,6},{7,8},{9,10},{11,12},{13,14},{15,0},{2,1},{4,3},... | collective-permute-start | bytes 786440 | tf_op jit(solution)/shard_map/ppermute | solution.py:379
  20.0 11.8 %collective-permute-start.9 = (bf16[256,512]{1,0:T(8,128)(2,1)S(1)}, bf16[256,512]{1,0:T(8,128)(2,1)S(1)}, u32[]{:S(2)}, u32[]{:S(2)}) collective-permute-start(bf16[256,512]{1,0:T(8,128)(2,1)S(1)} %get-tuple-element.52), channel_id=1, source_target_pairs={{1,2},{3,4},{5,6},{7,8},{9,10},{11,12},{13,14},{15,0},{2,1},{4,3},... | collective-permute-start | bytes 786440 | tf_op jit(solution)/shard_map/ppermute | solution.py:379
  22.6 7.9 %collective-permute-start.6 = (bf16[176,512]{1,0:T(8,128)(2,1)S(1)}, bf16[176,512]{1,0:T(8,128)(2,1)S(1)}, u32[]{:S(2)}, u32[]{:S(2)}) collective-permute-start(bf16[176,512]{1,0:T(8,128)(2,1)S(1)} %get-tuple-element.48), channel_id=1, source_target_pairs={{0,1},{1,0},{2,3},{3,2},{4,5},{5,4},{6,7},{7,6},{8,9},{9,8},{10,11... | collective-permute-start | bytes 540680 | tf_op jit(solution)/shard_map/ppermute | solution.py:285
  28.6 1.9 %collective-permute-start.7 = (bf16[176,512]{1,0:T(8,128)(2,1)S(1)}, bf16[176,512]{1,0:T(8,128)(2,1)S(1)}, u32[]{:S(2)}, u32[]{:S(2)}) collective-permute-start(bf16[176,512]{1,0:T(8,128)(2,1)S(1)} %get-tuple-element.49), channel_id=1, source_target_pairs={{0,1},{1,0},{2,3},{3,2},{4,5},{5,4},{6,7},{7,6},{8,9},{9,8},{10,11... | collective-permute-start | bytes 540680 | tf_op jit(solution)/shard_map/ppermute | solution.py:285
  28.7 1.8 %collective-permute-start.8 = (bf16[160,512]{1,0:T(8,128)(2,1)S(1)}, bf16[160,512]{1,0:T(8,128)(2,1)S(1)}, u32[]{:S(2)}, u32[]{:S(2)}) collective-permute-start(bf16[160,512]{1,0:T(8,128)(2,1)S(1)} %get-tuple-element.50), channel_id=1, source_target_pairs={{0,1},{1,0},{2,3},{3,2},{4,5},{5,4},{6,7},{7,6},{8,9},{9,8},{10,11... | collective-permute-start | bytes 491528 | tf_op jit(solution)/shard_map/ppermute | solution.py:285
  32.1 1.5 %collective-permute-start.10 = (bf16[128,768]{1,0:T(8,128)(2,1)S(1)}, bf16[128,768]{1,0:T(8,128)(2,1)S(1)}, u32[]{:S(2)}, u32[]{:S(2)}) collective-permute-start(bf16[128,768]{1,0:T(8,128)(2,1)S(1)} %query_end.3), channel_id=1, source_target_pairs={{0,1},{1,0},{2,3},{3,2},{4,5},{5,4},{6,7},{7,6},{8,9},{9,8},{10,11... | collective-permute-start | bytes 589832 | tf_op jit(solution)/shard_map/ppermute | solution.py:285
  33.6 4.9 %collective-permute-start.15 = (bf16[64,768]{1,0:T(8,128)(2,1)S(1)}, bf16[64,768]{1,0:T(8,128)(2,1)S(1)}, u32[]{:S(2)}, u32[]{:S(2)}) collective-permute-start(bf16[64,768]{1,0:T(8,128)(2,1)S(1)} %get-tuple-element.62.held), channel_id=1, source_target_pairs={{0,2},{1,3},{2,0},{3,1},{4,6},{5,7},{6,4},{7,5},{8,10},{9,11},{10,... | collective-permute-start | bytes 294920 | tf_op jit(solution)/shard_map/ppermute | solution.py:285
  35.3 7.7 %collective-permute-start.11 = (bf16[64,768]{1,0:T(8,128)(2,1)S(1)}, bf16[64,768]{1,0:T(8,128)(2,1)S(1)}, u32[]{:S(2)}, u32[]{:S(2)}) collective-permute-start(bf16[64,768]{1,0:T(8,128)(2,1)S(1)} %get-tuple-element.61.held), channel_id=1, source_target_pairs={{0,8},{1,9},{2,10},{3,11},{4,12},{5,13},{6,14},{7,15},{8,0},{9,1},... | collective-permute-start | bytes 294920 | tf_op jit(solution)/shard_map/ppermute | solution.py:285
  38.6 5.8 %collective-permute-start.16 = (bf16[64,768]{1,0:T(8,128)(2,1)S(1)}, bf16[64,768]{1,0:T(8,128)(2,1)S(1)}, u32[]{:S(2)}, u32[]{:S(2)}) collective-permute-start(bf16[64,768]{1,0:T(8,128)(2,1)S(1)} %add.9.held), channel_id=1, source_target_pairs={{0,4},{1,5},{2,6},{3,7},{4,0},{5,1},{6,2},{7,3},{8,12},{9,13},{10,... | collective-permute-start | bytes 294920 | tf_op jit(solution)/shard_map/ppermute | solution.py:285
  43.0 4.7 %collective-permute-start.12 = (bf16[64,768]{1,0:T(8,128)(2,1)S(1)}, bf16[64,768]{1,0:T(8,128)(2,1)S(1)}, u32[]{:S(2)}, u32[]{:S(2)}) collective-permute-start(bf16[64,768]{1,0:T(8,128)(2,1)S(1)} %add.6.held), channel_id=1, source_target_pairs={{0,2},{1,3},{2,0},{3,1},{4,6},{5,7},{6,4},{7,5},{8,10},{9,11},{10,... | collective-permute-start | bytes 294920 | tf_op jit(solution)/shard_map/ppermute | solution.py:285
  44.4 6.9 %collective-permute-start.17 = (bf16[64,768]{1,0:T(8,128)(2,1)S(1)}, bf16[64,768]{1,0:T(8,128)(2,1)S(1)}, u32[]{:S(2)}, u32[]{:S(2)}) collective-permute-start(bf16[64,768]{1,0:T(8,128)(2,1)S(1)} %add.10.held), channel_id=1, source_target_pairs={{0,8},{1,9},{2,10},{3,11},{4,12},{5,13},{6,14},{7,15},{8,0},{9,1},... | collective-permute-start | bytes 294920 | tf_op jit(solution)/shard_map/ppermute | solution.py:285
  47.7 4.7 %collective-permute-start.13 = (bf16[64,768]{1,0:T(8,128)(2,1)S(1)}, bf16[64,768]{1,0:T(8,128)(2,1)S(1)}, u32[]{:S(2)}, u32[]{:S(2)}) collective-permute-start(bf16[64,768]{1,0:T(8,128)(2,1)S(1)} %add.7.held), channel_id=1, source_target_pairs={{0,4},{1,5},{2,6},{3,7},{4,0},{5,1},{6,2},{7,3},{8,12},{9,13},{10,... | collective-permute-start | bytes 294920 | tf_op jit(solution)/shard_map/ppermute | solution.py:285
  51.3 1.4 %collective-permute-start.18 = (bf16[64,768]{1,0:T(8,128)(2,1)S(1)}, bf16[64,768]{1,0:T(8,128)(2,1)S(1)}, u32[]{:S(2)}, u32[]{:S(2)}) collective-permute-start(bf16[64,768]{1,0:T(8,128)(2,1)S(1)} %add.11.refs_0_), channel_id=1, source_target_pairs={{0,1},{1,0},{2,3},{3,2},{4,5},{5,4},{6,7},{7,6},{8,9},{9,8},{10,11... | collective-permute-start | bytes 294920 | tf_op jit(solution)/shard_map/ppermute | solution.py:285
  52.4 1.4 %collective-permute-start.14 = (bf16[64,768]{1,0:T(8,128)(2,1)S(1)}, bf16[64,768]{1,0:T(8,128)(2,1)S(1)}, u32[]{:S(2)}, u32[]{:S(2)}) collective-permute-start(bf16[64,768]{1,0:T(8,128)(2,1)S(1)} %add.8.refs_1_), channel_id=1, source_target_pairs={{0,1},{1,0},{2,3},{3,2},{4,5},{5,4},{6,7},{7,6},{8,9},{9,8},{10,11... | collective-permute-start | bytes 294920 | tf_op jit(solution)/shard_map/ppermute | solution.py:285

commit v20 on v17

--- a/solution.py
+++ b/solution.py
@@ -325,7 +325,7 @@
         last = k == len(bits) - 1
         got = [exchange(value, order[k]) for value, order in zip(held, orders)]
         for chain in range(2):
-            after = beside[k : k + 1] if chain == 0 else []
+            after = beside[k : k + 1] if chain == 0 else held[:1] if last else []
             held[chain] = call(
                 functools.partial(add_kernel, scale=scale if last else 1.0),
                 "add",
@@ -349,8 +349,8 @@
             aliases={len(values): 0} if begun else None,
         )(*values, *begun)
 
-    early = place([held[0], held[1], swapped[0]], [(0, True), (1, True), (0, False)])
-    return place([swapped[1]], [(1, False)], early)
+    early = place(held, [(0, True), (1, True)])
+    return place(swapped, [(0, False), (1, False)], early)
 
 
 def per_device(embeddings, edge_tiles, neighbour, propensity, queries, positives):

time: 55.2 us -> 55.6 us (level)
  waiting for transfers between devices: 7.66 us -> 8.6 us
    ppermute x15, waiting for transfers between devices: 4.51 us -> 8.59 us  [exchange(): return lax.ppermute(value, AXIS, [(i, i ^ mask) for i in range(count)])]
    ppermute x4, waiting for transfers between devices: 3.15 us -> 0.01 us  [off_swap(): return lax.ppermute(value, AXIS, off_route)]
    ppermute x15, starting transfers between devices: 16.5 us -> 15.9 us  [exchange(): return lax.ppermute(value, AXIS, [(i, i ^ mask) for i in range(count)])]
  transfers between devices with their start and end apart: 19 -> 19, of which waited for: 8 -> 7; matrix products, arithmetic and copies ran while one was open for 0% -> 0% of each run, Pallas kernels for 28% -> 28%
where the time goes in v20:
time: 55.6 us; the launch traced here: 55.1 us
  starting transfers between devices  27.1 us (49%)
  Pallas kernels  18.4 us (33%)
  waiting for transfers between devices  8.6 us (15%)
  between operations  0.92 us (2%)
    ppermute x15, starting transfers between devices, exchange(): return lax.ppermute(value, AXIS, [(i, i ^ mask) for i in range(count)])  15.9 us
    ppermute x4, starting transfers between devices, off_swap(): return lax.ppermute(value, AXIS, off_route)  11.2 us
    ppermute x15, waiting for transfers between devices, exchange(): return lax.ppermute(value, AXIS, [(i, i ^ mask) for i in range(count)])  8.59 us
    pallas_call x4, Pallas kernels, embed(): call(functools.partial(embed_kernel, blocks=blocks, turn=turn, scale=1.0...  4.57 us
    pallas_call x1, Pallas kernels, per_device(): call(hits_kernel, 'hits', [VMEM, HBM], [in_vmem(full, BF16), in_vmem(edge...  2.45 us
    pallas_call x2, Pallas kernels, signal_of(): call(functools.partial(signal_kernel, slot=slot), 'signal', [SMEM] + [VME...  2.41 us
    pallas_call x1, Pallas kernels, per_device(): call(functools.partial(project_kernel, scale=scale), 'project', [HBM] * 3...  2.02 us
    pallas_call x2, Pallas kernels, place(): call(functools.partial(place_kernel, places=places), 'place', [VMEM] * le...  1.54 us
  transfers between devices with their start and end apart: 19, of which 7 were waited for; matrix products, arithmetic and copies ran while one was open for 0% of the time, Pallas kernels for 28%

profile of v20, /device:TPU:0, one launch (start us, length us, event | category | flops | bytes accessed | tf_op | source)
XLA Modules:
  0.0 55.1 jit_solution(626678695187395224)
XLA Ops:
  0.6 2.0 %project.1 = (bf16[256,512]{1,0:T(8,128)(2,1)S(1)}, bf16[256,768]{1,0:T(8,128)(2,1)S(1)}, bf16[2048,768]{1,0:T(8,128)(2,1)S(1)}, s32[2,64]{1,0:T(2,128)S(4)}) custom-call(s32[2,64]{1,0:T(2,128)} %bitcast.6, bf16[256,768]{1,0:T(8,128)(2,1)} %queries.1, bf16[2048,768]{1,0:T(8,128)(2,1)} %embeddings.1), custom_call_target="tpu_custom_call" | custom-call | tf_op jit(solution)/shard_map/project/pallas_call | solution.py:378
  2.7 5.5 %collective-permute-start.4 = (bf16[256,512]{1,0:T(8,128)(2,1)S(1)}, bf16[256,512]{1,0:T(8,128)(2,1)S(1)}, u32[]{:S(2)}, u32[]{:S(2)}) collective-permute-start(bf16[256,512]{1,0:T(8,128)(2,1)S(1)} %get-tuple-element.44), channel_id=1, source_target_pairs={{1,2},{3,4},{5,6},{7,8},{9,10},{11,12},{13,14},{15,0},{2,1},{4,3},... | collective-permute-start | bytes 786440 | tf_op jit(solution)/shard_map/ppermute | solution.py:366
  8.2 1.1 %own.1 = (f32[4,256,512]{2,1,0:T(8,128)S(1)}, bf16[256,512]{1,0:T(8,128)(2,1)S(1)}, bf16[176,512]{1,0:T(8,128)(2,1)S(1)}, bf16[176,512]{1,0:T(8,128)(2,1)S(1)}, bf16[160,512]{1,0:T(8,128)(2,1)S(1)}) custom-call(s32[2,64]{1,0:T(2,128)S(4)} %get-tuple-element.34.lists, bf16[256,768]{1,0:T(8,128)(2,1)S(1)} %get-tuple-element.35.queries, ...), custom_call_target="tpu_custom_call" | custom-call | tf_op jit(solution)/shard_map/own/pallas_call | solution.py:392
  9.4 0.5 collective-permute-start.1
  9.9 0.6 %collective-permute-start.3 = (bf16[256,512]{1,0:T(8,128)(2,1)S(1)}, bf16[256,512]{1,0:T(8,128)(2,1)S(1)}, u32[]{:S(2)}, u32[]{:S(2)}) collective-permute-start(bf16[256,512]{1,0:T(8,128)(2,1)S(1)} %get-tuple-element.43), channel_id=1, source_target_pairs={{1,2},{3,4},{5,6},{7,8},{9,10},{11,12},{13,14},{15,0},{2,1},{4,3},... | collective-permute-start | bytes 786440 | tf_op jit(solution)/shard_map/ppermute | solution.py:366
  10.6 2.4 %hits.1 = (bf16[4,256,512]{2,1,0:T(8,128)(2,1)S(1)}, bf16[4,2,512,512]{3,2,1,0:T(8,128)(2,1)S(1)}) custom-call(s32[8,256]{1,0:T(8,128)S(1)} %bitcast.5, bf16[4,2,512,512]{3,2,1,0:T(8,128)(2,1)} %tiles.1), custom_call_target="tpu_custom_call" | custom-call | tf_op jit(solution)/shard_map/hits/pallas_call | solution.py:399
  13.1 0.8 %base.1 = f32[4,256,512]{2,1,0:T(8,128)S(1)} custom-call(s32[2,64]{1,0:T(2,128)S(4)} %get-tuple-element.34.lists, f32[4,256,512]{2,1,0:T(8,128)S(1)} %get-tuple-element.37.own, bf16[4,2,512,512]{3,2,1,0:T(8,128)(2,1)S(1)} %get-tuple-element.38.tiles, bf16[176,512]{1,0:T(8,128)(2,1)S(1)} %collective-permute-done.rest_0_, ...), custom_call_target="tpu_custom_call" | custom-call | tf_op jit(solution)/shard_map/base/pallas_call | solution.py:407
  13.8 0.6 %signal.2 = (bf16[4,256,512]{2,1,0:T(8,128)(2,1)S(1)}, bf16[256,512]{1,0:T(8,128)(2,1)S(1)}) custom-call(s32[2,64]{1,0:T(2,128)S(4)} %get-tuple-element.34.lists, f32[4,256,512]{2,1,0:T(8,128)S(1)} %base.1, bf16[4,256,512]{2,1,0:T(8,128)(2,1)S(1)} %get-tuple-element.42.hits, f32[1,2048]{1,0:T(1,128)S(1)} %bitcast.3, ...), custom_call_target="tpu_custom_call" | custom-call | flops 2000000000 | tf_op jit(solution)/shard_map/signal/pallas_call | solution.py:417
  14.5 5.0 %collective-permute-start.5 = (bf16[256,512]{1,0:T(8,128)(2,1)S(1)}, bf16[256,512]{1,0:T(8,128)(2,1)S(1)}, u32[]{:S(2)}, u32[]{:S(2)}) collective-permute-start(bf16[256,512]{1,0:T(8,128)(2,1)S(1)} %get-tuple-element.47), channel_id=1, source_target_pairs={{1,2},{3,4},{5,6},{7,8},{9,10},{11,12},{13,14},{15,0},{2,1},{4,3},... | collective-permute-start | bytes 786440 | tf_op jit(solution)/shard_map/ppermute | solution.py:366
  19.5 1.8 %signal.3 = (bf16[4,256,512]{2,1,0:T(8,128)(2,1)S(1)}, bf16[256,512]{1,0:T(8,128)(2,1)S(1)}) custom-call(s32[2,64]{1,0:T(2,128)S(4)} %get-tuple-element.34.lists, f32[4,256,512]{2,1,0:T(8,128)S(1)} %base.1, bf16[4,256,512]{2,1,0:T(8,128)(2,1)S(1)} %get-tuple-element.42.hits, f32[1,2048]{1,0:T(1,128)S(1)} %bitcast.4, ...), custom_call_target="tpu_custom_call", output_to_operand_aliasing={{0}: (6, {})} | custom-call | tf_op jit(solution)/shard_map/signal/pallas_call | solution.py:417
  21.4 0.8 %push.1 = (bf16[176,512]{1,0:T(8,128)(2,1)S(1)}, bf16[176,512]{1,0:T(8,128)(2,1)S(1)}, bf16[160,512]{1,0:T(8,128)(2,1)S(1)}) custom-call(s32[2,64]{1,0:T(2,128)S(4)} %get-tuple-element.34.lists, bf16[4,256,512]{2,1,0:T(8,128)(2,1)S(1)} %get-tuple-element.46.signal, bf16[4,2,512,512]{3,2,1,0:T(8,128)(2,1)S(1)} %get-tuple-element.38.tiles), custom_call_target="tpu_custom_call" | custom-call | tf_op jit(solution)/shard_map/push/pallas_call | solution.py:431
  22.2 5.6 %collective-permute-start.6 = (bf16[176,512]{1,0:T(8,128)(2,1)S(1)}, bf16[176,512]{1,0:T(8,128)(2,1)S(1)}, u32[]{:S(2)}, u32[]{:S(2)}) collective-permute-start(bf16[176,512]{1,0:T(8,128)(2,1)S(1)} %get-tuple-element.48), channel_id=1, source_target_pairs={{0,1},{1,0},{2,3},{3,2},{4,5},{5,4},{6,7},{7,6},{8,9},{9,8},{10,11... | collective-permute-start | bytes 540680 | tf_op jit(solution)/shard_map/ppermute | solution.py:272
  28.3 1.0 %query.1.part = f32[256,768]{1,0:T(8,128)S(1)} custom-call(bf16[4,256,512]{2,1,0:T(8,128)(2,1)S(1)} %get-tuple-element.46.signal, bf16[2048,768]{1,0:T(8,128)(2,1)S(1)} %get-tuple-element.36.embeddings), custom_call_target="tpu_custom_call" | custom-call | tf_op jit(solution)/shard_map/query/pallas_call | solution.py:441
  29.8 0.6 %query_on.1 = (f32[256,768]{1,0:T(8,128)S(1)}, bf16[2,256,512]{2,1,0:T(8,128)(2,1)S(1)}) custom-call(s32[2,64]{1,0:T(2,128)S(4)} %get-tuple-element.34.lists, f32[256,768]{1,0:T(8,128)S(1)} %query_half.1.part, bf16[2048,768]{1,0:T(8,128)(2,1)S(1)} %get-tuple-element.36.embeddings, bf16[176,512]{1,0:T(8,128)(2,1)S(1)} %collective-permute-done.6.rest_0_, ...), custom_call_target="tpu_custom_call" | custom-call | tf_op jit(solution)/shard_map/query_on/pallas_call | solution.py:449
  31.2 1.6 %collective-permute-start.10 = (bf16[128,768]{1,0:T(8,128)(2,1)S(1)}, bf16[128,768]{1,0:T(8,128)(2,1)S(1)}, u32[]{:S(2)}, u32[]{:S(2)}) collective-permute-start(bf16[128,768]{1,0:T(8,128)(2,1)S(1)} %query_end.3), channel_id=1, source_target_pairs={{0,1},{1,0},{2,3},{3,2},{4,5},{5,4},{6,7},{7,6},{8,9},{9,8},{10,11... | collective-permute-start | bytes 589832 | tf_op jit(solution)/shard_map/ppermute | solution.py:272
  33.1 0.8 %collective-permute-done.10.got = bf16[128,768]{1,0:T(8,128)(2,1)S(1)} collective-permute-done((bf16[128,768]{1,0:T(8,128)(2,1)S(1)}, bf16[128,768]{1,0:T(8,128)(2,1)S(1)}, u32[]{:S(2)}, u32[]{:S(2)}) %collective-permute-start.10) | collective-permute-done | bytes 196640 | tf_op jit(solution)/shard_map/ppermute | solution.py:272
  34.0 0.6 %collective-permute-start.11 = (bf16[64,768]{1,0:T(8,128)(2,1)S(1)}, bf16[64,768]{1,0:T(8,128)(2,1)S(1)}, u32[]{:S(2)}, u32[]{:S(2)}) collective-permute-start(bf16[64,768]{1,0:T(8,128)(2,1)S(1)} %get-tuple-element.61.held), channel_id=1, source_target_pairs={{0,2},{1,3},{2,0},{3,1},{4,6},{5,7},{6,4},{7,5},{8,10},{9,11},{10,... | collective-permute-start | bytes 294920 | tf_op jit(solution)/shard_map/ppermute | solution.py:272
  34.5 2.6 %collective-permute-start.15 = (bf16[64,768]{1,0:T(8,128)(2,1)S(1)}, bf16[64,768]{1,0:T(8,128)(2,1)S(1)}, u32[]{:S(2)}, u32[]{:S(2)}) collective-permute-start(bf16[64,768]{1,0:T(8,128)(2,1)S(1)} %get-tuple-element.65.held), channel_id=1, source_target_pairs={{0,8},{1,9},{2,10},{3,11},{4,12},{5,13},{6,14},{7,15},{8,0},{9,1},... | collective-permute-start | bytes 294920 | tf_op jit(solution)/shard_map/ppermute | solution.py:272
  37.1 0.9 %embed.5 = (bf16[2048,768]{1,0:T(8,128)(2,1)}, bf16[512,768]{1,0:T(8,128)(2,1)S(1)}, f32[8,128]{1,0:T(8,128)S(1)}) custom-call(s32[2,64]{1,0:T(2,128)S(4)} %get-tuple-element.34.lists, bf16[4,256,512]{2,1,0:T(8,128)(2,1)S(1)} %get-tuple-element.46.signal, bf16[2,256,512]{2,1,0:T(8,128)(2,1)S(1)} %get-tuple-element.51.on, ...), custom_call_target="tpu_custom_call" | custom-call | tf_op jit(solution)/shard_map/embed/pallas_call | solution.py:457
  38.0 1.1 %collective-permute-done.11.got = bf16[64,768]{1,0:T(8,128)(2,1)S(1)} collective-permute-done((bf16[64,768]{1,0:T(8,128)(2,1)S(1)}, bf16[64,768]{1,0:T(8,128)(2,1)S(1)}, u32[]{:S(2)}, u32[]{:S(2)}) %collective-permute-start.11) | collective-permute-done | bytes 98336 | tf_op jit(solution)/shard_map/ppermute | solution.py:272
  39.3 2.5 %collective-permute-done.15.got = bf16[64,768]{1,0:T(8,128)(2,1)S(1)} collective-permute-done((bf16[64,768]{1,0:T(8,128)(2,1)S(1)}, bf16[64,768]{1,0:T(8,128)(2,1)S(1)}, u32[]{:S(2)}, u32[]{:S(2)}) %collective-permute-start.15) | collective-permute-done | bytes 98336 | tf_op jit(solution)/shard_map/ppermute | solution.py:272
  41.8 1.8 %collective-permute-start.16 = (bf16[64,768]{1,0:T(8,128)(2,1)S(1)}, bf16[64,768]{1,0:T(8,128)(2,1)S(1)}, u32[]{:S(2)}, u32[]{:S(2)}) collective-permute-start(bf16[64,768]{1,0:T(8,128)(2,1)S(1)} %add.9.held), channel_id=1, source_target_pairs={{0,2},{1,3},{2,0},{3,1},{4,6},{5,7},{6,4},{7,5},{8,10},{9,11},{10,... | collective-permute-start | bytes 294920 | tf_op jit(solution)/shard_map/ppermute | solution.py:272
  43.6 0.9 %embed.6 = (bf16[2048,768]{1,0:T(8,128)(2,1)}, bf16[512,768]{1,0:T(8,128)(2,1)S(1)}, f32[8,128]{1,0:T(8,128)S(1)}) custom-call(s32[2,64]{1,0:T(2,128)S(4)} %get-tuple-element.34.lists, bf16[4,256,512]{2,1,0:T(8,128)(2,1)S(1)} %get-tuple-element.46.signal, bf16[2,256,512]{2,1,0:T(8,128)(2,1)S(1)} %get-tuple-element.51.on, ...), custom_call_target="tpu_custom_call", output_to_operand_aliasing={{0}: (6, {})} | custom-call | tf_op jit(solution)/shard_map/embed/pallas_call | solution.py:457
  44.5 0.6 %collective-permute-start.13 = (bf16[64,768]{1,0:T(8,128)(2,1)S(1)}, bf16[64,768]{1,0:T(8,128)(2,1)S(1)}, u32[]{:S(2)}, u32[]{:S(2)}) collective-permute-start(bf16[64,768]{1,0:T(8,128)(2,1)S(1)} %add.7.held), channel_id=1, source_target_pairs={{0,8},{1,9},{2,10},{3,11},{4,12},{5,13},{6,14},{7,15},{8,0},{9,1},... | collective-permute-start | bytes 294920 | tf_op jit(solution)/shard_map/ppermute | solution.py:272
  45.1 1.4 %collective-permute-done.16.got = bf16[64,768]{1,0:T(8,128)(2,1)S(1)} collective-permute-done((bf16[64,768]{1,0:T(8,128)(2,1)S(1)}, bf16[64,768]{1,0:T(8,128)(2,1)S(1)}, u32[]{:S(2)}, u32[]{:S(2)}) %collective-permute-start.16) | collective-permute-done | bytes 98336 | tf_op jit(solution)/shard_map/ppermute | solution.py:272
  46.5 1.3 %collective-permute-start.17 = (bf16[64,768]{1,0:T(8,128)(2,1)S(1)}, bf16[64,768]{1,0:T(8,128)(2,1)S(1)}, u32[]{:S(2)}, u32[]{:S(2)}) collective-permute-start(bf16[64,768]{1,0:T(8,128)(2,1)S(1)} %add.10.held), channel_id=1, source_target_pairs={{0,4},{1,5},{2,6},{3,7},{4,0},{5,1},{6,2},{7,3},{8,12},{9,13},{10,... | collective-permute-start | bytes 294920 | tf_op jit(solution)/shard_map/ppermute | solution.py:272
  47.8 2.3 %embed.7 = (bf16[2048,768]{1,0:T(8,128)(2,1)}, bf16[512,768]{1,0:T(8,128)(2,1)}, f32[8,128]{1,0:T(8,128)S(1)}) custom-call(s32[2,64]{1,0:T(2,128)S(4)} %get-tuple-element.34.lists, bf16[4,256,512]{2,1,0:T(8,128)(2,1)S(1)} %get-tuple-element.46.signal, bf16[2,256,512]{2,1,0:T(8,128)(2,1)S(1)} %get-tuple-element.51.on, ...), custom_call_target="tpu_custom_call", output_to_operand_aliasing={{0}: (7, {})} | custom-call | tf_op jit(solution)/shard_map/embed/pallas_call | solution.py:457
  50.1 1.9 %collective-permute-done.13.got = bf16[64,768]{1,0:T(8,128)(2,1)S(1)} collective-permute-done((bf16[64,768]{1,0:T(8,128)(2,1)S(1)}, bf16[64,768]{1,0:T(8,128)(2,1)S(1)}, u32[]{:S(2)}, u32[]{:S(2)}) %collective-permute-start.13) | collective-permute-done | bytes 98336 | tf_op jit(solution)/shard_map/ppermute | solution.py:272
  52.1 0.7 %collective-permute-done.17.got = bf16[64,768]{1,0:T(8,128)(2,1)S(1)} collective-permute-done((bf16[64,768]{1,0:T(8,128)(2,1)S(1)}, bf16[64,768]{1,0:T(8,128)(2,1)S(1)}, u32[]{:S(2)}, u32[]{:S(2)}) %collective-permute-start.17) | collective-permute-done | bytes 98336 | tf_op jit(solution)/shard_map/ppermute | solution.py:272
  52.9 0.5 collective-permute-start.14
  53.4 0.8 %place.2.refs_2_ = f32[256,768]{1,0:T(8,128)} custom-call(bf16[64,768]{1,0:T(8,128)(2,1)S(1)} %add.8.rest_0_.refs_0_, bf16[64,768]{1,0:T(8,128)(2,1)S(1)} %add.11.refs_1_), custom_call_target="tpu_custom_call" | custom-call | tf_op jit(solution)/shard_map/place/pallas_call | solution.py:339
  54.3 0.8 %place.3 = f32[256,768]{1,0:T(8,128)} custom-call(bf16[64,768]{1,0:T(8,128)(2,1)S(1)} %collective-permute-done.14.refs_0_, bf16[64,768]{1,0:T(8,128)(2,1)S(1)} %collective-permute-done.18.refs_1_, f32[256,768]{1,0:T(8,128)} %place.2.refs_2_), custom_call_target="tpu_custom_call", output_to_operand_aliasing={{}: (2, {})} | custom-call | tf_op jit(solution)/shard_map/place/pallas_call | solution.py:339
  (35 shorter events, 2.8 us)
Async XLA Ops:
  0.6 9.9 %copy-start.1 = (s32[256,8]{0,1:T(8,128)S(1)}, s32[256,8]{0,1:T(8,128)}, u32[]{:S(2)}) copy-start(s32[256,8]{0,1:T(8,128)} %param.11) | copy-start | bytes 24580
  2.7 11.2 %collective-permute-start.4 = (bf16[256,512]{1,0:T(8,128)(2,1)S(1)}, bf16[256,512]{1,0:T(8,128)(2,1)S(1)}, u32[]{:S(2)}, u32[]{:S(2)}) collective-permute-start(bf16[256,512]{1,0:T(8,128)(2,1)S(1)} %get-tuple-element.44), channel_id=1, source_target_pairs={{1,2},{3,4},{5,6},{7,8},{9,10},{11,12},{13,14},{15,0},{2,1},{4,3},... | collective-permute-start | bytes 786440 | tf_op jit(solution)/shard_map/ppermute | solution.py:366
  9.3 3.7 %collective-permute-start = (bf16[176,512]{1,0:T(8,128)(2,1)S(1)}, bf16[176,512]{1,0:T(8,128)(2,1)S(1)}, u32[]{:S(2)}, u32[]{:S(2)}) collective-permute-start(bf16[176,512]{1,0:T(8,128)(2,1)S(1)} %get-tuple-element.39), channel_id=1, source_target_pairs={{0,1},{1,0},{2,3},{3,2},{4,5},{5,4},{6,7},{7,6},{8,9},{9,8},{10,11... | collective-permute-start | bytes 540680 | tf_op jit(solution)/shard_map/ppermute | solution.py:272
  9.4 3.7 %collective-permute-start.1 = (bf16[176,512]{1,0:T(8,128)(2,1)S(1)}, bf16[176,512]{1,0:T(8,128)(2,1)S(1)}, u32[]{:S(2)}, u32[]{:S(2)}) collective-permute-start(bf16[176,512]{1,0:T(8,128)(2,1)S(1)} %get-tuple-element.40), channel_id=1, source_target_pairs={{0,1},{1,0},{2,3},{3,2},{4,5},{5,4},{6,7},{7,6},{8,9},{9,8},{10,11... | collective-permute-start | bytes 540680 | tf_op jit(solution)/shard_map/ppermute | solution.py:272
  9.9 3.2 %collective-permute-start.2 = (bf16[160,512]{1,0:T(8,128)(2,1)S(1)}, bf16[160,512]{1,0:T(8,128)(2,1)S(1)}, u32[]{:S(2)}, u32[]{:S(2)}) collective-permute-start(bf16[160,512]{1,0:T(8,128)(2,1)S(1)} %get-tuple-element.41), channel_id=1, source_target_pairs={{0,1},{1,0},{2,3},{3,2},{4,5},{5,4},{6,7},{7,6},{8,9},{9,8},{10,11... | collective-permute-start | bytes 491528 | tf_op jit(solution)/shard_map/ppermute | solution.py:272
  9.9 9.6 %collective-permute-start.3 = (bf16[256,512]{1,0:T(8,128)(2,1)S(1)}, bf16[256,512]{1,0:T(8,128)(2,1)S(1)}, u32[]{:S(2)}, u32[]{:S(2)}) collective-permute-start(bf16[256,512]{1,0:T(8,128)(2,1)S(1)} %get-tuple-element.43), channel_id=1, source_target_pairs={{1,2},{3,4},{5,6},{7,8},{9,10},{11,12},{13,14},{15,0},{2,1},{4,3},... | collective-permute-start | bytes 786440 | tf_op jit(solution)/shard_map/ppermute | solution.py:366
  13.0 0.8 %copy-start = (f32[2048]{0:T(1024)S(1)}, f32[2048]{0:T(1024)}, u32[]{:S(2)}) copy-start(f32[2048]{0:T(1024)} %param.9) | copy-start | bytes 24580
  14.5 14.8 %collective-permute-start.5 = (bf16[256,512]{1,0:T(8,128)(2,1)S(1)}, bf16[256,512]{1,0:T(8,128)(2,1)S(1)}, u32[]{:S(2)}, u32[]{:S(2)}) collective-permute-start(bf16[256,512]{1,0:T(8,128)(2,1)S(1)} %get-tuple-element.47), channel_id=1, source_target_pairs={{1,2},{3,4},{5,6},{7,8},{9,10},{11,12},{13,14},{15,0},{2,1},{4,3},... | collective-permute-start | bytes 786440 | tf_op jit(solution)/shard_map/ppermute | solution.py:366
  21.3 9.6 %collective-permute-start.9 = (bf16[256,512]{1,0:T(8,128)(2,1)S(1)}, bf16[256,512]{1,0:T(8,128)(2,1)S(1)}, u32[]{:S(2)}, u32[]{:S(2)}) collective-permute-start(bf16[256,512]{1,0:T(8,128)(2,1)S(1)} %get-tuple-element.52), channel_id=1, source_target_pairs={{1,2},{3,4},{5,6},{7,8},{9,10},{11,12},{13,14},{15,0},{2,1},{4,3},... | collective-permute-start | bytes 786440 | tf_op jit(solution)/shard_map/ppermute | solution.py:366
  22.2 7.5 %collective-permute-start.6 = (bf16[176,512]{1,0:T(8,128)(2,1)S(1)}, bf16[176,512]{1,0:T(8,128)(2,1)S(1)}, u32[]{:S(2)}, u32[]{:S(2)}) collective-permute-start(bf16[176,512]{1,0:T(8,128)(2,1)S(1)} %get-tuple-element.48), channel_id=1, source_target_pairs={{0,1},{1,0},{2,3},{3,2},{4,5},{5,4},{6,7},{7,6},{8,9},{9,8},{10,11... | collective-permute-start | bytes 540680 | tf_op jit(solution)/shard_map/ppermute | solution.py:272
  27.8 1.9 %collective-permute-start.7 = (bf16[176,512]{1,0:T(8,128)(2,1)S(1)}, bf16[176,512]{1,0:T(8,128)(2,1)S(1)}, u32[]{:S(2)}, u32[]{:S(2)}) collective-permute-start(bf16[176,512]{1,0:T(8,128)(2,1)S(1)} %get-tuple-element.49), channel_id=1, source_target_pairs={{0,1},{1,0},{2,3},{3,2},{4,5},{5,4},{6,7},{7,6},{8,9},{9,8},{10,11... | collective-permute-start | bytes 540680 | tf_op jit(solution)/shard_map/ppermute | solution.py:272
  27.9 1.8 %collective-permute-start.8 = (bf16[160,512]{1,0:T(8,128)(2,1)S(1)}, bf16[160,512]{1,0:T(8,128)(2,1)S(1)}, u32[]{:S(2)}, u32[]{:S(2)}) collective-permute-start(bf16[160,512]{1,0:T(8,128)(2,1)S(1)} %get-tuple-element.50), channel_id=1, source_target_pairs={{0,1},{1,0},{2,3},{3,2},{4,5},{5,4},{6,7},{7,6},{8,9},{9,8},{10,11... | collective-permute-start | bytes 491528 | tf_op jit(solution)/shard_map/ppermute | solution.py:272
  31.2 2.7 %collective-permute-start.10 = (bf16[128,768]{1,0:T(8,128)(2,1)S(1)}, bf16[128,768]{1,0:T(8,128)(2,1)S(1)}, u32[]{:S(2)}, u32[]{:S(2)}) collective-permute-start(bf16[128,768]{1,0:T(8,128)(2,1)S(1)} %query_end.3), channel_id=1, source_target_pairs={{0,1},{1,0},{2,3},{3,2},{4,5},{5,4},{6,7},{7,6},{8,9},{9,8},{10,11... | collective-permute-start | bytes 589832 | tf_op jit(solution)/shard_map/ppermute | solution.py:272
  34.0 5.1 %collective-permute-start.11 = (bf16[64,768]{1,0:T(8,128)(2,1)S(1)}, bf16[64,768]{1,0:T(8,128)(2,1)S(1)}, u32[]{:S(2)}, u32[]{:S(2)}) collective-permute-start(bf16[64,768]{1,0:T(8,128)(2,1)S(1)} %get-tuple-element.61.held), channel_id=1, source_target_pairs={{0,2},{1,3},{2,0},{3,1},{4,6},{5,7},{6,4},{7,5},{8,10},{9,11},{10,... | collective-permute-start | bytes 294920 | tf_op jit(solution)/shard_map/ppermute | solution.py:272
  34.5 7.2 %collective-permute-start.15 = (bf16[64,768]{1,0:T(8,128)(2,1)S(1)}, bf16[64,768]{1,0:T(8,128)(2,1)S(1)}, u32[]{:S(2)}, u32[]{:S(2)}) collective-permute-start(bf16[64,768]{1,0:T(8,128)(2,1)S(1)} %get-tuple-element.65.held), channel_id=1, source_target_pairs={{0,8},{1,9},{2,10},{3,11},{4,12},{5,13},{6,14},{7,15},{8,0},{9,1},... | collective-permute-start | bytes 294920 | tf_op jit(solution)/shard_map/ppermute | solution.py:272
  39.1 5.3 %collective-permute-start.12 = (bf16[64,768]{1,0:T(8,128)(2,1)S(1)}, bf16[64,768]{1,0:T(8,128)(2,1)S(1)}, u32[]{:S(2)}, u32[]{:S(2)}) collective-permute-start(bf16[64,768]{1,0:T(8,128)(2,1)S(1)} %add.6.held), channel_id=1, source_target_pairs={{0,4},{1,5},{2,6},{3,7},{4,0},{5,1},{6,2},{7,3},{8,12},{9,13},{10,... | collective-permute-start | bytes 294920 | tf_op jit(solution)/shard_map/ppermute | solution.py:272
  41.8 4.7 %collective-permute-start.16 = (bf16[64,768]{1,0:T(8,128)(2,1)S(1)}, bf16[64,768]{1,0:T(8,128)(2,1)S(1)}, u32[]{:S(2)}, u32[]{:S(2)}) collective-permute-start(bf16[64,768]{1,0:T(8,128)(2,1)S(1)} %add.9.held), channel_id=1, source_target_pairs={{0,2},{1,3},{2,0},{3,1},{4,6},{5,7},{6,4},{7,5},{8,10},{9,11},{10,... | collective-permute-start | bytes 294920 | tf_op jit(solution)/shard_map/ppermute | solution.py:272
  44.5 7.5 %collective-permute-start.13 = (bf16[64,768]{1,0:T(8,128)(2,1)S(1)}, bf16[64,768]{1,0:T(8,128)(2,1)S(1)}, u32[]{:S(2)}, u32[]{:S(2)}) collective-permute-start(bf16[64,768]{1,0:T(8,128)(2,1)S(1)} %add.7.held), channel_id=1, source_target_pairs={{0,8},{1,9},{2,10},{3,11},{4,12},{5,13},{6,14},{7,15},{8,0},{9,1},... | collective-permute-start | bytes 294920 | tf_op jit(solution)/shard_map/ppermute | solution.py:272
  46.5 6.2 %collective-permute-start.17 = (bf16[64,768]{1,0:T(8,128)(2,1)S(1)}, bf16[64,768]{1,0:T(8,128)(2,1)S(1)}, u32[]{:S(2)}, u32[]{:S(2)}) collective-permute-start(bf16[64,768]{1,0:T(8,128)(2,1)S(1)} %add.10.held), channel_id=1, source_target_pairs={{0,4},{1,5},{2,6},{3,7},{4,0},{5,1},{6,2},{7,3},{8,12},{9,13},{10,... | collective-permute-start | bytes 294920 | tf_op jit(solution)/shard_map/ppermute | solution.py:272
  52.8 1.4 %collective-permute-start.18 = (bf16[64,768]{1,0:T(8,128)(2,1)S(1)}, bf16[64,768]{1,0:T(8,128)(2,1)S(1)}, u32[]{:S(2)}, u32[]{:S(2)}) collective-permute-start(bf16[64,768]{1,0:T(8,128)(2,1)S(1)} %add.11.refs_1_), channel_id=1, source_target_pairs={{0,1},{1,0},{2,3},{3,2},{4,5},{5,4},{6,7},{7,6},{8,9},{9,8},{10,11... | collective-permute-start | bytes 294920 | tf_op jit(solution)/shard_map/ppermute | solution.py:272
  52.9 1.4 %collective-permute-start.14 = (bf16[64,768]{1,0:T(8,128)(2,1)S(1)}, bf16[64,768]{1,0:T(8,128)(2,1)S(1)}, u32[]{:S(2)}, u32[]{:S(2)}) collective-permute-start(bf16[64,768]{1,0:T(8,128)(2,1)S(1)} %add.8.rest_0_.refs_0_), channel_id=1, source_target_pairs={{0,1},{1,0},{2,3},{3,2},{4,5},{5,4},{6,7},{7,6},{8,9},{9,8},{10,11... | collective-permute-start | bytes 294920 | tf_op jit(solution)/shard_map/ppermute | solution.py:272

commit v21 on v17

--- a/solution.py
+++ b/solution.py
@@ -291,19 +291,21 @@
     rest[-1][...] = ((held[...].astype(F32) + got[...].astype(F32)) * scale).astype(BF16)
 
 
-def place_kernel(*refs, places):
-    out, wide, sem = refs[-3:]
-    rows = refs[0].shape[0]
+def end_kernel(held, got, before, out, *, scale):
+    rows = held.shape[0]
+    out[:rows, :] = before[...]
+    out[rows:, :] = ((held[...].astype(F32) + got[...].astype(F32)) * scale).astype(BF16)
+
+
+def place_kernel(held, *rest, own):
+    out, wide, sem = rest[-3:]
+    rows = held.shape[0]
     core = lax.axis_index(AXIS) % 2
-    copies = []
-    for k, (chain, own) in enumerate(places):
-        wide[k] = refs[k][...].astype(F32)
-        half = core if own else 1 - core
-        begin = pl.multiple_of((2 * half + chain) * rows, rows)
-        copies.append(pltpu.make_async_copy(wide.at[k], out.at[pl.ds(begin, rows), :], sem.at[k]))
-        copies[-1].start()
-    for copy in copies:
-        copy.wait()
+    half = core if own else 1 - core
+    wide[...] = held[...].astype(F32)
+    copy = pltpu.make_async_copy(wide, out.at[pl.ds(pl.multiple_of(half * rows, rows), rows), :], sem)
+    copy.start()
+    copy.wait()
 
 
 def sum_queries(kept, sent, beside, scale):
@@ -324,7 +326,7 @@
     for k in range(len(bits)):
         last = k == len(bits) - 1
         got = [exchange(value, order[k]) for value, order in zip(held, orders)]
-        for chain in range(2):
+        for chain in range(2 - last):
             after = beside[k : k + 1] if chain == 0 else []
             held[chain] = call(
                 functools.partial(add_kernel, scale=scale if last else 1.0),
@@ -333,24 +335,27 @@
                 piece,
                 flops=2 * 10**8 if last else 0,
             )(held[chain], got[chain], *after)
-    swapped = [exchange(value, 1) for value in held]
-
-    def place(values, places, *begun):
+    mine = call(
+        functools.partial(end_kernel, scale=scale),
+        "end",
+        [VMEM] * 3,
+        in_vmem((rows, width), BF16),
+        flops=2 * 10**8,
+    )(held[1], got[1], held[0])
+    other = exchange(mine, 1)
+
+    def place(half, own, *begun):
         return call(
-            functools.partial(place_kernel, places=places),
+            functools.partial(place_kernel, own=own),
             "place",
-            [VMEM] * len(values) + [ANY] * len(begun),
+            [VMEM] + [ANY] * len(begun),
             jax.ShapeDtypeStruct((2 * rows, width), F32),
             out_specs=ANY,
-            scratch=[
-                pltpu.VMEM((len(values), rows // 2, width), F32),
-                pltpu.SemaphoreType.DMA((len(values),)),
-            ],
-            aliases={len(values): 0} if begun else None,
-        )(*values, *begun)
-
-    early = place([held[0], held[1], swapped[0]], [(0, True), (1, True), (0, False)])
-    return place([swapped[1]], [(1, False)], early)
+            scratch=[pltpu.VMEM((rows, width), F32), pltpu.SemaphoreType.DMA],
+            aliases={1: 0} if begun else None,
+        )(half, *begun)
+
+    return place(other, False, place(mine, True))
 
 
 def per_device(embeddings, edge_tiles, neighbour, propensity, queries, positives):

time: 55.2 us -> 54.8 us (level); the launches traced: 54.4 us -> 55 us
  waiting for transfers between devices: 7.66 us -> 11.2 us
  starting transfers between devices: 27.4 us -> 24.3 us
    ppermute x15 -> x14, waiting for transfers between devices: 4.51 us -> 11.2 us  [exchange(): return lax.ppermute(value, AXIS, [(i, i ^ mask) for i in range(count)])]
    ppermute x15 -> x14, starting transfers between devices: 16.5 us -> 12.9 us  [exchange(): return lax.ppermute(value, AXIS, [(i, i ^ mask) for i in range(count)])]
    ppermute x4, waiting for transfers between devices: 3.15 us -> 0.01 us  [off_swap(): return lax.ppermute(value, AXIS, off_route)]
    pallas_call x2 -> x3, Pallas kernels: 1.55 us -> 1.6 us  [the longest x2 1.56 us: place(): call(functools.partial(place_kernel, own=own), 'place', [VMEM] + [ANY] *...]
  transfers between devices with their start and end apart: 19 -> 18, of which waited for: 8 -> 7; matrix products, arithmetic and copies ran while one was open for 0% -> 0% of each run, Pallas kernels for 28% -> 28%
where the time goes in v21:
time: 54.8 us; the launch traced here: 55 us
  starting transfers between devices  24.3 us (44%)
  Pallas kernels  18.6 us (34%)
  waiting for transfers between devices  11.2 us (20%)
  between operations  0.94 us (2%)
    ppermute x14, starting transfers between devices, exchange(): return lax.ppermute(value, AXIS, [(i, i ^ mask) for i in range(count)])  12.9 us
    ppermute x4, starting transfers between devices, off_swap(): return lax.ppermute(value, AXIS, off_route)  11.4 us
    ppermute x14, waiting for transfers between devices, exchange(): return lax.ppermute(value, AXIS, [(i, i ^ mask) for i in range(count)])  11.2 us
    pallas_call x4, Pallas kernels, embed(): call(functools.partial(embed_kernel, blocks=blocks, turn=turn, scale=1.0...  4.66 us
    pallas_call x1, Pallas kernels, per_device(): call(hits_kernel, 'hits', [VMEM, HBM], [in_vmem(full, BF16), in_vmem(edge...  2.45 us
    pallas_call x2, Pallas kernels, signal_of(): call(functools.partial(signal_kernel, slot=slot), 'signal', [SMEM] + [VME...  2.41 us
    pallas_call x1, Pallas kernels, per_device(): call(functools.partial(project_kernel, scale=scale), 'project', [HBM] * 3...  2.02 us
    pallas_call x2, Pallas kernels, place(): call(functools.partial(place_kernel, own=own), 'place', [VMEM] + [ANY] *...  1.56 us
  transfers between devices with their start and end apart: 18, of which 7 were waited for; matrix products, arithmetic and copies ran while one was open for 0% of the time, Pallas kernels for 28%

profile of v21, /device:TPU:0, one launch (start us, length us, event | category | flops | bytes accessed | tf_op | source)
XLA Modules:
  0.0 55.0 jit_solution(17265883600176667047)
XLA Ops:
  0.6 2.0 %project.1 = (bf16[256,512]{1,0:T(8,128)(2,1)S(1)}, bf16[256,768]{1,0:T(8,128)(2,1)S(1)}, bf16[2048,768]{1,0:T(8,128)(2,1)S(1)}, s32[2,64]{1,0:T(2,128)S(4)}) custom-call(s32[2,64]{1,0:T(2,128)} %bitcast.6, bf16[256,768]{1,0:T(8,128)(2,1)} %queries.1, bf16[2048,768]{1,0:T(8,128)(2,1)} %embeddings.1), custom_call_target="tpu_custom_call" | custom-call | tf_op jit(solution)/shard_map/project/pallas_call | solution.py:383
  2.7 5.7 %collective-permute-start.4 = (bf16[256,512]{1,0:T(8,128)(2,1)S(1)}, bf16[256,512]{1,0:T(8,128)(2,1)S(1)}, u32[]{:S(2)}, u32[]{:S(2)}) collective-permute-start(bf16[256,512]{1,0:T(8,128)(2,1)S(1)} %get-tuple-element.44), channel_id=1, source_target_pairs={{1,2},{3,4},{5,6},{7,8},{9,10},{11,12},{13,14},{15,0},{2,1},{4,3},... | collective-permute-start | bytes 786440 | tf_op jit(solution)/shard_map/ppermute | solution.py:371
  8.4 1.1 %own.1 = (f32[4,256,512]{2,1,0:T(8,128)S(1)}, bf16[256,512]{1,0:T(8,128)(2,1)S(1)}, bf16[176,512]{1,0:T(8,128)(2,1)S(1)}, bf16[176,512]{1,0:T(8,128)(2,1)S(1)}, bf16[160,512]{1,0:T(8,128)(2,1)S(1)}) custom-call(s32[2,64]{1,0:T(2,128)S(4)} %get-tuple-element.34.lists, bf16[256,768]{1,0:T(8,128)(2,1)S(1)} %get-tuple-element.35.queries, ...), custom_call_target="tpu_custom_call" | custom-call | tf_op jit(solution)/shard_map/own/pallas_call | solution.py:397
  9.5 0.5 collective-permute-start.1
  10.1 0.4 collective-permute-start.3
  10.6 2.4 %hits.1 = (bf16[4,256,512]{2,1,0:T(8,128)(2,1)S(1)}, bf16[4,2,512,512]{3,2,1,0:T(8,128)(2,1)S(1)}) custom-call(s32[8,256]{1,0:T(8,128)S(1)} %bitcast.5, bf16[4,2,512,512]{3,2,1,0:T(8,128)(2,1)} %tiles.1), custom_call_target="tpu_custom_call" | custom-call | tf_op jit(solution)/shard_map/hits/pallas_call | solution.py:404
  13.1 0.8 %base.1 = f32[4,256,512]{2,1,0:T(8,128)S(1)} custom-call(s32[2,64]{1,0:T(2,128)S(4)} %get-tuple-element.34.lists, f32[4,256,512]{2,1,0:T(8,128)S(1)} %get-tuple-element.37.own, bf16[4,2,512,512]{3,2,1,0:T(8,128)(2,1)S(1)} %get-tuple-element.38.tiles, bf16[176,512]{1,0:T(8,128)(2,1)S(1)} %collective-permute-done.rest_0_, ...), custom_call_target="tpu_custom_call" | custom-call | tf_op jit(solution)/shard_map/base/pallas_call | solution.py:412
  13.8 0.6 %signal.2 = (bf16[4,256,512]{2,1,0:T(8,128)(2,1)S(1)}, bf16[256,512]{1,0:T(8,128)(2,1)S(1)}) custom-call(s32[2,64]{1,0:T(2,128)S(4)} %get-tuple-element.34.lists, f32[4,256,512]{2,1,0:T(8,128)S(1)} %base.1, bf16[4,256,512]{2,1,0:T(8,128)(2,1)S(1)} %get-tuple-element.42.hits, f32[1,2048]{1,0:T(1,128)S(1)} %bitcast.3, ...), custom_call_target="tpu_custom_call" | custom-call | flops 2000000000 | tf_op jit(solution)/shard_map/signal/pallas_call | solution.py:422
  14.5 5.2 %collective-permute-start.5 = (bf16[256,512]{1,0:T(8,128)(2,1)S(1)}, bf16[256,512]{1,0:T(8,128)(2,1)S(1)}, u32[]{:S(2)}, u32[]{:S(2)}) collective-permute-start(bf16[256,512]{1,0:T(8,128)(2,1)S(1)} %get-tuple-element.47), channel_id=1, source_target_pairs={{1,2},{3,4},{5,6},{7,8},{9,10},{11,12},{13,14},{15,0},{2,1},{4,3},... | collective-permute-start | bytes 786440 | tf_op jit(solution)/shard_map/ppermute | solution.py:371
  19.7 1.8 %signal.3 = (bf16[4,256,512]{2,1,0:T(8,128)(2,1)S(1)}, bf16[256,512]{1,0:T(8,128)(2,1)S(1)}) custom-call(s32[2,64]{1,0:T(2,128)S(4)} %get-tuple-element.34.lists, f32[4,256,512]{2,1,0:T(8,128)S(1)} %base.1, bf16[4,256,512]{2,1,0:T(8,128)(2,1)S(1)} %get-tuple-element.42.hits, f32[1,2048]{1,0:T(1,128)S(1)} %bitcast.4, ...), custom_call_target="tpu_custom_call", output_to_operand_aliasing={{0}: (6, {})} | custom-call | tf_op jit(solution)/shard_map/signal/pallas_call | solution.py:422
  21.6 0.8 %push.1 = (bf16[176,512]{1,0:T(8,128)(2,1)S(1)}, bf16[176,512]{1,0:T(8,128)(2,1)S(1)}, bf16[160,512]{1,0:T(8,128)(2,1)S(1)}) custom-call(s32[2,64]{1,0:T(2,128)S(4)} %get-tuple-element.34.lists, bf16[4,256,512]{2,1,0:T(8,128)(2,1)S(1)} %get-tuple-element.46.signal, bf16[4,2,512,512]{3,2,1,0:T(8,128)(2,1)S(1)} %get-tuple-element.38.tiles), custom_call_target="tpu_custom_call" | custom-call | tf_op jit(solution)/shard_map/push/pallas_call | solution.py:436
  22.4 6.0 %collective-permute-start.6 = (bf16[176,512]{1,0:T(8,128)(2,1)S(1)}, bf16[176,512]{1,0:T(8,128)(2,1)S(1)}, u32[]{:S(2)}, u32[]{:S(2)}) collective-permute-start(bf16[176,512]{1,0:T(8,128)(2,1)S(1)} %get-tuple-element.48), channel_id=1, source_target_pairs={{0,1},{1,0},{2,3},{3,2},{4,5},{5,4},{6,7},{7,6},{8,9},{9,8},{10,11... | collective-permute-start | bytes 540680 | tf_op jit(solution)/shard_map/ppermute | solution.py:272
  28.9 1.0 %query.1.part = f32[256,768]{1,0:T(8,128)S(1)} custom-call(bf16[4,256,512]{2,1,0:T(8,128)(2,1)S(1)} %get-tuple-element.46.signal, bf16[2048,768]{1,0:T(8,128)(2,1)S(1)} %get-tuple-element.36.embeddings), custom_call_target="tpu_custom_call" | custom-call | tf_op jit(solution)/shard_map/query/pallas_call | solution.py:446
  30.3 0.6 %query_on.1 = (f32[256,768]{1,0:T(8,128)S(1)}, bf16[2,256,512]{2,1,0:T(8,128)(2,1)S(1)}) custom-call(s32[2,64]{1,0:T(2,128)S(4)} %get-tuple-element.34.lists, f32[256,768]{1,0:T(8,128)S(1)} %query_half.1.part, bf16[2048,768]{1,0:T(8,128)(2,1)S(1)} %get-tuple-element.36.embeddings, bf16[176,512]{1,0:T(8,128)(2,1)S(1)} %collective-permute-done.6.rest_0_, ...), custom_call_target="tpu_custom_call" | custom-call | tf_op jit(solution)/shard_map/query_on/pallas_call | solution.py:454
  31.0 0.5 embed.4
  31.8 1.2 %collective-permute-start.10 = (bf16[128,768]{1,0:T(8,128)(2,1)S(1)}, bf16[128,768]{1,0:T(8,128)(2,1)S(1)}, u32[]{:S(2)}, u32[]{:S(2)}) collective-permute-start(bf16[128,768]{1,0:T(8,128)(2,1)S(1)} %query_end.3), channel_id=1, source_target_pairs={{0,1},{1,0},{2,3},{3,2},{4,5},{5,4},{6,7},{7,6},{8,9},{9,8},{10,11... | collective-permute-start | bytes 589832 | tf_op jit(solution)/shard_map/ppermute | solution.py:272
  33.3 0.8 %collective-permute-done.10.got = bf16[128,768]{1,0:T(8,128)(2,1)S(1)} collective-permute-done((bf16[128,768]{1,0:T(8,128)(2,1)S(1)}, bf16[128,768]{1,0:T(8,128)(2,1)S(1)}, u32[]{:S(2)}, u32[]{:S(2)}) %collective-permute-start.10) | collective-permute-done | bytes 196640 | tf_op jit(solution)/shard_map/ppermute | solution.py:272
  34.1 1.0 %collective-permute-start.14 = (bf16[64,768]{1,0:T(8,128)(2,1)S(1)}, bf16[64,768]{1,0:T(8,128)(2,1)S(1)}, u32[]{:S(2)}, u32[]{:S(2)}) collective-permute-start(bf16[64,768]{1,0:T(8,128)(2,1)S(1)} %get-tuple-element.62.held), channel_id=1, source_target_pairs={{0,2},{1,3},{2,0},{3,1},{4,6},{5,7},{6,4},{7,5},{8,10},{9,11},{10,... | collective-permute-start | bytes 294920 | tf_op jit(solution)/shard_map/ppermute | solution.py:272
  35.1 1.4 %collective-permute-start.11 = (bf16[64,768]{1,0:T(8,128)(2,1)S(1)}, bf16[64,768]{1,0:T(8,128)(2,1)S(1)}, u32[]{:S(2)}, u32[]{:S(2)}) collective-permute-start(bf16[64,768]{1,0:T(8,128)(2,1)S(1)} %get-tuple-element.61.held), channel_id=1, source_target_pairs={{0,8},{1,9},{2,10},{3,11},{4,12},{5,13},{6,14},{7,15},{8,0},{9,1},... | collective-permute-start | bytes 294920 | tf_op jit(solution)/shard_map/ppermute | solution.py:272
  36.5 0.9 %embed.5 = (bf16[2048,768]{1,0:T(8,128)(2,1)}, bf16[512,768]{1,0:T(8,128)(2,1)S(1)}, f32[8,128]{1,0:T(8,128)S(1)}) custom-call(s32[2,64]{1,0:T(2,128)S(4)} %get-tuple-element.34.lists, bf16[4,256,512]{2,1,0:T(8,128)(2,1)S(1)} %get-tuple-element.46.signal, bf16[2,256,512]{2,1,0:T(8,128)(2,1)S(1)} %get-tuple-element.51.on, ...), custom_call_target="tpu_custom_call" | custom-call | tf_op jit(solution)/shard_map/embed/pallas_call | solution.py:462
  37.4 1.8 %collective-permute-done.14.got = bf16[64,768]{1,0:T(8,128)(2,1)S(1)} collective-permute-done((bf16[64,768]{1,0:T(8,128)(2,1)S(1)}, bf16[64,768]{1,0:T(8,128)(2,1)S(1)}, u32[]{:S(2)}, u32[]{:S(2)}) %collective-permute-start.14) | collective-permute-done | bytes 98336 | tf_op jit(solution)/shard_map/ppermute | solution.py:272
  39.3 0.5 collective-permute-start.15
  39.8 2.9 %collective-permute-done.11.got = bf16[64,768]{1,0:T(8,128)(2,1)S(1)} collective-permute-done((bf16[64,768]{1,0:T(8,128)(2,1)S(1)}, bf16[64,768]{1,0:T(8,128)(2,1)S(1)}, u32[]{:S(2)}, u32[]{:S(2)}) %collective-permute-start.11) | collective-permute-done | bytes 98336 | tf_op jit(solution)/shard_map/ppermute | solution.py:272
  42.8 1.3 %collective-permute-start.12 = (bf16[64,768]{1,0:T(8,128)(2,1)S(1)}, bf16[64,768]{1,0:T(8,128)(2,1)S(1)}, u32[]{:S(2)}, u32[]{:S(2)}) collective-permute-start(bf16[64,768]{1,0:T(8,128)(2,1)S(1)} %add.5.held), channel_id=1, source_target_pairs={{0,2},{1,3},{2,0},{3,1},{4,6},{5,7},{6,4},{7,5},{8,10},{9,11},{10,... | collective-permute-start | bytes 294920 | tf_op jit(solution)/shard_map/ppermute | solution.py:272
  44.1 0.9 %embed.6 = (bf16[2048,768]{1,0:T(8,128)(2,1)}, bf16[512,768]{1,0:T(8,128)(2,1)S(1)}, f32[8,128]{1,0:T(8,128)S(1)}) custom-call(s32[2,64]{1,0:T(2,128)S(4)} %get-tuple-element.34.lists, bf16[4,256,512]{2,1,0:T(8,128)(2,1)S(1)} %get-tuple-element.46.signal, bf16[2,256,512]{2,1,0:T(8,128)(2,1)S(1)} %get-tuple-element.51.on, ...), custom_call_target="tpu_custom_call", output_to_operand_aliasing={{0}: (6, {})} | custom-call | tf_op jit(solution)/shard_map/embed/pallas_call | solution.py:462
  45.2 2.3 %collective-permute-done.12.got = bf16[64,768]{1,0:T(8,128)(2,1)S(1)} collective-permute-done((bf16[64,768]{1,0:T(8,128)(2,1)S(1)}, bf16[64,768]{1,0:T(8,128)(2,1)S(1)}, u32[]{:S(2)}, u32[]{:S(2)}) %collective-permute-start.12) | collective-permute-done | bytes 98336 | tf_op jit(solution)/shard_map/ppermute | solution.py:272
  47.6 2.4 %embed.7 = (bf16[2048,768]{1,0:T(8,128)(2,1)}, bf16[512,768]{1,0:T(8,128)(2,1)}, f32[8,128]{1,0:T(8,128)S(1)}) custom-call(s32[2,64]{1,0:T(2,128)S(4)} %get-tuple-element.34.lists, bf16[4,256,512]{2,1,0:T(8,128)(2,1)S(1)} %get-tuple-element.46.signal, bf16[2,256,512]{2,1,0:T(8,128)(2,1)S(1)} %get-tuple-element.51.on, ...), custom_call_target="tpu_custom_call", output_to_operand_aliasing={{0}: (7, {})} | custom-call | tf_op jit(solution)/shard_map/embed/pallas_call | solution.py:462
  50.0 1.7 %collective-permute-done.16.got = bf16[64,768]{1,0:T(8,128)(2,1)S(1)} collective-permute-done((bf16[64,768]{1,0:T(8,128)(2,1)S(1)}, bf16[64,768]{1,0:T(8,128)(2,1)S(1)}, u32[]{:S(2)}, u32[]{:S(2)}) %collective-permute-start.16) | collective-permute-done | bytes 98336 | tf_op jit(solution)/shard_map/ppermute | solution.py:272
  51.7 1.0 %collective-permute-done.13.got = bf16[64,768]{1,0:T(8,128)(2,1)S(1)} collective-permute-done((bf16[64,768]{1,0:T(8,128)(2,1)S(1)}, bf16[64,768]{1,0:T(8,128)(2,1)S(1)}, u32[]{:S(2)}, u32[]{:S(2)}) %collective-permute-start.13) | collective-permute-done | bytes 98336 | tf_op jit(solution)/shard_map/ppermute | solution.py:272
  52.8 0.8 %place.2.rest_0_ = f32[256,768]{1,0:T(8,128)} custom-call(bf16[128,768]{1,0:T(8,128)(2,1)S(1)} %end.1.held), custom_call_target="tpu_custom_call" | custom-call | tf_op jit(solution)/shard_map/place/pallas_call | solution.py:348
  53.6 0.6 %collective-permute-done.17.held = bf16[128,768]{1,0:T(8,128)(2,1)S(1)} collective-permute-done((bf16[128,768]{1,0:T(8,128)(2,1)S(1)}, bf16[128,768]{1,0:T(8,128)(2,1)S(1)}, u32[]{:S(2)}, u32[]{:S(2)}) %collective-permute-start.17) | collective-permute-done | bytes 196640 | tf_op jit(solution)/shard_map/ppermute | solution.py:272
  54.2 0.8 %place.3 = f32[256,768]{1,0:T(8,128)} custom-call(bf16[128,768]{1,0:T(8,128)(2,1)S(1)} %collective-permute-done.17.held, f32[256,768]{1,0:T(8,128)} %place.2.rest_0_), custom_call_target="tpu_custom_call", output_to_operand_aliasing={{}: (1, {})} | custom-call | tf_op jit(solution)/shard_map/place/pallas_call | solution.py:348
  (33 shorter events, 2.2 us)
Async XLA Ops:
  0.6 9.9 %copy-start.1 = (s32[256,8]{0,1:T(8,128)S(1)}, s32[256,8]{0,1:T(8,128)}, u32[]{:S(2)}) copy-start(s32[256,8]{0,1:T(8,128)} %param.11) | copy-start | bytes 24580
  2.7 11.2 %collective-permute-start.4 = (bf16[256,512]{1,0:T(8,128)(2,1)S(1)}, bf16[256,512]{1,0:T(8,128)(2,1)S(1)}, u32[]{:S(2)}, u32[]{:S(2)}) collective-permute-start(bf16[256,512]{1,0:T(8,128)(2,1)S(1)} %get-tuple-element.44), channel_id=1, source_target_pairs={{1,2},{3,4},{5,6},{7,8},{9,10},{11,12},{13,14},{15,0},{2,1},{4,3},... | collective-permute-start | bytes 786440 | tf_op jit(solution)/shard_map/ppermute | solution.py:371
  9.5 3.6 %collective-permute-start = (bf16[176,512]{1,0:T(8,128)(2,1)S(1)}, bf16[176,512]{1,0:T(8,128)(2,1)S(1)}, u32[]{:S(2)}, u32[]{:S(2)}) collective-permute-start(bf16[176,512]{1,0:T(8,128)(2,1)S(1)} %get-tuple-element.39), channel_id=1, source_target_pairs={{0,1},{1,0},{2,3},{3,2},{4,5},{5,4},{6,7},{7,6},{8,9},{9,8},{10,11... | collective-permute-start | bytes 540680 | tf_op jit(solution)/shard_map/ppermute | solution.py:272
  9.5 3.5 %collective-permute-start.1 = (bf16[176,512]{1,0:T(8,128)(2,1)S(1)}, bf16[176,512]{1,0:T(8,128)(2,1)S(1)}, u32[]{:S(2)}, u32[]{:S(2)}) collective-permute-start(bf16[176,512]{1,0:T(8,128)(2,1)S(1)} %get-tuple-element.40), channel_id=1, source_target_pairs={{0,1},{1,0},{2,3},{3,2},{4,5},{5,4},{6,7},{7,6},{8,9},{9,8},{10,11... | collective-permute-start | bytes 540680 | tf_op jit(solution)/shard_map/ppermute | solution.py:272
  10.0 3.0 %collective-permute-start.2 = (bf16[160,512]{1,0:T(8,128)(2,1)S(1)}, bf16[160,512]{1,0:T(8,128)(2,1)S(1)}, u32[]{:S(2)}, u32[]{:S(2)}) collective-permute-start(bf16[160,512]{1,0:T(8,128)(2,1)S(1)} %get-tuple-element.41), channel_id=1, source_target_pairs={{0,1},{1,0},{2,3},{3,2},{4,5},{5,4},{6,7},{7,6},{8,9},{9,8},{10,11... | collective-permute-start | bytes 491528 | tf_op jit(solution)/shard_map/ppermute | solution.py:272
  10.1 9.6 %collective-permute-start.3 = (bf16[256,512]{1,0:T(8,128)(2,1)S(1)}, bf16[256,512]{1,0:T(8,128)(2,1)S(1)}, u32[]{:S(2)}, u32[]{:S(2)}) collective-permute-start(bf16[256,512]{1,0:T(8,128)(2,1)S(1)} %get-tuple-element.43), channel_id=1, source_target_pairs={{1,2},{3,4},{5,6},{7,8},{9,10},{11,12},{13,14},{15,0},{2,1},{4,3},... | collective-permute-start | bytes 786440 | tf_op jit(solution)/shard_map/ppermute | solution.py:371
  13.0 0.8 %copy-start = (f32[2048]{0:T(1024)S(1)}, f32[2048]{0:T(1024)}, u32[]{:S(2)}) copy-start(f32[2048]{0:T(1024)} %param.9) | copy-start | bytes 24580
  14.5 15.4 %collective-permute-start.5 = (bf16[256,512]{1,0:T(8,128)(2,1)S(1)}, bf16[256,512]{1,0:T(8,128)(2,1)S(1)}, u32[]{:S(2)}, u32[]{:S(2)}) collective-permute-start(bf16[256,512]{1,0:T(8,128)(2,1)S(1)} %get-tuple-element.47), channel_id=1, source_target_pairs={{1,2},{3,4},{5,6},{7,8},{9,10},{11,12},{13,14},{15,0},{2,1},{4,3},... | collective-permute-start | bytes 786440 | tf_op jit(solution)/shard_map/ppermute | solution.py:371
  21.5 10.0 %collective-permute-start.9 = (bf16[256,512]{1,0:T(8,128)(2,1)S(1)}, bf16[256,512]{1,0:T(8,128)(2,1)S(1)}, u32[]{:S(2)}, u32[]{:S(2)}) collective-permute-start(bf16[256,512]{1,0:T(8,128)(2,1)S(1)} %get-tuple-element.52), channel_id=1, source_target_pairs={{1,2},{3,4},{5,6},{7,8},{9,10},{11,12},{13,14},{15,0},{2,1},{4,3},... | collective-permute-start | bytes 786440 | tf_op jit(solution)/shard_map/ppermute | solution.py:371
  22.4 7.9 %collective-permute-start.6 = (bf16[176,512]{1,0:T(8,128)(2,1)S(1)}, bf16[176,512]{1,0:T(8,128)(2,1)S(1)}, u32[]{:S(2)}, u32[]{:S(2)}) collective-permute-start(bf16[176,512]{1,0:T(8,128)(2,1)S(1)} %get-tuple-element.48), channel_id=1, source_target_pairs={{0,1},{1,0},{2,3},{3,2},{4,5},{5,4},{6,7},{7,6},{8,9},{9,8},{10,11... | collective-permute-start | bytes 540680 | tf_op jit(solution)/shard_map/ppermute | solution.py:272
  28.4 1.9 %collective-permute-start.7 = (bf16[176,512]{1,0:T(8,128)(2,1)S(1)}, bf16[176,512]{1,0:T(8,128)(2,1)S(1)}, u32[]{:S(2)}, u32[]{:S(2)}) collective-permute-start(bf16[176,512]{1,0:T(8,128)(2,1)S(1)} %get-tuple-element.49), channel_id=1, source_target_pairs={{0,1},{1,0},{2,3},{3,2},{4,5},{5,4},{6,7},{7,6},{8,9},{9,8},{10,11... | collective-permute-start | bytes 540680 | tf_op jit(solution)/shard_map/ppermute | solution.py:272
  28.5 1.8 %collective-permute-start.8 = (bf16[160,512]{1,0:T(8,128)(2,1)S(1)}, bf16[160,512]{1,0:T(8,128)(2,1)S(1)}, u32[]{:S(2)}, u32[]{:S(2)}) collective-permute-start(bf16[160,512]{1,0:T(8,128)(2,1)S(1)} %get-tuple-element.50), channel_id=1, source_target_pairs={{0,1},{1,0},{2,3},{3,2},{4,5},{5,4},{6,7},{7,6},{8,9},{9,8},{10,11... | collective-permute-start | bytes 491528 | tf_op jit(solution)/shard_map/ppermute | solution.py:272
  31.8 2.3 %collective-permute-start.10 = (bf16[128,768]{1,0:T(8,128)(2,1)S(1)}, bf16[128,768]{1,0:T(8,128)(2,1)S(1)}, u32[]{:S(2)}, u32[]{:S(2)}) collective-permute-start(bf16[128,768]{1,0:T(8,128)(2,1)S(1)} %query_end.3), channel_id=1, source_target_pairs={{0,1},{1,0},{2,3},{3,2},{4,5},{5,4},{6,7},{7,6},{8,9},{9,8},{10,11... | collective-permute-start | bytes 589832 | tf_op jit(solution)/shard_map/ppermute | solution.py:272
  34.1 5.1 %collective-permute-start.14 = (bf16[64,768]{1,0:T(8,128)(2,1)S(1)}, bf16[64,768]{1,0:T(8,128)(2,1)S(1)}, u32[]{:S(2)}, u32[]{:S(2)}) collective-permute-start(bf16[64,768]{1,0:T(8,128)(2,1)S(1)} %get-tuple-element.62.held), channel_id=1, source_target_pairs={{0,2},{1,3},{2,0},{3,1},{4,6},{5,7},{6,4},{7,5},{8,10},{9,11},{10,... | collective-permute-start | bytes 294920 | tf_op jit(solution)/shard_map/ppermute | solution.py:272
  35.1 7.7 %collective-permute-start.11 = (bf16[64,768]{1,0:T(8,128)(2,1)S(1)}, bf16[64,768]{1,0:T(8,128)(2,1)S(1)}, u32[]{:S(2)}, u32[]{:S(2)}) collective-permute-start(bf16[64,768]{1,0:T(8,128)(2,1)S(1)} %get-tuple-element.61.held), channel_id=1, source_target_pairs={{0,8},{1,9},{2,10},{3,11},{4,12},{5,13},{6,14},{7,15},{8,0},{9,1},... | collective-permute-start | bytes 294920 | tf_op jit(solution)/shard_map/ppermute | solution.py:272
  39.3 5.7 %collective-permute-start.15 = (bf16[64,768]{1,0:T(8,128)(2,1)S(1)}, bf16[64,768]{1,0:T(8,128)(2,1)S(1)}, u32[]{:S(2)}, u32[]{:S(2)}) collective-permute-start(bf16[64,768]{1,0:T(8,128)(2,1)S(1)} %add.7.held), channel_id=1, source_target_pairs={{0,4},{1,5},{2,6},{3,7},{4,0},{5,1},{6,2},{7,3},{8,12},{9,13},{10,... | collective-permute-start | bytes 294920 | tf_op jit(solution)/shard_map/ppermute | solution.py:272
  42.8 4.7 %collective-permute-start.12 = (bf16[64,768]{1,0:T(8,128)(2,1)S(1)}, bf16[64,768]{1,0:T(8,128)(2,1)S(1)}, u32[]{:S(2)}, u32[]{:S(2)}) collective-permute-start(bf16[64,768]{1,0:T(8,128)(2,1)S(1)} %add.5.held), channel_id=1, source_target_pairs={{0,2},{1,3},{2,0},{3,1},{4,6},{5,7},{6,4},{7,5},{8,10},{9,11},{10,... | collective-permute-start | bytes 294920 | tf_op jit(solution)/shard_map/ppermute | solution.py:272
  45.1 6.6 %collective-permute-start.16 = (bf16[64,768]{1,0:T(8,128)(2,1)S(1)}, bf16[64,768]{1,0:T(8,128)(2,1)S(1)}, u32[]{:S(2)}, u32[]{:S(2)}) collective-permute-start(bf16[64,768]{1,0:T(8,128)(2,1)S(1)} %add.8.held), channel_id=1, source_target_pairs={{0,8},{1,9},{2,10},{3,11},{4,12},{5,13},{6,14},{7,15},{8,0},{9,1},... | collective-permute-start | bytes 294920 | tf_op jit(solution)/shard_map/ppermute | solution.py:272
  47.5 5.2 %collective-permute-start.13 = (bf16[64,768]{1,0:T(8,128)(2,1)S(1)}, bf16[64,768]{1,0:T(8,128)(2,1)S(1)}, u32[]{:S(2)}, u32[]{:S(2)}) collective-permute-start(bf16[64,768]{1,0:T(8,128)(2,1)S(1)} %add.6.held), channel_id=1, source_target_pairs={{0,4},{1,5},{2,6},{3,7},{4,0},{5,1},{6,2},{7,3},{8,12},{9,13},{10,... | collective-permute-start | bytes 294920 | tf_op jit(solution)/shard_map/ppermute | solution.py:272
  52.7 1.5 %collective-permute-start.17 = (bf16[128,768]{1,0:T(8,128)(2,1)S(1)}, bf16[128,768]{1,0:T(8,128)(2,1)S(1)}, u32[]{:S(2)}, u32[]{:S(2)}) collective-permute-start(bf16[128,768]{1,0:T(8,128)(2,1)S(1)} %end.1.held), channel_id=1, source_target_pairs={{0,1},{1,0},{2,3},{3,2},{4,5},{5,4},{6,7},{7,6},{8,9},{9,8},{10,11... | collective-permute-start | bytes 589832 | tf_op jit(solution)/shard_map/ppermute | solution.py:272

commit v22 on v20

--- a/solution.py
+++ b/solution.py
@@ -464,8 +464,10 @@
             aliases={len(values) - 1: 0} if turn > 1 else None,
         )(*values)
 
-    *outs, token = embed(0, [])
-    tokens = [token]
+    outs, tokens = [], []
+    for turn in range(blocks // 2):
+        *outs, token = embed(turn, outs)
+        tokens.append(token)
 
     def query_end(own, kind):
         return call(
@@ -473,14 +475,14 @@
             "query_end",
             [SMEM] + [VMEM] * 3 + [ANY],
             in_vmem((rows // 2, width), kind),
-        )(lists, part, back_b, embeddings, tokens[0])
+        )(lists, part, back_b, embeddings, tokens[blocks // 2 - 1])
 
     sent, kept = query_end(False, BF16), query_end(True, F32)
-    for turn in range(1, blocks):
+    for turn in range(blocks // 2, blocks):
         *outs, token = embed(turn, outs)
         tokens.append(token)
     grad_embed = outs[0]
-    grad_queries = sum_queries(kept, sent, tokens[1:], 1.0 / math.sqrt(labels_dev * count))
+    grad_queries = sum_queries(kept, sent, tokens[blocks // 2 :], 1.0 / math.sqrt(labels_dev * count))
     return (grad_embed, grad_queries)
 
 

time: 55.6 us -> 55.6 us (level); the launches traced: 55.1 us -> 56.1 us
  waiting for transfers between devices: 8.6 us -> 9.87 us
    ppermute x15, waiting for transfers between devices: 8.59 us -> 9.86 us  [exchange(): return lax.ppermute(value, AXIS, [(i, i ^ mask) for i in range(count)])]
    ppermute x15, starting transfers between devices: 15.9 us -> 15.3 us  [exchange(): return lax.ppermute(value, AXIS, [(i, i ^ mask) for i in range(count)])]
where the time goes in v22:
time: 55.6 us; the launch traced here: 56.1 us
  starting transfers between devices  26.7 us (48%)
  Pallas kernels  18.7 us (34%)
  waiting for transfers between devices  9.87 us (18%)
  between operations  0.92 us (2%)
    ppermute x15, starting transfers between devices, exchange(): return lax.ppermute(value, AXIS, [(i, i ^ mask) for i in range(count)])  15.3 us
    ppermute x4, starting transfers between devices, off_swap(): return lax.ppermute(value, AXIS, off_route)  11.4 us
    ppermute x15, waiting for transfers between devices, exchange(): return lax.ppermute(value, AXIS, [(i, i ^ mask) for i in range(count)])  9.86 us
    pallas_call x4, Pallas kernels, embed(): call(functools.partial(embed_kernel, blocks=blocks, turn=turn, scale=1.0...  4.8 us
    pallas_call x1, Pallas kernels, per_device(): call(hits_kernel, 'hits', [VMEM, HBM], [in_vmem(full, BF16), in_vmem(edge...  2.45 us
    pallas_call x2, Pallas kernels, signal_of(): call(functools.partial(signal_kernel, slot=slot), 'signal', [SMEM] + [VME...  2.42 us
    pallas_call x1, Pallas kernels, per_device(): call(functools.partial(project_kernel, scale=scale), 'project', [HBM] * 3...  2.02 us
    pallas_call x2, Pallas kernels, place(): call(functools.partial(place_kernel, places=places), 'place', [VMEM] * le...  1.54 us
  transfers between devices with their start and end apart: 19, of which 7 were waited for; matrix products, arithmetic and copies ran while one was open for 0% of the time, Pallas kernels for 28%

profile of v22, /device:TPU:0, one launch (start us, length us, event | category | flops | bytes accessed | tf_op | source)
XLA Modules:
  0.0 56.1 jit_solution(11282108428070610542)
XLA Ops:
  0.6 2.0 %project.1 = (bf16[256,512]{1,0:T(8,128)(2,1)S(1)}, bf16[256,768]{1,0:T(8,128)(2,1)S(1)}, bf16[2048,768]{1,0:T(8,128)(2,1)S(1)}, s32[2,64]{1,0:T(2,128)S(4)}) custom-call(s32[2,64]{1,0:T(2,128)} %bitcast.6, bf16[256,768]{1,0:T(8,128)(2,1)} %queries.1, bf16[2048,768]{1,0:T(8,128)(2,1)} %embeddings.1), custom_call_target="tpu_custom_call" | custom-call | tf_op jit(solution)/shard_map/project/pallas_call | solution.py:378
  2.7 5.5 %collective-permute-start.4 = (bf16[256,512]{1,0:T(8,128)(2,1)S(1)}, bf16[256,512]{1,0:T(8,128)(2,1)S(1)}, u32[]{:S(2)}, u32[]{:S(2)}) collective-permute-start(bf16[256,512]{1,0:T(8,128)(2,1)S(1)} %get-tuple-element.43), channel_id=1, source_target_pairs={{1,2},{3,4},{5,6},{7,8},{9,10},{11,12},{13,14},{15,0},{2,1},{4,3},... | collective-permute-start | bytes 786440 | tf_op jit(solution)/shard_map/ppermute | solution.py:366
  8.2 1.1 %own.1 = (f32[4,256,512]{2,1,0:T(8,128)S(1)}, bf16[256,512]{1,0:T(8,128)(2,1)S(1)}, bf16[176,512]{1,0:T(8,128)(2,1)S(1)}, bf16[176,512]{1,0:T(8,128)(2,1)S(1)}, bf16[160,512]{1,0:T(8,128)(2,1)S(1)}) custom-call(s32[2,64]{1,0:T(2,128)S(4)} %get-tuple-element.33.lists, bf16[256,768]{1,0:T(8,128)(2,1)S(1)} %get-tuple-element.34.queries, ...), custom_call_target="tpu_custom_call" | custom-call | tf_op jit(solution)/shard_map/own/pallas_call | solution.py:392
  9.4 0.5 collective-permute-start.1
  9.9 0.7 %collective-permute-start.3 = (bf16[256,512]{1,0:T(8,128)(2,1)S(1)}, bf16[256,512]{1,0:T(8,128)(2,1)S(1)}, u32[]{:S(2)}, u32[]{:S(2)}) collective-permute-start(bf16[256,512]{1,0:T(8,128)(2,1)S(1)} %get-tuple-element.42), channel_id=1, source_target_pairs={{1,2},{3,4},{5,6},{7,8},{9,10},{11,12},{13,14},{15,0},{2,1},{4,3},... | collective-permute-start | bytes 786440 | tf_op jit(solution)/shard_map/ppermute | solution.py:366
  10.7 2.4 %hits.1 = (bf16[4,256,512]{2,1,0:T(8,128)(2,1)S(1)}, bf16[4,2,512,512]{3,2,1,0:T(8,128)(2,1)S(1)}) custom-call(s32[8,256]{1,0:T(8,128)S(1)} %bitcast.5, bf16[4,2,512,512]{3,2,1,0:T(8,128)(2,1)} %tiles.1), custom_call_target="tpu_custom_call" | custom-call | tf_op jit(solution)/shard_map/hits/pallas_call | solution.py:399
  13.2 0.8 %base.1 = f32[4,256,512]{2,1,0:T(8,128)S(1)} custom-call(s32[2,64]{1,0:T(2,128)S(4)} %get-tuple-element.33.lists, f32[4,256,512]{2,1,0:T(8,128)S(1)} %get-tuple-element.36.own, bf16[4,2,512,512]{3,2,1,0:T(8,128)(2,1)S(1)} %get-tuple-element.37.tiles, bf16[176,512]{1,0:T(8,128)(2,1)S(1)} %collective-permute-done.rest_0_, ...), custom_call_target="tpu_custom_call" | custom-call | tf_op jit(solution)/shard_map/base/pallas_call | solution.py:407
  13.9 1.8 %signal.2 = (bf16[4,256,512]{2,1,0:T(8,128)(2,1)S(1)}, bf16[256,512]{1,0:T(8,128)(2,1)S(1)}) custom-call(s32[2,64]{1,0:T(2,128)S(4)} %get-tuple-element.33.lists, f32[4,256,512]{2,1,0:T(8,128)S(1)} %base.1, bf16[4,256,512]{2,1,0:T(8,128)(2,1)S(1)} %get-tuple-element.41.hits, f32[1,2048]{1,0:T(1,128)S(1)} %bitcast.3, ...), custom_call_target="tpu_custom_call" | custom-call | flops 2000000000 | tf_op jit(solution)/shard_map/signal/pallas_call | solution.py:417
  15.7 3.2 %collective-permute-start.5 = (bf16[256,512]{1,0:T(8,128)(2,1)S(1)}, bf16[256,512]{1,0:T(8,128)(2,1)S(1)}, u32[]{:S(2)}, u32[]{:S(2)}) collective-permute-start(bf16[256,512]{1,0:T(8,128)(2,1)S(1)} %get-tuple-element.46), channel_id=1, source_target_pairs={{1,2},{3,4},{5,6},{7,8},{9,10},{11,12},{13,14},{15,0},{2,1},{4,3},... | collective-permute-start | bytes 786440 | tf_op jit(solution)/shard_map/ppermute | solution.py:366
  19.0 0.6 %signal.3 = (bf16[4,256,512]{2,1,0:T(8,128)(2,1)S(1)}, bf16[256,512]{1,0:T(8,128)(2,1)S(1)}) custom-call(s32[2,64]{1,0:T(2,128)S(4)} %get-tuple-element.33.lists, f32[4,256,512]{2,1,0:T(8,128)S(1)} %base.1, bf16[4,256,512]{2,1,0:T(8,128)(2,1)S(1)} %get-tuple-element.41.hits, f32[1,2048]{1,0:T(1,128)S(1)} %bitcast.4, ...), custom_call_target="tpu_custom_call", output_to_operand_aliasing={{0}: (6, {})} | custom-call | tf_op jit(solution)/shard_map/signal/pallas_call | solution.py:417
  19.6 1.9 %collective-permute-start.9 = (bf16[256,512]{1,0:T(8,128)(2,1)S(1)}, bf16[256,512]{1,0:T(8,128)(2,1)S(1)}, u32[]{:S(2)}, u32[]{:S(2)}) collective-permute-start(bf16[256,512]{1,0:T(8,128)(2,1)S(1)} %get-tuple-element.51), channel_id=1, source_target_pairs={{1,2},{3,4},{5,6},{7,8},{9,10},{11,12},{13,14},{15,0},{2,1},{4,3},... | collective-permute-start | bytes 786440 | tf_op jit(solution)/shard_map/ppermute | solution.py:366
  21.5 0.8 %push.1 = (bf16[176,512]{1,0:T(8,128)(2,1)S(1)}, bf16[176,512]{1,0:T(8,128)(2,1)S(1)}, bf16[160,512]{1,0:T(8,128)(2,1)S(1)}) custom-call(s32[2,64]{1,0:T(2,128)S(4)} %get-tuple-element.33.lists, bf16[4,256,512]{2,1,0:T(8,128)(2,1)S(1)} %get-tuple-element.45.signal, bf16[4,2,512,512]{3,2,1,0:T(8,128)(2,1)S(1)} %get-tuple-element.37.tiles), custom_call_target="tpu_custom_call" | custom-call | tf_op jit(solution)/shard_map/push/pallas_call | solution.py:431
  22.3 6.2 %collective-permute-start.6 = (bf16[176,512]{1,0:T(8,128)(2,1)S(1)}, bf16[176,512]{1,0:T(8,128)(2,1)S(1)}, u32[]{:S(2)}, u32[]{:S(2)}) collective-permute-start(bf16[176,512]{1,0:T(8,128)(2,1)S(1)} %get-tuple-element.47), channel_id=1, source_target_pairs={{0,1},{1,0},{2,3},{3,2},{4,5},{5,4},{6,7},{7,6},{8,9},{9,8},{10,11... | collective-permute-start | bytes 540680 | tf_op jit(solution)/shard_map/ppermute | solution.py:272
  29.1 1.0 %query.1.part = f32[256,768]{1,0:T(8,128)S(1)} custom-call(bf16[4,256,512]{2,1,0:T(8,128)(2,1)S(1)} %get-tuple-element.45.signal, bf16[2048,768]{1,0:T(8,128)(2,1)S(1)} %get-tuple-element.35.embeddings), custom_call_target="tpu_custom_call" | custom-call | tf_op jit(solution)/shard_map/query/pallas_call | solution.py:441
  30.5 0.6 %query_on.1 = (f32[256,768]{1,0:T(8,128)S(1)}, bf16[2,256,512]{2,1,0:T(8,128)(2,1)S(1)}) custom-call(s32[2,64]{1,0:T(2,128)S(4)} %get-tuple-element.33.lists, f32[256,768]{1,0:T(8,128)S(1)} %query_half.1.part, bf16[2048,768]{1,0:T(8,128)(2,1)S(1)} %get-tuple-element.35.embeddings, bf16[176,512]{1,0:T(8,128)(2,1)S(1)} %collective-permute-done.6.rest_0_, ...), custom_call_target="tpu_custom_call" | custom-call | tf_op jit(solution)/shard_map/query_on/pallas_call | solution.py:449
  31.1 0.7 %embed.4 = (bf16[512,768]{1,0:T(8,128)(2,1)S(1)}, f32[8,128]{1,0:T(8,128)}) custom-call(s32[2,64]{1,0:T(2,128)S(4)} %get-tuple-element.33.lists, bf16[4,256,512]{2,1,0:T(8,128)(2,1)S(1)} %get-tuple-element.45.signal, bf16[2,256,512]{2,1,0:T(8,128)(2,1)S(1)} %get-tuple-element.50.on, bf16[256,512]{1,0:T(8,128)(2,1)S(1)} %collective-permute-done.5.received.off_a, ...), custom_call_target="tpu_custom_call" | custom-call | tf_op jit(solution)/shard_map/embed/pallas_call | solution.py:457
  31.8 0.9 %embed.5 = (bf16[2048,768]{1,0:T(8,128)(2,1)}, bf16[512,768]{1,0:T(8,128)(2,1)S(1)}, f32[8,128]{1,0:T(8,128)S(1)}) custom-call(s32[2,64]{1,0:T(2,128)S(4)} %get-tuple-element.33.lists, bf16[4,256,512]{2,1,0:T(8,128)(2,1)S(1)} %get-tuple-element.45.signal, bf16[2,256,512]{2,1,0:T(8,128)(2,1)S(1)} %get-tuple-element.50.on, ...), custom_call_target="tpu_custom_call" | custom-call | tf_op jit(solution)/shard_map/embed/pallas_call | solution.py:457
  33.5 1.0 %collective-permute-done.10.got = bf16[128,768]{1,0:T(8,128)(2,1)S(1)} collective-permute-done((bf16[128,768]{1,0:T(8,128)(2,1)S(1)}, bf16[128,768]{1,0:T(8,128)(2,1)S(1)}, u32[]{:S(2)}, u32[]{:S(2)}) %collective-permute-start.10) | collective-permute-done | bytes 196640 | tf_op jit(solution)/shard_map/ppermute | solution.py:272
  34.6 0.7 %collective-permute-start.11 = (bf16[64,768]{1,0:T(8,128)(2,1)S(1)}, bf16[64,768]{1,0:T(8,128)(2,1)S(1)}, u32[]{:S(2)}, u32[]{:S(2)}) collective-permute-start(bf16[64,768]{1,0:T(8,128)(2,1)S(1)} %get-tuple-element.60.held), channel_id=1, source_target_pairs={{0,2},{1,3},{2,0},{3,1},{4,6},{5,7},{6,4},{7,5},{8,10},{9,11},{10,... | collective-permute-start | bytes 294920 | tf_op jit(solution)/shard_map/ppermute | solution.py:272
  35.3 1.8 %collective-permute-start.15 = (bf16[64,768]{1,0:T(8,128)(2,1)S(1)}, bf16[64,768]{1,0:T(8,128)(2,1)S(1)}, u32[]{:S(2)}, u32[]{:S(2)}) collective-permute-start(bf16[64,768]{1,0:T(8,128)(2,1)S(1)} %get-tuple-element.63.held), channel_id=1, source_target_pairs={{0,8},{1,9},{2,10},{3,11},{4,12},{5,13},{6,14},{7,15},{8,0},{9,1},... | collective-permute-start | bytes 294920 | tf_op jit(solution)/shard_map/ppermute | solution.py:272
  37.1 0.9 %embed.6 = (bf16[2048,768]{1,0:T(8,128)(2,1)}, bf16[512,768]{1,0:T(8,128)(2,1)S(1)}, f32[8,128]{1,0:T(8,128)S(1)}) custom-call(s32[2,64]{1,0:T(2,128)S(4)} %get-tuple-element.33.lists, bf16[4,256,512]{2,1,0:T(8,128)(2,1)S(1)} %get-tuple-element.45.signal, bf16[2,256,512]{2,1,0:T(8,128)(2,1)S(1)} %get-tuple-element.50.on, ...), custom_call_target="tpu_custom_call", output_to_operand_aliasing={{0}: (6, {})} | custom-call | tf_op jit(solution)/shard_map/embed/pallas_call | solution.py:457
  38.0 1.5 %collective-permute-done.11.got = bf16[64,768]{1,0:T(8,128)(2,1)S(1)} collective-permute-done((bf16[64,768]{1,0:T(8,128)(2,1)S(1)}, bf16[64,768]{1,0:T(8,128)(2,1)S(1)}, u32[]{:S(2)}, u32[]{:S(2)}) %collective-permute-start.11) | collective-permute-done | bytes 98336 | tf_op jit(solution)/shard_map/ppermute | solution.py:272
  39.5 1.5 %collective-permute-start.12 = (bf16[64,768]{1,0:T(8,128)(2,1)S(1)}, bf16[64,768]{1,0:T(8,128)(2,1)S(1)}, u32[]{:S(2)}, u32[]{:S(2)}) collective-permute-start(bf16[64,768]{1,0:T(8,128)(2,1)S(1)} %add.6.held), channel_id=1, source_target_pairs={{0,4},{1,5},{2,6},{3,7},{4,0},{5,1},{6,2},{7,3},{8,12},{9,13},{10,... | collective-permute-start | bytes 294920 | tf_op jit(solution)/shard_map/ppermute | solution.py:272
  41.0 1.9 %collective-permute-done.15.got = bf16[64,768]{1,0:T(8,128)(2,1)S(1)} collective-permute-done((bf16[64,768]{1,0:T(8,128)(2,1)S(1)}, bf16[64,768]{1,0:T(8,128)(2,1)S(1)}, u32[]{:S(2)}, u32[]{:S(2)}) %collective-permute-start.15) | collective-permute-done | bytes 98336 | tf_op jit(solution)/shard_map/ppermute | solution.py:272
  43.0 1.5 %collective-permute-start.16 = (bf16[64,768]{1,0:T(8,128)(2,1)S(1)}, bf16[64,768]{1,0:T(8,128)(2,1)S(1)}, u32[]{:S(2)}, u32[]{:S(2)}) collective-permute-start(bf16[64,768]{1,0:T(8,128)(2,1)S(1)} %add.9.held), channel_id=1, source_target_pairs={{0,2},{1,3},{2,0},{3,1},{4,6},{5,7},{6,4},{7,5},{8,10},{9,11},{10,... | collective-permute-start | bytes 294920 | tf_op jit(solution)/shard_map/ppermute | solution.py:272
  44.4 2.3 %embed.7 = (bf16[2048,768]{1,0:T(8,128)(2,1)}, bf16[512,768]{1,0:T(8,128)(2,1)}, f32[8,128]{1,0:T(8,128)S(1)}) custom-call(s32[2,64]{1,0:T(2,128)S(4)} %get-tuple-element.33.lists, bf16[4,256,512]{2,1,0:T(8,128)(2,1)S(1)} %get-tuple-element.45.signal, bf16[2,256,512]{2,1,0:T(8,128)(2,1)S(1)} %get-tuple-element.50.on, ...), custom_call_target="tpu_custom_call", output_to_operand_aliasing={{0}: (7, {})} | custom-call | tf_op jit(solution)/shard_map/embed/pallas_call | solution.py:457
  46.9 0.8 %collective-permute-done.16.got = bf16[64,768]{1,0:T(8,128)(2,1)S(1)} collective-permute-done((bf16[64,768]{1,0:T(8,128)(2,1)S(1)}, bf16[64,768]{1,0:T(8,128)(2,1)S(1)}, u32[]{:S(2)}, u32[]{:S(2)}) %collective-permute-start.16) | collective-permute-done | bytes 98336 | tf_op jit(solution)/shard_map/ppermute | solution.py:272
  47.7 1.6 %collective-permute-start.17 = (bf16[64,768]{1,0:T(8,128)(2,1)S(1)}, bf16[64,768]{1,0:T(8,128)(2,1)S(1)}, u32[]{:S(2)}, u32[]{:S(2)}) collective-permute-start(bf16[64,768]{1,0:T(8,128)(2,1)S(1)} %add.10.held), channel_id=1, source_target_pairs={{0,4},{1,5},{2,6},{3,7},{4,0},{5,1},{6,2},{7,3},{8,12},{9,13},{10,... | collective-permute-start | bytes 294920 | tf_op jit(solution)/shard_map/ppermute | solution.py:272
  49.3 3.9 %collective-permute-done.13.got = bf16[64,768]{1,0:T(8,128)(2,1)S(1)} collective-permute-done((bf16[64,768]{1,0:T(8,128)(2,1)S(1)}, bf16[64,768]{1,0:T(8,128)(2,1)S(1)}, u32[]{:S(2)}, u32[]{:S(2)}) %collective-permute-start.13) | collective-permute-done | bytes 98336 | tf_op jit(solution)/shard_map/ppermute | solution.py:272
  53.3 0.6 collective-permute-done.17.got
  54.4 0.8 %place.2.refs_2_ = f32[256,768]{1,0:T(8,128)} custom-call(bf16[64,768]{1,0:T(8,128)(2,1)S(1)} %add.8.rest_0_.refs_0_, bf16[64,768]{1,0:T(8,128)(2,1)S(1)} %add.11.refs_1_), custom_call_target="tpu_custom_call" | custom-call | tf_op jit(solution)/shard_map/place/pallas_call | solution.py:339
  55.4 0.8 %place.3 = f32[256,768]{1,0:T(8,128)} custom-call(bf16[64,768]{1,0:T(8,128)(2,1)S(1)} %collective-permute-done.14.refs_0_, bf16[64,768]{1,0:T(8,128)(2,1)S(1)} %collective-permute-done.18.refs_1_, f32[256,768]{1,0:T(8,128)} %place.2.refs_2_), custom_call_target="tpu_custom_call", output_to_operand_aliasing={{}: (2, {})} | custom-call | tf_op jit(solution)/shard_map/place/pallas_call | solution.py:339
  (35 shorter events, 2.9 us)
Async XLA Ops:
  0.6 10.0 %copy-start.1 = (s32[256,8]{0,1:T(8,128)S(1)}, s32[256,8]{0,1:T(8,128)}, u32[]{:S(2)}) copy-start(s32[256,8]{0,1:T(8,128)} %param.11) | copy-start | bytes 24580
  2.7 11.3 %collective-permute-start.4 = (bf16[256,512]{1,0:T(8,128)(2,1)S(1)}, bf16[256,512]{1,0:T(8,128)(2,1)S(1)}, u32[]{:S(2)}, u32[]{:S(2)}) collective-permute-start(bf16[256,512]{1,0:T(8,128)(2,1)S(1)} %get-tuple-element.43), channel_id=1, source_target_pairs={{1,2},{3,4},{5,6},{7,8},{9,10},{11,12},{13,14},{15,0},{2,1},{4,3},... | collective-permute-start | bytes 786440 | tf_op jit(solution)/shard_map/ppermute | solution.py:366
  9.3 3.8 %collective-permute-start = (bf16[176,512]{1,0:T(8,128)(2,1)S(1)}, bf16[176,512]{1,0:T(8,128)(2,1)S(1)}, u32[]{:S(2)}, u32[]{:S(2)}) collective-permute-start(bf16[176,512]{1,0:T(8,128)(2,1)S(1)} %get-tuple-element.38), channel_id=1, source_target_pairs={{0,1},{1,0},{2,3},{3,2},{4,5},{5,4},{6,7},{7,6},{8,9},{9,8},{10,11... | collective-permute-start | bytes 540680 | tf_op jit(solution)/shard_map/ppermute | solution.py:272
  9.4 3.8 %collective-permute-start.1 = (bf16[176,512]{1,0:T(8,128)(2,1)S(1)}, bf16[176,512]{1,0:T(8,128)(2,1)S(1)}, u32[]{:S(2)}, u32[]{:S(2)}) collective-permute-start(bf16[176,512]{1,0:T(8,128)(2,1)S(1)} %get-tuple-element.39), channel_id=1, source_target_pairs={{0,1},{1,0},{2,3},{3,2},{4,5},{5,4},{6,7},{7,6},{8,9},{9,8},{10,11... | collective-permute-start | bytes 540680 | tf_op jit(solution)/shard_map/ppermute | solution.py:272
  9.9 3.3 %collective-permute-start.2 = (bf16[160,512]{1,0:T(8,128)(2,1)S(1)}, bf16[160,512]{1,0:T(8,128)(2,1)S(1)}, u32[]{:S(2)}, u32[]{:S(2)}) collective-permute-start(bf16[160,512]{1,0:T(8,128)(2,1)S(1)} %get-tuple-element.40), channel_id=1, source_target_pairs={{0,1},{1,0},{2,3},{3,2},{4,5},{5,4},{6,7},{7,6},{8,9},{9,8},{10,11... | collective-permute-start | bytes 491528 | tf_op jit(solution)/shard_map/ppermute | solution.py:272
  9.9 9.0 %collective-permute-start.3 = (bf16[256,512]{1,0:T(8,128)(2,1)S(1)}, bf16[256,512]{1,0:T(8,128)(2,1)S(1)}, u32[]{:S(2)}, u32[]{:S(2)}) collective-permute-start(bf16[256,512]{1,0:T(8,128)(2,1)S(1)} %get-tuple-element.42), channel_id=1, source_target_pairs={{1,2},{3,4},{5,6},{7,8},{9,10},{11,12},{13,14},{15,0},{2,1},{4,3},... | collective-permute-start | bytes 786440 | tf_op jit(solution)/shard_map/ppermute | solution.py:366
  13.1 0.8 %copy-start = (f32[2048]{0:T(1024)S(1)}, f32[2048]{0:T(1024)}, u32[]{:S(2)}) copy-start(f32[2048]{0:T(1024)} %param.9) | copy-start | bytes 24580
  15.7 14.3 %collective-permute-start.5 = (bf16[256,512]{1,0:T(8,128)(2,1)S(1)}, bf16[256,512]{1,0:T(8,128)(2,1)S(1)}, u32[]{:S(2)}, u32[]{:S(2)}) collective-permute-start(bf16[256,512]{1,0:T(8,128)(2,1)S(1)} %get-tuple-element.46), channel_id=1, source_target_pairs={{1,2},{3,4},{5,6},{7,8},{9,10},{11,12},{13,14},{15,0},{2,1},{4,3},... | collective-permute-start | bytes 786440 | tf_op jit(solution)/shard_map/ppermute | solution.py:366
  19.6 13.1 %collective-permute-start.9 = (bf16[256,512]{1,0:T(8,128)(2,1)S(1)}, bf16[256,512]{1,0:T(8,128)(2,1)S(1)}, u32[]{:S(2)}, u32[]{:S(2)}) collective-permute-start(bf16[256,512]{1,0:T(8,128)(2,1)S(1)} %get-tuple-element.51), channel_id=1, source_target_pairs={{1,2},{3,4},{5,6},{7,8},{9,10},{11,12},{13,14},{15,0},{2,1},{4,3},... | collective-permute-start | bytes 786440 | tf_op jit(solution)/shard_map/ppermute | solution.py:366
  22.3 8.2 %collective-permute-start.6 = (bf16[176,512]{1,0:T(8,128)(2,1)S(1)}, bf16[176,512]{1,0:T(8,128)(2,1)S(1)}, u32[]{:S(2)}, u32[]{:S(2)}) collective-permute-start(bf16[176,512]{1,0:T(8,128)(2,1)S(1)} %get-tuple-element.47), channel_id=1, source_target_pairs={{0,1},{1,0},{2,3},{3,2},{4,5},{5,4},{6,7},{7,6},{8,9},{9,8},{10,11... | collective-permute-start | bytes 540680 | tf_op jit(solution)/shard_map/ppermute | solution.py:272
  28.6 1.9 %collective-permute-start.7 = (bf16[176,512]{1,0:T(8,128)(2,1)S(1)}, bf16[176,512]{1,0:T(8,128)(2,1)S(1)}, u32[]{:S(2)}, u32[]{:S(2)}) collective-permute-start(bf16[176,512]{1,0:T(8,128)(2,1)S(1)} %get-tuple-element.48), channel_id=1, source_target_pairs={{0,1},{1,0},{2,3},{3,2},{4,5},{5,4},{6,7},{7,6},{8,9},{9,8},{10,11... | collective-permute-start | bytes 540680 | tf_op jit(solution)/shard_map/ppermute | solution.py:272
  28.6 1.8 %collective-permute-start.8 = (bf16[160,512]{1,0:T(8,128)(2,1)S(1)}, bf16[160,512]{1,0:T(8,128)(2,1)S(1)}, u32[]{:S(2)}, u32[]{:S(2)}) collective-permute-start(bf16[160,512]{1,0:T(8,128)(2,1)S(1)} %get-tuple-element.49), channel_id=1, source_target_pairs={{0,1},{1,0},{2,3},{3,2},{4,5},{5,4},{6,7},{7,6},{8,9},{9,8},{10,11... | collective-permute-start | bytes 491528 | tf_op jit(solution)/shard_map/ppermute | solution.py:272
  33.1 1.5 %collective-permute-start.10 = (bf16[128,768]{1,0:T(8,128)(2,1)S(1)}, bf16[128,768]{1,0:T(8,128)(2,1)S(1)}, u32[]{:S(2)}, u32[]{:S(2)}) collective-permute-start(bf16[128,768]{1,0:T(8,128)(2,1)S(1)} %query_end.3), channel_id=1, source_target_pairs={{0,1},{1,0},{2,3},{3,2},{4,5},{5,4},{6,7},{7,6},{8,9},{9,8},{10,11... | collective-permute-start | bytes 589832 | tf_op jit(solution)/shard_map/ppermute | solution.py:272
  34.6 4.9 %collective-permute-start.11 = (bf16[64,768]{1,0:T(8,128)(2,1)S(1)}, bf16[64,768]{1,0:T(8,128)(2,1)S(1)}, u32[]{:S(2)}, u32[]{:S(2)}) collective-permute-start(bf16[64,768]{1,0:T(8,128)(2,1)S(1)} %get-tuple-element.60.held), channel_id=1, source_target_pairs={{0,2},{1,3},{2,0},{3,1},{4,6},{5,7},{6,4},{7,5},{8,10},{9,11},{10,... | collective-permute-start | bytes 294920 | tf_op jit(solution)/shard_map/ppermute | solution.py:272
  35.3 7.7 %collective-permute-start.15 = (bf16[64,768]{1,0:T(8,128)(2,1)S(1)}, bf16[64,768]{1,0:T(8,128)(2,1)S(1)}, u32[]{:S(2)}, u32[]{:S(2)}) collective-permute-start(bf16[64,768]{1,0:T(8,128)(2,1)S(1)} %get-tuple-element.63.held), channel_id=1, source_target_pairs={{0,8},{1,9},{2,10},{3,11},{4,12},{5,13},{6,14},{7,15},{8,0},{9,1},... | collective-permute-start | bytes 294920 | tf_op jit(solution)/shard_map/ppermute | solution.py:272
  39.5 7.2 %collective-permute-start.12 = (bf16[64,768]{1,0:T(8,128)(2,1)S(1)}, bf16[64,768]{1,0:T(8,128)(2,1)S(1)}, u32[]{:S(2)}, u32[]{:S(2)}) collective-permute-start(bf16[64,768]{1,0:T(8,128)(2,1)S(1)} %add.6.held), channel_id=1, source_target_pairs={{0,4},{1,5},{2,6},{3,7},{4,0},{5,1},{6,2},{7,3},{8,12},{9,13},{10,... | collective-permute-start | bytes 294920 | tf_op jit(solution)/shard_map/ppermute | solution.py:272
  43.0 4.7 %collective-permute-start.16 = (bf16[64,768]{1,0:T(8,128)(2,1)S(1)}, bf16[64,768]{1,0:T(8,128)(2,1)S(1)}, u32[]{:S(2)}, u32[]{:S(2)}) collective-permute-start(bf16[64,768]{1,0:T(8,128)(2,1)S(1)} %add.9.held), channel_id=1, source_target_pairs={{0,2},{1,3},{2,0},{3,1},{4,6},{5,7},{6,4},{7,5},{8,10},{9,11},{10,... | collective-permute-start | bytes 294920 | tf_op jit(solution)/shard_map/ppermute | solution.py:272
  46.8 6.4 %collective-permute-start.13 = (bf16[64,768]{1,0:T(8,128)(2,1)S(1)}, bf16[64,768]{1,0:T(8,128)(2,1)S(1)}, u32[]{:S(2)}, u32[]{:S(2)}) collective-permute-start(bf16[64,768]{1,0:T(8,128)(2,1)S(1)} %add.7.held), channel_id=1, source_target_pairs={{0,8},{1,9},{2,10},{3,11},{4,12},{5,13},{6,14},{7,15},{8,0},{9,1},... | collective-permute-start | bytes 294920 | tf_op jit(solution)/shard_map/ppermute | solution.py:272
  47.7 6.1 %collective-permute-start.17 = (bf16[64,768]{1,0:T(8,128)(2,1)S(1)}, bf16[64,768]{1,0:T(8,128)(2,1)S(1)}, u32[]{:S(2)}, u32[]{:S(2)}) collective-permute-start(bf16[64,768]{1,0:T(8,128)(2,1)S(1)} %add.10.held), channel_id=1, source_target_pairs={{0,4},{1,5},{2,6},{3,7},{4,0},{5,1},{6,2},{7,3},{8,12},{9,13},{10,... | collective-permute-start | bytes 294920 | tf_op jit(solution)/shard_map/ppermute | solution.py:272
  53.9 1.4 %collective-permute-start.18 = (bf16[64,768]{1,0:T(8,128)(2,1)S(1)}, bf16[64,768]{1,0:T(8,128)(2,1)S(1)}, u32[]{:S(2)}, u32[]{:S(2)}) collective-permute-start(bf16[64,768]{1,0:T(8,128)(2,1)S(1)} %add.11.refs_1_), channel_id=1, source_target_pairs={{0,1},{1,0},{2,3},{3,2},{4,5},{5,4},{6,7},{7,6},{8,9},{9,8},{10,11... | collective-permute-start | bytes 294920 | tf_op jit(solution)/shard_map/ppermute | solution.py:272
  53.9 1.4 %collective-permute-start.14 = (bf16[64,768]{1,0:T(8,128)(2,1)S(1)}, bf16[64,768]{1,0:T(8,128)(2,1)S(1)}, u32[]{:S(2)}, u32[]{:S(2)}) collective-permute-start(bf16[64,768]{1,0:T(8,128)(2,1)S(1)} %add.8.rest_0_.refs_0_), channel_id=1, source_target_pairs={{0,1},{1,0},{2,3},{3,2},{4,5},{5,4},{6,7},{7,6},{8,9},{9,8},{10,11... | collective-permute-start | bytes 294920 | tf_op jit(solution)/shard_map/ppermute | solution.py:272
